TPU v7x, 32 devices: a whole 2x2x4 slice. The times are simulated.
32 devices in a mesh: dp: 2 (over core), expert: 4 (over z), tensor: 4 (over y, x).
Axes of the slice: x: 2, y: 2, z: 4, core: 2. Of those that a mesh axis runs over, the one named last changes fastest.
Arguments:
- tokens: bfloat16 [2048, 1024], P(('dp', 'expert')), may hold values from -6 to 6
- routes: int32 [2048, 8], P(('dp', 'expert')), may hold values from 0 to 31, all different within a row; in each aligned block of 256 rows (0 to 255, 256 to 511, ...) at most 80 rows name the same one
- gain_first: float32 [1024], replicated, may hold values from 0.5 to 1.5
- w_query: bfloat16 [1024, 1024], P(None, 'tensor'), may hold values from -0.25 to 0.25
- w_key: bfloat16 [1024, 512], P(None, 'tensor'), may hold values from -0.25 to 0.25
- w_value: bfloat16 [1024, 512], P(None, 'tensor'), may hold values from -0.1875 to 0.1875
- w_output: bfloat16 [1024, 1024], P('tensor'), may hold values from -1 to 1
- gain_second: float32 [1024], replicated, may hold values from 0.5 to 1.5
- w_router: bfloat16 [1024, 32], replicated, may hold values from -0.09375 to 0.09375
- w_gate: bfloat16 [32, 1024, 512], P('expert', None, 'tensor'), may hold values from -0.1875 to 0.1875
- w_up: bfloat16 [32, 1024, 512], P('expert', None, 'tensor'), may hold values from -0.1875 to 0.1875
- w_down: bfloat16 [32, 512, 1024], P('expert', 'tensor'), may hold values from -0.75 to 0.75
- cotangent: bfloat16 [2048, 1024], P(('dp', 'expert')), may hold values from -6 to 6
Outputs:
- output: bfloat16 [2048, 1024], P(('dp', 'expert'))
- loss_value: float32 [32], replicated
- input_grad: float32 [2048, 1024], P(('dp', 'expert'))
- grad_gain_first: float32 [1024], P(('dp', 'expert'))
- grad_w_query: float32 [1024, 1024], P(('dp', 'expert'), 'tensor')
- grad_w_key: float32 [1024, 512], P(('dp', 'expert'), 'tensor')
- grad_w_value: float32 [1024, 512], P(('dp', 'expert'), 'tensor')
- grad_w_output: float32 [1024, 1024], P('tensor', ('dp', 'expert'))
- grad_gain_second: float32 [1024], P(('dp', 'expert'))
- grad_router: float32 [1024, 32], P(('dp', 'expert'))
- grad_w_gate: float32 [32, 1024, 512], P('expert', None, 'tensor')
- grad_w_up: float32 [32, 1024, 512], P('expert', None, 'tensor')
- grad_w_down: float32 [32, 512, 1024], P('expert', 'tensor')
Inputs may be any that keep to these rules, and one draw needn't show every extreme that they name: `routes`: each token names 8 different experts. Among the 256 tokens of one sequence no expert is named more than 80 times, and in some sequence some expert is named exactly 80 times.
All inputs are finite; a program needn't handle non-finite values.
Results may differ from a plain program's by a relative error of at most 0.017.
The roundings to bfloat16 on the way count: a program that leaves them out, or rounds other values in their place, can miss the bound.
Values may be sent and summed in bfloat16 or wider, within the bound.
No kernel may reach another device: no remote copies, remote signals or barrier semaphores. Data moves between devices by JAX's collectives and lax.ppermute only.
A program may use at most 192 MiB of HBM per device.

v0:
```python
import jax
import jax.numpy as jnp
from jax import lax
from jax.sharding import PartitionSpec as P

HD = 64
TOP = 8
CAP = 80


EPS = 1e-06
ROPE_BASE = 10000.0
ROW_LIMIT = 1280
QUERY_LIMIT = 512
MASKED = -1e30


def in_blocks(x, dim, size):
    shape = x.shape
    parts = x.reshape(*shape[:dim], size, shape[dim] // size, *shape[dim + 1 :])
    return jnp.moveaxis(parts, dim, 0)


def sent_and_summed(x, axis, dim):
    size = lax.axis_size(axis)
    parts = lax.all_to_all(in_blocks(x, dim, size), axis, 0, 0, tiled=True)
    return jnp.sum(parts.astype(jnp.float32), axis=0)


def side_by_side(arrays, axis, dim, along):
    columns = [a.reshape(*a.shape[:along], -1) for a in arrays]
    both = jnp.concatenate(columns, axis=along)
    filled, at, finished = (sent_and_summed(both, axis, dim), 0, [])
    for a, column in zip(arrays, columns):
        slab = filled[..., at : at + column.shape[along]]
        finished.append(slab.reshape(*slab.shape[:along], *a.shape[along:]))
        at += column.shape[along]
    return tuple(finished)


def rope_tables(seq_len, head_dim):
    half_dim = head_dim // 2
    frequency = ROPE_BASE ** (-(jnp.arange(half_dim, dtype=jnp.float32) * 2.0) / head_dim)
    angles = jnp.arange(seq_len, dtype=jnp.float32)[:, None] * frequency[None, :]
    return (jnp.cos(angles)[:, None, :], jnp.sin(angles)[:, None, :])


def rotate(vectors, cosine_table, sine_table):
    half_dim = vectors.shape[-1] // 2
    first_half = vectors[..., :half_dim]
    second_half = vectors[..., half_dim:]
    return jnp.concatenate(
        [
            first_half * cosine_table - second_half * sine_table,
            second_half * cosine_table + first_half * sine_table,
        ],
        axis=-1,
    )


def rotate_back(gradient, cosine_table, sine_table):
    half_dim = gradient.shape[-1] // 2
    first_half = gradient[..., :half_dim]
    second_half = gradient[..., half_dim:]
    return jnp.concatenate(
        [
            first_half * cosine_table + second_half * sine_table,
            second_half * cosine_table - first_half * sine_table,
        ],
        axis=-1,
    )


def softmax_rows(scores):
    row_peak = jnp.max(scores, axis=-1, keepdims=True)
    exponent = jnp.exp(scores - row_peak)
    return exponent / jnp.sum(exponent, axis=-1, keepdims=True)


def route_slots(routes, experts):
    chosen = (routes[:, :, None] == jnp.arange(experts, dtype=jnp.int32)[None, None, :]).astype(
        jnp.int32
    )
    onehot = jnp.sum(chosen, axis=1)
    before = jnp.cumsum(onehot, axis=0) - onehot
    return (chosen, onehot, jnp.take_along_axis(before, routes, axis=1))


def attend(queries, key_rows, value_rows, score_scale):
    seq_len = queries.shape[0]
    query_block = min(seq_len, QUERY_LIMIT)
    key_place = jnp.arange(seq_len)
    scores = (
        jnp.einsum("bkgd,tkd->kgbt", queries, key_rows, preferred_element_type=jnp.float32)
        * score_scale
    )
    allowed = key_place[None, :] <= (0 + jnp.arange(query_block))[:, None]
    scores = jnp.where(allowed, scores, MASKED)
    row_peak = jnp.max(scores, axis=-1, keepdims=True)
    exponent = jnp.exp(scores - row_peak)
    row_total = jnp.sum(exponent, axis=-1, keepdims=True)
    soft_weights = (exponent / row_total).astype(jnp.bfloat16)
    mixed_list = jnp.einsum(
        "kgbt,tkd->bkgd", soft_weights, value_rows, preferred_element_type=jnp.float32
    )
    log_totals = [row_peak + jnp.log(row_total)]
    return (mixed_list, log_totals)


def attend_back(queries, key_rows, value_rows, grad_mixed, log_totals, score_scale):
    seq_len = queries.shape[0]
    query_block = min(seq_len, QUERY_LIMIT)
    key_place = jnp.arange(seq_len)
    grad_query_list = []
    grad_keys = jnp.zeros(key_rows.shape, jnp.float32)
    grad_values = jnp.zeros(value_rows.shape, jnp.float32)
    for block_index, row_start in enumerate(range(0, seq_len, query_block)):
        scores = (
            jnp.einsum("bkgd,tkd->kgbt", queries, key_rows, preferred_element_type=jnp.float32)
            * score_scale
        )
        allowed = key_place[None, :] <= (row_start + jnp.arange(query_block))[:, None]
        soft_weights = jnp.where(allowed, jnp.exp(scores - log_totals[block_index]), 0.0)
        grad_weights = jnp.einsum(
            "bkgd,tkd->kgbt", grad_mixed, value_rows, preferred_element_type=jnp.float32
        )
        grad_scores = (
            soft_weights
            * (grad_weights - jnp.sum(soft_weights * grad_weights, axis=-1, keepdims=True))
        ).astype(jnp.bfloat16)
        grad_values = jnp.einsum(
            "kgbt,bkgd->tkd",
            soft_weights.astype(jnp.bfloat16),
            grad_mixed,
            preferred_element_type=jnp.float32,
        )
        grad_query_list.append(
            jnp.einsum("kgbt,tkd->bkgd", grad_scores, key_rows, preferred_element_type=jnp.float32)
            * score_scale
        )
        grad_keys = (
            jnp.einsum("kgbt,bkgd->tkd", grad_scores, queries, preferred_element_type=jnp.float32)
            * score_scale
        )
    return (grad_query_list[0], grad_keys, grad_values)


def on_device(
    tokens,
    routes,
    gain_first,
    w_query,
    w_key,
    w_value,
    w_output,
    gain_second,
    w_router,
    w_gate,
    w_up,
    w_down,
    cotangent,
):
    seq_len, model_width = tokens.shape
    experts = w_router.shape[1]
    local_count = w_gate.shape[0]
    heads_dev = w_query.shape[1] // HD
    kv_dev = w_key.shape[1] // HD
    groups = heads_dev // kv_dev
    score_scale = HD ** (-0.5)
    token_count = seq_len * lax.axis_size("dp") * lax.axis_size("expert")
    tensor_parts = lax.axis_size("tensor")
    expert_parts = lax.axis_size("expert")
    share_size = CAP // tensor_parts
    share_start = lax.axis_index("tensor") * share_size
    cosine_table, sine_table = rope_tables(seq_len, HD)
    inputs_full = tokens.astype(jnp.float32)
    inverse_one = lax.rsqrt(jnp.mean(inputs_full * inputs_full, axis=-1, keepdims=True) + EPS)
    normed_one = (inputs_full * inverse_one * gain_first).astype(jnp.bfloat16)
    query_proj = jnp.dot(normed_one, w_query, preferred_element_type=jnp.float32).reshape(
        seq_len, heads_dev, HD
    )
    key_proj = jnp.dot(normed_one, w_key, preferred_element_type=jnp.float32).reshape(
        seq_len, kv_dev, HD
    )
    value_proj = jnp.dot(normed_one, w_value, preferred_element_type=jnp.float32)
    queries = (
        rotate(query_proj, cosine_table, sine_table)
        .astype(jnp.bfloat16)
        .reshape(seq_len, kv_dev, groups, HD)
    )
    key_rows = rotate(key_proj, cosine_table, sine_table).astype(jnp.bfloat16)
    value_rows = value_proj.astype(jnp.bfloat16).reshape(seq_len, kv_dev, HD)
    mixed_heads, log_totals = attend(queries, key_rows, value_rows, score_scale)
    mixed_heads = mixed_heads.reshape(seq_len, heads_dev * HD).astype(jnp.bfloat16)
    branch = lax.psum(jnp.dot(mixed_heads, w_output, preferred_element_type=jnp.float32), "tensor")
    residual = inputs_full + branch
    inverse_two = lax.rsqrt(jnp.mean(residual * residual, axis=-1, keepdims=True) + EPS)
    normed_two = (residual * inverse_two * gain_second).astype(jnp.bfloat16)
    logits = jnp.dot(normed_two, w_router, preferred_element_type=jnp.float32)
    probs_all = softmax_rows(logits)
    gate_weights = softmax_rows(jnp.take_along_axis(logits, routes, axis=1))
    chosen, onehot, slot_index = route_slots(routes, experts)
    counts, prob_sums = lax.psum(
        (jnp.sum(onehot, axis=0).astype(jnp.float32), jnp.sum(probs_all, axis=0)), ("dp", "expert")
    )
    fraction = counts / (token_count * TOP)
    balance = experts * fraction / token_count
    loss_value = experts * balance * prob_sums
    buffer = (
        jnp.zeros((experts, CAP, model_width), jnp.bfloat16)
        .at[routes, slot_index]
        .set(jnp.broadcast_to(normed_two[:, None, :], (seq_len, TOP, model_width)))
    )
    arrived = lax.all_to_all(buffer, "expert", split_axis=0, concat_axis=1, tiled=True)
    row_count = expert_parts * CAP
    row_block = min(row_count, ROW_LIMIT)
    blocks = row_count // row_block

    def expert_forward(expert_item):
        gate_w, up_w, down_w, rows_in = expert_item

        def block_step(running, rows_piece):
            gate_val = jnp.dot(rows_piece, gate_w, preferred_element_type=jnp.float32)
            up_val = jnp.dot(rows_piece, up_w, preferred_element_type=jnp.float32)
            hidden = (gate_val * jax.nn.sigmoid(gate_val) * up_val).astype(jnp.bfloat16)
            result = jnp.dot(hidden, down_w, preferred_element_type=jnp.float32).astype(
                jnp.bfloat16
            )
            return (running, (gate_val, up_val, result))

        running_end, pieces = lax.scan(
            block_step, jnp.zeros((), jnp.float32), rows_in.reshape(blocks, row_block, model_width)
        )
        return pieces

    gate_vals, up_vals, results = lax.map(expert_forward, (w_gate, w_up, w_down, arrived))
    inside_list = []
    local_slots = []
    for ranked in range(TOP):
        slot_now = slot_index[:, ranked]
        inside_list.append(
            ((slot_now >= share_start) & (slot_now < share_start + share_size))[:, None]
        )
        local_slots.append(jnp.clip(slot_now - share_start, 0, share_size - 1))
    cot_full = cotangent.astype(jnp.float32)
    mixture_part = jnp.zeros((seq_len, model_width), jnp.float32)
    gate_dots = []
    returned = lax.all_to_all(
        results.reshape(local_count, row_count, model_width),
        "expert",
        split_axis=1,
        concat_axis=0,
        tiled=True,
    )
    for ranked in range(TOP):
        picked = returned[routes[:, ranked], slot_index[:, ranked]].astype(jnp.float32)
        mixture_part = mixture_part + gate_weights[:, ranked : ranked + 1] * picked
        gate_dots.append(jnp.sum(cot_full * picked, axis=1))
    mixture, gate_grad = lax.psum((mixture_part, jnp.stack(gate_dots, axis=1)), "tensor")
    output = (residual + mixture).astype(jnp.bfloat16)
    grad_buffer = jnp.zeros((experts, CAP, model_width), jnp.bfloat16)
    for ranked in range(TOP):
        grad_buffer = grad_buffer.at[routes[:, ranked], slot_index[:, ranked]].set(
            (gate_weights[:, ranked : ranked + 1] * cot_full).astype(jnp.bfloat16)
        )
    grad_arrived = lax.all_to_all(grad_buffer, "expert", split_axis=0, concat_axis=1, tiled=True)

    def expert_backward(expert_item):
        gate_w, up_w, down_w, rows_in, gate_blocks, up_blocks, grad_rows = expert_item

        def block_step(running, pieces):
            grad_gate_w, grad_up_w, grad_down_w = running
            rows_piece, gate_val, up_val, grad_piece = pieces
            sigmoid_val = jax.nn.sigmoid(gate_val)
            activation = gate_val * sigmoid_val
            hidden = (activation * up_val).astype(jnp.bfloat16)
            grad_down_w = grad_down_w + jnp.einsum(
                "rf,rd->fd", hidden, grad_piece, preferred_element_type=jnp.float32
            )
            grad_hidden = jnp.einsum(
                "rd,fd->rf", grad_piece, down_w, preferred_element_type=jnp.float32
            )
            grad_gate = (
                grad_hidden * up_val * sigmoid_val * (1.0 + gate_val * (1.0 - sigmoid_val))
            ).astype(jnp.bfloat16)
            grad_up = (grad_hidden * activation).astype(jnp.bfloat16)
            grad_gate_w = grad_gate_w + jnp.einsum(
                "rd,rf->df", rows_piece, grad_gate, preferred_element_type=jnp.float32
            )
            grad_up_w = grad_up_w + jnp.einsum(
                "rd,rf->df", rows_piece, grad_up, preferred_element_type=jnp.float32
            )
            grad_rows_in = (
                jnp.einsum("rf,df->rd", grad_gate, gate_w, preferred_element_type=jnp.float32)
                + jnp.einsum("rf,df->rd", grad_up, up_w, preferred_element_type=jnp.float32)
            ).astype(jnp.bfloat16)
            return ((grad_gate_w, grad_up_w, grad_down_w), grad_rows_in)

        zero_in = jnp.zeros(gate_w.shape, jnp.float32)
        zero_out = jnp.zeros(down_w.shape, jnp.float32)
        sums, grad_in = lax.scan(
            block_step,
            (zero_in, zero_in, zero_out),
            (
                rows_in.reshape(blocks, row_block, model_width),
                gate_blocks,
                up_blocks,
                grad_rows.reshape(blocks, row_block, model_width),
            ),
        )
        return (sums[0], sums[1], sums[2], grad_in)

    grad_w_gate, grad_w_up, grad_w_down, grad_rows_in = lax.map(
        expert_backward, (w_gate, w_up, w_down, arrived, gate_vals, up_vals, grad_arrived)
    )
    grad_normed_part = jnp.zeros((seq_len, model_width), jnp.float32)
    grad_back = lax.all_to_all(
        grad_rows_in.reshape(local_count, row_count, model_width),
        "expert",
        split_axis=1,
        concat_axis=0,
        tiled=True,
    )
    for ranked in range(TOP):
        grad_normed_part = grad_normed_part + grad_back[
            routes[:, ranked], slot_index[:, ranked]
        ].astype(jnp.float32)
    grad_normed_two = lax.psum(grad_normed_part, "tensor")
    gate_mean = jnp.sum(gate_weights * gate_grad, axis=1, keepdims=True)
    grad_chosen = gate_weights * (gate_grad - gate_mean)
    grad_logits = probs_all * (
        balance[None, :] - jnp.sum(probs_all * balance[None, :], axis=1, keepdims=True)
    )
    grad_logits = grad_logits + jnp.sum(
        chosen.astype(jnp.float32) * grad_chosen[:, :, None], axis=1
    )
    grad_logits = grad_logits.astype(jnp.bfloat16)
    grad_router = jnp.einsum(
        "sd,se->de", normed_two, grad_logits, preferred_element_type=jnp.float32
    )
    grad_normed_two = grad_normed_two + jnp.einsum(
        "se,de->sd", grad_logits, w_router, preferred_element_type=jnp.float32
    )
    scaled_two = gain_second * grad_normed_two
    grad_gain_second = jnp.sum(grad_normed_two * residual * inverse_two, axis=0)
    grad_resid = (
        cot_full
        + inverse_two * scaled_two
        - residual * inverse_two**3 * jnp.mean(scaled_two * residual, axis=-1, keepdims=True)
    )
    grad_branch = grad_resid.astype(jnp.bfloat16)
    grad_w_output = jnp.einsum(
        "sa,sd->ad", mixed_heads, grad_branch, preferred_element_type=jnp.float32
    )
    grad_mixed = jnp.einsum(
        "sd,ad->sa", grad_branch, w_output, preferred_element_type=jnp.float32
    ).astype(jnp.bfloat16)
    grad_queries, grad_keys, grad_values = attend_back(
        queries,
        key_rows,
        value_rows,
        grad_mixed.reshape(seq_len, kv_dev, groups, HD),
        log_totals,
        score_scale,
    )
    grad_query_proj = (
        rotate_back(grad_queries.reshape(seq_len, heads_dev, HD), cosine_table, sine_table)
        .astype(jnp.bfloat16)
        .reshape(seq_len, heads_dev * HD)
    )
    grad_key_proj = (
        rotate_back(grad_keys, cosine_table, sine_table)
        .astype(jnp.bfloat16)
        .reshape(seq_len, kv_dev * HD)
    )
    grad_value_proj = grad_values.astype(jnp.bfloat16).reshape(seq_len, kv_dev * HD)
    grad_w_query = jnp.einsum(
        "sd,sa->da", normed_one, grad_query_proj, preferred_element_type=jnp.float32
    )
    grad_w_key = jnp.einsum(
        "sd,sa->da", normed_one, grad_key_proj, preferred_element_type=jnp.float32
    )
    grad_w_value = jnp.einsum(
        "sd,sa->da", normed_one, grad_value_proj, preferred_element_type=jnp.float32
    )
    grad_normed_one = (
        jnp.einsum("sa,da->sd", grad_query_proj, w_query, preferred_element_type=jnp.float32)
        + jnp.einsum("sa,da->sd", grad_key_proj, w_key, preferred_element_type=jnp.float32)
        + jnp.einsum("sa,da->sd", grad_value_proj, w_value, preferred_element_type=jnp.float32)
    )
    grad_normed_one = lax.psum(grad_normed_one.astype(jnp.bfloat16), "tensor").astype(jnp.float32)
    scaled_one = gain_first * grad_normed_one
    grad_gain_first = jnp.sum(grad_normed_one * inputs_full * inverse_one, axis=0)
    input_grad = (
        grad_resid
        + inverse_one * scaled_one
        - inputs_full * inverse_one**3 * jnp.mean(scaled_one * inputs_full, axis=-1, keepdims=True)
    )
    dense_sums = side_by_side(
        (
            grad_w_query.astype(jnp.bfloat16),
            grad_w_key.astype(jnp.bfloat16),
            grad_w_value.astype(jnp.bfloat16),
            grad_router.astype(jnp.bfloat16),
            grad_gain_first.astype(jnp.bfloat16),
            grad_gain_second.astype(jnp.bfloat16),
        ),
        ("dp", "expert"),
        0,
        1,
    )
    grad_w_output = lax.psum_scatter(
        grad_w_output, ("dp", "expert"), scatter_dimension=1, tiled=True
    )
    expert_sums = (
        lax.psum(grad_w_gate.astype(jnp.bfloat16), "dp").astype(jnp.float32),
        lax.psum(grad_w_up.astype(jnp.bfloat16), "dp").astype(jnp.float32),
        lax.psum(grad_w_down.astype(jnp.bfloat16), "dp").astype(jnp.float32),
    )
    return (
        output,
        loss_value,
        input_grad,
        dense_sums[4],
        dense_sums[0],
        dense_sums[1],
        dense_sums[2],
        grad_w_output,
        dense_sums[5],
        dense_sums[3],
        expert_sums[0],
        expert_sums[1],
        expert_sums[2],
    )


def solution(mesh):
    placed = (
        P(("dp", "expert"), None),
        P(("dp", "expert"), None),
        P(),
        P(None, "tensor"),
        P(None, "tensor"),
        P(None, "tensor"),
        P("tensor", None),
        P(),
        P(),
        P("expert", None, "tensor"),
        P("expert", None, "tensor"),
        P("expert", "tensor", None),
        P(("dp", "expert"), None),
    )
    return jax.shard_map(
        on_device,
        mesh=mesh,
        in_specs=placed,
        out_specs=(
            P(("dp", "expert"), None),
            P(),
            P(("dp", "expert"), None),
            P(("dp", "expert")),
            P(("dp", "expert"), "tensor"),
            P(("dp", "expert"), "tensor"),
            P(("dp", "expert"), "tensor"),
            P("tensor", ("dp", "expert")),
            P(("dp", "expert")),
            P(("dp", "expert"), None),
            P("expert", None, "tensor"),
            P("expert", None, "tensor"),
            P("expert", "tensor", None),
        ),
        check_vma=False,
    )
```

profile of v0, /device:TPU:0, one launch (start us, length us, event | category | flops | bytes accessed | tf_op | source)
XLA Modules:
  0.0 1356.1 jit_solution(9379267877645155424)
XLA Ops:
  20.7 13.6 %gather_fusion.17 = s32[2048]{0:T(1024)S(1)} fusion(s32[256,32]{1,0:T(8,128)S(1)} %bitcast_subtract_fusion, s32[2048]{0:T(1024)S(1)} %reshape.351), kind=kCustom, calls=%fused_computation.17 | custom fusion | bytes 32768 | tf_op jit(solution)/shard_map/jit(take_along_axis)/gather | solution.py:86
  34.5 39.5 %all-reduce.7.cloned.1.call-done = f32[256,1024]{1,0:T(8,128)} async-done(((f32[256,1024]{1,0:T(8,128)}), f32[256,1024]{1,0:T(8,128)}) %all-reduce.7.cloned.1.call-update) | async-done | bytes 1048592 | tf_op jit(solution)/shard_map/psum | solution.py:195
  76.0 16.8 %gather_fusion.16 = f32[2048]{0:T(1024)S(1)} fusion(f32[256,32]{0,1:T(8,128)S(1)} %get-tuple-element.438, s32[2048]{0:T(1024)S(1)} %reshape.351), kind=kCustom, calls=%fused_computation.16 | custom fusion | bytes 32768 | tf_op jit(solution)/shard_map/jit(take_along_axis)/gather | solution.py:201
  93.4 13.0 scatter_custom_fusion.8
  106.3 5.4 all-to-all-start
  111.8 115.9 %all-to-all-done = bf16[32,80,1024]{2,1,0:T(8,128)(2,1)} async-done(((bf16[32,80,1024]{2,1,0:T(8,128)(2,1)}), bf16[32,80,1024]{2,1,0:T(8,128)(2,1)}, u32[]{:S(2)}, u32[]{:S(2)}) %all-to-all-start) | async-done | bytes 5242912 | tf_op jit(solution)/shard_map/all_to_all | solution.py:214
  227.7 5.7 copy.275
  236.5 51.5 %while.5 = (s32[]{:T(128)}, f32[8,1,320,128]{3,2,1,0:T(8,128)}, f32[8,1,320,128]{3,2,1,0:T(8,128)}, bf16[8,1,320,1024]{3,2,1,0:T(8,128)(2,1)}, bf16[8,320,1024]{...) while((s32[]{:T(128)}, f32[8,1,320,128]{3,2,1,0:T(8,128)}, ...), condition=%wide.region_12.13_spmd, body=%wide.region_11.12_spmd.sunk | while | flops 252231680 | bytes 3739749 | solution.py:236
  287.9 7.6 copy.320
  295.6 5.1 all-to-all-start.1
  300.7 115.1 %all-to-all-done.1 = bf16[8,320,1024]{2,0,1:T(8,128)(2,1)} async-done(((bf16[8,320,1024]{2,0,1:T(8,128)(2,1)}), bf16[8,320,1024]{2,0,1:T(8,128)(2,1)}, u32[]{:S(2)}, u32[]{:S(2)}) %all-to-all-start.1) | async-done | bytes 5242912 | tf_op jit(solution)/shard_map/all_to_all | solution.py:248
  415.9 7.8 copy.277
  427.0 4.2 gather_fusion.6
  431.2 4.2 gather_fusion.5
  435.4 4.2 gather_fusion.4
  439.5 4.4 gather_fusion.3
  443.9 4.2 gather_fusion.2
  452.2 4.2 gather_fusion
  459.4 9.1 psum.75
  468.6 4.8 fusion.93
  476.5 36.2 %scatter_fusion = bf16[32,80,1024]{2,1,0:T(8,128)(2,1)} fusion(bf16[32,80,1024]{2,1,0:T(8,128)(2,1)} %broadcast.203, s32[256]{0:T(256)S(1)} %bitcast.378, bf16[256,1024]{1,0:T(8,128)(2,1)S(1)} %copy-done.15), kind=kCustom, calls=%fused_computation.18 | custom fusion | bytes 1574912 | tf_op jit(solution)/shard_map/scatter | solution.py:263
  512.7 36.3 %scatter_fusion.1 = bf16[32,80,1024]{2,1,0:T(8,128)(2,1)} fusion(bf16[32,80,1024]{2,1,0:T(8,128)(2,1)} %scatter_fusion, s32[256]{0:T(256)S(1)} %bitcast.377, bf16[256,1024]{1,0:T(8,128)(2,1)S(1)} %copy-done.14), kind=kCustom, calls=%fused_computation.19 | custom fusion | bytes 1574912 | tf_op jit(solution)/shard_map/scatter | solution.py:263
  549.0 36.4 %scatter_fusion.2 = bf16[32,80,1024]{2,1,0:T(8,128)(2,1)} fusion(bf16[32,80,1024]{2,1,0:T(8,128)(2,1)} %scatter_fusion.1, s32[256]{0:T(256)S(1)} %bitcast.376, bf16[256,1024]{1,0:T(8,128)(2,1)S(1)} %copy-done.13), kind=kCustom, calls=%fused_computation.20 | custom fusion | bytes 1574912 | tf_op jit(solution)/shard_map/scatter | solution.py:263
  585.4 36.1 %scatter_fusion.3 = bf16[32,80,1024]{2,1,0:T(8,128)(2,1)} fusion(bf16[32,80,1024]{2,1,0:T(8,128)(2,1)} %scatter_fusion.2, s32[256]{0:T(256)S(1)} %bitcast.375, bf16[256,1024]{1,0:T(8,128)(2,1)S(1)} %copy-done.12), kind=kCustom, calls=%fused_computation.21 | custom fusion | bytes 1574912 | tf_op jit(solution)/shard_map/scatter | solution.py:263
  621.6 36.2 %scatter_fusion.4 = bf16[32,80,1024]{2,1,0:T(8,128)(2,1)} fusion(bf16[32,80,1024]{2,1,0:T(8,128)(2,1)} %scatter_fusion.3, s32[256]{0:T(256)S(1)} %bitcast.374, bf16[256,1024]{1,0:T(8,128)(2,1)S(1)} %copy-done.11), kind=kCustom, calls=%fused_computation.22 | custom fusion | bytes 1574912 | tf_op jit(solution)/shard_map/scatter | solution.py:263
  657.7 36.2 %scatter_fusion.5 = bf16[32,80,1024]{2,1,0:T(8,128)(2,1)} fusion(bf16[32,80,1024]{2,1,0:T(8,128)(2,1)} %scatter_fusion.4, s32[256]{0:T(256)S(1)} %bitcast.373, bf16[256,1024]{1,0:T(8,128)(2,1)S(1)} %copy-done.10), kind=kCustom, calls=%fused_computation.23 | custom fusion | bytes 1574912 | tf_op jit(solution)/shard_map/scatter | solution.py:263
  693.9 36.1 %scatter_fusion.6 = bf16[32,80,1024]{2,1,0:T(8,128)(2,1)} fusion(bf16[32,80,1024]{2,1,0:T(8,128)(2,1)} %scatter_fusion.5, s32[256]{0:T(256)S(1)} %bitcast.372, bf16[256,1024]{1,0:T(8,128)(2,1)S(1)} %copy-done.9), kind=kCustom, calls=%fused_computation.24 | custom fusion | bytes 1574912 | tf_op jit(solution)/shard_map/scatter | solution.py:263
  730.1 36.1 %scatter_fusion.7 = bf16[32,80,1024]{2,1,0:T(8,128)(2,1)} fusion(bf16[32,80,1024]{2,1,0:T(8,128)(2,1)} %scatter_fusion.6, s32[256]{0:T(256)S(1)} %bitcast.371, bf16[256,1024]{1,0:T(8,128)(2,1)S(1)} %copy-done.8), kind=kCustom, calls=%fused_computation.25 | custom fusion | bytes 1574912 | tf_op jit(solution)/shard_map/scatter | solution.py:263
  766.2 5.1 all-to-all-start.2
  771.3 112.8 %all-to-all-done.2 = bf16[32,80,1024]{2,1,0:T(8,128)(2,1)} async-done(((bf16[32,80,1024]{2,1,0:T(8,128)(2,1)}), bf16[32,80,1024]{2,1,0:T(8,128)(2,1)}, u32[]{:S(2)}, u32[]{:S(2)}) %all-to-all-start.2) | async-done | bytes 5242912 | tf_op jit(solution)/shard_map/all_to_all | solution.py:266
  884.1 5.8 copy.278
  892.9 94.0 %while.12 = (s32[]{:T(128)}, bf16[8,1024,128]{2,1,0:T(8,128)(2,1)}, bf16[8,1024,128]{2,1,0:T(8,128)(2,1)}, bf16[8,128,1024]{2,1,0:T(8,128)(2,1)}, bf16[8,1,320,1...) while((s32[]{:T(128)}, bf16[8,1024,128]{2,1,0:T(8,128)(2,1)}, ...), condition=%wide.region_29.30_spmd, body=%wide.region_28.29_spmd.sunk | while | flops 504750080 | bytes 9410697 | solution.py:313
  986.9 5.4 copy.319
  992.3 117.9 %all_to_all.77 = bf16[8,320,1024]{2,0,1:T(8,128)(2,1)S(1)} all-to-all(bf16[8,320,1024]{2,0,1:T(8,128)(2,1)S(1)} %bitcast.369), channel_id=1, replica_groups=mesh['dp'=2,'expert'=4,'tensor'=4] {'expert'}, dimensions={1} | all-to-all | bytes 10485760 | tf_op jit(solution)/shard_map/all_to_all | solution.py:317
  1110.2 5.2 copy.280
  1122.2 4.2 gather_fusion.13
  1126.4 4.1 gather_fusion.12
  1130.5 4.4 gather_fusion.11
  1134.9 4.2 gather_fusion.10
  1139.1 4.2 gather_fusion.9
  1143.3 4.2 gather_fusion.8
  1151.2 13.9 %psum.72 = f32[32]{0:T(128)S(1)} all-reduce(f32[32]{0:T(128)S(1)} %convert_element_type.257), channel_id=1, replica_groups=mesh['dp'=2,'expert'=4,'tensor'=4] {'dp','expert'}, use_global_device_ids=true, to_apply=%region_15.16 | all-reduce | flops 32 | bytes 256 | tf_op jit(solution)/shard_map/psum | solution.py:203
  1165.5 53.2 %all-reduce.11.cloned.1.call-done = (f32[256,1024]{1,0:T(8,128)}, f32[256,1024]{1,0:T(8,128)}) async-done(((f32[256,1024]{1,0:T(8,128)}, f32[256,1024]{1,0:T(8,128)}), (f32[256,1024]{1,0:T(8,128)}, f32[256,1024]{1,0:T(8,128)})) %all-reduce.11.cloned.1.call-update) | async-done | bytes 2097168 | tf_op jit(solution)/shard_map/psum | solution.py:259
  1234.0 39.9 %all-reduce.9.cloned.1.call-done = bf16[256,1024]{1,0:T(8,128)(2,1)} async-done(((bf16[256,1024]{1,0:T(8,128)(2,1)}), bf16[256,1024]{1,0:T(8,128)(2,1)}) %all-reduce.9.cloned.1.call-update) | async-done | bytes 524304 | tf_op jit(solution)/shard_map/psum | solution.py:391
  1275.3 4.3 concatenate.95
  1279.6 4.6 all-to-all-start.4
  1285.7 35.5 %psum.73 = f32[32]{0:T(128)S(1)} all-reduce(f32[32]{0:T(128)S(1)} %get-tuple-element.306), channel_id=1, replica_groups=mesh['dp'=2,'expert'=4,'tensor'=4] {'dp','expert'}, use_global_device_ids=true, to_apply=%region_19.20 | all-reduce | flops 32 | bytes 256 | tf_op jit(solution)/shard_map/psum | solution.py:203
  1337.2 11.9 reduce-scatter.2.cloned.1.call-done
  (302 shorter events, 225.5 us)
Async XLA Ops:
  7.2 10.1 copy-start
  7.2 66.8 %all-reduce.7.cloned.1.call-start = ((), (), s32[]{:S(2)}) async-start(), calls=%async_computation.6 | async-start | bytes 2097152 | tf_op jit(solution)/shard_map/psum | solution.py:195
  7.3 9.3 copy-start.17
  9.2 5.1 copy-start.47
  9.4 4.9 copy-start.19
  9.4 4.9 copy-start.21
  10.9 5.7 copy-start.39
  14.2 4.4 copy-start.26
  20.7 53.3 %copy-start.3 = (bf16[256,1024]{1,0:T(8,128)(2,1)S(1)}, bf16[256,1024]{1,0:T(8,128)(2,1)}, u32[]{:S(2)}) copy-start(bf16[256,1024]{1,0:T(8,128)(2,1)} %param.17) | copy-start | bytes 1572868
  20.7 54.8 %copy-start.41 = (f32[1024]{0:T(1024)S(1)}, f32[1024]{0:T(1024)}, u32[]{:S(2)}) copy-start(f32[1024]{0:T(1024)} %param.24) | copy-start | bytes 12292
  20.7 54.9 %copy-start.27 = (bf16[1024,32]{0,1:T(8,128)(2,1)S(1)}, bf16[1024,32]{0,1:T(8,128)(2,1)}, u32[]{:S(2)}) copy-start(bf16[1024,32]{0,1:T(8,128)(2,1)} %param.25) | copy-start | bytes 196612
  75.9 17.0 %copy-start.51 = (s32[2]{0:T(128)S(1)}, s32[2]{0:T(128)}, u32[]{:S(2)}) copy-start(s32[2]{0:T(128)} %constant.155) | copy-start | bytes 28
  75.9 17.1 %copy-start.50 = (s32[2]{0:T(128)S(1)}, s32[2]{0:T(128)}, u32[]{:S(2)}) copy-start(s32[2]{0:T(128)} %constant.152) | copy-start | bytes 28
  106.3 121.4 %all-to-all-start = ((bf16[32,80,1024]{2,1,0:T(8,128)(2,1)}), bf16[32,80,1024]{2,1,0:T(8,128)(2,1)}, u32[]{:S(2)}, u32[]{:S(2)}) async-start(bf16[32,80,1024]{2,1,0:T(8,128)(2,1)} %bitcast.368), calls=%async_computation | async-start | bytes 10485760 | tf_op jit(solution)/shard_map/all_to_all | solution.py:214
  295.6 120.3 %all-to-all-start.1 = ((bf16[8,320,1024]{2,0,1:T(8,128)(2,1)}), bf16[8,320,1024]{2,0,1:T(8,128)(2,1)}, u32[]{:S(2)}, u32[]{:S(2)}) async-start(bf16[8,320,1024]{2,0,1:T(8,128)(2,1)} %bitcast.367), calls=%async_computation.1 | async-start | bytes 10485760 | tf_op jit(solution)/shard_map/all_to_all | solution.py:248
  448.1 8.3 copy-start.5
  473.4 3.0 copy-start.15
  476.5 36.2 %copy-start.14 = (bf16[256,1024]{1,0:T(8,128)(2,1)S(1)}, bf16[256,1024]{1,0:T(8,128)(2,1)}, u32[]{:S(2)}) copy-start(bf16[256,1024]{1,0:T(8,128)(2,1)} %get-tuple-element.387) | copy-start | bytes 1572868
  512.6 36.3 %copy-start.13 = (bf16[256,1024]{1,0:T(8,128)(2,1)S(1)}, bf16[256,1024]{1,0:T(8,128)(2,1)}, u32[]{:S(2)}) copy-start(bf16[256,1024]{1,0:T(8,128)(2,1)} %get-tuple-element.388) | copy-start | bytes 1572868
  549.0 36.4 %copy-start.12 = (bf16[256,1024]{1,0:T(8,128)(2,1)S(1)}, bf16[256,1024]{1,0:T(8,128)(2,1)}, u32[]{:S(2)}) copy-start(bf16[256,1024]{1,0:T(8,128)(2,1)} %get-tuple-element.389) | copy-start | bytes 1572868
  585.4 36.1 %copy-start.11 = (bf16[256,1024]{1,0:T(8,128)(2,1)S(1)}, bf16[256,1024]{1,0:T(8,128)(2,1)}, u32[]{:S(2)}) copy-start(bf16[256,1024]{1,0:T(8,128)(2,1)} %get-tuple-element.390) | copy-start | bytes 1572868
  621.6 36.2 %copy-start.10 = (bf16[256,1024]{1,0:T(8,128)(2,1)S(1)}, bf16[256,1024]{1,0:T(8,128)(2,1)}, u32[]{:S(2)}) copy-start(bf16[256,1024]{1,0:T(8,128)(2,1)} %get-tuple-element.391) | copy-start | bytes 1572868
  657.7 36.2 %copy-start.9 = (bf16[256,1024]{1,0:T(8,128)(2,1)S(1)}, bf16[256,1024]{1,0:T(8,128)(2,1)}, u32[]{:S(2)}) copy-start(bf16[256,1024]{1,0:T(8,128)(2,1)} %get-tuple-element.392) | copy-start | bytes 1572868
  693.9 36.2 %copy-start.8 = (bf16[256,1024]{1,0:T(8,128)(2,1)S(1)}, bf16[256,1024]{1,0:T(8,128)(2,1)}, u32[]{:S(2)}) copy-start(bf16[256,1024]{1,0:T(8,128)(2,1)} %get-tuple-element.386) | copy-start | bytes 1572868
  766.2 117.9 %all-to-all-start.2 = ((bf16[32,80,1024]{2,1,0:T(8,128)(2,1)}), bf16[32,80,1024]{2,1,0:T(8,128)(2,1)}, u32[]{:S(2)}, u32[]{:S(2)}) async-start(bf16[32,80,1024]{2,1,0:T(8,128)(2,1)} %scatter_fusion.7), calls=%async_computation.2 | async-start | bytes 10485760 | tf_op jit(solution)/shard_map/all_to_all | solution.py:266
  771.2 447.4 %all-reduce.11.cloned.1.call-start = ((), (), s32[]{:S(2)}) async-start(), calls=%async_computation.9 | async-start | bytes 4194304 | tf_op jit(solution)/shard_map/psum | solution.py:259
  1143.3 7.9 copy-start.52
  1143.3 21.9 %copy-start.44 = (f32[2,2,256]{2,1,0:T(2,128)S(1)}, f32[2,2,256]{2,1,0:T(2,128)}, u32[]{:S(2)}) copy-start(f32[2,2,256]{2,1,0:T(2,128)} %copy-done.43) | copy-start | bytes 12292
  1143.3 21.9 %copy-start.46 = (f32[2,2,256]{2,1,0:T(2,128)S(1)}, f32[2,2,256]{2,1,0:T(2,128)}, u32[]{:S(2)}) copy-start(f32[2,2,256]{2,1,0:T(2,128)} %copy-done.45) | copy-start | bytes 12292
  1151.2 72.3 %copy-start.18 = (pred[256,256]{0,1:T(8,128)(4,1)S(1)}, pred[256,256]{0,1:T(8,128)(4,1)}, u32[]{:S(2)}) copy-start(pred[256,256]{0,1:T(8,128)(4,1)} %copy-done.17) | copy-start | bytes 196612
  1151.2 122.7 %all-reduce.9.cloned.1.call-start = ((), (), s32[]{:S(2)}) async-start(), calls=%async_computation.7 | async-start | bytes 1048576 | tf_op jit(solution)/shard_map/psum | solution.py:391
  1218.7 6.4 copy-start.2
  1218.7 6.4 copy-start.40
  1223.1 2.7 copy-start.31
  1223.1 3.0 copy-start.36
  1223.1 3.0 copy-start.38
  1223.1 3.3 copy-start.20
  1223.1 3.3 copy-start.22
  1223.1 3.4 copy-start.32
  1223.5 3.3 copy-start.33
  1228.4 93.3 %all-reduce.13.cloned.1.call-start = ((), (), s32[]{:S(2)}) async-start(), calls=%async_computation.10 | async-start | bytes 12582912 | tf_op jit(solution)/shard_map/psum | solution.py:416
  1229.7 54.6 %copy-start.25 = (bf16[2,64,2,256]{3,1,2,0:T(8,128)(2,1)S(1)}, bf16[2,64,2,256]{3,1,2,0:T(8,128)(2,1)}, u32[]{:S(2)}) copy-start(bf16[2,64,2,256]{3,1,2,0:T(8,128)(2,1)} %copy-done.24) | copy-start | bytes 393220
  1279.6 52.2 %all-to-all-start.4 = ((bf16[8,128,546]{1,2,0:T(8,128)(2,1)}), bf16[8,128,546]{1,2,0:T(8,128)(2,1)}, u32[]{:S(2)}, u32[]{:S(2)}) async-start(bf16[8,128,546]{1,2,0:T(8,128)(2,1)} %concatenate.95), calls=%async_computation.4 | async-start | bytes 2260992 | tf_op jit(solution)/shard_map/all_to_all | solution.py:26
  1284.2 64.9 %reduce-scatter.2.cloned.1.call-start = ((), (), s32[]{:S(2)}) async-start(), calls=%async_computation.8 | async-start | bytes 1179648 | tf_op jit(solution)/shard_map/reduce_scatter | solution.py:412
  1321.7 4.0 copy-start.7
  1321.7 6.3 copy-start.6
  1325.8 4.8 copy-start.16
  1325.8 4.8 copy-start.49
  (14 other events, 21.3 us)
Sparse Core Ops, SparseCore 0:
  18.7 55.2 all-reduce.6
  1151.3 67.3 all-reduce.10
  1228.5 45.3 all-reduce.8
  1277.3 32.3 all-reduce.12
  1312.4 36.7 reduce-scatter.1
where the time goes:
time: 1380 us; the launch traced here: 1360 us
  waiting for transfers between devices  489 us (35%)
  local copies, waits for them, and re-layouts  457 us (33%)
  blocking collectives  176 us (13%)
  matrix products  163 us (12%)
  other arithmetic  34.4 us (2%)
  starting transfers between devices  20.3 us (1%)
  between operations  15.2 us (1%)
    scatter x8, local copies, waits for them, and re-layouts, on_device(): grad_buffer.at[routes[:, ranked], slot_index[:, ranked]]  290 us
    all_to_all x1, blocking collectives, on_device(): lax.all_to_all(grad_rows_in.reshape(local_count, row_count, model_width),...  118 us
    all_to_all x1, waiting for transfers between devices, on_device(): lax.all_to_all(buffer, 'expert', split_axis=0, concat_axis=1, tiled=True)  116 us
    all_to_all x1, waiting for transfers between devices, on_device(): lax.all_to_all(results.reshape(local_count, row_count, model_width), 'exp...  115 us
    all_to_all x1, waiting for transfers between devices, on_device(): lax.all_to_all(grad_buffer, 'expert', split_axis=0, concat_axis=1, tiled=...  113 us
    psum x1, waiting for transfers between devices, on_device(): lax.psum((mixture_part, jnp.stack(gate_dots, axis=1)), 'tensor')  53.2 us
    psum x2, blocking collectives, on_device(): lax.psum((jnp.sum(onehot, axis=0).astype(jnp.float32), jnp.sum(probs_all,...  49.5 us
    psum x1, waiting for transfers between devices, on_device(): lax.psum(grad_normed_one.astype(jnp.bfloat16), 'tensor').astype(jnp.float32)  39.9 us
  transfers between devices with their start and end apart: 9, of which 7 were waited for; matrix products, arithmetic and copies ran while one was open for 3% of the time, Pallas kernels for 0%

commit v1 on v0

v1 whole, which is shorter than its diff:
```python
import jax
import jax.numpy as jnp
from jax import lax
from jax.sharding import PartitionSpec as P

HD = 64
TOP = 8
EPS = 1e-06
ROPE_BASE = 10000.0
MASKED = -1e30
BF = jnp.bfloat16
F32 = jnp.float32
FEW = 8


def dot(a, b, dims):
    return lax.dot_general(a, b, (dims, ((), ())), preferred_element_type=F32)


def nn(a, b):
    return dot(a, b, ((1,), (0,)))


def nt(a, b):
    return dot(a, b, ((1,), (1,)))


def tn(a, b):
    return dot(a, b, ((0,), (0,)))


def swap(x, axis, distance):
    size = lax.axis_size(axis)
    return lax.ppermute(x, axis, [(i, i ^ distance) for i in range(size)])


def spread(x, axis):
    size = lax.axis_size(axis)
    if size <= FEW:
        return jnp.stack([swap(x, axis, r) for r in range(1, size)])
    whole = lax.all_gather(x, axis)
    return jnp.take(whole, jnp.arange(1, size) ^ lax.axis_index(axis), axis=0)


def deal(parts, axis):
    size = lax.axis_size(axis)
    if size <= FEW:
        return jnp.stack([swap(parts[r - 1], axis, r) for r in range(1, size)])
    order = jnp.arange(size) ^ lax.axis_index(axis)
    whole = jnp.concatenate([parts[:1], parts], axis=0)
    back = lax.all_to_all(jnp.take(whole, order, axis=0), axis, 0, 0, tiled=True)
    return jnp.take(back, order, axis=0)[1:]


def rope_tables(seq_len, head_dim):
    half_dim = head_dim // 2
    frequency = ROPE_BASE ** (-(jnp.arange(half_dim, dtype=F32) * 2.0) / head_dim)
    angles = jnp.arange(seq_len, dtype=F32)[:, None] * frequency[None, :]
    return (jnp.cos(angles)[:, None, :], jnp.sin(angles)[:, None, :])


def rotate(vectors, cosine, sine):
    half = vectors.shape[-1] // 2
    a, b = vectors[..., :half], vectors[..., half:]
    return jnp.concatenate([a * cosine - b * sine, b * cosine + a * sine], axis=-1)


def softmax_rows(scores):
    exponent = jnp.exp(scores - jnp.max(scores, axis=-1, keepdims=True))
    return exponent / jnp.sum(exponent, axis=-1, keepdims=True)


def on_device(
    tokens,
    routes,
    gain_first,
    w_query,
    w_key,
    w_value,
    w_output,
    gain_second,
    w_router,
    w_gate,
    w_up,
    w_down,
    cotangent,
):
    seq_len, width = tokens.shape
    experts = w_router.shape[1]
    local, _, hidden_dev = w_gate.shape
    heads_dev = w_query.shape[1] // HD
    kv_dev = w_key.shape[1] // HD
    groups = heads_dev // kv_dev
    scale = HD ** (-0.5)
    tensor_size = lax.axis_size("tensor")
    expert_size = lax.axis_size("expert")
    token_count = seq_len * lax.axis_size("dp") * expert_size
    quarter_len = seq_len // tensor_size
    last = tensor_size - 1
    t_me, e_me, d_me = lax.axis_index("tensor"), lax.axis_index("expert"), lax.axis_index("dp")

    def quarter(x, r):
        return lax.dynamic_slice_in_dim(x, (t_me ^ r) * quarter_len, quarter_len, 0)

    def natural(pieces):
        whole = jnp.zeros((seq_len, *pieces[0].shape[1:]), pieces[0].dtype)
        for r, piece in enumerate(pieces):
            whole = lax.dynamic_update_slice_in_dim(whole, piece, (t_me ^ r) * quarter_len, 0)
        return whole

    routes_own = jnp.concatenate([quarter(routes, r) for r in range(tensor_size)], axis=0)
    routes_all = jnp.concatenate([routes_own[None], spread(routes_own, "expert")], axis=0)
    cot_own = jnp.concatenate([quarter(cotangent, r) for r in range(tensor_size)], axis=0)
    cot_far = spread(quarter(cotangent, 0), "expert")
    cot_far = jnp.concatenate(
        [cot_far] + [swap(cot_far, "tensor", r) for r in range(1, tensor_size)], axis=1
    )
    cot_all = jnp.concatenate([cot_own[None], cot_far], axis=0).reshape(-1, width)
    down_flat = w_down.reshape(local * hidden_dev, width)
    cot_hidden = nt(cot_all, down_flat)

    cosine, sine = rope_tables(seq_len, HD)
    xf = tokens.astype(F32)
    inv_one = lax.rsqrt(jnp.mean(xf * xf, axis=-1, keepdims=True) + EPS)
    n_one = (xf * inv_one * gain_first).astype(BF)
    queries = rotate(nn(n_one, w_query).reshape(seq_len, heads_dev, HD), cosine, sine).astype(BF)
    queries = queries.reshape(seq_len, kv_dev, groups, HD)
    keys = rotate(nn(n_one, w_key).reshape(seq_len, kv_dev, HD), cosine, sine).astype(BF)
    values = nn(n_one, w_value).astype(BF).reshape(seq_len, kv_dev, HD)
    place = jnp.arange(seq_len)
    allowed = place[None, :] <= place[:, None]

    def scores_of():
        s = jnp.einsum("bkgd,tkd->kgbt", queries, keys, preferred_element_type=F32) * scale
        return jnp.where(allowed, s, MASKED)

    s = scores_of()
    peak = jnp.max(s, axis=-1, keepdims=True)
    e = jnp.exp(s - peak)
    total = jnp.sum(e, axis=-1, keepdims=True)
    lse = peak + jnp.log(total)
    o = jnp.einsum("kgbt,tkd->bkgd", (e / total).astype(BF), values, preferred_element_type=F32)
    o = o.reshape(seq_len, heads_dev * HD).astype(BF)
    attn_part = nn(o, w_output)
    attn = quarter(attn_part, 0)
    for r in range(1, tensor_size):
        attn = attn + swap(quarter(attn_part, r).astype(BF), "tensor", r).astype(F32)
    h = quarter(xf, 0) + attn
    inv_two = lax.rsqrt(jnp.mean(h * h, axis=-1, keepdims=True) + EPS)
    n_two = (h * inv_two * gain_second).astype(BF)

    own = [n_two] + [swap(n_two, "tensor", r) for r in range(1, tensor_size)]
    far_first = spread(own[0], "expert")
    far_last = spread(own[last], "expert")
    far = (
        [far_first]
        + [swap(far_first, "tensor", r) for r in range(1, last)]
        + [far_last]
    )
    n_all = jnp.concatenate(
        [jnp.concatenate(own, axis=0)[None], jnp.concatenate(far, axis=1)], axis=0
    ).reshape(-1, width)

    def route(rows, chosen_of):
        z = nn(rows, w_router)
        probs = softmax_rows(z)
        mask = jnp.any(
            chosen_of[:, :, None] == jnp.arange(experts, dtype=jnp.int32), axis=1
        )
        zc = jnp.where(mask, z, MASKED)
        ez = jnp.where(mask, jnp.exp(zc - jnp.max(zc, axis=-1, keepdims=True)), 0.0)
        return mask.astype(F32), probs, ez / jnp.sum(ez, axis=-1, keepdims=True)

    mask_all, _, gates_all = route(n_all, routes_all.reshape(-1, TOP))
    mask, probs, gates = route(n_two, quarter(routes, 0))
    counts = jnp.sum(mask_all, axis=0)
    counts = counts + swap(counts, "dp", 1)
    fraction = counts / (token_count * TOP)
    balance = experts * fraction / token_count
    prob_sums = lax.psum(jnp.sum(probs, axis=0), ("dp", "expert", "tensor"))
    loss_value = experts * balance * prob_sums

    local_gates = lax.dynamic_slice_in_dim(gates_all, e_me * local, local, 1)
    g = jnp.repeat(local_gates, hidden_dev, axis=1)
    gate_flat = jnp.moveaxis(w_gate, 1, 0).reshape(width, local * hidden_dev)
    up_flat = jnp.moveaxis(w_up, 1, 0).reshape(width, local * hidden_dev)
    gate_val = nn(n_all, gate_flat)
    up_val = nn(n_all, up_flat)
    sig = jax.nn.sigmoid(gate_val)
    act = gate_val * sig
    hid = act * up_val
    hid_g = (g * hid).astype(BF)
    dgates = jnp.sum((hid * cot_hidden).reshape(-1, local, hidden_dev), axis=-1)
    dgates_wide = lax.dynamic_update_slice_in_dim(
        jnp.zeros((dgates.shape[0], 128), F32), dgates, e_me * local, 1
    )
    dhid = g * cot_hidden
    d_gate = (dhid * up_val * sig * (1.0 + gate_val * (1.0 - sig))).astype(BF)
    d_up = (dhid * act).astype(BF)
    dn_part = nt(d_gate, gate_flat) + nt(d_up, up_flat)
    dn_part = jnp.concatenate([dn_part, dgates_wide], axis=1)
    dn_part = dn_part.reshape(expert_size, tensor_size, quarter_len, width + 128)
    moe_part = nn(hid_g, down_flat).reshape(expert_size, tensor_size, quarter_len, width)

    dn_sent = dn_part.astype(BF)
    near = dn_part[0, 0]
    from_last = deal(dn_sent[1:, last], "expert").astype(F32)
    first_sum = dn_part[1:, 0]
    for r in range(1, last):
        first_sum = first_sum + swap(dn_sent[1:, r], "tensor", r).astype(F32)
        near = near + swap(dn_sent[0, r], "tensor", r).astype(F32)
    through = dn_part[0, last] + jnp.sum(from_last, axis=0)
    near = near + swap(through.astype(BF), "tensor", last).astype(F32)
    near = near + jnp.sum(deal(first_sum.astype(BF), "expert").astype(F32), axis=0)
    dn_two, dgates_sum = near[:, :width], near[:, width : width + experts]

    moe_sent = moe_part.astype(BF)
    moe = moe_part[:, 0]
    for r in range(1, tensor_size):
        moe = moe + swap(moe_sent[:, r], "tensor", r).astype(F32)
    moe_sum = moe[0] + jnp.sum(deal(moe[1:].astype(BF), "expert").astype(F32), axis=0)
    out_piece = (h + moe_sum).astype(BF)
    output = natural([out_piece] + [swap(out_piece, "tensor", r) for r in range(1, tensor_size)])

    rows = (-1, local, hidden_dev)
    grad_gate = jnp.einsum("td,tef->edf", n_all, d_gate.reshape(rows), preferred_element_type=F32)
    grad_up = jnp.einsum("td,tef->edf", n_all, d_up.reshape(rows), preferred_element_type=F32)
    grad_down = jnp.einsum("tef,td->efd", hid_g.reshape(rows), cot_all, preferred_element_type=F32)
    expert_grads = []
    for grad in (grad_gate, grad_up, grad_down):
        sent = grad.astype(BF)
        expert_grads.append(sent.astype(F32) + swap(sent, "dp", 1).astype(F32))

    d_chosen = gates * (dgates_sum - jnp.sum(gates * dgates_sum, axis=1, keepdims=True))
    dz = probs * (balance - jnp.sum(probs * balance, axis=1, keepdims=True)) + d_chosen
    dz = dz.astype(BF)
    dn_two = dn_two + nt(dz, w_router)
    u_two = gain_second * dn_two
    gain_two_part = jnp.sum(dn_two * h * inv_two, axis=0)
    dh = (
        quarter(cotangent, 0).astype(F32)
        + inv_two * u_two
        - h * inv_two**3 * jnp.mean(u_two * h, axis=-1, keepdims=True)
    )
    da = dh.astype(BF)
    wide = jnp.concatenate([da, dz, jnp.zeros((quarter_len, 128 - experts), BF)], axis=1)
    wide = natural([wide] + [swap(wide, "tensor", r) for r in range(1, tensor_size)])
    da_all, dz_all = wide[:, :width], wide[:, width : width + experts]
    n_two_all = natural(own)
    grad_router = tn(n_two_all, dz_all)

    grad_wo = tn(da_all, o)
    do = nt(da_all, w_output).astype(BF).reshape(seq_len, kv_dev, groups, HD)
    p = jnp.exp(scores_of() - lse)
    dp = jnp.einsum("bkgd,tkd->kgbt", do, values, preferred_element_type=F32)
    ds = (p * (dp - jnp.sum(p * dp, axis=-1, keepdims=True))).astype(BF)
    dv = jnp.einsum("kgbt,bkgd->tkd", p.astype(BF), do, preferred_element_type=F32)
    dq = jnp.einsum("kgbt,tkd->bkgd", ds, keys, preferred_element_type=F32) * scale
    dk = jnp.einsum("kgbt,bkgd->tkd", ds, queries, preferred_element_type=F32) * scale
    dq = rotate(dq.reshape(seq_len, heads_dev, HD), cosine, -sine).reshape(seq_len, -1)
    dk = rotate(dk, cosine, -sine).reshape(seq_len, -1)
    dqkv = jnp.concatenate([dq, dk, dv.reshape(seq_len, -1)], axis=1).astype(BF)
    w_qkv = jnp.concatenate([w_query, w_key, w_value], axis=1)
    dn_one_part = nt(dqkv, w_qkv)
    gain_one_part = jnp.sum(dn_one_part * xf * inv_one, axis=0)
    dense = jnp.concatenate([tn(n_one, dqkv), grad_wo, grad_router], axis=1).astype(BF)
    dn_one = quarter(dn_one_part, 0)
    for r in range(1, tensor_size):
        dn_one = dn_one + swap(quarter(dn_one_part, r).astype(BF), "tensor", r).astype(F32)
    u_one = gain_first * dn_one
    xq, invq = quarter(xf, 0), quarter(inv_one, 0)
    ig = dh + invq * u_one - xq * invq**3 * jnp.mean(u_one * xq, axis=-1, keepdims=True)
    ig = ig.astype(BF)
    ig = natural([ig] + [swap(ig, "tensor", r) for r in range(1, tensor_size)])
    input_grad = ig.astype(F32)

    chunk = width // (lax.axis_size("dp") * expert_size)
    half = dense.shape[0] // 2
    kept = lax.dynamic_slice_in_dim(dense, d_me * half, half, 0)
    sent = lax.dynamic_slice_in_dim(dense, (1 - d_me) * half, half, 0)
    summed = kept.astype(F32) + swap(sent, "dp", 1).astype(F32)
    blocks = summed.reshape(expert_size, chunk, -1)
    blocks = jnp.take(blocks, jnp.arange(expert_size) ^ e_me, axis=0)
    dense_sum = blocks[0] + jnp.sum(deal(blocks[1:].astype(BF), "expert").astype(F32), axis=0)
    nq, nk = w_query.shape[1], w_key.shape[1]
    at = [nq, nq + nk, nq + 2 * nk, 2 * nq + 2 * nk]
    g_query, g_key, g_value, g_out, g_router = jnp.split(dense_sum, at, axis=1)

    gains = jnp.stack([gain_one_part, gain_two_part])
    gains = lax.psum_scatter(
        lax.psum(gains, "tensor"), ("dp", "expert"), scatter_dimension=1, tiled=True
    )
    return (
        output,
        loss_value,
        input_grad,
        gains[0],
        g_query,
        g_key,
        g_value,
        g_out.T,
        gains[1],
        g_router,
        expert_grads[0],
        expert_grads[1],
        expert_grads[2],
    )


def solution(mesh):
    rows = ("dp", "expert")
    placed = (
        P(rows, None),
        P(rows, None),
        P(),
        P(None, "tensor"),
        P(None, "tensor"),
        P(None, "tensor"),
        P("tensor", None),
        P(),
        P(),
        P("expert", None, "tensor"),
        P("expert", None, "tensor"),
        P("expert", "tensor", None),
        P(rows, None),
    )
    return jax.shard_map(
        on_device,
        mesh=mesh,
        in_specs=placed,
        out_specs=(
            P(rows, None),
            P(),
            P(rows, None),
            P(rows),
            P(rows, "tensor"),
            P(rows, "tensor"),
            P(rows, "tensor"),
            P("tensor", rows),
            P(rows),
            P(rows, None),
            P("expert", None, "tensor"),
            P("expert", None, "tensor"),
            P("expert", "tensor", None),
        ),
        check_vma=False,
    )
```

time: 1380 us -> 422 us (0.31); the launches traced: 1360 us -> 418 us
  local copies, waits for them, and re-layouts: 457 us -> 68.3 us
  waiting for transfers between devices: 489 us -> 108 us
  blocking collectives: 176 us -> 52.6 us
  matrix products: 163 us -> 45.4 us
  starting transfers between devices: 20.3 us -> 66.2 us
  other arithmetic: 34.4 us -> 62 us
    all_to_all x4 -> x0, waiting for transfers between devices: 344 us -> none  [the longest x1 116 us: on_device(): lax.all_to_all(buffer, 'expert', split_axis=0, concat_axis=1, tiled=True)]
    scatter x8 -> x0, local copies, waits for them, and re-layouts: 290 us -> none  [on_device(): grad_buffer.at[routes[:, ranked], slot_index[:, ranked]]]
    psum x4 -> x0, waiting for transfers between devices: 133 us -> none  [the longest x1 53.2 us: on_device(): lax.psum((mixture_part, jnp.stack(gate_dots, axis=1)), 'tensor')]
    dot_general x93 -> x27, matrix products: 163 us -> 45.4 us  [the longest x18 28.5 us: dot(): return lax.dot_general(a, b, (dims, ((), ())), preferred_element_type=F32)]
    all_to_all x1 -> x0, blocking collectives: 118 us -> none  [on_device(): lax.all_to_all(grad_rows_in.reshape(local_count, row_count, model_width),...]
    gather x24 -> x1, local copies, waits for them, and re-layouts: 95.7 us -> 3.37 us  [on_device(): blocks = jnp.take(blocks, jnp.arange(expert_size) ^ e_me, axis=0)]
    ppermute x0 -> x60, waiting for transfers between devices: none -> 80.7 us  [swap(): return lax.ppermute(x, axis, [(i, i ^ distance) for i in range(size)])]
    ppermute x0 -> x60, starting transfers between devices: none -> 66.2 us  [swap(): return lax.ppermute(x, axis, [(i, i ^ distance) for i in range(size)])]
  transfers between devices with their start and end apart: 9 -> 61, of which waited for: 7 -> 18; matrix products, arithmetic and copies ran while one was open for 3% -> 31% of each run, Pallas kernels for 0% -> 0%
where the time goes in v1:
time: 422 us; the launch traced here: 418 us
  waiting for transfers between devices  108 us (26%)
  local copies, waits for them, and re-layouts  68.3 us (16%)
  starting transfers between devices  66.2 us (16%)
  other arithmetic  62 us (15%)
  blocking collectives  52.6 us (12%)
  matrix products  45.4 us (11%)
  between operations  15.5 us (4%)
    ppermute x60, waiting for transfers between devices, swap(): return lax.ppermute(x, axis, [(i, i ^ distance) for i in range(size)])  80.7 us
    ppermute x60, starting transfers between devices, swap(): return lax.ppermute(x, axis, [(i, i ^ distance) for i in range(size)])  66.2 us
    psum x1, blocking collectives, on_device(): prob_sums = lax.psum(jnp.sum(probs, axis=0), ('dp', 'expert', 'tensor'))  42.6 us
    unnamed x157, local copies, waits for them, and re-layouts  29.5 us
    dot_general x18, matrix products, dot(): return lax.dot_general(a, b, (dims, ((), ())), preferred_element_type=F32)  28.5 us
    unnamed x2, waiting for transfers between devices  27 us
    add x3, other arithmetic, on_device(): expert_grads.append(sent.astype(F32) + swap(sent, 'dp', 1).astype(F32))  15.5 us
    psum x1, blocking collectives, on_device(): lax.psum(gains, 'tensor')  10.1 us
  transfers between devices with their start and end apart: 61, of which 18 were waited for; matrix products, arithmetic and copies ran while one was open for 31% of the time, Pallas kernels for 0%

profile of v1, /device:TPU:0, one launch (start us, length us, event | category | flops | bytes accessed | tf_op | source)
XLA Modules:
  0.0 417.8 jit_solution(17140586662573295887)
XLA Ops:
  8.9 5.0 %collective-permute-start.5 = (s32[256,8]{0,1:T(8,128)}, s32[256,8]{0,1:T(8,128)}, u32[]{:S(2)}, u32[]{:S(2)}) collective-permute-start(s32[256,8]{0,1:T(8,128)} %pad_add_fusion.1), channel_id=1, source_target_pairs={{0,12},{4,8},{8,4},{12,0},{1,13},{5,9},{9,5},{13,1},{2,14},{6,10},... | collective-permute-start | bytes 24584 | tf_op jit(solution)/shard_map/ppermute | solution.py:34
  14.6 1.8 constant_dynamic-slice_fusion.3
  16.4 3.8 collective-permute-start.29
  32.4 2.1 convert_element_type.193
  34.7 4.4 %copy.95 = bf16[8,1024,128]{1,2,0:T(8,128)(2,1)} copy(bf16[8,1024,128]{2,1,0:T(8,128)(2,1)} %param.22) | data formatting | bytes 4194304 | tf_op args[9]
  39.1 3.9 copy.96
  74.3 12.0 %collective-permute-done.7 = bf16[64,1024]{1,0:T(8,128)(2,1)S(1)} collective-permute-done((bf16[64,1024]{1,0:T(8,128)(2,1)}, bf16[64,1024]{1,0:T(8,128)(2,1)S(1)}, u32[]{:S(2)}, u32[]{:S(2)}) %collective-permute-start.7) | collective-permute-done | bytes 131104 | tf_op jit(solution)/shard_map/ppermute | solution.py:34
  92.2 2.4 collective-permute-start.14
  96.0 2.6 collective-permute-done.16
  98.5 4.2 collective-permute-done.15
  106.3 2.4 fusion.71
  108.7 2.4 fusion.70
  111.7 5.4 %multiply_convert_fusion = (bf16[1024,1024]{0,1:T(8,128)(2,1)S(1)}, bf16[1024,1024]{0,1:T(8,128)(2,1)S(1)}, bf16[1024,1024]{0,1:T(8,128)(2,1)}, f32[1024,1024]{0,1:T(8,128)S(1)}) fusion(f32[1024,8]{0,1:T(8,128)S(1)} %dynamic-slice_divide_fusion, f32[1024,1024]{0,1:T(8,128)S(1)} %fusion.70, f32[1024,1024]{0,1:T(8,128)S(1)} %fusion.71, ...), kind=kOutput, calls=%fused_computation.10 | convolution fusion | flops 2165309440 | bytes 23101440 | tf_op jit(solution)/shard_map/dot_general | solution.py:17
  118.9 2.5 fusion.72
  121.4 2.5 convolution_add_fusion
  124.0 2.6 pad_maximum_fusion
  126.6 6.1 %copy.101 = f32[1024,1152]{1,0:T(8,128)} copy(f32[1024,1152]{0,1:T(8,128)} %pad_maximum_fusion) | data formatting | bytes 9437184 | tf_op jit(solution)/shard_map/concatenate | solution.py:201
  132.7 2.4 slice_bitcast_fusion.21
  135.0 2.5 slice_bitcast_fusion.6
  137.5 5.4 %convert_bitcast_fusion.1 = bf16[8,1024,128]{1,2,0:T(8,128)(2,1)} fusion(bf16[1024,8,128]{0,2,1:T(8,128)(2,1)} %bitcast.284, bf16[1024,1024,1]{1,0,2:T(8,128)(2,1)S(1)} %bitcast.272), kind=kOutput, calls=%fused_computation.19 | convolution fusion | flops 2148532224 | bytes 6291456 | tf_op jit(solution)/shard_map/td,tef->edf/dot_general | solution.py:226
  142.9 3.7 convert_bitcast_fusion
  148.0 2.6 collective-permute-start.37
  151.9 4.1 copy.97
  156.0 6.1 %convolution_convert_fusion = bf16[8,128,1024]{2,1,0:T(8,128)(2,1)} fusion(bf16[1024,8,128]{0,2,1:T(8,128)(2,1)} %bitcast.276, bf16[1024,1024,1]{1,0,2:T(8,128)(2,1)} %bitcast.275), kind=kOutput, calls=%fused_computation.21 | convolution fusion | flops 2148532224 | bytes 6291456 | tf_op jit(solution)/shard_map/tef,td->efd/dot_general | solution.py:228
  162.1 2.3 fusion.67
  167.7 7.1 %collective-permute-done.36 = bf16[64,1152]{1,0:T(8,128)(2,1)S(1)} collective-permute-done((bf16[64,1152]{1,0:T(8,128)(2,1)S(1)}, bf16[64,1152]{1,0:T(8,128)(2,1)S(1)}, u32[]{:S(2)}, u32[]{:S(2)}) %collective-permute-start.36) | collective-permute-done | bytes 147488 | tf_op jit(solution)/shard_map/ppermute | solution.py:34
  181.9 7.8 %collective-permute-done.17 = bf16[4,64,1024]{2,1,0:T(8,128)(2,1)S(1)} collective-permute-done((bf16[4,64,1024]{2,1,0:T(8,128)(2,1)S(1)}, bf16[4,64,1024]{2,1,0:T(8,128)(2,1)S(1)}, u32[]{:S(2)}, u32[]{:S(2)}) %collective-permute-start.17) | collective-permute-done | bytes 524320 | tf_op jit(solution)/shard_map/ppermute | solution.py:34
  190.2 11.1 %collective-permute-done.19 = bf16[4,64,1024]{2,1,0:T(8,128)(2,1)S(1)} collective-permute-done((bf16[4,64,1024]{2,1,0:T(8,128)(2,1)S(1)}, bf16[4,64,1024]{2,1,0:T(8,128)(2,1)S(1)}, u32[]{:S(2)}, u32[]{:S(2)}) %collective-permute-start.19) | collective-permute-done | bytes 524320 | tf_op jit(solution)/shard_map/ppermute | solution.py:34
  203.0 3.6 collective-permute-done.18
  210.1 5.1 %collective-permute-done.43 = bf16[64,1152]{1,0:T(8,128)(2,1)S(1)} collective-permute-done((bf16[64,1152]{1,0:T(8,128)(2,1)S(1)}, bf16[64,1152]{1,0:T(8,128)(2,1)S(1)}, u32[]{:S(2)}, u32[]{:S(2)}) %collective-permute-start.43) | collective-permute-done | bytes 147488 | tf_op jit(solution)/shard_map/ppermute | solution.py:34
  215.2 3.4 collective-permute-start.20
  218.6 1.8 collective-permute-done.42
  228.8 42.6 %psum.14 = f32[32]{0:T(128)} all-reduce(f32[32]{0:T(128)} %get-tuple-element.68), channel_id=1, replica_groups=mesh['dp'=2,'expert'=4,'tensor'=4] {'dp','expert','tensor'}, use_global_device_ids=true, to_apply=%region_12.13 | all-reduce | flops 32 | bytes 256 | tf_op jit(solution)/shard_map/psum | solution.py:180
  272.7 2.3 collective-permute-start.44
  291.6 1.8 collective-permute-start.48
  298.2 27.0 %reduce-scatter.4.cloned.1.call-done = f32[128,2]{1,0:T(8,128)} async-done(((f32[1024,2]{1,0:T(8,128)}), f32[128,2]{1,0:T(8,128)}) %reduce-scatter.4.cloned.1.call-update) | async-done | bytes 1040
  326.1 10.1 %psum.16 = f32[2,128]{1,0:T(2,128)S(1)} all-reduce(f32[2,128]{1,0:T(2,128)S(1)} %copy.129), channel_id=1, replica_groups=mesh['dp'=2,'expert'=4,'tensor'=4] {'tensor'}, use_global_device_ids=true, to_apply=%region_26.27 | all-reduce | flops 256 | bytes 2048 | tf_op jit(solution)/shard_map/psum | solution.py:291
  342.3 1.9 constant_dynamic-update-slice_fusion.7
  345.6 2.4 collective-permute-start.50
  349.3 3.4 gather_fusion
  356.8 4.8 %collective-permute-done.52 = bf16[64,1024]{1,0:T(8,128)(2,1)S(1)} collective-permute-done((bf16[64,1024]{1,0:T(8,128)(2,1)}, bf16[64,1024]{1,0:T(8,128)(2,1)S(1)}, u32[]{:S(2)}, u32[]{:S(2)}) %collective-permute-start.52) | collective-permute-done | bytes 131104 | tf_op jit(solution)/shard_map/ppermute | solution.py:34
  364.7 6.8 %collective-permute-done.56 = bf16[128,800]{0,1:T(8,128)(2,1)S(1)} collective-permute-done((bf16[128,800]{0,1:T(8,128)(2,1)S(1)}, bf16[128,800]{0,1:T(8,128)(2,1)S(1)}, u32[]{:S(2)}, u32[]{:S(2)}) %collective-permute-start.56) | collective-permute-done | bytes 204832 | tf_op jit(solution)/shard_map/ppermute | solution.py:34
  371.5 9.4 %collective-permute-done.55 = bf16[128,800]{0,1:T(8,128)(2,1)S(1)} collective-permute-done((bf16[128,800]{0,1:T(8,128)(2,1)S(1)}, bf16[128,800]{0,1:T(8,128)(2,1)S(1)}, u32[]{:S(2)}, u32[]{:S(2)}) %collective-permute-start.55) | collective-permute-done | bytes 204832 | tf_op jit(solution)/shard_map/ppermute | solution.py:34
  384.6 5.2 %convert_add_fusion.1 = f32[8,1024,128]{1,2,0:T(8,128)} fusion(bf16[8,1024,128]{1,2,0:T(8,128)(2,1)} %collective-permute-done.58, bf16[8,1024,128]{1,2,0:T(8,128)(2,1)} %convert_bitcast_fusion), kind=kLoop, calls=%fused_computation.8 | loop fusion | flops 3145728 | bytes 8388608 | tf_op jit(solution)/shard_map/add | solution.py:232
  389.7 5.3 %copy.117 = f32[8,1024,128]{2,1,0:T(8,128)} copy(f32[8,1024,128]{1,2,0:T(8,128)} %convert_add_fusion.1) | data formatting | bytes 8388608
  395.0 5.2 %convert_add_fusion.2 = f32[8,1024,128]{1,2,0:T(8,128)} fusion(bf16[8,1024,128]{1,2,0:T(8,128)(2,1)} %collective-permute-done.57, bf16[8,1024,128]{1,2,0:T(8,128)(2,1)} %convert_bitcast_fusion.1), kind=kLoop, calls=%fused_computation.9 | loop fusion | flops 3145728 | bytes 8388608 | tf_op jit(solution)/shard_map/add | solution.py:232
  400.2 5.3 %copy.116 = f32[8,1024,128]{2,1,0:T(8,128)} copy(f32[8,1024,128]{1,2,0:T(8,128)} %convert_add_fusion.2) | data formatting | bytes 8388608
  405.5 5.2 %convert_add_fusion = f32[8,128,1024]{2,1,0:T(8,128)} fusion(bf16[8,128,1024]{2,1,0:T(8,128)(2,1)} %collective-permute-done.59, bf16[8,128,1024]{2,1,0:T(8,128)(2,1)} %convolution_convert_fusion), kind=kLoop, calls=%fused_computation.7 | loop fusion | flops 3145728 | bytes 8388608 | tf_op jit(solution)/shard_map/add | solution.py:232
  (368 shorter events, 128.7 us)
Async XLA Ops:
  7.2 318.0 %reduce-scatter.4.cloned.1.call-start = ((), (), s32[]{:S(2)}) async-start(), calls=%async_computation.1 | async-start | bytes 589824
  8.9 34.1 %collective-permute-start.5 = (s32[256,8]{0,1:T(8,128)}, s32[256,8]{0,1:T(8,128)}, u32[]{:S(2)}, u32[]{:S(2)}) collective-permute-start(s32[256,8]{0,1:T(8,128)} %pad_add_fusion.1), channel_id=1, source_target_pairs={{0,12},{4,8},{8,4},{12,0},{1,13},{5,9},{9,5},{13,1},{2,14},{6,10},... | collective-permute-start | bytes 24584 | tf_op jit(solution)/shard_map/ppermute | solution.py:34
  14.0 30.6 %collective-permute-start.4 = (s32[256,8]{0,1:T(8,128)}, s32[256,8]{0,1:T(8,128)}, u32[]{:S(2)}, u32[]{:S(2)}) collective-permute-start(s32[256,8]{0,1:T(8,128)} %pad_add_fusion.1), channel_id=1, source_target_pairs={{0,8},{4,12},{8,0},{12,4},{1,9},{5,13},{9,1},{13,5},{2,10},{6,14},... | collective-permute-start | bytes 24584 | tf_op jit(solution)/shard_map/ppermute | solution.py:34
  14.0 32.1 %collective-permute-start.3 = (s32[256,8]{0,1:T(8,128)}, s32[256,8]{0,1:T(8,128)}, u32[]{:S(2)}, u32[]{:S(2)}) collective-permute-start(s32[256,8]{0,1:T(8,128)} %pad_add_fusion.1), channel_id=1, source_target_pairs={{0,4},{4,0},{8,12},{12,8},{1,5},{5,1},{9,13},{13,9},{2,6},{6,2},{1... | collective-permute-start | bytes 24584 | tf_op jit(solution)/shard_map/ppermute | solution.py:34
  16.4 42.3 %collective-permute-start.29 = (bf16[64,1024]{1,0:T(8,128)(2,1)S(1)}, bf16[64,1024]{1,0:T(8,128)(2,1)}, u32[]{:S(2)}, u32[]{:S(2)}) collective-permute-start(bf16[64,1024]{1,0:T(8,128)(2,1)S(1)} %get-tuple-element.113), channel_id=1, source_target_pairs={{0,12},{4,8},{8,4},{12,0},{1,13},{5,9},{9,5},{13,1},{2,14},{6,10},... | collective-permute-start | bytes 393224 | tf_op jit(solution)/shard_map/ppermute | solution.py:34
  20.2 40.0 %collective-permute-start.28 = (bf16[64,1024]{1,0:T(8,128)(2,1)S(1)}, bf16[64,1024]{1,0:T(8,128)(2,1)}, u32[]{:S(2)}, u32[]{:S(2)}) collective-permute-start(bf16[64,1024]{1,0:T(8,128)(2,1)S(1)} %get-tuple-element.113), channel_id=1, source_target_pairs={{0,8},{4,12},{8,0},{12,4},{1,9},{5,13},{9,1},{13,5},{2,10},{6,14},... | collective-permute-start | bytes 393224 | tf_op jit(solution)/shard_map/ppermute | solution.py:34
  49.6 12.2 %collective-permute-start.27 = (bf16[64,1024]{1,0:T(8,128)(2,1)S(1)}, bf16[64,1024]{1,0:T(8,128)(2,1)S(1)}, u32[]{:S(2)}, u32[]{:S(2)}) collective-permute-start(bf16[64,1024]{1,0:T(8,128)(2,1)S(1)} %get-tuple-element.113), channel_id=1, source_target_pairs={{0,4},{4,0},{8,12},{12,8},{1,5},{5,1},{9,13},{13,9},{2,6},{6,2},{1... | collective-permute-start | bytes 393224 | tf_op jit(solution)/shard_map/ppermute | solution.py:34
  55.8 11.1 %collective-permute-start.11 = (bf16[64,1024]{1,0:T(8,128)(2,1)}, bf16[64,1024]{1,0:T(8,128)(2,1)}, u32[]{:S(2)}, u32[]{:S(2)}) collective-permute-start(bf16[64,1024]{1,0:T(8,128)(2,1)} %get-tuple-element.74), channel_id=1, source_target_pairs={{0,12},{4,8},{8,4},{12,0},{1,13},{5,9},{9,5},{13,1},{2,14},{6,10},... | collective-permute-start | bytes 393224 | tf_op jit(solution)/shard_map/ppermute | solution.py:34
  57.3 10.8 %collective-permute-start.10 = (bf16[64,1024]{1,0:T(8,128)(2,1)}, bf16[64,1024]{1,0:T(8,128)(2,1)}, u32[]{:S(2)}, u32[]{:S(2)}) collective-permute-start(bf16[64,1024]{1,0:T(8,128)(2,1)} %get-tuple-element.74), channel_id=1, source_target_pairs={{0,8},{4,12},{8,0},{12,4},{1,9},{5,13},{9,1},{13,5},{2,10},{6,14},... | collective-permute-start | bytes 393224 | tf_op jit(solution)/shard_map/ppermute | solution.py:34
  58.7 10.9 %collective-permute-start.9 = (bf16[64,1024]{1,0:T(8,128)(2,1)}, bf16[64,1024]{1,0:T(8,128)(2,1)}, u32[]{:S(2)}, u32[]{:S(2)}) collective-permute-start(bf16[64,1024]{1,0:T(8,128)(2,1)} %get-tuple-element.74), channel_id=1, source_target_pairs={{0,4},{4,0},{8,12},{12,8},{1,5},{5,1},{9,13},{13,9},{2,6},{6,2},{1... | collective-permute-start | bytes 393224 | tf_op jit(solution)/shard_map/ppermute | solution.py:34
  60.2 11.0 %collective-permute-start.6 = (bf16[64,1024]{1,0:T(8,128)(2,1)}, bf16[64,1024]{1,0:T(8,128)(2,1)}, u32[]{:S(2)}, u32[]{:S(2)}) collective-permute-start(bf16[64,1024]{1,0:T(8,128)(2,1)} %get-tuple-element.74), channel_id=1, source_target_pairs={{0,1},{1,0},{2,3},{3,2},{4,5},{5,4},{6,7},{7,6},{8,9},{9,8},{10,11... | collective-permute-start | bytes 393224 | tf_op jit(solution)/shard_map/ppermute | solution.py:34
  63.6 26.7 %collective-permute-start.32 = (bf16[3,64,1024]{2,1,0:T(8,128)(2,1)}, bf16[3,64,1024]{2,1,0:T(8,128)(2,1)}, u32[]{:S(2)}, u32[]{:S(2)}) collective-permute-start(bf16[3,64,1024]{2,1,0:T(8,128)(2,1)} %pad_maximum_fusion.3), channel_id=1, source_target_pairs={{0,3},{1,2},{2,1},{3,0},{4,7},{5,6},{6,5},{7,4},{8,11},{9,10},{10,... | collective-permute-start | bytes 1179656 | tf_op jit(solution)/shard_map/ppermute | solution.py:34
  67.0 24.8 %collective-permute-start.31 = (bf16[3,64,1024]{2,1,0:T(8,128)(2,1)}, bf16[3,64,1024]{2,1,0:T(8,128)(2,1)S(1)}, u32[]{:S(2)}, u32[]{:S(2)}) collective-permute-start(bf16[3,64,1024]{2,1,0:T(8,128)(2,1)} %pad_maximum_fusion.3), channel_id=1, source_target_pairs={{0,2},{1,3},{2,0},{3,1},{4,6},{5,7},{6,4},{7,5},{8,10},{9,11},{10,... | collective-permute-start | bytes 1179656 | tf_op jit(solution)/shard_map/ppermute | solution.py:34
  68.1 24.1 %collective-permute-start.30 = (bf16[3,64,1024]{2,1,0:T(8,128)(2,1)}, bf16[3,64,1024]{2,1,0:T(8,128)(2,1)S(1)}, u32[]{:S(2)}, u32[]{:S(2)}) collective-permute-start(bf16[3,64,1024]{2,1,0:T(8,128)(2,1)} %pad_maximum_fusion.3), channel_id=1, source_target_pairs={{0,1},{1,0},{2,3},{3,2},{4,5},{5,4},{6,7},{7,6},{8,9},{9,8},{10,11... | collective-permute-start | bytes 1179656 | tf_op jit(solution)/shard_map/ppermute | solution.py:34
  69.6 16.7 %collective-permute-start.7 = (bf16[64,1024]{1,0:T(8,128)(2,1)}, bf16[64,1024]{1,0:T(8,128)(2,1)S(1)}, u32[]{:S(2)}, u32[]{:S(2)}) collective-permute-start(bf16[64,1024]{1,0:T(8,128)(2,1)} %get-tuple-element.74), channel_id=1, source_target_pairs={{0,2},{1,3},{2,0},{3,1},{4,6},{5,7},{6,4},{7,5},{8,10},{9,11},{10,... | collective-permute-start | bytes 393224 | tf_op jit(solution)/shard_map/ppermute | solution.py:34
  71.3 16.4 %collective-permute-start.8 = (bf16[64,1024]{1,0:T(8,128)(2,1)}, bf16[64,1024]{1,0:T(8,128)(2,1)S(1)}, u32[]{:S(2)}, u32[]{:S(2)}) collective-permute-start(bf16[64,1024]{1,0:T(8,128)(2,1)} %get-tuple-element.74), channel_id=1, source_target_pairs={{0,3},{1,2},{2,1},{3,0},{4,7},{5,6},{6,5},{7,4},{8,11},{9,10},{10,... | collective-permute-start | bytes 393224 | tf_op jit(solution)/shard_map/ppermute | solution.py:34
  86.3 16.4 %collective-permute-start.13 = (bf16[3,64,1024]{2,1,0:T(8,128)(2,1)S(1)}, bf16[3,64,1024]{2,1,0:T(8,128)(2,1)S(1)}, u32[]{:S(2)}, u32[]{:S(2)}) collective-permute-start(bf16[3,64,1024]{2,1,0:T(8,128)(2,1)S(1)} %pad_maximum_fusion.2), channel_id=1, source_target_pairs={{0,2},{1,3},{2,0},{3,1},{4,6},{5,7},{6,4},{7,5},{8,10},{9,11},{10,... | collective-permute-start | bytes 1179656 | tf_op jit(solution)/shard_map/ppermute | solution.py:34
  87.7 15.0 %collective-permute-start.12 = (bf16[3,64,1024]{2,1,0:T(8,128)(2,1)S(1)}, bf16[3,64,1024]{2,1,0:T(8,128)(2,1)S(1)}, u32[]{:S(2)}, u32[]{:S(2)}) collective-permute-start(bf16[3,64,1024]{2,1,0:T(8,128)(2,1)S(1)} %pad_maximum_fusion.2), channel_id=1, source_target_pairs={{0,1},{1,0},{2,3},{3,2},{4,5},{5,4},{6,7},{7,6},{8,9},{9,8},{10,11... | collective-permute-start | bytes 1179656 | tf_op jit(solution)/shard_map/ppermute | solution.py:34
  91.8 10.9 %collective-permute-start.15 = (bf16[64,1024]{1,0:T(8,128)(2,1)S(1)}, bf16[64,1024]{1,0:T(8,128)(2,1)S(1)}, u32[]{:S(2)}, u32[]{:S(2)}) collective-permute-start(bf16[64,1024]{1,0:T(8,128)(2,1)S(1)} %collective-permute-done.8), channel_id=1, source_target_pairs={{0,8},{4,12},{8,0},{12,4},{1,9},{5,13},{9,1},{13,5},{2,10},{6,14},... | collective-permute-start | bytes 393224 | tf_op jit(solution)/shard_map/ppermute | solution.py:34
  92.2 10.4 %collective-permute-start.14 = (bf16[64,1024]{1,0:T(8,128)(2,1)S(1)}, bf16[64,1024]{1,0:T(8,128)(2,1)S(1)}, u32[]{:S(2)}, u32[]{:S(2)}) collective-permute-start(bf16[64,1024]{1,0:T(8,128)(2,1)S(1)} %collective-permute-done.8), channel_id=1, source_target_pairs={{0,4},{4,0},{8,12},{12,8},{1,5},{5,1},{9,13},{13,9},{2,6},{6,2},{1... | collective-permute-start | bytes 393224 | tf_op jit(solution)/shard_map/ppermute | solution.py:34
  137.5 27.1 %collective-permute-start.26 = (f32[32]{0:T(128)S(1)}, f32[32]{0:T(128)S(1)}, u32[]{:S(2)}, u32[]{:S(2)}) collective-permute-start(f32[32]{0:T(128)S(1)} %copy-done.65), channel_id=1, source_target_pairs={{0,16},{16,0},{1,17},{17,1},{2,18},{18,2},{3,19},{19,3},{4,20},{20... | collective-permute-start | bytes 392 | tf_op jit(solution)/shard_map/ppermute | solution.py:34
  146.6 74.5 %collective-permute-start.33 = (bf16[64,1152]{1,0:T(8,128)(2,1)}, bf16[64,1152]{1,0:T(8,128)(2,1)}, u32[]{:S(2)}, u32[]{:S(2)}) collective-permute-start(bf16[64,1152]{1,0:T(8,128)(2,1)} %get-tuple-element.93), channel_id=1, source_target_pairs={{0,1},{1,0},{2,3},{3,2},{4,5},{5,4},{6,7},{7,6},{8,9},{9,8},{10,11... | collective-permute-start | bytes 442376 | tf_op jit(solution)/shard_map/ppermute | solution.py:34
  148.0 18.3 %collective-permute-start.35 = (bf16[64,1152]{1,0:T(8,128)(2,1)}, bf16[64,1152]{1,0:T(8,128)(2,1)}, u32[]{:S(2)}, u32[]{:S(2)}) collective-permute-start(bf16[64,1152]{1,0:T(8,128)(2,1)} %get-tuple-element.94), channel_id=1, source_target_pairs={{0,4},{4,0},{8,12},{12,8},{1,5},{5,1},{9,13},{13,9},{2,6},{6,2},{1... | collective-permute-start | bytes 442376 | tf_op jit(solution)/shard_map/ppermute | solution.py:34
  148.0 19.1 %collective-permute-start.37 = (bf16[64,1152]{1,0:T(8,128)(2,1)}, bf16[64,1152]{1,0:T(8,128)(2,1)}, u32[]{:S(2)}, u32[]{:S(2)}) collective-permute-start(bf16[64,1152]{1,0:T(8,128)(2,1)} %get-tuple-element.95), channel_id=1, source_target_pairs={{0,12},{4,8},{8,4},{12,0},{1,13},{5,9},{9,5},{13,1},{2,14},{6,10},... | collective-permute-start | bytes 442376 | tf_op jit(solution)/shard_map/ppermute | solution.py:34
  150.7 70.6 %collective-permute-start.34 = (bf16[64,1152]{1,0:T(8,128)(2,1)}, bf16[64,1152]{1,0:T(8,128)(2,1)}, u32[]{:S(2)}, u32[]{:S(2)}) collective-permute-start(bf16[64,1152]{1,0:T(8,128)(2,1)} %get-tuple-element.96), channel_id=1, source_target_pairs={{0,2},{1,3},{2,0},{3,1},{4,6},{5,7},{6,4},{7,5},{8,10},{9,11},{10,... | collective-permute-start | bytes 442376 | tf_op jit(solution)/shard_map/ppermute | solution.py:34
  166.3 11.6 %collective-permute-start.39 = (bf16[3,64,1152]{2,1,0:T(8,128)(2,1)S(1)}, bf16[3,64,1152]{2,1,0:T(8,128)(2,1)S(1)}, u32[]{:S(2)}, u32[]{:S(2)}) collective-permute-start(bf16[3,64,1152]{2,1,0:T(8,128)(2,1)S(1)} %copy-done.36), channel_id=1, source_target_pairs={{0,1},{1,0},{2,3},{3,2},{4,5},{5,4},{6,7},{7,6},{8,9},{9,8},{10,11... | collective-permute-start | bytes 1327112 | tf_op jit(solution)/shard_map/ppermute | solution.py:34
  167.1 12.2 %collective-permute-start.40 = (bf16[3,64,1152]{2,1,0:T(8,128)(2,1)S(1)}, bf16[3,64,1152]{2,1,0:T(8,128)(2,1)S(1)}, u32[]{:S(2)}, u32[]{:S(2)}) collective-permute-start(bf16[3,64,1152]{2,1,0:T(8,128)(2,1)S(1)} %copy-done.35), channel_id=1, source_target_pairs={{0,2},{1,3},{2,0},{3,1},{4,6},{5,7},{6,4},{7,5},{8,10},{9,11},{10,... | collective-permute-start | bytes 1327112 | tf_op jit(solution)/shard_map/ppermute | solution.py:34
  174.8 14.8 %collective-permute-start.17 = (bf16[4,64,1024]{2,1,0:T(8,128)(2,1)S(1)}, bf16[4,64,1024]{2,1,0:T(8,128)(2,1)S(1)}, u32[]{:S(2)}, u32[]{:S(2)}) collective-permute-start(bf16[4,64,1024]{2,1,0:T(8,128)(2,1)S(1)} %get-tuple-element.100), channel_id=1, source_target_pairs={{0,1},{1,0},{2,3},{3,2},{4,5},{5,4},{6,7},{7,6},{8,9},{9,8},{10,11... | collective-permute-start | bytes 1572872 | tf_op jit(solution)/shard_map/ppermute | solution.py:34
  177.8 23.4 %collective-permute-start.19 = (bf16[4,64,1024]{2,1,0:T(8,128)(2,1)S(1)}, bf16[4,64,1024]{2,1,0:T(8,128)(2,1)S(1)}, u32[]{:S(2)}, u32[]{:S(2)}) collective-permute-start(bf16[4,64,1024]{2,1,0:T(8,128)(2,1)S(1)} %get-tuple-element.101), channel_id=1, source_target_pairs={{0,3},{1,2},{2,1},{3,0},{4,7},{5,6},{6,5},{7,4},{8,11},{9,10},{10,... | collective-permute-start | bytes 1572872 | tf_op jit(solution)/shard_map/ppermute | solution.py:34
  179.3 27.4 %collective-permute-start.18 = (bf16[4,64,1024]{2,1,0:T(8,128)(2,1)S(1)}, bf16[4,64,1024]{2,1,0:T(8,128)(2,1)S(1)}, u32[]{:S(2)}, u32[]{:S(2)}) collective-permute-start(bf16[4,64,1024]{2,1,0:T(8,128)(2,1)S(1)} %get-tuple-element.102), channel_id=1, source_target_pairs={{0,2},{1,3},{2,0},{3,1},{4,6},{5,7},{6,4},{7,5},{8,10},{9,11},{10,... | collective-permute-start | bytes 1572872 | tf_op jit(solution)/shard_map/ppermute | solution.py:34
  189.7 31.5 %collective-permute-start.38 = (bf16[64,1152]{1,0:T(8,128)(2,1)S(1)}, bf16[64,1152]{1,0:T(8,128)(2,1)S(1)}, u32[]{:S(2)}, u32[]{:S(2)}) collective-permute-start(bf16[64,1152]{1,0:T(8,128)(2,1)S(1)} %fusion.30), channel_id=1, source_target_pairs={{0,3},{1,2},{2,1},{3,0},{4,7},{5,6},{6,5},{7,4},{8,11},{9,10},{10,... | collective-permute-start | bytes 442376 | tf_op jit(solution)/shard_map/ppermute | solution.py:34
  209.2 11.2 %collective-permute-start.42 = (bf16[64,1152]{1,0:T(8,128)(2,1)S(1)}, bf16[64,1152]{1,0:T(8,128)(2,1)S(1)}, u32[]{:S(2)}, u32[]{:S(2)}) collective-permute-start(bf16[64,1152]{1,0:T(8,128)(2,1)S(1)} %get-tuple-element.121), channel_id=1, source_target_pairs={{0,8},{4,12},{8,0},{12,4},{1,9},{5,13},{9,1},{13,5},{2,10},{6,14},... | collective-permute-start | bytes 442376 | tf_op jit(solution)/shard_map/ppermute | solution.py:34
  215.2 57.5 %collective-permute-start.20 = (bf16[64,1024]{1,0:T(8,128)(2,1)}, bf16[64,1024]{1,0:T(8,128)(2,1)}, u32[]{:S(2)}, u32[]{:S(2)}) collective-permute-start(bf16[64,1024]{1,0:T(8,128)(2,1)} %get-tuple-element.116), channel_id=1, source_target_pairs={{0,4},{4,0},{8,12},{12,8},{1,5},{5,1},{9,13},{13,9},{2,6},{6,2},{1... | collective-permute-start | bytes 393224 | tf_op jit(solution)/shard_map/ppermute | solution.py:34
  220.4 54.6 %collective-permute-start.22 = (bf16[64,1024]{1,0:T(8,128)(2,1)}, bf16[64,1024]{1,0:T(8,128)(2,1)}, u32[]{:S(2)}, u32[]{:S(2)}) collective-permute-start(bf16[64,1024]{1,0:T(8,128)(2,1)} %get-tuple-element.117), channel_id=1, source_target_pairs={{0,12},{4,8},{8,4},{12,0},{1,13},{5,9},{9,5},{13,1},{2,14},{6,10},... | collective-permute-start | bytes 393224 | tf_op jit(solution)/shard_map/ppermute | solution.py:34
  221.1 53.9 %collective-permute-start.21 = (bf16[64,1024]{1,0:T(8,128)(2,1)}, bf16[64,1024]{1,0:T(8,128)(2,1)}, u32[]{:S(2)}, u32[]{:S(2)}) collective-permute-start(bf16[64,1024]{1,0:T(8,128)(2,1)} %get-tuple-element.118), channel_id=1, source_target_pairs={{0,8},{4,12},{8,0},{12,4},{1,9},{5,13},{9,1},{13,5},{2,10},{6,14},... | collective-permute-start | bytes 393224 | tf_op jit(solution)/shard_map/ppermute | solution.py:34
  226.7 54.4 %collective-permute-start.46 = (bf16[64,1152]{1,0:T(8,128)(2,1)S(1)}, bf16[64,1152]{1,0:T(8,128)(2,1)}, u32[]{:S(2)}, u32[]{:S(2)}) collective-permute-start(bf16[64,1152]{1,0:T(8,128)(2,1)S(1)} %concatenate.75), channel_id=1, source_target_pairs={{0,3},{1,2},{2,1},{3,0},{4,7},{5,6},{6,5},{7,4},{8,11},{9,10},{10,... | collective-permute-start | bytes 442376 | tf_op jit(solution)/shard_map/ppermute | solution.py:34
  228.2 52.0 %collective-permute-start.45 = (bf16[64,1152]{1,0:T(8,128)(2,1)S(1)}, bf16[64,1152]{1,0:T(8,128)(2,1)}, u32[]{:S(2)}, u32[]{:S(2)}) collective-permute-start(bf16[64,1152]{1,0:T(8,128)(2,1)S(1)} %concatenate.75), channel_id=1, source_target_pairs={{0,2},{1,3},{2,0},{3,1},{4,6},{5,7},{6,4},{7,5},{8,10},{9,11},{10,... | collective-permute-start | bytes 442376 | tf_op jit(solution)/shard_map/ppermute | solution.py:34
  277.9 60.4 %collective-permute-start.24 = (bf16[64,1024]{1,0:T(8,128)(2,1)}, bf16[64,1024]{1,0:T(8,128)(2,1)}, u32[]{:S(2)}, u32[]{:S(2)}) collective-permute-start(bf16[64,1024]{1,0:T(8,128)(2,1)} %get-tuple-element.83), channel_id=1, source_target_pairs={{0,2},{1,3},{2,0},{3,1},{4,6},{5,7},{6,4},{7,5},{8,10},{9,11},{10,... | collective-permute-start | bytes 393224 | tf_op jit(solution)/shard_map/ppermute | solution.py:34
  278.6 58.1 %collective-permute-start.23 = (bf16[64,1024]{1,0:T(8,128)(2,1)}, bf16[64,1024]{1,0:T(8,128)(2,1)}, u32[]{:S(2)}, u32[]{:S(2)}) collective-permute-start(bf16[64,1024]{1,0:T(8,128)(2,1)} %get-tuple-element.83), channel_id=1, source_target_pairs={{0,1},{1,0},{2,3},{3,2},{4,5},{5,4},{6,7},{7,6},{8,9},{9,8},{10,11... | collective-permute-start | bytes 393224 | tf_op jit(solution)/shard_map/ppermute | solution.py:34
  289.9 50.4 %collective-permute-start.47 = (bf16[64,1024]{1,0:T(8,128)(2,1)}, bf16[64,1024]{1,0:T(8,128)(2,1)S(1)}, u32[]{:S(2)}, u32[]{:S(2)}) collective-permute-start(bf16[64,1024]{1,0:T(8,128)(2,1)} %get-tuple-element.103), channel_id=1, source_target_pairs={{0,1},{1,0},{2,3},{3,2},{4,5},{5,4},{6,7},{7,6},{8,9},{9,8},{10,11... | collective-permute-start | bytes 393224 | tf_op jit(solution)/shard_map/ppermute | solution.py:34
  290.4 50.0 %collective-permute-start.49 = (bf16[64,1024]{1,0:T(8,128)(2,1)}, bf16[64,1024]{1,0:T(8,128)(2,1)}, u32[]{:S(2)}, u32[]{:S(2)}) collective-permute-start(bf16[64,1024]{1,0:T(8,128)(2,1)} %get-tuple-element.104), channel_id=1, source_target_pairs={{0,3},{1,2},{2,1},{3,0},{4,7},{5,6},{6,5},{7,4},{8,11},{9,10},{10,... | collective-permute-start | bytes 393224 | tf_op jit(solution)/shard_map/ppermute | solution.py:34
  291.6 49.3 %collective-permute-start.48 = (bf16[64,1024]{1,0:T(8,128)(2,1)}, bf16[64,1024]{1,0:T(8,128)(2,1)}, u32[]{:S(2)}, u32[]{:S(2)}) collective-permute-start(bf16[64,1024]{1,0:T(8,128)(2,1)} %get-tuple-element.105), channel_id=1, source_target_pairs={{0,2},{1,3},{2,0},{3,1},{4,6},{5,7},{6,4},{7,5},{8,10},{9,11},{10,... | collective-permute-start | bytes 393224 | tf_op jit(solution)/shard_map/ppermute | solution.py:34
  338.3 46.3 %collective-permute-start.58 = (bf16[8,1024,128]{1,2,0:T(8,128)(2,1)}, bf16[8,1024,128]{1,2,0:T(8,128)(2,1)}, u32[]{:S(2)}, u32[]{:S(2)}) collective-permute-start(bf16[8,1024,128]{1,2,0:T(8,128)(2,1)} %convert_bitcast_fusion), channel_id=1, source_target_pairs={{0,16},{16,0},{1,17},{17,1},{2,18},{18,2},{3,19},{19,3},{4,20},{20... | collective-permute-start | bytes 6291464 | tf_op jit(solution)/shard_map/ppermute | solution.py:34
  340.4 54.7 %collective-permute-start.57 = (bf16[8,1024,128]{1,2,0:T(8,128)(2,1)}, bf16[8,1024,128]{1,2,0:T(8,128)(2,1)}, u32[]{:S(2)}, u32[]{:S(2)}) collective-permute-start(bf16[8,1024,128]{1,2,0:T(8,128)(2,1)} %convert_bitcast_fusion.1), channel_id=1, source_target_pairs={{0,16},{16,0},{1,17},{17,1},{2,18},{18,2},{3,19},{19,3},{4,20},{20... | collective-permute-start | bytes 6291464 | tf_op jit(solution)/shard_map/ppermute | solution.py:34
  340.4 14.1 %collective-permute-start.25 = (bf16[64,1024]{1,0:T(8,128)(2,1)}, bf16[64,1024]{1,0:T(8,128)(2,1)}, u32[]{:S(2)}, u32[]{:S(2)}) collective-permute-start(bf16[64,1024]{1,0:T(8,128)(2,1)} %get-tuple-element.83), channel_id=1, source_target_pairs={{0,3},{1,2},{2,1},{3,0},{4,7},{5,6},{6,5},{7,4},{8,11},{9,10},{10,... | collective-permute-start | bytes 393224 | tf_op jit(solution)/shard_map/ppermute | solution.py:34
  354.5 51.0 %collective-permute-start.59 = (bf16[8,128,1024]{2,1,0:T(8,128)(2,1)}, bf16[8,128,1024]{2,1,0:T(8,128)(2,1)}, u32[]{:S(2)}, u32[]{:S(2)}) collective-permute-start(bf16[8,128,1024]{2,1,0:T(8,128)(2,1)} %convolution_convert_fusion), channel_id=1, source_target_pairs={{0,16},{16,0},{1,17},{17,1},{2,18},{18,2},{3,19},{19,3},{4,20},{20... | collective-permute-start | bytes 6291464 | tf_op jit(solution)/shard_map/ppermute | solution.py:34
  361.6 9.8 %collective-permute-start.56 = (bf16[128,800]{0,1:T(8,128)(2,1)S(1)}, bf16[128,800]{0,1:T(8,128)(2,1)S(1)}, u32[]{:S(2)}, u32[]{:S(2)}) collective-permute-start(bf16[128,800]{0,1:T(8,128)(2,1)S(1)} %get-tuple-element.110), channel_id=1, source_target_pairs={{0,12},{4,8},{8,4},{12,0},{1,13},{5,9},{9,5},{13,1},{2,14},{6,10},... | collective-permute-start | bytes 614408 | tf_op jit(solution)/shard_map/ppermute | solution.py:34
  362.7 18.2 %collective-permute-start.55 = (bf16[128,800]{0,1:T(8,128)(2,1)S(1)}, bf16[128,800]{0,1:T(8,128)(2,1)S(1)}, u32[]{:S(2)}, u32[]{:S(2)}) collective-permute-start(bf16[128,800]{0,1:T(8,128)(2,1)S(1)} %get-tuple-element.111), channel_id=1, source_target_pairs={{0,8},{4,12},{8,0},{12,4},{1,9},{5,13},{9,1},{13,5},{2,10},{6,14},... | collective-permute-start | bytes 614408 | tf_op jit(solution)/shard_map/ppermute | solution.py:34
  (87 other events, 793.2 us)
Sparse Core Ops, SparseCore 0:
  294.6 30.5 reduce-scatter.3

commit v2 on v1

v2 whole, which is shorter than its diff:
```python
import functools

import jax
import jax.numpy as jnp
import numpy as np
from jax import lax
from jax.experimental import pallas as pl
from jax.experimental.pallas import tpu as pltpu
from jax.sharding import PartitionSpec as P

HD = 64
TOP = 8
EPS = 1e-06
ROPE_BASE = 10000.0
MASKED = -1e30
BF = jnp.bfloat16
F32 = jnp.float32
FEW = 8
LANES = 128
MIB = 1 << 20


def dot(a, b, dims):
    return lax.dot_general(a, b, (dims, ((), ())), preferred_element_type=F32)


def nn(a, b):
    return dot(a, b, ((1,), (0,)))


def nt(a, b):
    return dot(a, b, ((1,), (1,)))


def tn(a, b):
    return dot(a, b, ((0,), (0,)))


def swap(x, axis, distance):
    size = lax.axis_size(axis)
    return lax.ppermute(x, axis, [(i, i ^ distance) for i in range(size)])


def spread(x, axis):
    size = lax.axis_size(axis)
    if size <= FEW:
        return jnp.stack([swap(x, axis, r) for r in range(1, size)])
    whole = lax.all_gather(x, axis)
    return jnp.take(whole, jnp.arange(1, size) ^ lax.axis_index(axis), axis=0)


def deal(parts, axis):
    size = lax.axis_size(axis)
    if size <= FEW:
        return jnp.stack([swap(parts[r - 1], axis, r) for r in range(1, size)])
    order = jnp.arange(size) ^ lax.axis_index(axis)
    whole = jnp.concatenate([parts[:1], parts], axis=0)
    back = lax.all_to_all(jnp.take(whole, order, axis=0), axis, 0, 0, tiled=True)
    return jnp.take(back, order, axis=0)[1:]


def rope_tables(seq_len):
    half = HD // 2
    frequency = ROPE_BASE ** (-(np.arange(half, dtype=np.float32) * 2.0) / HD)
    angles = np.arange(seq_len, dtype=np.float32)[:, None] * frequency[None, :].astype(np.float32)
    cosine, sine = np.cos(angles), np.sin(angles)
    heads = LANES // HD
    return (
        np.tile(cosine, (1, 2 * heads)).astype(np.float32),
        np.tile(np.concatenate([-sine, sine], axis=1), (1, heads)).astype(np.float32),
    )


def lane_of(shape):
    return lax.broadcasted_iota(jnp.int32, shape, 1)


def halves_swapped(x):
    first = lane_of(x.shape) % HD < HD // 2
    half = HD // 2
    return jnp.where(first, pltpu.roll(x, LANES - half, 1), pltpu.roll(x, half, 1))


def low_high(x, head):
    other = pltpu.roll(x.astype(F32), HD, 1).astype(x.dtype)
    low = lane_of(x.shape) < HD
    zero = jnp.zeros_like(x)
    at_low, at_high = (x, other) if head == 0 else (other, x)
    return jnp.where(low, at_low, zero), jnp.where(low, zero, at_high)


def causal(scores):
    rows = lax.broadcasted_iota(jnp.int32, scores.shape, 0)
    return lane_of(scores.shape) <= rows


def vmem():
    return pl.BlockSpec(memory_space=pltpu.VMEM)


def smem():
    return pl.BlockSpec(memory_space=pltpu.SMEM)


def shape(dims, kind):
    return jax.ShapeDtypeStruct(dims, kind)


def call(kernel, out_shape, operands, scalars=0, scratch=(), limit=40, flops=0, moved=0, name=None):
    return pl.pallas_call(
        kernel,
        out_shape=out_shape,
        in_specs=[smem()] * scalars + [vmem()] * (len(operands) - scalars),
        out_specs=jax.tree.map(lambda _: vmem(), out_shape),
        scratch_shapes=list(scratch),
        compiler_params=pltpu.CompilerParams(vmem_limit_bytes=limit * MIB),
        cost_estimate=pl.CostEstimate(flops=flops, bytes_accessed=moved, transcendentals=0),
        name=name,
    )(*operands)


def attend_kernel(me_ref, x_ref, gain_ref, wq_ref, wk_ref, wv_ref, wo_ref, cos_ref, sin_ref, *refs):
    n_ref, q_ref, k_ref, v_ref, o_ref, lse_ref = refs[:6]
    parts, whole = refs[6:-1], refs[-1]
    x = x_ref[...].astype(F32)
    inv = lax.rsqrt(jnp.mean(x * x, axis=-1, keepdims=True) + EPS)
    n = (x * inv * gain_ref[...]).astype(BF)
    n_ref[...] = n
    cosine, sine = cos_ref[...], sin_ref[...]
    q, k = nn(n, wq_ref[...]), nn(n, wk_ref[...])
    v_ref[...] = nn(n, wv_ref[...]).astype(BF)
    for at in range(0, q.shape[1], LANES):
        tile = q[:, at : at + LANES]
        q_ref[:, at : at + LANES] = (tile * cosine + halves_swapped(tile) * sine).astype(BF)
    for at in range(0, k.shape[1], LANES):
        tile = k[:, at : at + LANES]
        k_ref[:, at : at + LANES] = (tile * cosine + halves_swapped(tile) * sine).astype(BF)
    lse_all = jnp.zeros(lse_ref.shape, F32)
    for head in range(q.shape[1] // LANES):
        at = head // 2 * LANES
        keys = low_high(k_ref[:, at : at + LANES], head % 2)
        values = low_high(v_ref[:, at : at + LANES], head % 2)
        pair = q_ref[:, head * LANES : (head + 1) * LANES]
        mixed = 0.0
        for g in range(2):
            s = nt(pair, keys[g]) * HD ** (-0.5)
            s = jnp.where(causal(s), s, MASKED)
            peak = jnp.max(s, axis=-1, keepdims=True)
            e = jnp.exp(s - peak)
            total = jnp.sum(e, axis=-1, keepdims=True)
            mixed = mixed + nn((e / total).astype(BF), values[g])
            lse = peak + jnp.log(total)
            lse_all = jnp.where(lane_of(lse_all.shape) == 2 * head + g, lse, lse_all)
        o_ref[:, head * LANES : (head + 1) * LANES] = mixed.astype(BF)
    lse_ref[...] = lse_all
    whole[...] = nn(o_ref[...], wo_ref[...])
    for r, part in enumerate(parts):
        rows = part.shape[0]
        start = pl.multiple_of((me_ref[0] ^ r) * rows, rows)
        part[...] = whole[pl.ds(start, rows), :].astype(part.dtype)


def norm_two_kernel(me_ref, x_ref, gain_ref, own_ref, *refs):
    others, (h_ref, n_ref) = refs[:-2], refs[-2:]
    rows = h_ref.shape[0]
    start = pl.multiple_of(me_ref[0] * rows, rows)
    attn = own_ref[...]
    for other in others:
        attn = attn + other[...].astype(F32)
    h = x_ref[pl.ds(start, rows), :].astype(F32) + attn
    inv = lax.rsqrt(jnp.mean(h * h, axis=-1, keepdims=True) + EPS)
    h_ref[...] = h
    n_ref[...] = (h * inv * gain_ref[...]).astype(BF)


def router_of(rows, router_ref, routes, experts):
    z = nn(rows, router_ref[...])
    lane = lane_of(z.shape)
    z = jnp.where(lane < experts, z, MASKED)
    e = jnp.exp(z - jnp.max(z, axis=-1, keepdims=True))
    probs = e / jnp.sum(e, axis=-1, keepdims=True)
    chosen = lane == routes[:, 0:1]
    for k in range(1, routes.shape[1]):
        chosen = chosen | (lane == routes[:, k : k + 1])
    zc = jnp.where(chosen, z, MASKED)
    ec = jnp.where(chosen, jnp.exp(zc - jnp.max(zc, axis=-1, keepdims=True)), 0.0)
    return probs, ec / jnp.sum(ec, axis=-1, keepdims=True)


def hidden_cot_kernel(c0, c1, c2, c3, wd_ref, cot_ref, v_ref):
    rows = jnp.concatenate([c[0] for c in (c0, c1, c2, c3)], axis=0)
    cot_ref[0] = rows
    v_ref[0] = nt(rows, wd_ref[...])


def hidden_cot(pieces, down_flat):
    count, rows, width = pieces[0].shape
    out = down_flat.shape[0]
    piece = pl.BlockSpec((1, rows, width), lambda s: (s, 0, 0))
    return pl.pallas_call(
        hidden_cot_kernel,
        grid=(count,),
        in_specs=[piece] * 4 + [pl.BlockSpec((out, width), lambda s: (0, 0))],
        out_specs=[
            pl.BlockSpec((1, 4 * rows, width), lambda s: (s, 0, 0)),
            pl.BlockSpec((1, 4 * rows, out), lambda s: (s, 0, 0)),
        ],
        out_shape=[shape((count, 4 * rows, width), BF), shape((count, 4 * rows, out), F32)],
        compiler_params=pltpu.CompilerParams(vmem_limit_bytes=40 * MIB),
        cost_estimate=pl.CostEstimate(
            flops=2 * count * 4 * rows * width * out, bytes_accessed=0, transcendentals=0
        ),
        name="hidden_cot",
    )(*pieces, down_flat)


def experts_kernel(experts, base_ref, x0, x1, x2, x3, routes_ref, router_ref, wg_ref, wu_ref, v_ref, *refs):
    n_ref, dgu_ref, hg_ref, d0, d1, d2, d3, wcat = refs
    local, width, hidden = wg_ref.shape
    pair = 2 * hidden

    @pl.when(pl.program_id(0) == 0)
    def _():
        for e in range(local):
            wcat[:, e * pair : e * pair + hidden] = wg_ref[e]
            wcat[:, e * pair + hidden : (e + 1) * pair] = wu_ref[e]

    x = jnp.concatenate([piece[0] for piece in (x0, x1, x2, x3)], axis=0)
    n_ref[0] = x
    _, gates = router_of(x, router_ref, routes_ref[0], experts)
    lane = lane_of(gates.shape)
    dots = jnp.zeros(gates.shape, F32)
    for e in range(local):
        mine = lane == base_ref[0] + e
        g = jnp.sum(jnp.where(mine, gates, 0.0), axis=-1, keepdims=True)
        both = nn(x, wcat[:, e * pair : (e + 1) * pair])
        gate, up = both[:, :hidden], both[:, hidden:]
        v = v_ref[0, :, e * hidden : (e + 1) * hidden]
        sig = 1.0 / (1.0 + jnp.exp(-gate))
        act = gate * sig
        hid = act * up
        dots = jnp.where(mine, jnp.sum(hid * v, axis=-1, keepdims=True), dots)
        gv = g * v
        hg_ref[0, :, e * hidden : (e + 1) * hidden] = (g * hid).astype(BF)
        d_gate = gv * up * sig * (1.0 + gate * (1.0 - sig))
        dgu_ref[0, :, e * pair : e * pair + hidden] = d_gate.astype(BF)
        dgu_ref[0, :, e * pair + hidden : (e + 1) * pair] = (gv * act).astype(BF)
    rows = d0.shape[1]
    for r, d in enumerate((d0, d1, d2, d3)):
        d[0, :, width:] = dots[r * rows : (r + 1) * rows].astype(d.dtype)
    step = 256
    for at in range(0, width, step):
        dx = nt(dgu_ref[0], wcat[at : at + step, :])
        for r, d in enumerate((d0, d1, d2, d3)):
            d[0, :, at : at + step] = dx[r * rows : (r + 1) * rows].astype(d.dtype)


def run_experts(experts, base, pieces, routes, router, w_gate, w_up, v, kinds):
    count, rows, width = pieces[0].shape
    local, _, hidden = w_gate.shape
    per = lambda *dims: pl.BlockSpec((1, *dims), lambda s: (s, 0, 0))
    fixed = lambda dims: pl.BlockSpec(dims, lambda s: (0,) * len(dims))
    seq = 4 * rows
    return pl.pallas_call(
        functools.partial(experts_kernel, experts),
        grid=(count,),
        in_specs=[smem()]
        + [per(rows, width)] * 4
        + [per(seq, routes.shape[2]), fixed(router.shape), fixed(w_gate.shape), fixed(w_up.shape)]
        + [per(seq, local * hidden)],
        out_specs=[per(seq, width), per(seq, 2 * local * hidden), per(seq, local * hidden)]
        + [per(rows, width + LANES)] * 4,
        out_shape=[
            shape((count, seq, width), BF),
            shape((count, seq, 2 * local * hidden), BF),
            shape((count, seq, local * hidden), BF),
        ]
        + [shape((count, rows, width + LANES), kind) for kind in kinds],
        scratch_shapes=[pltpu.VMEM((width, 2 * local * hidden), BF)],
        compiler_params=pltpu.CompilerParams(vmem_limit_bytes=52 * MIB),
        cost_estimate=pl.CostEstimate(
            flops=8 * count * seq * width * local * hidden, bytes_accessed=0, transcendentals=0
        ),
        name="experts",
    )(base, *pieces, routes, router, w_gate, w_up, v)


def moe_kernel(h_ref, wd_ref, *parts):
    out = nn(h_ref[0], wd_ref[...])
    rows = parts[0].shape[1]
    for r, part in enumerate(parts):
        part[0] = out[r * rows : (r + 1) * rows].astype(part.dtype)


def run_moe(h, down_flat, kinds):
    count, seq, inner = h.shape
    width = down_flat.shape[1]
    rows = seq // 4
    return pl.pallas_call(
        moe_kernel,
        grid=(count,),
        in_specs=[
            pl.BlockSpec((1, seq, inner), lambda s: (s, 0, 0)),
            pl.BlockSpec((inner, width), lambda s: (0, 0)),
        ],
        out_specs=[pl.BlockSpec((1, rows, width), lambda s: (s, 0, 0))] * 4,
        out_shape=[shape((count, rows, width), kind) for kind in kinds],
        compiler_params=pltpu.CompilerParams(vmem_limit_bytes=40 * MIB),
        cost_estimate=pl.CostEstimate(
            flops=2 * count * seq * width * inner, bytes_accessed=0, transcendentals=0
        ),
        name="moe",
    )(h, down_flat)


def grads_kernel(n0, nf, dgu0, dguf, h0, hf, c0, cf, gate_ref, up_ref, down_ref):
    hidden = down_ref.shape[1]
    both = tn(n0[0], dgu0[0])
    down = tn(h0[0], c0[0])
    for s in range(nf.shape[0]):
        both = both + tn(nf[s], dguf[s])
        down = down + tn(hf[s], cf[s])
    gate_ref[0] = both[:, :hidden].astype(BF)
    up_ref[0] = both[:, hidden:].astype(BF)
    down_ref[0] = down.astype(BF)


def run_grads(n0, nf, dgu0, dguf, h0, hf, c0, cf, local, hidden):
    width = n0.shape[2]
    whole = lambda a: pl.BlockSpec(a.shape, lambda e: (0, 0, 0))
    cols = lambda a, w: pl.BlockSpec((*a.shape[:2], w), lambda e: (0, 0, e))
    flops = 6 * (n0.shape[0] + nf.shape[0]) * n0.shape[1] * width * hidden * local
    return pl.pallas_call(
        grads_kernel,
        grid=(local,),
        in_specs=[whole(n0), whole(nf), cols(dgu0, 2 * hidden), cols(dguf, 2 * hidden)]
        + [cols(h0, hidden), cols(hf, hidden), whole(c0), whole(cf)],
        out_specs=[
            pl.BlockSpec((1, width, hidden), lambda e: (e, 0, 0)),
            pl.BlockSpec((1, width, hidden), lambda e: (e, 0, 0)),
            pl.BlockSpec((1, hidden, width), lambda e: (e, 0, 0)),
        ],
        out_shape=[
            shape((local, width, hidden), BF),
            shape((local, width, hidden), BF),
            shape((local, hidden, width), BF),
        ],
        compiler_params=pltpu.CompilerParams(vmem_limit_bytes=56 * MIB),
        cost_estimate=pl.CostEstimate(flops=flops, bytes_accessed=0, transcendentals=0),
        name="expert_grads",
    )(n0, nf, dgu0, dguf, h0, hf, c0, cf)


def norm_back_kernel(experts, me_ref, count, h_ref, n_ref, gain_ref, router_ref, routes_ref, bal_ref, cot_ref, *refs):
    sums, (wide_ref, dh_ref, small_ref) = refs[:count], refs[count:]
    near = sums[0][...].astype(F32)
    for other in sums[1:]:
        near = near + other[...].astype(F32)
    rows, width = h_ref.shape
    dots = near[:, width:]
    probs, gates = router_of(n_ref[...], router_ref, routes_ref[...], experts)
    bal = bal_ref[...]
    d_chosen = gates * (dots - jnp.sum(gates * dots, axis=-1, keepdims=True))
    dz = probs * (bal - jnp.sum(probs * bal, axis=-1, keepdims=True)) + d_chosen
    dz = dz.astype(BF)
    wide_ref[:, width:] = dz
    dn = near[:, :width] + nt(dz, router_ref[...])
    h = h_ref[...]
    inv = lax.rsqrt(jnp.mean(h * h, axis=-1, keepdims=True) + EPS)
    u = gain_ref[...] * dn
    start = pl.multiple_of(me_ref[0] * rows, rows)
    dy = cot_ref[pl.ds(start, rows), :].astype(F32)
    dh = dy + inv * u - h * (inv * inv * inv * jnp.mean(u * h, axis=-1, keepdims=True))
    dh_ref[...] = dh
    wide_ref[:, :width] = dh.astype(BF)
    small_ref[...] = jnp.zeros(small_ref.shape, F32)
    small_ref[1:2, :] = jnp.sum(dn * h * inv, axis=0, keepdims=True)
    small_ref[2:3, : probs.shape[1]] = jnp.sum(probs, axis=0, keepdims=True)


def attend_back_kernel(
    me_ref, w0, w1, w2, w3, x_ref, q_ref, k_ref, v_ref, lse_ref, wq_ref, wk_ref, wv_ref, wo_ref, cos_ref, sin_ref,
    small_in, wide_ref, dq_ref, small_ref, p0, p1, p2, p3, do_ref, whole
):
    rows = w0.shape[0]
    width = x_ref.shape[1]
    for r, piece in enumerate((w0, w1, w2, w3)):
        start = pl.multiple_of((me_ref[0] ^ r) * rows, rows)
        wide_ref[pl.ds(start, rows), :] = piece[...]
    do_ref[...] = nt(wide_ref[:, :width], wo_ref[...]).astype(BF)
    cosine, sine = cos_ref[...], sin_ref[...]
    scale = HD ** (-0.5)
    heads, keys_wide = q_ref.shape[1], k_ref.shape[1]
    dk_tiles = [0.0] * (keys_wide // LANES)
    dv_tiles = [0.0] * (keys_wide // LANES)

    def back(tile):
        return (tile * cosine - halves_swapped(tile) * sine).astype(BF)

    for head in range(heads // LANES):
        at = head // 2 * LANES
        side = head % 2
        keys = low_high(k_ref[:, at : at + LANES], side)
        values = low_high(v_ref[:, at : at + LANES], side)
        pair = q_ref[:, head * LANES : (head + 1) * LANES]
        grad = do_ref[:, head * LANES : (head + 1) * LANES]
        dq = 0.0
        dk, dv = [], []
        for g in range(2):
            s = nt(pair, keys[g]) * scale
            lse = lse_ref[:, 2 * head + g : 2 * head + g + 1]
            p = jnp.where(causal(s), jnp.exp(s - lse), 0.0)
            dp = nt(grad, values[g])
            ds = (p * (dp - jnp.sum(p * dp, axis=-1, keepdims=True))).astype(BF)
            dq = dq + nn(ds, keys[g])
            dk.append(tn(ds, pair))
            dv.append(tn(p.astype(BF), grad))
        dq_ref[:, head * LANES : (head + 1) * LANES] = back(dq * scale)
        mine = lane_of(dk[0].shape) < HD
        if side == 0:
            dk_sum = jnp.where(mine, dk[0] + pltpu.roll(dk[1], HD, 1), 0.0)
            dv_sum = jnp.where(mine, dv[0] + pltpu.roll(dv[1], HD, 1), 0.0)
        else:
            dk_sum = jnp.where(mine, 0.0, pltpu.roll(dk[0], HD, 1) + dk[1])
            dv_sum = jnp.where(mine, 0.0, pltpu.roll(dv[0], HD, 1) + dv[1])
        dk_tiles[head // 2] = dk_tiles[head // 2] + dk_sum
        dv_tiles[head // 2] = dv_tiles[head // 2] + dv_sum
    for i, tile in enumerate(dk_tiles):
        at = heads + i * LANES
        dq_ref[:, at : at + LANES] = back(tile * scale)
    for i, tile in enumerate(dv_tiles):
        at = heads + keys_wide + i * LANES
        dq_ref[:, at : at + LANES] = tile.astype(BF)
    dn = nt(dq_ref[:, :heads], wq_ref[...])
    dn = dn + nt(dq_ref[:, heads : heads + keys_wide], wk_ref[...])
    whole[...] = dn + nt(dq_ref[:, heads + keys_wide :], wv_ref[...])
    for r, part in enumerate((p0, p1, p2, p3)):
        start = pl.multiple_of((me_ref[0] ^ r) * rows, rows)
        part[...] = whole[pl.ds(start, rows), :].astype(part.dtype)
    x = x_ref[...].astype(F32)
    inv = lax.rsqrt(jnp.mean(x * x, axis=-1, keepdims=True) + EPS)
    small_ref[...] = small_in[...]
    small_ref[0:1, :] = jnp.sum(whole[...] * x * inv, axis=0, keepdims=True)


def dense_early_kernel(me_ref, a0, a1, a2, a3, wide_ref, o_ref, kept_ref, sent_ref, n_ref, whole):
    rows = a0.shape[0]
    width = a0.shape[1]
    for r, piece in enumerate((a0, a1, a2, a3)):
        start = pl.multiple_of((me_ref[1] ^ r) * rows, rows)
        n_ref[pl.ds(start, rows), :] = piece[...]
    heads = o_ref.shape[1]
    whole[:, :heads] = tn(wide_ref[:, :width], o_ref[...])
    whole[:, heads:] = tn(n_ref[...], wide_ref[:, width:])
    half = kept_ref.shape[0]
    kept_ref[...] = whole[pl.ds(pl.multiple_of(me_ref[0] * half, half), half), :]
    sent_ref[...] = whole[pl.ds(pl.multiple_of((1 - me_ref[0]) * half, half), half), :].astype(BF)


def dense_late_kernel(me_ref, n_ref, dq_ref, kept_ref, sent_ref, whole):
    whole[...] = tn(n_ref[...], dq_ref[...])
    half = kept_ref.shape[0]
    kept_ref[...] = whole[pl.ds(pl.multiple_of(me_ref[0] * half, half), half), :]
    sent_ref[...] = whole[pl.ds(pl.multiple_of((1 - me_ref[0]) * half, half), half), :].astype(BF)


def input_grad_kernel(me_ref, x_ref, gain_ref, dh_ref, own_ref, *refs):
    others, ig_ref = refs[:-1], refs[-1]
    rows = dh_ref.shape[0]
    start = pl.multiple_of(me_ref[0] * rows, rows)
    x = x_ref[pl.ds(start, rows), :].astype(F32)
    inv = lax.rsqrt(jnp.mean(x * x, axis=-1, keepdims=True) + EPS)
    dn = own_ref[...]
    for other in others:
        dn = dn + other[...].astype(F32)
    u = gain_ref[...] * dn
    ig = dh_ref[...] + inv * u - x * (inv * inv * inv * jnp.mean(u * x, axis=-1, keepdims=True))
    ig_ref[...] = ig.astype(BF)


def natural_kernel(me_ref, *refs):
    pieces, out = refs[:-1], refs[-1]
    rows = pieces[0].shape[0]
    for r, piece in enumerate(pieces):
        start = pl.multiple_of((me_ref[0] ^ r) * rows, rows)
        out[pl.ds(start, rows), :] = piece[...].astype(out.dtype)


def ordered_sum_kernel(me_ref, *refs):
    pieces, out, held = refs[:-2], refs[-2], refs[-1]
    for r, piece in enumerate(pieces):
        held[me_ref[0] ^ r] = piece[...]
    total = held[0]
    for i in range(1, len(pieces)):
        total = total + held[i]
    out[...] = total


def ordered_sum(me, pieces):
    return call(
        ordered_sum_kernel,
        shape(pieces[0].shape, F32),
        (me, *pieces),
        scalars=1,
        scratch=[pltpu.VMEM((len(pieces), *pieces[0].shape), F32)],
        name="ordered_sum",
    )


def on_device(
    tokens,
    routes,
    gain_first,
    w_query,
    w_key,
    w_value,
    w_output,
    gain_second,
    w_router,
    w_gate,
    w_up,
    w_down,
    cotangent,
):
    seq_len, width = tokens.shape
    experts = w_router.shape[1]
    local, _, hidden = w_gate.shape
    tensor_size = lax.axis_size("tensor")
    expert_size = lax.axis_size("expert")
    dp_size = lax.axis_size("dp")
    token_count = seq_len * dp_size * expert_size
    rows = seq_len // tensor_size
    last = tensor_size - 1
    around = range(1, tensor_size)
    t_me, e_me, d_me = lax.axis_index("tensor"), lax.axis_index("expert"), lax.axis_index("dp")
    t_at = t_me.astype(jnp.int32).reshape(1)
    e_at = e_me.astype(jnp.int32).reshape(1)
    cosine, sine = rope_tables(seq_len)
    gain_one, gain_two = gain_first[None], gain_second[None]
    router = jnp.pad(w_router, ((0, 0), (0, LANES - experts)))
    down_flat = w_down.reshape(local * hidden, width)

    def quarter(x, r):
        return lax.dynamic_slice_in_dim(x, (t_me ^ r) * rows, rows, 0)

    cot_near = [quarter(cotangent, r) for r in range(tensor_size)]
    cot_first = spread(cot_near[0], "expert")
    routes_near = jnp.concatenate([quarter(routes, r) for r in range(tensor_size)], axis=0)
    routes_far = spread(routes_near, "expert")
    cot_far = [cot_first] + [swap(cot_first, "tensor", r) for r in around]
    cot0, v0 = hidden_cot([c[None] for c in cot_near], down_flat)
    cotf, vf = hidden_cot(cot_far, down_flat)
    everyone = jnp.concatenate([routes_near, routes_far.reshape(-1, TOP)], axis=0)
    named = everyone[:, :, None] == jnp.arange(LANES, dtype=jnp.int32)
    counts = jnp.sum(named.astype(F32), axis=(0, 1))[None]
    counts = counts + swap(counts, "dp", 1)
    balance = experts * (counts / (token_count * TOP)) / token_count

    heads, keys_wide = w_query.shape[1], w_key.shape[1]
    kinds = [F32] + [BF] * last
    n_one, q, k, v, o, lse, *parts = call(
        attend_kernel,
        [
            shape((seq_len, width), BF),
            shape((seq_len, heads), BF),
            shape((seq_len, keys_wide), BF),
            shape((seq_len, keys_wide), BF),
            shape((seq_len, heads), BF),
            shape((seq_len, LANES), F32),
        ]
        + [shape((rows, width), kind) for kind in kinds],
        (t_at, tokens, gain_one, w_query, w_key, w_value, w_output, cosine, sine),
        scalars=1,
        scratch=[pltpu.VMEM((seq_len, width), F32)],
        flops=2 * seq_len * width * 4 * heads,
        name="attend",
    )
    h, n_two = call(
        norm_two_kernel,
        [shape((rows, width), F32), shape((rows, width), BF)],
        (t_at, tokens, gain_two, parts[0], *[swap(parts[r], "tensor", r) for r in around]),
        scalars=1,
        name="norm_two",
    )

    own = [n_two] + [swap(n_two, "tensor", r) for r in around]
    far_first = spread(own[0], "expert")
    far_last = spread(own[last], "expert")
    far = [far_first] + [swap(far_first, "tensor", r) for r in range(1, last)] + [far_last]

    base = (e_me * local).astype(jnp.int32).reshape(1)
    n0, dgu0, h0, *near = run_experts(
        experts, base, [x[None] for x in own], routes_near[None], router, w_gate, w_up, v0,
        [F32, BF, BF, F32],
    )
    nf, dguf, hf, *away = run_experts(
        experts, base, far, routes_far, router, w_gate, w_up, vf, [F32, BF, BF, BF]
    )
    near = [x[0] for x in near]

    near_sums = [near[0]] + [swap(near[r], "tensor", r) for r in range(1, last)]
    first_sum = away[0]
    for r in range(1, last):
        first_sum = first_sum + swap(away[r], "tensor", r).astype(F32)
    from_last = deal(away[last], "expert")
    through = near[last] + jnp.sum(from_last.astype(F32), axis=0)
    near_sums.append(swap(through.astype(BF), "tensor", last))
    across = deal(first_sum.astype(BF), "expert")
    if expert_size <= FEW:
        near_sums.extend(across[r] for r in range(expert_size - 1))
    else:
        near_sums.append(jnp.sum(across.astype(F32), axis=0))

    m0 = run_moe(h0, down_flat, kinds)
    mf = run_moe(hf, down_flat, kinds)
    moe_near, moe_far = m0[0][0], mf[0]
    for r in around:
        moe_near = moe_near + swap(m0[r], "tensor", r)[0].astype(F32)
        moe_far = moe_far + swap(mf[r], "tensor", r).astype(F32)
    moe_sum = moe_near + jnp.sum(deal(moe_far.astype(BF), "expert").astype(F32), axis=0)
    out_piece = (h + moe_sum).astype(BF)
    output = call(
        natural_kernel,
        shape((seq_len, width), BF),
        (t_at, out_piece, *[swap(out_piece, "tensor", r) for r in around]),
        scalars=1,
        name="output",
    )

    grads = run_grads(n0, nf, dgu0, dguf, h0, hf, cot0, cotf, local, hidden)
    expert_grads = [x.astype(F32) + swap(x, "dp", 1).astype(F32) for x in grads]

    wide, dh, small = call(
        lambda me, *refs: norm_back_kernel(experts, me, len(near_sums), *refs),
        [shape((rows, width + LANES), BF), shape((rows, width), F32), shape((8, width), F32)],
        (t_at, h, n_two, gain_two, router, quarter(routes, 0), balance, cotangent, *near_sums),
        scalars=1,
        name="norm_back",
    )
    wides = [wide] + [swap(wide, "tensor", r) for r in around]

    wide_all, dqkv, small, *back_parts = call(
        attend_back_kernel,
        [
            shape((seq_len, width + LANES), BF),
            shape((seq_len, heads + 2 * keys_wide), BF),
            shape((8, width), F32),
        ]
        + [shape((rows, width), kind) for kind in kinds],
        (t_at, *wides, tokens, q, k, v, lse, w_query, w_key, w_value, w_output, cosine, sine, small),
        scalars=1,
        scratch=[pltpu.VMEM((seq_len, heads), BF), pltpu.VMEM((seq_len, width), F32)],
        flops=2 * seq_len * width * 4 * heads,
        name="attend_back",
    )
    ig = call(
        input_grad_kernel,
        shape((rows, width), BF),
        (t_at, tokens, gain_one, dh, back_parts[0])
        + tuple(swap(back_parts[r], "tensor", r) for r in around),
        scalars=1,
        name="input_grad",
    )
    input_grad = call(
        natural_kernel,
        shape((seq_len, width), F32),
        (t_at, ig, *[swap(ig, "tensor", r) for r in around]),
        scalars=1,
        name="input_grad_whole",
    )

    d_at = jnp.stack([d_me, t_me]).astype(jnp.int32)
    half = width // dp_size

    def summed(kept, sent):
        total = kept + swap(sent, "dp", 1).astype(F32)
        blocks = total.reshape(expert_size, half // expert_size, -1)
        first = lax.dynamic_index_in_dim(blocks, e_me, 0, keepdims=False)
        others = jnp.stack(
            [
                lax.dynamic_index_in_dim(blocks, e_me ^ r, 0, keepdims=False)
                for r in range(1, expert_size)
            ]
        )
        return first + jnp.sum(deal(others.astype(BF), "expert").astype(F32), axis=0)

    kept, sent, _ = call(
        dense_early_kernel,
        [
            shape((half, heads + LANES), F32),
            shape((half, heads + LANES), BF),
            shape((seq_len, width), BF),
        ],
        (d_at, *own, wide_all, o),
        scalars=1,
        scratch=[pltpu.VMEM((width, heads + LANES), F32)],
        flops=2 * seq_len * width * (heads + LANES),
        name="dense_early",
    )
    early = summed(kept, sent)
    kept, sent = call(
        dense_late_kernel,
        [shape((half, heads + 2 * keys_wide), F32), shape((half, heads + 2 * keys_wide), BF)],
        (d_at, n_one, dqkv),
        scalars=1,
        scratch=[pltpu.VMEM((width, heads + 2 * keys_wide), F32)],
        flops=2 * seq_len * width * (heads + 2 * keys_wide),
        name="dense_late",
    )
    late = summed(kept, sent)

    small = ordered_sum(t_at, [small] + [swap(small, "tensor", r) for r in around])
    small = small + swap(small, "dp", 1)
    if expert_size <= FEW:
        small = ordered_sum(e_at, [small] + [swap(small, "expert", r) for r in range(1, expert_size)])
    else:
        small = jnp.sum(lax.all_gather(small, "expert"), axis=0)
    chunk = width // (dp_size * expert_size)
    at = (d_me * expert_size + e_me) * chunk
    loss_value = (experts * balance * small[2:3, :LANES])[0, :experts]
    return (
        output,
        loss_value,
        input_grad,
        lax.dynamic_slice(small, (0, at), (1, chunk))[0],
        late[:, :heads],
        late[:, heads : heads + keys_wide],
        late[:, heads + keys_wide :],
        early[:, :heads].T,
        lax.dynamic_slice(small, (1, at), (1, chunk))[0],
        early[:, heads : heads + experts],
        expert_grads[0],
        expert_grads[1],
        expert_grads[2],
    )


def solution(mesh):
    rows = ("dp", "expert")
    placed = (
        P(rows, None),
        P(rows, None),
        P(),
        P(None, "tensor"),
        P(None, "tensor"),
        P(None, "tensor"),
        P("tensor", None),
        P(),
        P(),
        P("expert", None, "tensor"),
        P("expert", None, "tensor"),
        P("expert", "tensor", None),
        P(rows, None),
    )
    return jax.shard_map(
        on_device,
        mesh=mesh,
        in_specs=placed,
        out_specs=(
            P(rows, None),
            P(),
            P(rows, None),
            P(rows),
            P(rows, "tensor"),
            P(rows, "tensor"),
            P(rows, "tensor"),
            P("tensor", rows),
            P(rows),
            P(rows, None),
            P("expert", None, "tensor"),
            P("expert", None, "tensor"),
            P("expert", "tensor", None),
        ),
        check_vma=False,
    )
```

time: 422 us -> 277 us (0.66)
  blocking collectives: 52.6 us -> 0 us
  Pallas kernels: 0 us -> 50.4 us
  waiting for transfers between devices: 108 us -> 62.4 us
  matrix products: 45.4 us -> 0 us
  other arithmetic: 62 us -> 26.8 us
  starting transfers between devices: 66.2 us -> 98.9 us
  local copies, waits for them, and re-layouts: 68.3 us -> 35.7 us
  between operations: 15.5 us -> 1.46 us
    psum x2 -> x0, blocking collectives: 52.6 us -> none  [the longest x1 42.6 us: on_device(): prob_sums = lax.psum(jnp.sum(probs, axis=0), ('dp', 'expert', 'tensor'))]
    pallas_call x0 -> x18, Pallas kernels: none -> 50.4 us  [the longest x2 19.7 us: run_experts(): pl.pallas_call(functools.partial(experts_kernel, experts), grid=(count,),...]
    dot_general x27 -> x0, matrix products: 45.4 us -> none  [the longest x18 28.5 us: dot(): return lax.dot_general(a, b, (dims, ((), ())), preferred_element_type=F32)]
    ppermute x60 -> x74, starting transfers between devices: 66.2 us -> 98.9 us  [swap(): return lax.ppermute(x, axis, [(i, i ^ distance) for i in range(size)])]
    unnamed x2 -> x0, waiting for transfers between devices: 27 us -> none
    ppermute x60 -> x74, waiting for transfers between devices: 80.7 us -> 62.4 us  [swap(): return lax.ppermute(x, axis, [(i, i ^ distance) for i in range(size)])]
    dynamic_update_slice x14 -> x0, local copies, waits for them, and re-layouts: 9.58 us -> none  [the longest x13 9.57 us: natural(): lax.dynamic_update_slice_in_dim(whole, piece, (t_me ^ r) * quarter_len, 0)]
    concatenate x8 -> x0, other arithmetic: 8.08 us -> none  [the longest x1 2.59 us: on_device(): dn_part = jnp.concatenate([dn_part, dgates_wide], axis=1)]
  transfers between devices with their start and end apart: 61 -> 74, of which waited for: 18 -> 18; matrix products, arithmetic and copies ran while one was open for 31% -> 12% of each run, Pallas kernels for 0% -> 18%
where the time goes in v2:
time: 277 us; the launch traced here: 276 us
  starting transfers between devices  98.9 us (36%)
  waiting for transfers between devices  62.4 us (23%)
  Pallas kernels  50.4 us (18%)
  local copies, waits for them, and re-layouts  35.7 us (13%)
  other arithmetic  26.8 us (10%)
    ppermute x74, starting transfers between devices, swap(): return lax.ppermute(x, axis, [(i, i ^ distance) for i in range(size)])  98.9 us
    ppermute x74, waiting for transfers between devices, swap(): return lax.ppermute(x, axis, [(i, i ^ distance) for i in range(size)])  62.4 us
    unnamed x141, local copies, waits for them, and re-layouts  26.7 us
    pallas_call x2, Pallas kernels, run_experts(): pl.pallas_call(functools.partial(experts_kernel, experts), grid=(count,),...  19.7 us
    add x3, other arithmetic, on_device(): expert_grads = [x.astype(F32) + swap(x, 'dp', 1).astype(F32) for x in grads]  13.3 us
    pallas_call x1, Pallas kernels, run_grads(): pl.pallas_call(grads_kernel, grid=(local,), in_specs=[whole(n0), whole(nf...  13.1 us
    pallas_call x11, Pallas kernels, call(): pl.pallas_call(kernel, out_shape=out_shape, in_specs=[smem()] * scalars +...  10.7 us
  transfers between devices with their start and end apart: 74, of which 18 were waited for; matrix products, arithmetic and copies ran while one was open for 12% of the time, Pallas kernels for 18%

profile of v2, /device:TPU:0, one launch (start us, length us, event | category | flops | bytes accessed | tf_op | source)
XLA Modules:
  0.0 275.7 jit_solution(17353682392196123613)
XLA Ops:
  8.2 2.1 attend.1
  15.0 2.9 %collective-permute-start = (bf16[64,1024]{1,0:T(8,128)(2,1)S(1)}, bf16[64,1024]{1,0:T(8,128)(2,1)S(1)}, u32[]{:S(2)}, u32[]{:S(2)}) collective-permute-start(bf16[64,1024]{1,0:T(8,128)(2,1)S(1)} %get-tuple-element.69), channel_id=1, source_target_pairs={{0,1},{1,0},{2,3},{3,2},{4,5},{5,4},{6,7},{7,6},{8,9},{9,8},{10,11... | collective-permute-start | bytes 393224 | tf_op jit(solution)/shard_map/ppermute | solution.py:41
  21.7 4.1 %collective-permute-start.19 = (s32[256,8]{1,0:T(8,128)S(1)}, s32[256,8]{1,0:T(8,128)S(1)}, u32[]{:S(2)}, u32[]{:S(2)}) collective-permute-start(s32[256,8]{1,0:T(8,128)S(1)} %get-tuple-element.197), channel_id=1, source_target_pairs={{0,12},{4,8},{8,4},{12,0},{1,13},{5,9},{9,5},{13,1},{2,14},{6,10},... | collective-permute-start | bytes 24584 | tf_op jit(solution)/shard_map/ppermute | solution.py:41
  28.2 3.8 %collective-permute-start.22 = (bf16[64,1024]{1,0:T(8,128)(2,1)S(1)}, bf16[64,1024]{1,0:T(8,128)(2,1)}, u32[]{:S(2)}, u32[]{:S(2)}) collective-permute-start(bf16[64,1024]{1,0:T(8,128)(2,1)S(1)} %get-tuple-element.184), channel_id=1, source_target_pairs={{0,12},{4,8},{8,4},{12,0},{1,13},{5,9},{9,5},{13,1},{2,14},{6,10},... | collective-permute-start | bytes 393224 | tf_op jit(solution)/shard_map/ppermute | solution.py:41
  35.6 3.5 %collective-permute-start.20 = (bf16[64,1024]{1,0:T(8,128)(2,1)S(1)}, bf16[64,1024]{1,0:T(8,128)(2,1)}, u32[]{:S(2)}, u32[]{:S(2)}) collective-permute-start(bf16[64,1024]{1,0:T(8,128)(2,1)S(1)} %get-tuple-element.184), channel_id=1, source_target_pairs={{0,4},{4,0},{8,12},{12,8},{1,5},{5,1},{9,13},{13,9},{2,6},{6,2},{1... | collective-permute-start | bytes 393224 | tf_op jit(solution)/shard_map/ppermute | solution.py:41
  39.1 3.5 %collective-permute-done.18 = s32[256,8]{1,0:T(8,128)S(1)} collective-permute-done((s32[256,8]{1,0:T(8,128)S(1)}, s32[256,8]{1,0:T(8,128)S(1)}, u32[]{:S(2)}, u32[]{:S(2)}) %collective-permute-start.18) | collective-permute-done | bytes 8224 | tf_op jit(solution)/shard_map/ppermute | solution.py:41
  42.6 5.0 %collective-permute-start.11 = (bf16[64,1024]{1,0:T(8,128)(2,1)S(1)}, bf16[64,1024]{1,0:T(8,128)(2,1)}, u32[]{:S(2)}, u32[]{:S(2)}) collective-permute-start(bf16[64,1024]{1,0:T(8,128)(2,1)S(1)} %get-tuple-element.73.refs_1_.a0), channel_id=1, source_target_pairs={{0,12},{4,8},{8,4},{12,0},{1,13},{5,9},{9,5},{13,1},{2,14},{6,10},... | collective-permute-start | bytes 393224 | tf_op jit(solution)/shard_map/ppermute | solution.py:41
  47.6 2.4 collective-permute-start.5
  54.5 1.8 pad_add_fusion.routes_ref
  60.3 3.8 %collective-permute-start.16 = (bf16[64,1024]{1,0:T(8,128)(2,1)}, bf16[64,1024]{1,0:T(8,128)(2,1)S(1)}, u32[]{:S(2)}, u32[]{:S(2)}) collective-permute-start(bf16[64,1024]{1,0:T(8,128)(2,1)} %collective-permute-done.5.a3), channel_id=1, source_target_pairs={{0,12},{4,8},{8,4},{12,0},{1,13},{5,9},{9,5},{13,1},{2,14},{6,10},... | collective-permute-start | bytes 393224 | tf_op jit(solution)/shard_map/ppermute | solution.py:41
  64.1 4.1 %convert_reduce_fusion = f32[128]{0:T(128)S(1)} fusion(s32[1024,8]{1,0:T(8,128)} %copy.80), kind=kLoop, calls=%fused_computation.3 | loop fusion | flops 3145600 | bytes 33280 | tf_op jit(solution)/shard_map/reduce_sum | solution.py:555
  71.6 1.5 collective-permute-start.24
  76.1 1.5 collective-permute-start.13
  77.6 5.8 %experts.2 = (bf16[1,256,1024]{2,1,0:T(8,128)(2,1)}, bf16[1,256,2048]{2,1,0:T(8,128)(2,1)}, bf16[1,256,1024]{2,1,0:T(8,128)(2,1)}, f32[1,64,1152]{2,1,0:T(8,128)...) custom-call(s32[1]{0:T(128)} %bitcast.3.base_ref, ...), custom_call_target="tpu_custom_call" | custom-call | flops 2147483648 | tf_op jit(solution)/shard_map/experts/pallas_call | solution.py:264
  83.6 3.4 %collective-permute-done.24.c2 = bf16[3,64,1024]{2,1,0:T(8,128)(2,1)S(1)} collective-permute-done((bf16[3,64,1024]{2,1,0:T(8,128)(2,1)S(1)}, bf16[3,64,1024]{2,1,0:T(8,128)(2,1)S(1)}, u32[]{:S(2)}, u32[]{:S(2)}) %collective-permute-start.24) | collective-permute-done | bytes 393248 | tf_op jit(solution)/shard_map/ppermute | solution.py:41
  87.0 3.1 %collective-permute-done.25.c3 = bf16[3,64,1024]{2,1,0:T(8,128)(2,1)S(1)} collective-permute-done((bf16[3,64,1024]{2,1,0:T(8,128)(2,1)S(1)}, bf16[3,64,1024]{2,1,0:T(8,128)(2,1)S(1)}, u32[]{:S(2)}, u32[]{:S(2)}) %collective-permute-start.25) | collective-permute-done | bytes 393248 | tf_op jit(solution)/shard_map/ppermute | solution.py:41
  90.1 2.3 hidden_cot.3
  92.4 1.7 copy-done.49
  95.2 13.9 %experts.3 = (bf16[3,256,1024]{2,1,0:T(8,128)(2,1)}, bf16[3,256,2048]{2,1,0:T(8,128)(2,1)}, bf16[3,256,1024]{2,1,0:T(8,128)(2,1)}, f32[3,64,1152]{2,1,0:T(8,128)...) custom-call(s32[1]{0:T(128)} %bitcast.3.base_ref, ...), custom_call_target="tpu_custom_call" | custom-call | flops 6442450944 | tf_op jit(solution)/shard_map/experts/pallas_call | solution.py:264
  111.1 3.5 %collective-permute-start.38 = (bf16[64,1152]{1,0:T(8,128)(2,1)S(1)}, bf16[64,1152]{1,0:T(8,128)(2,1)S(1)}, u32[]{:S(2)}, u32[]{:S(2)}) collective-permute-start(bf16[64,1152]{1,0:T(8,128)(2,1)S(1)} %get-tuple-element.188), channel_id=1, source_target_pairs={{0,4},{4,0},{8,12},{12,8},{1,5},{5,1},{9,13},{13,9},{2,6},{6,2},{1... | collective-permute-start | bytes 442376 | tf_op jit(solution)/shard_map/ppermute | solution.py:41
  116.0 2.4 moe.3
  122.7 8.3 %collective-permute-done.28 = bf16[3,64,1024]{2,1,0:T(8,128)(2,1)S(1)} collective-permute-done((bf16[3,64,1024]{2,1,0:T(8,128)(2,1)S(1)}, bf16[3,64,1024]{2,1,0:T(8,128)(2,1)S(1)}, u32[]{:S(2)}, u32[]{:S(2)}) %collective-permute-start.28) | collective-permute-done | bytes 393248 | tf_op jit(solution)/shard_map/ppermute | solution.py:41
  131.9 4.3 %collective-permute-done.27 = bf16[3,64,1024]{2,1,0:T(8,128)(2,1)S(1)} collective-permute-done((bf16[3,64,1024]{2,1,0:T(8,128)(2,1)S(1)}, bf16[3,64,1024]{2,1,0:T(8,128)(2,1)S(1)}, u32[]{:S(2)}, u32[]{:S(2)}) %collective-permute-start.27) | collective-permute-done | bytes 393248 | tf_op jit(solution)/shard_map/ppermute | solution.py:41
  138.5 8.1 %collective-permute-done.43 = bf16[3,64,1152]{2,1,0:T(8,128)(2,1)S(1)} collective-permute-done((bf16[3,64,1152]{2,1,0:T(8,128)(2,1)S(1)}, bf16[3,64,1152]{2,1,0:T(8,128)(2,1)S(1)}, u32[]{:S(2)}, u32[]{:S(2)}) %collective-permute-start.43) | collective-permute-done | bytes 442400 | tf_op jit(solution)/shard_map/ppermute | solution.py:41
  146.6 3.4 %collective-permute-start.31 = (bf16[64,1024]{1,0:T(8,128)(2,1)S(1)}, bf16[64,1024]{1,0:T(8,128)(2,1)S(1)}, u32[]{:S(2)}, u32[]{:S(2)}) collective-permute-start(bf16[64,1024]{1,0:T(8,128)(2,1)S(1)} %get-tuple-element.192), channel_id=1, source_target_pairs={{0,12},{4,8},{8,4},{12,0},{1,13},{5,9},{9,5},{13,1},{2,14},{6,10},... | collective-permute-start | bytes 393224 | tf_op jit(solution)/shard_map/ppermute | solution.py:41
  151.3 3.4 %collective-permute-start.46 = (bf16[64,1152]{1,0:T(8,128)(2,1)S(1)}, bf16[64,1152]{1,0:T(8,128)(2,1)S(1)}, u32[]{:S(2)}, u32[]{:S(2)}) collective-permute-start(bf16[64,1152]{1,0:T(8,128)(2,1)S(1)} %get-tuple-element.185), channel_id=1, source_target_pairs={{0,12},{4,8},{8,4},{12,0},{1,13},{5,9},{9,5},{13,1},{2,14},{6,10},... | collective-permute-start | bytes 442376 | tf_op jit(solution)/shard_map/ppermute | solution.py:41
  154.6 3.2 %collective-permute-done.44.refs_11_ = bf16[64,1152]{1,0:T(8,128)(2,1)S(1)} collective-permute-done((bf16[64,1152]{1,0:T(8,128)(2,1)S(1)}, bf16[64,1152]{1,0:T(8,128)(2,1)S(1)}, u32[]{:S(2)}, u32[]{:S(2)}) %collective-permute-start.44) | collective-permute-done | bytes 147488 | tf_op jit(solution)/shard_map/ppermute | solution.py:41
  157.8 6.5 %collective-permute-done.45.refs_12_ = bf16[64,1152]{1,0:T(8,128)(2,1)S(1)} collective-permute-done((bf16[64,1152]{1,0:T(8,128)(2,1)S(1)}, bf16[64,1152]{1,0:T(8,128)(2,1)S(1)}, u32[]{:S(2)}, u32[]{:S(2)}) %collective-permute-start.45) | collective-permute-done | bytes 147488 | tf_op jit(solution)/shard_map/ppermute | solution.py:41
  168.8 3.5 %collective-permute-start.30 = (bf16[64,1024]{1,0:T(8,128)(2,1)S(1)}, bf16[64,1024]{1,0:T(8,128)(2,1)S(1)}, u32[]{:S(2)}, u32[]{:S(2)}) collective-permute-start(bf16[64,1024]{1,0:T(8,128)(2,1)S(1)} %get-tuple-element.193), channel_id=1, source_target_pairs={{0,8},{4,12},{8,0},{12,4},{1,9},{5,13},{9,1},{13,5},{2,10},{6,14},... | collective-permute-start | bytes 393224 | tf_op jit(solution)/shard_map/ppermute | solution.py:41
  177.4 2.7 attend_back.1
  182.8 2.0 collective-permute-done.50.refs_1_
  187.3 2.4 collective-permute-done.52.refs_3_
  193.4 1.6 collective-permute-start.34
  195.0 3.4 %collective-permute-start.54 = (f32[8,1024]{1,0:T(8,128)S(1)}, f32[8,1024]{1,0:T(8,128)S(1)}, u32[]{:S(2)}, u32[]{:S(2)}) collective-permute-start(f32[8,1024]{1,0:T(8,128)S(1)} %add.126.refs_0_), channel_id=1, source_target_pairs={{0,4},{4,0},{8,12},{12,8},{1,5},{5,1},{9,13},{13,9},{2,6},{6,2},{1... | collective-permute-start | bytes 98312 | tf_op jit(solution)/shard_map/ppermute | solution.py:41
  200.0 1.7 dense_early.1
  202.5 2.7 collective-permute-start.59
  206.7 13.1 %expert_grads.1 = (bf16[8,1024,128]{2,1,0:T(8,128)(2,1)}, bf16[8,1024,128]{2,1,0:T(8,128)(2,1)}, bf16[8,128,1024]{2,1,0:T(8,128)(2,1)}) custom-call(bf16[1,256,1024]{2,1,0:T(8,128)(2,1)} %get-tuple-element.114.n0, bf16[3,256,1024]{2,1,0:T(8,128)(2,1)} %get-tuple-element.115.nf, bf16[1,256,2048]{2,1,0:T(8,128)(2,1)} %get-tuple-element.116.dgu0, ...), custom_call_target="tpu_custom_call" | custom-call | flops 6442450944 | tf_op jit(solution)/shard_map/expert_grads/pallas_call | solution.py:333
  223.9 4.8 %collective-permute-done.60.refs_1_ = bf16[64,1024]{1,0:T(8,128)(2,1)S(1)} collective-permute-done((bf16[64,1024]{1,0:T(8,128)(2,1)S(1)}, bf16[64,1024]{1,0:T(8,128)(2,1)S(1)}, u32[]{:S(2)}, u32[]{:S(2)}) %collective-permute-start.60) | collective-permute-done | bytes 131104 | tf_op jit(solution)/shard_map/ppermute | solution.py:41
  229.1 2.4 collective-permute-start.70
  232.2 2.4 collective-permute-done.62.refs_3_
  234.6 2.0 collective-permute-start.69
  242.2 2.7 collective-permute-start.66
  245.5 4.7 %collective-permute-done.66 = bf16[128,512]{1,0:T(8,128)(2,1)S(1)} collective-permute-done((bf16[128,512]{1,0:T(8,128)(2,1)S(1)}, bf16[128,512]{1,0:T(8,128)(2,1)S(1)}, u32[]{:S(2)}, u32[]{:S(2)}) %collective-permute-start.66) | collective-permute-done | bytes 131104 | tf_op jit(solution)/shard_map/ppermute | solution.py:41
  250.2 5.0 %collective-permute-start.64 = (bf16[128,512]{1,0:T(8,128)(2,1)}, bf16[128,512]{1,0:T(8,128)(2,1)}, u32[]{:S(2)}, u32[]{:S(2)}) collective-permute-start(bf16[128,512]{1,0:T(8,128)(2,1)} %get-tuple-element.175), channel_id=1, source_target_pairs={{0,4},{4,0},{8,12},{12,8},{1,5},{5,1},{9,13},{13,9},{2,6},{6,2},{1... | collective-permute-start | bytes 393224 | tf_op jit(solution)/shard_map/ppermute | solution.py:41
  257.2 2.7 collective-permute-done.64
  262.3 4.2 %convert_add_fusion.2 = f32[8,1024,128]{2,1,0:T(8,128)} fusion(bf16[8,1024,128]{2,1,0:T(8,128)(2,1)} %collective-permute-done.71, bf16[8,1024,128]{2,1,0:T(8,128)(2,1)S(1)} %copy-done.53), kind=kLoop, calls=%fused_computation.2 | loop fusion | flops 3145728 | bytes 8388608 | tf_op jit(solution)/shard_map/add | solution.py:631
  266.5 4.0 %convert_add_fusion.1 = f32[8,1024,128]{2,1,0:T(8,128)} fusion(bf16[8,1024,128]{2,1,0:T(8,128)(2,1)} %collective-permute-done.72, bf16[8,1024,128]{2,1,0:T(8,128)(2,1)S(1)} %copy-done.52), kind=kLoop, calls=%fused_computation.1 | loop fusion | flops 3145728 | bytes 8388608 | tf_op jit(solution)/shard_map/add | solution.py:631
  270.5 5.2 %convert_add_fusion = f32[8,128,1024]{2,1,0:T(8,128)} fusion(bf16[8,128,1024]{2,1,0:T(8,128)(2,1)} %collective-permute-done.73, bf16[8,128,1024]{2,1,0:T(8,128)(2,1)} %get-tuple-element.122), kind=kLoop, calls=%fused_computation | loop fusion | flops 3145728 | bytes 8388608 | tf_op jit(solution)/shard_map/add | solution.py:631
  (300 shorter events, 87.6 us)
Async XLA Ops:
  15.0 10.7 %collective-permute-start = (bf16[64,1024]{1,0:T(8,128)(2,1)S(1)}, bf16[64,1024]{1,0:T(8,128)(2,1)S(1)}, u32[]{:S(2)}, u32[]{:S(2)}) collective-permute-start(bf16[64,1024]{1,0:T(8,128)(2,1)S(1)} %get-tuple-element.69), channel_id=1, source_target_pairs={{0,1},{1,0},{2,3},{3,2},{4,5},{5,4},{6,7},{7,6},{8,9},{9,8},{10,11... | collective-permute-start | bytes 393224 | tf_op jit(solution)/shard_map/ppermute | solution.py:41
  19.5 12.5 %collective-permute-start.2 = (bf16[64,1024]{1,0:T(8,128)(2,1)S(1)}, bf16[64,1024]{1,0:T(8,128)(2,1)S(1)}, u32[]{:S(2)}, u32[]{:S(2)}) collective-permute-start(bf16[64,1024]{1,0:T(8,128)(2,1)S(1)} %get-tuple-element.71), channel_id=1, source_target_pairs={{0,3},{1,2},{2,1},{3,0},{4,7},{5,6},{6,5},{7,4},{8,11},{9,10},{10,... | collective-permute-start | bytes 393224 | tf_op jit(solution)/shard_map/ppermute | solution.py:41
  21.7 13.9 %collective-permute-start.19 = (s32[256,8]{1,0:T(8,128)S(1)}, s32[256,8]{1,0:T(8,128)S(1)}, u32[]{:S(2)}, u32[]{:S(2)}) collective-permute-start(s32[256,8]{1,0:T(8,128)S(1)} %get-tuple-element.197), channel_id=1, source_target_pairs={{0,12},{4,8},{8,4},{12,0},{1,13},{5,9},{9,5},{13,1},{2,14},{6,10},... | collective-permute-start | bytes 24584 | tf_op jit(solution)/shard_map/ppermute | solution.py:41
  25.8 16.9 %collective-permute-start.18 = (s32[256,8]{1,0:T(8,128)S(1)}, s32[256,8]{1,0:T(8,128)S(1)}, u32[]{:S(2)}, u32[]{:S(2)}) collective-permute-start(s32[256,8]{1,0:T(8,128)S(1)} %get-tuple-element.197), channel_id=1, source_target_pairs={{0,8},{4,12},{8,0},{12,4},{1,9},{5,13},{9,1},{13,5},{2,10},{6,14},... | collective-permute-start | bytes 24584 | tf_op jit(solution)/shard_map/ppermute | solution.py:41
  25.8 21.9 %collective-permute-start.17 = (s32[256,8]{1,0:T(8,128)S(1)}, s32[256,8]{1,0:T(8,128)S(1)}, u32[]{:S(2)}, u32[]{:S(2)}) collective-permute-start(s32[256,8]{1,0:T(8,128)S(1)} %get-tuple-element.197), channel_id=1, source_target_pairs={{0,4},{4,0},{8,12},{12,8},{1,5},{5,1},{9,13},{13,9},{2,6},{6,2},{1... | collective-permute-start | bytes 24584 | tf_op jit(solution)/shard_map/ppermute | solution.py:41
  28.2 30.3 %collective-permute-start.22 = (bf16[64,1024]{1,0:T(8,128)(2,1)S(1)}, bf16[64,1024]{1,0:T(8,128)(2,1)}, u32[]{:S(2)}, u32[]{:S(2)}) collective-permute-start(bf16[64,1024]{1,0:T(8,128)(2,1)S(1)} %get-tuple-element.184), channel_id=1, source_target_pairs={{0,12},{4,8},{8,4},{12,0},{1,13},{5,9},{9,5},{13,1},{2,14},{6,10},... | collective-permute-start | bytes 393224 | tf_op jit(solution)/shard_map/ppermute | solution.py:41
  32.7 25.9 %collective-permute-start.21 = (bf16[64,1024]{1,0:T(8,128)(2,1)S(1)}, bf16[64,1024]{1,0:T(8,128)(2,1)}, u32[]{:S(2)}, u32[]{:S(2)}) collective-permute-start(bf16[64,1024]{1,0:T(8,128)(2,1)S(1)} %get-tuple-element.184), channel_id=1, source_target_pairs={{0,8},{4,12},{8,0},{12,4},{1,9},{5,13},{9,1},{13,5},{2,10},{6,14},... | collective-permute-start | bytes 393224 | tf_op jit(solution)/shard_map/ppermute | solution.py:41
  35.6 23.5 %collective-permute-start.20 = (bf16[64,1024]{1,0:T(8,128)(2,1)S(1)}, bf16[64,1024]{1,0:T(8,128)(2,1)}, u32[]{:S(2)}, u32[]{:S(2)}) collective-permute-start(bf16[64,1024]{1,0:T(8,128)(2,1)S(1)} %get-tuple-element.184), channel_id=1, source_target_pairs={{0,4},{4,0},{8,12},{12,8},{1,5},{5,1},{9,13},{13,9},{2,6},{6,2},{1... | collective-permute-start | bytes 393224 | tf_op jit(solution)/shard_map/ppermute | solution.py:41
  42.6 17.1 %collective-permute-start.11 = (bf16[64,1024]{1,0:T(8,128)(2,1)S(1)}, bf16[64,1024]{1,0:T(8,128)(2,1)}, u32[]{:S(2)}, u32[]{:S(2)}) collective-permute-start(bf16[64,1024]{1,0:T(8,128)(2,1)S(1)} %get-tuple-element.73.refs_1_.a0), channel_id=1, source_target_pairs={{0,12},{4,8},{8,4},{12,0},{1,13},{5,9},{9,5},{13,1},{2,14},{6,10},... | collective-permute-start | bytes 393224 | tf_op jit(solution)/shard_map/ppermute | solution.py:41
  47.6 12.7 %collective-permute-start.5 = (bf16[64,1024]{1,0:T(8,128)(2,1)S(1)}, bf16[64,1024]{1,0:T(8,128)(2,1)}, u32[]{:S(2)}, u32[]{:S(2)}) collective-permute-start(bf16[64,1024]{1,0:T(8,128)(2,1)S(1)} %get-tuple-element.73.refs_1_.a0), channel_id=1, source_target_pairs={{0,3},{1,2},{2,1},{3,0},{4,7},{5,6},{6,5},{7,4},{8,11},{9,10},{10,... | collective-permute-start | bytes 393224 | tf_op jit(solution)/shard_map/ppermute | solution.py:41
  58.5 9.7 %collective-permute-start.10 = (bf16[64,1024]{1,0:T(8,128)(2,1)S(1)}, bf16[64,1024]{1,0:T(8,128)(2,1)S(1)}, u32[]{:S(2)}, u32[]{:S(2)}) collective-permute-start(bf16[64,1024]{1,0:T(8,128)(2,1)S(1)} %get-tuple-element.73.refs_1_.a0), channel_id=1, source_target_pairs={{0,8},{4,12},{8,0},{12,4},{1,9},{5,13},{9,1},{13,5},{2,10},{6,14},... | collective-permute-start | bytes 393224 | tf_op jit(solution)/shard_map/ppermute | solution.py:41
  58.5 9.8 %collective-permute-start.9 = (bf16[64,1024]{1,0:T(8,128)(2,1)S(1)}, bf16[64,1024]{1,0:T(8,128)(2,1)S(1)}, u32[]{:S(2)}, u32[]{:S(2)}) collective-permute-start(bf16[64,1024]{1,0:T(8,128)(2,1)S(1)} %get-tuple-element.73.refs_1_.a0), channel_id=1, source_target_pairs={{0,4},{4,0},{8,12},{12,8},{1,5},{5,1},{9,13},{13,9},{2,6},{6,2},{1... | collective-permute-start | bytes 393224 | tf_op jit(solution)/shard_map/ppermute | solution.py:41
  59.2 11.0 %collective-permute-start.3 = (bf16[64,1024]{1,0:T(8,128)(2,1)S(1)}, bf16[64,1024]{1,0:T(8,128)(2,1)S(1)}, u32[]{:S(2)}, u32[]{:S(2)}) collective-permute-start(bf16[64,1024]{1,0:T(8,128)(2,1)S(1)} %get-tuple-element.73.refs_1_.a0), channel_id=1, source_target_pairs={{0,1},{1,0},{2,3},{3,2},{4,5},{5,4},{6,7},{7,6},{8,9},{9,8},{10,11... | collective-permute-start | bytes 393224 | tf_op jit(solution)/shard_map/ppermute | solution.py:41
  59.7 11.9 %collective-permute-start.4 = (bf16[64,1024]{1,0:T(8,128)(2,1)S(1)}, bf16[64,1024]{1,0:T(8,128)(2,1)S(1)}, u32[]{:S(2)}, u32[]{:S(2)}) collective-permute-start(bf16[64,1024]{1,0:T(8,128)(2,1)S(1)} %get-tuple-element.73.refs_1_.a0), channel_id=1, source_target_pairs={{0,2},{1,3},{2,0},{3,1},{4,6},{5,7},{6,4},{7,5},{8,10},{9,11},{10,... | collective-permute-start | bytes 393224 | tf_op jit(solution)/shard_map/ppermute | solution.py:41
  60.3 12.8 %collective-permute-start.16 = (bf16[64,1024]{1,0:T(8,128)(2,1)}, bf16[64,1024]{1,0:T(8,128)(2,1)S(1)}, u32[]{:S(2)}, u32[]{:S(2)}) collective-permute-start(bf16[64,1024]{1,0:T(8,128)(2,1)} %collective-permute-done.5.a3), channel_id=1, source_target_pairs={{0,12},{4,8},{8,4},{12,0},{1,13},{5,9},{9,5},{13,1},{2,14},{6,10},... | collective-permute-start | bytes 393224 | tf_op jit(solution)/shard_map/ppermute | solution.py:41
  70.2 13.3 %collective-permute-start.23 = (bf16[3,64,1024]{2,1,0:T(8,128)(2,1)S(1)}, bf16[3,64,1024]{2,1,0:T(8,128)(2,1)S(1)}, u32[]{:S(2)}, u32[]{:S(2)}) collective-permute-start(bf16[3,64,1024]{2,1,0:T(8,128)(2,1)S(1)} %pad_maximum_fusion.2.c0), channel_id=1, source_target_pairs={{0,1},{1,0},{2,3},{3,2},{4,5},{5,4},{6,7},{7,6},{8,9},{9,8},{10,11... | collective-permute-start | bytes 1179656 | tf_op jit(solution)/shard_map/ppermute | solution.py:41
  71.6 15.4 %collective-permute-start.24 = (bf16[3,64,1024]{2,1,0:T(8,128)(2,1)S(1)}, bf16[3,64,1024]{2,1,0:T(8,128)(2,1)S(1)}, u32[]{:S(2)}, u32[]{:S(2)}) collective-permute-start(bf16[3,64,1024]{2,1,0:T(8,128)(2,1)S(1)} %pad_maximum_fusion.2.c0), channel_id=1, source_target_pairs={{0,2},{1,3},{2,0},{3,1},{4,6},{5,7},{6,4},{7,5},{8,10},{9,11},{10,... | collective-permute-start | bytes 1179656 | tf_op jit(solution)/shard_map/ppermute | solution.py:41
  73.1 17.0 %collective-permute-start.25 = (bf16[3,64,1024]{2,1,0:T(8,128)(2,1)S(1)}, bf16[3,64,1024]{2,1,0:T(8,128)(2,1)S(1)}, u32[]{:S(2)}, u32[]{:S(2)}) collective-permute-start(bf16[3,64,1024]{2,1,0:T(8,128)(2,1)S(1)} %pad_maximum_fusion.2.c0), channel_id=1, source_target_pairs={{0,3},{1,2},{2,1},{3,0},{4,7},{5,6},{6,5},{7,4},{8,11},{9,10},{10,... | collective-permute-start | bytes 1179656 | tf_op jit(solution)/shard_map/ppermute | solution.py:41
  74.7 20.5 %collective-permute-start.12 = (bf16[3,64,1024]{2,1,0:T(8,128)(2,1)S(1)}, bf16[3,64,1024]{2,1,0:T(8,128)(2,1)S(1)}, u32[]{:S(2)}, u32[]{:S(2)}) collective-permute-start(bf16[3,64,1024]{2,1,0:T(8,128)(2,1)S(1)} %pad_maximum_fusion.x0), channel_id=1, source_target_pairs={{0,1},{1,0},{2,3},{3,2},{4,5},{5,4},{6,7},{7,6},{8,9},{9,8},{10,11... | collective-permute-start | bytes 1179656 | tf_op jit(solution)/shard_map/ppermute | solution.py:41
  76.1 19.1 %collective-permute-start.13 = (bf16[3,64,1024]{2,1,0:T(8,128)(2,1)S(1)}, bf16[3,64,1024]{2,1,0:T(8,128)(2,1)S(1)}, u32[]{:S(2)}, u32[]{:S(2)}) collective-permute-start(bf16[3,64,1024]{2,1,0:T(8,128)(2,1)S(1)} %pad_maximum_fusion.x0), channel_id=1, source_target_pairs={{0,2},{1,3},{2,0},{3,1},{4,6},{5,7},{6,4},{7,5},{8,10},{9,11},{10,... | collective-permute-start | bytes 1179656 | tf_op jit(solution)/shard_map/ppermute | solution.py:41
  83.5 66.6 %collective-permute-start.35 = (f32[1,128]{1,0:T(1,128)S(1)}, f32[1,128]{1,0:T(1,128)S(1)}, u32[]{:S(2)}, u32[]{:S(2)}) collective-permute-start(f32[1,128]{1,0:T(1,128)S(1)} %bitcast.143), channel_id=1, source_target_pairs={{0,16},{16,0},{1,17},{17,1},{2,18},{18,2},{3,19},{19,3},{4,20},{20... | collective-permute-start | bytes 1544 | tf_op jit(solution)/shard_map/ppermute | solution.py:41
  87.0 63.3 %collective-permute-start.36 = (bf16[64,1152]{1,0:T(8,128)(2,1)S(1)}, bf16[64,1152]{1,0:T(8,128)(2,1)S(1)}, u32[]{:S(2)}, u32[]{:S(2)}) collective-permute-start(bf16[64,1152]{1,0:T(8,128)(2,1)S(1)} %bitcast.119), channel_id=1, source_target_pairs={{0,1},{1,0},{2,3},{3,2},{4,5},{5,4},{6,7},{7,6},{8,9},{9,8},{10,11... | collective-permute-start | bytes 442376 | tf_op jit(solution)/shard_map/ppermute | solution.py:41
  111.1 10.4 %collective-permute-start.38 = (bf16[64,1152]{1,0:T(8,128)(2,1)S(1)}, bf16[64,1152]{1,0:T(8,128)(2,1)S(1)}, u32[]{:S(2)}, u32[]{:S(2)}) collective-permute-start(bf16[64,1152]{1,0:T(8,128)(2,1)S(1)} %get-tuple-element.188), channel_id=1, source_target_pairs={{0,4},{4,0},{8,12},{12,8},{1,5},{5,1},{9,13},{13,9},{2,6},{6,2},{1... | collective-permute-start | bytes 442376 | tf_op jit(solution)/shard_map/ppermute | solution.py:41
  118.4 12.6 %collective-permute-start.28 = (bf16[3,64,1024]{2,1,0:T(8,128)(2,1)S(1)}, bf16[3,64,1024]{2,1,0:T(8,128)(2,1)S(1)}, u32[]{:S(2)}, u32[]{:S(2)}) collective-permute-start(bf16[3,64,1024]{2,1,0:T(8,128)(2,1)S(1)} %get-tuple-element.85), channel_id=1, source_target_pairs={{0,3},{1,2},{2,1},{3,0},{4,7},{5,6},{6,5},{7,4},{8,11},{9,10},{10,... | collective-permute-start | bytes 1179656 | tf_op jit(solution)/shard_map/ppermute | solution.py:41
  120.5 15.6 %collective-permute-start.27 = (bf16[3,64,1024]{2,1,0:T(8,128)(2,1)S(1)}, bf16[3,64,1024]{2,1,0:T(8,128)(2,1)S(1)}, u32[]{:S(2)}, u32[]{:S(2)}) collective-permute-start(bf16[3,64,1024]{2,1,0:T(8,128)(2,1)S(1)} %get-tuple-element.84), channel_id=1, source_target_pairs={{0,2},{1,3},{2,0},{3,1},{4,6},{5,7},{6,4},{7,5},{8,10},{9,11},{10,... | collective-permute-start | bytes 1179656 | tf_op jit(solution)/shard_map/ppermute | solution.py:41
  121.6 15.5 %collective-permute-start.26 = (bf16[3,64,1024]{2,1,0:T(8,128)(2,1)S(1)}, bf16[3,64,1024]{2,1,0:T(8,128)(2,1)S(1)}, u32[]{:S(2)}, u32[]{:S(2)}) collective-permute-start(bf16[3,64,1024]{2,1,0:T(8,128)(2,1)S(1)} %get-tuple-element.83), channel_id=1, source_target_pairs={{0,1},{1,0},{2,3},{3,2},{4,5},{5,4},{6,7},{7,6},{8,9},{9,8},{10,11... | collective-permute-start | bytes 1179656 | tf_op jit(solution)/shard_map/ppermute | solution.py:41
  131.0 20.3 %collective-permute-start.37 = (bf16[64,1152]{1,0:T(8,128)(2,1)S(1)}, bf16[64,1152]{1,0:T(8,128)(2,1)S(1)}, u32[]{:S(2)}, u32[]{:S(2)}) collective-permute-start(bf16[64,1152]{1,0:T(8,128)(2,1)S(1)} %bitcast.118), channel_id=1, source_target_pairs={{0,2},{1,3},{2,0},{3,1},{4,6},{5,7},{6,4},{7,5},{8,10},{9,11},{10,... | collective-permute-start | bytes 442376 | tf_op jit(solution)/shard_map/ppermute | solution.py:41
  136.2 10.4 %collective-permute-start.43 = (bf16[3,64,1152]{2,1,0:T(8,128)(2,1)S(1)}, bf16[3,64,1152]{2,1,0:T(8,128)(2,1)S(1)}, u32[]{:S(2)}, u32[]{:S(2)}) collective-permute-start(bf16[3,64,1152]{2,1,0:T(8,128)(2,1)S(1)} %copy-done.66), channel_id=1, source_target_pairs={{0,2},{1,3},{2,0},{3,1},{4,6},{5,7},{6,4},{7,5},{8,10},{9,11},{10,... | collective-permute-start | bytes 1327112 | tf_op jit(solution)/shard_map/ppermute | solution.py:41
  146.6 25.7 %collective-permute-start.31 = (bf16[64,1024]{1,0:T(8,128)(2,1)S(1)}, bf16[64,1024]{1,0:T(8,128)(2,1)S(1)}, u32[]{:S(2)}, u32[]{:S(2)}) collective-permute-start(bf16[64,1024]{1,0:T(8,128)(2,1)S(1)} %get-tuple-element.192), channel_id=1, source_target_pairs={{0,12},{4,8},{8,4},{12,0},{1,13},{5,9},{9,5},{13,1},{2,14},{6,10},... | collective-permute-start | bytes 393224 | tf_op jit(solution)/shard_map/ppermute | solution.py:41
  150.3 14.1 %collective-permute-start.45 = (bf16[64,1152]{1,0:T(8,128)(2,1)S(1)}, bf16[64,1152]{1,0:T(8,128)(2,1)S(1)}, u32[]{:S(2)}, u32[]{:S(2)}) collective-permute-start(bf16[64,1152]{1,0:T(8,128)(2,1)S(1)} %get-tuple-element.186), channel_id=1, source_target_pairs={{0,8},{4,12},{8,0},{12,4},{1,9},{5,13},{9,1},{13,5},{2,10},{6,14},... | collective-permute-start | bytes 442376 | tf_op jit(solution)/shard_map/ppermute | solution.py:41
  151.3 13.1 %collective-permute-start.46 = (bf16[64,1152]{1,0:T(8,128)(2,1)S(1)}, bf16[64,1152]{1,0:T(8,128)(2,1)S(1)}, u32[]{:S(2)}, u32[]{:S(2)}) collective-permute-start(bf16[64,1152]{1,0:T(8,128)(2,1)S(1)} %get-tuple-element.185), channel_id=1, source_target_pairs={{0,12},{4,8},{8,4},{12,0},{1,13},{5,9},{9,5},{13,1},{2,14},{6,10},... | collective-permute-start | bytes 442376 | tf_op jit(solution)/shard_map/ppermute | solution.py:41
  168.8 12.0 %collective-permute-start.30 = (bf16[64,1024]{1,0:T(8,128)(2,1)S(1)}, bf16[64,1024]{1,0:T(8,128)(2,1)S(1)}, u32[]{:S(2)}, u32[]{:S(2)}) collective-permute-start(bf16[64,1024]{1,0:T(8,128)(2,1)S(1)} %get-tuple-element.193), channel_id=1, source_target_pairs={{0,8},{4,12},{8,0},{12,4},{1,9},{5,13},{9,1},{13,5},{2,10},{6,14},... | collective-permute-start | bytes 393224 | tf_op jit(solution)/shard_map/ppermute | solution.py:41
  173.8 15.9 %collective-permute-start.8 = (bf16[1,64,1024]{2,1,0:T(8,128)(2,1)}, bf16[1,64,1024]{2,1,0:T(8,128)(2,1)S(1)}, u32[]{:S(2)}, u32[]{:S(2)}) collective-permute-start(bf16[1,64,1024]{2,1,0:T(8,128)(2,1)} %get-tuple-element.79), channel_id=1, source_target_pairs={{0,3},{1,2},{2,1},{3,0},{4,7},{5,6},{6,5},{7,4},{8,11},{9,10},{10,... | collective-permute-start | bytes 393224 | tf_op jit(solution)/shard_map/ppermute | solution.py:41
  175.2 14.6 %collective-permute-start.7 = (bf16[1,64,1024]{2,1,0:T(8,128)(2,1)}, bf16[1,64,1024]{2,1,0:T(8,128)(2,1)S(1)}, u32[]{:S(2)}, u32[]{:S(2)}) collective-permute-start(bf16[1,64,1024]{2,1,0:T(8,128)(2,1)} %get-tuple-element.78), channel_id=1, source_target_pairs={{0,2},{1,3},{2,0},{3,1},{4,6},{5,7},{6,4},{7,5},{8,10},{9,11},{10,... | collective-permute-start | bytes 393224 | tf_op jit(solution)/shard_map/ppermute | solution.py:41
  175.9 13.9 %collective-permute-start.6 = (bf16[1,64,1024]{2,1,0:T(8,128)(2,1)}, bf16[1,64,1024]{2,1,0:T(8,128)(2,1)}, u32[]{:S(2)}, u32[]{:S(2)}) collective-permute-start(bf16[1,64,1024]{2,1,0:T(8,128)(2,1)} %get-tuple-element.77), channel_id=1, source_target_pairs={{0,1},{1,0},{2,3},{3,2},{4,5},{5,4},{6,7},{7,6},{8,9},{9,8},{10,11... | collective-permute-start | bytes 393224 | tf_op jit(solution)/shard_map/ppermute | solution.py:41
  191.5 10.2 %collective-permute-start.32 = (bf16[64,1024]{1,0:T(8,128)(2,1)S(1)}, bf16[64,1024]{1,0:T(8,128)(2,1)S(1)}, u32[]{:S(2)}, u32[]{:S(2)}) collective-permute-start(bf16[64,1024]{1,0:T(8,128)(2,1)S(1)} %fusion.2.refs_0_), channel_id=1, source_target_pairs={{0,1},{1,0},{2,3},{3,2},{4,5},{5,4},{6,7},{7,6},{8,9},{9,8},{10,11... | collective-permute-start | bytes 393224 | tf_op jit(solution)/shard_map/ppermute | solution.py:41
  192.1 9.7 %collective-permute-start.33 = (bf16[64,1024]{1,0:T(8,128)(2,1)S(1)}, bf16[64,1024]{1,0:T(8,128)(2,1)S(1)}, u32[]{:S(2)}, u32[]{:S(2)}) collective-permute-start(bf16[64,1024]{1,0:T(8,128)(2,1)S(1)} %fusion.2.refs_0_), channel_id=1, source_target_pairs={{0,2},{1,3},{2,0},{3,1},{4,6},{5,7},{6,4},{7,5},{8,10},{9,11},{10,... | collective-permute-start | bytes 393224 | tf_op jit(solution)/shard_map/ppermute | solution.py:41
  195.0 10.2 %collective-permute-start.54 = (f32[8,1024]{1,0:T(8,128)S(1)}, f32[8,1024]{1,0:T(8,128)S(1)}, u32[]{:S(2)}, u32[]{:S(2)}) collective-permute-start(f32[8,1024]{1,0:T(8,128)S(1)} %add.126.refs_0_), channel_id=1, source_target_pairs={{0,4},{4,0},{8,12},{12,8},{1,5},{5,1},{9,13},{13,9},{2,6},{6,2},{1... | collective-permute-start | bytes 98312 | tf_op jit(solution)/shard_map/ppermute | solution.py:41
  201.7 20.4 %collective-permute-start.57 = (bf16[64,1024]{1,0:T(8,128)(2,1)S(1)}, bf16[64,1024]{1,0:T(8,128)(2,1)S(1)}, u32[]{:S(2)}, u32[]{:S(2)}) collective-permute-start(bf16[64,1024]{1,0:T(8,128)(2,1)S(1)} %get-tuple-element.103), channel_id=1, source_target_pairs={{0,1},{1,0},{2,3},{3,2},{4,5},{5,4},{6,7},{7,6},{8,9},{9,8},{10,11... | collective-permute-start | bytes 393224 | tf_op jit(solution)/shard_map/ppermute | solution.py:41
  201.8 20.7 %collective-permute-start.58 = (bf16[64,1024]{1,0:T(8,128)(2,1)S(1)}, bf16[64,1024]{1,0:T(8,128)(2,1)S(1)}, u32[]{:S(2)}, u32[]{:S(2)}) collective-permute-start(bf16[64,1024]{1,0:T(8,128)(2,1)S(1)} %get-tuple-element.104), channel_id=1, source_target_pairs={{0,2},{1,3},{2,0},{3,1},{4,6},{5,7},{6,4},{7,5},{8,10},{9,11},{10,... | collective-permute-start | bytes 393224 | tf_op jit(solution)/shard_map/ppermute | solution.py:41
  202.5 20.2 %collective-permute-start.59 = (bf16[64,1024]{1,0:T(8,128)(2,1)S(1)}, bf16[64,1024]{1,0:T(8,128)(2,1)S(1)}, u32[]{:S(2)}, u32[]{:S(2)}) collective-permute-start(bf16[64,1024]{1,0:T(8,128)(2,1)S(1)} %get-tuple-element.105), channel_id=1, source_target_pairs={{0,3},{1,2},{2,1},{3,0},{4,7},{5,6},{6,5},{7,4},{8,11},{9,10},{10,... | collective-permute-start | bytes 393224 | tf_op jit(solution)/shard_map/ppermute | solution.py:41
  205.2 17.8 %collective-permute-start.67 = (bf16[512,384]{1,0:T(8,128)(2,1)S(1)}, bf16[512,384]{1,0:T(8,128)(2,1)S(1)}, u32[]{:S(2)}, u32[]{:S(2)}) collective-permute-start(bf16[512,384]{1,0:T(8,128)(2,1)S(1)} %get-tuple-element.113), channel_id=1, source_target_pairs={{0,16},{16,0},{1,17},{17,1},{2,18},{18,2},{3,19},{19,3},{4,20},{20... | collective-permute-start | bytes 1179656 | tf_op jit(solution)/shard_map/ppermute | solution.py:41
  205.2 16.6 %collective-permute-start.56 = (f32[8,1024]{1,0:T(8,128)S(1)}, f32[8,1024]{1,0:T(8,128)S(1)}, u32[]{:S(2)}, u32[]{:S(2)}) collective-permute-start(f32[8,1024]{1,0:T(8,128)S(1)} %add.126.refs_0_), channel_id=1, source_target_pairs={{0,12},{4,8},{8,4},{12,0},{1,13},{5,9},{9,5},{13,1},{2,14},{6,10},... | collective-permute-start | bytes 98312 | tf_op jit(solution)/shard_map/ppermute | solution.py:41
  221.8 40.5 %collective-permute-start.71 = (bf16[8,1024,128]{2,1,0:T(8,128)(2,1)}, bf16[8,1024,128]{2,1,0:T(8,128)(2,1)}, u32[]{:S(2)}, u32[]{:S(2)}) collective-permute-start(bf16[8,1024,128]{2,1,0:T(8,128)(2,1)} %get-tuple-element.120), channel_id=1, source_target_pairs={{0,16},{16,0},{1,17},{17,1},{2,18},{18,2},{3,19},{19,3},{4,20},{20... | collective-permute-start | bytes 6291464 | tf_op jit(solution)/shard_map/ppermute | solution.py:41
  222.1 44.4 %collective-permute-start.72 = (bf16[8,1024,128]{2,1,0:T(8,128)(2,1)}, bf16[8,1024,128]{2,1,0:T(8,128)(2,1)}, u32[]{:S(2)}, u32[]{:S(2)}) collective-permute-start(bf16[8,1024,128]{2,1,0:T(8,128)(2,1)} %get-tuple-element.121), channel_id=1, source_target_pairs={{0,16},{16,0},{1,17},{17,1},{2,18},{18,2},{3,19},{19,3},{4,20},{20... | collective-permute-start | bytes 6291464 | tf_op jit(solution)/shard_map/ppermute | solution.py:41
  222.5 18.7 %collective-permute-start.63 = (bf16[512,512]{1,0:T(8,128)(2,1)S(1)}, bf16[512,512]{1,0:T(8,128)(2,1)S(1)}, u32[]{:S(2)}, u32[]{:S(2)}) collective-permute-start(bf16[512,512]{1,0:T(8,128)(2,1)S(1)} %get-tuple-element.109), channel_id=1, source_target_pairs={{0,16},{16,0},{1,17},{17,1},{2,18},{18,2},{3,19},{19,3},{4,20},{20... | collective-permute-start | bytes 1572872 | tf_op jit(solution)/shard_map/ppermute | solution.py:41
  240.1 30.3 %collective-permute-start.73 = (bf16[8,128,1024]{2,1,0:T(8,128)(2,1)}, bf16[8,128,1024]{2,1,0:T(8,128)(2,1)}, u32[]{:S(2)}, u32[]{:S(2)}) collective-permute-start(bf16[8,128,1024]{2,1,0:T(8,128)(2,1)} %get-tuple-element.122), channel_id=1, source_target_pairs={{0,16},{16,0},{1,17},{17,1},{2,18},{18,2},{3,19},{19,3},{4,20},{20... | collective-permute-start | bytes 6291464 | tf_op jit(solution)/shard_map/ppermute | solution.py:41
  245.0 12.2 %collective-permute-start.65 = (bf16[128,512]{1,0:T(8,128)(2,1)}, bf16[128,512]{1,0:T(8,128)(2,1)}, u32[]{:S(2)}, u32[]{:S(2)}) collective-permute-start(bf16[128,512]{1,0:T(8,128)(2,1)} %get-tuple-element.177), channel_id=1, source_target_pairs={{0,8},{4,12},{8,0},{12,4},{1,9},{5,13},{9,1},{13,5},{2,10},{6,14},... | collective-permute-start | bytes 393224 | tf_op jit(solution)/shard_map/ppermute | solution.py:41
  (93 other events, 814.1 us)

commit v3 on v2

v3 whole, which is shorter than its diff:
```python
import functools

import jax
import jax.numpy as jnp
import numpy as np
from jax import lax
from jax.experimental import pallas as pl
from jax.experimental.pallas import tpu as pltpu
from jax.sharding import PartitionSpec as P

HD = 64
TOP = 8
EPS = 1e-06
ROPE_BASE = 10000.0
MASKED = -1e30
BF = jnp.bfloat16
F32 = jnp.float32
FEW = 8
LANES = 128
MIB = 1 << 20


def dot(a, b, dims):
    return lax.dot_general(a, b, (dims, ((), ())), preferred_element_type=F32)


def nn(a, b):
    return dot(a, b, ((1,), (0,)))


def nt(a, b):
    return dot(a, b, ((1,), (1,)))


def tn(a, b):
    return dot(a, b, ((0,), (0,)))


def swap(x, axis, distance):
    size = lax.axis_size(axis)
    return lax.ppermute(x, axis, [(i, i ^ distance) for i in range(size)])


def spread(x, axis):
    size = lax.axis_size(axis)
    if size <= FEW:
        return [swap(x, axis, r) for r in range(1, size)]
    whole = lax.all_gather(x, axis)
    order = jnp.arange(1, size) ^ lax.axis_index(axis)
    return list(jnp.take(whole, order, axis=0))


def deal(parts, axis):
    size = lax.axis_size(axis)
    if size <= FEW:
        return [swap(part, axis, r + 1) for r, part in enumerate(parts)]
    order = jnp.arange(size) ^ lax.axis_index(axis)
    whole = jnp.take(jnp.stack([parts[0], *parts]), order, axis=0)
    back = lax.all_to_all(whole, axis, 0, 0, tiled=True)
    return list(jnp.take(back, order, axis=0)[1:])


def rope_tables(seq_len):
    half = HD // 2
    frequency = ROPE_BASE ** (-(np.arange(half, dtype=np.float32) * 2.0) / HD)
    angles = np.arange(seq_len, dtype=np.float32)[:, None] * frequency[None, :].astype(np.float32)
    cosine, sine = np.cos(angles), np.sin(angles)
    heads = LANES // HD
    return (
        np.tile(cosine, (1, 2 * heads)).astype(np.float32),
        np.tile(np.concatenate([-sine, sine], axis=1), (1, heads)).astype(np.float32),
    )


def lane_of(shape):
    return lax.broadcasted_iota(jnp.int32, shape, 1)


def halves_swapped(x):
    first = lane_of(x.shape) % HD < HD // 2
    half = HD // 2
    return jnp.where(first, pltpu.roll(x, LANES - half, 1), pltpu.roll(x, half, 1))


def low_high(x, head):
    other = pltpu.roll(x.astype(F32), HD, 1).astype(x.dtype)
    low = lane_of(x.shape) < HD
    zero = jnp.zeros_like(x)
    at_low, at_high = (x, other) if head == 0 else (other, x)
    return jnp.where(low, at_low, zero), jnp.where(low, zero, at_high)


def causal(scores):
    rows = lax.broadcasted_iota(jnp.int32, scores.shape, 0)
    return lane_of(scores.shape) <= rows


def shape(dims, kind):
    return jax.ShapeDtypeStruct(dims, kind)


def whole_block(dims):
    return pl.BlockSpec(dims, lambda i: (0,) * len(dims))


def call(kernel, outs, operands, name, places="", out_places="", scratch=(), limit=40, flops=0):
    kinds = {"s": pltpu.SMEM, "v": pltpu.VMEM}

    def spec(place, x):
        if not isinstance(place, str):
            return place
        if place == "b":
            return whole_block(x.shape)
        return pl.BlockSpec(memory_space=kinds[place])

    places = [*places] + ["v"] * (len(operands) - len(places))
    out_places = [*out_places] + ["v"] * (len(outs) - len(out_places))
    return pl.pallas_call(
        kernel,
        grid=(1,),
        out_shape=outs,
        in_specs=[spec(p, x) for p, x in zip(places, operands)],
        out_specs=[spec(p, x) for p, x in zip(out_places, outs)],
        scratch_shapes=list(scratch),
        compiler_params=pltpu.CompilerParams(vmem_limit_bytes=limit * MIB),
        cost_estimate=pl.CostEstimate(flops=int(100.0*(flops)), bytes_accessed=0, transcendentals=0),
        name=name,
    )(*operands)


def tied(first, then):
    return lax.optimization_barrier((first, then))


def pieces_kernel(me_ref, cot_ref, routes_ref, router_ref, both_ref, c1, c2, router_out, held):
    rows, width = c1.shape[0], cot_ref.shape[1]
    eye = lax.broadcasted_iota(jnp.int32, (TOP, LANES), 0) == lane_of((TOP, LANES))
    held[...] = tn(routes_ref[...].astype(F32).astype(BF), eye.astype(F32).astype(BF))
    for r, c in enumerate((both_ref.at[0], c1, c2, both_ref.at[1])):
        start = pl.multiple_of((me_ref[0] ^ r) * rows, rows)
        c[:, :width] = cot_ref[pl.ds(start, rows), :]
        c[:, width:] = held[pl.ds(start, rows), :].astype(BF)
    router_out[...] = jnp.zeros(router_out.shape, BF)
    router_out[: router_ref.shape[0], :] = router_ref[...]


def sorted_cots_kernel(own_ref, *refs):
    others, (far_ref, first_ref, last_ref) = refs[:-3], refs[-3:]
    for i, x in enumerate((own_ref, *others)):
        first_ref[i] = x[0]
        last_ref[i] = x[1]
        if i:
            far_ref[i - 1] = x[0]


def attend_kernel(
    me_ref, x_ref, gain_ref, wq_ref, wk_ref, wv_ref, wo_ref, cos_ref, sin_ref, *refs
):
    n_ref, q_ref, k_ref, v_ref, o_ref, lse_ref, xq_ref = refs[:7]
    parts, whole = refs[7:-1], refs[-1]
    rows, width = xq_ref.shape
    starts = [pl.multiple_of((me_ref[0] ^ r) * rows, rows) for r in range(4)]
    xq_ref[...] = x_ref[pl.ds(starts[0], rows), :]
    x = x_ref[...].astype(F32)
    inv = lax.rsqrt(jnp.mean(x * x, axis=-1, keepdims=True) + EPS)
    n = (x * inv * gain_ref[...]).astype(BF)
    n_ref[...] = n
    cosine, sine = cos_ref[...], sin_ref[...]
    q, k = nn(n, wq_ref[...]), nn(n, wk_ref[...])
    v_ref[...] = nn(n, wv_ref[...]).astype(BF)
    for at in range(0, q.shape[1], LANES):
        tile = q[:, at : at + LANES]
        q_ref[:, at : at + LANES] = (tile * cosine + halves_swapped(tile) * sine).astype(BF)
    for at in range(0, k.shape[1], LANES):
        tile = k[:, at : at + LANES]
        k_ref[:, at : at + LANES] = (tile * cosine + halves_swapped(tile) * sine).astype(BF)
    lse_all = jnp.zeros(lse_ref.shape, F32)
    for head in range(q.shape[1] // LANES):
        at = head // 2 * LANES
        keys = low_high(k_ref[:, at : at + LANES], head % 2)
        values = low_high(v_ref[:, at : at + LANES], head % 2)
        pair = q_ref[:, head * LANES : (head + 1) * LANES]
        mixed = 0.0
        for g in range(2):
            s = nt(pair, keys[g]) * HD ** (-0.5)
            s = jnp.where(causal(s), s, MASKED)
            peak = jnp.max(s, axis=-1, keepdims=True)
            e = jnp.exp(s - peak)
            total = jnp.sum(e, axis=-1, keepdims=True)
            mixed = mixed + nn((e / total).astype(BF), values[g])
            lse = peak + jnp.log(total)
            lse_all = jnp.where(lane_of(lse_all.shape) == 2 * head + g, lse, lse_all)
        o_ref[:, head * LANES : (head + 1) * LANES] = mixed.astype(BF)
    lse_ref[...] = lse_all
    whole[...] = nn(o_ref[...], wo_ref[...])
    for start, part in zip(starts, parts):
        part[...] = whole[pl.ds(start, rows), :].astype(part.dtype)


def norm_two_kernel(x_ref, gain_ref, own_ref, *refs):
    others, (h_ref, n_ref) = refs[:-2], refs[-2:]
    attn = own_ref[...]
    for other in others:
        attn = attn + other[...].astype(F32)
    h = x_ref[...].astype(F32) + attn
    inv = lax.rsqrt(jnp.mean(h * h, axis=-1, keepdims=True) + EPS)
    h_ref[...] = h
    n_ref[...] = (h * inv * gain_ref[...]).astype(BF)


def together_kernel(*refs):
    pieces, out = refs[:-1], refs[-1]
    at = 0
    for piece in pieces:
        if len(piece.shape) == 2:
            out[at] = piece[...]
            at += 1
        else:
            out[at : at + piece.shape[0]] = piece[...]
            at += piece.shape[0]


def together(pieces):
    count = sum(1 if x.ndim == 2 else x.shape[0] for x in pieces)
    return call(
        together_kernel, [shape((count, *pieces[0].shape[-2:]), pieces[0].dtype)], pieces, "together"
    )[0]


def router_of(rows, router_ref, routes, experts):
    z = nt(rows, router_ref[...])
    lane = lane_of(z.shape)
    z = jnp.where(lane < experts, z, MASKED)
    e = jnp.exp(z - jnp.max(z, axis=-1, keepdims=True))
    probs = e / jnp.sum(e, axis=-1, keepdims=True)
    chosen = chosen_of(lane, routes)
    zc = jnp.where(chosen, z, MASKED)
    ec = jnp.where(chosen, jnp.exp(zc - jnp.max(zc, axis=-1, keepdims=True)), 0.0)
    return probs, ec / jnp.sum(ec, axis=-1, keepdims=True)


def chosen_of(lane, routes):
    place, named = lane.astype(F32), routes.astype(F32)
    chosen = place == named[:, 0:1]
    for k in range(1, TOP):
        chosen = chosen | (place == named[:, k : k + 1])
    return chosen


def weights_kernel(wg_ref, wu_ref, out_ref):
    hidden = wg_ref.shape[2]
    out_ref[:, :hidden] = wg_ref[0]
    out_ref[:, hidden:] = wu_ref[0]


def gate_up_weights(w_gate, w_up):
    local, width, hidden = w_gate.shape
    block = pl.BlockSpec((1, width, hidden), lambda e: (e, 0, 0))
    return pl.pallas_call(
        weights_kernel,
        grid=(local,),
        in_specs=[block, block],
        out_specs=pl.BlockSpec((width, 2 * hidden), lambda e: (0, e)),
        out_shape=shape((width, 2 * hidden * local), BF),
        compiler_params=pltpu.CompilerParams(vmem_limit_bytes=30 * MIB),
        cost_estimate=pl.CostEstimate(flops=int(100.0*(0)), bytes_accessed=4 * w_gate.size * 2, transcendentals=0),
        name="gate_up_weights",
    )(w_gate, w_up)


def experts_kernel(experts, base_ref, x_ref, c_ref, router_ref, wcat, wd_ref, dgu_ref, hg_ref, d_ref, m_ref, count_ref):
    hidden = LANES
    pair = 2 * hidden
    width = x_ref.shape[1]
    x = x_ref[...]
    routes = c_ref[:, width:]
    named = chosen_of(lane_of(routes.shape), routes).astype(F32)
    count_ref[0] = jnp.broadcast_to(jnp.sum(named, axis=0, keepdims=True), count_ref.shape[1:])
    _, gates = router_of(x, router_ref, routes, experts)
    lane = lane_of(gates.shape)
    dots = jnp.zeros(gates.shape, F32)
    for e in range(hg_ref.shape[1] // hidden):
        mine = lane == base_ref[0] + e
        g = jnp.sum(jnp.where(mine, gates, 0.0), axis=-1, keepdims=True)
        both = nn(x, wcat[:, e * pair : (e + 1) * pair])
        v = nt(c_ref[:, :width], wd_ref[e * hidden : (e + 1) * hidden, :])
        gate, up = both[:, :hidden], both[:, hidden:]
        sig = 1.0 / (1.0 + jnp.exp(-gate))
        act = gate * sig
        hid = act * up
        dots = jnp.where(mine, jnp.sum(hid * v, axis=-1, keepdims=True), dots)
        gv = g * v
        hg_ref[:, e * hidden : (e + 1) * hidden] = (g * hid).astype(BF)
        d_gate = gv * up * sig * (1.0 + gate * (1.0 - sig))
        dgu_ref[:, e * pair : e * pair + hidden] = d_gate.astype(BF)
        dgu_ref[:, e * pair + hidden : (e + 1) * pair] = (gv * act).astype(BF)
    d_ref[:, width:] = dots.astype(d_ref.dtype)
    step = 256
    for at in range(0, width, step):
        d_ref[:, at : at + step] = nt(dgu_ref[...], wcat[at : at + step, :]).astype(d_ref.dtype)
    m_ref[...] = nn(hg_ref[...], wd_ref[...]).astype(m_ref.dtype)


def run_experts(experts, base, x, c, router, wcat, down_flat, kind):
    count, rows, width = x.shape
    inner = down_flat.shape[0]
    wide = width + LANES
    total = count * rows
    step = min(total, 256)
    per = lambda w: pl.BlockSpec((step, w), lambda i: (i, 0))
    resident = pl.BlockSpec(memory_space=pltpu.VMEM)
    dgu, hid, d, m, counts = pl.pallas_call(
        functools.partial(experts_kernel, experts),
        grid=(total // step,),
        in_specs=[pl.BlockSpec(memory_space=pltpu.SMEM), per(width), per(wide)] + [resident] * 3,
        out_specs=[per(2 * inner), per(inner), per(wide), per(width)]
        + [pl.BlockSpec((1, 8, LANES), lambda i: (i, 0, 0))],
        out_shape=[
            shape((total, 2 * inner), BF),
            shape((total, inner), BF),
            shape((total, wide), kind),
            shape((total, width), kind),
            shape((total // step, 8, LANES), F32),
        ],
        compiler_params=pltpu.CompilerParams(vmem_limit_bytes=30 * MIB),
        cost_estimate=pl.CostEstimate(flops=int(100.0*(12 * total * width * inner)), bytes_accessed=0, transcendentals=0),
        name="experts",
    )(base, x.reshape(total, width), c.reshape(total, wide), router, wcat, down_flat)
    return dgu, hid, d.reshape(count, rows, wide), m.reshape(count, rows, width), counts


def split_sum_kernel(count, near, *refs):
    ins, outs = refs[:count], refs[count:]
    for s in range(ins[0].shape[0]):
        total = ins[0][s].astype(F32)
        for x in ins[1:]:
            total = total + x[s].astype(F32)
        outs[s][...] = total.astype(outs[s].dtype)


def split_sum(arrays, name):
    count, *dims = arrays[0].shape
    outs = [shape(dims, F32)] + [shape(dims, BF)] * (count - 1)
    return call(functools.partial(split_sum_kernel, len(arrays), True), outs, arrays, name)


def add_kernel(*refs):
    pieces, out = refs[:-1], refs[-1]
    total = pieces[0][...].astype(F32)
    for piece in pieces[1:]:
        total = total + piece[...].astype(F32)
    out[...] = total.astype(out.dtype)


def added(pieces, kind, name):
    return call(add_kernel, [shape(pieces[0].shape, kind)], pieces, name)[0]


def grads_kernel(*refs):
    ns, dgus, hs, cs = (refs[4 * i : 4 * i + 4] for i in range(4))
    out_ref = refs[16]
    hidden, width = hs[0].shape[1], ns[0].shape[1]
    both, down = 0.0, 0.0
    for n, dgu, h, c in zip(ns, dgus, hs, cs):
        both = both + tn(n[...], dgu[...])
        down = down + tn(h[...], c[:, :width])
    out_ref[0, :width, :] = both[:, :hidden].astype(BF)
    out_ref[0, width : 2 * width, :] = both[:, hidden:].astype(BF)
    for at in range(0, width, hidden):
        out_ref[0, 2 * width + at : 2 * width + at + hidden, :] = down[:, at : at + hidden].astype(BF)


def run_grads(n, dgu, h, c, local, hidden):
    width = n[0].shape[-1]
    flat = lambda xs: [x.reshape(-1, x.shape[-1]) for x in xs]
    n, c = flat(n), flat(c)
    whole = lambda xs: [pl.BlockSpec(x.shape, lambda e: (0, 0)) for x in xs]
    cols = lambda xs, w: [pl.BlockSpec((x.shape[0], w), lambda e: (0, e)) for x in xs]
    few = n[0].shape[0] <= 512
    return pl.pallas_call(
        grads_kernel,
        grid=(local,),
        in_specs=whole(n) + cols(dgu, 2 * hidden) + cols(h, hidden) + whole(c),
        out_specs=pl.BlockSpec((1, 3 * width, hidden), lambda e: (e, 0, 0)),
        out_shape=shape((local, 3 * width, hidden), BF),
        compiler_params=pltpu.CompilerParams(vmem_limit_bytes=(32 if few else 58) * MIB),
        cost_estimate=pl.CostEstimate(flops=int(100.0*(24 * n[0].size * hidden * local)), bytes_accessed=0, transcendentals=0),
        name="expert_grads",
    )(*n, *dgu, *h, *c)


def both_copies_kernel(mine_ref, other_ref, gate_ref, up_ref, down_ref):
    width, hidden = gate_ref.shape[1:]

    def total(at, count):
        rows = pl.ds(at, count)
        return mine_ref[0, rows, :].astype(F32) + other_ref[0, rows, :].astype(F32)

    gate_ref[0] = total(0, width)
    up_ref[0] = total(width, width)
    for at in range(0, width, hidden):
        down_ref[0, :, at : at + hidden] = total(2 * width + at, hidden)


def both_copies(mine, other):
    local, rows, hidden = mine.shape
    width = rows // 3
    block = lambda *dims: pl.BlockSpec((1, *dims), lambda e: (e, 0, 0))
    return pl.pallas_call(
        both_copies_kernel,
        grid=(local,),
        in_specs=[block(rows, hidden)] * 2,
        out_specs=[block(width, hidden), block(width, hidden), block(hidden, width)],
        out_shape=[
            shape((local, width, hidden), F32),
            shape((local, width, hidden), F32),
            shape((local, hidden, width), F32),
        ],
        compiler_params=pltpu.CompilerParams(vmem_limit_bytes=58 * MIB),
        cost_estimate=pl.CostEstimate(flops=int(100.0*(0)), bytes_accessed=8 * mine.size, transcendentals=0),
        name="both_copies",
    )(mine, other)


def norm_back_kernel(experts, count, h_ref, n_ref, gain_ref, router_ref, bal_ref, cot_ref, *refs):
    sums, (wide_ref, dh_ref, small_ref) = refs[:count], refs[count:]
    near = sums[0][...].astype(F32)
    for other in sums[1:]:
        near = near + other[...].astype(F32)
    rows, width = h_ref.shape
    dots = near[:, width:]
    probs, gates = router_of(n_ref[...], router_ref, cot_ref[0, :, width:], experts)
    bal = bal_ref[...]
    d_chosen = gates * (dots - jnp.sum(gates * dots, axis=-1, keepdims=True))
    dz = probs * (bal - jnp.sum(probs * bal, axis=-1, keepdims=True)) + d_chosen
    dz = dz.astype(BF)
    wide_ref[:, width:] = dz
    dn = near[:, :width] + nn(dz, router_ref[...])
    h = h_ref[...]
    inv = lax.rsqrt(jnp.mean(h * h, axis=-1, keepdims=True) + EPS)
    u = gain_ref[...] * dn
    dy = cot_ref[0, :, :width].astype(F32)
    dh = dy + inv * u - h * (inv * inv * inv * jnp.mean(u * h, axis=-1, keepdims=True))
    dh_ref[...] = dh
    wide_ref[:, :width] = dh.astype(BF)
    small_ref[...] = jnp.zeros(small_ref.shape, F32)
    small_ref[1:2, :] = jnp.sum(dn * h * inv, axis=0, keepdims=True)
    small_ref[2:3, : probs.shape[1]] = jnp.sum(probs, axis=0, keepdims=True)


def attend_back_kernel(
    me_ref, w0, w1, w2, w3, x_ref, q_ref, k_ref, v_ref, lse_ref, wq_ref, wk_ref, wv_ref, wo_ref, cos_ref, sin_ref,
    small_in, wide_ref, dq_ref, p0, p1, p2, p3, do_ref, whole, small_ref
):
    rows = w0.shape[0]
    width = x_ref.shape[1]
    for r, piece in enumerate((w0, w1, w2, w3)):
        start = pl.multiple_of((me_ref[0] ^ r) * rows, rows)
        wide_ref[pl.ds(start, rows), :] = piece[...]
    do_ref[...] = nt(wide_ref[:, :width], wo_ref[...]).astype(BF)
    cosine, sine = cos_ref[...], sin_ref[...]
    scale = HD ** (-0.5)
    heads, keys_wide = q_ref.shape[1], k_ref.shape[1]
    dk_tiles = [0.0] * (keys_wide // LANES)
    dv_tiles = [0.0] * (keys_wide // LANES)

    def back(tile):
        return (tile * cosine - halves_swapped(tile) * sine).astype(BF)

    for head in range(heads // LANES):
        at = head // 2 * LANES
        side = head % 2
        keys = low_high(k_ref[:, at : at + LANES], side)
        values = low_high(v_ref[:, at : at + LANES], side)
        pair = q_ref[:, head * LANES : (head + 1) * LANES]
        grad = do_ref[:, head * LANES : (head + 1) * LANES]
        dq = 0.0
        dk, dv = [], []
        for g in range(2):
            s = nt(pair, keys[g]) * scale
            lse = lse_ref[:, 2 * head + g : 2 * head + g + 1]
            p = jnp.where(causal(s), jnp.exp(s - lse), 0.0)
            dp = nt(grad, values[g])
            ds = (p * (dp - jnp.sum(p * dp, axis=-1, keepdims=True))).astype(BF)
            dq = dq + nn(ds, keys[g])
            dk.append(tn(ds, pair))
            dv.append(tn(p.astype(BF), grad))
        dq_ref[:, head * LANES : (head + 1) * LANES] = back(dq * scale)
        mine = lane_of(dk[0].shape) < HD
        if side == 0:
            dk_sum = jnp.where(mine, dk[0] + pltpu.roll(dk[1], HD, 1), 0.0)
            dv_sum = jnp.where(mine, dv[0] + pltpu.roll(dv[1], HD, 1), 0.0)
        else:
            dk_sum = jnp.where(mine, 0.0, pltpu.roll(dk[0], HD, 1) + dk[1])
            dv_sum = jnp.where(mine, 0.0, pltpu.roll(dv[0], HD, 1) + dv[1])
        dk_tiles[head // 2] = dk_tiles[head // 2] + dk_sum
        dv_tiles[head // 2] = dv_tiles[head // 2] + dv_sum
    for i, tile in enumerate(dk_tiles):
        at = heads + i * LANES
        dq_ref[:, at : at + LANES] = back(tile * scale)
    for i, tile in enumerate(dv_tiles):
        at = heads + keys_wide + i * LANES
        dq_ref[:, at : at + LANES] = tile.astype(BF)
    dn = nt(dq_ref[:, :heads], wq_ref[...])
    dn = dn + nt(dq_ref[:, heads : heads + keys_wide], wk_ref[...])
    whole[...] = dn + nt(dq_ref[:, heads + keys_wide :], wv_ref[...])
    x = x_ref[...].astype(F32)
    inv = lax.rsqrt(jnp.mean(x * x, axis=-1, keepdims=True) + EPS)
    small_ref[...] = small_in[...]
    small_ref[0:1, :] = jnp.sum(whole[...] * x * inv, axis=0, keepdims=True)
    small = small_ref[...]
    high = small.astype(BF)
    both = jnp.concatenate([high.astype(F32), small - high.astype(F32)], axis=0).astype(BF)
    for r, part in enumerate((p0, p1, p2, p3)):
        start = pl.multiple_of((me_ref[0] ^ r) * rows, rows)
        part[:rows, :] = whole[pl.ds(start, rows), :].astype(part.dtype)
        part[rows:, :] = both.astype(part.dtype)


def dense_kernel(me_ref, a0, a1, a2, a3, wide_ref, o_ref, n_ref, dq_ref, kept_ref, sent_ref, two_ref, whole):
    rows, width = a0.shape[1:]
    for r, piece in enumerate((a0, a1, a2, a3)):
        start = pl.multiple_of((me_ref[1] ^ r) * rows, rows)
        two_ref[pl.ds(start, rows), :] = piece[0]
    columns, heads = dq_ref.shape[1], o_ref.shape[1]
    whole[:, :columns] = tn(n_ref[...], dq_ref[...])
    whole[:, columns : columns + heads] = tn(wide_ref[:, :width], o_ref[...])
    whole[:, columns + heads :] = tn(two_ref[...], wide_ref[:, width:])
    half = kept_ref.shape[0]
    kept_ref[...] = whole[pl.ds(pl.multiple_of(me_ref[0] * half, half), half), :]
    sent_ref[...] = whole[pl.ds(pl.multiple_of((1 - me_ref[0]) * half, half), half), :].astype(BF)


def input_grad_kernel(me_ref, x_ref, gain_ref, dh_ref, *refs):
    parts, (ig_ref, small_ref, held) = refs[:-3], refs[-3:]
    rows = dh_ref.shape[0]
    x = x_ref[...].astype(F32)
    inv = lax.rsqrt(jnp.mean(x * x, axis=-1, keepdims=True) + EPS)
    dn = parts[0][:rows, :].astype(F32)
    for part in parts[1:]:
        dn = dn + part[:rows, :].astype(F32)
    u = gain_ref[...] * dn
    ig = dh_ref[...] + inv * u - x * (inv * inv * inv * jnp.mean(u * x, axis=-1, keepdims=True))
    ig_ref[...] = ig.astype(BF)
    for r, part in enumerate(parts):
        both = part[rows:, :].astype(F32)
        held[me_ref[0] ^ r] = both[:8] + both[8:]
    total = held[0]
    for i in range(1, len(parts)):
        total = total + held[i]
    small_ref[...] = total


def natural_kernel(me_ref, *refs):
    pieces, out = refs[:-1], refs[-1]
    rows = pieces[0].shape[0]
    for r, piece in enumerate(pieces):
        start = pl.multiple_of((me_ref[0] ^ r) * rows, rows)
        out[pl.ds(start, rows), :] = piece[...].astype(out.dtype)


def ordered_sum_kernel(me_ref, *refs):
    pieces, out, held = refs[:-2], refs[-2], refs[-1]
    for r, piece in enumerate(pieces):
        held[me_ref[0] ^ r] = piece[...]
    total = held[0]
    for i in range(1, len(pieces)):
        total = total + held[i]
    out[...] = total


def ordered_sum(me, pieces):
    return call(
        ordered_sum_kernel,
        [shape(pieces[0].shape, F32)],
        (me, *pieces),
        "ordered_sum",
        "s",
        scratch=[pltpu.VMEM((len(pieces), *pieces[0].shape), F32)],
    )[0]


def kept_and_dealt_kernel(me_ref, kept_ref, got_ref, *outs):
    rows = outs[0].shape[0]
    for r, out in enumerate(outs):
        start = pl.multiple_of((me_ref[0] ^ r) * rows, rows)
        at = pl.ds(start, rows)
        out[...] = (kept_ref[at, :] + got_ref[at, :].astype(F32)).astype(out.dtype)


def dense_sum_kernel(mine_ref, *refs):
    others, (q_ref, k_ref, v_ref, o_ref, r_ref) = refs[:-5], refs[-5:]
    total = mine_ref[...]
    for other in others:
        total = total + other[...].astype(F32)
    at = 0
    for out in (q_ref, k_ref, v_ref):
        out[...] = total[:, at : at + out.shape[1]]
        at += out.shape[1]
    o_ref[...] = total[:, at : at + o_ref.shape[0]].T
    at += o_ref.shape[0]
    r_ref[...] = total[:, at : at + r_ref.shape[1]]


def on_device(
    tokens,
    routes,
    gain_first,
    w_query,
    w_key,
    w_value,
    w_output,
    gain_second,
    w_router,
    w_gate,
    w_up,
    w_down,
    cotangent,
):
    seq_len, width = tokens.shape
    experts = w_router.shape[1]
    local, _, hidden = w_gate.shape
    tensor_size = lax.axis_size("tensor")
    expert_size = lax.axis_size("expert")
    dp_size = lax.axis_size("dp")
    token_count = seq_len * dp_size * expert_size
    rows = seq_len // tensor_size
    wide_width = width + LANES
    last = tensor_size - 1
    around = range(1, tensor_size)
    t_me, e_me, d_me = lax.axis_index("tensor"), lax.axis_index("expert"), lax.axis_index("dp")
    t_at = t_me.astype(jnp.int32).reshape(1)
    e_at = e_me.astype(jnp.int32).reshape(1)
    base = (e_me * local).astype(jnp.int32).reshape(1)
    d_at = jnp.stack([d_me, t_me]).astype(jnp.int32)
    cosine, sine = rope_tables(seq_len)
    gain_one, gain_two = gain_first[None], gain_second[None]
    down_flat = w_down.reshape(local * hidden, width)

    cot_ends, cot_one, cot_two, router = call(
        pieces_kernel,
        [shape((2, rows, wide_width), BF)]
        + [shape((rows, wide_width), BF)] * 2
        + [shape((LANES, width), BF)],
        (t_at, cotangent, routes.T, w_router.T),
        "pieces",
        "sbbb",
        scratch=[pltpu.VMEM((seq_len, LANES), F32)],
        limit=58,
    )
    cot_got = spread(cot_ends, "expert")

    heads, keys_wide = w_query.shape[1], w_key.shape[1]
    n_one, q, k, v, o, lse, xq, *rest = call(
        attend_kernel,
        [
            shape((seq_len, width), BF),
            shape((seq_len, heads), BF),
            shape((seq_len, keys_wide), BF),
            shape((seq_len, keys_wide), BF),
            shape((seq_len, heads), BF),
            shape((seq_len, LANES), F32),
            shape((rows, width), BF),
        ]
        + [shape((rows, width), F32)]
        + [shape((rows, width), BF)] * last,
        (t_at, tokens, gain_one, w_query, w_key, w_value, w_output, cosine, sine),
        "attend",
        "s" + "b" * 8,
        "bbbbbbv",
        scratch=[pltpu.VMEM((seq_len, width), F32)],
        limit=58,
        flops=2 * seq_len * width * 4 * heads,
    )
    parts = rest
    got = [swap(parts[r], "tensor", r) for r in around]
    h, n_two = call(
        norm_two_kernel,
        [shape((rows, width), F32), shape((rows, width), BF)],
        (xq, gain_two, parts[0], *got),
        "norm_two",
        "vb",
        "vv",
    )

    wcat = gate_up_weights(w_gate, w_up)
    count = expert_size
    cot_far, cot_first, cot_last = call(
        sorted_cots_kernel,
        [shape((n, rows, wide_width), BF) for n in (count - 1, count, count)],
        (cot_ends, *cot_got),
        "sorted_cots",
    )
    cot_middle = [swap(cot_far, "tensor", r) for r in range(1, last)]
    cots = [
        cot_first,
        together([cot_one, cot_middle[0]]),
        together([cot_two, cot_middle[1]]),
        cot_last,
    ]

    two_got = []
    for r in range(1, expert_size):
        if expert_size <= FEW:
            cot_got[r - 1], two = tied(cot_got[r - 1], n_two)
            two_got.append(swap(two, "expert", r))
    if expert_size > FEW:
        two_got = spread(n_two, "expert")
    first = together([n_two, *two_got])
    twos = [first] + [swap(first, "tensor", r) for r in range(1, last)]
    _, late = tied(cot_middle, first)
    twos.append(swap(late, "tensor", last))

    run = functools.partial(
        run_experts, experts, base, router=router, wcat=wcat, down_flat=down_flat
    )
    made = [run(twos[0], cots[0], kind=F32)]
    got = []
    for r in around:
        held, (two, cot) = tied(made[-1], (twos[r], cots[r]))
        made[-1] = held
        made.append(run(two, cot, kind=BF))
        got.append(swap(made[-1][2], "tensor", r))
    dgus, hids, ds, moes, counts = zip(*made)
    grads = run_grads(twos, dgus, hids, cots, local, hidden)
    counts = sum(jnp.sum(x[:, :1], axis=0) for x in counts)
    counts = counts + swap(counts, "dp", 1)
    balance = experts * (counts / (token_count * TOP)) / token_count
    grads, got = tied(grads, got)
    got, moes = tied(got, moes)
    near, *across = split_sum([ds[0], *got], "dn_sum")
    near_sums = [near, *deal(across, "expert")]
    moe_got = [swap(moes[r], "tensor", r) for r in range(1, last)]
    moe_got, near_sums = tied(moe_got, near_sums)

    wide, dh, small = call(
        functools.partial(norm_back_kernel, experts, len(near_sums)),
        [shape((rows, wide_width), BF), shape((rows, width), F32), shape((8, width), F32)],
        (h, n_two, gain_two, router, balance, cot_ends, *near_sums),
        "norm_back",
        "v",
        "vvv",
    )
    wides = [wide] + [swap(wide, "tensor", r) for r in around]
    wides, grads = tied(wides, grads)
    moe_got.append(swap(moes[last], "tensor", last))
    moe_got, wides = tied(moe_got, wides)
    part_rows = rows + 16
    wide_all, dqkv, *back_parts = call(
        attend_back_kernel,
        [
            shape((seq_len, wide_width), BF),
            shape((seq_len, heads + 2 * keys_wide), BF),
            shape((part_rows, width), F32),
        ]
        + [shape((part_rows, width), BF)] * last,
        (t_at, *wides, tokens, q, k, v, lse, w_query, w_key, w_value, w_output, cosine, sine, small),
        "attend_back",
        "s" + "v" * tensor_size + "b" * 11,
        "bb",
        limit=58,
        scratch=[
            pltpu.VMEM((seq_len, heads), BF),
            pltpu.VMEM((seq_len, width), F32),
            pltpu.VMEM((8, width), F32),
        ],
        flops=2 * seq_len * width * 4 * heads,
    )
    part_sums = [back_parts[0]] + [swap(back_parts[r], "tensor", r) for r in around]
    part_sums, moe_got = tied(part_sums, moe_got)
    moe_near, *moe_across = split_sum([moes[0], *moe_got], "moe_sum")
    moe_sums = [moe_near, *deal(moe_across, "expert")]
    ig, small = call(
        input_grad_kernel,
        [shape((rows, width), BF), shape((8, width), F32)],
        (t_at, xq, gain_one, dh, *part_sums),
        "input_grad",
        "svbv",
        scratch=[pltpu.VMEM((tensor_size, 8, width), F32)],
    )
    igs = [ig] + [swap(ig, "tensor", r) for r in around]
    expert_grads = both_copies(grads, swap(grads, "dp", 1))
    expert_grads, igs = tied(expert_grads, igs)
    input_grad = call(
        natural_kernel, [shape((seq_len, width), F32)], (t_at, *igs), "input_grad_whole", "s", "b"
    )[0]
    out_piece = added([h, *moe_sums], BF, "out_piece")
    output = call(
        natural_kernel,
        [shape((seq_len, width), BF)],
        (t_at, out_piece, *[swap(out_piece, "tensor", r) for r in around]),
        "output",
        "s",
        "b",
    )[0]

    half = width // dp_size
    chunk = half // expert_size

    columns = heads + 2 * keys_wide
    all_columns = columns + heads + LANES
    own_block = pl.BlockSpec((1, rows, width), lambda i: (0, 0, 0))
    kept, sent = call(
        dense_kernel,
        [shape((half, all_columns), F32), shape((half, all_columns), BF)],
        (d_at, *twos, wide_all, o, n_one, dqkv),
        "dense",
        ["s"] + [own_block] * tensor_size + ["b"] * 4,
        "vv",
        limit=54,
        scratch=[
            pltpu.VMEM((seq_len, width), BF),
            pltpu.VMEM((width, all_columns), F32),
        ],
        flops=2 * seq_len * width * all_columns,
    )
    mine, *others = call(
        kept_and_dealt_kernel,
        [shape((chunk, all_columns), F32)] + [shape((chunk, all_columns), BF)] * (expert_size - 1),
        (e_at, kept, swap(sent, "dp", 1)),
        "dense_dealt",
        "s",
    )
    g_query, g_key, g_value, g_out, g_router = call(
        dense_sum_kernel,
        [
            shape((chunk, heads), F32),
            shape((chunk, keys_wide), F32),
            shape((chunk, keys_wide), F32),
            shape((heads, chunk), F32),
            shape((chunk, LANES), F32),
        ],
        (mine, *deal(others, "expert")),
        "dense_sum",
        "",
        "bbbbb",
    )

    small = small + swap(small, "dp", 1)
    small = ordered_sum(e_at, [small, *spread(small, "expert")])
    at = (d_me * expert_size + e_me) * chunk
    loss_value = (experts * balance * small[2:3, :LANES])[0, :experts]
    return (
        output,
        loss_value,
        input_grad,
        lax.dynamic_slice(small, (0, at), (1, chunk))[0],
        g_query,
        g_key,
        g_value,
        g_out,
        lax.dynamic_slice(small, (1, at), (1, chunk))[0],
        g_router[:, :experts],
        expert_grads[0],
        expert_grads[1],
        expert_grads[2],
    )


def solution(mesh):
    rows = ("dp", "expert")
    placed = (
        P(rows, None),
        P(rows, None),
        P(),
        P(None, "tensor"),
        P(None, "tensor"),
        P(None, "tensor"),
        P("tensor", None),
        P(),
        P(),
        P("expert", None, "tensor"),
        P("expert", None, "tensor"),
        P("expert", "tensor", None),
        P(rows, None),
    )
    return jax.shard_map(
        on_device,
        mesh=mesh,
        in_specs=placed,
        out_specs=(
            P(rows, None),
            P(),
            P(rows, None),
            P(rows),
            P(rows, "tensor"),
            P(rows, "tensor"),
            P(rows, "tensor"),
            P("tensor", rows),
            P(rows),
            P(rows, None),
            P("expert", None, "tensor"),
            P("expert", None, "tensor"),
            P("expert", "tensor", None),
        ),
        check_vma=False,
    )
```

time: 277 us -> 226 us (0.82)
  starting transfers between devices: 98.9 us -> 65.7 us
  local copies, waits for them, and re-layouts: 35.7 us -> 9.21 us
  other arithmetic: 26.8 us -> 1.21 us
  Pallas kernels: 50.4 us -> 74.5 us
  waiting for transfers between devices: 62.4 us -> 73.2 us
    ppermute x74 -> x48, starting transfers between devices: 98.9 us -> 65.7 us  [swap(): return lax.ppermute(x, axis, [(i, i ^ distance) for i in range(size)])]
    pallas_call x18 -> x26, Pallas kernels: 50.4 us -> 74.5 us  [the longest x19 27.1 us: call(): pl.pallas_call(kernel, grid=(1,), out_shape=outs, in_specs=[spec(p, x) fo...]
    unnamed x141 -> x81, local copies, waits for them, and re-layouts: 26.7 us -> 8.7 us
    add x7 -> x1, other arithmetic: 13.7 us -> 0.01 us  [on_device(): counts = sum((jnp.sum(x[:, :1], axis=0) for x in counts))]
    ppermute x74 -> x48, waiting for transfers between devices: 62.4 us -> 73.2 us  [swap(): return lax.ppermute(x, axis, [(i, i ^ distance) for i in range(size)])]
    reduce_sum x5 -> x0, other arithmetic: 6.39 us -> none  [the longest x1 4.13 us: on_device(): counts = jnp.sum(named.astype(F32), axis=(0, 1))[None]]
    another operation x4 -> x0, other arithmetic: 3.9 us -> none  [spread(): return jnp.stack([swap(x, axis, r) for r in range(1, size)])]
  transfers between devices with their start and end apart: 74 -> 48, of which waited for: 18 -> 21; matrix products, arithmetic and copies ran while one was open for 12% -> 1% of each run, Pallas kernels for 18% -> 32%
where the time goes in v3:
time: 226 us; the launch traced here: 225 us
  Pallas kernels  74.5 us (33%)
  waiting for transfers between devices  73.2 us (32%)
  starting transfers between devices  65.7 us (29%)
  local copies, waits for them, and re-layouts  9.21 us (4%)
    ppermute x48, waiting for transfers between devices, swap(): return lax.ppermute(x, axis, [(i, i ^ distance) for i in range(size)])  73.2 us
    ppermute x48, starting transfers between devices, swap(): return lax.ppermute(x, axis, [(i, i ^ distance) for i in range(size)])  65.7 us
    pallas_call x19, Pallas kernels, call(): pl.pallas_call(kernel, grid=(1,), out_shape=outs, in_specs=[spec(p, x) fo...  27.1 us
    pallas_call x4, Pallas kernels, run_experts(): pl.pallas_call(functools.partial(experts_kernel, experts), grid=(total //...  23.6 us
    pallas_call x1, Pallas kernels, both_copies(): pl.pallas_call(both_copies_kernel, grid=(local,), in_specs=[block(rows, h...  11.1 us
    pallas_call x1, Pallas kernels, run_grads(): pl.pallas_call(grads_kernel, grid=(local,), in_specs=whole(n) + cols(dgu,...  11.1 us
    unnamed x81, local copies, waits for them, and re-layouts  8.7 us
  transfers between devices with their start and end apart: 48, of which 21 were waited for; matrix products, arithmetic and copies ran while one was open for 1% of the time, Pallas kernels for 32%

profile of v3, /device:TPU:0, one launch (start us, length us, event | category | flops | bytes accessed | tf_op | source)
XLA Modules:
  0.0 224.9 jit_solution(3075594368245521963)
XLA Ops:
  0.6 2.1 pieces.1
  2.7 5.0 %collective-permute-start.7 = (bf16[2,64,1152]{2,1,0:T(8,128)(2,1)}, bf16[2,64,1152]{2,1,0:T(8,128)(2,1)S(1)}, u32[]{:S(2)}, u32[]{:S(2)}) collective-permute-start(bf16[2,64,1152]{2,1,0:T(8,128)(2,1)} %get-tuple-element.159.own_ref.cot_ref), channel_id=1, source_target_pairs={{0,12},{4,8},{8,4},{12,0},{1,13},{5,9},{9,5},{13,1},{2,14},{6,10},... | collective-permute-start | bytes 884744 | tf_op jit(solution)/shard_map/ppermute | solution.py:41
  8.4 4.7 %attend.1 = (bf16[256,1024]{1,0:T(8,128)(2,1)}, bf16[256,256]{1,0:T(8,128)(2,1)}, bf16[256,128]{1,0:T(8,128)(2,1)}, bf16[256,128]{1,0:T(8,128)(2,1)}, bf16[256,2...) custom-call(s32[1]{0:T(128)} %bitcast.me_ref, ...), custom_call_target="tpu_custom_call" | custom-call | flops 53687091200 | tf_op jit(solution)/shard_map/attend/pallas_call | solution.py:118
  13.0 1.7 collective-permute-start
  14.7 1.5 collective-permute-start.1
  16.2 2.0 collective-permute-done.refs_0_
  18.2 2.7 %collective-permute-start.2 = (bf16[64,1024]{1,0:T(8,128)(2,1)}, bf16[64,1024]{1,0:T(8,128)(2,1)S(1)}, u32[]{:S(2)}, u32[]{:S(2)}) collective-permute-start(bf16[64,1024]{1,0:T(8,128)(2,1)} %get-tuple-element.156), channel_id=1, source_target_pairs={{0,3},{1,2},{2,1},{3,0},{4,7},{5,6},{6,5},{7,4},{8,11},{9,10},{10,... | collective-permute-start | bytes 393224 | tf_op jit(solution)/shard_map/ppermute | solution.py:41
  20.9 3.4 %collective-permute-done.2.refs_2_ = bf16[64,1024]{1,0:T(8,128)(2,1)S(1)} collective-permute-done((bf16[64,1024]{1,0:T(8,128)(2,1)}, bf16[64,1024]{1,0:T(8,128)(2,1)S(1)}, u32[]{:S(2)}, u32[]{:S(2)}) %collective-permute-start.2) | collective-permute-done | bytes 131104 | tf_op jit(solution)/shard_map/ppermute | solution.py:41
  26.3 6.8 %collective-permute-done.5.refs_1_ = bf16[2,64,1152]{2,1,0:T(8,128)(2,1)S(1)} collective-permute-done((bf16[2,64,1152]{2,1,0:T(8,128)(2,1)}, bf16[2,64,1152]{2,1,0:T(8,128)(2,1)S(1)}, u32[]{:S(2)}, u32[]{:S(2)}) %collective-permute-start.5) | collective-permute-done | bytes 294944 | tf_op jit(solution)/shard_map/ppermute | solution.py:41
  33.1 3.0 %collective-permute-start.6 = (bf16[64,1024]{1,0:T(8,128)(2,1)S(1)}, bf16[64,1024]{1,0:T(8,128)(2,1)}, u32[]{:S(2)}, u32[]{:S(2)}) collective-permute-start(bf16[64,1024]{1,0:T(8,128)(2,1)S(1)} %get-tuple-element.162.refs_0_.n_ref), channel_id=1, source_target_pairs={{0,8},{4,12},{8,0},{12,4},{1,9},{5,13},{9,1},{13,5},{2,10},{6,14},... | collective-permute-start | bytes 393224 | tf_op jit(solution)/shard_map/ppermute | solution.py:41
  37.5 1.6 copy-done.2
  41.5 1.5 collective-permute-start.12
  45.7 1.8 together.3.a0
  47.5 1.5 collective-permute-start.10
  50.6 5.4 %experts.4 = (bf16[256,2048]{1,0:T(8,128)(2,1)S(1)}, bf16[256,1024]{1,0:T(8,128)(2,1)S(1)}, f32[256,1152]{1,0:T(8,128)S(1)}, f32[256,1024]{1,0:T(8,128)S(1)}, f32[1,8,128]{2,1,0:T(8,128)S(1)}) custom-call(s32[1]{0:T(128)} %bitcast.9.base_ref, bf16[256,1024]{1,0:T(8,128)(2,1)} %bitcast.5.x_ref.refs_0_, bf16[256,1152]{1,0:T(8,128)(2,1)S(1)} %bitcast.55, ...), custom_call_target="tpu_custom_call" | custom-call | flops 322122547200 | tf_op jit(solution)/shard_map/experts/pallas_call | solution.py:312
  60.0 7.7 %collective-permute-done.9.a1 = bf16[4,64,1024]{2,1,0:T(8,128)(2,1)} collective-permute-done((bf16[4,64,1024]{2,1,0:T(8,128)(2,1)}, bf16[4,64,1024]{2,1,0:T(8,128)(2,1)}, u32[]{:S(2)}, u32[]{:S(2)}) %collective-permute-start.9) | collective-permute-done | bytes 524320 | tf_op jit(solution)/shard_map/ppermute | solution.py:41
  67.7 5.9 %experts.5 = (bf16[256,2048]{1,0:T(8,128)(2,1)S(1)}, bf16[256,1024]{1,0:T(8,128)(2,1)S(1)}, bf16[256,1152]{1,0:T(8,128)(2,1)}, bf16[256,1024]{1,0:T(8,128)(2,1)S(1)}, f32[1,8,128]{2,1,0:T(8,128)S(1)}) custom-call(s32[1]{0:T(128)} %bitcast.9.base_ref, bf16[256,1024]{1,0:T(8,128)(2,1)} %bitcast.14.x_ref, bf16[256,1152]{1,0:T(8,128)(2,1)S(1)} %bitcast.44, ...), custom_call_target="tpu_custom_call" | custom-call | flops 322122547200 | tf_op jit(solution)/shard_map/experts/pallas_call | solution.py:312
  75.1 6.0 %experts.6 = (bf16[256,2048]{1,0:T(8,128)(2,1)S(1)}, bf16[256,1024]{1,0:T(8,128)(2,1)S(1)}, bf16[256,1152]{1,0:T(8,128)(2,1)}, bf16[256,1024]{1,0:T(8,128)(2,1)S(1)}, f32[1,8,128]{2,1,0:T(8,128)S(1)}) custom-call(s32[1]{0:T(128)} %bitcast.9.base_ref, bf16[256,1024]{1,0:T(8,128)(2,1)} %bitcast.18.x_ref, bf16[256,1152]{1,0:T(8,128)(2,1)S(1)} %bitcast.42, ...), custom_call_target="tpu_custom_call" | custom-call | flops 322122547200 | tf_op jit(solution)/shard_map/experts/pallas_call | solution.py:312
  81.6 6.3 %experts.7 = (bf16[256,2048]{1,0:T(8,128)(2,1)S(1)}, bf16[256,1024]{1,0:T(8,128)(2,1)S(1)}, bf16[256,1152]{1,0:T(8,128)(2,1)}, bf16[256,1024]{1,0:T(8,128)(2,1)}, f32[1,8,128]{2,1,0:T(8,128)S(1)}) custom-call(s32[1]{0:T(128)} %bitcast.9.base_ref, bf16[256,1024]{1,0:T(8,128)(2,1)} %bitcast.22.x_ref, bf16[256,1152]{1,0:T(8,128)(2,1)S(1)} %bitcast.57, ...), custom_call_target="tpu_custom_call" | custom-call | flops 322122547200 | tf_op jit(solution)/shard_map/experts/pallas_call | solution.py:312
  89.4 11.1 %expert_grads.1.mine_ref = bf16[8,3072,128]{2,1,0:T(8,128)(2,1)S(1)} custom-call(bf16[256,1024]{1,0:T(8,128)(2,1)} %bitcast.5.x_ref.refs_0_, bf16[256,1024]{1,0:T(8,128)(2,1)} %bitcast.6.refs_1_, bf16[256,1024]{1,0:T(8,128)(2,1)} %bitcast.7.refs_2_, bf16[256,1024]{1,0:T(8,128)(2,1)} %bitcast.8.refs_3_, bf16[256,2048]{1,0:T(8,128)(2,1)S(1)} %get-tuple-element.173.refs_4_, ...), custom_call_target="tpu_custom_call" | custom-call | flops 644245094400 | tf_op jit(solution)/shard_map/expert_grads/pallas_call | solution.py:380
  100.5 2.6 %copy-done = bf16[8,3072,128]{2,1,0:T(8,128)(2,1)} copy-done((bf16[8,3072,128]{2,1,0:T(8,128)(2,1)}, bf16[8,3072,128]{2,1,0:T(8,128)(2,1)S(1)}, u32[]{:S(2)}) %copy-start) | copy-done | bytes 6291480
  103.1 2.8 %collective-permute-done.15.refs_2_ = bf16[4,64,1152]{2,1,0:T(8,128)(2,1)} collective-permute-done((bf16[4,64,1152]{2,1,0:T(8,128)(2,1)}, bf16[4,64,1152]{2,1,0:T(8,128)(2,1)}, u32[]{:S(2)}, u32[]{:S(2)}) %collective-permute-start.15) | collective-permute-done | bytes 589856 | tf_op jit(solution)/shard_map/ppermute | solution.py:41
  107.0 1.7 dn_sum.1
  108.7 2.4 %collective-permute-start.22 = (bf16[4,64,1024]{2,1,0:T(8,128)(2,1)}, bf16[4,64,1024]{2,1,0:T(8,128)(2,1)S(1)}, u32[]{:S(2)}, u32[]{:S(2)}) collective-permute-start(bf16[4,64,1024]{2,1,0:T(8,128)(2,1)} %bitcast.28), channel_id=1, source_target_pairs={{0,3},{1,2},{2,1},{3,0},{4,7},{5,6},{6,5},{7,4},{8,11},{9,10},{10,... | collective-permute-start | bytes 1572872 | tf_op jit(solution)/shard_map/ppermute | solution.py:41
  112.3 3.3 %collective-permute-start.20 = (bf16[64,1152]{1,0:T(8,128)(2,1)S(1)}, bf16[64,1152]{1,0:T(8,128)(2,1)S(1)}, u32[]{:S(2)}, u32[]{:S(2)}) collective-permute-start(bf16[64,1152]{1,0:T(8,128)(2,1)S(1)} %get-tuple-element.216), channel_id=1, source_target_pairs={{0,8},{4,12},{8,0},{12,4},{1,9},{5,13},{9,1},{13,5},{2,10},{6,14},... | collective-permute-start | bytes 442376 | tf_op jit(solution)/shard_map/ppermute | solution.py:41
  116.6 9.9 %collective-permute-done.20.refs_2_ = bf16[64,1152]{1,0:T(8,128)(2,1)S(1)} collective-permute-done((bf16[64,1152]{1,0:T(8,128)(2,1)S(1)}, bf16[64,1152]{1,0:T(8,128)(2,1)S(1)}, u32[]{:S(2)}, u32[]{:S(2)}) %collective-permute-start.20) | collective-permute-done | bytes 147488 | tf_op jit(solution)/shard_map/ppermute | solution.py:41
  130.6 1.6 collective-permute-start.24
  132.8 3.5 %collective-permute-done.26.w3 = bf16[64,1152]{1,0:T(8,128)(2,1)S(1)} collective-permute-done((bf16[64,1152]{1,0:T(8,128)(2,1)S(1)}, bf16[64,1152]{1,0:T(8,128)(2,1)S(1)}, u32[]{:S(2)}, u32[]{:S(2)}) %collective-permute-start.26) | collective-permute-done | bytes 147488 | tf_op jit(solution)/shard_map/ppermute | solution.py:41
  137.7 5.5 %attend_back.1 = (bf16[256,1152]{1,0:T(8,128)(2,1)}, bf16[256,512]{1,0:T(8,128)(2,1)}, f32[80,1024]{1,0:T(8,128)}, bf16[80,1024]{1,0:T(8,128)(2,1)}, bf16[80,1024]{1,0:T(8,128)(2,1)}, /*index=5*/bf16[80,1024]{1,0:T(8,128)(2,1)}) custom-call(s32[1]{0:T(128)} %bitcast.me_ref, bf16[64,1152]{1,0:T(8,128)(2,1)} %copy-done.28, bf16[64,1152]{1,0:T(8,128)(2,1)} %copy-done.39, ...), custom_call_target="tpu_custom_call" | custom-call | flops 53687091200 | tf_op jit(solution)/shard_map/attend_back/pallas_call | solution.py:118
  143.2 4.1 %dense.1 = (f32[512,896]{1,0:T(8,128)}, bf16[512,896]{1,0:T(8,128)(2,1)}) custom-call(s32[2]{0:T(128)} %pad_add_fusion.me_ref, bf16[4,64,1024]{2,1,0:T(8,128)(2,1)} %together.3.a0, bf16[4,64,1024]{2,1,0:T(8,128)(2,1)} %collective-permute-done.9.a1, bf16[4,64,1024]{2,1,0:T(8,128)(2,1)} %collective-permute-done.10.a2, ...), custom_call_target="tpu_custom_call" | custom-call | flops 46976204800 | tf_op jit(solution)/shard_map/dense/pallas_call | solution.py:118
  149.3 1.7 collective-permute-start.29
  151.0 3.5 %collective-permute-done.27.refs_1_ = bf16[80,1024]{1,0:T(8,128)(2,1)S(1)} collective-permute-done((bf16[80,1024]{1,0:T(8,128)(2,1)S(1)}, bf16[80,1024]{1,0:T(8,128)(2,1)S(1)}, u32[]{:S(2)}, u32[]{:S(2)}) %collective-permute-start.27) | collective-permute-done | bytes 163872 | tf_op jit(solution)/shard_map/ppermute | solution.py:41
  154.9 3.6 %collective-permute-done.29.refs_3_ = bf16[80,1024]{1,0:T(8,128)(2,1)S(1)} collective-permute-done((bf16[80,1024]{1,0:T(8,128)(2,1)S(1)}, bf16[80,1024]{1,0:T(8,128)(2,1)S(1)}, u32[]{:S(2)}, u32[]{:S(2)}) %collective-permute-start.29) | collective-permute-done | bytes 163872 | tf_op jit(solution)/shard_map/ppermute | solution.py:41
  158.7 3.8 %collective-permute-start.30 = (bf16[64,1024]{1,0:T(8,128)(2,1)S(1)}, bf16[64,1024]{1,0:T(8,128)(2,1)S(1)}, u32[]{:S(2)}, u32[]{:S(2)}) collective-permute-start(bf16[64,1024]{1,0:T(8,128)(2,1)S(1)} %get-tuple-element.255), channel_id=1, source_target_pairs={{0,4},{4,0},{8,12},{12,8},{1,5},{5,1},{9,13},{13,9},{2,6},{6,2},{1... | collective-permute-start | bytes 393224 | tf_op jit(solution)/shard_map/ppermute | solution.py:41
  162.9 2.0 collective-permute-start.32
  164.9 2.0 collective-permute-done.30.refs_2_
  166.9 8.1 %collective-permute-done.31.refs_3_ = bf16[64,1024]{1,0:T(8,128)(2,1)S(1)} collective-permute-done((bf16[64,1024]{1,0:T(8,128)(2,1)S(1)}, bf16[64,1024]{1,0:T(8,128)(2,1)S(1)}, u32[]{:S(2)}, u32[]{:S(2)}) %collective-permute-start.31) | collective-permute-done | bytes 131104 | tf_op jit(solution)/shard_map/ppermute | solution.py:41
  178.3 1.9 collective-permute-start.39
  180.3 3.8 %collective-permute-done.39.refs_3_ = f32[8,1024]{1,0:T(8,128)S(1)} collective-permute-done((f32[8,1024]{1,0:T(8,128)S(1)}, f32[8,1024]{1,0:T(8,128)S(1)}, u32[]{:S(2)}, u32[]{:S(2)}) %collective-permute-start.39) | collective-permute-done | bytes 32800 | tf_op jit(solution)/shard_map/ppermute | solution.py:41
  186.8 2.5 %collective-permute-done.38.refs_2_ = f32[8,1024]{1,0:T(8,128)S(1)} collective-permute-done((f32[8,1024]{1,0:T(8,128)S(1)}, f32[8,1024]{1,0:T(8,128)S(1)}, u32[]{:S(2)}, u32[]{:S(2)}) %collective-permute-start.38) | collective-permute-done | bytes 32800 | tf_op jit(solution)/shard_map/ppermute | solution.py:41
  189.7 2.1 collective-permute-start.46
  191.9 1.8 collective-permute-start.33
  193.7 1.8 collective-permute-start.47
  196.1 1.9 collective-permute-done.33.refs_1_
  198.6 2.7 %collective-permute-start.42 = (bf16[64,1024]{1,0:T(8,128)(2,1)S(1)}, bf16[64,1024]{1,0:T(8,128)(2,1)S(1)}, u32[]{:S(2)}, u32[]{:S(2)}) collective-permute-start(bf16[64,1024]{1,0:T(8,128)(2,1)S(1)} %get-tuple-element.269.refs_0_), channel_id=1, source_target_pairs={{0,2},{1,3},{2,0},{3,1},{4,6},{5,7},{6,4},{7,5},{8,10},{9,11},{10,... | collective-permute-start | bytes 393224 | tf_op jit(solution)/shard_map/ppermute | solution.py:41
  201.3 6.9 %collective-permute-done.46.refs_1_ = bf16[128,896]{1,0:T(8,128)(2,1)S(1)} collective-permute-done((bf16[128,896]{1,0:T(8,128)(2,1)S(1)}, bf16[128,896]{1,0:T(8,128)(2,1)S(1)}, u32[]{:S(2)}, u32[]{:S(2)}) %collective-permute-start.46) | collective-permute-done | bytes 229408 | tf_op jit(solution)/shard_map/ppermute | solution.py:41
  208.2 1.7 collective-permute-start.41
  212.7 11.1 %both_copies.1 = (f32[8,1024,128]{2,1,0:T(8,128)}, f32[8,1024,128]{2,1,0:T(8,128)}, f32[8,128,1024]{2,1,0:T(8,128)}) custom-call(bf16[8,3072,128]{2,1,0:T(8,128)(2,1)} %copy-done, bf16[8,3072,128]{2,1,0:T(8,128)(2,1)} %collective-permute-done.40.other_ref), custom_call_target="tpu_custom_call" | custom-call | bytes 25165824 | tf_op jit(solution)/shard_map/both_copies/pallas_call | solution.py:409
  (161 shorter events, 41.9 us)
Async XLA Ops:
  2.7 23.6 %collective-permute-start.7 = (bf16[2,64,1152]{2,1,0:T(8,128)(2,1)}, bf16[2,64,1152]{2,1,0:T(8,128)(2,1)S(1)}, u32[]{:S(2)}, u32[]{:S(2)}) collective-permute-start(bf16[2,64,1152]{2,1,0:T(8,128)(2,1)} %get-tuple-element.159.own_ref.cot_ref), channel_id=1, source_target_pairs={{0,12},{4,8},{8,4},{12,0},{1,13},{5,9},{9,5},{13,1},{2,14},{6,10},... | collective-permute-start | bytes 884744 | tf_op jit(solution)/shard_map/ppermute | solution.py:41
  7.8 25.3 %collective-permute-start.5 = (bf16[2,64,1152]{2,1,0:T(8,128)(2,1)}, bf16[2,64,1152]{2,1,0:T(8,128)(2,1)S(1)}, u32[]{:S(2)}, u32[]{:S(2)}) collective-permute-start(bf16[2,64,1152]{2,1,0:T(8,128)(2,1)} %get-tuple-element.159.own_ref.cot_ref), channel_id=1, source_target_pairs={{0,8},{4,12},{8,0},{12,4},{1,9},{5,13},{9,1},{13,5},{2,10},{6,14},... | collective-permute-start | bytes 884744 | tf_op jit(solution)/shard_map/ppermute | solution.py:41
  7.8 25.3 %collective-permute-start.3 = (bf16[2,64,1152]{2,1,0:T(8,128)(2,1)}, bf16[2,64,1152]{2,1,0:T(8,128)(2,1)S(1)}, u32[]{:S(2)}, u32[]{:S(2)}) collective-permute-start(bf16[2,64,1152]{2,1,0:T(8,128)(2,1)} %get-tuple-element.159.own_ref.cot_ref), channel_id=1, source_target_pairs={{0,4},{4,0},{8,12},{12,8},{1,5},{5,1},{9,13},{13,9},{2,6},{6,2},{1... | collective-permute-start | bytes 884744 | tf_op jit(solution)/shard_map/ppermute | solution.py:41
  13.0 5.2 %collective-permute-start = (bf16[64,1024]{1,0:T(8,128)(2,1)}, bf16[64,1024]{1,0:T(8,128)(2,1)S(1)}, u32[]{:S(2)}, u32[]{:S(2)}) collective-permute-start(bf16[64,1024]{1,0:T(8,128)(2,1)} %get-tuple-element.154), channel_id=1, source_target_pairs={{0,1},{1,0},{2,3},{3,2},{4,5},{5,4},{6,7},{7,6},{8,9},{9,8},{10,11... | collective-permute-start | bytes 393224 | tf_op jit(solution)/shard_map/ppermute | solution.py:41
  14.7 6.1 %collective-permute-start.1 = (bf16[64,1024]{1,0:T(8,128)(2,1)}, bf16[64,1024]{1,0:T(8,128)(2,1)S(1)}, u32[]{:S(2)}, u32[]{:S(2)}) collective-permute-start(bf16[64,1024]{1,0:T(8,128)(2,1)} %get-tuple-element.155), channel_id=1, source_target_pairs={{0,2},{1,3},{2,0},{3,1},{4,6},{5,7},{6,4},{7,5},{8,10},{9,11},{10,... | collective-permute-start | bytes 393224 | tf_op jit(solution)/shard_map/ppermute | solution.py:41
  18.2 6.1 %collective-permute-start.2 = (bf16[64,1024]{1,0:T(8,128)(2,1)}, bf16[64,1024]{1,0:T(8,128)(2,1)S(1)}, u32[]{:S(2)}, u32[]{:S(2)}) collective-permute-start(bf16[64,1024]{1,0:T(8,128)(2,1)} %get-tuple-element.156), channel_id=1, source_target_pairs={{0,3},{1,2},{2,1},{3,0},{4,7},{5,6},{6,5},{7,4},{8,11},{9,10},{10,... | collective-permute-start | bytes 393224 | tf_op jit(solution)/shard_map/ppermute | solution.py:41
  33.1 11.4 %collective-permute-start.4 = (bf16[64,1024]{1,0:T(8,128)(2,1)S(1)}, bf16[64,1024]{1,0:T(8,128)(2,1)S(1)}, u32[]{:S(2)}, u32[]{:S(2)}) collective-permute-start(bf16[64,1024]{1,0:T(8,128)(2,1)S(1)} %get-tuple-element.162.refs_0_.n_ref), channel_id=1, source_target_pairs={{0,4},{4,0},{8,12},{12,8},{1,5},{5,1},{9,13},{13,9},{2,6},{6,2},{1... | collective-permute-start | bytes 393224 | tf_op jit(solution)/shard_map/ppermute | solution.py:41
  33.1 12.6 %collective-permute-start.6 = (bf16[64,1024]{1,0:T(8,128)(2,1)S(1)}, bf16[64,1024]{1,0:T(8,128)(2,1)}, u32[]{:S(2)}, u32[]{:S(2)}) collective-permute-start(bf16[64,1024]{1,0:T(8,128)(2,1)S(1)} %get-tuple-element.162.refs_0_.n_ref), channel_id=1, source_target_pairs={{0,8},{4,12},{8,0},{12,4},{1,9},{5,13},{9,1},{13,5},{2,10},{6,14},... | collective-permute-start | bytes 393224 | tf_op jit(solution)/shard_map/ppermute | solution.py:41
  36.2 9.6 %collective-permute-start.8 = (bf16[64,1024]{1,0:T(8,128)(2,1)S(1)}, bf16[64,1024]{1,0:T(8,128)(2,1)}, u32[]{:S(2)}, u32[]{:S(2)}) collective-permute-start(bf16[64,1024]{1,0:T(8,128)(2,1)S(1)} %get-tuple-element.162.refs_0_.n_ref), channel_id=1, source_target_pairs={{0,12},{4,8},{8,4},{12,0},{1,13},{5,9},{9,5},{13,1},{2,14},{6,10},... | collective-permute-start | bytes 393224 | tf_op jit(solution)/shard_map/ppermute | solution.py:41
  41.5 14.5 %collective-permute-start.12 = (bf16[3,64,1152]{2,1,0:T(8,128)(2,1)}, bf16[3,64,1152]{2,1,0:T(8,128)(2,1)}, u32[]{:S(2)}, u32[]{:S(2)}) collective-permute-start(bf16[3,64,1152]{2,1,0:T(8,128)(2,1)} %get-tuple-element.163), channel_id=1, source_target_pairs={{0,2},{1,3},{2,0},{3,1},{4,6},{5,7},{6,4},{7,5},{8,10},{9,11},{10,... | collective-permute-start | bytes 1327112 | tf_op jit(solution)/shard_map/ppermute | solution.py:41
  43.0 13.4 %collective-permute-start.11 = (bf16[3,64,1152]{2,1,0:T(8,128)(2,1)}, bf16[3,64,1152]{2,1,0:T(8,128)(2,1)}, u32[]{:S(2)}, u32[]{:S(2)}) collective-permute-start(bf16[3,64,1152]{2,1,0:T(8,128)(2,1)} %get-tuple-element.163), channel_id=1, source_target_pairs={{0,1},{1,0},{2,3},{3,2},{4,5},{5,4},{6,7},{7,6},{8,9},{9,8},{10,11... | collective-permute-start | bytes 1327112 | tf_op jit(solution)/shard_map/ppermute | solution.py:41
  47.5 27.6 %collective-permute-start.10 = (bf16[4,64,1024]{2,1,0:T(8,128)(2,1)}, bf16[4,64,1024]{2,1,0:T(8,128)(2,1)}, u32[]{:S(2)}, u32[]{:S(2)}) collective-permute-start(bf16[4,64,1024]{2,1,0:T(8,128)(2,1)} %together.3.a0), channel_id=1, source_target_pairs={{0,2},{1,3},{2,0},{3,1},{4,6},{5,7},{6,4},{7,5},{8,10},{9,11},{10,... | collective-permute-start | bytes 1572872 | tf_op jit(solution)/shard_map/ppermute | solution.py:41
  49.1 18.6 %collective-permute-start.9 = (bf16[4,64,1024]{2,1,0:T(8,128)(2,1)}, bf16[4,64,1024]{2,1,0:T(8,128)(2,1)}, u32[]{:S(2)}, u32[]{:S(2)}) collective-permute-start(bf16[4,64,1024]{2,1,0:T(8,128)(2,1)} %together.3.a0), channel_id=1, source_target_pairs={{0,1},{1,0},{2,3},{3,2},{4,5},{5,4},{6,7},{7,6},{8,9},{9,8},{10,11... | collective-permute-start | bytes 1572872 | tf_op jit(solution)/shard_map/ppermute | solution.py:41
  56.4 25.2 %collective-permute-start.13 = (bf16[4,64,1024]{2,1,0:T(8,128)(2,1)}, bf16[4,64,1024]{2,1,0:T(8,128)(2,1)}, u32[]{:S(2)}, u32[]{:S(2)}) collective-permute-start(bf16[4,64,1024]{2,1,0:T(8,128)(2,1)} %together.3.a0), channel_id=1, source_target_pairs={{0,3},{1,2},{2,1},{3,0},{4,7},{5,6},{6,5},{7,4},{8,11},{9,10},{10,... | collective-permute-start | bytes 1572872 | tf_op jit(solution)/shard_map/ppermute | solution.py:41
  73.6 29.5 %collective-permute-start.14 = (bf16[4,64,1152]{2,1,0:T(8,128)(2,1)}, bf16[4,64,1152]{2,1,0:T(8,128)(2,1)}, u32[]{:S(2)}, u32[]{:S(2)}) collective-permute-start(bf16[4,64,1152]{2,1,0:T(8,128)(2,1)} %bitcast.16), channel_id=1, source_target_pairs={{0,1},{1,0},{2,3},{3,2},{4,5},{5,4},{6,7},{7,6},{8,9},{9,8},{10,11... | collective-permute-start | bytes 1769480 | tf_op jit(solution)/shard_map/ppermute | solution.py:41
  81.1 24.8 %collective-permute-start.15 = (bf16[4,64,1152]{2,1,0:T(8,128)(2,1)}, bf16[4,64,1152]{2,1,0:T(8,128)(2,1)}, u32[]{:S(2)}, u32[]{:S(2)}) collective-permute-start(bf16[4,64,1152]{2,1,0:T(8,128)(2,1)} %bitcast.20), channel_id=1, source_target_pairs={{0,2},{1,3},{2,0},{3,1},{4,6},{5,7},{6,4},{7,5},{8,10},{9,11},{10,... | collective-permute-start | bytes 1769480 | tf_op jit(solution)/shard_map/ppermute | solution.py:41
  87.9 18.0 %collective-permute-start.16 = (bf16[4,64,1152]{2,1,0:T(8,128)(2,1)}, bf16[4,64,1152]{2,1,0:T(8,128)(2,1)}, u32[]{:S(2)}, u32[]{:S(2)}) collective-permute-start(bf16[4,64,1152]{2,1,0:T(8,128)(2,1)} %bitcast.27), channel_id=1, source_target_pairs={{0,3},{1,2},{2,1},{3,0},{4,7},{5,6},{6,5},{7,4},{8,11},{9,10},{10,... | collective-permute-start | bytes 1769480 | tf_op jit(solution)/shard_map/ppermute | solution.py:41
  105.9 20.7 %collective-permute-start.17 = (bf16[4,64,1024]{2,1,0:T(8,128)(2,1)S(1)}, bf16[4,64,1024]{2,1,0:T(8,128)(2,1)S(1)}, u32[]{:S(2)}, u32[]{:S(2)}) collective-permute-start(bf16[4,64,1024]{2,1,0:T(8,128)(2,1)S(1)} %bitcast.59), channel_id=1, source_target_pairs={{0,1},{1,0},{2,3},{3,2},{4,5},{5,4},{6,7},{7,6},{8,9},{9,8},{10,11... | collective-permute-start | bytes 1572872 | tf_op jit(solution)/shard_map/ppermute | solution.py:41
  106.5 20.1 %collective-permute-start.18 = (bf16[4,64,1024]{2,1,0:T(8,128)(2,1)S(1)}, bf16[4,64,1024]{2,1,0:T(8,128)(2,1)S(1)}, u32[]{:S(2)}, u32[]{:S(2)}) collective-permute-start(bf16[4,64,1024]{2,1,0:T(8,128)(2,1)S(1)} %bitcast.60), channel_id=1, source_target_pairs={{0,2},{1,3},{2,0},{3,1},{4,6},{5,7},{6,4},{7,5},{8,10},{9,11},{10,... | collective-permute-start | bytes 1572872 | tf_op jit(solution)/shard_map/ppermute | solution.py:41
  108.7 7.0 %collective-permute-start.19 = (bf16[64,1152]{1,0:T(8,128)(2,1)S(1)}, bf16[64,1152]{1,0:T(8,128)(2,1)S(1)}, u32[]{:S(2)}, u32[]{:S(2)}) collective-permute-start(bf16[64,1152]{1,0:T(8,128)(2,1)S(1)} %get-tuple-element.215), channel_id=1, source_target_pairs={{0,4},{4,0},{8,12},{12,8},{1,5},{5,1},{9,13},{13,9},{2,6},{6,2},{1... | collective-permute-start | bytes 442376 | tf_op jit(solution)/shard_map/ppermute | solution.py:41
  108.7 28.2 %collective-permute-start.22 = (bf16[4,64,1024]{2,1,0:T(8,128)(2,1)}, bf16[4,64,1024]{2,1,0:T(8,128)(2,1)S(1)}, u32[]{:S(2)}, u32[]{:S(2)}) collective-permute-start(bf16[4,64,1024]{2,1,0:T(8,128)(2,1)} %bitcast.28), channel_id=1, source_target_pairs={{0,3},{1,2},{2,1},{3,0},{4,7},{5,6},{6,5},{7,4},{8,11},{9,10},{10,... | collective-permute-start | bytes 1572872 | tf_op jit(solution)/shard_map/ppermute | solution.py:41
  111.2 1.1 collective-permute-start.23
  112.3 14.2 %collective-permute-start.20 = (bf16[64,1152]{1,0:T(8,128)(2,1)S(1)}, bf16[64,1152]{1,0:T(8,128)(2,1)S(1)}, u32[]{:S(2)}, u32[]{:S(2)}) collective-permute-start(bf16[64,1152]{1,0:T(8,128)(2,1)S(1)} %get-tuple-element.216), channel_id=1, source_target_pairs={{0,8},{4,12},{8,0},{12,4},{1,9},{5,13},{9,1},{13,5},{2,10},{6,14},... | collective-permute-start | bytes 442376 | tf_op jit(solution)/shard_map/ppermute | solution.py:41
  115.6 10.9 %collective-permute-start.21 = (bf16[64,1152]{1,0:T(8,128)(2,1)S(1)}, bf16[64,1152]{1,0:T(8,128)(2,1)S(1)}, u32[]{:S(2)}, u32[]{:S(2)}) collective-permute-start(bf16[64,1152]{1,0:T(8,128)(2,1)S(1)} %get-tuple-element.217), channel_id=1, source_target_pairs={{0,12},{4,8},{8,4},{12,0},{1,13},{5,9},{9,5},{13,1},{2,14},{6,10},... | collective-permute-start | bytes 442376 | tf_op jit(solution)/shard_map/ppermute | solution.py:41
  128.7 7.6 %collective-permute-start.26 = (bf16[64,1152]{1,0:T(8,128)(2,1)S(1)}, bf16[64,1152]{1,0:T(8,128)(2,1)S(1)}, u32[]{:S(2)}, u32[]{:S(2)}) collective-permute-start(bf16[64,1152]{1,0:T(8,128)(2,1)S(1)} %get-tuple-element.235.w0), channel_id=1, source_target_pairs={{0,3},{1,2},{2,1},{3,0},{4,7},{5,6},{6,5},{7,4},{8,11},{9,10},{10,... | collective-permute-start | bytes 442376 | tf_op jit(solution)/shard_map/ppermute | solution.py:41
  129.6 7.4 %collective-permute-start.25 = (bf16[64,1152]{1,0:T(8,128)(2,1)S(1)}, bf16[64,1152]{1,0:T(8,128)(2,1)S(1)}, u32[]{:S(2)}, u32[]{:S(2)}) collective-permute-start(bf16[64,1152]{1,0:T(8,128)(2,1)S(1)} %get-tuple-element.235.w0), channel_id=1, source_target_pairs={{0,2},{1,3},{2,0},{3,1},{4,6},{5,7},{6,4},{7,5},{8,10},{9,11},{10,... | collective-permute-start | bytes 442376 | tf_op jit(solution)/shard_map/ppermute | solution.py:41
  130.6 6.4 %collective-permute-start.24 = (bf16[64,1152]{1,0:T(8,128)(2,1)S(1)}, bf16[64,1152]{1,0:T(8,128)(2,1)S(1)}, u32[]{:S(2)}, u32[]{:S(2)}) collective-permute-start(bf16[64,1152]{1,0:T(8,128)(2,1)S(1)} %get-tuple-element.235.w0), channel_id=1, source_target_pairs={{0,1},{1,0},{2,3},{3,2},{4,5},{5,4},{6,7},{7,6},{8,9},{9,8},{10,11... | collective-permute-start | bytes 442376 | tf_op jit(solution)/shard_map/ppermute | solution.py:41
  137.0 75.7 %collective-permute-start.40 = (bf16[8,3072,128]{2,1,0:T(8,128)(2,1)}, bf16[8,3072,128]{2,1,0:T(8,128)(2,1)}, u32[]{:S(2)}, u32[]{:S(2)}) collective-permute-start(bf16[8,3072,128]{2,1,0:T(8,128)(2,1)} %copy-done), channel_id=1, source_target_pairs={{0,16},{16,0},{1,17},{17,1},{2,18},{18,2},{3,19},{19,3},{4,20},{20... | collective-permute-start | bytes 18874376 | tf_op jit(solution)/shard_map/ppermute | solution.py:41
  147.4 37.8 %collective-permute-start.44 = (bf16[512,896]{1,0:T(8,128)(2,1)}, bf16[512,896]{1,0:T(8,128)(2,1)S(1)}, u32[]{:S(2)}, u32[]{:S(2)}) collective-permute-start(bf16[512,896]{1,0:T(8,128)(2,1)} %get-tuple-element.278), channel_id=1, source_target_pairs={{0,16},{16,0},{1,17},{17,1},{2,18},{18,2},{3,19},{19,3},{4,20},{20... | collective-permute-start | bytes 2752520 | tf_op jit(solution)/shard_map/ppermute | solution.py:41
  147.5 7.1 %collective-permute-start.27 = (bf16[80,1024]{1,0:T(8,128)(2,1)S(1)}, bf16[80,1024]{1,0:T(8,128)(2,1)S(1)}, u32[]{:S(2)}, u32[]{:S(2)}) collective-permute-start(bf16[80,1024]{1,0:T(8,128)(2,1)S(1)} %copy-done.36), channel_id=1, source_target_pairs={{0,1},{1,0},{2,3},{3,2},{4,5},{5,4},{6,7},{7,6},{8,9},{9,8},{10,11... | collective-permute-start | bytes 491528 | tf_op jit(solution)/shard_map/ppermute | solution.py:41
  148.4 6.4 %collective-permute-start.28 = (bf16[80,1024]{1,0:T(8,128)(2,1)S(1)}, bf16[80,1024]{1,0:T(8,128)(2,1)S(1)}, u32[]{:S(2)}, u32[]{:S(2)}) collective-permute-start(bf16[80,1024]{1,0:T(8,128)(2,1)S(1)} %copy-done.35), channel_id=1, source_target_pairs={{0,2},{1,3},{2,0},{3,1},{4,6},{5,7},{6,4},{7,5},{8,10},{9,11},{10,... | collective-permute-start | bytes 491528 | tf_op jit(solution)/shard_map/ppermute | solution.py:41
  149.3 9.2 %collective-permute-start.29 = (bf16[80,1024]{1,0:T(8,128)(2,1)S(1)}, bf16[80,1024]{1,0:T(8,128)(2,1)S(1)}, u32[]{:S(2)}, u32[]{:S(2)}) collective-permute-start(bf16[80,1024]{1,0:T(8,128)(2,1)S(1)} %copy-done.34), channel_id=1, source_target_pairs={{0,3},{1,2},{2,1},{3,0},{4,7},{5,6},{6,5},{7,4},{8,11},{9,10},{10,... | collective-permute-start | bytes 491528 | tf_op jit(solution)/shard_map/ppermute | solution.py:41
  158.7 8.2 %collective-permute-start.30 = (bf16[64,1024]{1,0:T(8,128)(2,1)S(1)}, bf16[64,1024]{1,0:T(8,128)(2,1)S(1)}, u32[]{:S(2)}, u32[]{:S(2)}) collective-permute-start(bf16[64,1024]{1,0:T(8,128)(2,1)S(1)} %get-tuple-element.255), channel_id=1, source_target_pairs={{0,4},{4,0},{8,12},{12,8},{1,5},{5,1},{9,13},{13,9},{2,6},{6,2},{1... | collective-permute-start | bytes 393224 | tf_op jit(solution)/shard_map/ppermute | solution.py:41
  162.5 12.5 %collective-permute-start.31 = (bf16[64,1024]{1,0:T(8,128)(2,1)S(1)}, bf16[64,1024]{1,0:T(8,128)(2,1)S(1)}, u32[]{:S(2)}, u32[]{:S(2)}) collective-permute-start(bf16[64,1024]{1,0:T(8,128)(2,1)S(1)} %get-tuple-element.256), channel_id=1, source_target_pairs={{0,8},{4,12},{8,0},{12,4},{1,9},{5,13},{9,1},{13,5},{2,10},{6,14},... | collective-permute-start | bytes 393224 | tf_op jit(solution)/shard_map/ppermute | solution.py:41
  162.9 12.0 %collective-permute-start.32 = (bf16[64,1024]{1,0:T(8,128)(2,1)S(1)}, bf16[64,1024]{1,0:T(8,128)(2,1)S(1)}, u32[]{:S(2)}, u32[]{:S(2)}) collective-permute-start(bf16[64,1024]{1,0:T(8,128)(2,1)S(1)} %get-tuple-element.257), channel_id=1, source_target_pairs={{0,12},{4,8},{8,4},{12,0},{1,13},{5,9},{9,5},{13,1},{2,14},{6,10},... | collective-permute-start | bytes 393224 | tf_op jit(solution)/shard_map/ppermute | solution.py:41
  175.0 16.9 %collective-permute-start.35 = (bf16[64,1024]{1,0:T(8,128)(2,1)S(1)}, bf16[64,1024]{1,0:T(8,128)(2,1)S(1)}, u32[]{:S(2)}, u32[]{:S(2)}) collective-permute-start(bf16[64,1024]{1,0:T(8,128)(2,1)S(1)} %out_piece.1.refs_0_), channel_id=1, source_target_pairs={{0,3},{1,2},{2,1},{3,0},{4,7},{5,6},{6,5},{7,4},{8,11},{9,10},{10,... | collective-permute-start | bytes 393224 | tf_op jit(solution)/shard_map/ppermute | solution.py:41
  176.1 17.5 %collective-permute-start.34 = (bf16[64,1024]{1,0:T(8,128)(2,1)S(1)}, bf16[64,1024]{1,0:T(8,128)(2,1)S(1)}, u32[]{:S(2)}, u32[]{:S(2)}) collective-permute-start(bf16[64,1024]{1,0:T(8,128)(2,1)S(1)} %out_piece.1.refs_0_), channel_id=1, source_target_pairs={{0,2},{1,3},{2,0},{3,1},{4,6},{5,7},{6,4},{7,5},{8,10},{9,11},{10,... | collective-permute-start | bytes 393224 | tf_op jit(solution)/shard_map/ppermute | solution.py:41
  177.1 1.3 collective-permute-start.36
  178.3 5.8 %collective-permute-start.39 = (f32[8,1024]{1,0:T(8,128)S(1)}, f32[8,1024]{1,0:T(8,128)S(1)}, u32[]{:S(2)}, u32[]{:S(2)}) collective-permute-start(f32[8,1024]{1,0:T(8,128)S(1)} %add.56.refs_0_), channel_id=1, source_target_pairs={{0,12},{4,8},{8,4},{12,0},{1,13},{5,9},{9,5},{13,1},{2,14},{6,10},... | collective-permute-start | bytes 98312 | tf_op jit(solution)/shard_map/ppermute | solution.py:41
  184.1 5.2 %collective-permute-start.38 = (f32[8,1024]{1,0:T(8,128)S(1)}, f32[8,1024]{1,0:T(8,128)S(1)}, u32[]{:S(2)}, u32[]{:S(2)}) collective-permute-start(f32[8,1024]{1,0:T(8,128)S(1)} %add.56.refs_0_), channel_id=1, source_target_pairs={{0,8},{4,12},{8,0},{12,4},{1,9},{5,13},{9,1},{13,5},{2,10},{6,14},... | collective-permute-start | bytes 98312 | tf_op jit(solution)/shard_map/ppermute | solution.py:41
  185.2 4.5 %collective-permute-start.37 = (f32[8,1024]{1,0:T(8,128)S(1)}, f32[8,1024]{1,0:T(8,128)S(1)}, u32[]{:S(2)}, u32[]{:S(2)}) collective-permute-start(f32[8,1024]{1,0:T(8,128)S(1)} %add.56.refs_0_), channel_id=1, source_target_pairs={{0,4},{4,0},{8,12},{12,8},{1,5},{5,1},{9,13},{13,9},{2,6},{6,2},{1... | collective-permute-start | bytes 98312 | tf_op jit(solution)/shard_map/ppermute | solution.py:41
  189.3 9.3 %collective-permute-start.45 = (bf16[128,896]{1,0:T(8,128)(2,1)S(1)}, bf16[128,896]{1,0:T(8,128)(2,1)S(1)}, u32[]{:S(2)}, u32[]{:S(2)}) collective-permute-start(bf16[128,896]{1,0:T(8,128)(2,1)S(1)} %get-tuple-element.280), channel_id=1, source_target_pairs={{0,4},{4,0},{8,12},{12,8},{1,5},{5,1},{9,13},{13,9},{2,6},{6,2},{1... | collective-permute-start | bytes 688136 | tf_op jit(solution)/shard_map/ppermute | solution.py:41
  189.7 18.4 %collective-permute-start.46 = (bf16[128,896]{1,0:T(8,128)(2,1)S(1)}, bf16[128,896]{1,0:T(8,128)(2,1)S(1)}, u32[]{:S(2)}, u32[]{:S(2)}) collective-permute-start(bf16[128,896]{1,0:T(8,128)(2,1)S(1)} %get-tuple-element.281), channel_id=1, source_target_pairs={{0,8},{4,12},{8,0},{12,4},{1,9},{5,13},{9,1},{13,5},{2,10},{6,14},... | collective-permute-start | bytes 688136 | tf_op jit(solution)/shard_map/ppermute | solution.py:41
  191.9 6.0 %collective-permute-start.33 = (bf16[64,1024]{1,0:T(8,128)(2,1)S(1)}, bf16[64,1024]{1,0:T(8,128)(2,1)S(1)}, u32[]{:S(2)}, u32[]{:S(2)}) collective-permute-start(bf16[64,1024]{1,0:T(8,128)(2,1)S(1)} %out_piece.1.refs_0_), channel_id=1, source_target_pairs={{0,1},{1,0},{2,3},{3,2},{4,5},{5,4},{6,7},{7,6},{8,9},{9,8},{10,11... | collective-permute-start | bytes 393224 | tf_op jit(solution)/shard_map/ppermute | solution.py:41
  193.7 17.6 %collective-permute-start.47 = (bf16[128,896]{1,0:T(8,128)(2,1)S(1)}, bf16[128,896]{1,0:T(8,128)(2,1)S(1)}, u32[]{:S(2)}, u32[]{:S(2)}) collective-permute-start(bf16[128,896]{1,0:T(8,128)(2,1)S(1)} %get-tuple-element.282), channel_id=1, source_target_pairs={{0,12},{4,8},{8,4},{12,0},{1,13},{5,9},{9,5},{13,1},{2,14},{6,10},... | collective-permute-start | bytes 688136 | tf_op jit(solution)/shard_map/ppermute | solution.py:41
  197.9 25.9 %collective-permute-start.43 = (bf16[64,1024]{1,0:T(8,128)(2,1)S(1)}, bf16[64,1024]{1,0:T(8,128)(2,1)S(1)}, u32[]{:S(2)}, u32[]{:S(2)}) collective-permute-start(bf16[64,1024]{1,0:T(8,128)(2,1)S(1)} %get-tuple-element.269.refs_0_), channel_id=1, source_target_pairs={{0,3},{1,2},{2,1},{3,0},{4,7},{5,6},{6,5},{7,4},{8,11},{9,10},{10,... | collective-permute-start | bytes 393224 | tf_op jit(solution)/shard_map/ppermute | solution.py:41
  198.6 25.2 %collective-permute-start.42 = (bf16[64,1024]{1,0:T(8,128)(2,1)S(1)}, bf16[64,1024]{1,0:T(8,128)(2,1)S(1)}, u32[]{:S(2)}, u32[]{:S(2)}) collective-permute-start(bf16[64,1024]{1,0:T(8,128)(2,1)S(1)} %get-tuple-element.269.refs_0_), channel_id=1, source_target_pairs={{0,2},{1,3},{2,0},{3,1},{4,6},{5,7},{6,4},{7,5},{8,10},{9,11},{10,... | collective-permute-start | bytes 393224 | tf_op jit(solution)/shard_map/ppermute | solution.py:41
  208.2 15.7 %collective-permute-start.41 = (bf16[64,1024]{1,0:T(8,128)(2,1)S(1)}, bf16[64,1024]{1,0:T(8,128)(2,1)S(1)}, u32[]{:S(2)}, u32[]{:S(2)}) collective-permute-start(bf16[64,1024]{1,0:T(8,128)(2,1)S(1)} %get-tuple-element.269.refs_0_), channel_id=1, source_target_pairs={{0,1},{1,0},{2,3},{3,2},{4,5},{5,4},{6,7},{7,6},{8,9},{9,8},{10,11... | collective-permute-start | bytes 393224 | tf_op jit(solution)/shard_map/ppermute | solution.py:41
  (40 other events, 651.9 us)

commit v4 on v3

--- a/solution.py
+++ b/solution.py
@@ -132,25 +132,17 @@
     return lax.optimization_barrier((first, then))
 
 
-def pieces_kernel(me_ref, cot_ref, routes_ref, router_ref, both_ref, c1, c2, router_out, held):
-    rows, width = c1.shape[0], cot_ref.shape[1]
+def pieces_kernel(me_ref, cot_ref, routes_ref, router_ref, *refs):
+    cots, (router_out, held) = refs[:-2], refs[-2:]
+    rows, width = cots[0].shape[0], cot_ref.shape[1]
     eye = lax.broadcasted_iota(jnp.int32, (TOP, LANES), 0) == lane_of((TOP, LANES))
     held[...] = tn(routes_ref[...].astype(F32).astype(BF), eye.astype(F32).astype(BF))
-    for r, c in enumerate((both_ref.at[0], c1, c2, both_ref.at[1])):
+    for r, c in enumerate(cots):
         start = pl.multiple_of((me_ref[0] ^ r) * rows, rows)
         c[:, :width] = cot_ref[pl.ds(start, rows), :]
         c[:, width:] = held[pl.ds(start, rows), :].astype(BF)
     router_out[...] = jnp.zeros(router_out.shape, BF)
     router_out[: router_ref.shape[0], :] = router_ref[...]
-
-
-def sorted_cots_kernel(own_ref, *refs):
-    others, (far_ref, first_ref, last_ref) = refs[:-3], refs[-3:]
-    for i, x in enumerate((own_ref, *others)):
-        first_ref[i] = x[0]
-        last_ref[i] = x[1]
-        if i:
-            far_ref[i - 1] = x[0]
 
 
 def attend_kernel(
@@ -247,6 +239,20 @@
     return chosen
 
 
+def counts_kernel(*refs):
+    pieces, out = refs[:-1], refs[-1]
+    total = 0.0
+    for piece in pieces:
+        width = piece.shape[-1] - LANES
+        blocks = [piece[:, width:]] if len(piece.shape) == 2 else [
+            piece[i, :, width:] for i in range(piece.shape[0])
+        ]
+        for routes in blocks:
+            named = chosen_of(lane_of(routes.shape), routes).astype(F32)
+            total = total + jnp.sum(named, axis=0, keepdims=True)
+    out[...] = total
+
+
 def weights_kernel(wg_ref, wu_ref, out_ref):
     hidden = wg_ref.shape[2]
     out_ref[:, :hidden] = wg_ref[0]
@@ -268,14 +274,19 @@
     )(w_gate, w_up)
 
 
-def experts_kernel(experts, base_ref, x_ref, c_ref, router_ref, wcat, wd_ref, dgu_ref, hg_ref, d_ref, m_ref, count_ref):
+def experts_kernel(experts, base_ref, x_ref, own_ref, far_ref, router_ref, wcat, wd_ref, *refs):
+    cot_ref, dgu_ref, hg_ref, *ds, m_ref = refs
     hidden = LANES
     pair = 2 * hidden
-    width = x_ref.shape[1]
-    x = x_ref[...]
-    routes = c_ref[:, width:]
-    named = chosen_of(lane_of(routes.shape), routes).astype(F32)
-    count_ref[0] = jnp.broadcast_to(jnp.sum(named, axis=0, keepdims=True), count_ref.shape[1:])
+    rows, width = cot_ref.shape
+    x = x_ref[...].reshape(rows, width)
+    if far_ref is None:
+        routes = own_ref[:, width:]
+        cot_ref[...] = own_ref[:, :width]
+    else:
+        pieces = [own_ref[...]] + [far_ref[i] for i in range(far_ref.shape[0])]
+        routes = jnp.concatenate([piece[:, width:] for piece in pieces], axis=0)
+        cot_ref[...] = jnp.concatenate([piece[:, :width] for piece in pieces], axis=0)
     _, gates = router_of(x, router_ref, routes, experts)
     lane = lane_of(gates.shape)
     dots = jnp.zeros(gates.shape, F32)
@@ -283,7 +294,7 @@
         mine = lane == base_ref[0] + e
         g = jnp.sum(jnp.where(mine, gates, 0.0), axis=-1, keepdims=True)
         both = nn(x, wcat[:, e * pair : (e + 1) * pair])
-        v = nt(c_ref[:, :width], wd_ref[e * hidden : (e + 1) * hidden, :])
+        v = nt(cot_ref[...], wd_ref[e * hidden : (e + 1) * hidden, :])
         gate, up = both[:, :hidden], both[:, hidden:]
         sig = 1.0 / (1.0 + jnp.exp(-gate))
         act = gate * sig
@@ -294,39 +305,86 @@
         d_gate = gv * up * sig * (1.0 + gate * (1.0 - sig))
         dgu_ref[:, e * pair : e * pair + hidden] = d_gate.astype(BF)
         dgu_ref[:, e * pair + hidden : (e + 1) * pair] = (gv * act).astype(BF)
-    d_ref[:, width:] = dots.astype(d_ref.dtype)
+
+    def put(outs, columns, value):
+        at = 0
+        for out in outs:
+            part = value.astype(out.dtype)
+            if len(out.shape) == 2:
+                out[:, columns] = part[at : at + out.shape[0]]
+                at += out.shape[0]
+            else:
+                step = out.shape[1]
+                for i in range(out.shape[0]):
+                    out[i, :, columns] = part[i * step : (i + 1) * step]
+
+    put(ds, slice(width, width + LANES), dots)
     step = 256
     for at in range(0, width, step):
-        d_ref[:, at : at + step] = nt(dgu_ref[...], wcat[at : at + step, :]).astype(d_ref.dtype)
-    m_ref[...] = nn(hg_ref[...], wd_ref[...]).astype(m_ref.dtype)
-
-
-def run_experts(experts, base, x, c, router, wcat, down_flat, kind):
+        put(ds, slice(at, at + step), nt(dgu_ref[...], wcat[at : at + step, :]))
+    put([m_ref], slice(0, width), nn(hg_ref[...], wd_ref[...]))
+
+
+def run_experts(experts, base, x, own, far, router, wcat, down_flat, kind, apart=False):
     count, rows, width = x.shape
     inner = down_flat.shape[0]
     wide = width + LANES
     total = count * rows
-    step = min(total, 256)
-    per = lambda w: pl.BlockSpec((step, w), lambda i: (i, 0))
+    few = count <= FEW
+    step = total if few else 256
     resident = pl.BlockSpec(memory_space=pltpu.VMEM)
-    dgu, hid, d, m, counts = pl.pallas_call(
-        functools.partial(experts_kernel, experts),
+    per = lambda w: resident if few else pl.BlockSpec((step, w), lambda i: (i, 0))
+    kernel = functools.partial(experts_kernel, experts)
+    if few:
+        data, dims = [x, own, far], lambda w: (count, rows, w)
+    else:
+        joined = jnp.concatenate([own[None], far], axis=0)
+        data, dims = [x.reshape(total, width), joined.reshape(total, wide)], lambda w: (total, w)
+        whole_kernel = kernel
+        kernel = lambda b, x, c, *refs: whole_kernel(b, x, c, None, *refs)
+    if few and apart:
+        d_shapes = [shape((rows, wide), BF if i else F32) for i in range(count)]
+    else:
+        d_shapes = [shape(dims(wide), kind)]
+    cot, dgu, hid, *d, m = pl.pallas_call(
+        kernel,
         grid=(total // step,),
-        in_specs=[pl.BlockSpec(memory_space=pltpu.SMEM), per(width), per(wide)] + [resident] * 3,
-        out_specs=[per(2 * inner), per(inner), per(wide), per(width)]
-        + [pl.BlockSpec((1, 8, LANES), lambda i: (i, 0, 0))],
+        in_specs=[pl.BlockSpec(memory_space=pltpu.SMEM)]
+        + [per(z.shape[-1]) for z in data]
+        + [resident] * 3,
+        out_specs=[per(width), per(2 * inner), per(inner)]
+        + [per(wide)] * len(d_shapes)
+        + [per(width)],
         out_shape=[
+            shape((total, width), BF),
             shape((total, 2 * inner), BF),
             shape((total, inner), BF),
-            shape((total, wide), kind),
-            shape((total, width), kind),
-            shape((total // step, 8, LANES), F32),
+            *d_shapes,
+            shape(dims(width), BF),
         ],
         compiler_params=pltpu.CompilerParams(vmem_limit_bytes=30 * MIB),
-        cost_estimate=pl.CostEstimate(flops=int(100.0*(12 * total * width * inner)), bytes_accessed=0, transcendentals=0),
+        cost_estimate=pl.CostEstimate(flops=int(100.0*(total * width * inner // 8)), bytes_accessed=0, transcendentals=0),
         name="experts",
-    )(base, x.reshape(total, width), c.reshape(total, wide), router, wcat, down_flat)
-    return dgu, hid, d.reshape(count, rows, wide), m.reshape(count, rows, width), counts
+    )(base, *data, router, wcat, down_flat)
+    if not few:
+        d = list(d[0].reshape(count, rows, wide)) if apart else [d[0].reshape(count, rows, wide)]
+    return cot, dgu, hid, d if apart else d[0], m.reshape(count, rows, width)
+
+
+def ordered_rows_kernel(me_ref, *refs):
+    pieces, out = refs[:-1], refs[-1]
+    for r, piece in enumerate(pieces):
+        for i in range(piece.shape[0]):
+            out[me_ref[1] ^ r, me_ref[0] ^ i] = piece[i]
+
+
+def ordered_rows(me, pieces):
+    count, *dims = pieces[0].shape
+    if count <= FEW:
+        out = [shape((len(pieces), count, *dims), pieces[0].dtype)]
+        return call(ordered_rows_kernel, out, (me, *pieces), "ordered_rows", "s")[0]
+    rows = jnp.take(jnp.stack(pieces), jnp.arange(len(pieces)) ^ me[1], axis=0)
+    return jnp.take(rows, jnp.arange(count) ^ me[0], axis=1)
 
 
 def split_sum_kernel(count, near, *refs):
@@ -363,7 +421,7 @@
     both, down = 0.0, 0.0
     for n, dgu, h, c in zip(ns, dgus, hs, cs):
         both = both + tn(n[...], dgu[...])
-        down = down + tn(h[...], c[:, :width])
+        down = down + tn(h[...], c[...])
     out_ref[0, :width, :] = both[:, :hidden].astype(BF)
     out_ref[0, width : 2 * width, :] = both[:, hidden:].astype(BF)
     for at in range(0, width, hidden):
@@ -429,7 +487,7 @@
         near = near + other[...].astype(F32)
     rows, width = h_ref.shape
     dots = near[:, width:]
-    probs, gates = router_of(n_ref[...], router_ref, cot_ref[0, :, width:], experts)
+    probs, gates = router_of(n_ref[...], router_ref, cot_ref[:, width:], experts)
     bal = bal_ref[...]
     d_chosen = gates * (dots - jnp.sum(gates * dots, axis=-1, keepdims=True))
     dz = probs * (bal - jnp.sum(probs * bal, axis=-1, keepdims=True)) + d_chosen
@@ -439,7 +497,7 @@
     h = h_ref[...]
     inv = lax.rsqrt(jnp.mean(h * h, axis=-1, keepdims=True) + EPS)
     u = gain_ref[...] * dn
-    dy = cot_ref[0, :, :width].astype(F32)
+    dy = cot_ref[:, :width].astype(F32)
     dh = dy + inv * u - h * (inv * inv * inv * jnp.mean(u * h, axis=-1, keepdims=True))
     dh_ref[...] = dh
     wide_ref[:, :width] = dh.astype(BF)
@@ -450,7 +508,7 @@
 
 def attend_back_kernel(
     me_ref, w0, w1, w2, w3, x_ref, q_ref, k_ref, v_ref, lse_ref, wq_ref, wk_ref, wv_ref, wo_ref, cos_ref, sin_ref,
-    small_in, wide_ref, dq_ref, p0, p1, p2, p3, do_ref, whole, small_ref
+    small_in, wide_ref, dq_ref, small_ref, p0, p1, p2, p3, do_ref, whole
 ):
     rows = w0.shape[0]
     width = x_ref.shape[1]
@@ -508,13 +566,9 @@
     inv = lax.rsqrt(jnp.mean(x * x, axis=-1, keepdims=True) + EPS)
     small_ref[...] = small_in[...]
     small_ref[0:1, :] = jnp.sum(whole[...] * x * inv, axis=0, keepdims=True)
-    small = small_ref[...]
-    high = small.astype(BF)
-    both = jnp.concatenate([high.astype(F32), small - high.astype(F32)], axis=0).astype(BF)
     for r, part in enumerate((p0, p1, p2, p3)):
         start = pl.multiple_of((me_ref[0] ^ r) * rows, rows)
-        part[:rows, :] = whole[pl.ds(start, rows), :].astype(part.dtype)
-        part[rows:, :] = both.astype(part.dtype)
+        part[...] = whole[pl.ds(start, rows), :].astype(part.dtype)
 
 
 def dense_kernel(me_ref, a0, a1, a2, a3, wide_ref, o_ref, n_ref, dq_ref, kept_ref, sent_ref, two_ref, whole):
@@ -531,24 +585,24 @@
     sent_ref[...] = whole[pl.ds(pl.multiple_of((1 - me_ref[0]) * half, half), half), :].astype(BF)
 
 
-def input_grad_kernel(me_ref, x_ref, gain_ref, dh_ref, *refs):
-    parts, (ig_ref, small_ref, held) = refs[:-3], refs[-3:]
-    rows = dh_ref.shape[0]
+def input_grad_kernel(x_ref, gain_ref, dh_ref, *refs):
+    parts, ig_ref = refs[:-1], refs[-1]
     x = x_ref[...].astype(F32)
     inv = lax.rsqrt(jnp.mean(x * x, axis=-1, keepdims=True) + EPS)
-    dn = parts[0][:rows, :].astype(F32)
+    dn = parts[0][...].astype(F32)
     for part in parts[1:]:
-        dn = dn + part[:rows, :].astype(F32)
+        dn = dn + part[...].astype(F32)
     u = gain_ref[...] * dn
     ig = dh_ref[...] + inv * u - x * (inv * inv * inv * jnp.mean(u * x, axis=-1, keepdims=True))
     ig_ref[...] = ig.astype(BF)
-    for r, part in enumerate(parts):
-        both = part[rows:, :].astype(F32)
-        held[me_ref[0] ^ r] = both[:8] + both[8:]
-    total = held[0]
-    for i in range(1, len(parts)):
-        total = total + held[i]
-    small_ref[...] = total
+
+
+def out_kernel(h_ref, moe_ref, small_ref, out_ref):
+    rows = h_ref.shape[0]
+    out_ref[:rows, :] = (h_ref[...] + moe_ref[...].astype(F32)).astype(BF)
+    small = small_ref[...]
+    high = small.astype(BF).astype(F32)
+    out_ref[rows:, :] = jnp.concatenate([high, small - high], axis=0).astype(BF)
 
 
 def natural_kernel(me_ref, *refs):
@@ -557,6 +611,20 @@
     for r, piece in enumerate(pieces):
         start = pl.multiple_of((me_ref[0] ^ r) * rows, rows)
         out[pl.ds(start, rows), :] = piece[...].astype(out.dtype)
+
+
+def out_whole_kernel(me_ref, *refs):
+    pieces, (out_ref, small_ref, held) = refs[:-3], refs[-3:]
+    rows = pieces[0].shape[0] - 16
+    for r, piece in enumerate(pieces):
+        start = pl.multiple_of((me_ref[0] ^ r) * rows, rows)
+        out_ref[pl.ds(start, rows), :] = piece[:rows, :]
+        both = piece[rows:, :].astype(F32)
+        held[me_ref[0] ^ r] = both[:8] + both[8:]
+    total = held[0]
+    for i in range(1, len(pieces)):
+        total = total + held[i]
+    small_ref[...] = total
 
 
 def ordered_sum_kernel(me_ref, *refs):
@@ -633,22 +701,22 @@
     e_at = e_me.astype(jnp.int32).reshape(1)
     base = (e_me * local).astype(jnp.int32).reshape(1)
     d_at = jnp.stack([d_me, t_me]).astype(jnp.int32)
+    me = jnp.stack([e_me, t_me]).astype(jnp.int32)
     cosine, sine = rope_tables(seq_len)
     gain_one, gain_two = gain_first[None], gain_second[None]
     down_flat = w_down.reshape(local * hidden, width)
 
-    cot_ends, cot_one, cot_two, router = call(
+    *cot_near, router = call(
         pieces_kernel,
-        [shape((2, rows, wide_width), BF)]
-        + [shape((rows, wide_width), BF)] * 2
-        + [shape((LANES, width), BF)],
+        [shape((rows, wide_width), BF)] * tensor_size + [shape((LANES, width), BF)],
         (t_at, cotangent, routes.T, w_router.T),
         "pieces",
         "sbbb",
         scratch=[pltpu.VMEM((seq_len, LANES), F32)],
         limit=58,
     )
-    cot_got = spread(cot_ends, "expert")
+    cot_got = spread(cot_near[0], "expert")
+    cot_got[0], tokens = tied(cot_got[0], tokens)
 
     heads, keys_wide = w_query.shape[1], w_key.shape[1]
     n_one, q, k, v, o, lse, xq, *rest = call(
@@ -669,7 +737,7 @@
         "s" + "b" * 8,
         "bbbbbbv",
         scratch=[pltpu.VMEM((seq_len, width), F32)],
-        limit=58,
+        limit=30,
         flops=2 * seq_len * width * 4 * heads,
     )
     parts = rest
@@ -683,77 +751,67 @@
         "vv",
     )
 
+    n_two, cot_got = tied(n_two, cot_got)
+    cot_far = together(cot_got)
     wcat = gate_up_weights(w_gate, w_up)
-    count = expert_size
-    cot_far, cot_first, cot_last = call(
-        sorted_cots_kernel,
-        [shape((n, rows, wide_width), BF) for n in (count - 1, count, count)],
-        (cot_ends, *cot_got),
-        "sorted_cots",
-    )
-    cot_middle = [swap(cot_far, "tensor", r) for r in range(1, last)]
-    cots = [
-        cot_first,
-        together([cot_one, cot_middle[0]]),
-        together([cot_two, cot_middle[1]]),
-        cot_last,
-    ]
-
-    two_got = []
-    for r in range(1, expert_size):
-        if expert_size <= FEW:
-            cot_got[r - 1], two = tied(cot_got[r - 1], n_two)
-            two_got.append(swap(two, "expert", r))
-    if expert_size > FEW:
-        two_got = spread(n_two, "expert")
+    two_got = spread(n_two, "expert")
+    two_got[0], cot_late = tied(two_got[0], cot_far)
+    cot_far = [cot_far] + [swap(cot_far, "tensor", r) for r in range(1, last)]
+    cot_far.append(swap(cot_late, "tensor", last))
+
     first = together([n_two, *two_got])
     twos = [first] + [swap(first, "tensor", r) for r in range(1, last)]
-    _, late = tied(cot_middle, first)
+    _, late = tied(cot_far[:last], first)
     twos.append(swap(late, "tensor", last))
 
     run = functools.partial(
         run_experts, experts, base, router=router, wcat=wcat, down_flat=down_flat
     )
-    made = [run(twos[0], cots[0], kind=F32)]
+    counts = call(counts_kernel, [shape((1, LANES), F32)], (*cot_near, *cot_far), "counts")[0]
+    counts = counts + swap(counts, "dp", 1)
+    balance = experts * (counts / (token_count * TOP)) / token_count
+    made = [run(twos[0], cot_near[0], cot_far[0], kind=F32)]
     got = []
     for r in around:
-        held, (two, cot) = tied(made[-1], (twos[r], cots[r]))
-        made[-1] = held
-        made.append(run(two, cot, kind=BF))
-        got.append(swap(made[-1][2], "tensor", r))
-    dgus, hids, ds, moes, counts = zip(*made)
+        made[-1], (two, cot) = tied(made[-1], (twos[r], cot_far[r]))
+        if r == last:
+            balance, two = tied(balance, two)
+        made.append(run(two, cot_near[r], cot, kind=BF, apart=r == last))
+        if r < last:
+            got.append(swap(made[-1][3], "tensor", r))
+    cots, dgus, hids, ds, moes = zip(*made)
+    near_last, *far_last = ds[last]
+    from_last = deal(far_last, "expert")
     grads = run_grads(twos, dgus, hids, cots, local, hidden)
-    counts = sum(jnp.sum(x[:, :1], axis=0) for x in counts)
-    counts = counts + swap(counts, "dp", 1)
-    balance = experts * (counts / (token_count * TOP)) / token_count
-    grads, got = tied(grads, got)
-    got, moes = tied(got, moes)
+    grads, (got, from_last) = tied(grads, (got, from_last))
     near, *across = split_sum([ds[0], *got], "dn_sum")
-    near_sums = [near, *deal(across, "expert")]
-    moe_got = [swap(moes[r], "tensor", r) for r in range(1, last)]
-    moe_got, near_sums = tied(moe_got, near_sums)
+    across, moes = tied(across, moes)
+    moe = lax.psum_scatter(ordered_rows(me, moes), "tensor", scatter_dimension=0, tiled=False)
+    through = added([near_last, *from_last], BF, "through")
+    near_sums = [near, swap(through, "tensor", last), *deal(across, "expert")]
 
     wide, dh, small = call(
         functools.partial(norm_back_kernel, experts, len(near_sums)),
         [shape((rows, wide_width), BF), shape((rows, width), F32), shape((8, width), F32)],
-        (h, n_two, gain_two, router, balance, cot_ends, *near_sums),
+        (h, n_two, gain_two, router, balance, cot_near[0], *near_sums),
         "norm_back",
         "v",
         "vvv",
     )
     wides = [wide] + [swap(wide, "tensor", r) for r in around]
-    wides, grads = tied(wides, grads)
-    moe_got.append(swap(moes[last], "tensor", last))
-    moe_got, wides = tied(moe_got, wides)
-    part_rows = rows + 16
-    wide_all, dqkv, *back_parts = call(
+    grads_got = swap(grads, "dp", 1)
+    (moe, grads_got), wides = tied((moe, grads_got), wides)
+    moe = lax.psum_scatter(moe, "expert", scatter_dimension=0, tiled=False)
+
+    wide_all, dqkv, small, *back_parts = call(
         attend_back_kernel,
         [
             shape((seq_len, wide_width), BF),
             shape((seq_len, heads + 2 * keys_wide), BF),
-            shape((part_rows, width), F32),
+            shape((8, width), F32),
+            shape((rows, width), F32),
         ]
-        + [shape((part_rows, width), BF)] * last,
+        + [shape((rows, width), BF)] * last,
         (t_at, *wides, tokens, q, k, v, lse, w_query, w_key, w_value, w_output, cosine, sine, small),
         "attend_back",
         "s" + "v" * tensor_size + "b" * 11,
@@ -762,38 +820,10 @@
         scratch=[
             pltpu.VMEM((seq_len, heads), BF),
             pltpu.VMEM((seq_len, width), F32),
-            pltpu.VMEM((8, width), F32),
         ],
         flops=2 * seq_len * width * 4 * heads,
     )
     part_sums = [back_parts[0]] + [swap(back_parts[r], "tensor", r) for r in around]
-    part_sums, moe_got = tied(part_sums, moe_got)
-    moe_near, *moe_across = split_sum([moes[0], *moe_got], "moe_sum")
-    moe_sums = [moe_near, *deal(moe_across, "expert")]
-    ig, small = call(
-        input_grad_kernel,
-        [shape((rows, width), BF), shape((8, width), F32)],
-        (t_at, xq, gain_one, dh, *part_sums),
-        "input_grad",
-        "svbv",
-        scratch=[pltpu.VMEM((tensor_size, 8, width), F32)],
-    )
-    igs = [ig] + [swap(ig, "tensor", r) for r in around]
-    expert_grads = both_copies(grads, swap(grads, "dp", 1))
-    expert_grads, igs = tied(expert_grads, igs)
-    input_grad = call(
-        natural_kernel, [shape((seq_len, width), F32)], (t_at, *igs), "input_grad_whole", "s", "b"
-    )[0]
-    out_piece = added([h, *moe_sums], BF, "out_piece")
-    output = call(
-        natural_kernel,
-        [shape((seq_len, width), BF)],
-        (t_at, out_piece, *[swap(out_piece, "tensor", r) for r in around]),
-        "output",
-        "s",
-        "b",
-    )[0]
-
     half = width // dp_size
     chunk = half // expert_size
 
@@ -812,7 +842,7 @@
             pltpu.VMEM((seq_len, width), BF),
             pltpu.VMEM((width, all_columns), F32),
         ],
-        flops=2 * seq_len * width * all_columns,
+        flops=1,
     )
     mine, *others = call(
         kept_and_dealt_kernel,
@@ -820,6 +850,28 @@
         (e_at, kept, swap(sent, "dp", 1)),
         "dense_dealt",
         "s",
+    )
+    (mine, others), part_sums = tied((mine, others), part_sums)
+    ig = call(
+        input_grad_kernel, [shape((rows, width), BF)], (xq, gain_one, dh, *part_sums), "input_grad", "vb"
+    )[0]
+    igs = [ig] + [swap(ig, "tensor", r) for r in around]
+    expert_grads = both_copies(grads, grads_got)
+    expert_grads, igs = tied(expert_grads, igs)
+    input_grad = call(
+        natural_kernel, [shape((seq_len, width), F32)], (t_at, *igs), "input_grad_whole", "s", "b"
+    )[0]
+    small = small + swap(small, "dp", 1)
+    small = ordered_sum(e_at, [small, *spread(small, "expert")])
+    out_piece = call(out_kernel, [shape((rows + 16, width), BF)], (h, moe, small), "out_piece")[0]
+    output, small = call(
+        out_whole_kernel,
+        [shape((seq_len, width), BF), shape((8, width), F32)],
+        (t_at, out_piece, *[swap(out_piece, "tensor", r) for r in around]),
+        "output",
+        "s",
+        "bv",
+        scratch=[pltpu.VMEM((tensor_size, 8, width), F32)],
     )
     g_query, g_key, g_value, g_out, g_router = call(
         dense_sum_kernel,
@@ -836,8 +888,6 @@
         "bbbbb",
     )
 
-    small = small + swap(small, "dp", 1)
-    small = ordered_sum(e_at, [small, *spread(small, "expert")])
     at = (d_me * expert_size + e_me) * chunk
     loss_value = (experts * balance * small[2:3, :LANES])[0, :experts]
     return (
@@ -851,9 +901,7 @@
         g_out,
         lax.dynamic_slice(small, (1, at), (1, chunk))[0],
         g_router[:, :experts],
-        expert_grads[0],
-        expert_grads[1],
-        expert_grads[2],
+        *expert_grads,
     )
 
 

time: 226 us -> 230 us (1.018)
  between operations: 1.11 us -> 14.4 us
  local copies, waits for them, and re-layouts: 9.21 us -> 18.1 us
  waiting for transfers between devices: 73.2 us -> 64.6 us
  starting transfers between devices: 65.7 us -> 58.5 us
  Pallas kernels: 74.5 us -> 72 us
    ppermute x48 -> x46, waiting for transfers between devices: 73.2 us -> 49.8 us  [swap(): return lax.ppermute(x, axis, [(i, i ^ distance) for i in range(size)])]
    unnamed x0 -> x3, waiting for transfers between devices: none -> 14.9 us
    unnamed x81 -> x89, local copies, waits for them, and re-layouts: 8.7 us -> 17.6 us
    ppermute x48 -> x46, starting transfers between devices: 65.7 us -> 58.1 us  [swap(): return lax.ppermute(x, axis, [(i, i ^ distance) for i in range(size)])]
  transfers between devices with their start and end apart: 48 -> 48, of which waited for: 21 -> 18; matrix products, arithmetic and copies ran while one was open for 1% -> 1% of each run, Pallas kernels for 32% -> 26%
where the time goes in v4:
time: 230 us; the launch traced here: 229 us
  Pallas kernels  72 us (31%)
  waiting for transfers between devices  64.6 us (28%)
  starting transfers between devices  58.5 us (25%)
  local copies, waits for them, and re-layouts  18.1 us (8%)
  between operations  14.4 us (6%)
    ppermute x46, starting transfers between devices, swap(): return lax.ppermute(x, axis, [(i, i ^ distance) for i in range(size)])  58.1 us
    ppermute x46, waiting for transfers between devices, swap(): return lax.ppermute(x, axis, [(i, i ^ distance) for i in range(size)])  49.8 us
    pallas_call x19, Pallas kernels, call(): pl.pallas_call(kernel, grid=(1,), out_shape=outs, in_specs=[spec(p, x) fo...  25 us
    pallas_call x4, Pallas kernels, run_experts(): pl.pallas_call(kernel, grid=(total // step,), in_specs=[pl.BlockSpec(memo...  23.5 us
    unnamed x89, local copies, waits for them, and re-layouts  17.6 us
    unnamed x3, waiting for transfers between devices  14.9 us
    pallas_call x1, Pallas kernels, both_copies(): pl.pallas_call(both_copies_kernel, grid=(local,), in_specs=[block(rows, h...  11.1 us
    pallas_call x1, Pallas kernels, run_grads(): pl.pallas_call(grads_kernel, grid=(local,), in_specs=whole(n) + cols(dgu,...  10.8 us
  transfers between devices with their start and end apart: 48, of which 18 were waited for; matrix products, arithmetic and copies ran while one was open for 1% of the time, Pallas kernels for 26%

profile of v4, /device:TPU:0, one launch (start us, length us, event | category | flops | bytes accessed | tf_op | source)
XLA Modules:
  0.0 228.8 jit_solution(14632943259780908208)
XLA Ops:
  7.2 2.2 pieces.1
  9.4 3.0 %collective-permute-start = (bf16[64,1152]{1,0:T(8,128)(2,1)}, bf16[64,1152]{1,0:T(8,128)(2,1)S(1)}, u32[]{:S(2)}, u32[]{:S(2)}) collective-permute-start(bf16[64,1152]{1,0:T(8,128)(2,1)} %get-tuple-element.148.own_ref.refs_0_.cot_ref), channel_id=1, source_target_pairs={{0,4},{4,0},{8,12},{12,8},{1,5},{5,1},{9,13},{13,9},{2,6},{6,2},{1... | collective-permute-start | bytes 442376 | tf_op jit(solution)/shard_map/ppermute | solution.py:41
  12.4 2.5 %collective-permute-start.5 = (bf16[64,1152]{1,0:T(8,128)(2,1)}, bf16[64,1152]{1,0:T(8,128)(2,1)S(1)}, u32[]{:S(2)}, u32[]{:S(2)}) collective-permute-start(bf16[64,1152]{1,0:T(8,128)(2,1)} %get-tuple-element.148.own_ref.refs_0_.cot_ref), channel_id=1, source_target_pairs={{0,12},{4,8},{8,4},{12,0},{1,13},{5,9},{9,5},{13,1},{2,14},{6,10},... | collective-permute-start | bytes 442376 | tf_op jit(solution)/shard_map/ppermute | solution.py:41
  15.0 1.8 collective-permute-done.refs_0_
  24.3 2.1 attend.1
  30.5 1.5 collective-permute-start.1
  32.0 1.5 collective-permute-start.2
  34.0 2.6 %collective-permute-done.1.refs_0_ = bf16[64,1024]{1,0:T(8,128)(2,1)S(1)} collective-permute-done((bf16[64,1024]{1,0:T(8,128)(2,1)S(1)}, bf16[64,1024]{1,0:T(8,128)(2,1)S(1)}, u32[]{:S(2)}, u32[]{:S(2)}) %collective-permute-start.1) | collective-permute-done | bytes 131104 | tf_op jit(solution)/shard_map/ppermute | solution.py:41
  36.7 3.0 %collective-permute-done.2.refs_1_ = bf16[64,1024]{1,0:T(8,128)(2,1)S(1)} collective-permute-done((bf16[64,1024]{1,0:T(8,128)(2,1)S(1)}, bf16[64,1024]{1,0:T(8,128)(2,1)S(1)}, u32[]{:S(2)}, u32[]{:S(2)}) %collective-permute-start.2) | collective-permute-done | bytes 131104 | tf_op jit(solution)/shard_map/ppermute | solution.py:41
  39.9 2.2 collective-permute-start.6
  43.2 1.8 collective-permute-done.6.refs_1_
  45.7 6.6 %collective-permute-start.8 = (bf16[64,1024]{1,0:T(8,128)(2,1)S(1)}, bf16[64,1024]{1,0:T(8,128)(2,1)S(1)}, u32[]{:S(2)}, u32[]{:S(2)}) collective-permute-start(bf16[64,1024]{1,0:T(8,128)(2,1)S(1)} %get-tuple-element.158.refs_0_.n_ref), channel_id=1, source_target_pairs={{0,12},{4,8},{8,4},{12,0},{1,13},{5,9},{9,5},{13,1},{2,14},{6,10},... | collective-permute-start | bytes 393224 | tf_op jit(solution)/shard_map/ppermute | solution.py:41
  52.3 1.6 copy-done.1
  54.0 1.5 gate_up_weights.1.wcat
  55.5 2.7 %collective-permute-done.7.refs_2_ = bf16[64,1024]{1,0:T(8,128)(2,1)S(1)} collective-permute-done((bf16[64,1024]{1,0:T(8,128)(2,1)S(1)}, bf16[64,1024]{1,0:T(8,128)(2,1)S(1)}, u32[]{:S(2)}, u32[]{:S(2)}) %collective-permute-start.7) | collective-permute-done | bytes 131104 | tf_op jit(solution)/shard_map/ppermute | solution.py:41
  58.2 2.4 %collective-permute-start.11 = (bf16[4,64,1024]{2,1,0:T(8,128)(2,1)S(1)}, bf16[4,64,1024]{2,1,0:T(8,128)(2,1)S(1)}, u32[]{:S(2)}, u32[]{:S(2)}) collective-permute-start(bf16[4,64,1024]{2,1,0:T(8,128)(2,1)S(1)} %together.3.x_ref.a0), channel_id=1, source_target_pairs={{0,2},{1,3},{2,0},{3,1},{4,6},{5,7},{6,4},{7,5},{8,10},{9,11},{10,... | collective-permute-start | bytes 1572872 | tf_op jit(solution)/shard_map/ppermute | solution.py:41
  61.8 4.5 %collective-permute-done.14.refs_7_.far_ref = bf16[3,64,1152]{2,1,0:T(8,128)(2,1)} collective-permute-done((bf16[3,64,1152]{2,1,0:T(8,128)(2,1)S(1)}, bf16[3,64,1152]{2,1,0:T(8,128)(2,1)}, u32[]{:S(2)}, u32[]{:S(2)}) %collective-permute-start.14) | collective-permute-done | bytes 442400 | tf_op jit(solution)/shard_map/ppermute | solution.py:41
  66.4 2.4 %counts.1 = f32[1,128]{1,0:T(1,128)S(1)} custom-call(bf16[64,1152]{1,0:T(8,128)(2,1)S(1)} %copy-done.4, bf16[64,1152]{1,0:T(8,128)(2,1)S(1)} %copy-done.17, bf16[64,1152]{1,0:T(8,128)(2,1)S(1)} %copy-done.16, bf16[64,1152]{1,0:T(8,128)(2,1)S(1)} %copy-done.15, bf16[3,64,1152]{2,1,0:T(8,128)(2,1)S(1)} %together.2.far_ref.refs_4_, ...), custom_call_target="tpu_custom_call" | custom-call | tf_op jit(solution)/shard_map/counts/pallas_call | solution.py:118
  68.8 4.5 %experts.4 = (bf16[256,1024]{1,0:T(8,128)(2,1)S(1)}, bf16[256,2048]{1,0:T(8,128)(2,1)S(1)}, bf16[256,1024]{1,0:T(8,128)(2,1)S(1)}, f32[4,64,1152]{2,1,0:T(8,128)S(1)}, bf16[4,64,1024]{2,1,0:T(8,128)(2,1)S(1)}) custom-call(s32[1]{0:T(128)} %bitcast.6.base_ref, bf16[4,64,1024]{2,1,0:T(8,128)(2,1)S(1)} %together.3.x_ref.a0, bf16[64,1152]{1,0:T(8,128)(2,1)S(1)} %copy-done.4, ...), custom_call_target="tpu_custom_call" | custom-call | flops 3355443200 | tf_op jit(solution)/shard_map/experts/pallas_call | solution.py:349
  73.9 6.2 %experts.5 = (bf16[256,1024]{1,0:T(8,128)(2,1)S(1)}, bf16[256,2048]{1,0:T(8,128)(2,1)S(1)}, bf16[256,1024]{1,0:T(8,128)(2,1)S(1)}, bf16[4,64,1152]{2,1,0:T(8,128)(2,1)}, bf16[4,64,1024]{2,1,0:T(8,128)(2,1)S(1)}) custom-call(s32[1]{0:T(128)} %bitcast.6.base_ref, bf16[4,64,1024]{2,1,0:T(8,128)(2,1)S(1)} %collective-permute-done.9.x_ref.a1, ...), custom_call_target="tpu_custom_call" | custom-call | flops 3355443200 | tf_op jit(solution)/shard_map/experts/pallas_call | solution.py:349
  80.1 1.6 collective-permute-start.16
  81.7 6.5 %experts.6 = (bf16[256,1024]{1,0:T(8,128)(2,1)S(1)}, bf16[256,2048]{1,0:T(8,128)(2,1)S(1)}, bf16[256,1024]{1,0:T(8,128)(2,1)S(1)}, bf16[4,64,1152]{2,1,0:T(8,128)(2,1)}, bf16[4,64,1024]{2,1,0:T(8,128)(2,1)S(1)}) custom-call(s32[1]{0:T(128)} %bitcast.6.base_ref, bf16[4,64,1024]{2,1,0:T(8,128)(2,1)S(1)} %collective-permute-done.11.x_ref.a2, ...), custom_call_target="tpu_custom_call" | custom-call | flops 3355443200 | tf_op jit(solution)/shard_map/experts/pallas_call | solution.py:349
  89.7 6.2 %experts.7 = (bf16[256,1024]{1,0:T(8,128)(2,1)S(1)}, bf16[256,2048]{1,0:T(8,128)(2,1)S(1)}, bf16[256,1024]{1,0:T(8,128)(2,1)S(1)}, f32[64,1152]{1,0:T(8,128)S(1)...) custom-call(s32[1]{0:T(128)} %bitcast.6.base_ref, ...), custom_call_target="tpu_custom_call" | custom-call | flops 3355443200 | tf_op jit(solution)/shard_map/experts/pallas_call | solution.py:349
  96.0 4.0 %collective-permute-start.19 = (bf16[64,1152]{1,0:T(8,128)(2,1)}, bf16[64,1152]{1,0:T(8,128)(2,1)}, u32[]{:S(2)}, u32[]{:S(2)}) collective-permute-start(bf16[64,1152]{1,0:T(8,128)(2,1)} %get-tuple-element.205), channel_id=1, source_target_pairs={{0,8},{4,12},{8,0},{12,4},{1,9},{5,13},{9,1},{13,5},{2,10},{6,14},... | collective-permute-start | bytes 442376 | tf_op jit(solution)/shard_map/ppermute | solution.py:41
  100.4 10.8 %expert_grads.1.mine_ref = bf16[8,3072,128]{2,1,0:T(8,128)(2,1)} custom-call(bf16[256,1024]{1,0:T(8,128)(2,1)S(1)} %bitcast.23, bf16[256,1024]{1,0:T(8,128)(2,1)S(1)} %bitcast.25, bf16[256,1024]{1,0:T(8,128)(2,1)S(1)} %bitcast.24, bf16[256,1024]{1,0:T(8,128)(2,1)S(1)} %bitcast.26, bf16[256,2048]{1,0:T(8,128)(2,1)S(1)} %get-tuple-element.171.refs_4_, ...), custom_call_target="tpu_custom_call" | custom-call | flops 644245094400 | tf_op jit(solution)/shard_map/expert_grads/pallas_call | solution.py:438
  113.7 2.0 ordered_rows.1
  116.0 2.4 %collective-permute-start.23 = (bf16[64,1152]{1,0:T(8,128)(2,1)S(1)}, bf16[64,1152]{1,0:T(8,128)(2,1)S(1)}, u32[]{:S(2)}, u32[]{:S(2)}) collective-permute-start(bf16[64,1152]{1,0:T(8,128)(2,1)S(1)} %copy-done.32), channel_id=1, source_target_pairs={{0,4},{4,0},{8,12},{12,8},{1,5},{5,1},{9,13},{13,9},{2,6},{6,2},{1... | collective-permute-start | bytes 442376 | tf_op jit(solution)/shard_map/ppermute | solution.py:41
  118.4 1.6 collective-permute-start.24
  123.4 2.5 %collective-permute-done.23.refs_2_ = bf16[64,1152]{1,0:T(8,128)(2,1)S(1)} collective-permute-done((bf16[64,1152]{1,0:T(8,128)(2,1)S(1)}, bf16[64,1152]{1,0:T(8,128)(2,1)S(1)}, u32[]{:S(2)}, u32[]{:S(2)}) %collective-permute-start.23) | collective-permute-done | bytes 147488 | tf_op jit(solution)/shard_map/ppermute | solution.py:41
  125.8 6.5 %collective-permute-done.24.refs_3_ = bf16[64,1152]{1,0:T(8,128)(2,1)S(1)} collective-permute-done((bf16[64,1152]{1,0:T(8,128)(2,1)S(1)}, bf16[64,1152]{1,0:T(8,128)(2,1)S(1)}, u32[]{:S(2)}, u32[]{:S(2)}) %collective-permute-start.24) | collective-permute-done | bytes 147488 | tf_op jit(solution)/shard_map/ppermute | solution.py:41
  136.3 1.6 collective-permute-start.26
  138.4 5.1 %collective-permute-done.28.w3 = bf16[64,1152]{1,0:T(8,128)(2,1)S(1)} collective-permute-done((bf16[64,1152]{1,0:T(8,128)(2,1)S(1)}, bf16[64,1152]{1,0:T(8,128)(2,1)S(1)}, u32[]{:S(2)}, u32[]{:S(2)}) %collective-permute-start.28) | collective-permute-done | bytes 147488 | tf_op jit(solution)/shard_map/ppermute | solution.py:41
  143.6 1.5 collective-permute-done.27.w2
  145.1 14.8 %reduce-scatter.7.cloned.1.call-done = bf16[1,4,64,1024]{3,2,1,0:T(8,128)(2,1)} async-done(((bf16[4,4,64,1024]{3,2,1,0:T(8,128)(2,1)}), bf16[1,4,64,1024]{3,2,1,0:T(8,128)(2,1)}) %reduce-scatter.7.cloned.1.call-update) | async-done | bytes 524304
  160.0 5.5 %attend_back.1 = (bf16[256,1152]{1,0:T(8,128)(2,1)}, bf16[256,512]{1,0:T(8,128)(2,1)}, f32[8,1024]{1,0:T(8,128)}, f32[64,1024]{1,0:T(8,128)}, bf16[64,1024]{1,0:...) custom-call(s32[1]{0:T(128)} %bitcast.me_ref, bf16[64,1152]{1,0:T(8,128)(2,1)} %copy-done.30, ...), custom_call_target="tpu_custom_call" | custom-call | flops 53687091200 | tf_op jit(solution)/shard_map/attend_back/pallas_call | solution.py:118
  165.5 4.0 %dense.1 = (f32[512,896]{1,0:T(8,128)}, bf16[512,896]{1,0:T(8,128)(2,1)}) custom-call(s32[2]{0:T(128)} %pad_add_fusion.1.me_ref, bf16[4,64,1024]{2,1,0:T(8,128)(2,1)} %copy-done.2, bf16[4,64,1024]{2,1,0:T(8,128)(2,1)} %copy-done.10, bf16[4,64,1024]{2,1,0:T(8,128)(2,1)} %copy-done.9, bf16[4,64,1024]{2,1,0:T(8,128)(2,1)} %copy-done.11, ...), custom_call_target="tpu_custom_call" | custom-call | flops 100 | tf_op jit(solution)/shard_map/dense/pallas_call | solution.py:118
  169.6 1.5 collective-permute-start.37
  173.1 1.5 copy-done.3
  176.1 3.6 %collective-permute-done.38.refs_2_ = bf16[64,1024]{1,0:T(8,128)(2,1)S(1)} collective-permute-done((bf16[64,1024]{1,0:T(8,128)(2,1)}, bf16[64,1024]{1,0:T(8,128)(2,1)S(1)}, u32[]{:S(2)}, u32[]{:S(2)}) %collective-permute-start.38) | collective-permute-done | bytes 131104 | tf_op jit(solution)/shard_map/ppermute | solution.py:41
  179.7 1.5 collective-permute-start.43
  181.4 1.5 collective-permute-start.42
  184.1 2.4 %collective-permute-start.32 = (f32[8,1024]{1,0:T(8,128)S(1)}, f32[8,1024]{1,0:T(8,128)S(1)}, u32[]{:S(2)}, u32[]{:S(2)}) collective-permute-start(f32[8,1024]{1,0:T(8,128)S(1)} %add.18.refs_0_), channel_id=1, source_target_pairs={{0,12},{4,8},{8,4},{12,0},{1,13},{5,9},{9,5},{13,1},{2,14},{6,10},... | collective-permute-start | bytes 98312 | tf_op jit(solution)/shard_map/ppermute | solution.py:41
  187.2 6.8 %collective-permute-done.32.refs_3_ = f32[8,1024]{1,0:T(8,128)S(1)} collective-permute-done((f32[8,1024]{1,0:T(8,128)S(1)}, f32[8,1024]{1,0:T(8,128)S(1)}, u32[]{:S(2)}, u32[]{:S(2)}) %collective-permute-start.32) | collective-permute-done | bytes 32800 | tf_op jit(solution)/shard_map/ppermute | solution.py:41
  194.1 1.5 collective-permute-start.40
  195.5 3.9 %collective-permute-done.30.refs_1_ = f32[8,1024]{1,0:T(8,128)S(1)} collective-permute-done((f32[8,1024]{1,0:T(8,128)S(1)}, f32[8,1024]{1,0:T(8,128)S(1)}, u32[]{:S(2)}, u32[]{:S(2)}) %collective-permute-start.30) | collective-permute-done | bytes 32800 | tf_op jit(solution)/shard_map/ppermute | solution.py:41
  199.7 2.1 collective-permute-start.45
  202.8 1.9 collective-permute-start.35
  206.4 11.1 %both_copies.1 = (f32[8,1024,128]{2,1,0:T(8,128)}, f32[8,1024,128]{2,1,0:T(8,128)}, f32[8,128,1024]{2,1,0:T(8,128)}) custom-call(bf16[8,3072,128]{2,1,0:T(8,128)(2,1)} %expert_grads.1.mine_ref, bf16[8,3072,128]{2,1,0:T(8,128)(2,1)} %collective-permute-done.21.other_ref), custom_call_target="tpu_custom_call" | custom-call | bytes 25165824 | tf_op jit(solution)/shard_map/both_copies/pallas_call | solution.py:467
  (171 shorter events, 41.7 us)
Async XLA Ops:
  7.2 152.8 %reduce-scatter.7.cloned.1.call-start = ((), (), s32[]{:S(2)}) async-start(), calls=%async_computation.3 | async-start | bytes 2621440
  9.4 7.4 %collective-permute-start = (bf16[64,1152]{1,0:T(8,128)(2,1)}, bf16[64,1152]{1,0:T(8,128)(2,1)S(1)}, u32[]{:S(2)}, u32[]{:S(2)}) collective-permute-start(bf16[64,1152]{1,0:T(8,128)(2,1)} %get-tuple-element.148.own_ref.refs_0_.cot_ref), channel_id=1, source_target_pairs={{0,4},{4,0},{8,12},{12,8},{1,5},{5,1},{9,13},{13,9},{2,6},{6,2},{1... | collective-permute-start | bytes 442376 | tf_op jit(solution)/shard_map/ppermute | solution.py:41
  12.4 27.4 %collective-permute-start.5 = (bf16[64,1152]{1,0:T(8,128)(2,1)}, bf16[64,1152]{1,0:T(8,128)(2,1)S(1)}, u32[]{:S(2)}, u32[]{:S(2)}) collective-permute-start(bf16[64,1152]{1,0:T(8,128)(2,1)} %get-tuple-element.148.own_ref.refs_0_.cot_ref), channel_id=1, source_target_pairs={{0,12},{4,8},{8,4},{12,0},{1,13},{5,9},{9,5},{13,1},{2,14},{6,10},... | collective-permute-start | bytes 442376 | tf_op jit(solution)/shard_map/ppermute | solution.py:41
  14.9 25.0 %collective-permute-start.4 = (bf16[64,1152]{1,0:T(8,128)(2,1)}, bf16[64,1152]{1,0:T(8,128)(2,1)S(1)}, u32[]{:S(2)}, u32[]{:S(2)}) collective-permute-start(bf16[64,1152]{1,0:T(8,128)(2,1)} %get-tuple-element.148.own_ref.refs_0_.cot_ref), channel_id=1, source_target_pairs={{0,8},{4,12},{8,0},{12,4},{1,9},{5,13},{9,1},{13,5},{2,10},{6,14},... | collective-permute-start | bytes 442376 | tf_op jit(solution)/shard_map/ppermute | solution.py:41
  30.5 6.1 %collective-permute-start.1 = (bf16[64,1024]{1,0:T(8,128)(2,1)S(1)}, bf16[64,1024]{1,0:T(8,128)(2,1)S(1)}, u32[]{:S(2)}, u32[]{:S(2)}) collective-permute-start(bf16[64,1024]{1,0:T(8,128)(2,1)S(1)} %get-tuple-element.152), channel_id=1, source_target_pairs={{0,1},{1,0},{2,3},{3,2},{4,5},{5,4},{6,7},{7,6},{8,9},{9,8},{10,11... | collective-permute-start | bytes 393224 | tf_op jit(solution)/shard_map/ppermute | solution.py:41
  32.0 7.6 %collective-permute-start.2 = (bf16[64,1024]{1,0:T(8,128)(2,1)S(1)}, bf16[64,1024]{1,0:T(8,128)(2,1)S(1)}, u32[]{:S(2)}, u32[]{:S(2)}) collective-permute-start(bf16[64,1024]{1,0:T(8,128)(2,1)S(1)} %get-tuple-element.153), channel_id=1, source_target_pairs={{0,2},{1,3},{2,0},{3,1},{4,6},{5,7},{6,4},{7,5},{8,10},{9,11},{10,... | collective-permute-start | bytes 393224 | tf_op jit(solution)/shard_map/ppermute | solution.py:41
  33.5 6.1 %collective-permute-start.3 = (bf16[64,1024]{1,0:T(8,128)(2,1)S(1)}, bf16[64,1024]{1,0:T(8,128)(2,1)S(1)}, u32[]{:S(2)}, u32[]{:S(2)}) collective-permute-start(bf16[64,1024]{1,0:T(8,128)(2,1)S(1)} %get-tuple-element.154), channel_id=1, source_target_pairs={{0,3},{1,2},{2,1},{3,0},{4,7},{5,6},{6,5},{7,4},{8,11},{9,10},{10,... | collective-permute-start | bytes 393224 | tf_op jit(solution)/shard_map/ppermute | solution.py:41
  39.9 5.1 %collective-permute-start.6 = (bf16[64,1024]{1,0:T(8,128)(2,1)S(1)}, bf16[64,1024]{1,0:T(8,128)(2,1)S(1)}, u32[]{:S(2)}, u32[]{:S(2)}) collective-permute-start(bf16[64,1024]{1,0:T(8,128)(2,1)S(1)} %get-tuple-element.158.refs_0_.n_ref), channel_id=1, source_target_pairs={{0,4},{4,0},{8,12},{12,8},{1,5},{5,1},{9,13},{13,9},{2,6},{6,2},{1... | collective-permute-start | bytes 393224 | tf_op jit(solution)/shard_map/ppermute | solution.py:41
  42.1 19.7 %collective-permute-start.12 = (bf16[3,64,1152]{2,1,0:T(8,128)(2,1)S(1)}, bf16[3,64,1152]{2,1,0:T(8,128)(2,1)}, u32[]{:S(2)}, u32[]{:S(2)}) collective-permute-start(bf16[3,64,1152]{2,1,0:T(8,128)(2,1)S(1)} %together.2.far_ref.refs_4_), channel_id=1, source_target_pairs={{0,2},{1,3},{2,0},{3,1},{4,6},{5,7},{6,4},{7,5},{8,10},{9,11},{10,... | collective-permute-start | bytes 1327112 | tf_op jit(solution)/shard_map/ppermute | solution.py:41
  42.8 19.0 %collective-permute-start.10 = (bf16[3,64,1152]{2,1,0:T(8,128)(2,1)S(1)}, bf16[3,64,1152]{2,1,0:T(8,128)(2,1)}, u32[]{:S(2)}, u32[]{:S(2)}) collective-permute-start(bf16[3,64,1152]{2,1,0:T(8,128)(2,1)S(1)} %together.2.far_ref.refs_4_), channel_id=1, source_target_pairs={{0,1},{1,0},{2,3},{3,2},{4,5},{5,4},{6,7},{7,6},{8,9},{9,8},{10,11... | collective-permute-start | bytes 1327112 | tf_op jit(solution)/shard_map/ppermute | solution.py:41
  45.0 21.3 %collective-permute-start.14 = (bf16[3,64,1152]{2,1,0:T(8,128)(2,1)S(1)}, bf16[3,64,1152]{2,1,0:T(8,128)(2,1)}, u32[]{:S(2)}, u32[]{:S(2)}) collective-permute-start(bf16[3,64,1152]{2,1,0:T(8,128)(2,1)S(1)} %together.2.far_ref.refs_4_), channel_id=1, source_target_pairs={{0,3},{1,2},{2,1},{3,0},{4,7},{5,6},{6,5},{7,4},{8,11},{9,10},{10,... | collective-permute-start | bytes 1327112 | tf_op jit(solution)/shard_map/ppermute | solution.py:41
  45.7 9.8 %collective-permute-start.8 = (bf16[64,1024]{1,0:T(8,128)(2,1)S(1)}, bf16[64,1024]{1,0:T(8,128)(2,1)S(1)}, u32[]{:S(2)}, u32[]{:S(2)}) collective-permute-start(bf16[64,1024]{1,0:T(8,128)(2,1)S(1)} %get-tuple-element.158.refs_0_.n_ref), channel_id=1, source_target_pairs={{0,12},{4,8},{8,4},{12,0},{1,13},{5,9},{9,5},{13,1},{2,14},{6,10},... | collective-permute-start | bytes 393224 | tf_op jit(solution)/shard_map/ppermute | solution.py:41
  52.3 5.9 %collective-permute-start.7 = (bf16[64,1024]{1,0:T(8,128)(2,1)S(1)}, bf16[64,1024]{1,0:T(8,128)(2,1)S(1)}, u32[]{:S(2)}, u32[]{:S(2)}) collective-permute-start(bf16[64,1024]{1,0:T(8,128)(2,1)S(1)} %get-tuple-element.158.refs_0_.n_ref), channel_id=1, source_target_pairs={{0,8},{4,12},{8,0},{12,4},{1,9},{5,13},{9,1},{13,5},{2,10},{6,14},... | collective-permute-start | bytes 393224 | tf_op jit(solution)/shard_map/ppermute | solution.py:41
  58.2 23.4 %collective-permute-start.11 = (bf16[4,64,1024]{2,1,0:T(8,128)(2,1)S(1)}, bf16[4,64,1024]{2,1,0:T(8,128)(2,1)S(1)}, u32[]{:S(2)}, u32[]{:S(2)}) collective-permute-start(bf16[4,64,1024]{2,1,0:T(8,128)(2,1)S(1)} %together.3.x_ref.a0), channel_id=1, source_target_pairs={{0,2},{1,3},{2,0},{3,1},{4,6},{5,7},{6,4},{7,5},{8,10},{9,11},{10,... | collective-permute-start | bytes 1572872 | tf_op jit(solution)/shard_map/ppermute | solution.py:41
  60.6 13.2 %collective-permute-start.9 = (bf16[4,64,1024]{2,1,0:T(8,128)(2,1)S(1)}, bf16[4,64,1024]{2,1,0:T(8,128)(2,1)S(1)}, u32[]{:S(2)}, u32[]{:S(2)}) collective-permute-start(bf16[4,64,1024]{2,1,0:T(8,128)(2,1)S(1)} %together.3.x_ref.a0), channel_id=1, source_target_pairs={{0,1},{1,0},{2,3},{3,2},{4,5},{5,4},{6,7},{7,6},{8,9},{9,8},{10,11... | collective-permute-start | bytes 1572872 | tf_op jit(solution)/shard_map/ppermute | solution.py:41
  68.7 5.1 %collective-permute-start.15 = (f32[1,128]{1,0:T(1,128)S(1)}, f32[1,128]{1,0:T(1,128)S(1)}, u32[]{:S(2)}, u32[]{:S(2)}) collective-permute-start(f32[1,128]{1,0:T(1,128)S(1)} %counts.1), channel_id=1, source_target_pairs={{0,16},{16,0},{1,17},{17,1},{2,18},{18,2},{3,19},{19,3},{4,20},{20... | collective-permute-start | bytes 1544 | tf_op jit(solution)/shard_map/ppermute | solution.py:41
  73.3 16.4 %collective-permute-start.13 = (bf16[4,64,1024]{2,1,0:T(8,128)(2,1)S(1)}, bf16[4,64,1024]{2,1,0:T(8,128)(2,1)S(1)}, u32[]{:S(2)}, u32[]{:S(2)}) collective-permute-start(bf16[4,64,1024]{2,1,0:T(8,128)(2,1)S(1)} %together.3.x_ref.a0), channel_id=1, source_target_pairs={{0,3},{1,2},{2,1},{3,0},{4,7},{5,6},{6,5},{7,4},{8,11},{9,10},{10,... | collective-permute-start | bytes 1572872 | tf_op jit(solution)/shard_map/ppermute | solution.py:41
  80.1 31.3 %collective-permute-start.16 = (bf16[4,64,1152]{2,1,0:T(8,128)(2,1)}, bf16[4,64,1152]{2,1,0:T(8,128)(2,1)}, u32[]{:S(2)}, u32[]{:S(2)}) collective-permute-start(bf16[4,64,1152]{2,1,0:T(8,128)(2,1)} %get-tuple-element.178), channel_id=1, source_target_pairs={{0,1},{1,0},{2,3},{3,2},{4,5},{5,4},{6,7},{7,6},{8,9},{9,8},{10,11... | collective-permute-start | bytes 1769480 | tf_op jit(solution)/shard_map/ppermute | solution.py:41
  88.2 23.2 %collective-permute-start.17 = (bf16[4,64,1152]{2,1,0:T(8,128)(2,1)}, bf16[4,64,1152]{2,1,0:T(8,128)(2,1)}, u32[]{:S(2)}, u32[]{:S(2)}) collective-permute-start(bf16[4,64,1152]{2,1,0:T(8,128)(2,1)} %get-tuple-element.187), channel_id=1, source_target_pairs={{0,2},{1,3},{2,0},{3,1},{4,6},{5,7},{6,4},{7,5},{8,10},{9,11},{10,... | collective-permute-start | bytes 1769480 | tf_op jit(solution)/shard_map/ppermute | solution.py:41
  95.9 15.3 %collective-permute-start.18 = (bf16[64,1152]{1,0:T(8,128)(2,1)}, bf16[64,1152]{1,0:T(8,128)(2,1)}, u32[]{:S(2)}, u32[]{:S(2)}) collective-permute-start(bf16[64,1152]{1,0:T(8,128)(2,1)} %get-tuple-element.204), channel_id=1, source_target_pairs={{0,4},{4,0},{8,12},{12,8},{1,5},{5,1},{9,13},{13,9},{2,6},{6,2},{1... | collective-permute-start | bytes 442376 | tf_op jit(solution)/shard_map/ppermute | solution.py:41
  96.0 15.4 %collective-permute-start.19 = (bf16[64,1152]{1,0:T(8,128)(2,1)}, bf16[64,1152]{1,0:T(8,128)(2,1)}, u32[]{:S(2)}, u32[]{:S(2)}) collective-permute-start(bf16[64,1152]{1,0:T(8,128)(2,1)} %get-tuple-element.205), channel_id=1, source_target_pairs={{0,8},{4,12},{8,0},{12,4},{1,9},{5,13},{9,1},{13,5},{2,10},{6,14},... | collective-permute-start | bytes 442376 | tf_op jit(solution)/shard_map/ppermute | solution.py:41
  100.0 11.4 %collective-permute-start.20 = (bf16[64,1152]{1,0:T(8,128)(2,1)}, bf16[64,1152]{1,0:T(8,128)(2,1)}, u32[]{:S(2)}, u32[]{:S(2)}) collective-permute-start(bf16[64,1152]{1,0:T(8,128)(2,1)} %get-tuple-element.206), channel_id=1, source_target_pairs={{0,12},{4,8},{8,4},{12,0},{1,13},{5,9},{9,5},{13,1},{2,14},{6,10},... | collective-permute-start | bytes 442376 | tf_op jit(solution)/shard_map/ppermute | solution.py:41
  111.4 48.6 %collective-permute-start.21 = (bf16[8,3072,128]{2,1,0:T(8,128)(2,1)}, bf16[8,3072,128]{2,1,0:T(8,128)(2,1)}, u32[]{:S(2)}, u32[]{:S(2)}) collective-permute-start(bf16[8,3072,128]{2,1,0:T(8,128)(2,1)} %expert_grads.1.mine_ref), channel_id=1, source_target_pairs={{0,16},{16,0},{1,17},{17,1},{2,18},{18,2},{3,19},{19,3},{4,20},{20... | collective-permute-start | bytes 18874376 | tf_op jit(solution)/shard_map/ppermute | solution.py:41
  115.7 86.2 %reduce-scatter.5.cloned.1.call-start = ((), (), s32[]{:S(2)}) async-start(), calls=%async_computation.2 | async-start | bytes 655360 | tf_op jit(solution)/shard_map/reduce_scatter | solution.py:804
  116.0 9.8 %collective-permute-start.23 = (bf16[64,1152]{1,0:T(8,128)(2,1)S(1)}, bf16[64,1152]{1,0:T(8,128)(2,1)S(1)}, u32[]{:S(2)}, u32[]{:S(2)}) collective-permute-start(bf16[64,1152]{1,0:T(8,128)(2,1)S(1)} %copy-done.32), channel_id=1, source_target_pairs={{0,4},{4,0},{8,12},{12,8},{1,5},{5,1},{9,13},{13,9},{2,6},{6,2},{1... | collective-permute-start | bytes 442376 | tf_op jit(solution)/shard_map/ppermute | solution.py:41
  118.4 13.9 %collective-permute-start.24 = (bf16[64,1152]{1,0:T(8,128)(2,1)S(1)}, bf16[64,1152]{1,0:T(8,128)(2,1)S(1)}, u32[]{:S(2)}, u32[]{:S(2)}) collective-permute-start(bf16[64,1152]{1,0:T(8,128)(2,1)S(1)} %get-tuple-element.228), channel_id=1, source_target_pairs={{0,8},{4,12},{8,0},{12,4},{1,9},{5,13},{9,1},{13,5},{2,10},{6,14},... | collective-permute-start | bytes 442376 | tf_op jit(solution)/shard_map/ppermute | solution.py:41
  120.0 12.3 %collective-permute-start.25 = (bf16[64,1152]{1,0:T(8,128)(2,1)S(1)}, bf16[64,1152]{1,0:T(8,128)(2,1)S(1)}, u32[]{:S(2)}, u32[]{:S(2)}) collective-permute-start(bf16[64,1152]{1,0:T(8,128)(2,1)S(1)} %get-tuple-element.229), channel_id=1, source_target_pairs={{0,12},{4,8},{8,4},{12,0},{1,13},{5,9},{9,5},{13,1},{2,14},{6,10},... | collective-permute-start | bytes 442376 | tf_op jit(solution)/shard_map/ppermute | solution.py:41
  122.7 10.3 %collective-permute-start.22 = (bf16[64,1152]{1,0:T(8,128)(2,1)S(1)}, bf16[64,1152]{1,0:T(8,128)(2,1)S(1)}, u32[]{:S(2)}, u32[]{:S(2)}) collective-permute-start(bf16[64,1152]{1,0:T(8,128)(2,1)S(1)} %through.1), channel_id=1, source_target_pairs={{0,3},{1,2},{2,1},{3,0},{4,7},{5,6},{6,5},{7,4},{8,11},{9,10},{10,... | collective-permute-start | bytes 442376 | tf_op jit(solution)/shard_map/ppermute | solution.py:41
  134.4 9.2 %collective-permute-start.28 = (bf16[64,1152]{1,0:T(8,128)(2,1)S(1)}, bf16[64,1152]{1,0:T(8,128)(2,1)S(1)}, u32[]{:S(2)}, u32[]{:S(2)}) collective-permute-start(bf16[64,1152]{1,0:T(8,128)(2,1)S(1)} %get-tuple-element.232.w0), channel_id=1, source_target_pairs={{0,3},{1,2},{2,1},{3,0},{4,7},{5,6},{6,5},{7,4},{8,11},{9,10},{10,... | collective-permute-start | bytes 442376 | tf_op jit(solution)/shard_map/ppermute | solution.py:41
  135.1 10.0 %collective-permute-start.27 = (bf16[64,1152]{1,0:T(8,128)(2,1)S(1)}, bf16[64,1152]{1,0:T(8,128)(2,1)S(1)}, u32[]{:S(2)}, u32[]{:S(2)}) collective-permute-start(bf16[64,1152]{1,0:T(8,128)(2,1)S(1)} %get-tuple-element.232.w0), channel_id=1, source_target_pairs={{0,2},{1,3},{2,0},{3,1},{4,6},{5,7},{6,4},{7,5},{8,10},{9,11},{10,... | collective-permute-start | bytes 442376 | tf_op jit(solution)/shard_map/ppermute | solution.py:41
  136.3 8.9 %collective-permute-start.26 = (bf16[64,1152]{1,0:T(8,128)(2,1)S(1)}, bf16[64,1152]{1,0:T(8,128)(2,1)S(1)}, u32[]{:S(2)}, u32[]{:S(2)}) collective-permute-start(bf16[64,1152]{1,0:T(8,128)(2,1)S(1)} %get-tuple-element.232.w0), channel_id=1, source_target_pairs={{0,1},{1,0},{2,3},{3,2},{4,5},{5,4},{6,7},{7,6},{8,9},{9,8},{10,11... | collective-permute-start | bytes 442376 | tf_op jit(solution)/shard_map/ppermute | solution.py:41
  169.5 3.6 %collective-permute-start.36 = (bf16[512,896]{1,0:T(8,128)(2,1)}, bf16[512,896]{1,0:T(8,128)(2,1)S(1)}, u32[]{:S(2)}, u32[]{:S(2)}) collective-permute-start(bf16[512,896]{1,0:T(8,128)(2,1)} %get-tuple-element.254), channel_id=1, source_target_pairs={{0,16},{16,0},{1,17},{17,1},{2,18},{18,2},{3,19},{19,3},{4,20},{20... | collective-permute-start | bytes 2752520 | tf_op jit(solution)/shard_map/ppermute | solution.py:41
  169.6 6.6 %collective-permute-start.37 = (bf16[64,1024]{1,0:T(8,128)(2,1)}, bf16[64,1024]{1,0:T(8,128)(2,1)S(1)}, u32[]{:S(2)}, u32[]{:S(2)}) collective-permute-start(bf16[64,1024]{1,0:T(8,128)(2,1)} %get-tuple-element.260), channel_id=1, source_target_pairs={{0,1},{1,0},{2,3},{3,2},{4,5},{5,4},{6,7},{7,6},{8,9},{9,8},{10,11... | collective-permute-start | bytes 393224 | tf_op jit(solution)/shard_map/ppermute | solution.py:41
  171.1 8.6 %collective-permute-start.38 = (bf16[64,1024]{1,0:T(8,128)(2,1)}, bf16[64,1024]{1,0:T(8,128)(2,1)S(1)}, u32[]{:S(2)}, u32[]{:S(2)}) collective-permute-start(bf16[64,1024]{1,0:T(8,128)(2,1)} %get-tuple-element.261), channel_id=1, source_target_pairs={{0,2},{1,3},{2,0},{3,1},{4,6},{5,7},{6,4},{7,5},{8,10},{9,11},{10,... | collective-permute-start | bytes 393224 | tf_op jit(solution)/shard_map/ppermute | solution.py:41
  171.7 8.0 %collective-permute-start.39 = (bf16[64,1024]{1,0:T(8,128)(2,1)}, bf16[64,1024]{1,0:T(8,128)(2,1)S(1)}, u32[]{:S(2)}, u32[]{:S(2)}) collective-permute-start(bf16[64,1024]{1,0:T(8,128)(2,1)} %get-tuple-element.262), channel_id=1, source_target_pairs={{0,3},{1,2},{2,1},{3,0},{4,7},{5,6},{6,5},{7,4},{8,11},{9,10},{10,... | collective-permute-start | bytes 393224 | tf_op jit(solution)/shard_map/ppermute | solution.py:41
  179.7 25.5 %collective-permute-start.43 = (bf16[128,896]{1,0:T(8,128)(2,1)S(1)}, bf16[128,896]{1,0:T(8,128)(2,1)S(1)}, u32[]{:S(2)}, u32[]{:S(2)}) collective-permute-start(bf16[128,896]{1,0:T(8,128)(2,1)S(1)} %get-tuple-element.272), channel_id=1, source_target_pairs={{0,4},{4,0},{8,12},{12,8},{1,5},{5,1},{9,13},{13,9},{2,6},{6,2},{1... | collective-permute-start | bytes 688136 | tf_op jit(solution)/shard_map/ppermute | solution.py:41
  181.4 18.3 %collective-permute-start.42 = (bf16[64,1024]{1,0:T(8,128)(2,1)S(1)}, bf16[64,1024]{1,0:T(8,128)(2,1)S(1)}, u32[]{:S(2)}, u32[]{:S(2)}) collective-permute-start(bf16[64,1024]{1,0:T(8,128)(2,1)S(1)} %input_grad.1.refs_0_), channel_id=1, source_target_pairs={{0,3},{1,2},{2,1},{3,0},{4,7},{5,6},{6,5},{7,4},{8,11},{9,10},{10,... | collective-permute-start | bytes 393224 | tf_op jit(solution)/shard_map/ppermute | solution.py:41
  182.9 1.2 collective-permute-start.29
  184.1 9.9 %collective-permute-start.32 = (f32[8,1024]{1,0:T(8,128)S(1)}, f32[8,1024]{1,0:T(8,128)S(1)}, u32[]{:S(2)}, u32[]{:S(2)}) collective-permute-start(f32[8,1024]{1,0:T(8,128)S(1)} %add.18.refs_0_), channel_id=1, source_target_pairs={{0,12},{4,8},{8,4},{12,0},{1,13},{5,9},{9,5},{13,1},{2,14},{6,10},... | collective-permute-start | bytes 98312 | tf_op jit(solution)/shard_map/ppermute | solution.py:41
  186.5 9.0 %collective-permute-start.31 = (f32[8,1024]{1,0:T(8,128)S(1)}, f32[8,1024]{1,0:T(8,128)S(1)}, u32[]{:S(2)}, u32[]{:S(2)}) collective-permute-start(f32[8,1024]{1,0:T(8,128)S(1)} %add.18.refs_0_), channel_id=1, source_target_pairs={{0,8},{4,12},{8,0},{12,4},{1,9},{5,13},{9,1},{13,5},{2,10},{6,14},... | collective-permute-start | bytes 98312 | tf_op jit(solution)/shard_map/ppermute | solution.py:41
  186.6 16.2 %collective-permute-start.41 = (bf16[64,1024]{1,0:T(8,128)(2,1)S(1)}, bf16[64,1024]{1,0:T(8,128)(2,1)S(1)}, u32[]{:S(2)}, u32[]{:S(2)}) collective-permute-start(bf16[64,1024]{1,0:T(8,128)(2,1)S(1)} %input_grad.1.refs_0_), channel_id=1, source_target_pairs={{0,2},{1,3},{2,0},{3,1},{4,6},{5,7},{6,4},{7,5},{8,10},{9,11},{10,... | collective-permute-start | bytes 393224 | tf_op jit(solution)/shard_map/ppermute | solution.py:41
  194.1 10.6 %collective-permute-start.40 = (bf16[64,1024]{1,0:T(8,128)(2,1)S(1)}, bf16[64,1024]{1,0:T(8,128)(2,1)S(1)}, u32[]{:S(2)}, u32[]{:S(2)}) collective-permute-start(bf16[64,1024]{1,0:T(8,128)(2,1)S(1)} %input_grad.1.refs_0_), channel_id=1, source_target_pairs={{0,1},{1,0},{2,3},{3,2},{4,5},{5,4},{6,7},{7,6},{8,9},{9,8},{10,11... | collective-permute-start | bytes 393224 | tf_op jit(solution)/shard_map/ppermute | solution.py:41
  195.5 3.9 %collective-permute-start.30 = (f32[8,1024]{1,0:T(8,128)S(1)}, f32[8,1024]{1,0:T(8,128)S(1)}, u32[]{:S(2)}, u32[]{:S(2)}) collective-permute-start(f32[8,1024]{1,0:T(8,128)S(1)} %add.18.refs_0_), channel_id=1, source_target_pairs={{0,4},{4,0},{8,12},{12,8},{1,5},{5,1},{9,13},{13,9},{2,6},{6,2},{1... | collective-permute-start | bytes 98312 | tf_op jit(solution)/shard_map/ppermute | solution.py:41
  199.4 19.1 %collective-permute-start.44 = (bf16[128,896]{1,0:T(8,128)(2,1)S(1)}, bf16[128,896]{1,0:T(8,128)(2,1)S(1)}, u32[]{:S(2)}, u32[]{:S(2)}) collective-permute-start(bf16[128,896]{1,0:T(8,128)(2,1)S(1)} %get-tuple-element.273), channel_id=1, source_target_pairs={{0,8},{4,12},{8,0},{12,4},{1,9},{5,13},{9,1},{13,5},{2,10},{6,14},... | collective-permute-start | bytes 688136 | tf_op jit(solution)/shard_map/ppermute | solution.py:41
  199.7 18.9 %collective-permute-start.45 = (bf16[128,896]{1,0:T(8,128)(2,1)S(1)}, bf16[128,896]{1,0:T(8,128)(2,1)S(1)}, u32[]{:S(2)}, u32[]{:S(2)}) collective-permute-start(bf16[128,896]{1,0:T(8,128)(2,1)S(1)} %get-tuple-element.274), channel_id=1, source_target_pairs={{0,12},{4,8},{8,4},{12,0},{1,13},{5,9},{9,5},{13,1},{2,14},{6,10},... | collective-permute-start | bytes 688136 | tf_op jit(solution)/shard_map/ppermute | solution.py:41
  202.8 17.2 %collective-permute-start.35 = (bf16[80,1024]{1,0:T(8,128)(2,1)S(1)}, bf16[80,1024]{1,0:T(8,128)(2,1)S(1)}, u32[]{:S(2)}, u32[]{:S(2)}) collective-permute-start(bf16[80,1024]{1,0:T(8,128)(2,1)S(1)} %out_piece.1.refs_0_), channel_id=1, source_target_pairs={{0,3},{1,2},{2,1},{3,0},{4,7},{5,6},{6,5},{7,4},{8,11},{9,10},{10,... | collective-permute-start | bytes 491528 | tf_op jit(solution)/shard_map/ppermute | solution.py:41
  204.7 15.4 %collective-permute-start.34 = (bf16[80,1024]{1,0:T(8,128)(2,1)S(1)}, bf16[80,1024]{1,0:T(8,128)(2,1)S(1)}, u32[]{:S(2)}, u32[]{:S(2)}) collective-permute-start(bf16[80,1024]{1,0:T(8,128)(2,1)S(1)} %out_piece.1.refs_0_), channel_id=1, source_target_pairs={{0,2},{1,3},{2,0},{3,1},{4,6},{5,7},{6,4},{7,5},{8,10},{9,11},{10,... | collective-permute-start | bytes 491528 | tf_op jit(solution)/shard_map/ppermute | solution.py:41
  205.3 14.8 %collective-permute-start.33 = (bf16[80,1024]{1,0:T(8,128)(2,1)S(1)}, bf16[80,1024]{1,0:T(8,128)(2,1)S(1)}, u32[]{:S(2)}, u32[]{:S(2)}) collective-permute-start(bf16[80,1024]{1,0:T(8,128)(2,1)S(1)} %out_piece.1.refs_0_), channel_id=1, source_target_pairs={{0,1},{1,0},{2,3},{3,2},{4,5},{5,4},{6,7},{7,6},{8,9},{9,8},{10,11... | collective-permute-start | bytes 491528 | tf_op jit(solution)/shard_map/ppermute | solution.py:41
  (44 other events, 450.0 us)
Sparse Core Ops, SparseCore 0:
  115.8 44.0 reduce-scatter.6
  169.7 24.5 reduce-scatter.4

commit v5 on v4

--- a/solution.py
+++ b/solution.py
@@ -360,7 +360,7 @@
             shape((total, 2 * inner), BF),
             shape((total, inner), BF),
             *d_shapes,
-            shape(dims(width), BF),
+            shape(dims(width), kind),
         ],
         compiler_params=pltpu.CompilerParams(vmem_limit_bytes=30 * MIB),
         cost_estimate=pl.CostEstimate(flops=int(100.0*(total * width * inner // 8)), bytes_accessed=0, transcendentals=0),
@@ -371,22 +371,6 @@
     return cot, dgu, hid, d if apart else d[0], m.reshape(count, rows, width)
 
 
-def ordered_rows_kernel(me_ref, *refs):
-    pieces, out = refs[:-1], refs[-1]
-    for r, piece in enumerate(pieces):
-        for i in range(piece.shape[0]):
-            out[me_ref[1] ^ r, me_ref[0] ^ i] = piece[i]
-
-
-def ordered_rows(me, pieces):
-    count, *dims = pieces[0].shape
-    if count <= FEW:
-        out = [shape((len(pieces), count, *dims), pieces[0].dtype)]
-        return call(ordered_rows_kernel, out, (me, *pieces), "ordered_rows", "s")[0]
-    rows = jnp.take(jnp.stack(pieces), jnp.arange(len(pieces)) ^ me[1], axis=0)
-    return jnp.take(rows, jnp.arange(count) ^ me[0], axis=1)
-
-
 def split_sum_kernel(count, near, *refs):
     ins, outs = refs[:count], refs[count:]
     for s in range(ins[0].shape[0]):
@@ -400,6 +384,15 @@
     count, *dims = arrays[0].shape
     outs = [shape(dims, F32)] + [shape(dims, BF)] * (count - 1)
     return call(functools.partial(split_sum_kernel, len(arrays), True), outs, arrays, name)
+
+
+def moe_sum_kernel(me_ref, *refs):
+    pieces, out = refs[:-1], refs[-1]
+    for s in range(out.shape[0]):
+        total = pieces[0][s].astype(F32)
+        for x in pieces[1:]:
+            total = total + x[s].astype(F32)
+        out[me_ref[0] ^ s] = total.astype(out.dtype)
 
 
 def add_kernel(*refs):
@@ -597,9 +590,13 @@
     ig_ref[...] = ig.astype(BF)
 
 
-def out_kernel(h_ref, moe_ref, small_ref, out_ref):
+def out_kernel(h_ref, small_ref, *refs):
+    moes, out_ref = refs[:-1], refs[-1]
     rows = h_ref.shape[0]
-    out_ref[:rows, :] = (h_ref[...] + moe_ref[...].astype(F32)).astype(BF)
+    out = h_ref[...]
+    for moe in moes:
+        out = out + moe[...].astype(F32)
+    out_ref[:rows, :] = out.astype(BF)
     small = small_ref[...]
     high = small.astype(BF).astype(F32)
     out_ref[rows:, :] = jnp.concatenate([high, small - high], axis=0).astype(BF)
@@ -627,37 +624,33 @@
     small_ref[...] = total
 
 
-def ordered_sum_kernel(me_ref, *refs):
-    pieces, out, held = refs[:-2], refs[-2], refs[-1]
-    for r, piece in enumerate(pieces):
-        held[me_ref[0] ^ r] = piece[...]
-    total = held[0]
-    for i in range(1, len(pieces)):
-        total = total + held[i]
-    out[...] = total
-
-
-def ordered_sum(me, pieces):
-    return call(
-        ordered_sum_kernel,
-        [shape(pieces[0].shape, F32)],
-        (me, *pieces),
-        "ordered_sum",
-        "s",
-        scratch=[pltpu.VMEM((len(pieces), *pieces[0].shape), F32)],
-    )[0]
-
-
-def kept_and_dealt_kernel(me_ref, kept_ref, got_ref, *outs):
-    rows = outs[0].shape[0]
+def kept_and_dealt_kernel(me_ref, kept_ref, got_ref, small_ref, small_got_ref, *outs):
+    small_out, outs = outs[-1], outs[:-1]
+    small = small_ref[...] + small_got_ref[...]
+    high = small[:4].astype(BF).astype(F32)
+    both = jnp.concatenate([high, small[:4] - high], axis=0).astype(BF).astype(F32)
+    small_out[...] = both
+    rows, columns = outs[0].shape
+    upper = lane_of((8, LANES)) >= HD
+    parts = []
+    for at in range(0, both.shape[1], LANES):
+        tile = both[:, at : at + LANES]
+        parts += [jnp.where(upper, pltpu.roll(tile, HD, 1), 0.0), jnp.where(upper, tile, 0.0)]
+    if len(parts) * 8 == rows:
+        extra = jnp.concatenate(parts, axis=0)
+    else:
+        extra = jnp.zeros((rows, LANES), F32)
     for r, out in enumerate(outs):
         start = pl.multiple_of((me_ref[0] ^ r) * rows, rows)
         at = pl.ds(start, rows)
-        out[...] = (kept_ref[at, :] + got_ref[at, :].astype(F32)).astype(out.dtype)
-
-
-def dense_sum_kernel(mine_ref, *refs):
-    others, (q_ref, k_ref, v_ref, o_ref, r_ref) = refs[:-5], refs[-5:]
+        total = kept_ref[at, :] + got_ref[at, :].astype(F32)
+        out[:, : columns - LANES] = total[:, : columns - LANES].astype(out.dtype)
+        out[:, columns - LANES :] = (total[:, columns - LANES :] + extra).astype(out.dtype)
+
+
+def dense_sum_kernel(me_ref, small_ref, mine_ref, *refs):
+    others, outs, held = refs[:-7], refs[-7:-1], refs[-1]
+    q_ref, k_ref, v_ref, o_ref, r_ref, small_out = outs
     total = mine_ref[...]
     for other in others:
         total = total + other[...].astype(F32)
@@ -668,6 +661,19 @@
     o_ref[...] = total[:, at : at + o_ref.shape[0]].T
     at += o_ref.shape[0]
     r_ref[...] = total[:, at : at + r_ref.shape[1]]
+    held[me_ref[0]] = small_ref[...]
+    if total.shape[0] * HD != 8 * small_ref.shape[1]:
+        others = []
+    lower = lane_of((8, LANES)) < HD
+    for i, other in enumerate(others):
+        for j in range(small_ref.shape[1] // LANES):
+            first = other[16 * j : 16 * j + 16, at : at + LANES].astype(F32)
+            tile = jnp.where(lower, pltpu.roll(first[:8], HD, 1), first[8:])
+            held[me_ref[0] ^ (i + 1), :, j * LANES : (j + 1) * LANES] = tile
+    small = held[0] if others else small_ref[...]
+    for i in range(1, len(others) + 1):
+        small = small + held[i]
+    small_out[...] = jnp.concatenate([small[:4] + small[4:], jnp.zeros_like(small[:4])], axis=0)
 
 
 def on_device(
@@ -701,7 +707,6 @@
     e_at = e_me.astype(jnp.int32).reshape(1)
     base = (e_me * local).astype(jnp.int32).reshape(1)
     d_at = jnp.stack([d_me, t_me]).astype(jnp.int32)
-    me = jnp.stack([e_me, t_me]).astype(jnp.int32)
     cosine, sine = rope_tables(seq_len)
     gain_one, gain_two = gain_first[None], gain_second[None]
     down_flat = w_down.reshape(local * hidden, width)
@@ -737,7 +742,7 @@
         "s" + "b" * 8,
         "bbbbbbv",
         scratch=[pltpu.VMEM((seq_len, width), F32)],
-        limit=30,
+        limit=58,
         flops=2 * seq_len * width * 4 * heads,
     )
     parts = rest
@@ -785,10 +790,14 @@
     grads = run_grads(twos, dgus, hids, cots, local, hidden)
     grads, (got, from_last) = tied(grads, (got, from_last))
     near, *across = split_sum([ds[0], *got], "dn_sum")
-    across, moes = tied(across, moes)
-    moe = lax.psum_scatter(ordered_rows(me, moes), "tensor", scatter_dimension=0, tiled=False)
     through = added([near_last, *from_last], BF, "through")
-    near_sums = [near, swap(through, "tensor", last), *deal(across, "expert")]
+    across[0], middle = tied(across[0], moes[1:last])
+    across = deal(across, "expert")
+    near_sums = [near, swap(through, "tensor", last), *across]
+    moe_got = [swap(middle[r - 1], "tensor", r) for r in range(1, last)]
+    moe_got, near_sums = tied(moe_got, near_sums)
+    near_sums[2], moe_last = tied(near_sums[2], moes[last])
+    moe_got.append(swap(moe_last, "tensor", last))
 
     wide, dh, small = call(
         functools.partial(norm_back_kernel, experts, len(near_sums)),
@@ -799,8 +808,16 @@
         "vvv",
     )
     wides = [wide] + [swap(wide, "tensor", r) for r in around]
-    grads_got = swap(grads, "dp", 1)
-    (moe, grads_got), wides = tied((moe, grads_got), wides)
+    _, late_grads = tied(wide, grads)
+    grads_got = swap(late_grads, "dp", 1)
+    grads_got, wides = tied(grads_got, wides)
+    moe = call(
+        moe_sum_kernel,
+        [shape((expert_size, rows, width), BF)],
+        (e_at, moes[0], *moe_got),
+        "moe_sum",
+        "s",
+    )[0]
     moe = lax.psum_scatter(moe, "expert", scatter_dimension=0, tiled=False)
 
     wide_all, dqkv, small, *back_parts = call(
@@ -844,36 +861,22 @@
         ],
         flops=1,
     )
-    mine, *others = call(
+    mine, *others, small = call(
         kept_and_dealt_kernel,
-        [shape((chunk, all_columns), F32)] + [shape((chunk, all_columns), BF)] * (expert_size - 1),
-        (e_at, kept, swap(sent, "dp", 1)),
+        [shape((chunk, all_columns), F32)]
+        + [shape((chunk, all_columns), BF)] * (expert_size - 1)
+        + [shape((8, width), F32)],
+        (e_at, kept, swap(sent, "dp", 1), small, swap(small, "dp", 1)),
         "dense_dealt",
         "s",
     )
-    (mine, others), part_sums = tied((mine, others), part_sums)
+    others = deal(others, "expert")
+    others[0], part_sums = tied(others[0], part_sums)
     ig = call(
         input_grad_kernel, [shape((rows, width), BF)], (xq, gain_one, dh, *part_sums), "input_grad", "vb"
     )[0]
     igs = [ig] + [swap(ig, "tensor", r) for r in around]
-    expert_grads = both_copies(grads, grads_got)
-    expert_grads, igs = tied(expert_grads, igs)
-    input_grad = call(
-        natural_kernel, [shape((seq_len, width), F32)], (t_at, *igs), "input_grad_whole", "s", "b"
-    )[0]
-    small = small + swap(small, "dp", 1)
-    small = ordered_sum(e_at, [small, *spread(small, "expert")])
-    out_piece = call(out_kernel, [shape((rows + 16, width), BF)], (h, moe, small), "out_piece")[0]
-    output, small = call(
-        out_whole_kernel,
-        [shape((seq_len, width), BF), shape((8, width), F32)],
-        (t_at, out_piece, *[swap(out_piece, "tensor", r) for r in around]),
-        "output",
-        "s",
-        "bv",
-        scratch=[pltpu.VMEM((tensor_size, 8, width), F32)],
-    )
-    g_query, g_key, g_value, g_out, g_router = call(
+    g_query, g_key, g_value, g_out, g_router, small = call(
         dense_sum_kernel,
         [
             shape((chunk, heads), F32),
@@ -881,13 +884,33 @@
             shape((chunk, keys_wide), F32),
             shape((heads, chunk), F32),
             shape((chunk, LANES), F32),
+            shape((8, width), F32),
         ],
-        (mine, *deal(others, "expert")),
+        (e_at, small, mine, *others),
         "dense_sum",
-        "",
-        "bbbbb",
-    )
-
+        "s",
+        "bbbbbv",
+        scratch=[pltpu.VMEM((expert_size, 8, width), F32)],
+    )
+    if chunk * HD != 8 * width:
+        small = jnp.sum(lax.all_gather(small, "expert"), axis=0)
+    igs, small = tied(igs, small)
+    input_grad = call(
+        natural_kernel, [shape((seq_len, width), F32)], (t_at, *igs), "input_grad_whole", "s", "b"
+    )[0]
+    out_piece = call(out_kernel, [shape((rows + 16, width), BF)], (h, small, moe), "out_piece")[0]
+    outs = [out_piece] + [swap(out_piece, "tensor", r) for r in around]
+    expert_grads = both_copies(grads, grads_got)
+    expert_grads, outs = tied(expert_grads, outs)
+    output, small = call(
+        out_whole_kernel,
+        [shape((seq_len, width), BF), shape((8, width), F32)],
+        (t_at, *outs),
+        "output",
+        "s",
+        "bv",
+        scratch=[pltpu.VMEM((tensor_size, 8, width), F32)],
+    )
     at = (d_me * expert_size + e_me) * chunk
     loss_value = (experts * balance * small[2:3, :LANES])[0, :experts]
     return (

time: 230 us -> 225 us (0.978)
  waiting for transfers between devices: 64.6 us -> 47.3 us
  starting transfers between devices: 58.5 us -> 75.4 us
  local copies, waits for them, and re-layouts: 18.1 us -> 10.1 us
  Pallas kernels: 72 us -> 74.8 us
    ppermute x46, starting transfers between devices: 58.1 us -> 75.3 us  [swap(): return lax.ppermute(x, axis, [(i, i ^ distance) for i in range(size)])]
    unnamed x3 -> x1, waiting for transfers between devices: 14.9 us -> 0.02 us
    unnamed x89 -> x73, local copies, waits for them, and re-layouts: 17.6 us -> 9.62 us
    pallas_call x19 -> x18, Pallas kernels: 25 us -> 28.6 us  [call(): pl.pallas_call(kernel, grid=(1,), out_shape=outs, in_specs=[spec(p, x) fo...]
    ppermute x46, waiting for transfers between devices: 49.8 us -> 47.3 us  [swap(): return lax.ppermute(x, axis, [(i, i ^ distance) for i in range(size)])]
  transfers between devices with their start and end apart: 48 -> 47, of which waited for: 18 -> 19; matrix products, arithmetic and copies ran while one was open for 1% -> 1% of each run, Pallas kernels for 26% -> 31%
where the time goes in v5:
time: 225 us; the launch traced here: 223 us
  starting transfers between devices  75.4 us (34%)
  Pallas kernels  74.8 us (33%)
  waiting for transfers between devices  47.3 us (21%)
  between operations  14.5 us (6%)
  local copies, waits for them, and re-layouts  10.1 us (4%)
    ppermute x46, starting transfers between devices, swap(): return lax.ppermute(x, axis, [(i, i ^ distance) for i in range(size)])  75.3 us
    ppermute x46, waiting for transfers between devices, swap(): return lax.ppermute(x, axis, [(i, i ^ distance) for i in range(size)])  47.3 us
    pallas_call x18, Pallas kernels, call(): pl.pallas_call(kernel, grid=(1,), out_shape=outs, in_specs=[spec(p, x) fo...  28.6 us
    pallas_call x4, Pallas kernels, run_experts(): pl.pallas_call(kernel, grid=(total // step,), in_specs=[pl.BlockSpec(memo...  22.6 us
    pallas_call x1, Pallas kernels, both_copies(): pl.pallas_call(both_copies_kernel, grid=(local,), in_specs=[block(rows, h...  11.1 us
    pallas_call x1, Pallas kernels, run_grads(): pl.pallas_call(grads_kernel, grid=(local,), in_specs=whole(n) + cols(dgu,...  10.9 us
    unnamed x73, local copies, waits for them, and re-layouts  9.62 us
  transfers between devices with their start and end apart: 47, of which 19 were waited for; matrix products, arithmetic and copies ran while one was open for 1% of the time, Pallas kernels for 31%

profile of v5, /device:TPU:0, one launch (start us, length us, event | category | flops | bytes accessed | tf_op | source)
XLA Modules:
  0.0 223.2 jit_solution(5106506769847589503)
XLA Ops:
  7.2 2.2 pieces.1
  9.4 3.0 %collective-permute-start = (bf16[64,1152]{1,0:T(8,128)(2,1)}, bf16[64,1152]{1,0:T(8,128)(2,1)S(1)}, u32[]{:S(2)}, u32[]{:S(2)}) collective-permute-start(bf16[64,1152]{1,0:T(8,128)(2,1)} %get-tuple-element.157.own_ref.refs_0_.cot_ref), channel_id=1, source_target_pairs={{0,4},{4,0},{8,12},{12,8},{1,5},{5,1},{9,13},{13,9},{2,6},{6,2},{1... | collective-permute-start | bytes 442376 | tf_op jit(solution)/shard_map/ppermute | solution.py:41
  12.4 2.6 %collective-permute-start.4 = (bf16[64,1152]{1,0:T(8,128)(2,1)}, bf16[64,1152]{1,0:T(8,128)(2,1)S(1)}, u32[]{:S(2)}, u32[]{:S(2)}) collective-permute-start(bf16[64,1152]{1,0:T(8,128)(2,1)} %get-tuple-element.157.own_ref.refs_0_.cot_ref), channel_id=1, source_target_pairs={{0,8},{4,12},{8,0},{12,4},{1,9},{5,13},{9,1},{13,5},{2,10},{6,14},... | collective-permute-start | bytes 442376 | tf_op jit(solution)/shard_map/ppermute | solution.py:41
  15.0 3.5 %collective-permute-done.refs_0_ = bf16[64,1152]{1,0:T(8,128)(2,1)S(1)} collective-permute-done((bf16[64,1152]{1,0:T(8,128)(2,1)}, bf16[64,1152]{1,0:T(8,128)(2,1)S(1)}, u32[]{:S(2)}, u32[]{:S(2)}) %collective-permute-start) | collective-permute-done | bytes 147488 | tf_op jit(solution)/shard_map/ppermute | solution.py:41
  18.5 4.7 %attend.1 = (bf16[256,1024]{1,0:T(8,128)(2,1)}, bf16[256,256]{1,0:T(8,128)(2,1)}, bf16[256,128]{1,0:T(8,128)(2,1)}, bf16[256,128]{1,0:T(8,128)(2,1)}, bf16[256,2...) custom-call(s32[1]{0:T(128)} %bitcast.me_ref, ...), custom_call_target="tpu_custom_call" | custom-call | flops 53687091200 | tf_op jit(solution)/shard_map/attend/pallas_call | solution.py:118
  23.2 1.7 collective-permute-start.1
  24.9 1.5 collective-permute-start.2
  26.6 1.7 collective-permute-done.1.refs_0_
  28.3 1.7 collective-permute-done.2.refs_1_
  30.0 2.4 %collective-permute-done.3.refs_2_ = bf16[64,1024]{1,0:T(8,128)(2,1)S(1)} collective-permute-done((bf16[64,1024]{1,0:T(8,128)(2,1)}, bf16[64,1024]{1,0:T(8,128)(2,1)S(1)}, u32[]{:S(2)}, u32[]{:S(2)}) %collective-permute-start.3) | collective-permute-done | bytes 131104 | tf_op jit(solution)/shard_map/ppermute | solution.py:41
  36.1 3.5 %collective-permute-done.6.refs_1_ = bf16[64,1024]{1,0:T(8,128)(2,1)S(1)} collective-permute-done((bf16[64,1024]{1,0:T(8,128)(2,1)S(1)}, bf16[64,1024]{1,0:T(8,128)(2,1)S(1)}, u32[]{:S(2)}, u32[]{:S(2)}) %collective-permute-start.6) | collective-permute-done | bytes 131104 | tf_op jit(solution)/shard_map/ppermute | solution.py:41
  40.0 2.6 %collective-permute-start.7 = (bf16[64,1024]{1,0:T(8,128)(2,1)S(1)}, bf16[64,1024]{1,0:T(8,128)(2,1)}, u32[]{:S(2)}, u32[]{:S(2)}) collective-permute-start(bf16[64,1024]{1,0:T(8,128)(2,1)S(1)} %get-tuple-element.166.refs_0_.n_ref), channel_id=1, source_target_pairs={{0,8},{4,12},{8,0},{12,4},{1,9},{5,13},{9,1},{13,5},{2,10},{6,14},... | collective-permute-start | bytes 393224 | tf_op jit(solution)/shard_map/ppermute | solution.py:41
  42.6 1.5 collective-permute-start.8
  44.1 1.6 copy-done.1
  45.7 1.5 gate_up_weights.1.wcat
  47.2 3.0 %collective-permute-done.7.refs_2_ = bf16[64,1024]{1,0:T(8,128)(2,1)} collective-permute-done((bf16[64,1024]{1,0:T(8,128)(2,1)S(1)}, bf16[64,1024]{1,0:T(8,128)(2,1)}, u32[]{:S(2)}, u32[]{:S(2)}) %collective-permute-start.7) | collective-permute-done | bytes 131104 | tf_op jit(solution)/shard_map/ppermute | solution.py:41
  51.3 1.3 collective-permute-start.9
  52.6 1.6 collective-permute-start.10
  54.2 3.7 %collective-permute-done.14.refs_7_.far_ref = bf16[3,64,1152]{2,1,0:T(8,128)(2,1)S(1)} collective-permute-done((bf16[3,64,1152]{2,1,0:T(8,128)(2,1)S(1)}, bf16[3,64,1152]{2,1,0:T(8,128)(2,1)S(1)}, u32[]{:S(2)}, u32[]{:S(2)}) %collective-permute-start.14) | collective-permute-done | bytes 442400 | tf_op jit(solution)/shard_map/ppermute | solution.py:41
  57.9 2.2 %counts.1 = f32[1,128]{1,0:T(1,128)S(1)} custom-call(bf16[64,1152]{1,0:T(8,128)(2,1)S(1)} %copy-done.6, bf16[64,1152]{1,0:T(8,128)(2,1)S(1)} %copy-done.23, bf16[64,1152]{1,0:T(8,128)(2,1)S(1)} %copy-done.22, bf16[64,1152]{1,0:T(8,128)(2,1)S(1)} %copy-done.21, bf16[3,64,1152]{2,1,0:T(8,128)(2,1)S(1)} %together.2.far_ref.refs_4_, ...), custom_call_target="tpu_custom_call" | custom-call | tf_op jit(solution)/shard_map/counts/pallas_call | solution.py:118
  60.2 4.5 %experts.4 = (bf16[256,1024]{1,0:T(8,128)(2,1)S(1)}, bf16[256,2048]{1,0:T(8,128)(2,1)S(1)}, bf16[256,1024]{1,0:T(8,128)(2,1)S(1)}, f32[4,64,1152]{2,1,0:T(8,128)S(1)}, f32[4,64,1024]{2,1,0:T(8,128)S(1)}) custom-call(s32[1]{0:T(128)} %bitcast.9.base_ref, bf16[4,64,1024]{2,1,0:T(8,128)(2,1)S(1)} %together.3.x_ref.a0, bf16[64,1152]{1,0:T(8,128)(2,1)S(1)} %copy-done.6, ...), custom_call_target="tpu_custom_call" | custom-call | flops 3355443200 | tf_op jit(solution)/shard_map/experts/pallas_call | solution.py:349
  67.0 6.3 %experts.5 = (bf16[256,1024]{1,0:T(8,128)(2,1)S(1)}, bf16[256,2048]{1,0:T(8,128)(2,1)S(1)}, bf16[256,1024]{1,0:T(8,128)(2,1)S(1)}, bf16[4,64,1152]{2,1,0:T(8,128)(2,1)}, bf16[4,64,1024]{2,1,0:T(8,128)(2,1)S(1)}) custom-call(s32[1]{0:T(128)} %bitcast.9.base_ref, bf16[4,64,1024]{2,1,0:T(8,128)(2,1)S(1)} %collective-permute-done.9.x_ref.a1, ...), custom_call_target="tpu_custom_call" | custom-call | flops 3355443200 | tf_op jit(solution)/shard_map/experts/pallas_call | solution.py:349
  73.3 1.4 collective-permute-start.16
  74.7 6.5 %experts.6 = (bf16[256,1024]{1,0:T(8,128)(2,1)S(1)}, bf16[256,2048]{1,0:T(8,128)(2,1)S(1)}, bf16[256,1024]{1,0:T(8,128)(2,1)S(1)}, bf16[4,64,1152]{2,1,0:T(8,128)(2,1)}, bf16[4,64,1024]{2,1,0:T(8,128)(2,1)S(1)}) custom-call(s32[1]{0:T(128)} %bitcast.9.base_ref, bf16[4,64,1024]{2,1,0:T(8,128)(2,1)S(1)} %collective-permute-done.10.x_ref.a2, ...), custom_call_target="tpu_custom_call" | custom-call | flops 3355443200 | tf_op jit(solution)/shard_map/experts/pallas_call | solution.py:349
  82.0 5.3 %experts.7 = (bf16[256,1024]{1,0:T(8,128)(2,1)S(1)}, bf16[256,2048]{1,0:T(8,128)(2,1)S(1)}, bf16[256,1024]{1,0:T(8,128)(2,1)S(1)}, f32[64,1152]{1,0:T(8,128)S(1)...) custom-call(s32[1]{0:T(128)} %bitcast.9.base_ref, ...), custom_call_target="tpu_custom_call" | custom-call | flops 3355443200 | tf_op jit(solution)/shard_map/experts/pallas_call | solution.py:349
  87.3 4.3 %collective-permute-start.19 = (bf16[64,1152]{1,0:T(8,128)(2,1)}, bf16[64,1152]{1,0:T(8,128)(2,1)}, u32[]{:S(2)}, u32[]{:S(2)}) collective-permute-start(bf16[64,1152]{1,0:T(8,128)(2,1)} %get-tuple-element.212), channel_id=1, source_target_pairs={{0,8},{4,12},{8,0},{12,4},{1,9},{5,13},{9,1},{13,5},{2,10},{6,14},... | collective-permute-start | bytes 442376 | tf_op jit(solution)/shard_map/ppermute | solution.py:41
  91.8 10.9 %expert_grads.1.mine_ref = bf16[8,3072,128]{2,1,0:T(8,128)(2,1)} custom-call(bf16[256,1024]{1,0:T(8,128)(2,1)S(1)} %bitcast.21, bf16[256,1024]{1,0:T(8,128)(2,1)S(1)} %bitcast.22, bf16[256,1024]{1,0:T(8,128)(2,1)S(1)} %bitcast.23, bf16[256,1024]{1,0:T(8,128)(2,1)S(1)} %bitcast.24, bf16[256,2048]{1,0:T(8,128)(2,1)S(1)} %get-tuple-element.178.refs_4_, ...), custom_call_target="tpu_custom_call" | custom-call | flops 644245094400 | tf_op jit(solution)/shard_map/expert_grads/pallas_call | solution.py:431
  103.0 1.5 dn_sum.1
  107.2 2.0 collective-permute-start.23
  109.2 2.4 %collective-permute-start.24 = (bf16[64,1152]{1,0:T(8,128)(2,1)S(1)}, bf16[64,1152]{1,0:T(8,128)(2,1)S(1)}, u32[]{:S(2)}, u32[]{:S(2)}) collective-permute-start(bf16[64,1152]{1,0:T(8,128)(2,1)S(1)} %get-tuple-element.230), channel_id=1, source_target_pairs={{0,4},{4,0},{8,12},{12,8},{1,5},{5,1},{9,13},{13,9},{2,6},{6,2},{1... | collective-permute-start | bytes 442376 | tf_op jit(solution)/shard_map/ppermute | solution.py:41
  111.6 1.6 collective-permute-start.25
  113.2 7.6 %collective-permute-done.23.refs_1_ = bf16[64,1152]{1,0:T(8,128)(2,1)S(1)} collective-permute-done((bf16[64,1152]{1,0:T(8,128)(2,1)S(1)}, bf16[64,1152]{1,0:T(8,128)(2,1)S(1)}, u32[]{:S(2)}, u32[]{:S(2)}) %collective-permute-start.23) | collective-permute-done | bytes 147488 | tf_op jit(solution)/shard_map/ppermute | solution.py:41
  120.7 3.4 %collective-permute-start.26 = (bf16[64,1152]{1,0:T(8,128)(2,1)S(1)}, bf16[64,1152]{1,0:T(8,128)(2,1)S(1)}, u32[]{:S(2)}, u32[]{:S(2)}) collective-permute-start(bf16[64,1152]{1,0:T(8,128)(2,1)S(1)} %get-tuple-element.232), channel_id=1, source_target_pairs={{0,12},{4,8},{8,4},{12,0},{1,13},{5,9},{9,5},{13,1},{2,14},{6,10},... | collective-permute-start | bytes 442376 | tf_op jit(solution)/shard_map/ppermute | solution.py:41
  124.1 3.6 %collective-permute-done.26.refs_4_ = bf16[64,1152]{1,0:T(8,128)(2,1)S(1)} collective-permute-done((bf16[64,1152]{1,0:T(8,128)(2,1)S(1)}, bf16[64,1152]{1,0:T(8,128)(2,1)S(1)}, u32[]{:S(2)}, u32[]{:S(2)}) %collective-permute-start.26) | collective-permute-done | bytes 147488 | tf_op jit(solution)/shard_map/ppermute | solution.py:41
  131.8 1.6 collective-permute-start.30
  136.9 3.1 %collective-permute-done.30.w3 = bf16[64,1152]{1,0:T(8,128)(2,1)S(1)} collective-permute-done((bf16[64,1152]{1,0:T(8,128)(2,1)S(1)}, bf16[64,1152]{1,0:T(8,128)(2,1)S(1)}, u32[]{:S(2)}, u32[]{:S(2)}) %collective-permute-start.30) | collective-permute-done | bytes 147488 | tf_op jit(solution)/shard_map/ppermute | solution.py:41
  140.8 5.4 %attend_back.1 = (bf16[256,1152]{1,0:T(8,128)(2,1)}, bf16[256,512]{1,0:T(8,128)(2,1)}, f32[8,1024]{1,0:T(8,128)}, f32[64,1024]{1,0:T(8,128)}, bf16[64,1024]{1,0:...) custom-call(s32[1]{0:T(128)} %bitcast.me_ref, bf16[64,1152]{1,0:T(8,128)(2,1)} %copy-done.30, ...), custom_call_target="tpu_custom_call" | custom-call | flops 53687091200 | tf_op jit(solution)/shard_map/attend_back/pallas_call | solution.py:118
  146.2 4.1 %dense.1 = (f32[512,896]{1,0:T(8,128)}, bf16[512,896]{1,0:T(8,128)(2,1)}) custom-call(s32[2]{0:T(128)} %pad_add_fusion.me_ref, bf16[4,64,1024]{2,1,0:T(8,128)(2,1)} %copy-done.2, bf16[4,64,1024]{2,1,0:T(8,128)(2,1)} %copy-done.12, bf16[4,64,1024]{2,1,0:T(8,128)(2,1)} %copy-done.13, bf16[4,64,1024]{2,1,0:T(8,128)(2,1)} %copy-done.14, ...), custom_call_target="tpu_custom_call" | custom-call | flops 100 | tf_op jit(solution)/shard_map/dense/pallas_call | solution.py:118
  153.3 1.4 dense_dealt.1
  154.7 11.9 %collective-permute-start.33 = (bf16[128,896]{1,0:T(8,128)(2,1)S(1)}, bf16[128,896]{1,0:T(8,128)(2,1)S(1)}, u32[]{:S(2)}, u32[]{:S(2)}) collective-permute-start(bf16[128,896]{1,0:T(8,128)(2,1)S(1)} %get-tuple-element.263), channel_id=1, source_target_pairs={{0,4},{4,0},{8,12},{12,8},{1,5},{5,1},{9,13},{13,9},{2,6},{6,2},{1... | collective-permute-start | bytes 688136 | tf_op jit(solution)/shard_map/ppermute | solution.py:41
  166.6 2.4 %collective-permute-start.34 = (bf16[64,1024]{1,0:T(8,128)(2,1)}, bf16[64,1024]{1,0:T(8,128)(2,1)S(1)}, u32[]{:S(2)}, u32[]{:S(2)}) collective-permute-start(bf16[64,1024]{1,0:T(8,128)(2,1)} %get-tuple-element.265), channel_id=1, source_target_pairs={{0,1},{1,0},{2,3},{3,2},{4,5},{5,4},{6,7},{7,6},{8,9},{9,8},{10,11... | collective-permute-start | bytes 393224 | tf_op jit(solution)/shard_map/ppermute | solution.py:41
  170.5 1.9 collective-permute-start.40
  173.2 3.1 %collective-permute-start.41 = (bf16[128,896]{1,0:T(8,128)(2,1)S(1)}, bf16[128,896]{1,0:T(8,128)(2,1)S(1)}, u32[]{:S(2)}, u32[]{:S(2)}) collective-permute-start(bf16[128,896]{1,0:T(8,128)(2,1)S(1)} %get-tuple-element.276), channel_id=1, source_target_pairs={{0,12},{4,8},{8,4},{12,0},{1,13},{5,9},{9,5},{13,1},{2,14},{6,10},... | collective-permute-start | bytes 688136 | tf_op jit(solution)/shard_map/ppermute | solution.py:41
  179.1 6.8 %collective-permute-start.37 = (bf16[64,1024]{1,0:T(8,128)(2,1)S(1)}, bf16[64,1024]{1,0:T(8,128)(2,1)S(1)}, u32[]{:S(2)}, u32[]{:S(2)}) collective-permute-start(bf16[64,1024]{1,0:T(8,128)(2,1)S(1)} %input_grad.1.refs_0_), channel_id=1, source_target_pairs={{0,1},{1,0},{2,3},{3,2},{4,5},{5,4},{6,7},{7,6},{8,9},{9,8},{10,11... | collective-permute-start | bytes 393224 | tf_op jit(solution)/shard_map/ppermute | solution.py:41
  186.0 1.5 collective-permute-start.39
  187.5 7.9 %collective-permute-done.40.refs_1_ = bf16[128,896]{1,0:T(8,128)(2,1)S(1)} collective-permute-done((bf16[128,896]{1,0:T(8,128)(2,1)S(1)}, bf16[128,896]{1,0:T(8,128)(2,1)S(1)}, u32[]{:S(2)}, u32[]{:S(2)}) %collective-permute-start.40) | collective-permute-done | bytes 229408 | tf_op jit(solution)/shard_map/ppermute | solution.py:41
  197.2 2.8 %collective-permute-start.43 = (bf16[80,1024]{1,0:T(8,128)(2,1)S(1)}, bf16[80,1024]{1,0:T(8,128)(2,1)S(1)}, u32[]{:S(2)}, u32[]{:S(2)}) collective-permute-start(bf16[80,1024]{1,0:T(8,128)(2,1)S(1)} %out_piece.1.refs_0_), channel_id=1, source_target_pairs={{0,1},{1,0},{2,3},{3,2},{4,5},{5,4},{6,7},{7,6},{8,9},{9,8},{10,11... | collective-permute-start | bytes 491528 | tf_op jit(solution)/shard_map/ppermute | solution.py:41
  201.5 11.1 %both_copies.1 = (f32[8,1024,128]{2,1,0:T(8,128)}, f32[8,1024,128]{2,1,0:T(8,128)}, f32[8,128,1024]{2,1,0:T(8,128)}) custom-call(bf16[8,3072,128]{2,1,0:T(8,128)(2,1)} %expert_grads.1.mine_ref, bf16[8,3072,128]{2,1,0:T(8,128)(2,1)} %collective-permute-done.27.other_ref), custom_call_target="tpu_custom_call" | custom-call | bytes 25165824 | tf_op jit(solution)/shard_map/both_copies/pallas_call | solution.py:460
  (149 shorter events, 34.9 us)
Async XLA Ops:
  7.2 189.1 %reduce-scatter.2.cloned.1.call-start = ((), (), s32[]{:S(2)}) async-start(), calls=%async_computation.1 | async-start | bytes 655360 | tf_op jit(solution)/shard_map/reduce_scatter | solution.py:821
  9.4 9.1 %collective-permute-start = (bf16[64,1152]{1,0:T(8,128)(2,1)}, bf16[64,1152]{1,0:T(8,128)(2,1)S(1)}, u32[]{:S(2)}, u32[]{:S(2)}) collective-permute-start(bf16[64,1152]{1,0:T(8,128)(2,1)} %get-tuple-element.157.own_ref.refs_0_.cot_ref), channel_id=1, source_target_pairs={{0,4},{4,0},{8,12},{12,8},{1,5},{5,1},{9,13},{13,9},{2,6},{6,2},{1... | collective-permute-start | bytes 442376 | tf_op jit(solution)/shard_map/ppermute | solution.py:41
  12.4 22.1 %collective-permute-start.4 = (bf16[64,1152]{1,0:T(8,128)(2,1)}, bf16[64,1152]{1,0:T(8,128)(2,1)S(1)}, u32[]{:S(2)}, u32[]{:S(2)}) collective-permute-start(bf16[64,1152]{1,0:T(8,128)(2,1)} %get-tuple-element.157.own_ref.refs_0_.cot_ref), channel_id=1, source_target_pairs={{0,8},{4,12},{8,0},{12,4},{1,9},{5,13},{9,1},{13,5},{2,10},{6,14},... | collective-permute-start | bytes 442376 | tf_op jit(solution)/shard_map/ppermute | solution.py:41
  15.0 19.5 %collective-permute-start.5 = (bf16[64,1152]{1,0:T(8,128)(2,1)}, bf16[64,1152]{1,0:T(8,128)(2,1)S(1)}, u32[]{:S(2)}, u32[]{:S(2)}) collective-permute-start(bf16[64,1152]{1,0:T(8,128)(2,1)} %get-tuple-element.157.own_ref.refs_0_.cot_ref), channel_id=1, source_target_pairs={{0,12},{4,8},{8,4},{12,0},{1,13},{5,9},{9,5},{13,1},{2,14},{6,10},... | collective-permute-start | bytes 442376 | tf_op jit(solution)/shard_map/ppermute | solution.py:41
  23.2 5.2 %collective-permute-start.1 = (bf16[64,1024]{1,0:T(8,128)(2,1)}, bf16[64,1024]{1,0:T(8,128)(2,1)S(1)}, u32[]{:S(2)}, u32[]{:S(2)}) collective-permute-start(bf16[64,1024]{1,0:T(8,128)(2,1)} %get-tuple-element.161), channel_id=1, source_target_pairs={{0,1},{1,0},{2,3},{3,2},{4,5},{5,4},{6,7},{7,6},{8,9},{9,8},{10,11... | collective-permute-start | bytes 393224 | tf_op jit(solution)/shard_map/ppermute | solution.py:41
  24.9 5.2 %collective-permute-start.2 = (bf16[64,1024]{1,0:T(8,128)(2,1)}, bf16[64,1024]{1,0:T(8,128)(2,1)S(1)}, u32[]{:S(2)}, u32[]{:S(2)}) collective-permute-start(bf16[64,1024]{1,0:T(8,128)(2,1)} %get-tuple-element.162), channel_id=1, source_target_pairs={{0,2},{1,3},{2,0},{3,1},{4,6},{5,7},{6,4},{7,5},{8,10},{9,11},{10,... | collective-permute-start | bytes 393224 | tf_op jit(solution)/shard_map/ppermute | solution.py:41
  26.4 6.1 %collective-permute-start.3 = (bf16[64,1024]{1,0:T(8,128)(2,1)}, bf16[64,1024]{1,0:T(8,128)(2,1)S(1)}, u32[]{:S(2)}, u32[]{:S(2)}) collective-permute-start(bf16[64,1024]{1,0:T(8,128)(2,1)} %get-tuple-element.163), channel_id=1, source_target_pairs={{0,3},{1,2},{2,1},{3,0},{4,7},{5,6},{6,5},{7,4},{8,11},{9,10},{10,... | collective-permute-start | bytes 393224 | tf_op jit(solution)/shard_map/ppermute | solution.py:41
  34.5 5.0 %collective-permute-start.6 = (bf16[64,1024]{1,0:T(8,128)(2,1)S(1)}, bf16[64,1024]{1,0:T(8,128)(2,1)S(1)}, u32[]{:S(2)}, u32[]{:S(2)}) collective-permute-start(bf16[64,1024]{1,0:T(8,128)(2,1)S(1)} %get-tuple-element.166.refs_0_.n_ref), channel_id=1, source_target_pairs={{0,4},{4,0},{8,12},{12,8},{1,5},{5,1},{9,13},{13,9},{2,6},{6,2},{1... | collective-permute-start | bytes 393224 | tf_op jit(solution)/shard_map/ppermute | solution.py:41
  35.0 19.2 %collective-permute-start.11 = (bf16[3,64,1152]{2,1,0:T(8,128)(2,1)S(1)}, bf16[3,64,1152]{2,1,0:T(8,128)(2,1)}, u32[]{:S(2)}, u32[]{:S(2)}) collective-permute-start(bf16[3,64,1152]{2,1,0:T(8,128)(2,1)S(1)} %together.2.far_ref.refs_4_), channel_id=1, source_target_pairs={{0,1},{1,0},{2,3},{3,2},{4,5},{5,4},{6,7},{7,6},{8,9},{9,8},{10,11... | collective-permute-start | bytes 1327112 | tf_op jit(solution)/shard_map/ppermute | solution.py:41
  35.6 18.6 %collective-permute-start.12 = (bf16[3,64,1152]{2,1,0:T(8,128)(2,1)S(1)}, bf16[3,64,1152]{2,1,0:T(8,128)(2,1)}, u32[]{:S(2)}, u32[]{:S(2)}) collective-permute-start(bf16[3,64,1152]{2,1,0:T(8,128)(2,1)S(1)} %together.2.far_ref.refs_4_), channel_id=1, source_target_pairs={{0,2},{1,3},{2,0},{3,1},{4,6},{5,7},{6,4},{7,5},{8,10},{9,11},{10,... | collective-permute-start | bytes 1327112 | tf_op jit(solution)/shard_map/ppermute | solution.py:41
  39.6 18.3 %collective-permute-start.14 = (bf16[3,64,1152]{2,1,0:T(8,128)(2,1)S(1)}, bf16[3,64,1152]{2,1,0:T(8,128)(2,1)S(1)}, u32[]{:S(2)}, u32[]{:S(2)}) collective-permute-start(bf16[3,64,1152]{2,1,0:T(8,128)(2,1)S(1)} %together.2.far_ref.refs_4_), channel_id=1, source_target_pairs={{0,3},{1,2},{2,1},{3,0},{4,7},{5,6},{6,5},{7,4},{8,11},{9,10},{10,... | collective-permute-start | bytes 1327112 | tf_op jit(solution)/shard_map/ppermute | solution.py:41
  40.0 10.2 %collective-permute-start.7 = (bf16[64,1024]{1,0:T(8,128)(2,1)S(1)}, bf16[64,1024]{1,0:T(8,128)(2,1)}, u32[]{:S(2)}, u32[]{:S(2)}) collective-permute-start(bf16[64,1024]{1,0:T(8,128)(2,1)S(1)} %get-tuple-element.166.refs_0_.n_ref), channel_id=1, source_target_pairs={{0,8},{4,12},{8,0},{12,4},{1,9},{5,13},{9,1},{13,5},{2,10},{6,14},... | collective-permute-start | bytes 393224 | tf_op jit(solution)/shard_map/ppermute | solution.py:41
  42.6 7.6 %collective-permute-start.8 = (bf16[64,1024]{1,0:T(8,128)(2,1)S(1)}, bf16[64,1024]{1,0:T(8,128)(2,1)}, u32[]{:S(2)}, u32[]{:S(2)}) collective-permute-start(bf16[64,1024]{1,0:T(8,128)(2,1)S(1)} %get-tuple-element.166.refs_0_.n_ref), channel_id=1, source_target_pairs={{0,12},{4,8},{8,4},{12,0},{1,13},{5,9},{9,5},{13,1},{2,14},{6,10},... | collective-permute-start | bytes 393224 | tf_op jit(solution)/shard_map/ppermute | solution.py:41
  51.3 40.5 %copy-start.2 = (bf16[4,64,1024]{2,1,0:T(8,128)(2,1)}, bf16[4,64,1024]{2,1,0:T(8,128)(2,1)S(1)}, u32[]{:S(2)}) copy-start(bf16[4,64,1024]{2,1,0:T(8,128)(2,1)S(1)} %together.3.x_ref.a0) | copy-start | bytes 1572868
  51.3 15.7 %collective-permute-start.9 = (bf16[4,64,1024]{2,1,0:T(8,128)(2,1)S(1)}, bf16[4,64,1024]{2,1,0:T(8,128)(2,1)S(1)}, u32[]{:S(2)}, u32[]{:S(2)}) collective-permute-start(bf16[4,64,1024]{2,1,0:T(8,128)(2,1)S(1)} %together.3.x_ref.a0), channel_id=1, source_target_pairs={{0,1},{1,0},{2,3},{3,2},{4,5},{5,4},{6,7},{7,6},{8,9},{9,8},{10,11... | collective-permute-start | bytes 1572872 | tf_op jit(solution)/shard_map/ppermute | solution.py:41
  52.6 22.1 %collective-permute-start.10 = (bf16[4,64,1024]{2,1,0:T(8,128)(2,1)S(1)}, bf16[4,64,1024]{2,1,0:T(8,128)(2,1)S(1)}, u32[]{:S(2)}, u32[]{:S(2)}) collective-permute-start(bf16[4,64,1024]{2,1,0:T(8,128)(2,1)S(1)} %together.3.x_ref.a0), channel_id=1, source_target_pairs={{0,2},{1,3},{2,0},{3,1},{4,6},{5,7},{6,4},{7,5},{8,10},{9,11},{10,... | collective-permute-start | bytes 1572872 | tf_op jit(solution)/shard_map/ppermute | solution.py:41
  60.1 6.9 %collective-permute-start.15 = (f32[1,128]{1,0:T(1,128)S(1)}, f32[1,128]{1,0:T(1,128)S(1)}, u32[]{:S(2)}, u32[]{:S(2)}) collective-permute-start(f32[1,128]{1,0:T(1,128)S(1)} %counts.1), channel_id=1, source_target_pairs={{0,16},{16,0},{1,17},{17,1},{2,18},{18,2},{3,19},{19,3},{4,20},{20... | collective-permute-start | bytes 1544 | tf_op jit(solution)/shard_map/ppermute | solution.py:41
  65.7 16.3 %collective-permute-start.13 = (bf16[4,64,1024]{2,1,0:T(8,128)(2,1)S(1)}, bf16[4,64,1024]{2,1,0:T(8,128)(2,1)S(1)}, u32[]{:S(2)}, u32[]{:S(2)}) collective-permute-start(bf16[4,64,1024]{2,1,0:T(8,128)(2,1)S(1)} %together.3.x_ref.a0), channel_id=1, source_target_pairs={{0,3},{1,2},{2,1},{3,0},{4,7},{5,6},{6,5},{7,4},{8,11},{9,10},{10,... | collective-permute-start | bytes 1572872 | tf_op jit(solution)/shard_map/ppermute | solution.py:41
  73.3 29.7 %collective-permute-start.16 = (bf16[4,64,1152]{2,1,0:T(8,128)(2,1)}, bf16[4,64,1152]{2,1,0:T(8,128)(2,1)}, u32[]{:S(2)}, u32[]{:S(2)}) collective-permute-start(bf16[4,64,1152]{2,1,0:T(8,128)(2,1)} %get-tuple-element.185), channel_id=1, source_target_pairs={{0,1},{1,0},{2,3},{3,2},{4,5},{5,4},{6,7},{7,6},{8,9},{9,8},{10,11... | collective-permute-start | bytes 1769480 | tf_op jit(solution)/shard_map/ppermute | solution.py:41
  81.2 21.8 %collective-permute-start.17 = (bf16[4,64,1152]{2,1,0:T(8,128)(2,1)}, bf16[4,64,1152]{2,1,0:T(8,128)(2,1)}, u32[]{:S(2)}, u32[]{:S(2)}) collective-permute-start(bf16[4,64,1152]{2,1,0:T(8,128)(2,1)} %get-tuple-element.194), channel_id=1, source_target_pairs={{0,2},{1,3},{2,0},{3,1},{4,6},{5,7},{6,4},{7,5},{8,10},{9,11},{10,... | collective-permute-start | bytes 1769480 | tf_op jit(solution)/shard_map/ppermute | solution.py:41
  87.3 15.3 %collective-permute-start.18 = (bf16[64,1152]{1,0:T(8,128)(2,1)}, bf16[64,1152]{1,0:T(8,128)(2,1)}, u32[]{:S(2)}, u32[]{:S(2)}) collective-permute-start(bf16[64,1152]{1,0:T(8,128)(2,1)} %get-tuple-element.211), channel_id=1, source_target_pairs={{0,4},{4,0},{8,12},{12,8},{1,5},{5,1},{9,13},{13,9},{2,6},{6,2},{1... | collective-permute-start | bytes 442376 | tf_op jit(solution)/shard_map/ppermute | solution.py:41
  87.3 15.6 %collective-permute-start.19 = (bf16[64,1152]{1,0:T(8,128)(2,1)}, bf16[64,1152]{1,0:T(8,128)(2,1)}, u32[]{:S(2)}, u32[]{:S(2)}) collective-permute-start(bf16[64,1152]{1,0:T(8,128)(2,1)} %get-tuple-element.212), channel_id=1, source_target_pairs={{0,8},{4,12},{8,0},{12,4},{1,9},{5,13},{9,1},{13,5},{2,10},{6,14},... | collective-permute-start | bytes 442376 | tf_op jit(solution)/shard_map/ppermute | solution.py:41
  91.6 11.4 %collective-permute-start.20 = (bf16[64,1152]{1,0:T(8,128)(2,1)}, bf16[64,1152]{1,0:T(8,128)(2,1)}, u32[]{:S(2)}, u32[]{:S(2)}) collective-permute-start(bf16[64,1152]{1,0:T(8,128)(2,1)} %get-tuple-element.213), channel_id=1, source_target_pairs={{0,12},{4,8},{8,4},{12,0},{1,13},{5,9},{9,5},{13,1},{2,14},{6,10},... | collective-permute-start | bytes 442376 | tf_op jit(solution)/shard_map/ppermute | solution.py:41
  104.4 23.3 %collective-permute-start.21 = (bf16[4,64,1024]{2,1,0:T(8,128)(2,1)S(1)}, bf16[4,64,1024]{2,1,0:T(8,128)(2,1)S(1)}, u32[]{:S(2)}, u32[]{:S(2)}) collective-permute-start(bf16[4,64,1024]{2,1,0:T(8,128)(2,1)S(1)} %get-tuple-element.223), channel_id=1, source_target_pairs={{0,1},{1,0},{2,3},{3,2},{4,5},{5,4},{6,7},{7,6},{8,9},{9,8},{10,11... | collective-permute-start | bytes 1572872 | tf_op jit(solution)/shard_map/ppermute | solution.py:41
  104.9 22.8 %collective-permute-start.22 = (bf16[4,64,1024]{2,1,0:T(8,128)(2,1)S(1)}, bf16[4,64,1024]{2,1,0:T(8,128)(2,1)S(1)}, u32[]{:S(2)}, u32[]{:S(2)}) collective-permute-start(bf16[4,64,1024]{2,1,0:T(8,128)(2,1)S(1)} %get-tuple-element.224), channel_id=1, source_target_pairs={{0,2},{1,3},{2,0},{3,1},{4,6},{5,7},{6,4},{7,5},{8,10},{9,11},{10,... | collective-permute-start | bytes 1572872 | tf_op jit(solution)/shard_map/ppermute | solution.py:41
  107.2 13.6 %collective-permute-start.23 = (bf16[64,1152]{1,0:T(8,128)(2,1)S(1)}, bf16[64,1152]{1,0:T(8,128)(2,1)S(1)}, u32[]{:S(2)}, u32[]{:S(2)}) collective-permute-start(bf16[64,1152]{1,0:T(8,128)(2,1)S(1)} %through.1), channel_id=1, source_target_pairs={{0,3},{1,2},{2,1},{3,0},{4,7},{5,6},{6,5},{7,4},{8,11},{9,10},{10,... | collective-permute-start | bytes 442376 | tf_op jit(solution)/shard_map/ppermute | solution.py:41
  109.2 15.0 %collective-permute-start.24 = (bf16[64,1152]{1,0:T(8,128)(2,1)S(1)}, bf16[64,1152]{1,0:T(8,128)(2,1)S(1)}, u32[]{:S(2)}, u32[]{:S(2)}) collective-permute-start(bf16[64,1152]{1,0:T(8,128)(2,1)S(1)} %get-tuple-element.230), channel_id=1, source_target_pairs={{0,4},{4,0},{8,12},{12,8},{1,5},{5,1},{9,13},{13,9},{2,6},{6,2},{1... | collective-permute-start | bytes 442376 | tf_op jit(solution)/shard_map/ppermute | solution.py:41
  111.6 12.6 %collective-permute-start.25 = (bf16[64,1152]{1,0:T(8,128)(2,1)S(1)}, bf16[64,1152]{1,0:T(8,128)(2,1)S(1)}, u32[]{:S(2)}, u32[]{:S(2)}) collective-permute-start(bf16[64,1152]{1,0:T(8,128)(2,1)S(1)} %get-tuple-element.231), channel_id=1, source_target_pairs={{0,8},{4,12},{8,0},{12,4},{1,9},{5,13},{9,1},{13,5},{2,10},{6,14},... | collective-permute-start | bytes 442376 | tf_op jit(solution)/shard_map/ppermute | solution.py:41
  120.7 7.0 %collective-permute-start.26 = (bf16[64,1152]{1,0:T(8,128)(2,1)S(1)}, bf16[64,1152]{1,0:T(8,128)(2,1)S(1)}, u32[]{:S(2)}, u32[]{:S(2)}) collective-permute-start(bf16[64,1152]{1,0:T(8,128)(2,1)S(1)} %get-tuple-element.232), channel_id=1, source_target_pairs={{0,12},{4,8},{8,4},{12,0},{1,13},{5,9},{9,5},{13,1},{2,14},{6,10},... | collective-permute-start | bytes 442376 | tf_op jit(solution)/shard_map/ppermute | solution.py:41
  129.9 10.5 %collective-permute-start.27 = (bf16[8,3072,128]{2,1,0:T(8,128)(2,1)}, bf16[8,3072,128]{2,1,0:T(8,128)(2,1)}, u32[]{:S(2)}, u32[]{:S(2)}) collective-permute-start(bf16[8,3072,128]{2,1,0:T(8,128)(2,1)} %expert_grads.1.mine_ref), channel_id=1, source_target_pairs={{0,16},{16,0},{1,17},{17,1},{2,18},{18,2},{3,19},{19,3},{4,20},{20... | collective-permute-start | bytes 18874376 | tf_op jit(solution)/shard_map/ppermute | solution.py:41
  129.9 6.6 %collective-permute-start.28 = (bf16[64,1152]{1,0:T(8,128)(2,1)S(1)}, bf16[64,1152]{1,0:T(8,128)(2,1)S(1)}, u32[]{:S(2)}, u32[]{:S(2)}) collective-permute-start(bf16[64,1152]{1,0:T(8,128)(2,1)S(1)} %get-tuple-element.247.w0), channel_id=1, source_target_pairs={{0,1},{1,0},{2,3},{3,2},{4,5},{5,4},{6,7},{7,6},{8,9},{9,8},{10,11... | collective-permute-start | bytes 442376 | tf_op jit(solution)/shard_map/ppermute | solution.py:41
  130.6 6.4 %collective-permute-start.29 = (bf16[64,1152]{1,0:T(8,128)(2,1)S(1)}, bf16[64,1152]{1,0:T(8,128)(2,1)S(1)}, u32[]{:S(2)}, u32[]{:S(2)}) collective-permute-start(bf16[64,1152]{1,0:T(8,128)(2,1)S(1)} %get-tuple-element.247.w0), channel_id=1, source_target_pairs={{0,2},{1,3},{2,0},{3,1},{4,6},{5,7},{6,4},{7,5},{8,10},{9,11},{10,... | collective-permute-start | bytes 442376 | tf_op jit(solution)/shard_map/ppermute | solution.py:41
  131.8 8.3 %collective-permute-start.30 = (bf16[64,1152]{1,0:T(8,128)(2,1)S(1)}, bf16[64,1152]{1,0:T(8,128)(2,1)S(1)}, u32[]{:S(2)}, u32[]{:S(2)}) collective-permute-start(bf16[64,1152]{1,0:T(8,128)(2,1)S(1)} %get-tuple-element.247.w0), channel_id=1, source_target_pairs={{0,3},{1,2},{2,1},{3,0},{4,7},{5,6},{6,5},{7,4},{8,11},{9,10},{10,... | collective-permute-start | bytes 442376 | tf_op jit(solution)/shard_map/ppermute | solution.py:41
  134.0 16.9 %collective-permute-start.42 = (bf16[4,64,1024]{2,1,0:T(8,128)(2,1)}, bf16[4,64,1024]{2,1,0:T(8,128)(2,1)S(1)}, u32[]{:S(2)}, u32[]{:S(2)}) collective-permute-start(bf16[4,64,1024]{2,1,0:T(8,128)(2,1)} %get-tuple-element.282), channel_id=1, source_target_pairs={{0,3},{1,2},{2,1},{3,0},{4,7},{5,6},{6,5},{7,4},{8,11},{9,10},{10,... | collective-permute-start | bytes 1572872 | tf_op jit(solution)/shard_map/ppermute | solution.py:41
  150.3 2.9 %collective-permute-start.31 = (bf16[512,896]{1,0:T(8,128)(2,1)}, bf16[512,896]{1,0:T(8,128)(2,1)}, u32[]{:S(2)}, u32[]{:S(2)}) collective-permute-start(bf16[512,896]{1,0:T(8,128)(2,1)} %get-tuple-element.261), channel_id=1, source_target_pairs={{0,16},{16,0},{1,17},{17,1},{2,18},{18,2},{3,19},{19,3},{4,20},{20... | collective-permute-start | bytes 2752520 | tf_op jit(solution)/shard_map/ppermute | solution.py:41
  152.0 1.3 collective-permute-start.32
  154.7 22.3 %collective-permute-start.33 = (bf16[128,896]{1,0:T(8,128)(2,1)S(1)}, bf16[128,896]{1,0:T(8,128)(2,1)S(1)}, u32[]{:S(2)}, u32[]{:S(2)}) collective-permute-start(bf16[128,896]{1,0:T(8,128)(2,1)S(1)} %get-tuple-element.263), channel_id=1, source_target_pairs={{0,4},{4,0},{8,12},{12,8},{1,5},{5,1},{9,13},{13,9},{2,6},{6,2},{1... | collective-permute-start | bytes 688136 | tf_op jit(solution)/shard_map/ppermute | solution.py:41
  166.6 6.6 %collective-permute-start.34 = (bf16[64,1024]{1,0:T(8,128)(2,1)}, bf16[64,1024]{1,0:T(8,128)(2,1)S(1)}, u32[]{:S(2)}, u32[]{:S(2)}) collective-permute-start(bf16[64,1024]{1,0:T(8,128)(2,1)} %get-tuple-element.265), channel_id=1, source_target_pairs={{0,1},{1,0},{2,3},{3,2},{4,5},{5,4},{6,7},{7,6},{8,9},{9,8},{10,11... | collective-permute-start | bytes 393224 | tf_op jit(solution)/shard_map/ppermute | solution.py:41
  169.0 8.0 %collective-permute-start.35 = (bf16[64,1024]{1,0:T(8,128)(2,1)}, bf16[64,1024]{1,0:T(8,128)(2,1)S(1)}, u32[]{:S(2)}, u32[]{:S(2)}) collective-permute-start(bf16[64,1024]{1,0:T(8,128)(2,1)} %get-tuple-element.266), channel_id=1, source_target_pairs={{0,2},{1,3},{2,0},{3,1},{4,6},{5,7},{6,4},{7,5},{8,10},{9,11},{10,... | collective-permute-start | bytes 393224 | tf_op jit(solution)/shard_map/ppermute | solution.py:41
  169.9 7.1 %collective-permute-start.36 = (bf16[64,1024]{1,0:T(8,128)(2,1)S(1)}, bf16[64,1024]{1,0:T(8,128)(2,1)S(1)}, u32[]{:S(2)}, u32[]{:S(2)}) collective-permute-start(bf16[64,1024]{1,0:T(8,128)(2,1)S(1)} %copy-done.35), channel_id=1, source_target_pairs={{0,3},{1,2},{2,1},{3,0},{4,7},{5,6},{6,5},{7,4},{8,11},{9,10},{10,... | collective-permute-start | bytes 393224 | tf_op jit(solution)/shard_map/ppermute | solution.py:41
  170.5 24.9 %collective-permute-start.40 = (bf16[128,896]{1,0:T(8,128)(2,1)S(1)}, bf16[128,896]{1,0:T(8,128)(2,1)S(1)}, u32[]{:S(2)}, u32[]{:S(2)}) collective-permute-start(bf16[128,896]{1,0:T(8,128)(2,1)S(1)} %get-tuple-element.275), channel_id=1, source_target_pairs={{0,8},{4,12},{8,0},{12,4},{1,9},{5,13},{9,1},{13,5},{2,10},{6,14},... | collective-permute-start | bytes 688136 | tf_op jit(solution)/shard_map/ppermute | solution.py:41
  173.2 22.2 %collective-permute-start.41 = (bf16[128,896]{1,0:T(8,128)(2,1)S(1)}, bf16[128,896]{1,0:T(8,128)(2,1)S(1)}, u32[]{:S(2)}, u32[]{:S(2)}) collective-permute-start(bf16[128,896]{1,0:T(8,128)(2,1)S(1)} %get-tuple-element.276), channel_id=1, source_target_pairs={{0,12},{4,8},{8,4},{12,0},{1,13},{5,9},{9,5},{13,1},{2,14},{6,10},... | collective-permute-start | bytes 688136 | tf_op jit(solution)/shard_map/ppermute | solution.py:41
  179.1 17.1 %collective-permute-start.37 = (bf16[64,1024]{1,0:T(8,128)(2,1)S(1)}, bf16[64,1024]{1,0:T(8,128)(2,1)S(1)}, u32[]{:S(2)}, u32[]{:S(2)}) collective-permute-start(bf16[64,1024]{1,0:T(8,128)(2,1)S(1)} %input_grad.1.refs_0_), channel_id=1, source_target_pairs={{0,1},{1,0},{2,3},{3,2},{4,5},{5,4},{6,7},{7,6},{8,9},{9,8},{10,11... | collective-permute-start | bytes 393224 | tf_op jit(solution)/shard_map/ppermute | solution.py:41
  185.9 10.3 %collective-permute-start.38 = (bf16[64,1024]{1,0:T(8,128)(2,1)S(1)}, bf16[64,1024]{1,0:T(8,128)(2,1)S(1)}, u32[]{:S(2)}, u32[]{:S(2)}) collective-permute-start(bf16[64,1024]{1,0:T(8,128)(2,1)S(1)} %input_grad.1.refs_0_), channel_id=1, source_target_pairs={{0,2},{1,3},{2,0},{3,1},{4,6},{5,7},{6,4},{7,5},{8,10},{9,11},{10,... | collective-permute-start | bytes 393224 | tf_op jit(solution)/shard_map/ppermute | solution.py:41
  186.0 10.3 %collective-permute-start.39 = (bf16[64,1024]{1,0:T(8,128)(2,1)S(1)}, bf16[64,1024]{1,0:T(8,128)(2,1)S(1)}, u32[]{:S(2)}, u32[]{:S(2)}) collective-permute-start(bf16[64,1024]{1,0:T(8,128)(2,1)S(1)} %input_grad.1.refs_0_), channel_id=1, source_target_pairs={{0,3},{1,2},{2,1},{3,0},{4,7},{5,6},{6,5},{7,4},{8,11},{9,10},{10,... | collective-permute-start | bytes 393224 | tf_op jit(solution)/shard_map/ppermute | solution.py:41
  197.2 17.2 %collective-permute-start.43 = (bf16[80,1024]{1,0:T(8,128)(2,1)S(1)}, bf16[80,1024]{1,0:T(8,128)(2,1)S(1)}, u32[]{:S(2)}, u32[]{:S(2)}) collective-permute-start(bf16[80,1024]{1,0:T(8,128)(2,1)S(1)} %out_piece.1.refs_0_), channel_id=1, source_target_pairs={{0,1},{1,0},{2,3},{3,2},{4,5},{5,4},{6,7},{7,6},{8,9},{9,8},{10,11... | collective-permute-start | bytes 491528 | tf_op jit(solution)/shard_map/ppermute | solution.py:41
  200.0 14.4 %collective-permute-start.44 = (bf16[80,1024]{1,0:T(8,128)(2,1)S(1)}, bf16[80,1024]{1,0:T(8,128)(2,1)S(1)}, u32[]{:S(2)}, u32[]{:S(2)}) collective-permute-start(bf16[80,1024]{1,0:T(8,128)(2,1)S(1)} %out_piece.1.refs_0_), channel_id=1, source_target_pairs={{0,2},{1,3},{2,0},{3,1},{4,6},{5,7},{6,4},{7,5},{8,10},{9,11},{10,... | collective-permute-start | bytes 491528 | tf_op jit(solution)/shard_map/ppermute | solution.py:41
  201.0 13.4 %collective-permute-start.45 = (bf16[80,1024]{1,0:T(8,128)(2,1)S(1)}, bf16[80,1024]{1,0:T(8,128)(2,1)S(1)}, u32[]{:S(2)}, u32[]{:S(2)}) collective-permute-start(bf16[80,1024]{1,0:T(8,128)(2,1)S(1)} %out_piece.1.refs_0_), channel_id=1, source_target_pairs={{0,3},{1,2},{2,1},{3,0},{4,7},{5,6},{6,5},{7,4},{8,11},{9,10},{10,... | collective-permute-start | bytes 491528 | tf_op jit(solution)/shard_map/ppermute | solution.py:41
  (35 other events, 454.4 us)
Sparse Core Ops, SparseCore 0:
  152.1 40.3 reduce-scatter.1

commit v6 on v5

--- a/solution.py
+++ b/solution.py
@@ -386,15 +386,6 @@
     return call(functools.partial(split_sum_kernel, len(arrays), True), outs, arrays, name)
 
 
-def moe_sum_kernel(me_ref, *refs):
-    pieces, out = refs[:-1], refs[-1]
-    for s in range(out.shape[0]):
-        total = pieces[0][s].astype(F32)
-        for x in pieces[1:]:
-            total = total + x[s].astype(F32)
-        out[me_ref[0] ^ s] = total.astype(out.dtype)
-
-
 def add_kernel(*refs):
     pieces, out = refs[:-1], refs[-1]
     total = pieces[0][...].astype(F32)
@@ -752,7 +743,7 @@
         [shape((rows, width), F32), shape((rows, width), BF)],
         (xq, gain_two, parts[0], *got),
         "norm_two",
-        "vb",
+        "bbb",
         "vv",
     )
 
@@ -791,13 +782,12 @@
     grads, (got, from_last) = tied(grads, (got, from_last))
     near, *across = split_sum([ds[0], *got], "dn_sum")
     through = added([near_last, *from_last], BF, "through")
-    across[0], middle = tied(across[0], moes[1:last])
+    across[0], (middle, moe_last) = tied(across[0], (moes[1:last], moes[last]))
     across = deal(across, "expert")
     near_sums = [near, swap(through, "tensor", last), *across]
     moe_got = [swap(middle[r - 1], "tensor", r) for r in range(1, last)]
+    moe_got.append(swap(moe_last, "tensor", last))
     moe_got, near_sums = tied(moe_got, near_sums)
-    near_sums[2], moe_last = tied(near_sums[2], moes[last])
-    moe_got.append(swap(moe_last, "tensor", last))
 
     wide, dh, small = call(
         functools.partial(norm_back_kernel, experts, len(near_sums)),
@@ -811,14 +801,9 @@
     _, late_grads = tied(wide, grads)
     grads_got = swap(late_grads, "dp", 1)
     grads_got, wides = tied(grads_got, wides)
-    moe = call(
-        moe_sum_kernel,
-        [shape((expert_size, rows, width), BF)],
-        (e_at, moes[0], *moe_got),
-        "moe_sum",
-        "s",
-    )[0]
-    moe = lax.psum_scatter(moe, "expert", scatter_dimension=0, tiled=False)
+    moe_near, *moe_across = split_sum([moes[0], *moe_got], "moe_sum")
+    moe_across, wides = tied(moe_across, wides)
+    moe_sums = [moe_near, *deal(moe_across, "expert")]
 
     wide_all, dqkv, small, *back_parts = call(
         attend_back_kernel,
@@ -873,7 +858,7 @@
     others = deal(others, "expert")
     others[0], part_sums = tied(others[0], part_sums)
     ig = call(
-        input_grad_kernel, [shape((rows, width), BF)], (xq, gain_one, dh, *part_sums), "input_grad", "vb"
+        input_grad_kernel, [shape((rows, width), BF)], (xq, gain_one, dh, *part_sums), "input_grad", "bbbb"
     )[0]
     igs = [ig] + [swap(ig, "tensor", r) for r in around]
     g_query, g_key, g_value, g_out, g_router, small = call(
@@ -898,7 +883,7 @@
     input_grad = call(
         natural_kernel, [shape((seq_len, width), F32)], (t_at, *igs), "input_grad_whole", "s", "b"
     )[0]
-    out_piece = call(out_kernel, [shape((rows + 16, width), BF)], (h, small, moe), "out_piece")[0]
+    out_piece = call(out_kernel, [shape((rows + 16, width), BF)], (h, small, *moe_sums), "out_piece")[0]
     outs = [out_piece] + [swap(out_piece, "tensor", r) for r in around]
     expert_grads = both_copies(grads, grads_got)
     expert_grads, outs = tied(expert_grads, outs)

time: 225 us -> 226 us (level)
  waiting for transfers between devices: 47.3 us -> 77.6 us
  between operations: 14.5 us -> 1.06 us
  starting transfers between devices: 75.4 us -> 63.2 us
  Pallas kernels: 74.8 us -> 72.5 us
    ppermute x46 -> x49, waiting for transfers between devices: 47.3 us -> 77.6 us  [swap(): return lax.ppermute(x, axis, [(i, i ^ distance) for i in range(size)])]
    ppermute x46 -> x49, starting transfers between devices: 75.3 us -> 63.2 us  [swap(): return lax.ppermute(x, axis, [(i, i ^ distance) for i in range(size)])]
    pallas_call x18, Pallas kernels: 28.6 us -> 25.8 us  [call(): pl.pallas_call(kernel, grid=(1,), out_shape=outs, in_specs=[spec(p, x) fo...]
    unnamed x73 -> x67, local copies, waits for them, and re-layouts: 9.62 us -> 8.68 us
  transfers between devices with their start and end apart: 47 -> 49, of which waited for: 19 -> 18; matrix products, arithmetic and copies ran while one was open for 1% -> 1% of each run, Pallas kernels for 31% -> 26%
where the time goes in v6:
time: 226 us; the launch traced here: 225 us
  waiting for transfers between devices  77.6 us (34%)
  Pallas kernels  72.5 us (32%)
  starting transfers between devices  63.2 us (28%)
  local copies, waits for them, and re-layouts  9.2 us (4%)
    ppermute x49, waiting for transfers between devices, swap(): return lax.ppermute(x, axis, [(i, i ^ distance) for i in range(size)])  77.6 us
    ppermute x49, starting transfers between devices, swap(): return lax.ppermute(x, axis, [(i, i ^ distance) for i in range(size)])  63.2 us
    pallas_call x18, Pallas kernels, call(): pl.pallas_call(kernel, grid=(1,), out_shape=outs, in_specs=[spec(p, x) fo...  25.8 us
    pallas_call x4, Pallas kernels, run_experts(): pl.pallas_call(kernel, grid=(total // step,), in_specs=[pl.BlockSpec(memo...  23.4 us
    pallas_call x1, Pallas kernels, both_copies(): pl.pallas_call(both_copies_kernel, grid=(local,), in_specs=[block(rows, h...  11.1 us
    pallas_call x1, Pallas kernels, run_grads(): pl.pallas_call(grads_kernel, grid=(local,), in_specs=whole(n) + cols(dgu,...  10.7 us
    unnamed x67, local copies, waits for them, and re-layouts  8.68 us
  transfers between devices with their start and end apart: 49, of which 18 were waited for; matrix products, arithmetic and copies ran while one was open for 1% of the time, Pallas kernels for 26%

profile of v6, /device:TPU:0, one launch (start us, length us, event | category | flops | bytes accessed | tf_op | source)
XLA Modules:
  0.0 224.8 jit_solution(10983240153318910546)
XLA Ops:
  0.6 2.2 pieces.1
  2.8 3.0 %collective-permute-start = (bf16[64,1152]{1,0:T(8,128)(2,1)}, bf16[64,1152]{1,0:T(8,128)(2,1)S(1)}, u32[]{:S(2)}, u32[]{:S(2)}) collective-permute-start(bf16[64,1152]{1,0:T(8,128)(2,1)} %get-tuple-element.168.own_ref.refs_0_.cot_ref), channel_id=1, source_target_pairs={{0,4},{4,0},{8,12},{12,8},{1,5},{5,1},{9,13},{13,9},{2,6},{6,2},{1... | collective-permute-start | bytes 442376 | tf_op jit(solution)/shard_map/ppermute | solution.py:41
  5.8 2.6 %collective-permute-start.4 = (bf16[64,1152]{1,0:T(8,128)(2,1)}, bf16[64,1152]{1,0:T(8,128)(2,1)S(1)}, u32[]{:S(2)}, u32[]{:S(2)}) collective-permute-start(bf16[64,1152]{1,0:T(8,128)(2,1)} %get-tuple-element.168.own_ref.refs_0_.cot_ref), channel_id=1, source_target_pairs={{0,8},{4,12},{8,0},{12,4},{1,9},{5,13},{9,1},{13,5},{2,10},{6,14},... | collective-permute-start | bytes 442376 | tf_op jit(solution)/shard_map/ppermute | solution.py:41
  8.4 3.5 %collective-permute-done.refs_0_ = bf16[64,1152]{1,0:T(8,128)(2,1)S(1)} collective-permute-done((bf16[64,1152]{1,0:T(8,128)(2,1)}, bf16[64,1152]{1,0:T(8,128)(2,1)S(1)}, u32[]{:S(2)}, u32[]{:S(2)}) %collective-permute-start) | collective-permute-done | bytes 147488 | tf_op jit(solution)/shard_map/ppermute | solution.py:41
  11.9 4.7 %attend.1 = (bf16[256,1024]{1,0:T(8,128)(2,1)}, bf16[256,256]{1,0:T(8,128)(2,1)}, bf16[256,128]{1,0:T(8,128)(2,1)}, bf16[256,128]{1,0:T(8,128)(2,1)}, bf16[256,2...) custom-call(s32[1]{0:T(128)} %bitcast.me_ref, ...), custom_call_target="tpu_custom_call" | custom-call | flops 53687091200 | tf_op jit(solution)/shard_map/attend/pallas_call | solution.py:118
  16.6 1.7 collective-permute-start.1
  18.3 1.5 collective-permute-start.2
  20.1 1.7 collective-permute-done.1.refs_0_
  21.7 1.7 collective-permute-done.2.refs_1_
  23.5 2.4 %collective-permute-done.3.refs_2_ = bf16[64,1024]{1,0:T(8,128)(2,1)S(1)} collective-permute-done((bf16[64,1024]{1,0:T(8,128)(2,1)}, bf16[64,1024]{1,0:T(8,128)(2,1)S(1)}, u32[]{:S(2)}, u32[]{:S(2)}) %collective-permute-start.3) | collective-permute-done | bytes 131104 | tf_op jit(solution)/shard_map/ppermute | solution.py:41
  29.5 3.5 %collective-permute-done.6.refs_1_ = bf16[64,1024]{1,0:T(8,128)(2,1)S(1)} collective-permute-done((bf16[64,1024]{1,0:T(8,128)(2,1)S(1)}, bf16[64,1024]{1,0:T(8,128)(2,1)S(1)}, u32[]{:S(2)}, u32[]{:S(2)}) %collective-permute-start.6) | collective-permute-done | bytes 131104 | tf_op jit(solution)/shard_map/ppermute | solution.py:41
  33.4 2.6 %collective-permute-start.7 = (bf16[64,1024]{1,0:T(8,128)(2,1)S(1)}, bf16[64,1024]{1,0:T(8,128)(2,1)S(1)}, u32[]{:S(2)}, u32[]{:S(2)}) collective-permute-start(bf16[64,1024]{1,0:T(8,128)(2,1)S(1)} %get-tuple-element.177.refs_0_.n_ref), channel_id=1, source_target_pairs={{0,8},{4,12},{8,0},{12,4},{1,9},{5,13},{9,1},{13,5},{2,10},{6,14},... | collective-permute-start | bytes 393224 | tf_op jit(solution)/shard_map/ppermute | solution.py:41
  36.0 1.5 collective-permute-start.8
  37.5 1.6 copy-done.1
  39.1 1.5 gate_up_weights.1.wcat
  40.6 2.9 %collective-permute-done.7.refs_2_ = bf16[64,1024]{1,0:T(8,128)(2,1)S(1)} collective-permute-done((bf16[64,1024]{1,0:T(8,128)(2,1)S(1)}, bf16[64,1024]{1,0:T(8,128)(2,1)S(1)}, u32[]{:S(2)}, u32[]{:S(2)}) %collective-permute-start.7) | collective-permute-done | bytes 131104 | tf_op jit(solution)/shard_map/ppermute | solution.py:41
  44.9 1.6 collective-permute-start.10
  46.5 4.9 %collective-permute-done.14.refs_7_.far_ref = bf16[3,64,1152]{2,1,0:T(8,128)(2,1)} collective-permute-done((bf16[3,64,1152]{2,1,0:T(8,128)(2,1)S(1)}, bf16[3,64,1152]{2,1,0:T(8,128)(2,1)}, u32[]{:S(2)}, u32[]{:S(2)}) %collective-permute-start.14) | collective-permute-done | bytes 442400 | tf_op jit(solution)/shard_map/ppermute | solution.py:41
  51.4 2.4 %counts.1 = f32[1,128]{1,0:T(1,128)S(1)} custom-call(bf16[64,1152]{1,0:T(8,128)(2,1)S(1)} %copy-done.6, bf16[64,1152]{1,0:T(8,128)(2,1)S(1)} %copy-done.19, bf16[64,1152]{1,0:T(8,128)(2,1)S(1)} %copy-done.18, bf16[64,1152]{1,0:T(8,128)(2,1)S(1)} %copy-done.17, bf16[3,64,1152]{2,1,0:T(8,128)(2,1)S(1)} %together.2.far_ref.refs_4_, ...), custom_call_target="tpu_custom_call" | custom-call | tf_op jit(solution)/shard_map/counts/pallas_call | solution.py:118
  53.8 4.5 %experts.4 = (bf16[256,1024]{1,0:T(8,128)(2,1)S(1)}, bf16[256,2048]{1,0:T(8,128)(2,1)S(1)}, bf16[256,1024]{1,0:T(8,128)(2,1)S(1)}, f32[4,64,1152]{2,1,0:T(8,128)S(1)}, f32[4,64,1024]{2,1,0:T(8,128)S(1)}) custom-call(s32[1]{0:T(128)} %bitcast.9.base_ref, bf16[4,64,1024]{2,1,0:T(8,128)(2,1)S(1)} %together.3.x_ref.a0, bf16[64,1152]{1,0:T(8,128)(2,1)S(1)} %copy-done.6, ...), custom_call_target="tpu_custom_call" | custom-call | flops 3355443200 | tf_op jit(solution)/shard_map/experts/pallas_call | solution.py:349
  60.6 6.2 %experts.5 = (bf16[256,1024]{1,0:T(8,128)(2,1)S(1)}, bf16[256,2048]{1,0:T(8,128)(2,1)S(1)}, bf16[256,1024]{1,0:T(8,128)(2,1)S(1)}, bf16[4,64,1152]{2,1,0:T(8,128)(2,1)}, bf16[4,64,1024]{2,1,0:T(8,128)(2,1)S(1)}) custom-call(s32[1]{0:T(128)} %bitcast.9.base_ref, bf16[4,64,1024]{2,1,0:T(8,128)(2,1)S(1)} %collective-permute-done.9.x_ref.a1, ...), custom_call_target="tpu_custom_call" | custom-call | flops 3355443200 | tf_op jit(solution)/shard_map/experts/pallas_call | solution.py:349
  66.8 1.4 collective-permute-start.16
  68.3 6.5 %experts.6 = (bf16[256,1024]{1,0:T(8,128)(2,1)S(1)}, bf16[256,2048]{1,0:T(8,128)(2,1)S(1)}, bf16[256,1024]{1,0:T(8,128)(2,1)S(1)}, bf16[4,64,1152]{2,1,0:T(8,128)(2,1)}, bf16[4,64,1024]{2,1,0:T(8,128)(2,1)S(1)}) custom-call(s32[1]{0:T(128)} %bitcast.9.base_ref, bf16[4,64,1024]{2,1,0:T(8,128)(2,1)S(1)} %collective-permute-done.10.x_ref.a2, ...), custom_call_target="tpu_custom_call" | custom-call | flops 3355443200 | tf_op jit(solution)/shard_map/experts/pallas_call | solution.py:349
  75.5 6.2 %experts.7 = (bf16[256,1024]{1,0:T(8,128)(2,1)S(1)}, bf16[256,2048]{1,0:T(8,128)(2,1)S(1)}, bf16[256,1024]{1,0:T(8,128)(2,1)S(1)}, f32[64,1152]{1,0:T(8,128)S(1)...) custom-call(s32[1]{0:T(128)} %bitcast.9.base_ref, ...), custom_call_target="tpu_custom_call" | custom-call | flops 3355443200 | tf_op jit(solution)/shard_map/experts/pallas_call | solution.py:349
  81.7 4.3 %collective-permute-start.19 = (bf16[64,1152]{1,0:T(8,128)(2,1)}, bf16[64,1152]{1,0:T(8,128)(2,1)}, u32[]{:S(2)}, u32[]{:S(2)}) collective-permute-start(bf16[64,1152]{1,0:T(8,128)(2,1)} %get-tuple-element.223), channel_id=1, source_target_pairs={{0,8},{4,12},{8,0},{12,4},{1,9},{5,13},{9,1},{13,5},{2,10},{6,14},... | collective-permute-start | bytes 442376 | tf_op jit(solution)/shard_map/ppermute | solution.py:41
  86.2 10.7 %expert_grads.1.mine_ref = bf16[8,3072,128]{2,1,0:T(8,128)(2,1)} custom-call(bf16[256,1024]{1,0:T(8,128)(2,1)S(1)} %bitcast.20, bf16[256,1024]{1,0:T(8,128)(2,1)S(1)} %bitcast.21, bf16[256,1024]{1,0:T(8,128)(2,1)S(1)} %bitcast.22, bf16[256,1024]{1,0:T(8,128)(2,1)S(1)} %bitcast.23, bf16[256,2048]{1,0:T(8,128)(2,1)S(1)} %get-tuple-element.189.refs_4_, ...), custom_call_target="tpu_custom_call" | custom-call | flops 644245094400 | tf_op jit(solution)/shard_map/expert_grads/pallas_call | solution.py:422
  97.4 1.4 dn_sum.1
  100.4 1.9 collective-permute-start.23
  104.6 2.4 %collective-permute-start.25 = (bf16[64,1152]{1,0:T(8,128)(2,1)S(1)}, bf16[64,1152]{1,0:T(8,128)(2,1)S(1)}, u32[]{:S(2)}, u32[]{:S(2)}) collective-permute-start(bf16[64,1152]{1,0:T(8,128)(2,1)S(1)} %get-tuple-element.243), channel_id=1, source_target_pairs={{0,4},{4,0},{8,12},{12,8},{1,5},{5,1},{9,13},{13,9},{2,6},{6,2},{1... | collective-permute-start | bytes 442376 | tf_op jit(solution)/shard_map/ppermute | solution.py:41
  107.0 20.1 %collective-permute-done.24.refs_1_ = bf16[64,1152]{1,0:T(8,128)(2,1)S(1)} collective-permute-done((bf16[64,1152]{1,0:T(8,128)(2,1)S(1)}, bf16[64,1152]{1,0:T(8,128)(2,1)S(1)}, u32[]{:S(2)}, u32[]{:S(2)}) %collective-permute-start.24) | collective-permute-done | bytes 147488 | tf_op jit(solution)/shard_map/ppermute | solution.py:41
  127.1 4.9 %collective-permute-start.26 = (bf16[64,1152]{1,0:T(8,128)(2,1)S(1)}, bf16[64,1152]{1,0:T(8,128)(2,1)S(1)}, u32[]{:S(2)}, u32[]{:S(2)}) collective-permute-start(bf16[64,1152]{1,0:T(8,128)(2,1)S(1)} %get-tuple-element.244), channel_id=1, source_target_pairs={{0,8},{4,12},{8,0},{12,4},{1,9},{5,13},{9,1},{13,5},{2,10},{6,14},... | collective-permute-start | bytes 442376 | tf_op jit(solution)/shard_map/ppermute | solution.py:41
  132.4 9.3 %collective-permute-done.26.refs_3_ = bf16[64,1152]{1,0:T(8,128)(2,1)S(1)} collective-permute-done((bf16[64,1152]{1,0:T(8,128)(2,1)S(1)}, bf16[64,1152]{1,0:T(8,128)(2,1)S(1)}, u32[]{:S(2)}, u32[]{:S(2)}) %collective-permute-start.26) | collective-permute-done | bytes 147488 | tf_op jit(solution)/shard_map/ppermute | solution.py:41
  143.3 3.0 %collective-permute-start.31 = (bf16[64,1152]{1,0:T(8,128)(2,1)S(1)}, bf16[64,1152]{1,0:T(8,128)(2,1)S(1)}, u32[]{:S(2)}, u32[]{:S(2)}) collective-permute-start(bf16[64,1152]{1,0:T(8,128)(2,1)S(1)} %get-tuple-element.269.w0), channel_id=1, source_target_pairs={{0,3},{1,2},{2,1},{3,0},{4,7},{5,6},{6,5},{7,4},{8,11},{9,10},{10,... | collective-permute-start | bytes 442376 | tf_op jit(solution)/shard_map/ppermute | solution.py:41
  149.4 2.9 %collective-permute-done.30.w2 = bf16[64,1152]{1,0:T(8,128)(2,1)S(1)} collective-permute-done((bf16[64,1152]{1,0:T(8,128)(2,1)S(1)}, bf16[64,1152]{1,0:T(8,128)(2,1)S(1)}, u32[]{:S(2)}, u32[]{:S(2)}) %collective-permute-start.30) | collective-permute-done | bytes 147488 | tf_op jit(solution)/shard_map/ppermute | solution.py:41
  153.2 5.5 %attend_back.1 = (bf16[256,1152]{1,0:T(8,128)(2,1)}, bf16[256,512]{1,0:T(8,128)(2,1)}, f32[8,1024]{1,0:T(8,128)}, f32[64,1024]{1,0:T(8,128)}, bf16[64,1024]{1,0:...) custom-call(s32[1]{0:T(128)} %bitcast.me_ref, bf16[64,1152]{1,0:T(8,128)(2,1)} %copy-done.25, ...), custom_call_target="tpu_custom_call" | custom-call | flops 53687091200 | tf_op jit(solution)/shard_map/attend_back/pallas_call | solution.py:118
  158.7 4.1 %dense.1 = (f32[512,896]{1,0:T(8,128)}, bf16[512,896]{1,0:T(8,128)(2,1)}) custom-call(s32[2]{0:T(128)} %pad_add_fusion.me_ref, bf16[4,64,1024]{2,1,0:T(8,128)(2,1)} %copy-done.2, bf16[4,64,1024]{2,1,0:T(8,128)(2,1)} %copy-done.10, bf16[4,64,1024]{2,1,0:T(8,128)(2,1)} %copy-done.11, bf16[4,64,1024]{2,1,0:T(8,128)(2,1)} %copy-done.12, ...), custom_call_target="tpu_custom_call" | custom-call | flops 100 | tf_op jit(solution)/shard_map/dense/pallas_call | solution.py:118
  163.3 2.2 collective-permute-done.33.small_got_ref
  165.5 1.5 copy-done.3
  168.1 3.5 %collective-permute-start.34 = (bf16[128,896]{1,0:T(8,128)(2,1)S(1)}, bf16[128,896]{1,0:T(8,128)(2,1)S(1)}, u32[]{:S(2)}, u32[]{:S(2)}) collective-permute-start(bf16[128,896]{1,0:T(8,128)(2,1)S(1)} %get-tuple-element.285), channel_id=1, source_target_pairs={{0,4},{4,0},{8,12},{12,8},{1,5},{5,1},{9,13},{13,9},{2,6},{6,2},{1... | collective-permute-start | bytes 688136 | tf_op jit(solution)/shard_map/ppermute | solution.py:41
  173.2 1.9 collective-permute-start.37
  175.1 2.3 %collective-permute-done.35.refs_1_ = bf16[64,1024]{1,0:T(8,128)(2,1)S(1)} collective-permute-done((bf16[64,1024]{1,0:T(8,128)(2,1)S(1)}, bf16[64,1024]{1,0:T(8,128)(2,1)S(1)}, u32[]{:S(2)}, u32[]{:S(2)}) %collective-permute-start.35) | collective-permute-done | bytes 131104 | tf_op jit(solution)/shard_map/ppermute | solution.py:41
  178.0 2.7 %collective-permute-done.36.refs_2_ = bf16[64,1024]{1,0:T(8,128)(2,1)S(1)} collective-permute-done((bf16[64,1024]{1,0:T(8,128)(2,1)S(1)}, bf16[64,1024]{1,0:T(8,128)(2,1)S(1)}, u32[]{:S(2)}, u32[]{:S(2)}) %collective-permute-start.36) | collective-permute-done | bytes 131104 | tf_op jit(solution)/shard_map/ppermute | solution.py:41
  183.1 9.7 %collective-permute-done.41.refs_1_ = bf16[128,896]{1,0:T(8,128)(2,1)S(1)} collective-permute-done((bf16[128,896]{1,0:T(8,128)(2,1)S(1)}, bf16[128,896]{1,0:T(8,128)(2,1)S(1)}, u32[]{:S(2)}, u32[]{:S(2)}) %collective-permute-start.41) | collective-permute-done | bytes 229408 | tf_op jit(solution)/shard_map/ppermute | solution.py:41
  193.7 3.3 %collective-permute-start.44 = (bf16[64,1024]{1,0:T(8,128)(2,1)S(1)}, bf16[64,1024]{1,0:T(8,128)(2,1)S(1)}, u32[]{:S(2)}, u32[]{:S(2)}) collective-permute-start(bf16[64,1024]{1,0:T(8,128)(2,1)S(1)} %get-tuple-element.303), channel_id=1, source_target_pairs={{0,8},{4,12},{8,0},{12,4},{1,9},{5,13},{9,1},{13,5},{2,10},{6,14},... | collective-permute-start | bytes 393224 | tf_op jit(solution)/shard_map/ppermute | solution.py:41
  197.0 3.2 %collective-permute-start.45 = (bf16[64,1024]{1,0:T(8,128)(2,1)S(1)}, bf16[64,1024]{1,0:T(8,128)(2,1)S(1)}, u32[]{:S(2)}, u32[]{:S(2)}) collective-permute-start(bf16[64,1024]{1,0:T(8,128)(2,1)S(1)} %get-tuple-element.304), channel_id=1, source_target_pairs={{0,12},{4,8},{8,4},{12,0},{1,13},{5,9},{9,5},{13,1},{2,14},{6,10},... | collective-permute-start | bytes 393224 | tf_op jit(solution)/shard_map/ppermute | solution.py:41
  201.0 5.3 %collective-permute-done.44.refs_2_ = bf16[64,1024]{1,0:T(8,128)(2,1)S(1)} collective-permute-done((bf16[64,1024]{1,0:T(8,128)(2,1)S(1)}, bf16[64,1024]{1,0:T(8,128)(2,1)S(1)}, u32[]{:S(2)}, u32[]{:S(2)}) %collective-permute-start.44) | collective-permute-done | bytes 131104 | tf_op jit(solution)/shard_map/ppermute | solution.py:41
  206.4 1.4 collective-permute-start.46
  210.0 11.1 %both_copies.1 = (f32[8,1024,128]{2,1,0:T(8,128)}, f32[8,1024,128]{2,1,0:T(8,128)}, f32[8,128,1024]{2,1,0:T(8,128)}) custom-call(bf16[8,3072,128]{2,1,0:T(8,128)(2,1)} %expert_grads.1.mine_ref, bf16[8,3072,128]{2,1,0:T(8,128)(2,1)} %collective-permute-done.28.other_ref), custom_call_target="tpu_custom_call" | custom-call | bytes 25165824 | tf_op jit(solution)/shard_map/both_copies/pallas_call | solution.py:451
  (146 shorter events, 33.0 us)
Async XLA Ops:
  2.8 9.1 %collective-permute-start = (bf16[64,1152]{1,0:T(8,128)(2,1)}, bf16[64,1152]{1,0:T(8,128)(2,1)S(1)}, u32[]{:S(2)}, u32[]{:S(2)}) collective-permute-start(bf16[64,1152]{1,0:T(8,128)(2,1)} %get-tuple-element.168.own_ref.refs_0_.cot_ref), channel_id=1, source_target_pairs={{0,4},{4,0},{8,12},{12,8},{1,5},{5,1},{9,13},{13,9},{2,6},{6,2},{1... | collective-permute-start | bytes 442376 | tf_op jit(solution)/shard_map/ppermute | solution.py:41
  5.8 22.1 %collective-permute-start.4 = (bf16[64,1152]{1,0:T(8,128)(2,1)}, bf16[64,1152]{1,0:T(8,128)(2,1)S(1)}, u32[]{:S(2)}, u32[]{:S(2)}) collective-permute-start(bf16[64,1152]{1,0:T(8,128)(2,1)} %get-tuple-element.168.own_ref.refs_0_.cot_ref), channel_id=1, source_target_pairs={{0,8},{4,12},{8,0},{12,4},{1,9},{5,13},{9,1},{13,5},{2,10},{6,14},... | collective-permute-start | bytes 442376 | tf_op jit(solution)/shard_map/ppermute | solution.py:41
  8.4 19.5 %collective-permute-start.5 = (bf16[64,1152]{1,0:T(8,128)(2,1)}, bf16[64,1152]{1,0:T(8,128)(2,1)S(1)}, u32[]{:S(2)}, u32[]{:S(2)}) collective-permute-start(bf16[64,1152]{1,0:T(8,128)(2,1)} %get-tuple-element.168.own_ref.refs_0_.cot_ref), channel_id=1, source_target_pairs={{0,12},{4,8},{8,4},{12,0},{1,13},{5,9},{9,5},{13,1},{2,14},{6,10},... | collective-permute-start | bytes 442376 | tf_op jit(solution)/shard_map/ppermute | solution.py:41
  16.6 5.2 %collective-permute-start.1 = (bf16[64,1024]{1,0:T(8,128)(2,1)}, bf16[64,1024]{1,0:T(8,128)(2,1)S(1)}, u32[]{:S(2)}, u32[]{:S(2)}) collective-permute-start(bf16[64,1024]{1,0:T(8,128)(2,1)} %get-tuple-element.172), channel_id=1, source_target_pairs={{0,1},{1,0},{2,3},{3,2},{4,5},{5,4},{6,7},{7,6},{8,9},{9,8},{10,11... | collective-permute-start | bytes 393224 | tf_op jit(solution)/shard_map/ppermute | solution.py:41
  18.3 5.2 %collective-permute-start.2 = (bf16[64,1024]{1,0:T(8,128)(2,1)}, bf16[64,1024]{1,0:T(8,128)(2,1)S(1)}, u32[]{:S(2)}, u32[]{:S(2)}) collective-permute-start(bf16[64,1024]{1,0:T(8,128)(2,1)} %get-tuple-element.173), channel_id=1, source_target_pairs={{0,2},{1,3},{2,0},{3,1},{4,6},{5,7},{6,4},{7,5},{8,10},{9,11},{10,... | collective-permute-start | bytes 393224 | tf_op jit(solution)/shard_map/ppermute | solution.py:41
  19.8 6.1 %collective-permute-start.3 = (bf16[64,1024]{1,0:T(8,128)(2,1)}, bf16[64,1024]{1,0:T(8,128)(2,1)S(1)}, u32[]{:S(2)}, u32[]{:S(2)}) collective-permute-start(bf16[64,1024]{1,0:T(8,128)(2,1)} %get-tuple-element.174), channel_id=1, source_target_pairs={{0,3},{1,2},{2,1},{3,0},{4,7},{5,6},{6,5},{7,4},{8,11},{9,10},{10,... | collective-permute-start | bytes 393224 | tf_op jit(solution)/shard_map/ppermute | solution.py:41
  27.9 5.0 %collective-permute-start.6 = (bf16[64,1024]{1,0:T(8,128)(2,1)S(1)}, bf16[64,1024]{1,0:T(8,128)(2,1)S(1)}, u32[]{:S(2)}, u32[]{:S(2)}) collective-permute-start(bf16[64,1024]{1,0:T(8,128)(2,1)S(1)} %get-tuple-element.177.refs_0_.n_ref), channel_id=1, source_target_pairs={{0,4},{4,0},{8,12},{12,8},{1,5},{5,1},{9,13},{13,9},{2,6},{6,2},{1... | collective-permute-start | bytes 393224 | tf_op jit(solution)/shard_map/ppermute | solution.py:41
  28.4 18.1 %collective-permute-start.11 = (bf16[3,64,1152]{2,1,0:T(8,128)(2,1)S(1)}, bf16[3,64,1152]{2,1,0:T(8,128)(2,1)}, u32[]{:S(2)}, u32[]{:S(2)}) collective-permute-start(bf16[3,64,1152]{2,1,0:T(8,128)(2,1)S(1)} %together.2.far_ref.refs_4_), channel_id=1, source_target_pairs={{0,1},{1,0},{2,3},{3,2},{4,5},{5,4},{6,7},{7,6},{8,9},{9,8},{10,11... | collective-permute-start | bytes 1327112 | tf_op jit(solution)/shard_map/ppermute | solution.py:41
  29.0 17.5 %collective-permute-start.12 = (bf16[3,64,1152]{2,1,0:T(8,128)(2,1)S(1)}, bf16[3,64,1152]{2,1,0:T(8,128)(2,1)}, u32[]{:S(2)}, u32[]{:S(2)}) collective-permute-start(bf16[3,64,1152]{2,1,0:T(8,128)(2,1)S(1)} %together.2.far_ref.refs_4_), channel_id=1, source_target_pairs={{0,2},{1,3},{2,0},{3,1},{4,6},{5,7},{6,4},{7,5},{8,10},{9,11},{10,... | collective-permute-start | bytes 1327112 | tf_op jit(solution)/shard_map/ppermute | solution.py:41
  33.0 18.4 %collective-permute-start.14 = (bf16[3,64,1152]{2,1,0:T(8,128)(2,1)S(1)}, bf16[3,64,1152]{2,1,0:T(8,128)(2,1)}, u32[]{:S(2)}, u32[]{:S(2)}) collective-permute-start(bf16[3,64,1152]{2,1,0:T(8,128)(2,1)S(1)} %together.2.far_ref.refs_4_), channel_id=1, source_target_pairs={{0,3},{1,2},{2,1},{3,0},{4,7},{5,6},{6,5},{7,4},{8,11},{9,10},{10,... | collective-permute-start | bytes 1327112 | tf_op jit(solution)/shard_map/ppermute | solution.py:41
  33.4 10.1 %collective-permute-start.7 = (bf16[64,1024]{1,0:T(8,128)(2,1)S(1)}, bf16[64,1024]{1,0:T(8,128)(2,1)S(1)}, u32[]{:S(2)}, u32[]{:S(2)}) collective-permute-start(bf16[64,1024]{1,0:T(8,128)(2,1)S(1)} %get-tuple-element.177.refs_0_.n_ref), channel_id=1, source_target_pairs={{0,8},{4,12},{8,0},{12,4},{1,9},{5,13},{9,1},{13,5},{2,10},{6,14},... | collective-permute-start | bytes 393224 | tf_op jit(solution)/shard_map/ppermute | solution.py:41
  36.0 7.5 %collective-permute-start.8 = (bf16[64,1024]{1,0:T(8,128)(2,1)S(1)}, bf16[64,1024]{1,0:T(8,128)(2,1)S(1)}, u32[]{:S(2)}, u32[]{:S(2)}) collective-permute-start(bf16[64,1024]{1,0:T(8,128)(2,1)S(1)} %get-tuple-element.177.refs_0_.n_ref), channel_id=1, source_target_pairs={{0,12},{4,8},{8,4},{12,0},{1,13},{5,9},{9,5},{13,1},{2,14},{6,10},... | collective-permute-start | bytes 393224 | tf_op jit(solution)/shard_map/ppermute | solution.py:41
  43.6 16.9 %collective-permute-start.9 = (bf16[4,64,1024]{2,1,0:T(8,128)(2,1)S(1)}, bf16[4,64,1024]{2,1,0:T(8,128)(2,1)S(1)}, u32[]{:S(2)}, u32[]{:S(2)}) collective-permute-start(bf16[4,64,1024]{2,1,0:T(8,128)(2,1)S(1)} %together.3.x_ref.a0), channel_id=1, source_target_pairs={{0,1},{1,0},{2,3},{3,2},{4,5},{5,4},{6,7},{7,6},{8,9},{9,8},{10,11... | collective-permute-start | bytes 1572872 | tf_op jit(solution)/shard_map/ppermute | solution.py:41
  44.9 23.4 %collective-permute-start.10 = (bf16[4,64,1024]{2,1,0:T(8,128)(2,1)S(1)}, bf16[4,64,1024]{2,1,0:T(8,128)(2,1)S(1)}, u32[]{:S(2)}, u32[]{:S(2)}) collective-permute-start(bf16[4,64,1024]{2,1,0:T(8,128)(2,1)S(1)} %together.3.x_ref.a0), channel_id=1, source_target_pairs={{0,2},{1,3},{2,0},{3,1},{4,6},{5,7},{6,4},{7,5},{8,10},{9,11},{10,... | collective-permute-start | bytes 1572872 | tf_op jit(solution)/shard_map/ppermute | solution.py:41
  53.7 6.8 %collective-permute-start.15 = (f32[1,128]{1,0:T(1,128)S(1)}, f32[1,128]{1,0:T(1,128)S(1)}, u32[]{:S(2)}, u32[]{:S(2)}) collective-permute-start(f32[1,128]{1,0:T(1,128)S(1)} %counts.1), channel_id=1, source_target_pairs={{0,16},{16,0},{1,17},{17,1},{2,18},{18,2},{3,19},{19,3},{4,20},{20... | collective-permute-start | bytes 1544 | tf_op jit(solution)/shard_map/ppermute | solution.py:41
  59.3 16.2 %collective-permute-start.13 = (bf16[4,64,1024]{2,1,0:T(8,128)(2,1)S(1)}, bf16[4,64,1024]{2,1,0:T(8,128)(2,1)S(1)}, u32[]{:S(2)}, u32[]{:S(2)}) collective-permute-start(bf16[4,64,1024]{2,1,0:T(8,128)(2,1)S(1)} %together.3.x_ref.a0), channel_id=1, source_target_pairs={{0,3},{1,2},{2,1},{3,0},{4,7},{5,6},{6,5},{7,4},{8,11},{9,10},{10,... | collective-permute-start | bytes 1572872 | tf_op jit(solution)/shard_map/ppermute | solution.py:41
  66.8 30.6 %collective-permute-start.16 = (bf16[4,64,1152]{2,1,0:T(8,128)(2,1)}, bf16[4,64,1152]{2,1,0:T(8,128)(2,1)}, u32[]{:S(2)}, u32[]{:S(2)}) collective-permute-start(bf16[4,64,1152]{2,1,0:T(8,128)(2,1)} %get-tuple-element.196), channel_id=1, source_target_pairs={{0,1},{1,0},{2,3},{3,2},{4,5},{5,4},{6,7},{7,6},{8,9},{9,8},{10,11... | collective-permute-start | bytes 1769480 | tf_op jit(solution)/shard_map/ppermute | solution.py:41
  74.7 22.6 %collective-permute-start.17 = (bf16[4,64,1152]{2,1,0:T(8,128)(2,1)}, bf16[4,64,1152]{2,1,0:T(8,128)(2,1)}, u32[]{:S(2)}, u32[]{:S(2)}) collective-permute-start(bf16[4,64,1152]{2,1,0:T(8,128)(2,1)} %get-tuple-element.205), channel_id=1, source_target_pairs={{0,2},{1,3},{2,0},{3,1},{4,6},{5,7},{6,4},{7,5},{8,10},{9,11},{10,... | collective-permute-start | bytes 1769480 | tf_op jit(solution)/shard_map/ppermute | solution.py:41
  81.7 15.2 %collective-permute-start.18 = (bf16[64,1152]{1,0:T(8,128)(2,1)}, bf16[64,1152]{1,0:T(8,128)(2,1)}, u32[]{:S(2)}, u32[]{:S(2)}) collective-permute-start(bf16[64,1152]{1,0:T(8,128)(2,1)} %get-tuple-element.222), channel_id=1, source_target_pairs={{0,4},{4,0},{8,12},{12,8},{1,5},{5,1},{9,13},{13,9},{2,6},{6,2},{1... | collective-permute-start | bytes 442376 | tf_op jit(solution)/shard_map/ppermute | solution.py:41
  81.7 15.6 %collective-permute-start.19 = (bf16[64,1152]{1,0:T(8,128)(2,1)}, bf16[64,1152]{1,0:T(8,128)(2,1)}, u32[]{:S(2)}, u32[]{:S(2)}) collective-permute-start(bf16[64,1152]{1,0:T(8,128)(2,1)} %get-tuple-element.223), channel_id=1, source_target_pairs={{0,8},{4,12},{8,0},{12,4},{1,9},{5,13},{9,1},{13,5},{2,10},{6,14},... | collective-permute-start | bytes 442376 | tf_op jit(solution)/shard_map/ppermute | solution.py:41
  86.0 11.4 %collective-permute-start.20 = (bf16[64,1152]{1,0:T(8,128)(2,1)}, bf16[64,1152]{1,0:T(8,128)(2,1)}, u32[]{:S(2)}, u32[]{:S(2)}) collective-permute-start(bf16[64,1152]{1,0:T(8,128)(2,1)} %get-tuple-element.224), channel_id=1, source_target_pairs={{0,12},{4,8},{8,4},{12,0},{1,13},{5,9},{9,5},{13,1},{2,14},{6,10},... | collective-permute-start | bytes 442376 | tf_op jit(solution)/shard_map/ppermute | solution.py:41
  98.8 42.9 %collective-permute-start.21 = (bf16[4,64,1024]{2,1,0:T(8,128)(2,1)S(1)}, bf16[4,64,1024]{2,1,0:T(8,128)(2,1)S(1)}, u32[]{:S(2)}, u32[]{:S(2)}) collective-permute-start(bf16[4,64,1024]{2,1,0:T(8,128)(2,1)S(1)} %get-tuple-element.235), channel_id=1, source_target_pairs={{0,1},{1,0},{2,3},{3,2},{4,5},{5,4},{6,7},{7,6},{8,9},{9,8},{10,11... | collective-permute-start | bytes 1572872 | tf_op jit(solution)/shard_map/ppermute | solution.py:41
  99.1 42.6 %collective-permute-start.22 = (bf16[4,64,1024]{2,1,0:T(8,128)(2,1)S(1)}, bf16[4,64,1024]{2,1,0:T(8,128)(2,1)S(1)}, u32[]{:S(2)}, u32[]{:S(2)}) collective-permute-start(bf16[4,64,1024]{2,1,0:T(8,128)(2,1)S(1)} %get-tuple-element.236), channel_id=1, source_target_pairs={{0,2},{1,3},{2,0},{3,1},{4,6},{5,7},{6,4},{7,5},{8,10},{9,11},{10,... | collective-permute-start | bytes 1572872 | tf_op jit(solution)/shard_map/ppermute | solution.py:41
  100.4 41.3 %collective-permute-start.23 = (bf16[4,64,1024]{2,1,0:T(8,128)(2,1)S(1)}, bf16[4,64,1024]{2,1,0:T(8,128)(2,1)S(1)}, u32[]{:S(2)}, u32[]{:S(2)}) collective-permute-start(bf16[4,64,1024]{2,1,0:T(8,128)(2,1)S(1)} %get-tuple-element.237), channel_id=1, source_target_pairs={{0,3},{1,2},{2,1},{3,0},{4,7},{5,6},{6,5},{7,4},{8,11},{9,10},{10,... | collective-permute-start | bytes 1572872 | tf_op jit(solution)/shard_map/ppermute | solution.py:41
  103.5 23.6 %collective-permute-start.24 = (bf16[64,1152]{1,0:T(8,128)(2,1)S(1)}, bf16[64,1152]{1,0:T(8,128)(2,1)S(1)}, u32[]{:S(2)}, u32[]{:S(2)}) collective-permute-start(bf16[64,1152]{1,0:T(8,128)(2,1)S(1)} %through.1), channel_id=1, source_target_pairs={{0,3},{1,2},{2,1},{3,0},{4,7},{5,6},{6,5},{7,4},{8,11},{9,10},{10,... | collective-permute-start | bytes 442376 | tf_op jit(solution)/shard_map/ppermute | solution.py:41
  104.6 27.4 %collective-permute-start.25 = (bf16[64,1152]{1,0:T(8,128)(2,1)S(1)}, bf16[64,1152]{1,0:T(8,128)(2,1)S(1)}, u32[]{:S(2)}, u32[]{:S(2)}) collective-permute-start(bf16[64,1152]{1,0:T(8,128)(2,1)S(1)} %get-tuple-element.243), channel_id=1, source_target_pairs={{0,4},{4,0},{8,12},{12,8},{1,5},{5,1},{9,13},{13,9},{2,6},{6,2},{1... | collective-permute-start | bytes 442376 | tf_op jit(solution)/shard_map/ppermute | solution.py:41
  127.1 14.6 %collective-permute-start.26 = (bf16[64,1152]{1,0:T(8,128)(2,1)S(1)}, bf16[64,1152]{1,0:T(8,128)(2,1)S(1)}, u32[]{:S(2)}, u32[]{:S(2)}) collective-permute-start(bf16[64,1152]{1,0:T(8,128)(2,1)S(1)} %get-tuple-element.244), channel_id=1, source_target_pairs={{0,8},{4,12},{8,0},{12,4},{1,9},{5,13},{9,1},{13,5},{2,10},{6,14},... | collective-permute-start | bytes 442376 | tf_op jit(solution)/shard_map/ppermute | solution.py:41
  132.0 9.8 %collective-permute-start.27 = (bf16[64,1152]{1,0:T(8,128)(2,1)S(1)}, bf16[64,1152]{1,0:T(8,128)(2,1)S(1)}, u32[]{:S(2)}, u32[]{:S(2)}) collective-permute-start(bf16[64,1152]{1,0:T(8,128)(2,1)S(1)} %get-tuple-element.245), channel_id=1, source_target_pairs={{0,12},{4,8},{8,4},{12,0},{1,13},{5,9},{9,5},{13,1},{2,14},{6,10},... | collective-permute-start | bytes 442376 | tf_op jit(solution)/shard_map/ppermute | solution.py:41
  142.6 10.6 %collective-permute-start.28 = (bf16[8,3072,128]{2,1,0:T(8,128)(2,1)}, bf16[8,3072,128]{2,1,0:T(8,128)(2,1)}, u32[]{:S(2)}, u32[]{:S(2)}) collective-permute-start(bf16[8,3072,128]{2,1,0:T(8,128)(2,1)} %expert_grads.1.mine_ref), channel_id=1, source_target_pairs={{0,16},{16,0},{1,17},{17,1},{2,18},{18,2},{3,19},{19,3},{4,20},{20... | collective-permute-start | bytes 18874376 | tf_op jit(solution)/shard_map/ppermute | solution.py:41
  142.7 6.7 %collective-permute-start.29 = (bf16[64,1152]{1,0:T(8,128)(2,1)S(1)}, bf16[64,1152]{1,0:T(8,128)(2,1)S(1)}, u32[]{:S(2)}, u32[]{:S(2)}) collective-permute-start(bf16[64,1152]{1,0:T(8,128)(2,1)S(1)} %get-tuple-element.269.w0), channel_id=1, source_target_pairs={{0,1},{1,0},{2,3},{3,2},{4,5},{5,4},{6,7},{7,6},{8,9},{9,8},{10,11... | collective-permute-start | bytes 442376 | tf_op jit(solution)/shard_map/ppermute | solution.py:41
  143.2 9.1 %collective-permute-start.30 = (bf16[64,1152]{1,0:T(8,128)(2,1)S(1)}, bf16[64,1152]{1,0:T(8,128)(2,1)S(1)}, u32[]{:S(2)}, u32[]{:S(2)}) collective-permute-start(bf16[64,1152]{1,0:T(8,128)(2,1)S(1)} %get-tuple-element.269.w0), channel_id=1, source_target_pairs={{0,2},{1,3},{2,0},{3,1},{4,6},{5,7},{6,4},{7,5},{8,10},{9,11},{10,... | collective-permute-start | bytes 442376 | tf_op jit(solution)/shard_map/ppermute | solution.py:41
  143.3 9.0 %collective-permute-start.31 = (bf16[64,1152]{1,0:T(8,128)(2,1)S(1)}, bf16[64,1152]{1,0:T(8,128)(2,1)S(1)}, u32[]{:S(2)}, u32[]{:S(2)}) collective-permute-start(bf16[64,1152]{1,0:T(8,128)(2,1)S(1)} %get-tuple-element.269.w0), channel_id=1, source_target_pairs={{0,3},{1,2},{2,1},{3,0},{4,7},{5,6},{6,5},{7,4},{8,11},{9,10},{10,... | collective-permute-start | bytes 442376 | tf_op jit(solution)/shard_map/ppermute | solution.py:41
  162.8 2.7 %collective-permute-start.32 = (bf16[512,896]{1,0:T(8,128)(2,1)}, bf16[512,896]{1,0:T(8,128)(2,1)S(1)}, u32[]{:S(2)}, u32[]{:S(2)}) collective-permute-start(bf16[512,896]{1,0:T(8,128)(2,1)} %get-tuple-element.283), channel_id=1, source_target_pairs={{0,16},{16,0},{1,17},{17,1},{2,18},{18,2},{3,19},{19,3},{4,20},{20... | collective-permute-start | bytes 2752520 | tf_op jit(solution)/shard_map/ppermute | solution.py:41
  168.1 12.7 %collective-permute-start.34 = (bf16[128,896]{1,0:T(8,128)(2,1)S(1)}, bf16[128,896]{1,0:T(8,128)(2,1)S(1)}, u32[]{:S(2)}, u32[]{:S(2)}) collective-permute-start(bf16[128,896]{1,0:T(8,128)(2,1)S(1)} %get-tuple-element.285), channel_id=1, source_target_pairs={{0,4},{4,0},{8,12},{12,8},{1,5},{5,1},{9,13},{13,9},{2,6},{6,2},{1... | collective-permute-start | bytes 688136 | tf_op jit(solution)/shard_map/ppermute | solution.py:41
  171.6 5.8 %collective-permute-start.35 = (bf16[64,1024]{1,0:T(8,128)(2,1)S(1)}, bf16[64,1024]{1,0:T(8,128)(2,1)S(1)}, u32[]{:S(2)}, u32[]{:S(2)}) collective-permute-start(bf16[64,1024]{1,0:T(8,128)(2,1)S(1)} %copy-done.32), channel_id=1, source_target_pairs={{0,1},{1,0},{2,3},{3,2},{4,5},{5,4},{6,7},{7,6},{8,9},{9,8},{10,11... | collective-permute-start | bytes 393224 | tf_op jit(solution)/shard_map/ppermute | solution.py:41
  172.9 7.8 %collective-permute-start.36 = (bf16[64,1024]{1,0:T(8,128)(2,1)S(1)}, bf16[64,1024]{1,0:T(8,128)(2,1)S(1)}, u32[]{:S(2)}, u32[]{:S(2)}) collective-permute-start(bf16[64,1024]{1,0:T(8,128)(2,1)S(1)} %copy-done.31), channel_id=1, source_target_pairs={{0,2},{1,3},{2,0},{3,1},{4,6},{5,7},{6,4},{7,5},{8,10},{9,11},{10,... | collective-permute-start | bytes 393224 | tf_op jit(solution)/shard_map/ppermute | solution.py:41
  173.2 7.5 %collective-permute-start.37 = (bf16[64,1024]{1,0:T(8,128)(2,1)S(1)}, bf16[64,1024]{1,0:T(8,128)(2,1)S(1)}, u32[]{:S(2)}, u32[]{:S(2)}) collective-permute-start(bf16[64,1024]{1,0:T(8,128)(2,1)S(1)} %copy-done.30), channel_id=1, source_target_pairs={{0,3},{1,2},{2,1},{3,0},{4,7},{5,6},{6,5},{7,4},{8,11},{9,10},{10,... | collective-permute-start | bytes 393224 | tf_op jit(solution)/shard_map/ppermute | solution.py:41
  175.1 17.7 %collective-permute-start.41 = (bf16[128,896]{1,0:T(8,128)(2,1)S(1)}, bf16[128,896]{1,0:T(8,128)(2,1)S(1)}, u32[]{:S(2)}, u32[]{:S(2)}) collective-permute-start(bf16[128,896]{1,0:T(8,128)(2,1)S(1)} %get-tuple-element.297), channel_id=1, source_target_pairs={{0,8},{4,12},{8,0},{12,4},{1,9},{5,13},{9,1},{13,5},{2,10},{6,14},... | collective-permute-start | bytes 688136 | tf_op jit(solution)/shard_map/ppermute | solution.py:41
  177.4 16.3 %collective-permute-start.42 = (bf16[128,896]{1,0:T(8,128)(2,1)S(1)}, bf16[128,896]{1,0:T(8,128)(2,1)S(1)}, u32[]{:S(2)}, u32[]{:S(2)}) collective-permute-start(bf16[128,896]{1,0:T(8,128)(2,1)S(1)} %get-tuple-element.298), channel_id=1, source_target_pairs={{0,12},{4,8},{8,4},{12,0},{1,13},{5,9},{9,5},{13,1},{2,14},{6,10},... | collective-permute-start | bytes 688136 | tf_op jit(solution)/shard_map/ppermute | solution.py:41
  180.9 16.1 %collective-permute-start.38 = (bf16[64,1024]{1,0:T(8,128)(2,1)S(1)}, bf16[64,1024]{1,0:T(8,128)(2,1)S(1)}, u32[]{:S(2)}, u32[]{:S(2)}) collective-permute-start(bf16[64,1024]{1,0:T(8,128)(2,1)S(1)} %input_grad.1.refs_0_), channel_id=1, source_target_pairs={{0,1},{1,0},{2,3},{3,2},{4,5},{5,4},{6,7},{7,6},{8,9},{9,8},{10,11... | collective-permute-start | bytes 393224 | tf_op jit(solution)/shard_map/ppermute | solution.py:41
  181.7 19.3 %collective-permute-start.43 = (bf16[64,1024]{1,0:T(8,128)(2,1)S(1)}, bf16[64,1024]{1,0:T(8,128)(2,1)S(1)}, u32[]{:S(2)}, u32[]{:S(2)}) collective-permute-start(bf16[64,1024]{1,0:T(8,128)(2,1)S(1)} %get-tuple-element.302), channel_id=1, source_target_pairs={{0,4},{4,0},{8,12},{12,8},{1,5},{5,1},{9,13},{13,9},{2,6},{6,2},{1... | collective-permute-start | bytes 393224 | tf_op jit(solution)/shard_map/ppermute | solution.py:41
  182.0 19.0 %collective-permute-start.39 = (bf16[64,1024]{1,0:T(8,128)(2,1)S(1)}, bf16[64,1024]{1,0:T(8,128)(2,1)S(1)}, u32[]{:S(2)}, u32[]{:S(2)}) collective-permute-start(bf16[64,1024]{1,0:T(8,128)(2,1)S(1)} %input_grad.1.refs_0_), channel_id=1, source_target_pairs={{0,2},{1,3},{2,0},{3,1},{4,6},{5,7},{6,4},{7,5},{8,10},{9,11},{10,... | collective-permute-start | bytes 393224 | tf_op jit(solution)/shard_map/ppermute | solution.py:41
  192.8 8.3 %collective-permute-start.40 = (bf16[64,1024]{1,0:T(8,128)(2,1)S(1)}, bf16[64,1024]{1,0:T(8,128)(2,1)S(1)}, u32[]{:S(2)}, u32[]{:S(2)}) collective-permute-start(bf16[64,1024]{1,0:T(8,128)(2,1)S(1)} %input_grad.1.refs_0_), channel_id=1, source_target_pairs={{0,3},{1,2},{2,1},{3,0},{4,7},{5,6},{6,5},{7,4},{8,11},{9,10},{10,... | collective-permute-start | bytes 393224 | tf_op jit(solution)/shard_map/ppermute | solution.py:41
  193.7 12.6 %collective-permute-start.44 = (bf16[64,1024]{1,0:T(8,128)(2,1)S(1)}, bf16[64,1024]{1,0:T(8,128)(2,1)S(1)}, u32[]{:S(2)}, u32[]{:S(2)}) collective-permute-start(bf16[64,1024]{1,0:T(8,128)(2,1)S(1)} %get-tuple-element.303), channel_id=1, source_target_pairs={{0,8},{4,12},{8,0},{12,4},{1,9},{5,13},{9,1},{13,5},{2,10},{6,14},... | collective-permute-start | bytes 393224 | tf_op jit(solution)/shard_map/ppermute | solution.py:41
  197.0 9.3 %collective-permute-start.45 = (bf16[64,1024]{1,0:T(8,128)(2,1)S(1)}, bf16[64,1024]{1,0:T(8,128)(2,1)S(1)}, u32[]{:S(2)}, u32[]{:S(2)}) collective-permute-start(bf16[64,1024]{1,0:T(8,128)(2,1)S(1)} %get-tuple-element.304), channel_id=1, source_target_pairs={{0,12},{4,8},{8,4},{12,0},{1,13},{5,9},{9,5},{13,1},{2,14},{6,10},... | collective-permute-start | bytes 393224 | tf_op jit(solution)/shard_map/ppermute | solution.py:41
  206.4 16.4 %collective-permute-start.46 = (bf16[80,1024]{1,0:T(8,128)(2,1)S(1)}, bf16[80,1024]{1,0:T(8,128)(2,1)S(1)}, u32[]{:S(2)}, u32[]{:S(2)}) collective-permute-start(bf16[80,1024]{1,0:T(8,128)(2,1)S(1)} %out_piece.1.refs_0_), channel_id=1, source_target_pairs={{0,1},{1,0},{2,3},{3,2},{4,5},{5,4},{6,7},{7,6},{8,9},{9,8},{10,11... | collective-permute-start | bytes 491528 | tf_op jit(solution)/shard_map/ppermute | solution.py:41
  207.8 15.0 %collective-permute-start.47 = (bf16[80,1024]{1,0:T(8,128)(2,1)S(1)}, bf16[80,1024]{1,0:T(8,128)(2,1)S(1)}, u32[]{:S(2)}, u32[]{:S(2)}) collective-permute-start(bf16[80,1024]{1,0:T(8,128)(2,1)S(1)} %out_piece.1.refs_0_), channel_id=1, source_target_pairs={{0,2},{1,3},{2,0},{3,1},{4,6},{5,7},{6,4},{7,5},{8,10},{9,11},{10,... | collective-permute-start | bytes 491528 | tf_op jit(solution)/shard_map/ppermute | solution.py:41
  208.7 14.1 %collective-permute-start.48 = (bf16[80,1024]{1,0:T(8,128)(2,1)S(1)}, bf16[80,1024]{1,0:T(8,128)(2,1)S(1)}, u32[]{:S(2)}, u32[]{:S(2)}) collective-permute-start(bf16[80,1024]{1,0:T(8,128)(2,1)S(1)} %out_piece.1.refs_0_), channel_id=1, source_target_pairs={{0,3},{1,2},{2,1},{3,0},{4,7},{5,6},{6,5},{7,4},{8,11},{9,10},{10,... | collective-permute-start | bytes 491528 | tf_op jit(solution)/shard_map/ppermute | solution.py:41
  (34 other events, 526.6 us)

commit v7 on v6

--- a/solution.py
+++ b/solution.py
@@ -362,7 +362,7 @@
             *d_shapes,
             shape(dims(width), kind),
         ],
-        compiler_params=pltpu.CompilerParams(vmem_limit_bytes=30 * MIB),
+        compiler_params=pltpu.CompilerParams(vmem_limit_bytes=(14 if few else 30) * MIB),
         cost_estimate=pl.CostEstimate(flops=int(100.0*(total * width * inner // 8)), bytes_accessed=0, transcendentals=0),
         name="experts",
     )(base, *data, router, wcat, down_flat)
@@ -425,7 +425,7 @@
         in_specs=whole(n) + cols(dgu, 2 * hidden) + cols(h, hidden) + whole(c),
         out_specs=pl.BlockSpec((1, 3 * width, hidden), lambda e: (e, 0, 0)),
         out_shape=shape((local, 3 * width, hidden), BF),
-        compiler_params=pltpu.CompilerParams(vmem_limit_bytes=(32 if few else 58) * MIB),
+        compiler_params=pltpu.CompilerParams(vmem_limit_bytes=(20 if few else 58) * MIB),
         cost_estimate=pl.CostEstimate(flops=int(100.0*(24 * n[0].size * hidden * local)), bytes_accessed=0, transcendentals=0),
         name="expert_grads",
     )(*n, *dgu, *h, *c)
@@ -745,6 +745,7 @@
         "norm_two",
         "bbb",
         "vv",
+        limit=58,
     )
 
     n_two, cot_got = tied(n_two, cot_got)
@@ -782,11 +783,10 @@
     grads, (got, from_last) = tied(grads, (got, from_last))
     near, *across = split_sum([ds[0], *got], "dn_sum")
     through = added([near_last, *from_last], BF, "through")
-    across[0], (middle, moe_last) = tied(across[0], (moes[1:last], moes[last]))
+    across[0], middle = tied(across[0], moes[1:last])
     across = deal(across, "expert")
     near_sums = [near, swap(through, "tensor", last), *across]
     moe_got = [swap(middle[r - 1], "tensor", r) for r in range(1, last)]
-    moe_got.append(swap(moe_last, "tensor", last))
     moe_got, near_sums = tied(moe_got, near_sums)
 
     wide, dh, small = call(
@@ -801,9 +801,8 @@
     _, late_grads = tied(wide, grads)
     grads_got = swap(late_grads, "dp", 1)
     grads_got, wides = tied(grads_got, wides)
-    moe_near, *moe_across = split_sum([moes[0], *moe_got], "moe_sum")
-    moe_across, wides = tied(moe_across, wides)
-    moe_sums = [moe_near, *deal(moe_across, "expert")]
+    wides, moe_last = tied(wides, moes[last])
+    moe_got.append(swap(moe_last, "tensor", last))
 
     wide_all, dqkv, small, *back_parts = call(
         attend_back_kernel,
@@ -857,10 +856,14 @@
     )
     others = deal(others, "expert")
     others[0], part_sums = tied(others[0], part_sums)
+    moe_near, *moe_across = split_sum([moes[0], *moe_got], "moe_sum")
+    moe_sums = [moe_near, *deal(moe_across, "expert")]
     ig = call(
-        input_grad_kernel, [shape((rows, width), BF)], (xq, gain_one, dh, *part_sums), "input_grad", "bbbb"
+        input_grad_kernel, [shape((rows, width), BF)], (xq, gain_one, dh, *part_sums), "input_grad", "bbbb", limit=58
     )[0]
     igs = [ig] + [swap(ig, "tensor", r) for r in around]
+    expert_grads = both_copies(grads, grads_got)
+    expert_grads, others = tied(expert_grads, others)
     g_query, g_key, g_value, g_out, g_router, small = call(
         dense_sum_kernel,
         [
@@ -885,8 +888,6 @@
     )[0]
     out_piece = call(out_kernel, [shape((rows + 16, width), BF)], (h, small, *moe_sums), "out_piece")[0]
     outs = [out_piece] + [swap(out_piece, "tensor", r) for r in around]
-    expert_grads = both_copies(grads, grads_got)
-    expert_grads, outs = tied(expert_grads, outs)
     output, small = call(
         out_whole_kernel,
         [shape((seq_len, width), BF), shape((8, width), F32)],

time: 226 us -> 207 us (0.916)
  waiting for transfers between devices: 77.6 us -> 51.3 us
  starting transfers between devices: 63.2 us -> 69.9 us
  Pallas kernels: 72.5 us -> 74.9 us
    ppermute x49, waiting for transfers between devices: 77.6 us -> 51.3 us  [swap(): return lax.ppermute(x, axis, [(i, i ^ distance) for i in range(size)])]
    ppermute x49, starting transfers between devices: 63.2 us -> 69.9 us  [swap(): return lax.ppermute(x, axis, [(i, i ^ distance) for i in range(size)])]
    pallas_call x18, Pallas kernels: 25.8 us -> 29.4 us  [call(): pl.pallas_call(kernel, grid=(1,), out_shape=outs, in_specs=[spec(p, x) fo...]
    unnamed x67 -> x75, local copies, waits for them, and re-layouts: 8.68 us -> 7.81 us
  transfers between devices with their start and end apart: 49 -> 49, of which waited for: 18 -> 16; matrix products, arithmetic and copies ran while one was open for 1% -> 1% of each run, Pallas kernels for 26% -> 29%
where the time goes in v7:
time: 207 us
  Pallas kernels  74.9 us (36%)
  starting transfers between devices  69.9 us (34%)
  waiting for transfers between devices  51.3 us (25%)
  local copies, waits for them, and re-layouts  8.32 us (4%)
    ppermute x49, starting transfers between devices, swap(): return lax.ppermute(x, axis, [(i, i ^ distance) for i in range(size)])  69.9 us
    ppermute x49, waiting for transfers between devices, swap(): return lax.ppermute(x, axis, [(i, i ^ distance) for i in range(size)])  51.3 us
    pallas_call x18, Pallas kernels, call(): pl.pallas_call(kernel, grid=(1,), out_shape=outs, in_specs=[spec(p, x) fo...  29.4 us
    pallas_call x4, Pallas kernels, run_experts(): pl.pallas_call(kernel, grid=(total // step,), in_specs=[pl.BlockSpec(memo...  22.2 us
    pallas_call x1, Pallas kernels, both_copies(): pl.pallas_call(both_copies_kernel, grid=(local,), in_specs=[block(rows, h...  11.1 us
    pallas_call x1, Pallas kernels, run_grads(): pl.pallas_call(grads_kernel, grid=(local,), in_specs=whole(n) + cols(dgu,...  10.7 us
    unnamed x75, local copies, waits for them, and re-layouts  7.81 us
  transfers between devices with their start and end apart: 49, of which 16 were waited for; matrix products, arithmetic and copies ran while one was open for 1% of the time, Pallas kernels for 29%

profile of v7, /device:TPU:0, one launch (start us, length us, event | category | flops | bytes accessed | tf_op | source)
XLA Modules:
  0.0 206.8 jit_solution(2705549600860613064)
XLA Ops:
  0.6 2.2 %pieces.1 = (bf16[64,1152]{1,0:T(8,128)(2,1)}, bf16[64,1152]{1,0:T(8,128)(2,1)}, bf16[64,1152]{1,0:T(8,128)(2,1)}, bf16[64,1152]{1,0:T(8,128)(2,1)}, bf16[128,1024]{1,0:T(8,128)(2,1)}) custom-call(s32[1]{0:T(128)} %bitcast.me_ref, bf16[256,1024]{1,0:T(8,128)(2,1)} %cot_ref.1, s32[8,256]{1,0:T(8,128)} %bitcast.32, bf16[32,1024]{1,0:T(8,128)(2,1)} %bitcast.31), custom_call_target="tpu_custom_call" | custom-call | tf_op jit(solution)/shard_map/pieces/pallas_call | solution.py:118
  2.8 3.0 %collective-permute-start = (bf16[64,1152]{1,0:T(8,128)(2,1)}, bf16[64,1152]{1,0:T(8,128)(2,1)S(1)}, u32[]{:S(2)}, u32[]{:S(2)}) collective-permute-start(bf16[64,1152]{1,0:T(8,128)(2,1)} %get-tuple-element.163.refs_0_.own_ref.cot_ref), channel_id=1, source_target_pairs={{0,4},{4,0},{8,12},{12,8},{1,5},{5,1},{9,13},{13,9},{2,6},{6,2},{1... | collective-permute-start | bytes 442376 | tf_op jit(solution)/shard_map/ppermute | solution.py:41
  5.8 2.5 %collective-permute-start.5 = (bf16[64,1152]{1,0:T(8,128)(2,1)}, bf16[64,1152]{1,0:T(8,128)(2,1)S(1)}, u32[]{:S(2)}, u32[]{:S(2)}) collective-permute-start(bf16[64,1152]{1,0:T(8,128)(2,1)} %get-tuple-element.163.refs_0_.own_ref.cot_ref), channel_id=1, source_target_pairs={{0,12},{4,8},{8,4},{12,0},{1,13},{5,9},{9,5},{13,1},{2,14},{6,10},... | collective-permute-start | bytes 442376 | tf_op jit(solution)/shard_map/ppermute | solution.py:41
  8.4 1.8 collective-permute-done.refs_0_
  10.2 4.7 %attend.1 = (bf16[256,1024]{1,0:T(8,128)(2,1)}, bf16[256,256]{1,0:T(8,128)(2,1)}, bf16[256,128]{1,0:T(8,128)(2,1)}, bf16[256,128]{1,0:T(8,128)(2,1)}, bf16[256,2...) custom-call(s32[1]{0:T(128)} %bitcast.me_ref, ...), custom_call_target="tpu_custom_call" | custom-call | flops 53687091200 | tf_op jit(solution)/shard_map/attend/pallas_call | solution.py:118
  16.4 1.5 collective-permute-start.2
  18.4 2.9 %collective-permute-done.1.refs_0_ = bf16[64,1024]{1,0:T(8,128)(2,1)S(1)} collective-permute-done((bf16[64,1024]{1,0:T(8,128)(2,1)}, bf16[64,1024]{1,0:T(8,128)(2,1)S(1)}, u32[]{:S(2)}, u32[]{:S(2)}) %collective-permute-start.1) | collective-permute-done | bytes 131104 | tf_op jit(solution)/shard_map/ppermute | solution.py:41
  21.2 3.0 %collective-permute-done.2.refs_1_ = bf16[64,1024]{1,0:T(8,128)(2,1)S(1)} collective-permute-done((bf16[64,1024]{1,0:T(8,128)(2,1)}, bf16[64,1024]{1,0:T(8,128)(2,1)S(1)}, u32[]{:S(2)}, u32[]{:S(2)}) %collective-permute-start.2) | collective-permute-done | bytes 131104 | tf_op jit(solution)/shard_map/ppermute | solution.py:41
  24.9 2.0 norm_two.1
  26.9 2.2 %collective-permute-start.8 = (bf16[64,1024]{1,0:T(8,128)(2,1)}, bf16[64,1024]{1,0:T(8,128)(2,1)S(1)}, u32[]{:S(2)}, u32[]{:S(2)}) collective-permute-start(bf16[64,1024]{1,0:T(8,128)(2,1)} %get-tuple-element.173.refs_0_.n_ref), channel_id=1, source_target_pairs={{0,4},{4,0},{8,12},{12,8},{1,5},{5,1},{9,13},{13,9},{2,6},{6,2},{1... | collective-permute-start | bytes 393224 | tf_op jit(solution)/shard_map/ppermute | solution.py:41
  30.3 2.0 collective-permute-done.8.refs_1_
  33.0 6.5 %collective-permute-start.12 = (bf16[64,1024]{1,0:T(8,128)(2,1)}, bf16[64,1024]{1,0:T(8,128)(2,1)S(1)}, u32[]{:S(2)}, u32[]{:S(2)}) collective-permute-start(bf16[64,1024]{1,0:T(8,128)(2,1)} %get-tuple-element.173.refs_0_.n_ref), channel_id=1, source_target_pairs={{0,12},{4,8},{8,4},{12,0},{1,13},{5,9},{9,5},{13,1},{2,14},{6,10},... | collective-permute-start | bytes 393224 | tf_op jit(solution)/shard_map/ppermute | solution.py:41
  39.5 1.6 copy-done.1
  41.1 1.5 gate_up_weights.1.wcat
  42.6 2.9 %collective-permute-done.11.refs_2_ = bf16[64,1024]{1,0:T(8,128)(2,1)S(1)} collective-permute-done((bf16[64,1024]{1,0:T(8,128)(2,1)}, bf16[64,1024]{1,0:T(8,128)(2,1)S(1)}, u32[]{:S(2)}, u32[]{:S(2)}) %collective-permute-start.11) | collective-permute-done | bytes 131104 | tf_op jit(solution)/shard_map/ppermute | solution.py:41
  46.4 2.7 %collective-permute-start.13 = (bf16[4,64,1024]{2,1,0:T(8,128)(2,1)S(1)}, bf16[4,64,1024]{2,1,0:T(8,128)(2,1)S(1)}, u32[]{:S(2)}, u32[]{:S(2)}) collective-permute-start(bf16[4,64,1024]{2,1,0:T(8,128)(2,1)S(1)} %together.3.x_ref.a0), channel_id=1, source_target_pairs={{0,1},{1,0},{2,3},{3,2},{4,5},{5,4},{6,7},{7,6},{8,9},{9,8},{10,11... | collective-permute-start | bytes 1572872 | tf_op jit(solution)/shard_map/ppermute | solution.py:41
  49.1 4.1 %collective-permute-done.9.refs_7_.far_ref = bf16[3,64,1152]{2,1,0:T(8,128)(2,1)S(1)} collective-permute-done((bf16[3,64,1152]{2,1,0:T(8,128)(2,1)S(1)}, bf16[3,64,1152]{2,1,0:T(8,128)(2,1)S(1)}, u32[]{:S(2)}, u32[]{:S(2)}) %collective-permute-start.9) | collective-permute-done | bytes 442400 | tf_op jit(solution)/shard_map/ppermute | solution.py:41
  53.3 2.2 %counts.1 = f32[1,128]{1,0:T(1,128)S(1)} custom-call(bf16[64,1152]{1,0:T(8,128)(2,1)S(1)} %copy-done.5, bf16[64,1152]{1,0:T(8,128)(2,1)S(1)} %copy-done.17, bf16[64,1152]{1,0:T(8,128)(2,1)S(1)} %copy-done.16, bf16[64,1152]{1,0:T(8,128)(2,1)S(1)} %copy-done.15, bf16[3,64,1152]{2,1,0:T(8,128)(2,1)S(1)} %together.2.refs_4_.far_ref, ...), custom_call_target="tpu_custom_call" | custom-call | tf_op jit(solution)/shard_map/counts/pallas_call | solution.py:118
  55.6 4.5 %experts.4 = (bf16[256,1024]{1,0:T(8,128)(2,1)S(1)}, bf16[256,2048]{1,0:T(8,128)(2,1)S(1)}, bf16[256,1024]{1,0:T(8,128)(2,1)S(1)}, f32[4,64,1152]{2,1,0:T(8,128)S(1)}, f32[4,64,1024]{2,1,0:T(8,128)S(1)}) custom-call(s32[1]{0:T(128)} %bitcast.5.base_ref, bf16[4,64,1024]{2,1,0:T(8,128)(2,1)S(1)} %together.3.x_ref.a0, bf16[64,1152]{1,0:T(8,128)(2,1)S(1)} %copy-done.5, ...), custom_call_target="tpu_custom_call" | custom-call | flops 3355443200 | tf_op jit(solution)/shard_map/experts/pallas_call | solution.py:349
  60.5 6.3 %experts.5 = (bf16[256,1024]{1,0:T(8,128)(2,1)S(1)}, bf16[256,2048]{1,0:T(8,128)(2,1)S(1)}, bf16[256,1024]{1,0:T(8,128)(2,1)S(1)}, bf16[4,64,1152]{2,1,0:T(8,128)(2,1)}, bf16[4,64,1024]{2,1,0:T(8,128)(2,1)S(1)}) custom-call(s32[1]{0:T(128)} %bitcast.5.base_ref, bf16[4,64,1024]{2,1,0:T(8,128)(2,1)S(1)} %collective-permute-done.13.x_ref.a1, ...), custom_call_target="tpu_custom_call" | custom-call | flops 3355443200 | tf_op jit(solution)/shard_map/experts/pallas_call | solution.py:349
  66.8 1.8 collective-permute-start.16
  68.5 6.5 %experts.6 = (bf16[256,1024]{1,0:T(8,128)(2,1)S(1)}, bf16[256,2048]{1,0:T(8,128)(2,1)S(1)}, bf16[256,1024]{1,0:T(8,128)(2,1)S(1)}, bf16[4,64,1152]{2,1,0:T(8,128)(2,1)}, bf16[4,64,1024]{2,1,0:T(8,128)(2,1)S(1)}) custom-call(s32[1]{0:T(128)} %bitcast.5.base_ref, bf16[4,64,1024]{2,1,0:T(8,128)(2,1)S(1)} %collective-permute-done.14.x_ref.a2, ...), custom_call_target="tpu_custom_call" | custom-call | flops 3355443200 | tf_op jit(solution)/shard_map/experts/pallas_call | solution.py:349
  76.4 5.0 %experts.7 = (bf16[256,1024]{1,0:T(8,128)(2,1)S(1)}, bf16[256,2048]{1,0:T(8,128)(2,1)S(1)}, bf16[256,1024]{1,0:T(8,128)(2,1)S(1)}, f32[64,1152]{1,0:T(8,128)S(1)...) custom-call(s32[1]{0:T(128)} %bitcast.5.base_ref, ...), custom_call_target="tpu_custom_call" | custom-call | flops 3355443200 | tf_op jit(solution)/shard_map/experts/pallas_call | solution.py:349
  81.5 3.9 %collective-permute-start.19 = (bf16[64,1152]{1,0:T(8,128)(2,1)}, bf16[64,1152]{1,0:T(8,128)(2,1)}, u32[]{:S(2)}, u32[]{:S(2)}) collective-permute-start(bf16[64,1152]{1,0:T(8,128)(2,1)} %get-tuple-element.221), channel_id=1, source_target_pairs={{0,8},{4,12},{8,0},{12,4},{1,9},{5,13},{9,1},{13,5},{2,10},{6,14},... | collective-permute-start | bytes 442376 | tf_op jit(solution)/shard_map/ppermute | solution.py:41
  86.0 10.7 %expert_grads.1.mine_ref = bf16[8,3072,128]{2,1,0:T(8,128)(2,1)} custom-call(bf16[256,1024]{1,0:T(8,128)(2,1)S(1)} %bitcast.20, bf16[256,1024]{1,0:T(8,128)(2,1)S(1)} %bitcast.22, bf16[256,1024]{1,0:T(8,128)(2,1)S(1)} %bitcast.21, bf16[256,1024]{1,0:T(8,128)(2,1)S(1)} %bitcast.23, bf16[256,2048]{1,0:T(8,128)(2,1)S(1)} %get-tuple-element.206.refs_4_, ...), custom_call_target="tpu_custom_call" | custom-call | flops 644245094400 | tf_op jit(solution)/shard_map/expert_grads/pallas_call | solution.py:422
  99.9 1.9 collective-permute-start.24
  101.8 1.9 collective-permute-start.25
  108.8 6.6 %collective-permute-done.25.refs_3_ = bf16[64,1152]{1,0:T(8,128)(2,1)S(1)} collective-permute-done((bf16[64,1152]{1,0:T(8,128)(2,1)S(1)}, bf16[64,1152]{1,0:T(8,128)(2,1)S(1)}, u32[]{:S(2)}, u32[]{:S(2)}) %collective-permute-start.25) | collective-permute-done | bytes 147488 | tf_op jit(solution)/shard_map/ppermute | solution.py:41
  117.6 2.3 %collective-permute-start.30 = (bf16[64,1152]{1,0:T(8,128)(2,1)S(1)}, bf16[64,1152]{1,0:T(8,128)(2,1)S(1)}, u32[]{:S(2)}, u32[]{:S(2)}) collective-permute-start(bf16[64,1152]{1,0:T(8,128)(2,1)S(1)} %get-tuple-element.252.w0), channel_id=1, source_target_pairs={{0,3},{1,2},{2,1},{3,0},{4,7},{5,6},{6,5},{7,4},{8,11},{9,10},{10,... | collective-permute-start | bytes 442376 | tf_op jit(solution)/shard_map/ppermute | solution.py:41
  121.7 3.5 %collective-permute-done.30.w3 = bf16[64,1152]{1,0:T(8,128)(2,1)S(1)} collective-permute-done((bf16[64,1152]{1,0:T(8,128)(2,1)S(1)}, bf16[64,1152]{1,0:T(8,128)(2,1)S(1)}, u32[]{:S(2)}, u32[]{:S(2)}) %collective-permute-start.30) | collective-permute-done | bytes 147488 | tf_op jit(solution)/shard_map/ppermute | solution.py:41
  125.2 2.8 %collective-permute-done.29.w2 = bf16[64,1152]{1,0:T(8,128)(2,1)S(1)} collective-permute-done((bf16[64,1152]{1,0:T(8,128)(2,1)S(1)}, bf16[64,1152]{1,0:T(8,128)(2,1)S(1)}, u32[]{:S(2)}, u32[]{:S(2)}) %collective-permute-start.29) | collective-permute-done | bytes 147488 | tf_op jit(solution)/shard_map/ppermute | solution.py:41
  128.7 5.5 %attend_back.1 = (bf16[256,1152]{1,0:T(8,128)(2,1)}, bf16[256,512]{1,0:T(8,128)(2,1)}, f32[8,1024]{1,0:T(8,128)}, f32[64,1024]{1,0:T(8,128)}, bf16[64,1024]{1,0:...) custom-call(s32[1]{0:T(128)} %bitcast.me_ref, bf16[64,1152]{1,0:T(8,128)(2,1)} %copy-done.23, ...), custom_call_target="tpu_custom_call" | custom-call | flops 53687091200 | tf_op jit(solution)/shard_map/attend_back/pallas_call | solution.py:118
  134.2 4.0 %dense.1 = (f32[512,896]{1,0:T(8,128)}, bf16[512,896]{1,0:T(8,128)(2,1)}) custom-call(s32[2]{0:T(128)} %pad_add_fusion.me_ref, bf16[4,64,1024]{2,1,0:T(8,128)(2,1)} %copy-done.2, bf16[4,64,1024]{2,1,0:T(8,128)(2,1)} %copy-done.10, bf16[4,64,1024]{2,1,0:T(8,128)(2,1)} %copy-done.9, bf16[4,64,1024]{2,1,0:T(8,128)(2,1)} %copy-done.11, ...), custom_call_target="tpu_custom_call" | custom-call | flops 100 | tf_op jit(solution)/shard_map/dense/pallas_call | solution.py:118
  138.3 2.0 collective-permute-start.42
  141.6 1.5 copy-done.3
  144.2 2.3 %collective-permute-start.33 = (bf16[128,896]{1,0:T(8,128)(2,1)S(1)}, bf16[128,896]{1,0:T(8,128)(2,1)S(1)}, u32[]{:S(2)}, u32[]{:S(2)}) collective-permute-start(bf16[128,896]{1,0:T(8,128)(2,1)S(1)} %get-tuple-element.268), channel_id=1, source_target_pairs={{0,4},{4,0},{8,12},{12,8},{1,5},{5,1},{9,13},{13,9},{2,6},{6,2},{1... | collective-permute-start | bytes 688136 | tf_op jit(solution)/shard_map/ppermute | solution.py:41
  148.3 1.7 collective-permute-start.36
  150.0 6.6 %collective-permute-done.34.refs_1_ = bf16[64,1024]{1,0:T(8,128)(2,1)S(1)} collective-permute-done((bf16[64,1024]{1,0:T(8,128)(2,1)S(1)}, bf16[64,1024]{1,0:T(8,128)(2,1)S(1)}, u32[]{:S(2)}, u32[]{:S(2)}) %collective-permute-start.34) | collective-permute-done | bytes 131104 | tf_op jit(solution)/shard_map/ppermute | solution.py:41
  156.6 4.0 %collective-permute-start.40 = (bf16[128,896]{1,0:T(8,128)(2,1)S(1)}, bf16[128,896]{1,0:T(8,128)(2,1)S(1)}, u32[]{:S(2)}, u32[]{:S(2)}) collective-permute-start(bf16[128,896]{1,0:T(8,128)(2,1)S(1)} %get-tuple-element.284), channel_id=1, source_target_pairs={{0,8},{4,12},{8,0},{12,4},{1,9},{5,13},{9,1},{13,5},{2,10},{6,14},... | collective-permute-start | bytes 688136 | tf_op jit(solution)/shard_map/ppermute | solution.py:41
  162.1 2.1 %input_grad.1.refs_0_ = bf16[64,1024]{1,0:T(8,128)(2,1)} custom-call(bf16[64,1024]{1,0:T(8,128)(2,1)} %get-tuple-element.165.x_ref, f32[1,1024]{1,0:T(1,128)} %bitcast.34, f32[64,1024]{1,0:T(8,128)} %copy-done.14, f32[64,1024]{1,0:T(8,128)} %get-tuple-element.273.refs_0_, bf16[64,1024]{1,0:T(8,128)(2,1)} %copy-done.25, bf16[64,1024]{1,0:T(8,128)(2,1)} %copy-done.26, ...), custom_call_target="tpu_custom_call" | custom-call | tf_op jit(solution)/shard_map/input_grad/pallas_call | solution.py:118
  164.1 1.7 collective-permute-start.39
  167.6 8.5 %collective-permute-done.40.refs_1_ = bf16[128,896]{1,0:T(8,128)(2,1)S(1)} collective-permute-done((bf16[128,896]{1,0:T(8,128)(2,1)S(1)}, bf16[128,896]{1,0:T(8,128)(2,1)S(1)}, u32[]{:S(2)}, u32[]{:S(2)}) %collective-permute-start.40) | collective-permute-done | bytes 229408 | tf_op jit(solution)/shard_map/ppermute | solution.py:41
  177.2 3.6 %collective-permute-start.44 = (bf16[64,1024]{1,0:T(8,128)(2,1)S(1)}, bf16[64,1024]{1,0:T(8,128)(2,1)S(1)}, u32[]{:S(2)}, u32[]{:S(2)}) collective-permute-start(bf16[64,1024]{1,0:T(8,128)(2,1)S(1)} %get-tuple-element.297), channel_id=1, source_target_pairs={{0,8},{4,12},{8,0},{12,4},{1,9},{5,13},{9,1},{13,5},{2,10},{6,14},... | collective-permute-start | bytes 393224 | tf_op jit(solution)/shard_map/ppermute | solution.py:41
  180.8 2.6 %collective-permute-start.45 = (bf16[64,1024]{1,0:T(8,128)(2,1)S(1)}, bf16[64,1024]{1,0:T(8,128)(2,1)S(1)}, u32[]{:S(2)}, u32[]{:S(2)}) collective-permute-start(bf16[64,1024]{1,0:T(8,128)(2,1)S(1)} %get-tuple-element.298), channel_id=1, source_target_pairs={{0,12},{4,8},{8,4},{12,0},{1,13},{5,9},{9,5},{13,1},{2,14},{6,10},... | collective-permute-start | bytes 393224 | tf_op jit(solution)/shard_map/ppermute | solution.py:41
  183.4 11.1 %both_copies.1 = (f32[8,1024,128]{2,1,0:T(8,128)}, f32[8,1024,128]{2,1,0:T(8,128)}, f32[8,128,1024]{2,1,0:T(8,128)}) custom-call(bf16[8,3072,128]{2,1,0:T(8,128)(2,1)} %expert_grads.1.mine_ref, bf16[8,3072,128]{2,1,0:T(8,128)(2,1)} %collective-permute-done.27.other_ref), custom_call_target="tpu_custom_call" | custom-call | bytes 25165824 | tf_op jit(solution)/shard_map/both_copies/pallas_call | solution.py:451
  195.5 1.7 collective-permute-start.48
  200.8 2.4 %collective-permute-done.48.refs_3_ = bf16[80,1024]{1,0:T(8,128)(2,1)S(1)} collective-permute-done((bf16[80,1024]{1,0:T(8,128)(2,1)S(1)}, bf16[80,1024]{1,0:T(8,128)(2,1)S(1)}, u32[]{:S(2)}, u32[]{:S(2)}) %collective-permute-start.48) | collective-permute-done | bytes 163872 | tf_op jit(solution)/shard_map/ppermute | solution.py:41
  203.1 1.7 collective-permute-done.47.refs_2_
  (154 shorter events, 35.9 us)
Async XLA Ops:
  2.8 7.4 %collective-permute-start = (bf16[64,1152]{1,0:T(8,128)(2,1)}, bf16[64,1152]{1,0:T(8,128)(2,1)S(1)}, u32[]{:S(2)}, u32[]{:S(2)}) collective-permute-start(bf16[64,1152]{1,0:T(8,128)(2,1)} %get-tuple-element.163.refs_0_.own_ref.cot_ref), channel_id=1, source_target_pairs={{0,4},{4,0},{8,12},{12,8},{1,5},{5,1},{9,13},{13,9},{2,6},{6,2},{1... | collective-permute-start | bytes 442376 | tf_op jit(solution)/shard_map/ppermute | solution.py:41
  5.8 21.1 %collective-permute-start.5 = (bf16[64,1152]{1,0:T(8,128)(2,1)}, bf16[64,1152]{1,0:T(8,128)(2,1)S(1)}, u32[]{:S(2)}, u32[]{:S(2)}) collective-permute-start(bf16[64,1152]{1,0:T(8,128)(2,1)} %get-tuple-element.163.refs_0_.own_ref.cot_ref), channel_id=1, source_target_pairs={{0,12},{4,8},{8,4},{12,0},{1,13},{5,9},{9,5},{13,1},{2,14},{6,10},... | collective-permute-start | bytes 442376 | tf_op jit(solution)/shard_map/ppermute | solution.py:41
  8.3 18.6 %collective-permute-start.4 = (bf16[64,1152]{1,0:T(8,128)(2,1)}, bf16[64,1152]{1,0:T(8,128)(2,1)S(1)}, u32[]{:S(2)}, u32[]{:S(2)}) collective-permute-start(bf16[64,1152]{1,0:T(8,128)(2,1)} %get-tuple-element.163.refs_0_.own_ref.cot_ref), channel_id=1, source_target_pairs={{0,8},{4,12},{8,0},{12,4},{1,9},{5,13},{9,1},{13,5},{2,10},{6,14},... | collective-permute-start | bytes 442376 | tf_op jit(solution)/shard_map/ppermute | solution.py:41
  14.9 6.3 %collective-permute-start.1 = (bf16[64,1024]{1,0:T(8,128)(2,1)}, bf16[64,1024]{1,0:T(8,128)(2,1)S(1)}, u32[]{:S(2)}, u32[]{:S(2)}) collective-permute-start(bf16[64,1024]{1,0:T(8,128)(2,1)} %get-tuple-element.167), channel_id=1, source_target_pairs={{0,1},{1,0},{2,3},{3,2},{4,5},{5,4},{6,7},{7,6},{8,9},{9,8},{10,11... | collective-permute-start | bytes 393224 | tf_op jit(solution)/shard_map/ppermute | solution.py:41
  16.4 7.8 %collective-permute-start.2 = (bf16[64,1024]{1,0:T(8,128)(2,1)}, bf16[64,1024]{1,0:T(8,128)(2,1)S(1)}, u32[]{:S(2)}, u32[]{:S(2)}) collective-permute-start(bf16[64,1024]{1,0:T(8,128)(2,1)} %get-tuple-element.168), channel_id=1, source_target_pairs={{0,2},{1,3},{2,0},{3,1},{4,6},{5,7},{6,4},{7,5},{8,10},{9,11},{10,... | collective-permute-start | bytes 393224 | tf_op jit(solution)/shard_map/ppermute | solution.py:41
  17.9 6.3 %collective-permute-start.3 = (bf16[64,1024]{1,0:T(8,128)(2,1)}, bf16[64,1024]{1,0:T(8,128)(2,1)S(1)}, u32[]{:S(2)}, u32[]{:S(2)}) collective-permute-start(bf16[64,1024]{1,0:T(8,128)(2,1)} %get-tuple-element.169), channel_id=1, source_target_pairs={{0,3},{1,2},{2,1},{3,0},{4,7},{5,6},{6,5},{7,4},{8,11},{9,10},{10,... | collective-permute-start | bytes 393224 | tf_op jit(solution)/shard_map/ppermute | solution.py:41
  26.9 5.3 %collective-permute-start.8 = (bf16[64,1024]{1,0:T(8,128)(2,1)}, bf16[64,1024]{1,0:T(8,128)(2,1)S(1)}, u32[]{:S(2)}, u32[]{:S(2)}) collective-permute-start(bf16[64,1024]{1,0:T(8,128)(2,1)} %get-tuple-element.173.refs_0_.n_ref), channel_id=1, source_target_pairs={{0,4},{4,0},{8,12},{12,8},{1,5},{5,1},{9,13},{13,9},{2,6},{6,2},{1... | collective-permute-start | bytes 393224 | tf_op jit(solution)/shard_map/ppermute | solution.py:41
  29.1 20.0 %collective-permute-start.7 = (bf16[3,64,1152]{2,1,0:T(8,128)(2,1)S(1)}, bf16[3,64,1152]{2,1,0:T(8,128)(2,1)}, u32[]{:S(2)}, u32[]{:S(2)}) collective-permute-start(bf16[3,64,1152]{2,1,0:T(8,128)(2,1)S(1)} %together.2.refs_4_.far_ref), channel_id=1, source_target_pairs={{0,2},{1,3},{2,0},{3,1},{4,6},{5,7},{6,4},{7,5},{8,10},{9,11},{10,... | collective-permute-start | bytes 1327112 | tf_op jit(solution)/shard_map/ppermute | solution.py:41
  29.8 19.4 %collective-permute-start.6 = (bf16[3,64,1152]{2,1,0:T(8,128)(2,1)S(1)}, bf16[3,64,1152]{2,1,0:T(8,128)(2,1)}, u32[]{:S(2)}, u32[]{:S(2)}) collective-permute-start(bf16[3,64,1152]{2,1,0:T(8,128)(2,1)S(1)} %together.2.refs_4_.far_ref), channel_id=1, source_target_pairs={{0,1},{1,0},{2,3},{3,2},{4,5},{5,4},{6,7},{7,6},{8,9},{9,8},{10,11... | collective-permute-start | bytes 1327112 | tf_op jit(solution)/shard_map/ppermute | solution.py:41
  32.2 21.0 %collective-permute-start.9 = (bf16[3,64,1152]{2,1,0:T(8,128)(2,1)S(1)}, bf16[3,64,1152]{2,1,0:T(8,128)(2,1)S(1)}, u32[]{:S(2)}, u32[]{:S(2)}) collective-permute-start(bf16[3,64,1152]{2,1,0:T(8,128)(2,1)S(1)} %together.2.refs_4_.far_ref), channel_id=1, source_target_pairs={{0,3},{1,2},{2,1},{3,0},{4,7},{5,6},{6,5},{7,4},{8,11},{9,10},{10,... | collective-permute-start | bytes 1327112 | tf_op jit(solution)/shard_map/ppermute | solution.py:41
  33.0 9.6 %collective-permute-start.12 = (bf16[64,1024]{1,0:T(8,128)(2,1)}, bf16[64,1024]{1,0:T(8,128)(2,1)S(1)}, u32[]{:S(2)}, u32[]{:S(2)}) collective-permute-start(bf16[64,1024]{1,0:T(8,128)(2,1)} %get-tuple-element.173.refs_0_.n_ref), channel_id=1, source_target_pairs={{0,12},{4,8},{8,4},{12,0},{1,13},{5,9},{9,5},{13,1},{2,14},{6,10},... | collective-permute-start | bytes 393224 | tf_op jit(solution)/shard_map/ppermute | solution.py:41
  39.5 6.1 %collective-permute-start.11 = (bf16[64,1024]{1,0:T(8,128)(2,1)}, bf16[64,1024]{1,0:T(8,128)(2,1)S(1)}, u32[]{:S(2)}, u32[]{:S(2)}) collective-permute-start(bf16[64,1024]{1,0:T(8,128)(2,1)} %get-tuple-element.173.refs_0_.n_ref), channel_id=1, source_target_pairs={{0,8},{4,12},{8,0},{12,4},{1,9},{5,13},{9,1},{13,5},{2,10},{6,14},... | collective-permute-start | bytes 393224 | tf_op jit(solution)/shard_map/ppermute | solution.py:41
  45.6 22.9 %collective-permute-start.14 = (bf16[4,64,1024]{2,1,0:T(8,128)(2,1)S(1)}, bf16[4,64,1024]{2,1,0:T(8,128)(2,1)S(1)}, u32[]{:S(2)}, u32[]{:S(2)}) collective-permute-start(bf16[4,64,1024]{2,1,0:T(8,128)(2,1)S(1)} %together.3.x_ref.a0), channel_id=1, source_target_pairs={{0,2},{1,3},{2,0},{3,1},{4,6},{5,7},{6,4},{7,5},{8,10},{9,11},{10,... | collective-permute-start | bytes 1572872 | tf_op jit(solution)/shard_map/ppermute | solution.py:41
  46.4 14.1 %collective-permute-start.13 = (bf16[4,64,1024]{2,1,0:T(8,128)(2,1)S(1)}, bf16[4,64,1024]{2,1,0:T(8,128)(2,1)S(1)}, u32[]{:S(2)}, u32[]{:S(2)}) collective-permute-start(bf16[4,64,1024]{2,1,0:T(8,128)(2,1)S(1)} %together.3.x_ref.a0), channel_id=1, source_target_pairs={{0,1},{1,0},{2,3},{3,2},{4,5},{5,4},{6,7},{7,6},{8,9},{9,8},{10,11... | collective-permute-start | bytes 1572872 | tf_op jit(solution)/shard_map/ppermute | solution.py:41
  55.5 5.0 %collective-permute-start.10 = (f32[1,128]{1,0:T(1,128)S(1)}, f32[1,128]{1,0:T(1,128)S(1)}, u32[]{:S(2)}, u32[]{:S(2)}) collective-permute-start(f32[1,128]{1,0:T(1,128)S(1)} %counts.1), channel_id=1, source_target_pairs={{0,16},{16,0},{1,17},{17,1},{2,18},{18,2},{3,19},{19,3},{4,20},{20... | collective-permute-start | bytes 1544 | tf_op jit(solution)/shard_map/ppermute | solution.py:41
  60.1 16.3 %collective-permute-start.15 = (bf16[4,64,1024]{2,1,0:T(8,128)(2,1)S(1)}, bf16[4,64,1024]{2,1,0:T(8,128)(2,1)S(1)}, u32[]{:S(2)}, u32[]{:S(2)}) collective-permute-start(bf16[4,64,1024]{2,1,0:T(8,128)(2,1)S(1)} %together.3.x_ref.a0), channel_id=1, source_target_pairs={{0,3},{1,2},{2,1},{3,0},{4,7},{5,6},{6,5},{7,4},{8,11},{9,10},{10,... | collective-permute-start | bytes 1572872 | tf_op jit(solution)/shard_map/ppermute | solution.py:41
  66.8 30.0 %collective-permute-start.16 = (bf16[4,64,1152]{2,1,0:T(8,128)(2,1)}, bf16[4,64,1152]{2,1,0:T(8,128)(2,1)}, u32[]{:S(2)}, u32[]{:S(2)}) collective-permute-start(bf16[4,64,1152]{2,1,0:T(8,128)(2,1)} %get-tuple-element.193), channel_id=1, source_target_pairs={{0,1},{1,0},{2,3},{3,2},{4,5},{5,4},{6,7},{7,6},{8,9},{9,8},{10,11... | collective-permute-start | bytes 1769480 | tf_op jit(solution)/shard_map/ppermute | solution.py:41
  75.0 21.7 %collective-permute-start.17 = (bf16[4,64,1152]{2,1,0:T(8,128)(2,1)}, bf16[4,64,1152]{2,1,0:T(8,128)(2,1)}, u32[]{:S(2)}, u32[]{:S(2)}) collective-permute-start(bf16[4,64,1152]{2,1,0:T(8,128)(2,1)} %get-tuple-element.200), channel_id=1, source_target_pairs={{0,2},{1,3},{2,0},{3,1},{4,6},{5,7},{6,4},{7,5},{8,10},{9,11},{10,... | collective-permute-start | bytes 1769480 | tf_op jit(solution)/shard_map/ppermute | solution.py:41
  81.4 15.3 %collective-permute-start.18 = (bf16[64,1152]{1,0:T(8,128)(2,1)}, bf16[64,1152]{1,0:T(8,128)(2,1)}, u32[]{:S(2)}, u32[]{:S(2)}) collective-permute-start(bf16[64,1152]{1,0:T(8,128)(2,1)} %get-tuple-element.220), channel_id=1, source_target_pairs={{0,4},{4,0},{8,12},{12,8},{1,5},{5,1},{9,13},{13,9},{2,6},{6,2},{1... | collective-permute-start | bytes 442376 | tf_op jit(solution)/shard_map/ppermute | solution.py:41
  81.5 15.2 %collective-permute-start.19 = (bf16[64,1152]{1,0:T(8,128)(2,1)}, bf16[64,1152]{1,0:T(8,128)(2,1)}, u32[]{:S(2)}, u32[]{:S(2)}) collective-permute-start(bf16[64,1152]{1,0:T(8,128)(2,1)} %get-tuple-element.221), channel_id=1, source_target_pairs={{0,8},{4,12},{8,0},{12,4},{1,9},{5,13},{9,1},{13,5},{2,10},{6,14},... | collective-permute-start | bytes 442376 | tf_op jit(solution)/shard_map/ppermute | solution.py:41
  85.4 11.3 %collective-permute-start.20 = (bf16[64,1152]{1,0:T(8,128)(2,1)}, bf16[64,1152]{1,0:T(8,128)(2,1)}, u32[]{:S(2)}, u32[]{:S(2)}) collective-permute-start(bf16[64,1152]{1,0:T(8,128)(2,1)} %get-tuple-element.222), channel_id=1, source_target_pairs={{0,12},{4,8},{8,4},{12,0},{1,13},{5,9},{9,5},{13,1},{2,14},{6,10},... | collective-permute-start | bytes 442376 | tf_op jit(solution)/shard_map/ppermute | solution.py:41
  98.1 17.3 %collective-permute-start.21 = (bf16[4,64,1024]{2,1,0:T(8,128)(2,1)S(1)}, bf16[4,64,1024]{2,1,0:T(8,128)(2,1)S(1)}, u32[]{:S(2)}, u32[]{:S(2)}) collective-permute-start(bf16[4,64,1024]{2,1,0:T(8,128)(2,1)S(1)} %get-tuple-element.228), channel_id=1, source_target_pairs={{0,1},{1,0},{2,3},{3,2},{4,5},{5,4},{6,7},{7,6},{8,9},{9,8},{10,11... | collective-permute-start | bytes 1572872 | tf_op jit(solution)/shard_map/ppermute | solution.py:41
  99.1 16.4 %collective-permute-start.22 = (bf16[4,64,1024]{2,1,0:T(8,128)(2,1)S(1)}, bf16[4,64,1024]{2,1,0:T(8,128)(2,1)S(1)}, u32[]{:S(2)}, u32[]{:S(2)}) collective-permute-start(bf16[4,64,1024]{2,1,0:T(8,128)(2,1)S(1)} %get-tuple-element.229), channel_id=1, source_target_pairs={{0,2},{1,3},{2,0},{3,1},{4,6},{5,7},{6,4},{7,5},{8,10},{9,11},{10,... | collective-permute-start | bytes 1572872 | tf_op jit(solution)/shard_map/ppermute | solution.py:41
  99.9 7.5 %collective-permute-start.24 = (bf16[64,1152]{1,0:T(8,128)(2,1)S(1)}, bf16[64,1152]{1,0:T(8,128)(2,1)S(1)}, u32[]{:S(2)}, u32[]{:S(2)}) collective-permute-start(bf16[64,1152]{1,0:T(8,128)(2,1)S(1)} %get-tuple-element.235), channel_id=1, source_target_pairs={{0,4},{4,0},{8,12},{12,8},{1,5},{5,1},{9,13},{13,9},{2,6},{6,2},{1... | collective-permute-start | bytes 442376 | tf_op jit(solution)/shard_map/ppermute | solution.py:41
  101.8 13.6 %collective-permute-start.25 = (bf16[64,1152]{1,0:T(8,128)(2,1)S(1)}, bf16[64,1152]{1,0:T(8,128)(2,1)S(1)}, u32[]{:S(2)}, u32[]{:S(2)}) collective-permute-start(bf16[64,1152]{1,0:T(8,128)(2,1)S(1)} %get-tuple-element.236), channel_id=1, source_target_pairs={{0,8},{4,12},{8,0},{12,4},{1,9},{5,13},{9,1},{13,5},{2,10},{6,14},... | collective-permute-start | bytes 442376 | tf_op jit(solution)/shard_map/ppermute | solution.py:41
  103.7 11.7 %collective-permute-start.26 = (bf16[64,1152]{1,0:T(8,128)(2,1)S(1)}, bf16[64,1152]{1,0:T(8,128)(2,1)S(1)}, u32[]{:S(2)}, u32[]{:S(2)}) collective-permute-start(bf16[64,1152]{1,0:T(8,128)(2,1)S(1)} %get-tuple-element.237), channel_id=1, source_target_pairs={{0,12},{4,8},{8,4},{12,0},{1,13},{5,9},{9,5},{13,1},{2,14},{6,10},... | collective-permute-start | bytes 442376 | tf_op jit(solution)/shard_map/ppermute | solution.py:41
  107.5 8.0 %collective-permute-start.23 = (bf16[64,1152]{1,0:T(8,128)(2,1)S(1)}, bf16[64,1152]{1,0:T(8,128)(2,1)S(1)}, u32[]{:S(2)}, u32[]{:S(2)}) collective-permute-start(bf16[64,1152]{1,0:T(8,128)(2,1)S(1)} %through.1), channel_id=1, source_target_pairs={{0,3},{1,2},{2,1},{3,0},{4,7},{5,6},{6,5},{7,4},{8,11},{9,10},{10,... | collective-permute-start | bytes 442376 | tf_op jit(solution)/shard_map/ppermute | solution.py:41
  117.6 10.5 %collective-permute-start.27 = (bf16[8,3072,128]{2,1,0:T(8,128)(2,1)}, bf16[8,3072,128]{2,1,0:T(8,128)(2,1)}, u32[]{:S(2)}, u32[]{:S(2)}) collective-permute-start(bf16[8,3072,128]{2,1,0:T(8,128)(2,1)} %expert_grads.1.mine_ref), channel_id=1, source_target_pairs={{0,16},{16,0},{1,17},{17,1},{2,18},{18,2},{3,19},{19,3},{4,20},{20... | collective-permute-start | bytes 18874376 | tf_op jit(solution)/shard_map/ppermute | solution.py:41
  117.6 7.6 %collective-permute-start.30 = (bf16[64,1152]{1,0:T(8,128)(2,1)S(1)}, bf16[64,1152]{1,0:T(8,128)(2,1)S(1)}, u32[]{:S(2)}, u32[]{:S(2)}) collective-permute-start(bf16[64,1152]{1,0:T(8,128)(2,1)S(1)} %get-tuple-element.252.w0), channel_id=1, source_target_pairs={{0,3},{1,2},{2,1},{3,0},{4,7},{5,6},{6,5},{7,4},{8,11},{9,10},{10,... | collective-permute-start | bytes 442376 | tf_op jit(solution)/shard_map/ppermute | solution.py:41
  120.0 8.0 %collective-permute-start.29 = (bf16[64,1152]{1,0:T(8,128)(2,1)S(1)}, bf16[64,1152]{1,0:T(8,128)(2,1)S(1)}, u32[]{:S(2)}, u32[]{:S(2)}) collective-permute-start(bf16[64,1152]{1,0:T(8,128)(2,1)S(1)} %get-tuple-element.252.w0), channel_id=1, source_target_pairs={{0,2},{1,3},{2,0},{3,1},{4,6},{5,7},{6,4},{7,5},{8,10},{9,11},{10,... | collective-permute-start | bytes 442376 | tf_op jit(solution)/shard_map/ppermute | solution.py:41
  120.6 7.4 %collective-permute-start.28 = (bf16[64,1152]{1,0:T(8,128)(2,1)S(1)}, bf16[64,1152]{1,0:T(8,128)(2,1)S(1)}, u32[]{:S(2)}, u32[]{:S(2)}) collective-permute-start(bf16[64,1152]{1,0:T(8,128)(2,1)S(1)} %get-tuple-element.252.w0), channel_id=1, source_target_pairs={{0,1},{1,0},{2,3},{3,2},{4,5},{5,4},{6,7},{7,6},{8,9},{9,8},{10,11... | collective-permute-start | bytes 442376 | tf_op jit(solution)/shard_map/ppermute | solution.py:41
  138.2 3.4 %collective-permute-start.31 = (bf16[512,896]{1,0:T(8,128)(2,1)}, bf16[512,896]{1,0:T(8,128)(2,1)S(1)}, u32[]{:S(2)}, u32[]{:S(2)}) collective-permute-start(bf16[512,896]{1,0:T(8,128)(2,1)} %get-tuple-element.266), channel_id=1, source_target_pairs={{0,16},{16,0},{1,17},{17,1},{2,18},{18,2},{3,19},{19,3},{4,20},{20... | collective-permute-start | bytes 2752520 | tf_op jit(solution)/shard_map/ppermute | solution.py:41
  138.3 27.6 %collective-permute-start.42 = (bf16[4,64,1024]{2,1,0:T(8,128)(2,1)S(1)}, bf16[4,64,1024]{2,1,0:T(8,128)(2,1)S(1)}, u32[]{:S(2)}, u32[]{:S(2)}) collective-permute-start(bf16[4,64,1024]{2,1,0:T(8,128)(2,1)S(1)} %copy-done.22), channel_id=1, source_target_pairs={{0,3},{1,2},{2,1},{3,0},{4,7},{5,6},{6,5},{7,4},{8,11},{9,10},{10,... | collective-permute-start | bytes 1572872 | tf_op jit(solution)/shard_map/ppermute | solution.py:41
  144.2 17.2 %collective-permute-start.33 = (bf16[128,896]{1,0:T(8,128)(2,1)S(1)}, bf16[128,896]{1,0:T(8,128)(2,1)S(1)}, u32[]{:S(2)}, u32[]{:S(2)}) collective-permute-start(bf16[128,896]{1,0:T(8,128)(2,1)S(1)} %get-tuple-element.268), channel_id=1, source_target_pairs={{0,4},{4,0},{8,12},{12,8},{1,5},{5,1},{9,13},{13,9},{2,6},{6,2},{1... | collective-permute-start | bytes 688136 | tf_op jit(solution)/shard_map/ppermute | solution.py:41
  146.5 10.1 %collective-permute-start.34 = (bf16[64,1024]{1,0:T(8,128)(2,1)S(1)}, bf16[64,1024]{1,0:T(8,128)(2,1)S(1)}, u32[]{:S(2)}, u32[]{:S(2)}) collective-permute-start(bf16[64,1024]{1,0:T(8,128)(2,1)S(1)} %copy-done.36), channel_id=1, source_target_pairs={{0,1},{1,0},{2,3},{3,2},{4,5},{5,4},{6,7},{7,6},{8,9},{9,8},{10,11... | collective-permute-start | bytes 393224 | tf_op jit(solution)/shard_map/ppermute | solution.py:41
  147.5 13.1 %collective-permute-start.35 = (bf16[64,1024]{1,0:T(8,128)(2,1)S(1)}, bf16[64,1024]{1,0:T(8,128)(2,1)S(1)}, u32[]{:S(2)}, u32[]{:S(2)}) collective-permute-start(bf16[64,1024]{1,0:T(8,128)(2,1)S(1)} %copy-done.35), channel_id=1, source_target_pairs={{0,2},{1,3},{2,0},{3,1},{4,6},{5,7},{6,4},{7,5},{8,10},{9,11},{10,... | collective-permute-start | bytes 393224 | tf_op jit(solution)/shard_map/ppermute | solution.py:41
  148.3 13.1 %collective-permute-start.36 = (bf16[64,1024]{1,0:T(8,128)(2,1)S(1)}, bf16[64,1024]{1,0:T(8,128)(2,1)S(1)}, u32[]{:S(2)}, u32[]{:S(2)}) collective-permute-start(bf16[64,1024]{1,0:T(8,128)(2,1)S(1)} %copy-done.34), channel_id=1, source_target_pairs={{0,3},{1,2},{2,1},{3,0},{4,7},{5,6},{6,5},{7,4},{8,11},{9,10},{10,... | collective-permute-start | bytes 393224 | tf_op jit(solution)/shard_map/ppermute | solution.py:41
  156.6 19.5 %collective-permute-start.40 = (bf16[128,896]{1,0:T(8,128)(2,1)S(1)}, bf16[128,896]{1,0:T(8,128)(2,1)S(1)}, u32[]{:S(2)}, u32[]{:S(2)}) collective-permute-start(bf16[128,896]{1,0:T(8,128)(2,1)S(1)} %get-tuple-element.284), channel_id=1, source_target_pairs={{0,8},{4,12},{8,0},{12,4},{1,9},{5,13},{9,1},{13,5},{2,10},{6,14},... | collective-permute-start | bytes 688136 | tf_op jit(solution)/shard_map/ppermute | solution.py:41
  160.6 16.6 %collective-permute-start.41 = (bf16[128,896]{1,0:T(8,128)(2,1)S(1)}, bf16[128,896]{1,0:T(8,128)(2,1)S(1)}, u32[]{:S(2)}, u32[]{:S(2)}) collective-permute-start(bf16[128,896]{1,0:T(8,128)(2,1)S(1)} %get-tuple-element.285), channel_id=1, source_target_pairs={{0,12},{4,8},{8,4},{12,0},{1,13},{5,9},{9,5},{13,1},{2,14},{6,10},... | collective-permute-start | bytes 688136 | tf_op jit(solution)/shard_map/ppermute | solution.py:41
  164.1 16.7 %collective-permute-start.39 = (bf16[64,1024]{1,0:T(8,128)(2,1)}, bf16[64,1024]{1,0:T(8,128)(2,1)S(1)}, u32[]{:S(2)}, u32[]{:S(2)}) collective-permute-start(bf16[64,1024]{1,0:T(8,128)(2,1)} %input_grad.1.refs_0_), channel_id=1, source_target_pairs={{0,3},{1,2},{2,1},{3,0},{4,7},{5,6},{6,5},{7,4},{8,11},{9,10},{10,... | collective-permute-start | bytes 393224 | tf_op jit(solution)/shard_map/ppermute | solution.py:41
  166.1 29.3 %collective-permute-start.43 = (bf16[64,1024]{1,0:T(8,128)(2,1)S(1)}, bf16[64,1024]{1,0:T(8,128)(2,1)S(1)}, u32[]{:S(2)}, u32[]{:S(2)}) collective-permute-start(bf16[64,1024]{1,0:T(8,128)(2,1)S(1)} %get-tuple-element.296), channel_id=1, source_target_pairs={{0,4},{4,0},{8,12},{12,8},{1,5},{5,1},{9,13},{13,9},{2,6},{6,2},{1... | collective-permute-start | bytes 393224 | tf_op jit(solution)/shard_map/ppermute | solution.py:41
  166.4 29.0 %collective-permute-start.38 = (bf16[64,1024]{1,0:T(8,128)(2,1)}, bf16[64,1024]{1,0:T(8,128)(2,1)S(1)}, u32[]{:S(2)}, u32[]{:S(2)}) collective-permute-start(bf16[64,1024]{1,0:T(8,128)(2,1)} %input_grad.1.refs_0_), channel_id=1, source_target_pairs={{0,2},{1,3},{2,0},{3,1},{4,6},{5,7},{6,4},{7,5},{8,10},{9,11},{10,... | collective-permute-start | bytes 393224 | tf_op jit(solution)/shard_map/ppermute | solution.py:41
  176.1 19.3 %collective-permute-start.37 = (bf16[64,1024]{1,0:T(8,128)(2,1)}, bf16[64,1024]{1,0:T(8,128)(2,1)S(1)}, u32[]{:S(2)}, u32[]{:S(2)}) collective-permute-start(bf16[64,1024]{1,0:T(8,128)(2,1)} %input_grad.1.refs_0_), channel_id=1, source_target_pairs={{0,1},{1,0},{2,3},{3,2},{4,5},{5,4},{6,7},{7,6},{8,9},{9,8},{10,11... | collective-permute-start | bytes 393224 | tf_op jit(solution)/shard_map/ppermute | solution.py:41
  177.2 18.2 %collective-permute-start.44 = (bf16[64,1024]{1,0:T(8,128)(2,1)S(1)}, bf16[64,1024]{1,0:T(8,128)(2,1)S(1)}, u32[]{:S(2)}, u32[]{:S(2)}) collective-permute-start(bf16[64,1024]{1,0:T(8,128)(2,1)S(1)} %get-tuple-element.297), channel_id=1, source_target_pairs={{0,8},{4,12},{8,0},{12,4},{1,9},{5,13},{9,1},{13,5},{2,10},{6,14},... | collective-permute-start | bytes 393224 | tf_op jit(solution)/shard_map/ppermute | solution.py:41
  180.8 14.6 %collective-permute-start.45 = (bf16[64,1024]{1,0:T(8,128)(2,1)S(1)}, bf16[64,1024]{1,0:T(8,128)(2,1)S(1)}, u32[]{:S(2)}, u32[]{:S(2)}) collective-permute-start(bf16[64,1024]{1,0:T(8,128)(2,1)S(1)} %get-tuple-element.298), channel_id=1, source_target_pairs={{0,12},{4,8},{8,4},{12,0},{1,13},{5,9},{9,5},{13,1},{2,14},{6,10},... | collective-permute-start | bytes 393224 | tf_op jit(solution)/shard_map/ppermute | solution.py:41
  195.5 7.6 %collective-permute-start.48 = (bf16[80,1024]{1,0:T(8,128)(2,1)S(1)}, bf16[80,1024]{1,0:T(8,128)(2,1)S(1)}, u32[]{:S(2)}, u32[]{:S(2)}) collective-permute-start(bf16[80,1024]{1,0:T(8,128)(2,1)S(1)} %out_piece.1.refs_0_), channel_id=1, source_target_pairs={{0,3},{1,2},{2,1},{3,0},{4,7},{5,6},{6,5},{7,4},{8,11},{9,10},{10,... | collective-permute-start | bytes 491528 | tf_op jit(solution)/shard_map/ppermute | solution.py:41
  197.2 7.6 %collective-permute-start.47 = (bf16[80,1024]{1,0:T(8,128)(2,1)S(1)}, bf16[80,1024]{1,0:T(8,128)(2,1)S(1)}, u32[]{:S(2)}, u32[]{:S(2)}) collective-permute-start(bf16[80,1024]{1,0:T(8,128)(2,1)S(1)} %out_piece.1.refs_0_), channel_id=1, source_target_pairs={{0,2},{1,3},{2,0},{3,1},{4,6},{5,7},{6,4},{7,5},{8,10},{9,11},{10,... | collective-permute-start | bytes 491528 | tf_op jit(solution)/shard_map/ppermute | solution.py:41
  198.1 6.7 %collective-permute-start.46 = (bf16[80,1024]{1,0:T(8,128)(2,1)S(1)}, bf16[80,1024]{1,0:T(8,128)(2,1)S(1)}, u32[]{:S(2)}, u32[]{:S(2)}) collective-permute-start(bf16[80,1024]{1,0:T(8,128)(2,1)S(1)} %out_piece.1.refs_0_), channel_id=1, source_target_pairs={{0,1},{1,0},{2,3},{3,2},{4,5},{5,4},{6,7},{7,6},{8,9},{9,8},{10,11... | collective-permute-start | bytes 491528 | tf_op jit(solution)/shard_map/ppermute | solution.py:41
  (38 other events, 438.1 us)

commit v8 on v7

--- a/solution.py
+++ b/solution.py
@@ -492,12 +492,13 @@
 
 def attend_back_kernel(
     me_ref, w0, w1, w2, w3, x_ref, q_ref, k_ref, v_ref, lse_ref, wq_ref, wk_ref, wv_ref, wo_ref, cos_ref, sin_ref,
-    small_in, wide_ref, dq_ref, small_ref, p0, p1, p2, p3, do_ref, whole
+    small_in, a0, a1, a2, a3, o_ref, n_ref, small_ref, p0, p1, p2, p3, kept_ref, sent_ref,
+    do_ref, whole, wide_ref, dq_ref, two_ref, dense
 ):
     rows = w0.shape[0]
     width = x_ref.shape[1]
     for r, piece in enumerate((w0, w1, w2, w3)):
-        start = pl.multiple_of((me_ref[0] ^ r) * rows, rows)
+        start = pl.multiple_of((me_ref[1] ^ r) * rows, rows)
         wide_ref[pl.ds(start, rows), :] = piece[...]
     do_ref[...] = nt(wide_ref[:, :width], wo_ref[...]).astype(BF)
     cosine, sine = cos_ref[...], sin_ref[...]
@@ -551,22 +552,18 @@
     small_ref[...] = small_in[...]
     small_ref[0:1, :] = jnp.sum(whole[...] * x * inv, axis=0, keepdims=True)
     for r, part in enumerate((p0, p1, p2, p3)):
-        start = pl.multiple_of((me_ref[0] ^ r) * rows, rows)
+        start = pl.multiple_of((me_ref[1] ^ r) * rows, rows)
         part[...] = whole[pl.ds(start, rows), :].astype(part.dtype)
-
-
-def dense_kernel(me_ref, a0, a1, a2, a3, wide_ref, o_ref, n_ref, dq_ref, kept_ref, sent_ref, two_ref, whole):
-    rows, width = a0.shape[1:]
     for r, piece in enumerate((a0, a1, a2, a3)):
         start = pl.multiple_of((me_ref[1] ^ r) * rows, rows)
         two_ref[pl.ds(start, rows), :] = piece[0]
-    columns, heads = dq_ref.shape[1], o_ref.shape[1]
-    whole[:, :columns] = tn(n_ref[...], dq_ref[...])
-    whole[:, columns : columns + heads] = tn(wide_ref[:, :width], o_ref[...])
-    whole[:, columns + heads :] = tn(two_ref[...], wide_ref[:, width:])
+    columns = dq_ref.shape[1]
+    dense[:, :columns] = tn(n_ref[...], dq_ref[...])
+    dense[:, columns : columns + heads] = tn(wide_ref[:, :width], o_ref[...])
+    dense[:, columns + heads :] = tn(two_ref[...], wide_ref[:, width:])
     half = kept_ref.shape[0]
-    kept_ref[...] = whole[pl.ds(pl.multiple_of(me_ref[0] * half, half), half), :]
-    sent_ref[...] = whole[pl.ds(pl.multiple_of((1 - me_ref[0]) * half, half), half), :].astype(BF)
+    kept_ref[...] = dense[pl.ds(pl.multiple_of(me_ref[0] * half, half), half), :]
+    sent_ref[...] = dense[pl.ds(pl.multiple_of((1 - me_ref[0]) * half, half), half), :].astype(BF)
 
 
 def input_grad_kernel(x_ref, gain_ref, dh_ref, *refs):
@@ -801,69 +798,55 @@
     _, late_grads = tied(wide, grads)
     grads_got = swap(late_grads, "dp", 1)
     grads_got, wides = tied(grads_got, wides)
-    wides, moe_last = tied(wides, moes[last])
-    moe_got.append(swap(moe_last, "tensor", last))
-
-    wide_all, dqkv, small, *back_parts = call(
+    half = width // dp_size
+    chunk = half // expert_size
+    columns = heads + 2 * keys_wide
+    all_columns = columns + heads + LANES
+    own_block = pl.BlockSpec((1, rows, width), lambda i: (0, 0, 0))
+    small, *back_parts, kept, sent = call(
         attend_back_kernel,
-        [
-            shape((seq_len, wide_width), BF),
-            shape((seq_len, heads + 2 * keys_wide), BF),
-            shape((8, width), F32),
-            shape((rows, width), F32),
-        ]
-        + [shape((rows, width), BF)] * last,
-        (t_at, *wides, tokens, q, k, v, lse, w_query, w_key, w_value, w_output, cosine, sine, small),
+        [shape((8, width), F32), shape((rows, width), F32)]
+        + [shape((rows, width), BF)] * last
+        + [shape((half, all_columns), F32), shape((half, all_columns), BF)],
+        (d_at, *wides, tokens, q, k, v, lse, w_query, w_key, w_value, w_output, cosine, sine, small)
+        + (*twos, o, n_one),
         "attend_back",
-        "s" + "v" * tensor_size + "b" * 11,
-        "bb",
+        ["s"] + ["v"] * tensor_size + ["b"] * 12 + [own_block] * tensor_size + ["b"] * 2,
+        "bvvvvbb",
         limit=58,
         scratch=[
             pltpu.VMEM((seq_len, heads), BF),
             pltpu.VMEM((seq_len, width), F32),
-        ],
-        flops=2 * seq_len * width * 4 * heads,
-    )
-    part_sums = [back_parts[0]] + [swap(back_parts[r], "tensor", r) for r in around]
-    half = width // dp_size
-    chunk = half // expert_size
-
-    columns = heads + 2 * keys_wide
-    all_columns = columns + heads + LANES
-    own_block = pl.BlockSpec((1, rows, width), lambda i: (0, 0, 0))
-    kept, sent = call(
-        dense_kernel,
-        [shape((half, all_columns), F32), shape((half, all_columns), BF)],
-        (d_at, *twos, wide_all, o, n_one, dqkv),
-        "dense",
-        ["s"] + [own_block] * tensor_size + ["b"] * 4,
-        "vv",
-        limit=54,
-        scratch=[
+            pltpu.VMEM((seq_len, wide_width), BF),
+            pltpu.VMEM((seq_len, columns), BF),
             pltpu.VMEM((seq_len, width), BF),
             pltpu.VMEM((width, all_columns), F32),
         ],
-        flops=1,
-    )
+        flops=2 * seq_len * width * 4 * heads,
+    )
+    part_sums = [back_parts[0]] + [swap(back_parts[r], "tensor", r) for r in around]
+    sent = swap(sent, "dp", 1)
     mine, *others, small = call(
         kept_and_dealt_kernel,
         [shape((chunk, all_columns), F32)]
         + [shape((chunk, all_columns), BF)] * (expert_size - 1)
         + [shape((8, width), F32)],
-        (e_at, kept, swap(sent, "dp", 1), small, swap(small, "dp", 1)),
+        (e_at, kept, sent, small, swap(small, "dp", 1)),
         "dense_dealt",
-        "s",
+        "sbbbb",
+        limit=58,
     )
     others = deal(others, "expert")
-    others[0], part_sums = tied(others[0], part_sums)
+    expert_grads = both_copies(grads, grads_got)
+    (expert_grads, others[0]), part_sums = tied((expert_grads, others[0]), part_sums)
+    _, moe_last = tied(part_sums, moes[last])
+    moe_got.append(swap(moe_last, "tensor", last))
     moe_near, *moe_across = split_sum([moes[0], *moe_got], "moe_sum")
     moe_sums = [moe_near, *deal(moe_across, "expert")]
     ig = call(
         input_grad_kernel, [shape((rows, width), BF)], (xq, gain_one, dh, *part_sums), "input_grad", "bbbb", limit=58
     )[0]
     igs = [ig] + [swap(ig, "tensor", r) for r in around]
-    expert_grads = both_copies(grads, grads_got)
-    expert_grads, others = tied(expert_grads, others)
     g_query, g_key, g_value, g_out, g_router, small = call(
         dense_sum_kernel,
         [

time: 207 us -> 212 us (1.024)
  local copies, waits for them, and re-layouts: 8.32 us -> 11.8 us
    unnamed x75 -> x95, local copies, waits for them, and re-layouts: 7.81 us -> 11.3 us
    pallas_call x18 -> x17, Pallas kernels: 29.4 us -> 29.9 us  [call(): pl.pallas_call(kernel, grid=(1,), out_shape=outs, in_specs=[spec(p, x) fo...]
  transfers between devices with their start and end apart: 49 -> 49, of which waited for: 16 -> 18; matrix products, arithmetic and copies ran while one was open for 1% -> 1% of each run, Pallas kernels for 29% -> 28%
where the time goes in v8:
time: 212 us; the launch traced here: 211 us
  Pallas kernels  74.8 us (35%)
  starting transfers between devices  70.1 us (33%)
  waiting for transfers between devices  52.1 us (25%)
  local copies, waits for them, and re-layouts  11.8 us (6%)
    ppermute x49, starting transfers between devices, swap(): return lax.ppermute(x, axis, [(i, i ^ distance) for i in range(size)])  70.1 us
    ppermute x49, waiting for transfers between devices, swap(): return lax.ppermute(x, axis, [(i, i ^ distance) for i in range(size)])  52.1 us
    pallas_call x17, Pallas kernels, call(): pl.pallas_call(kernel, grid=(1,), out_shape=outs, in_specs=[spec(p, x) fo...  29.9 us
    pallas_call x4, Pallas kernels, run_experts(): pl.pallas_call(kernel, grid=(total // step,), in_specs=[pl.BlockSpec(memo...  21.6 us
    unnamed x95, local copies, waits for them, and re-layouts  11.3 us
    pallas_call x1, Pallas kernels, both_copies(): pl.pallas_call(both_copies_kernel, grid=(local,), in_specs=[block(rows, h...  11.1 us
    pallas_call x1, Pallas kernels, run_grads(): pl.pallas_call(grads_kernel, grid=(local,), in_specs=whole(n) + cols(dgu,...  10.6 us
  transfers between devices with their start and end apart: 49, of which 18 were waited for; matrix products, arithmetic and copies ran while one was open for 1% of the time, Pallas kernels for 28%

profile of v8, /device:TPU:0, one launch (start us, length us, event | category | flops | bytes accessed | tf_op | source)
XLA Modules:
  0.0 211.0 jit_solution(12818882953329795621)
XLA Ops:
  0.6 2.2 %pieces.1 = (bf16[64,1152]{1,0:T(8,128)(2,1)}, bf16[64,1152]{1,0:T(8,128)(2,1)}, bf16[64,1152]{1,0:T(8,128)(2,1)}, bf16[64,1152]{1,0:T(8,128)(2,1)}, bf16[128,1024]{1,0:T(8,128)(2,1)}) custom-call(s32[1]{0:T(128)} %bitcast.me_ref, bf16[256,1024]{1,0:T(8,128)(2,1)} %cot_ref.1, s32[8,256]{1,0:T(8,128)} %bitcast.32, bf16[32,1024]{1,0:T(8,128)(2,1)} %bitcast.31), custom_call_target="tpu_custom_call" | custom-call | tf_op jit(solution)/shard_map/pieces/pallas_call | solution.py:118
  2.8 3.0 %collective-permute-start = (bf16[64,1152]{1,0:T(8,128)(2,1)}, bf16[64,1152]{1,0:T(8,128)(2,1)S(1)}, u32[]{:S(2)}, u32[]{:S(2)}) collective-permute-start(bf16[64,1152]{1,0:T(8,128)(2,1)} %get-tuple-element.154.refs_0_.own_ref.cot_ref), channel_id=1, source_target_pairs={{0,4},{4,0},{8,12},{12,8},{1,5},{5,1},{9,13},{13,9},{2,6},{6,2},{1... | collective-permute-start | bytes 442376 | tf_op jit(solution)/shard_map/ppermute | solution.py:41
  5.8 2.6 %collective-permute-start.4 = (bf16[64,1152]{1,0:T(8,128)(2,1)}, bf16[64,1152]{1,0:T(8,128)(2,1)S(1)}, u32[]{:S(2)}, u32[]{:S(2)}) collective-permute-start(bf16[64,1152]{1,0:T(8,128)(2,1)} %get-tuple-element.154.refs_0_.own_ref.cot_ref), channel_id=1, source_target_pairs={{0,8},{4,12},{8,0},{12,4},{1,9},{5,13},{9,1},{13,5},{2,10},{6,14},... | collective-permute-start | bytes 442376 | tf_op jit(solution)/shard_map/ppermute | solution.py:41
  8.4 3.5 %collective-permute-done.refs_0_ = bf16[64,1152]{1,0:T(8,128)(2,1)S(1)} collective-permute-done((bf16[64,1152]{1,0:T(8,128)(2,1)}, bf16[64,1152]{1,0:T(8,128)(2,1)S(1)}, u32[]{:S(2)}, u32[]{:S(2)}) %collective-permute-start) | collective-permute-done | bytes 147488 | tf_op jit(solution)/shard_map/ppermute | solution.py:41
  11.9 4.6 %attend.1 = (bf16[256,1024]{1,0:T(8,128)(2,1)}, bf16[256,256]{1,0:T(8,128)(2,1)}, bf16[256,128]{1,0:T(8,128)(2,1)}, bf16[256,128]{1,0:T(8,128)(2,1)}, bf16[256,2...) custom-call(s32[1]{0:T(128)} %bitcast.me_ref, ...), custom_call_target="tpu_custom_call" | custom-call | flops 53687091200 | tf_op jit(solution)/shard_map/attend/pallas_call | solution.py:118
  16.5 1.7 collective-permute-start.1
  20.0 1.7 collective-permute-done.1.refs_0_
  21.7 1.7 collective-permute-done.2.refs_1_
  23.4 2.4 %collective-permute-done.3.refs_2_ = bf16[64,1024]{1,0:T(8,128)(2,1)S(1)} collective-permute-done((bf16[64,1024]{1,0:T(8,128)(2,1)}, bf16[64,1024]{1,0:T(8,128)(2,1)S(1)}, u32[]{:S(2)}, u32[]{:S(2)}) %collective-permute-start.3) | collective-permute-done | bytes 131104 | tf_op jit(solution)/shard_map/ppermute | solution.py:41
  26.5 2.0 norm_two.1
  30.1 3.7 %collective-permute-done.8.refs_1_ = bf16[64,1024]{1,0:T(8,128)(2,1)S(1)} collective-permute-done((bf16[64,1024]{1,0:T(8,128)(2,1)}, bf16[64,1024]{1,0:T(8,128)(2,1)S(1)}, u32[]{:S(2)}, u32[]{:S(2)}) %collective-permute-start.8) | collective-permute-done | bytes 131104 | tf_op jit(solution)/shard_map/ppermute | solution.py:41
  34.9 2.6 %collective-permute-start.11 = (bf16[64,1024]{1,0:T(8,128)(2,1)}, bf16[64,1024]{1,0:T(8,128)(2,1)S(1)}, u32[]{:S(2)}, u32[]{:S(2)}) collective-permute-start(bf16[64,1024]{1,0:T(8,128)(2,1)} %get-tuple-element.164.refs_0_.n_ref), channel_id=1, source_target_pairs={{0,8},{4,12},{8,0},{12,4},{1,9},{5,13},{9,1},{13,5},{2,10},{6,14},... | collective-permute-start | bytes 393224 | tf_op jit(solution)/shard_map/ppermute | solution.py:41
  39.0 1.6 copy-done.1
  42.2 2.8 %collective-permute-done.11.refs_2_ = bf16[64,1024]{1,0:T(8,128)(2,1)S(1)} collective-permute-done((bf16[64,1024]{1,0:T(8,128)(2,1)}, bf16[64,1024]{1,0:T(8,128)(2,1)S(1)}, u32[]{:S(2)}, u32[]{:S(2)}) %collective-permute-start.11) | collective-permute-done | bytes 131104 | tf_op jit(solution)/shard_map/ppermute | solution.py:41
  49.7 1.6 collective-permute-start.14
  51.3 2.2 %counts.1 = f32[1,128]{1,0:T(1,128)S(1)} custom-call(bf16[64,1152]{1,0:T(8,128)(2,1)S(1)} %copy-done.3, bf16[64,1152]{1,0:T(8,128)(2,1)S(1)} %copy-done.13, bf16[64,1152]{1,0:T(8,128)(2,1)S(1)} %copy-done.12, bf16[64,1152]{1,0:T(8,128)(2,1)S(1)} %copy-done.11, bf16[3,64,1152]{2,1,0:T(8,128)(2,1)S(1)} %together.2.refs_4_.far_ref, ...), custom_call_target="tpu_custom_call" | custom-call | tf_op jit(solution)/shard_map/counts/pallas_call | solution.py:118
  53.7 4.3 %experts.4 = (bf16[256,1024]{1,0:T(8,128)(2,1)S(1)}, bf16[256,2048]{1,0:T(8,128)(2,1)S(1)}, bf16[256,1024]{1,0:T(8,128)(2,1)S(1)}, f32[4,64,1152]{2,1,0:T(8,128)S(1)}, f32[4,64,1024]{2,1,0:T(8,128)S(1)}) custom-call(s32[1]{0:T(128)} %bitcast.5.base_ref, bf16[4,64,1024]{2,1,0:T(8,128)(2,1)S(1)} %together.3.x_ref.a0, bf16[64,1152]{1,0:T(8,128)(2,1)S(1)} %copy-done.3, ...), custom_call_target="tpu_custom_call" | custom-call | flops 3355443200 | tf_op jit(solution)/shard_map/experts/pallas_call | solution.py:349
  59.0 6.1 %experts.5 = (bf16[256,1024]{1,0:T(8,128)(2,1)S(1)}, bf16[256,2048]{1,0:T(8,128)(2,1)S(1)}, bf16[256,1024]{1,0:T(8,128)(2,1)S(1)}, bf16[4,64,1152]{2,1,0:T(8,128)(2,1)}, bf16[4,64,1024]{2,1,0:T(8,128)(2,1)S(1)}) custom-call(s32[1]{0:T(128)} %bitcast.5.base_ref, bf16[4,64,1024]{2,1,0:T(8,128)(2,1)S(1)} %collective-permute-done.13.x_ref.a1, ...), custom_call_target="tpu_custom_call" | custom-call | flops 3355443200 | tf_op jit(solution)/shard_map/experts/pallas_call | solution.py:349
  66.4 6.4 %experts.6 = (bf16[256,1024]{1,0:T(8,128)(2,1)S(1)}, bf16[256,2048]{1,0:T(8,128)(2,1)S(1)}, bf16[256,1024]{1,0:T(8,128)(2,1)S(1)}, bf16[4,64,1152]{2,1,0:T(8,128)(2,1)}, bf16[4,64,1024]{2,1,0:T(8,128)(2,1)S(1)}) custom-call(s32[1]{0:T(128)} %bitcast.5.base_ref, bf16[4,64,1024]{2,1,0:T(8,128)(2,1)S(1)} %collective-permute-done.14.x_ref.a2, ...), custom_call_target="tpu_custom_call" | custom-call | flops 3355443200 | tf_op jit(solution)/shard_map/experts/pallas_call | solution.py:349
  74.9 4.8 %experts.7 = (bf16[256,1024]{1,0:T(8,128)(2,1)S(1)}, bf16[256,2048]{1,0:T(8,128)(2,1)S(1)}, bf16[256,1024]{1,0:T(8,128)(2,1)S(1)}, f32[64,1152]{1,0:T(8,128)S(1)...) custom-call(s32[1]{0:T(128)} %bitcast.5.base_ref, ...), custom_call_target="tpu_custom_call" | custom-call | flops 3355443200 | tf_op jit(solution)/shard_map/experts/pallas_call | solution.py:349
  80.5 8.6 %collective-permute-start.18 = (bf16[64,1152]{1,0:T(8,128)(2,1)}, bf16[64,1152]{1,0:T(8,128)(2,1)}, u32[]{:S(2)}, u32[]{:S(2)}) collective-permute-start(bf16[64,1152]{1,0:T(8,128)(2,1)} %get-tuple-element.211), channel_id=1, source_target_pairs={{0,4},{4,0},{8,12},{12,8},{1,5},{5,1},{9,13},{13,9},{2,6},{6,2},{1... | collective-permute-start | bytes 442376 | tf_op jit(solution)/shard_map/ppermute | solution.py:41
  89.1 1.9 collective-permute-start.19
  92.6 10.6 %expert_grads.1.mine_ref = bf16[8,3072,128]{2,1,0:T(8,128)(2,1)} custom-call(bf16[256,1024]{1,0:T(8,128)(2,1)S(1)} %bitcast.20, bf16[256,1024]{1,0:T(8,128)(2,1)S(1)} %bitcast.28, bf16[256,1024]{1,0:T(8,128)(2,1)S(1)} %bitcast.29, bf16[256,1024]{1,0:T(8,128)(2,1)S(1)} %bitcast.30, bf16[256,2048]{1,0:T(8,128)(2,1)S(1)} %get-tuple-element.197.refs_4_, ...), custom_call_target="tpu_custom_call" | custom-call | flops 644245094400 | tf_op jit(solution)/shard_map/expert_grads/pallas_call | solution.py:422
  106.2 3.2 %collective-permute-start.23 = (bf16[64,1152]{1,0:T(8,128)(2,1)S(1)}, bf16[64,1152]{1,0:T(8,128)(2,1)S(1)}, u32[]{:S(2)}, u32[]{:S(2)}) collective-permute-start(bf16[64,1152]{1,0:T(8,128)(2,1)S(1)} %through.1), channel_id=1, source_target_pairs={{0,3},{1,2},{2,1},{3,0},{4,7},{5,6},{6,5},{7,4},{8,11},{9,10},{10,... | collective-permute-start | bytes 442376 | tf_op jit(solution)/shard_map/ppermute | solution.py:41
  110.0 2.3 %collective-permute-start.25 = (bf16[64,1152]{1,0:T(8,128)(2,1)S(1)}, bf16[64,1152]{1,0:T(8,128)(2,1)S(1)}, u32[]{:S(2)}, u32[]{:S(2)}) collective-permute-start(bf16[64,1152]{1,0:T(8,128)(2,1)S(1)} %get-tuple-element.227), channel_id=1, source_target_pairs={{0,8},{4,12},{8,0},{12,4},{1,9},{5,13},{9,1},{13,5},{2,10},{6,14},... | collective-permute-start | bytes 442376 | tf_op jit(solution)/shard_map/ppermute | solution.py:41
  112.3 2.7 %collective-permute-done.23.refs_1_ = bf16[64,1152]{1,0:T(8,128)(2,1)S(1)} collective-permute-done((bf16[64,1152]{1,0:T(8,128)(2,1)S(1)}, bf16[64,1152]{1,0:T(8,128)(2,1)S(1)}, u32[]{:S(2)}, u32[]{:S(2)}) %collective-permute-start.23) | collective-permute-done | bytes 147488 | tf_op jit(solution)/shard_map/ppermute | solution.py:41
  115.1 2.6 %collective-permute-start.26 = (bf16[64,1152]{1,0:T(8,128)(2,1)S(1)}, bf16[64,1152]{1,0:T(8,128)(2,1)S(1)}, u32[]{:S(2)}, u32[]{:S(2)}) collective-permute-start(bf16[64,1152]{1,0:T(8,128)(2,1)S(1)} %get-tuple-element.228), channel_id=1, source_target_pairs={{0,12},{4,8},{8,4},{12,0},{1,13},{5,9},{9,5},{13,1},{2,14},{6,10},... | collective-permute-start | bytes 442376 | tf_op jit(solution)/shard_map/ppermute | solution.py:41
  117.7 4.3 %collective-permute-done.26.refs_4_ = bf16[64,1152]{1,0:T(8,128)(2,1)S(1)} collective-permute-done((bf16[64,1152]{1,0:T(8,128)(2,1)S(1)}, bf16[64,1152]{1,0:T(8,128)(2,1)S(1)}, u32[]{:S(2)}, u32[]{:S(2)}) %collective-permute-start.26) | collective-permute-done | bytes 147488 | tf_op jit(solution)/shard_map/ppermute | solution.py:41
  124.5 2.0 collective-permute-start.29
  128.2 2.6 %collective-permute-done.28.w1 = bf16[64,1152]{1,0:T(8,128)(2,1)S(1)} collective-permute-done((bf16[64,1152]{1,0:T(8,128)(2,1)S(1)}, bf16[64,1152]{1,0:T(8,128)(2,1)S(1)}, u32[]{:S(2)}, u32[]{:S(2)}) %collective-permute-start.28) | collective-permute-done | bytes 147488 | tf_op jit(solution)/shard_map/ppermute | solution.py:41
  130.8 2.4 %collective-permute-done.29.w2 = bf16[64,1152]{1,0:T(8,128)(2,1)S(1)} collective-permute-done((bf16[64,1152]{1,0:T(8,128)(2,1)S(1)}, bf16[64,1152]{1,0:T(8,128)(2,1)S(1)}, u32[]{:S(2)}, u32[]{:S(2)}) %collective-permute-start.29) | collective-permute-done | bytes 147488 | tf_op jit(solution)/shard_map/ppermute | solution.py:41
  133.2 1.7 collective-permute-done.30.w3
  135.6 7.5 %attend_back.1 = (f32[8,1024]{1,0:T(8,128)}, f32[64,1024]{1,0:T(8,128)}, bf16[64,1024]{1,0:T(8,128)(2,1)}, bf16[64,1024]{1,0:T(8,128)(2,1)}, bf16[64,1024]{1,0:T...) custom-call(s32[2]{0:T(128)} %pad_add_fusion.me_ref, bf16[64,1152]{1,0:T(8,128)(2,1)} %copy-done.32, ...), custom_call_target="tpu_custom_call" | custom-call | flops 53687091200 | tf_op jit(solution)/shard_map/attend_back/pallas_call | solution.py:118
  143.6 2.2 %collective-permute-done.32.small_got_ref = f32[8,1024]{1,0:T(8,128)S(1)} collective-permute-done((f32[8,1024]{1,0:T(8,128)}, f32[8,1024]{1,0:T(8,128)S(1)}, u32[]{:S(2)}, u32[]{:S(2)}) %collective-permute-start.32) | collective-permute-done | bytes 32800 | tf_op jit(solution)/shard_map/ppermute | solution.py:41
  146.8 2.9 %dense_dealt.1 = (f32[128,896]{1,0:T(8,128)}, bf16[128,896]{1,0:T(8,128)(2,1)}, bf16[128,896]{1,0:T(8,128)(2,1)}, bf16[128,896]{1,0:T(8,128)(2,1)}, f32[8,1024]{1,0:T(8,128)}) custom-call(s32[1]{0:T(128)} %bitcast.11.me_ref, f32[512,896]{1,0:T(8,128)} %get-tuple-element.253.kept_ref, bf16[512,896]{1,0:T(8,128)(2,1)} %copy-done.34, ...), custom_call_target="tpu_custom_call" | custom-call | tf_op jit(solution)/shard_map/dense_dealt/pallas_call | solution.py:118
  150.2 1.8 collective-permute-start.35
  153.2 11.1 %both_copies.1 = (f32[8,1024,128]{2,1,0:T(8,128)}, f32[8,1024,128]{2,1,0:T(8,128)}, f32[8,128,1024]{2,1,0:T(8,128)}) custom-call(bf16[8,3072,128]{2,1,0:T(8,128)(2,1)} %expert_grads.1.mine_ref, bf16[8,3072,128]{2,1,0:T(8,128)(2,1)} %collective-permute-done.27.other_ref), custom_call_target="tpu_custom_call" | custom-call | bytes 25165824 | tf_op jit(solution)/shard_map/both_copies/pallas_call | solution.py:451
  164.5 1.9 collective-permute-start.42
  166.3 3.0 %collective-permute-start.40 = (bf16[128,896]{1,0:T(8,128)(2,1)S(1)}, bf16[128,896]{1,0:T(8,128)(2,1)S(1)}, u32[]{:S(2)}, u32[]{:S(2)}) collective-permute-start(bf16[128,896]{1,0:T(8,128)(2,1)S(1)} %copy-done.43), channel_id=1, source_target_pairs={{0,8},{4,12},{8,0},{12,4},{1,9},{5,13},{9,1},{13,5},{2,10},{6,14},... | collective-permute-start | bytes 688136 | tf_op jit(solution)/shard_map/ppermute | solution.py:41
  170.7 2.1 input_grad.1.refs_0_
  174.5 5.6 %collective-permute-done.42.refs_3_ = bf16[4,64,1024]{2,1,0:T(8,128)(2,1)S(1)} collective-permute-done((bf16[4,64,1024]{2,1,0:T(8,128)(2,1)S(1)}, bf16[4,64,1024]{2,1,0:T(8,128)(2,1)S(1)}, u32[]{:S(2)}, u32[]{:S(2)}) %collective-permute-start.42) | collective-permute-done | bytes 524320 | tf_op jit(solution)/shard_map/ppermute | solution.py:41
  180.0 1.8 collective-permute-start.39
  182.0 2.9 %collective-permute-done.40.refs_1_ = bf16[128,896]{1,0:T(8,128)(2,1)S(1)} collective-permute-done((bf16[128,896]{1,0:T(8,128)(2,1)S(1)}, bf16[128,896]{1,0:T(8,128)(2,1)S(1)}, u32[]{:S(2)}, u32[]{:S(2)}) %collective-permute-start.40) | collective-permute-done | bytes 229408 | tf_op jit(solution)/shard_map/ppermute | solution.py:41
  184.9 5.8 %collective-permute-start.44 = (bf16[64,1024]{1,0:T(8,128)(2,1)S(1)}, bf16[64,1024]{1,0:T(8,128)(2,1)S(1)}, u32[]{:S(2)}, u32[]{:S(2)}) collective-permute-start(bf16[64,1024]{1,0:T(8,128)(2,1)S(1)} %get-tuple-element.279), channel_id=1, source_target_pairs={{0,8},{4,12},{8,0},{12,4},{1,9},{5,13},{9,1},{13,5},{2,10},{6,14},... | collective-permute-start | bytes 393224 | tf_op jit(solution)/shard_map/ppermute | solution.py:41
  192.4 7.1 %collective-permute-done.44.refs_2_ = bf16[64,1024]{1,0:T(8,128)(2,1)S(1)} collective-permute-done((bf16[64,1024]{1,0:T(8,128)(2,1)S(1)}, bf16[64,1024]{1,0:T(8,128)(2,1)S(1)}, u32[]{:S(2)}, u32[]{:S(2)}) %collective-permute-start.44) | collective-permute-done | bytes 131104 | tf_op jit(solution)/shard_map/ppermute | solution.py:41
  201.4 1.8 collective-permute-start.48
  204.9 1.9 collective-permute-done.46.refs_1_
  206.8 2.3 %collective-permute-done.47.refs_2_ = bf16[80,1024]{1,0:T(8,128)(2,1)S(1)} collective-permute-done((bf16[80,1024]{1,0:T(8,128)(2,1)S(1)}, bf16[80,1024]{1,0:T(8,128)(2,1)S(1)}, u32[]{:S(2)}, u32[]{:S(2)}) %collective-permute-start.47) | collective-permute-done | bytes 163872 | tf_op jit(solution)/shard_map/ppermute | solution.py:41
  (173 shorter events, 41.7 us)
Async XLA Ops:
  2.8 9.1 %collective-permute-start = (bf16[64,1152]{1,0:T(8,128)(2,1)}, bf16[64,1152]{1,0:T(8,128)(2,1)S(1)}, u32[]{:S(2)}, u32[]{:S(2)}) collective-permute-start(bf16[64,1152]{1,0:T(8,128)(2,1)} %get-tuple-element.154.refs_0_.own_ref.cot_ref), channel_id=1, source_target_pairs={{0,4},{4,0},{8,12},{12,8},{1,5},{5,1},{9,13},{13,9},{2,6},{6,2},{1... | collective-permute-start | bytes 442376 | tf_op jit(solution)/shard_map/ppermute | solution.py:41
  5.8 22.7 %collective-permute-start.4 = (bf16[64,1152]{1,0:T(8,128)(2,1)}, bf16[64,1152]{1,0:T(8,128)(2,1)S(1)}, u32[]{:S(2)}, u32[]{:S(2)}) collective-permute-start(bf16[64,1152]{1,0:T(8,128)(2,1)} %get-tuple-element.154.refs_0_.own_ref.cot_ref), channel_id=1, source_target_pairs={{0,8},{4,12},{8,0},{12,4},{1,9},{5,13},{9,1},{13,5},{2,10},{6,14},... | collective-permute-start | bytes 442376 | tf_op jit(solution)/shard_map/ppermute | solution.py:41
  8.4 20.1 %collective-permute-start.5 = (bf16[64,1152]{1,0:T(8,128)(2,1)}, bf16[64,1152]{1,0:T(8,128)(2,1)S(1)}, u32[]{:S(2)}, u32[]{:S(2)}) collective-permute-start(bf16[64,1152]{1,0:T(8,128)(2,1)} %get-tuple-element.154.refs_0_.own_ref.cot_ref), channel_id=1, source_target_pairs={{0,12},{4,8},{8,4},{12,0},{1,13},{5,9},{9,5},{13,1},{2,14},{6,10},... | collective-permute-start | bytes 442376 | tf_op jit(solution)/shard_map/ppermute | solution.py:41
  16.5 5.2 %collective-permute-start.1 = (bf16[64,1024]{1,0:T(8,128)(2,1)}, bf16[64,1024]{1,0:T(8,128)(2,1)S(1)}, u32[]{:S(2)}, u32[]{:S(2)}) collective-permute-start(bf16[64,1024]{1,0:T(8,128)(2,1)} %get-tuple-element.158), channel_id=1, source_target_pairs={{0,1},{1,0},{2,3},{3,2},{4,5},{5,4},{6,7},{7,6},{8,9},{9,8},{10,11... | collective-permute-start | bytes 393224 | tf_op jit(solution)/shard_map/ppermute | solution.py:41
  18.3 5.2 %collective-permute-start.2 = (bf16[64,1024]{1,0:T(8,128)(2,1)}, bf16[64,1024]{1,0:T(8,128)(2,1)S(1)}, u32[]{:S(2)}, u32[]{:S(2)}) collective-permute-start(bf16[64,1024]{1,0:T(8,128)(2,1)} %get-tuple-element.159), channel_id=1, source_target_pairs={{0,2},{1,3},{2,0},{3,1},{4,6},{5,7},{6,4},{7,5},{8,10},{9,11},{10,... | collective-permute-start | bytes 393224 | tf_op jit(solution)/shard_map/ppermute | solution.py:41
  19.8 6.1 %collective-permute-start.3 = (bf16[64,1024]{1,0:T(8,128)(2,1)}, bf16[64,1024]{1,0:T(8,128)(2,1)S(1)}, u32[]{:S(2)}, u32[]{:S(2)}) collective-permute-start(bf16[64,1024]{1,0:T(8,128)(2,1)} %get-tuple-element.160), channel_id=1, source_target_pairs={{0,3},{1,2},{2,1},{3,0},{4,7},{5,6},{6,5},{7,4},{8,11},{9,10},{10,... | collective-permute-start | bytes 393224 | tf_op jit(solution)/shard_map/ppermute | solution.py:41
  28.5 5.2 %collective-permute-start.8 = (bf16[64,1024]{1,0:T(8,128)(2,1)}, bf16[64,1024]{1,0:T(8,128)(2,1)S(1)}, u32[]{:S(2)}, u32[]{:S(2)}) collective-permute-start(bf16[64,1024]{1,0:T(8,128)(2,1)} %get-tuple-element.164.refs_0_.n_ref), channel_id=1, source_target_pairs={{0,4},{4,0},{8,12},{12,8},{1,5},{5,1},{9,13},{13,9},{2,6},{6,2},{1... | collective-permute-start | bytes 393224 | tf_op jit(solution)/shard_map/ppermute | solution.py:41
  28.9 22.3 %collective-permute-start.6 = (bf16[3,64,1152]{2,1,0:T(8,128)(2,1)S(1)}, bf16[3,64,1152]{2,1,0:T(8,128)(2,1)}, u32[]{:S(2)}, u32[]{:S(2)}) collective-permute-start(bf16[3,64,1152]{2,1,0:T(8,128)(2,1)S(1)} %together.2.refs_4_.far_ref), channel_id=1, source_target_pairs={{0,1},{1,0},{2,3},{3,2},{4,5},{5,4},{6,7},{7,6},{8,9},{9,8},{10,11... | collective-permute-start | bytes 1327112 | tf_op jit(solution)/shard_map/ppermute | solution.py:41
  29.6 21.7 %collective-permute-start.7 = (bf16[3,64,1152]{2,1,0:T(8,128)(2,1)S(1)}, bf16[3,64,1152]{2,1,0:T(8,128)(2,1)}, u32[]{:S(2)}, u32[]{:S(2)}) collective-permute-start(bf16[3,64,1152]{2,1,0:T(8,128)(2,1)S(1)} %together.2.refs_4_.far_ref), channel_id=1, source_target_pairs={{0,2},{1,3},{2,0},{3,1},{4,6},{5,7},{6,4},{7,5},{8,10},{9,11},{10,... | collective-permute-start | bytes 1327112 | tf_op jit(solution)/shard_map/ppermute | solution.py:41
  34.4 16.9 %collective-permute-start.9 = (bf16[3,64,1152]{2,1,0:T(8,128)(2,1)S(1)}, bf16[3,64,1152]{2,1,0:T(8,128)(2,1)S(1)}, u32[]{:S(2)}, u32[]{:S(2)}) collective-permute-start(bf16[3,64,1152]{2,1,0:T(8,128)(2,1)S(1)} %together.2.refs_4_.far_ref), channel_id=1, source_target_pairs={{0,3},{1,2},{2,1},{3,0},{4,7},{5,6},{6,5},{7,4},{8,11},{9,10},{10,... | collective-permute-start | bytes 1327112 | tf_op jit(solution)/shard_map/ppermute | solution.py:41
  34.9 10.1 %collective-permute-start.11 = (bf16[64,1024]{1,0:T(8,128)(2,1)}, bf16[64,1024]{1,0:T(8,128)(2,1)S(1)}, u32[]{:S(2)}, u32[]{:S(2)}) collective-permute-start(bf16[64,1024]{1,0:T(8,128)(2,1)} %get-tuple-element.164.refs_0_.n_ref), channel_id=1, source_target_pairs={{0,8},{4,12},{8,0},{12,4},{1,9},{5,13},{9,1},{13,5},{2,10},{6,14},... | collective-permute-start | bytes 393224 | tf_op jit(solution)/shard_map/ppermute | solution.py:41
  37.5 8.1 %collective-permute-start.12 = (bf16[64,1024]{1,0:T(8,128)(2,1)}, bf16[64,1024]{1,0:T(8,128)(2,1)S(1)}, u32[]{:S(2)}, u32[]{:S(2)}) collective-permute-start(bf16[64,1024]{1,0:T(8,128)(2,1)} %get-tuple-element.164.refs_0_.n_ref), channel_id=1, source_target_pairs={{0,12},{4,8},{8,4},{12,0},{1,13},{5,9},{9,5},{13,1},{2,14},{6,10},... | collective-permute-start | bytes 393224 | tf_op jit(solution)/shard_map/ppermute | solution.py:41
  48.2 10.8 %collective-permute-start.13 = (bf16[4,64,1024]{2,1,0:T(8,128)(2,1)S(1)}, bf16[4,64,1024]{2,1,0:T(8,128)(2,1)S(1)}, u32[]{:S(2)}, u32[]{:S(2)}) collective-permute-start(bf16[4,64,1024]{2,1,0:T(8,128)(2,1)S(1)} %together.3.x_ref.a0), channel_id=1, source_target_pairs={{0,1},{1,0},{2,3},{3,2},{4,5},{5,4},{6,7},{7,6},{8,9},{9,8},{10,11... | collective-permute-start | bytes 1572872 | tf_op jit(solution)/shard_map/ppermute | solution.py:41
  49.7 16.7 %collective-permute-start.14 = (bf16[4,64,1024]{2,1,0:T(8,128)(2,1)S(1)}, bf16[4,64,1024]{2,1,0:T(8,128)(2,1)S(1)}, u32[]{:S(2)}, u32[]{:S(2)}) collective-permute-start(bf16[4,64,1024]{2,1,0:T(8,128)(2,1)S(1)} %together.3.x_ref.a0), channel_id=1, source_target_pairs={{0,2},{1,3},{2,0},{3,1},{4,6},{5,7},{6,4},{7,5},{8,10},{9,11},{10,... | collective-permute-start | bytes 1572872 | tf_op jit(solution)/shard_map/ppermute | solution.py:41
  53.6 5.0 %collective-permute-start.10 = (f32[1,128]{1,0:T(1,128)S(1)}, f32[1,128]{1,0:T(1,128)S(1)}, u32[]{:S(2)}, u32[]{:S(2)}) collective-permute-start(f32[1,128]{1,0:T(1,128)S(1)} %counts.1), channel_id=1, source_target_pairs={{0,16},{16,0},{1,17},{17,1},{2,18},{18,2},{3,19},{19,3},{4,20},{20... | collective-permute-start | bytes 1544 | tf_op jit(solution)/shard_map/ppermute | solution.py:41
  58.0 16.9 %collective-permute-start.15 = (bf16[4,64,1024]{2,1,0:T(8,128)(2,1)S(1)}, bf16[4,64,1024]{2,1,0:T(8,128)(2,1)S(1)}, u32[]{:S(2)}, u32[]{:S(2)}) collective-permute-start(bf16[4,64,1024]{2,1,0:T(8,128)(2,1)S(1)} %together.3.x_ref.a0), channel_id=1, source_target_pairs={{0,3},{1,2},{2,1},{3,0},{4,7},{5,6},{6,5},{7,4},{8,11},{9,10},{10,... | collective-permute-start | bytes 1572872 | tf_op jit(solution)/shard_map/ppermute | solution.py:41
  65.1 38.1 %collective-permute-start.16 = (bf16[4,64,1152]{2,1,0:T(8,128)(2,1)}, bf16[4,64,1152]{2,1,0:T(8,128)(2,1)}, u32[]{:S(2)}, u32[]{:S(2)}) collective-permute-start(bf16[4,64,1152]{2,1,0:T(8,128)(2,1)} %get-tuple-element.184), channel_id=1, source_target_pairs={{0,1},{1,0},{2,3},{3,2},{4,5},{5,4},{6,7},{7,6},{8,9},{9,8},{10,11... | collective-permute-start | bytes 1769480 | tf_op jit(solution)/shard_map/ppermute | solution.py:41
  73.5 29.7 %collective-permute-start.17 = (bf16[4,64,1152]{2,1,0:T(8,128)(2,1)}, bf16[4,64,1152]{2,1,0:T(8,128)(2,1)}, u32[]{:S(2)}, u32[]{:S(2)}) collective-permute-start(bf16[4,64,1152]{2,1,0:T(8,128)(2,1)} %get-tuple-element.191), channel_id=1, source_target_pairs={{0,2},{1,3},{2,0},{3,1},{4,6},{5,7},{6,4},{7,5},{8,10},{9,11},{10,... | collective-permute-start | bytes 1769480 | tf_op jit(solution)/shard_map/ppermute | solution.py:41
  80.5 22.7 %collective-permute-start.18 = (bf16[64,1152]{1,0:T(8,128)(2,1)}, bf16[64,1152]{1,0:T(8,128)(2,1)}, u32[]{:S(2)}, u32[]{:S(2)}) collective-permute-start(bf16[64,1152]{1,0:T(8,128)(2,1)} %get-tuple-element.211), channel_id=1, source_target_pairs={{0,4},{4,0},{8,12},{12,8},{1,5},{5,1},{9,13},{13,9},{2,6},{6,2},{1... | collective-permute-start | bytes 442376 | tf_op jit(solution)/shard_map/ppermute | solution.py:41
  89.1 14.1 %collective-permute-start.19 = (bf16[64,1152]{1,0:T(8,128)(2,1)}, bf16[64,1152]{1,0:T(8,128)(2,1)}, u32[]{:S(2)}, u32[]{:S(2)}) collective-permute-start(bf16[64,1152]{1,0:T(8,128)(2,1)} %get-tuple-element.212), channel_id=1, source_target_pairs={{0,8},{4,12},{8,0},{12,4},{1,9},{5,13},{9,1},{13,5},{2,10},{6,14},... | collective-permute-start | bytes 442376 | tf_op jit(solution)/shard_map/ppermute | solution.py:41
  91.0 12.2 %collective-permute-start.20 = (bf16[64,1152]{1,0:T(8,128)(2,1)}, bf16[64,1152]{1,0:T(8,128)(2,1)}, u32[]{:S(2)}, u32[]{:S(2)}) collective-permute-start(bf16[64,1152]{1,0:T(8,128)(2,1)} %get-tuple-element.213), channel_id=1, source_target_pairs={{0,12},{4,8},{8,4},{12,0},{1,13},{5,9},{9,5},{13,1},{2,14},{6,10},... | collective-permute-start | bytes 442376 | tf_op jit(solution)/shard_map/ppermute | solution.py:41
  104.7 17.3 %collective-permute-start.21 = (bf16[4,64,1024]{2,1,0:T(8,128)(2,1)S(1)}, bf16[4,64,1024]{2,1,0:T(8,128)(2,1)S(1)}, u32[]{:S(2)}, u32[]{:S(2)}) collective-permute-start(bf16[4,64,1024]{2,1,0:T(8,128)(2,1)S(1)} %get-tuple-element.219), channel_id=1, source_target_pairs={{0,1},{1,0},{2,3},{3,2},{4,5},{5,4},{6,7},{7,6},{8,9},{9,8},{10,11... | collective-permute-start | bytes 1572872 | tf_op jit(solution)/shard_map/ppermute | solution.py:41
  105.1 16.9 %collective-permute-start.22 = (bf16[4,64,1024]{2,1,0:T(8,128)(2,1)S(1)}, bf16[4,64,1024]{2,1,0:T(8,128)(2,1)S(1)}, u32[]{:S(2)}, u32[]{:S(2)}) collective-permute-start(bf16[4,64,1024]{2,1,0:T(8,128)(2,1)S(1)} %copy-done.31), channel_id=1, source_target_pairs={{0,2},{1,3},{2,0},{3,1},{4,6},{5,7},{6,4},{7,5},{8,10},{9,11},{10,... | collective-permute-start | bytes 1572872 | tf_op jit(solution)/shard_map/ppermute | solution.py:41
  106.2 8.8 %collective-permute-start.23 = (bf16[64,1152]{1,0:T(8,128)(2,1)S(1)}, bf16[64,1152]{1,0:T(8,128)(2,1)S(1)}, u32[]{:S(2)}, u32[]{:S(2)}) collective-permute-start(bf16[64,1152]{1,0:T(8,128)(2,1)S(1)} %through.1), channel_id=1, source_target_pairs={{0,3},{1,2},{2,1},{3,0},{4,7},{5,6},{6,5},{7,4},{8,11},{9,10},{10,... | collective-permute-start | bytes 442376 | tf_op jit(solution)/shard_map/ppermute | solution.py:41
  109.4 8.3 %collective-permute-start.24 = (bf16[64,1152]{1,0:T(8,128)(2,1)S(1)}, bf16[64,1152]{1,0:T(8,128)(2,1)S(1)}, u32[]{:S(2)}, u32[]{:S(2)}) collective-permute-start(bf16[64,1152]{1,0:T(8,128)(2,1)S(1)} %get-tuple-element.226), channel_id=1, source_target_pairs={{0,4},{4,0},{8,12},{12,8},{1,5},{5,1},{9,13},{13,9},{2,6},{6,2},{1... | collective-permute-start | bytes 442376 | tf_op jit(solution)/shard_map/ppermute | solution.py:41
  110.0 7.7 %collective-permute-start.25 = (bf16[64,1152]{1,0:T(8,128)(2,1)S(1)}, bf16[64,1152]{1,0:T(8,128)(2,1)S(1)}, u32[]{:S(2)}, u32[]{:S(2)}) collective-permute-start(bf16[64,1152]{1,0:T(8,128)(2,1)S(1)} %get-tuple-element.227), channel_id=1, source_target_pairs={{0,8},{4,12},{8,0},{12,4},{1,9},{5,13},{9,1},{13,5},{2,10},{6,14},... | collective-permute-start | bytes 442376 | tf_op jit(solution)/shard_map/ppermute | solution.py:41
  115.1 6.9 %collective-permute-start.26 = (bf16[64,1152]{1,0:T(8,128)(2,1)S(1)}, bf16[64,1152]{1,0:T(8,128)(2,1)S(1)}, u32[]{:S(2)}, u32[]{:S(2)}) collective-permute-start(bf16[64,1152]{1,0:T(8,128)(2,1)S(1)} %get-tuple-element.228), channel_id=1, source_target_pairs={{0,12},{4,8},{8,4},{12,0},{1,13},{5,9},{9,5},{13,1},{2,14},{6,10},... | collective-permute-start | bytes 442376 | tf_op jit(solution)/shard_map/ppermute | solution.py:41
  124.1 10.8 %collective-permute-start.27 = (bf16[8,3072,128]{2,1,0:T(8,128)(2,1)}, bf16[8,3072,128]{2,1,0:T(8,128)(2,1)}, u32[]{:S(2)}, u32[]{:S(2)}) collective-permute-start(bf16[8,3072,128]{2,1,0:T(8,128)(2,1)} %expert_grads.1.mine_ref), channel_id=1, source_target_pairs={{0,16},{16,0},{1,17},{17,1},{2,18},{18,2},{3,19},{19,3},{4,20},{20... | collective-permute-start | bytes 18874376 | tf_op jit(solution)/shard_map/ppermute | solution.py:41
  124.1 6.6 %collective-permute-start.28 = (bf16[64,1152]{1,0:T(8,128)(2,1)S(1)}, bf16[64,1152]{1,0:T(8,128)(2,1)S(1)}, u32[]{:S(2)}, u32[]{:S(2)}) collective-permute-start(bf16[64,1152]{1,0:T(8,128)(2,1)S(1)} %get-tuple-element.242.w0), channel_id=1, source_target_pairs={{0,1},{1,0},{2,3},{3,2},{4,5},{5,4},{6,7},{7,6},{8,9},{9,8},{10,11... | collective-permute-start | bytes 442376 | tf_op jit(solution)/shard_map/ppermute | solution.py:41
  124.5 8.7 %collective-permute-start.29 = (bf16[64,1152]{1,0:T(8,128)(2,1)S(1)}, bf16[64,1152]{1,0:T(8,128)(2,1)S(1)}, u32[]{:S(2)}, u32[]{:S(2)}) collective-permute-start(bf16[64,1152]{1,0:T(8,128)(2,1)S(1)} %get-tuple-element.242.w0), channel_id=1, source_target_pairs={{0,2},{1,3},{2,0},{3,1},{4,6},{5,7},{6,4},{7,5},{8,10},{9,11},{10,... | collective-permute-start | bytes 442376 | tf_op jit(solution)/shard_map/ppermute | solution.py:41
  126.5 8.4 %collective-permute-start.30 = (bf16[64,1152]{1,0:T(8,128)(2,1)S(1)}, bf16[64,1152]{1,0:T(8,128)(2,1)S(1)}, u32[]{:S(2)}, u32[]{:S(2)}) collective-permute-start(bf16[64,1152]{1,0:T(8,128)(2,1)S(1)} %get-tuple-element.242.w0), channel_id=1, source_target_pairs={{0,3},{1,2},{2,1},{3,0},{4,7},{5,6},{6,5},{7,4},{8,11},{9,10},{10,... | collective-permute-start | bytes 442376 | tf_op jit(solution)/shard_map/ppermute | solution.py:41
  143.0 2.8 %collective-permute-start.31 = (bf16[512,896]{1,0:T(8,128)(2,1)}, bf16[512,896]{1,0:T(8,128)(2,1)S(1)}, u32[]{:S(2)}, u32[]{:S(2)}) collective-permute-start(bf16[512,896]{1,0:T(8,128)(2,1)} %get-tuple-element.254), channel_id=1, source_target_pairs={{0,16},{16,0},{1,17},{17,1},{2,18},{18,2},{3,19},{19,3},{4,20},{20... | collective-permute-start | bytes 2752520 | tf_op jit(solution)/shard_map/ppermute | solution.py:41
  149.6 14.8 %collective-permute-start.33 = (bf16[128,896]{1,0:T(8,128)(2,1)}, bf16[128,896]{1,0:T(8,128)(2,1)S(1)}, u32[]{:S(2)}, u32[]{:S(2)}) collective-permute-start(bf16[128,896]{1,0:T(8,128)(2,1)} %get-tuple-element.256), channel_id=1, source_target_pairs={{0,4},{4,0},{8,12},{12,8},{1,5},{5,1},{9,13},{13,9},{2,6},{6,2},{1... | collective-permute-start | bytes 688136 | tf_op jit(solution)/shard_map/ppermute | solution.py:41
  149.6 14.7 %collective-permute-start.34 = (bf16[64,1024]{1,0:T(8,128)(2,1)}, bf16[64,1024]{1,0:T(8,128)(2,1)S(1)}, u32[]{:S(2)}, u32[]{:S(2)}) collective-permute-start(bf16[64,1024]{1,0:T(8,128)(2,1)} %get-tuple-element.258), channel_id=1, source_target_pairs={{0,1},{1,0},{2,3},{3,2},{4,5},{5,4},{6,7},{7,6},{8,9},{9,8},{10,11... | collective-permute-start | bytes 393224 | tf_op jit(solution)/shard_map/ppermute | solution.py:41
  150.2 14.2 %collective-permute-start.35 = (bf16[64,1024]{1,0:T(8,128)(2,1)}, bf16[64,1024]{1,0:T(8,128)(2,1)S(1)}, u32[]{:S(2)}, u32[]{:S(2)}) collective-permute-start(bf16[64,1024]{1,0:T(8,128)(2,1)} %get-tuple-element.259), channel_id=1, source_target_pairs={{0,2},{1,3},{2,0},{3,1},{4,6},{5,7},{6,4},{7,5},{8,10},{9,11},{10,... | collective-permute-start | bytes 393224 | tf_op jit(solution)/shard_map/ppermute | solution.py:41
  152.0 12.4 %collective-permute-start.36 = (bf16[64,1024]{1,0:T(8,128)(2,1)}, bf16[64,1024]{1,0:T(8,128)(2,1)S(1)}, u32[]{:S(2)}, u32[]{:S(2)}) collective-permute-start(bf16[64,1024]{1,0:T(8,128)(2,1)} %get-tuple-element.260), channel_id=1, source_target_pairs={{0,3},{1,2},{2,1},{3,0},{4,7},{5,6},{6,5},{7,4},{8,11},{9,10},{10,... | collective-permute-start | bytes 393224 | tf_op jit(solution)/shard_map/ppermute | solution.py:41
  164.5 15.6 %collective-permute-start.42 = (bf16[4,64,1024]{2,1,0:T(8,128)(2,1)S(1)}, bf16[4,64,1024]{2,1,0:T(8,128)(2,1)S(1)}, u32[]{:S(2)}, u32[]{:S(2)}) collective-permute-start(bf16[4,64,1024]{2,1,0:T(8,128)(2,1)S(1)} %copy-done.24), channel_id=1, source_target_pairs={{0,3},{1,2},{2,1},{3,0},{4,7},{5,6},{6,5},{7,4},{8,11},{9,10},{10,... | collective-permute-start | bytes 1572872 | tf_op jit(solution)/shard_map/ppermute | solution.py:41
  166.3 18.6 %collective-permute-start.40 = (bf16[128,896]{1,0:T(8,128)(2,1)S(1)}, bf16[128,896]{1,0:T(8,128)(2,1)S(1)}, u32[]{:S(2)}, u32[]{:S(2)}) collective-permute-start(bf16[128,896]{1,0:T(8,128)(2,1)S(1)} %copy-done.43), channel_id=1, source_target_pairs={{0,8},{4,12},{8,0},{12,4},{1,9},{5,13},{9,1},{13,5},{2,10},{6,14},... | collective-permute-start | bytes 688136 | tf_op jit(solution)/shard_map/ppermute | solution.py:41
  169.3 15.6 %collective-permute-start.41 = (bf16[128,896]{1,0:T(8,128)(2,1)S(1)}, bf16[128,896]{1,0:T(8,128)(2,1)S(1)}, u32[]{:S(2)}, u32[]{:S(2)}) collective-permute-start(bf16[128,896]{1,0:T(8,128)(2,1)S(1)} %copy-done.42), channel_id=1, source_target_pairs={{0,12},{4,8},{8,4},{12,0},{1,13},{5,9},{9,5},{13,1},{2,14},{6,10},... | collective-permute-start | bytes 688136 | tf_op jit(solution)/shard_map/ppermute | solution.py:41
  172.8 17.9 %collective-permute-start.37 = (bf16[64,1024]{1,0:T(8,128)(2,1)}, bf16[64,1024]{1,0:T(8,128)(2,1)S(1)}, u32[]{:S(2)}, u32[]{:S(2)}) collective-permute-start(bf16[64,1024]{1,0:T(8,128)(2,1)} %input_grad.1.refs_0_), channel_id=1, source_target_pairs={{0,1},{1,0},{2,3},{3,2},{4,5},{5,4},{6,7},{7,6},{8,9},{9,8},{10,11... | collective-permute-start | bytes 393224 | tf_op jit(solution)/shard_map/ppermute | solution.py:41
  173.5 18.9 %collective-permute-start.38 = (bf16[64,1024]{1,0:T(8,128)(2,1)}, bf16[64,1024]{1,0:T(8,128)(2,1)S(1)}, u32[]{:S(2)}, u32[]{:S(2)}) collective-permute-start(bf16[64,1024]{1,0:T(8,128)(2,1)} %input_grad.1.refs_0_), channel_id=1, source_target_pairs={{0,2},{1,3},{2,0},{3,1},{4,6},{5,7},{6,4},{7,5},{8,10},{9,11},{10,... | collective-permute-start | bytes 393224 | tf_op jit(solution)/shard_map/ppermute | solution.py:41
  180.0 12.3 %collective-permute-start.39 = (bf16[64,1024]{1,0:T(8,128)(2,1)}, bf16[64,1024]{1,0:T(8,128)(2,1)S(1)}, u32[]{:S(2)}, u32[]{:S(2)}) collective-permute-start(bf16[64,1024]{1,0:T(8,128)(2,1)} %input_grad.1.refs_0_), channel_id=1, source_target_pairs={{0,3},{1,2},{2,1},{3,0},{4,7},{5,6},{6,5},{7,4},{8,11},{9,10},{10,... | collective-permute-start | bytes 393224 | tf_op jit(solution)/shard_map/ppermute | solution.py:41
  184.9 7.5 %collective-permute-start.43 = (bf16[64,1024]{1,0:T(8,128)(2,1)S(1)}, bf16[64,1024]{1,0:T(8,128)(2,1)S(1)}, u32[]{:S(2)}, u32[]{:S(2)}) collective-permute-start(bf16[64,1024]{1,0:T(8,128)(2,1)S(1)} %get-tuple-element.278), channel_id=1, source_target_pairs={{0,4},{4,0},{8,12},{12,8},{1,5},{5,1},{9,13},{13,9},{2,6},{6,2},{1... | collective-permute-start | bytes 393224 | tf_op jit(solution)/shard_map/ppermute | solution.py:41
  184.9 14.6 %collective-permute-start.44 = (bf16[64,1024]{1,0:T(8,128)(2,1)S(1)}, bf16[64,1024]{1,0:T(8,128)(2,1)S(1)}, u32[]{:S(2)}, u32[]{:S(2)}) collective-permute-start(bf16[64,1024]{1,0:T(8,128)(2,1)S(1)} %get-tuple-element.279), channel_id=1, source_target_pairs={{0,8},{4,12},{8,0},{12,4},{1,9},{5,13},{9,1},{13,5},{2,10},{6,14},... | collective-permute-start | bytes 393224 | tf_op jit(solution)/shard_map/ppermute | solution.py:41
  190.7 8.8 %collective-permute-start.45 = (bf16[64,1024]{1,0:T(8,128)(2,1)S(1)}, bf16[64,1024]{1,0:T(8,128)(2,1)S(1)}, u32[]{:S(2)}, u32[]{:S(2)}) collective-permute-start(bf16[64,1024]{1,0:T(8,128)(2,1)S(1)} %get-tuple-element.280), channel_id=1, source_target_pairs={{0,12},{4,8},{8,4},{12,0},{1,13},{5,9},{9,5},{13,1},{2,14},{6,10},... | collective-permute-start | bytes 393224 | tf_op jit(solution)/shard_map/ppermute | solution.py:41
  199.6 7.2 %collective-permute-start.46 = (bf16[80,1024]{1,0:T(8,128)(2,1)S(1)}, bf16[80,1024]{1,0:T(8,128)(2,1)S(1)}, u32[]{:S(2)}, u32[]{:S(2)}) collective-permute-start(bf16[80,1024]{1,0:T(8,128)(2,1)S(1)} %out_piece.1.refs_0_), channel_id=1, source_target_pairs={{0,1},{1,0},{2,3},{3,2},{4,5},{5,4},{6,7},{7,6},{8,9},{9,8},{10,11... | collective-permute-start | bytes 491528 | tf_op jit(solution)/shard_map/ppermute | solution.py:41
  200.3 8.8 %collective-permute-start.47 = (bf16[80,1024]{1,0:T(8,128)(2,1)S(1)}, bf16[80,1024]{1,0:T(8,128)(2,1)S(1)}, u32[]{:S(2)}, u32[]{:S(2)}) collective-permute-start(bf16[80,1024]{1,0:T(8,128)(2,1)S(1)} %out_piece.1.refs_0_), channel_id=1, source_target_pairs={{0,2},{1,3},{2,0},{3,1},{4,6},{5,7},{6,4},{7,5},{8,10},{9,11},{10,... | collective-permute-start | bytes 491528 | tf_op jit(solution)/shard_map/ppermute | solution.py:41
  201.4 7.7 %collective-permute-start.48 = (bf16[80,1024]{1,0:T(8,128)(2,1)S(1)}, bf16[80,1024]{1,0:T(8,128)(2,1)S(1)}, u32[]{:S(2)}, u32[]{:S(2)}) collective-permute-start(bf16[80,1024]{1,0:T(8,128)(2,1)S(1)} %out_piece.1.refs_0_), channel_id=1, source_target_pairs={{0,3},{1,2},{2,1},{3,0},{4,7},{5,6},{6,5},{7,4},{8,11},{9,10},{10,... | collective-permute-start | bytes 491528 | tf_op jit(solution)/shard_map/ppermute | solution.py:41
  (48 other events, 528.1 us)

commit v9 on v7

--- a/solution.py
+++ b/solution.py
@@ -41,10 +41,14 @@
     return lax.ppermute(x, axis, [(i, i ^ distance) for i in range(size)])
 
 
+def backwards(make, size):
+    return [make(r) for r in range(size - 1, 0, -1)][::-1]
+
+
 def spread(x, axis):
     size = lax.axis_size(axis)
     if size <= FEW:
-        return [swap(x, axis, r) for r in range(1, size)]
+        return backwards(lambda r: swap(x, axis, r), size)
     whole = lax.all_gather(x, axis)
     order = jnp.arange(1, size) ^ lax.axis_index(axis)
     return list(jnp.take(whole, order, axis=0))
@@ -53,7 +57,7 @@
 def deal(parts, axis):
     size = lax.axis_size(axis)
     if size <= FEW:
-        return [swap(part, axis, r + 1) for r, part in enumerate(parts)]
+        return backwards(lambda r: swap(parts[r - 1], axis, r), size)
     order = jnp.arange(size) ^ lax.axis_index(axis)
     whole = jnp.take(jnp.stack([parts[0], *parts]), order, axis=0)
     back = lax.all_to_all(whole, axis, 0, 0, tiled=True)
@@ -431,33 +435,29 @@
     )(*n, *dgu, *h, *c)
 
 
-def both_copies_kernel(mine_ref, other_ref, gate_ref, up_ref, down_ref):
-    width, hidden = gate_ref.shape[1:]
-
-    def total(at, count):
-        rows = pl.ds(at, count)
-        return mine_ref[0, rows, :].astype(F32) + other_ref[0, rows, :].astype(F32)
-
-    gate_ref[0] = total(0, width)
-    up_ref[0] = total(width, width)
-    for at in range(0, width, hidden):
-        down_ref[0, :, at : at + hidden] = total(2 * width + at, hidden)
-
-
-def both_copies(mine, other):
+def both_copies_kernel(mine_ref, other_ref, out_ref):
+    for e in range(mine_ref.shape[0]):
+        total = mine_ref[e].astype(F32) + other_ref[e].astype(F32)
+        hidden = total.shape[1]
+        if out_ref.shape[2] == hidden:
+            out_ref[e] = total
+        else:
+            for at in range(0, total.shape[0], hidden):
+                out_ref[e, :, at : at + hidden] = total[at : at + hidden]
+
+
+def both_copies(mine, other, which):
     local, rows, hidden = mine.shape
     width = rows // 3
-    block = lambda *dims: pl.BlockSpec((1, *dims), lambda e: (e, 0, 0))
+    dims = (hidden, width) if which == 2 else (width, hidden)
+    step = min(local, 2)
+    block = pl.BlockSpec((step, width, hidden), lambda e: (e, which, 0))
     return pl.pallas_call(
         both_copies_kernel,
-        grid=(local,),
-        in_specs=[block(rows, hidden)] * 2,
-        out_specs=[block(width, hidden), block(width, hidden), block(hidden, width)],
-        out_shape=[
-            shape((local, width, hidden), F32),
-            shape((local, width, hidden), F32),
-            shape((local, hidden, width), F32),
-        ],
+        grid=(local // step,),
+        in_specs=[block, block],
+        out_specs=pl.BlockSpec((step, *dims), lambda e: (e, 0, 0)),
+        out_shape=shape((local, *dims), F32),
         compiler_params=pltpu.CompilerParams(vmem_limit_bytes=58 * MIB),
         cost_estimate=pl.CostEstimate(flops=int(100.0*(0)), bytes_accessed=8 * mine.size, transcendentals=0),
         name="both_copies",
@@ -737,7 +737,7 @@
         flops=2 * seq_len * width * 4 * heads,
     )
     parts = rest
-    got = [swap(parts[r], "tensor", r) for r in around]
+    got = backwards(lambda r: swap(parts[r], "tensor", r), tensor_size)
     h, n_two = call(
         norm_two_kernel,
         [shape((rows, width), F32), shape((rows, width), BF)],
@@ -753,11 +753,11 @@
     wcat = gate_up_weights(w_gate, w_up)
     two_got = spread(n_two, "expert")
     two_got[0], cot_late = tied(two_got[0], cot_far)
-    cot_far = [cot_far] + [swap(cot_far, "tensor", r) for r in range(1, last)]
+    cot_far = [cot_far] + backwards(lambda r: swap(cot_far, "tensor", r), last)
     cot_far.append(swap(cot_late, "tensor", last))
 
     first = together([n_two, *two_got])
-    twos = [first] + [swap(first, "tensor", r) for r in range(1, last)]
+    twos = [first] + backwards(lambda r: swap(first, "tensor", r), last)
     _, late = tied(cot_far[:last], first)
     twos.append(swap(late, "tensor", last))
 
@@ -782,9 +782,10 @@
     grads = run_grads(twos, dgus, hids, cots, local, hidden)
     grads, (got, from_last) = tied(grads, (got, from_last))
     near, *across = split_sum([ds[0], *got], "dn_sum")
-    through = added([near_last, *from_last], BF, "through")
     across[0], middle = tied(across[0], moes[1:last])
     across = deal(across, "expert")
+    across[0], near_last = tied(across[0], near_last)
+    through = added([near_last, *from_last], BF, "through")
     near_sums = [near, swap(through, "tensor", last), *across]
     moe_got = [swap(middle[r - 1], "tensor", r) for r in range(1, last)]
     moe_got, near_sums = tied(moe_got, near_sums)
@@ -797,7 +798,7 @@
         "v",
         "vvv",
     )
-    wides = [wide] + [swap(wide, "tensor", r) for r in around]
+    wides = [wide] + backwards(lambda r: swap(wide, "tensor", r), tensor_size)
     _, late_grads = tied(wide, grads)
     grads_got = swap(late_grads, "dp", 1)
     grads_got, wides = tied(grads_got, wides)
@@ -824,7 +825,7 @@
         ],
         flops=2 * seq_len * width * 4 * heads,
     )
-    part_sums = [back_parts[0]] + [swap(back_parts[r], "tensor", r) for r in around]
+    part_sums = [back_parts[0]] + backwards(lambda r: swap(back_parts[r], "tensor", r), tensor_size)
     half = width // dp_size
     chunk = half // expert_size
 
@@ -855,15 +856,16 @@
         "s",
     )
     others = deal(others, "expert")
-    others[0], part_sums = tied(others[0], part_sums)
+    grad_gate = both_copies(grads, grads_got, 0)
+    (grad_gate, others[0]), part_sums = tied((grad_gate, others[0]), part_sums)
     moe_near, *moe_across = split_sum([moes[0], *moe_got], "moe_sum")
     moe_sums = [moe_near, *deal(moe_across, "expert")]
     ig = call(
         input_grad_kernel, [shape((rows, width), BF)], (xq, gain_one, dh, *part_sums), "input_grad", "bbbb", limit=58
     )[0]
-    igs = [ig] + [swap(ig, "tensor", r) for r in around]
-    expert_grads = both_copies(grads, grads_got)
-    expert_grads, others = tied(expert_grads, others)
+    igs = [ig] + backwards(lambda r: swap(ig, "tensor", r), tensor_size)
+    grad_up = both_copies(grads, grads_got, 1)
+    grad_up, others = tied(grad_up, others)
     g_query, g_key, g_value, g_out, g_router, small = call(
         dense_sum_kernel,
         [
@@ -887,7 +889,9 @@
         natural_kernel, [shape((seq_len, width), F32)], (t_at, *igs), "input_grad_whole", "s", "b"
     )[0]
     out_piece = call(out_kernel, [shape((rows + 16, width), BF)], (h, small, *moe_sums), "out_piece")[0]
-    outs = [out_piece] + [swap(out_piece, "tensor", r) for r in around]
+    outs = [out_piece] + backwards(lambda r: swap(out_piece, "tensor", r), tensor_size)
+    grad_down = both_copies(grads, grads_got, 2)
+    grad_down, outs = tied(grad_down, outs)
     output, small = call(
         out_whole_kernel,
         [shape((seq_len, width), BF), shape((8, width), F32)],
@@ -910,7 +914,9 @@
         g_out,
         lax.dynamic_slice(small, (1, at), (1, chunk))[0],
         g_router[:, :experts],
-        *expert_grads,
+        grad_gate,
+        grad_up,
+        grad_down,
     )
 
 

time: 207 us -> 202 us (0.976)
  starting transfers between devices: 69.9 us -> 64.4 us
  waiting for transfers between devices: 51.3 us -> 48.1 us
  Pallas kernels: 74.9 us -> 78.1 us
    ppermute x49, starting transfers between devices: 69.9 us -> 64.4 us  [swap(): return lax.ppermute(x, axis, [(i, i ^ distance) for i in range(size)])]
    ppermute x49, waiting for transfers between devices: 51.3 us -> 48.1 us  [swap(): return lax.ppermute(x, axis, [(i, i ^ distance) for i in range(size)])]
    pallas_call x1 -> x3, Pallas kernels: 11.1 us -> 14.3 us  [both_copies(): pl.pallas_call(both_copies_kernel, grid=(local // step,), in_specs=[block...]
  transfers between devices with their start and end apart: 49 -> 49, of which waited for: 16 -> 15; matrix products, arithmetic and copies ran while one was open for 1% -> 1% of each run, Pallas kernels for 29% -> 31%
where the time goes in v9:
time: 202 us; the launch traced here: 201 us
  Pallas kernels  78.1 us (39%)
  starting transfers between devices  64.4 us (32%)
  waiting for transfers between devices  48.1 us (24%)
  local copies, waits for them, and re-layouts  8.43 us (4%)
    ppermute x49, starting transfers between devices, swap(): return lax.ppermute(x, axis, [(i, i ^ distance) for i in range(size)])  64.4 us
    ppermute x49, waiting for transfers between devices, swap(): return lax.ppermute(x, axis, [(i, i ^ distance) for i in range(size)])  48.1 us
    pallas_call x18, Pallas kernels, call(): pl.pallas_call(kernel, grid=(1,), out_shape=outs, in_specs=[spec(p, x) fo...  29.4 us
    pallas_call x4, Pallas kernels, run_experts(): pl.pallas_call(kernel, grid=(total // step,), in_specs=[pl.BlockSpec(memo...  22.2 us
    pallas_call x3, Pallas kernels, both_copies(): pl.pallas_call(both_copies_kernel, grid=(local // step,), in_specs=[block...  14.3 us
    pallas_call x1, Pallas kernels, run_grads(): pl.pallas_call(grads_kernel, grid=(local,), in_specs=whole(n) + cols(dgu,...  10.7 us
    unnamed x75, local copies, waits for them, and re-layouts  7.92 us
  transfers between devices with their start and end apart: 49, of which 15 were waited for; matrix products, arithmetic and copies ran while one was open for 1% of the time, Pallas kernels for 31%

profile of v9, /device:TPU:0, one launch (start us, length us, event | category | flops | bytes accessed | tf_op | source)
XLA Modules:
  0.0 201.3 jit_solution(13661499577309833016)
XLA Ops:
  0.6 2.2 %pieces.1 = (bf16[64,1152]{1,0:T(8,128)(2,1)}, bf16[64,1152]{1,0:T(8,128)(2,1)}, bf16[64,1152]{1,0:T(8,128)(2,1)}, bf16[64,1152]{1,0:T(8,128)(2,1)}, bf16[128,1024]{1,0:T(8,128)(2,1)}) custom-call(s32[1]{0:T(128)} %bitcast.me_ref, bf16[256,1024]{1,0:T(8,128)(2,1)} %cot_ref.1, s32[8,256]{1,0:T(8,128)} %bitcast.32, bf16[32,1024]{1,0:T(8,128)(2,1)} %bitcast.31), custom_call_target="tpu_custom_call" | custom-call | tf_op jit(solution)/shard_map/pieces/pallas_call | solution.py:122
  2.8 3.0 %collective-permute-start = (bf16[64,1152]{1,0:T(8,128)(2,1)}, bf16[64,1152]{1,0:T(8,128)(2,1)S(1)}, u32[]{:S(2)}, u32[]{:S(2)}) collective-permute-start(bf16[64,1152]{1,0:T(8,128)(2,1)} %get-tuple-element.166.own_ref.refs_0_.cot_ref), channel_id=1, source_target_pairs={{0,4},{4,0},{8,12},{12,8},{1,5},{5,1},{9,13},{13,9},{2,6},{6,2},{1... | collective-permute-start | bytes 442376 | tf_op jit(solution)/shard_map/ppermute | solution.py:41
  5.8 2.6 %collective-permute-start.4 = (bf16[64,1152]{1,0:T(8,128)(2,1)}, bf16[64,1152]{1,0:T(8,128)(2,1)S(1)}, u32[]{:S(2)}, u32[]{:S(2)}) collective-permute-start(bf16[64,1152]{1,0:T(8,128)(2,1)} %get-tuple-element.166.own_ref.refs_0_.cot_ref), channel_id=1, source_target_pairs={{0,8},{4,12},{8,0},{12,4},{1,9},{5,13},{9,1},{13,5},{2,10},{6,14},... | collective-permute-start | bytes 442376 | tf_op jit(solution)/shard_map/ppermute | solution.py:41
  8.4 3.5 %collective-permute-done.refs_0_ = bf16[64,1152]{1,0:T(8,128)(2,1)S(1)} collective-permute-done((bf16[64,1152]{1,0:T(8,128)(2,1)}, bf16[64,1152]{1,0:T(8,128)(2,1)S(1)}, u32[]{:S(2)}, u32[]{:S(2)}) %collective-permute-start) | collective-permute-done | bytes 147488 | tf_op jit(solution)/shard_map/ppermute | solution.py:41
  11.9 4.7 %attend.1 = (bf16[256,1024]{1,0:T(8,128)(2,1)}, bf16[256,256]{1,0:T(8,128)(2,1)}, bf16[256,128]{1,0:T(8,128)(2,1)}, bf16[256,128]{1,0:T(8,128)(2,1)}, bf16[256,2...) custom-call(s32[1]{0:T(128)} %bitcast.me_ref, ...), custom_call_target="tpu_custom_call" | custom-call | flops 53687091200 | tf_op jit(solution)/shard_map/attend/pallas_call | solution.py:122
  16.6 1.7 collective-permute-start.1
  18.3 1.5 collective-permute-start.2
  20.1 1.7 collective-permute-done.1.refs_0_
  21.8 1.7 collective-permute-done.2.refs_1_
  23.5 2.4 %collective-permute-done.3.refs_2_ = bf16[64,1024]{1,0:T(8,128)(2,1)S(1)} collective-permute-done((bf16[64,1024]{1,0:T(8,128)(2,1)}, bf16[64,1024]{1,0:T(8,128)(2,1)S(1)}, u32[]{:S(2)}, u32[]{:S(2)}) %collective-permute-start.3) | collective-permute-done | bytes 131104 | tf_op jit(solution)/shard_map/ppermute | solution.py:41
  26.5 2.0 %norm_two.1 = (f32[64,1024]{1,0:T(8,128)}, bf16[64,1024]{1,0:T(8,128)(2,1)}) custom-call(bf16[64,1024]{1,0:T(8,128)(2,1)} %get-tuple-element.168.x_ref, f32[1,1024]{1,0:T(1,128)} %bitcast.25, f32[64,1024]{1,0:T(8,128)} %get-tuple-element.169.own_ref, bf16[64,1024]{1,0:T(8,128)(2,1)} %copy-done.28, bf16[64,1024]{1,0:T(8,128)(2,1)} %copy-done.29, ...), custom_call_target="tpu_custom_call" | custom-call | tf_op jit(solution)/shard_map/norm_two/pallas_call | solution.py:122
  30.1 3.7 %collective-permute-done.6.refs_1_ = bf16[64,1024]{1,0:T(8,128)(2,1)S(1)} collective-permute-done((bf16[64,1024]{1,0:T(8,128)(2,1)}, bf16[64,1024]{1,0:T(8,128)(2,1)S(1)}, u32[]{:S(2)}, u32[]{:S(2)}) %collective-permute-start.6) | collective-permute-done | bytes 131104 | tf_op jit(solution)/shard_map/ppermute | solution.py:41
  34.3 2.6 %collective-permute-start.7 = (bf16[64,1024]{1,0:T(8,128)(2,1)}, bf16[64,1024]{1,0:T(8,128)(2,1)S(1)}, u32[]{:S(2)}, u32[]{:S(2)}) collective-permute-start(bf16[64,1024]{1,0:T(8,128)(2,1)} %get-tuple-element.175.refs_0_.n_ref), channel_id=1, source_target_pairs={{0,8},{4,12},{8,0},{12,4},{1,9},{5,13},{9,1},{13,5},{2,10},{6,14},... | collective-permute-start | bytes 393224 | tf_op jit(solution)/shard_map/ppermute | solution.py:41
  38.4 1.6 copy-done.1
  40.0 1.5 gate_up_weights.1.wcat
  41.5 2.9 %collective-permute-done.7.refs_2_ = bf16[64,1024]{1,0:T(8,128)(2,1)S(1)} collective-permute-done((bf16[64,1024]{1,0:T(8,128)(2,1)}, bf16[64,1024]{1,0:T(8,128)(2,1)S(1)}, u32[]{:S(2)}, u32[]{:S(2)}) %collective-permute-start.7) | collective-permute-done | bytes 131104 | tf_op jit(solution)/shard_map/ppermute | solution.py:41
  46.0 1.6 collective-permute-start.10
  47.6 4.4 %collective-permute-done.14.refs_7_.far_ref = bf16[3,64,1152]{2,1,0:T(8,128)(2,1)S(1)} collective-permute-done((bf16[3,64,1152]{2,1,0:T(8,128)(2,1)S(1)}, bf16[3,64,1152]{2,1,0:T(8,128)(2,1)S(1)}, u32[]{:S(2)}, u32[]{:S(2)}) %collective-permute-start.14) | collective-permute-done | bytes 442400 | tf_op jit(solution)/shard_map/ppermute | solution.py:41
  51.9 2.2 %counts.1 = f32[1,128]{1,0:T(1,128)S(1)} custom-call(bf16[64,1152]{1,0:T(8,128)(2,1)S(1)} %copy-done.5, bf16[64,1152]{1,0:T(8,128)(2,1)S(1)} %copy-done.17, bf16[64,1152]{1,0:T(8,128)(2,1)S(1)} %copy-done.16, bf16[64,1152]{1,0:T(8,128)(2,1)S(1)} %copy-done.15, bf16[3,64,1152]{2,1,0:T(8,128)(2,1)S(1)} %together.2.far_ref.refs_4_, ...), custom_call_target="tpu_custom_call" | custom-call | tf_op jit(solution)/shard_map/counts/pallas_call | solution.py:122
  54.3 4.5 %experts.4 = (bf16[256,1024]{1,0:T(8,128)(2,1)S(1)}, bf16[256,2048]{1,0:T(8,128)(2,1)S(1)}, bf16[256,1024]{1,0:T(8,128)(2,1)S(1)}, f32[4,64,1152]{2,1,0:T(8,128)S(1)}, f32[4,64,1024]{2,1,0:T(8,128)S(1)}) custom-call(s32[1]{0:T(128)} %bitcast.9.base_ref, bf16[4,64,1024]{2,1,0:T(8,128)(2,1)S(1)} %together.3.x_ref.a0, bf16[64,1152]{1,0:T(8,128)(2,1)S(1)} %copy-done.5, ...), custom_call_target="tpu_custom_call" | custom-call | flops 3355443200 | tf_op jit(solution)/shard_map/experts/pallas_call | solution.py:353
  60.1 6.3 %experts.5 = (bf16[256,1024]{1,0:T(8,128)(2,1)S(1)}, bf16[256,2048]{1,0:T(8,128)(2,1)S(1)}, bf16[256,1024]{1,0:T(8,128)(2,1)S(1)}, bf16[4,64,1152]{2,1,0:T(8,128)(2,1)}, bf16[4,64,1024]{2,1,0:T(8,128)(2,1)S(1)}) custom-call(s32[1]{0:T(128)} %bitcast.9.base_ref, bf16[4,64,1024]{2,1,0:T(8,128)(2,1)S(1)} %collective-permute-done.9.x_ref.a1, ...), custom_call_target="tpu_custom_call" | custom-call | flops 3355443200 | tf_op jit(solution)/shard_map/experts/pallas_call | solution.py:353
  67.8 6.5 %experts.6 = (bf16[256,1024]{1,0:T(8,128)(2,1)S(1)}, bf16[256,2048]{1,0:T(8,128)(2,1)S(1)}, bf16[256,1024]{1,0:T(8,128)(2,1)S(1)}, bf16[4,64,1152]{2,1,0:T(8,128)(2,1)}, bf16[4,64,1024]{2,1,0:T(8,128)(2,1)S(1)}) custom-call(s32[1]{0:T(128)} %bitcast.9.base_ref, bf16[4,64,1024]{2,1,0:T(8,128)(2,1)S(1)} %collective-permute-done.10.x_ref.a2, ...), custom_call_target="tpu_custom_call" | custom-call | flops 3355443200 | tf_op jit(solution)/shard_map/experts/pallas_call | solution.py:353
  75.1 5.0 %experts.7 = (bf16[256,1024]{1,0:T(8,128)(2,1)S(1)}, bf16[256,2048]{1,0:T(8,128)(2,1)S(1)}, bf16[256,1024]{1,0:T(8,128)(2,1)S(1)}, f32[64,1152]{1,0:T(8,128)S(1)...) custom-call(s32[1]{0:T(128)} %bitcast.9.base_ref, ...), custom_call_target="tpu_custom_call" | custom-call | flops 3355443200 | tf_op jit(solution)/shard_map/experts/pallas_call | solution.py:353
  80.1 4.7 %collective-permute-start.18 = (bf16[64,1152]{1,0:T(8,128)(2,1)}, bf16[64,1152]{1,0:T(8,128)(2,1)}, u32[]{:S(2)}, u32[]{:S(2)}) collective-permute-start(bf16[64,1152]{1,0:T(8,128)(2,1)} %get-tuple-element.220), channel_id=1, source_target_pairs={{0,4},{4,0},{8,12},{12,8},{1,5},{5,1},{9,13},{13,9},{2,6},{6,2},{1... | collective-permute-start | bytes 442376 | tf_op jit(solution)/shard_map/ppermute | solution.py:41
  84.7 2.4 %collective-permute-start.20 = (bf16[64,1152]{1,0:T(8,128)(2,1)}, bf16[64,1152]{1,0:T(8,128)(2,1)}, u32[]{:S(2)}, u32[]{:S(2)}) collective-permute-start(bf16[64,1152]{1,0:T(8,128)(2,1)} %get-tuple-element.222), channel_id=1, source_target_pairs={{0,12},{4,8},{8,4},{12,0},{1,13},{5,9},{9,5},{13,1},{2,14},{6,10},... | collective-permute-start | bytes 442376 | tf_op jit(solution)/shard_map/ppermute | solution.py:41
  87.2 10.7 %expert_grads.1.mine_ref = bf16[8,3072,128]{2,1,0:T(8,128)(2,1)} custom-call(bf16[256,1024]{1,0:T(8,128)(2,1)S(1)} %bitcast.20, bf16[256,1024]{1,0:T(8,128)(2,1)S(1)} %bitcast.21, bf16[256,1024]{1,0:T(8,128)(2,1)S(1)} %bitcast.22, bf16[256,1024]{1,0:T(8,128)(2,1)S(1)} %bitcast.23, bf16[256,2048]{1,0:T(8,128)(2,1)S(1)} %get-tuple-element.187.refs_4_, ...), custom_call_target="tpu_custom_call" | custom-call | flops 644245094400 | tf_op jit(solution)/shard_map/expert_grads/pallas_call | solution.py:426
  99.7 1.9 collective-permute-start.23
  104.3 2.2 %collective-permute-done.23.refs_2_ = bf16[64,1152]{1,0:T(8,128)(2,1)S(1)} collective-permute-done((bf16[64,1152]{1,0:T(8,128)(2,1)S(1)}, bf16[64,1152]{1,0:T(8,128)(2,1)S(1)}, u32[]{:S(2)}, u32[]{:S(2)}) %collective-permute-start.23) | collective-permute-done | bytes 147488 | tf_op jit(solution)/shard_map/ppermute | solution.py:41
  107.7 1.8 collective-permute-start.24
  109.5 5.7 %collective-permute-done.25.refs_3_ = bf16[64,1152]{1,0:T(8,128)(2,1)S(1)} collective-permute-done((bf16[64,1152]{1,0:T(8,128)(2,1)S(1)}, bf16[64,1152]{1,0:T(8,128)(2,1)S(1)}, u32[]{:S(2)}, u32[]{:S(2)}) %collective-permute-start.25) | collective-permute-done | bytes 147488 | tf_op jit(solution)/shard_map/ppermute | solution.py:41
  117.3 1.7 collective-permute-start.28
  119.3 1.5 collective-permute-start.30
  121.4 2.6 %collective-permute-done.28.w1 = bf16[64,1152]{1,0:T(8,128)(2,1)S(1)} collective-permute-done((bf16[64,1152]{1,0:T(8,128)(2,1)S(1)}, bf16[64,1152]{1,0:T(8,128)(2,1)S(1)}, u32[]{:S(2)}, u32[]{:S(2)}) %collective-permute-start.28) | collective-permute-done | bytes 147488 | tf_op jit(solution)/shard_map/ppermute | solution.py:41
  124.0 4.2 %collective-permute-done.29.w2 = bf16[64,1152]{1,0:T(8,128)(2,1)S(1)} collective-permute-done((bf16[64,1152]{1,0:T(8,128)(2,1)S(1)}, bf16[64,1152]{1,0:T(8,128)(2,1)S(1)}, u32[]{:S(2)}, u32[]{:S(2)}) %collective-permute-start.29) | collective-permute-done | bytes 147488 | tf_op jit(solution)/shard_map/ppermute | solution.py:41
  128.8 5.5 %attend_back.1 = (bf16[256,1152]{1,0:T(8,128)(2,1)}, bf16[256,512]{1,0:T(8,128)(2,1)}, f32[8,1024]{1,0:T(8,128)}, f32[64,1024]{1,0:T(8,128)}, bf16[64,1024]{1,0:...) custom-call(s32[1]{0:T(128)} %bitcast.me_ref, bf16[64,1152]{1,0:T(8,128)(2,1)} %copy-done.23, ...), custom_call_target="tpu_custom_call" | custom-call | flops 53687091200 | tf_op jit(solution)/shard_map/attend_back/pallas_call | solution.py:122
  134.4 4.0 %dense.1 = (f32[512,896]{1,0:T(8,128)}, bf16[512,896]{1,0:T(8,128)(2,1)}) custom-call(s32[2]{0:T(128)} %pad_add_fusion.me_ref, bf16[4,64,1024]{2,1,0:T(8,128)(2,1)} %copy-done.2, bf16[4,64,1024]{2,1,0:T(8,128)(2,1)} %copy-done.9, bf16[4,64,1024]{2,1,0:T(8,128)(2,1)} %copy-done.10, bf16[4,64,1024]{2,1,0:T(8,128)(2,1)} %copy-done.11, ...), custom_call_target="tpu_custom_call" | custom-call | flops 100 | tf_op jit(solution)/shard_map/dense/pallas_call | solution.py:122
  143.7 2.2 %collective-permute-start.33 = (bf16[128,896]{1,0:T(8,128)(2,1)S(1)}, bf16[128,896]{1,0:T(8,128)(2,1)S(1)}, u32[]{:S(2)}, u32[]{:S(2)}) collective-permute-start(bf16[128,896]{1,0:T(8,128)(2,1)S(1)} %get-tuple-element.274), channel_id=1, source_target_pairs={{0,4},{4,0},{8,12},{12,8},{1,5},{5,1},{9,13},{13,9},{2,6},{6,2},{1... | collective-permute-start | bytes 688136 | tf_op jit(solution)/shard_map/ppermute | solution.py:41
  146.5 1.6 collective-permute-start.35
  149.4 6.4 %collective-permute-done.34.refs_1_ = bf16[64,1024]{1,0:T(8,128)(2,1)S(1)} collective-permute-done((bf16[64,1024]{1,0:T(8,128)(2,1)S(1)}, bf16[64,1024]{1,0:T(8,128)(2,1)S(1)}, u32[]{:S(2)}, u32[]{:S(2)}) %collective-permute-start.34) | collective-permute-done | bytes 131104 | tf_op jit(solution)/shard_map/ppermute | solution.py:41
  155.8 4.0 %collective-permute-start.40 = (bf16[128,896]{1,0:T(8,128)(2,1)S(1)}, bf16[128,896]{1,0:T(8,128)(2,1)S(1)}, u32[]{:S(2)}, u32[]{:S(2)}) collective-permute-start(bf16[128,896]{1,0:T(8,128)(2,1)S(1)} %get-tuple-element.286), channel_id=1, source_target_pairs={{0,8},{4,12},{8,0},{12,4},{1,9},{5,13},{9,1},{13,5},{2,10},{6,14},... | collective-permute-start | bytes 688136 | tf_op jit(solution)/shard_map/ppermute | solution.py:41
  160.3 4.7 %both_copies.4 = f32[8,1024,128]{2,1,0:T(8,128)} custom-call(bf16[8,3072,128]{2,1,0:T(8,128)(2,1)} %expert_grads.1.mine_ref, bf16[8,3072,128]{2,1,0:T(8,128)(2,1)} %collective-permute-done.27.other_ref), custom_call_target="tpu_custom_call" | custom-call | bytes 25165824 | tf_op jit(solution)/shard_map/both_copies/pallas_call | solution.py:455
  165.7 2.1 %input_grad.1.refs_0_ = bf16[64,1024]{1,0:T(8,128)(2,1)} custom-call(bf16[64,1024]{1,0:T(8,128)(2,1)} %get-tuple-element.168.x_ref, f32[1,1024]{1,0:T(1,128)} %bitcast.34, f32[64,1024]{1,0:T(8,128)} %copy-done.14, f32[64,1024]{1,0:T(8,128)} %get-tuple-element.279.refs_0_, bf16[64,1024]{1,0:T(8,128)(2,1)} %copy-done.25, bf16[64,1024]{1,0:T(8,128)(2,1)} %copy-done.26, ...), custom_call_target="tpu_custom_call" | custom-call | tf_op jit(solution)/shard_map/input_grad/pallas_call | solution.py:122
  170.7 4.3 %collective-permute-done.40.refs_1_ = bf16[128,896]{1,0:T(8,128)(2,1)S(1)} collective-permute-done((bf16[128,896]{1,0:T(8,128)(2,1)S(1)}, bf16[128,896]{1,0:T(8,128)(2,1)S(1)}, u32[]{:S(2)}, u32[]{:S(2)}) %collective-permute-start.40) | collective-permute-done | bytes 229408 | tf_op jit(solution)/shard_map/ppermute | solution.py:41
  175.0 1.8 collective-permute-start.39
  176.7 2.4 %collective-permute-start.44 = (bf16[64,1024]{1,0:T(8,128)(2,1)S(1)}, bf16[64,1024]{1,0:T(8,128)(2,1)S(1)}, u32[]{:S(2)}, u32[]{:S(2)}) collective-permute-start(bf16[64,1024]{1,0:T(8,128)(2,1)S(1)} %get-tuple-element.299), channel_id=1, source_target_pairs={{0,8},{4,12},{8,0},{12,4},{1,9},{5,13},{9,1},{13,5},{2,10},{6,14},... | collective-permute-start | bytes 393224 | tf_op jit(solution)/shard_map/ppermute | solution.py:41
  179.2 3.3 %collective-permute-start.45 = (bf16[64,1024]{1,0:T(8,128)(2,1)S(1)}, bf16[64,1024]{1,0:T(8,128)(2,1)S(1)}, u32[]{:S(2)}, u32[]{:S(2)}) collective-permute-start(bf16[64,1024]{1,0:T(8,128)(2,1)S(1)} %get-tuple-element.300), channel_id=1, source_target_pairs={{0,12},{4,8},{8,4},{12,0},{1,13},{5,9},{9,5},{13,1},{2,14},{6,10},... | collective-permute-start | bytes 393224 | tf_op jit(solution)/shard_map/ppermute | solution.py:41
  182.4 4.7 %both_copies.5 = f32[8,1024,128]{2,1,0:T(8,128)} custom-call(bf16[8,3072,128]{2,1,0:T(8,128)(2,1)} %expert_grads.1.mine_ref, bf16[8,3072,128]{2,1,0:T(8,128)(2,1)} %collective-permute-done.27.other_ref), custom_call_target="tpu_custom_call" | custom-call | bytes 25165824 | tf_op jit(solution)/shard_map/both_copies/pallas_call | solution.py:455
  192.8 4.8 %both_copies.3 = f32[8,128,1024]{2,1,0:T(8,128)} custom-call(bf16[8,3072,128]{2,1,0:T(8,128)(2,1)} %expert_grads.1.mine_ref, bf16[8,3072,128]{2,1,0:T(8,128)(2,1)} %collective-permute-done.27.other_ref), custom_call_target="tpu_custom_call" | custom-call | bytes 25165824 | tf_op jit(solution)/shard_map/both_copies/pallas_call | solution.py:455
  (156 shorter events, 39.6 us)
Async XLA Ops:
  2.8 9.1 %collective-permute-start = (bf16[64,1152]{1,0:T(8,128)(2,1)}, bf16[64,1152]{1,0:T(8,128)(2,1)S(1)}, u32[]{:S(2)}, u32[]{:S(2)}) collective-permute-start(bf16[64,1152]{1,0:T(8,128)(2,1)} %get-tuple-element.166.own_ref.refs_0_.cot_ref), channel_id=1, source_target_pairs={{0,4},{4,0},{8,12},{12,8},{1,5},{5,1},{9,13},{13,9},{2,6},{6,2},{1... | collective-permute-start | bytes 442376 | tf_op jit(solution)/shard_map/ppermute | solution.py:41
  5.8 22.7 %collective-permute-start.4 = (bf16[64,1152]{1,0:T(8,128)(2,1)}, bf16[64,1152]{1,0:T(8,128)(2,1)S(1)}, u32[]{:S(2)}, u32[]{:S(2)}) collective-permute-start(bf16[64,1152]{1,0:T(8,128)(2,1)} %get-tuple-element.166.own_ref.refs_0_.cot_ref), channel_id=1, source_target_pairs={{0,8},{4,12},{8,0},{12,4},{1,9},{5,13},{9,1},{13,5},{2,10},{6,14},... | collective-permute-start | bytes 442376 | tf_op jit(solution)/shard_map/ppermute | solution.py:41
  8.4 20.1 %collective-permute-start.5 = (bf16[64,1152]{1,0:T(8,128)(2,1)}, bf16[64,1152]{1,0:T(8,128)(2,1)S(1)}, u32[]{:S(2)}, u32[]{:S(2)}) collective-permute-start(bf16[64,1152]{1,0:T(8,128)(2,1)} %get-tuple-element.166.own_ref.refs_0_.cot_ref), channel_id=1, source_target_pairs={{0,12},{4,8},{8,4},{12,0},{1,13},{5,9},{9,5},{13,1},{2,14},{6,10},... | collective-permute-start | bytes 442376 | tf_op jit(solution)/shard_map/ppermute | solution.py:41
  16.6 5.2 %collective-permute-start.1 = (bf16[64,1024]{1,0:T(8,128)(2,1)}, bf16[64,1024]{1,0:T(8,128)(2,1)S(1)}, u32[]{:S(2)}, u32[]{:S(2)}) collective-permute-start(bf16[64,1024]{1,0:T(8,128)(2,1)} %get-tuple-element.170), channel_id=1, source_target_pairs={{0,1},{1,0},{2,3},{3,2},{4,5},{5,4},{6,7},{7,6},{8,9},{9,8},{10,11... | collective-permute-start | bytes 393224 | tf_op jit(solution)/shard_map/ppermute | solution.py:41
  18.3 5.2 %collective-permute-start.2 = (bf16[64,1024]{1,0:T(8,128)(2,1)}, bf16[64,1024]{1,0:T(8,128)(2,1)S(1)}, u32[]{:S(2)}, u32[]{:S(2)}) collective-permute-start(bf16[64,1024]{1,0:T(8,128)(2,1)} %get-tuple-element.171), channel_id=1, source_target_pairs={{0,2},{1,3},{2,0},{3,1},{4,6},{5,7},{6,4},{7,5},{8,10},{9,11},{10,... | collective-permute-start | bytes 393224 | tf_op jit(solution)/shard_map/ppermute | solution.py:41
  19.8 6.1 %collective-permute-start.3 = (bf16[64,1024]{1,0:T(8,128)(2,1)}, bf16[64,1024]{1,0:T(8,128)(2,1)S(1)}, u32[]{:S(2)}, u32[]{:S(2)}) collective-permute-start(bf16[64,1024]{1,0:T(8,128)(2,1)} %get-tuple-element.172), channel_id=1, source_target_pairs={{0,3},{1,2},{2,1},{3,0},{4,7},{5,6},{6,5},{7,4},{8,11},{9,10},{10,... | collective-permute-start | bytes 393224 | tf_op jit(solution)/shard_map/ppermute | solution.py:41
  28.6 5.2 %collective-permute-start.6 = (bf16[64,1024]{1,0:T(8,128)(2,1)}, bf16[64,1024]{1,0:T(8,128)(2,1)S(1)}, u32[]{:S(2)}, u32[]{:S(2)}) collective-permute-start(bf16[64,1024]{1,0:T(8,128)(2,1)} %get-tuple-element.175.refs_0_.n_ref), channel_id=1, source_target_pairs={{0,4},{4,0},{8,12},{12,8},{1,5},{5,1},{9,13},{13,9},{2,6},{6,2},{1... | collective-permute-start | bytes 393224 | tf_op jit(solution)/shard_map/ppermute | solution.py:41
  29.0 18.5 %collective-permute-start.11 = (bf16[3,64,1152]{2,1,0:T(8,128)(2,1)S(1)}, bf16[3,64,1152]{2,1,0:T(8,128)(2,1)}, u32[]{:S(2)}, u32[]{:S(2)}) collective-permute-start(bf16[3,64,1152]{2,1,0:T(8,128)(2,1)S(1)} %together.2.far_ref.refs_4_), channel_id=1, source_target_pairs={{0,1},{1,0},{2,3},{3,2},{4,5},{5,4},{6,7},{7,6},{8,9},{9,8},{10,11... | collective-permute-start | bytes 1327112 | tf_op jit(solution)/shard_map/ppermute | solution.py:41
  29.6 17.9 %collective-permute-start.12 = (bf16[3,64,1152]{2,1,0:T(8,128)(2,1)S(1)}, bf16[3,64,1152]{2,1,0:T(8,128)(2,1)}, u32[]{:S(2)}, u32[]{:S(2)}) collective-permute-start(bf16[3,64,1152]{2,1,0:T(8,128)(2,1)S(1)} %together.2.far_ref.refs_4_), channel_id=1, source_target_pairs={{0,2},{1,3},{2,0},{3,1},{4,6},{5,7},{6,4},{7,5},{8,10},{9,11},{10,... | collective-permute-start | bytes 1327112 | tf_op jit(solution)/shard_map/ppermute | solution.py:41
  33.8 18.1 %collective-permute-start.14 = (bf16[3,64,1152]{2,1,0:T(8,128)(2,1)S(1)}, bf16[3,64,1152]{2,1,0:T(8,128)(2,1)S(1)}, u32[]{:S(2)}, u32[]{:S(2)}) collective-permute-start(bf16[3,64,1152]{2,1,0:T(8,128)(2,1)S(1)} %together.2.far_ref.refs_4_), channel_id=1, source_target_pairs={{0,3},{1,2},{2,1},{3,0},{4,7},{5,6},{6,5},{7,4},{8,11},{9,10},{10,... | collective-permute-start | bytes 1327112 | tf_op jit(solution)/shard_map/ppermute | solution.py:41
  34.3 10.1 %collective-permute-start.7 = (bf16[64,1024]{1,0:T(8,128)(2,1)}, bf16[64,1024]{1,0:T(8,128)(2,1)S(1)}, u32[]{:S(2)}, u32[]{:S(2)}) collective-permute-start(bf16[64,1024]{1,0:T(8,128)(2,1)} %get-tuple-element.175.refs_0_.n_ref), channel_id=1, source_target_pairs={{0,8},{4,12},{8,0},{12,4},{1,9},{5,13},{9,1},{13,5},{2,10},{6,14},... | collective-permute-start | bytes 393224 | tf_op jit(solution)/shard_map/ppermute | solution.py:41
  36.9 7.5 %collective-permute-start.8 = (bf16[64,1024]{1,0:T(8,128)(2,1)}, bf16[64,1024]{1,0:T(8,128)(2,1)S(1)}, u32[]{:S(2)}, u32[]{:S(2)}) collective-permute-start(bf16[64,1024]{1,0:T(8,128)(2,1)} %get-tuple-element.175.refs_0_.n_ref), channel_id=1, source_target_pairs={{0,12},{4,8},{8,4},{12,0},{1,13},{5,9},{9,5},{13,1},{2,14},{6,10},... | collective-permute-start | bytes 393224 | tf_op jit(solution)/shard_map/ppermute | solution.py:41
  44.5 15.6 %collective-permute-start.9 = (bf16[4,64,1024]{2,1,0:T(8,128)(2,1)S(1)}, bf16[4,64,1024]{2,1,0:T(8,128)(2,1)S(1)}, u32[]{:S(2)}, u32[]{:S(2)}) collective-permute-start(bf16[4,64,1024]{2,1,0:T(8,128)(2,1)S(1)} %together.3.x_ref.a0), channel_id=1, source_target_pairs={{0,1},{1,0},{2,3},{3,2},{4,5},{5,4},{6,7},{7,6},{8,9},{9,8},{10,11... | collective-permute-start | bytes 1572872 | tf_op jit(solution)/shard_map/ppermute | solution.py:41
  46.0 21.8 %collective-permute-start.10 = (bf16[4,64,1024]{2,1,0:T(8,128)(2,1)S(1)}, bf16[4,64,1024]{2,1,0:T(8,128)(2,1)S(1)}, u32[]{:S(2)}, u32[]{:S(2)}) collective-permute-start(bf16[4,64,1024]{2,1,0:T(8,128)(2,1)S(1)} %together.3.x_ref.a0), channel_id=1, source_target_pairs={{0,2},{1,3},{2,0},{3,1},{4,6},{5,7},{6,4},{7,5},{8,10},{9,11},{10,... | collective-permute-start | bytes 1572872 | tf_op jit(solution)/shard_map/ppermute | solution.py:41
  54.2 5.9 %collective-permute-start.15 = (f32[1,128]{1,0:T(1,128)S(1)}, f32[1,128]{1,0:T(1,128)S(1)}, u32[]{:S(2)}, u32[]{:S(2)}) collective-permute-start(f32[1,128]{1,0:T(1,128)S(1)} %counts.1), channel_id=1, source_target_pairs={{0,16},{16,0},{1,17},{17,1},{2,18},{18,2},{3,19},{19,3},{4,20},{20... | collective-permute-start | bytes 1544 | tf_op jit(solution)/shard_map/ppermute | solution.py:41
  58.8 16.3 %collective-permute-start.13 = (bf16[4,64,1024]{2,1,0:T(8,128)(2,1)S(1)}, bf16[4,64,1024]{2,1,0:T(8,128)(2,1)S(1)}, u32[]{:S(2)}, u32[]{:S(2)}) collective-permute-start(bf16[4,64,1024]{2,1,0:T(8,128)(2,1)S(1)} %together.3.x_ref.a0), channel_id=1, source_target_pairs={{0,3},{1,2},{2,1},{3,0},{4,7},{5,6},{6,5},{7,4},{8,11},{9,10},{10,... | collective-permute-start | bytes 1572872 | tf_op jit(solution)/shard_map/ppermute | solution.py:41
  66.4 31.5 %collective-permute-start.16 = (bf16[4,64,1152]{2,1,0:T(8,128)(2,1)}, bf16[4,64,1152]{2,1,0:T(8,128)(2,1)}, u32[]{:S(2)}, u32[]{:S(2)}) collective-permute-start(bf16[4,64,1152]{2,1,0:T(8,128)(2,1)} %get-tuple-element.194), channel_id=1, source_target_pairs={{0,1},{1,0},{2,3},{3,2},{4,5},{5,4},{6,7},{7,6},{8,9},{9,8},{10,11... | collective-permute-start | bytes 1769480 | tf_op jit(solution)/shard_map/ppermute | solution.py:41
  74.3 23.6 %collective-permute-start.17 = (bf16[4,64,1152]{2,1,0:T(8,128)(2,1)}, bf16[4,64,1152]{2,1,0:T(8,128)(2,1)}, u32[]{:S(2)}, u32[]{:S(2)}) collective-permute-start(bf16[4,64,1152]{2,1,0:T(8,128)(2,1)} %get-tuple-element.203), channel_id=1, source_target_pairs={{0,2},{1,3},{2,0},{3,1},{4,6},{5,7},{6,4},{7,5},{8,10},{9,11},{10,... | collective-permute-start | bytes 1769480 | tf_op jit(solution)/shard_map/ppermute | solution.py:41
  80.1 17.8 %collective-permute-start.18 = (bf16[64,1152]{1,0:T(8,128)(2,1)}, bf16[64,1152]{1,0:T(8,128)(2,1)}, u32[]{:S(2)}, u32[]{:S(2)}) collective-permute-start(bf16[64,1152]{1,0:T(8,128)(2,1)} %get-tuple-element.220), channel_id=1, source_target_pairs={{0,4},{4,0},{8,12},{12,8},{1,5},{5,1},{9,13},{13,9},{2,6},{6,2},{1... | collective-permute-start | bytes 442376 | tf_op jit(solution)/shard_map/ppermute | solution.py:41
  84.7 13.1 %collective-permute-start.19 = (bf16[64,1152]{1,0:T(8,128)(2,1)}, bf16[64,1152]{1,0:T(8,128)(2,1)}, u32[]{:S(2)}, u32[]{:S(2)}) collective-permute-start(bf16[64,1152]{1,0:T(8,128)(2,1)} %get-tuple-element.221), channel_id=1, source_target_pairs={{0,8},{4,12},{8,0},{12,4},{1,9},{5,13},{9,1},{13,5},{2,10},{6,14},... | collective-permute-start | bytes 442376 | tf_op jit(solution)/shard_map/ppermute | solution.py:41
  84.7 13.1 %collective-permute-start.20 = (bf16[64,1152]{1,0:T(8,128)(2,1)}, bf16[64,1152]{1,0:T(8,128)(2,1)}, u32[]{:S(2)}, u32[]{:S(2)}) collective-permute-start(bf16[64,1152]{1,0:T(8,128)(2,1)} %get-tuple-element.222), channel_id=1, source_target_pairs={{0,12},{4,8},{8,4},{12,0},{1,13},{5,9},{9,5},{13,1},{2,14},{6,10},... | collective-permute-start | bytes 442376 | tf_op jit(solution)/shard_map/ppermute | solution.py:41
  99.3 15.9 %collective-permute-start.21 = (bf16[4,64,1024]{2,1,0:T(8,128)(2,1)S(1)}, bf16[4,64,1024]{2,1,0:T(8,128)(2,1)S(1)}, u32[]{:S(2)}, u32[]{:S(2)}) collective-permute-start(bf16[4,64,1024]{2,1,0:T(8,128)(2,1)S(1)} %get-tuple-element.232), channel_id=1, source_target_pairs={{0,1},{1,0},{2,3},{3,2},{4,5},{5,4},{6,7},{7,6},{8,9},{9,8},{10,11... | collective-permute-start | bytes 1572872 | tf_op jit(solution)/shard_map/ppermute | solution.py:41
  99.7 15.4 %collective-permute-start.22 = (bf16[4,64,1024]{2,1,0:T(8,128)(2,1)S(1)}, bf16[4,64,1024]{2,1,0:T(8,128)(2,1)S(1)}, u32[]{:S(2)}, u32[]{:S(2)}) collective-permute-start(bf16[4,64,1024]{2,1,0:T(8,128)(2,1)S(1)} %get-tuple-element.233), channel_id=1, source_target_pairs={{0,2},{1,3},{2,0},{3,1},{4,6},{5,7},{6,4},{7,5},{8,10},{9,11},{10,... | collective-permute-start | bytes 1572872 | tf_op jit(solution)/shard_map/ppermute | solution.py:41
  99.7 6.8 %collective-permute-start.23 = (bf16[64,1152]{1,0:T(8,128)(2,1)S(1)}, bf16[64,1152]{1,0:T(8,128)(2,1)S(1)}, u32[]{:S(2)}, u32[]{:S(2)}) collective-permute-start(bf16[64,1152]{1,0:T(8,128)(2,1)S(1)} %get-tuple-element.235), channel_id=1, source_target_pairs={{0,4},{4,0},{8,12},{12,8},{1,5},{5,1},{9,13},{13,9},{2,6},{6,2},{1... | collective-permute-start | bytes 442376 | tf_op jit(solution)/shard_map/ppermute | solution.py:41
  101.6 13.6 %collective-permute-start.25 = (bf16[64,1152]{1,0:T(8,128)(2,1)S(1)}, bf16[64,1152]{1,0:T(8,128)(2,1)S(1)}, u32[]{:S(2)}, u32[]{:S(2)}) collective-permute-start(bf16[64,1152]{1,0:T(8,128)(2,1)S(1)} %get-tuple-element.242), channel_id=1, source_target_pairs={{0,8},{4,12},{8,0},{12,4},{1,9},{5,13},{9,1},{13,5},{2,10},{6,14},... | collective-permute-start | bytes 442376 | tf_op jit(solution)/shard_map/ppermute | solution.py:41
  102.9 12.3 %collective-permute-start.26 = (bf16[64,1152]{1,0:T(8,128)(2,1)S(1)}, bf16[64,1152]{1,0:T(8,128)(2,1)S(1)}, u32[]{:S(2)}, u32[]{:S(2)}) collective-permute-start(bf16[64,1152]{1,0:T(8,128)(2,1)S(1)} %get-tuple-element.243), channel_id=1, source_target_pairs={{0,12},{4,8},{8,4},{12,0},{1,13},{5,9},{9,5},{13,1},{2,14},{6,10},... | collective-permute-start | bytes 442376 | tf_op jit(solution)/shard_map/ppermute | solution.py:41
  107.7 7.5 %collective-permute-start.24 = (bf16[64,1152]{1,0:T(8,128)(2,1)S(1)}, bf16[64,1152]{1,0:T(8,128)(2,1)S(1)}, u32[]{:S(2)}, u32[]{:S(2)}) collective-permute-start(bf16[64,1152]{1,0:T(8,128)(2,1)S(1)} %through.1), channel_id=1, source_target_pairs={{0,3},{1,2},{2,1},{3,0},{4,7},{5,6},{6,5},{7,4},{8,11},{9,10},{10,... | collective-permute-start | bytes 442376 | tf_op jit(solution)/shard_map/ppermute | solution.py:41
  117.3 10.8 %collective-permute-start.27 = (bf16[8,3072,128]{2,1,0:T(8,128)(2,1)}, bf16[8,3072,128]{2,1,0:T(8,128)(2,1)}, u32[]{:S(2)}, u32[]{:S(2)}) collective-permute-start(bf16[8,3072,128]{2,1,0:T(8,128)(2,1)} %expert_grads.1.mine_ref), channel_id=1, source_target_pairs={{0,16},{16,0},{1,17},{17,1},{2,18},{18,2},{3,19},{19,3},{4,20},{20... | collective-permute-start | bytes 18874376 | tf_op jit(solution)/shard_map/ppermute | solution.py:41
  117.3 6.6 %collective-permute-start.28 = (bf16[64,1152]{1,0:T(8,128)(2,1)S(1)}, bf16[64,1152]{1,0:T(8,128)(2,1)S(1)}, u32[]{:S(2)}, u32[]{:S(2)}) collective-permute-start(bf16[64,1152]{1,0:T(8,128)(2,1)S(1)} %get-tuple-element.258.w0), channel_id=1, source_target_pairs={{0,1},{1,0},{2,3},{3,2},{4,5},{5,4},{6,7},{7,6},{8,9},{9,8},{10,11... | collective-permute-start | bytes 442376 | tf_op jit(solution)/shard_map/ppermute | solution.py:41
  119.0 9.1 %collective-permute-start.29 = (bf16[64,1152]{1,0:T(8,128)(2,1)S(1)}, bf16[64,1152]{1,0:T(8,128)(2,1)S(1)}, u32[]{:S(2)}, u32[]{:S(2)}) collective-permute-start(bf16[64,1152]{1,0:T(8,128)(2,1)S(1)} %get-tuple-element.258.w0), channel_id=1, source_target_pairs={{0,2},{1,3},{2,0},{3,1},{4,6},{5,7},{6,4},{7,5},{8,10},{9,11},{10,... | collective-permute-start | bytes 442376 | tf_op jit(solution)/shard_map/ppermute | solution.py:41
  119.3 8.9 %collective-permute-start.30 = (bf16[64,1152]{1,0:T(8,128)(2,1)S(1)}, bf16[64,1152]{1,0:T(8,128)(2,1)S(1)}, u32[]{:S(2)}, u32[]{:S(2)}) collective-permute-start(bf16[64,1152]{1,0:T(8,128)(2,1)S(1)} %get-tuple-element.258.w0), channel_id=1, source_target_pairs={{0,3},{1,2},{2,1},{3,0},{4,7},{5,6},{6,5},{7,4},{8,11},{9,10},{10,... | collective-permute-start | bytes 442376 | tf_op jit(solution)/shard_map/ppermute | solution.py:41
  138.4 2.7 %collective-permute-start.31 = (bf16[512,896]{1,0:T(8,128)(2,1)}, bf16[512,896]{1,0:T(8,128)(2,1)S(1)}, u32[]{:S(2)}, u32[]{:S(2)}) collective-permute-start(bf16[512,896]{1,0:T(8,128)(2,1)} %get-tuple-element.272), channel_id=1, source_target_pairs={{0,16},{16,0},{1,17},{17,1},{2,18},{18,2},{3,19},{19,3},{4,20},{20... | collective-permute-start | bytes 2752520 | tf_op jit(solution)/shard_map/ppermute | solution.py:41
  138.4 30.8 %collective-permute-start.42 = (bf16[4,64,1024]{2,1,0:T(8,128)(2,1)S(1)}, bf16[4,64,1024]{2,1,0:T(8,128)(2,1)S(1)}, u32[]{:S(2)}, u32[]{:S(2)}) collective-permute-start(bf16[4,64,1024]{2,1,0:T(8,128)(2,1)S(1)} %copy-done.22), channel_id=1, source_target_pairs={{0,3},{1,2},{2,1},{3,0},{4,7},{5,6},{6,5},{7,4},{8,11},{9,10},{10,... | collective-permute-start | bytes 1572872 | tf_op jit(solution)/shard_map/ppermute | solution.py:41
  143.7 21.4 %collective-permute-start.33 = (bf16[128,896]{1,0:T(8,128)(2,1)S(1)}, bf16[128,896]{1,0:T(8,128)(2,1)S(1)}, u32[]{:S(2)}, u32[]{:S(2)}) collective-permute-start(bf16[128,896]{1,0:T(8,128)(2,1)S(1)} %get-tuple-element.274), channel_id=1, source_target_pairs={{0,4},{4,0},{8,12},{12,8},{1,5},{5,1},{9,13},{13,9},{2,6},{6,2},{1... | collective-permute-start | bytes 688136 | tf_op jit(solution)/shard_map/ppermute | solution.py:41
  145.9 9.9 %collective-permute-start.34 = (bf16[64,1024]{1,0:T(8,128)(2,1)S(1)}, bf16[64,1024]{1,0:T(8,128)(2,1)S(1)}, u32[]{:S(2)}, u32[]{:S(2)}) collective-permute-start(bf16[64,1024]{1,0:T(8,128)(2,1)S(1)} %copy-done.36), channel_id=1, source_target_pairs={{0,1},{1,0},{2,3},{3,2},{4,5},{5,4},{6,7},{7,6},{8,9},{9,8},{10,11... | collective-permute-start | bytes 393224 | tf_op jit(solution)/shard_map/ppermute | solution.py:41
  146.5 13.2 %collective-permute-start.35 = (bf16[64,1024]{1,0:T(8,128)(2,1)S(1)}, bf16[64,1024]{1,0:T(8,128)(2,1)S(1)}, u32[]{:S(2)}, u32[]{:S(2)}) collective-permute-start(bf16[64,1024]{1,0:T(8,128)(2,1)S(1)} %copy-done.35), channel_id=1, source_target_pairs={{0,2},{1,3},{2,0},{3,1},{4,6},{5,7},{6,4},{7,5},{8,10},{9,11},{10,... | collective-permute-start | bytes 393224 | tf_op jit(solution)/shard_map/ppermute | solution.py:41
  148.1 16.9 %collective-permute-start.36 = (bf16[64,1024]{1,0:T(8,128)(2,1)S(1)}, bf16[64,1024]{1,0:T(8,128)(2,1)S(1)}, u32[]{:S(2)}, u32[]{:S(2)}) collective-permute-start(bf16[64,1024]{1,0:T(8,128)(2,1)S(1)} %copy-done.34), channel_id=1, source_target_pairs={{0,3},{1,2},{2,1},{3,0},{4,7},{5,6},{6,5},{7,4},{8,11},{9,10},{10,... | collective-permute-start | bytes 393224 | tf_op jit(solution)/shard_map/ppermute | solution.py:41
  155.8 19.2 %collective-permute-start.40 = (bf16[128,896]{1,0:T(8,128)(2,1)S(1)}, bf16[128,896]{1,0:T(8,128)(2,1)S(1)}, u32[]{:S(2)}, u32[]{:S(2)}) collective-permute-start(bf16[128,896]{1,0:T(8,128)(2,1)S(1)} %get-tuple-element.286), channel_id=1, source_target_pairs={{0,8},{4,12},{8,0},{12,4},{1,9},{5,13},{9,1},{13,5},{2,10},{6,14},... | collective-permute-start | bytes 688136 | tf_op jit(solution)/shard_map/ppermute | solution.py:41
  159.7 17.0 %collective-permute-start.41 = (bf16[128,896]{1,0:T(8,128)(2,1)S(1)}, bf16[128,896]{1,0:T(8,128)(2,1)S(1)}, u32[]{:S(2)}, u32[]{:S(2)}) collective-permute-start(bf16[128,896]{1,0:T(8,128)(2,1)S(1)} %get-tuple-element.287), channel_id=1, source_target_pairs={{0,12},{4,8},{8,4},{12,0},{1,13},{5,9},{9,5},{13,1},{2,14},{6,10},... | collective-permute-start | bytes 688136 | tf_op jit(solution)/shard_map/ppermute | solution.py:41
  167.8 11.4 %collective-permute-start.37 = (bf16[64,1024]{1,0:T(8,128)(2,1)}, bf16[64,1024]{1,0:T(8,128)(2,1)S(1)}, u32[]{:S(2)}, u32[]{:S(2)}) collective-permute-start(bf16[64,1024]{1,0:T(8,128)(2,1)} %input_grad.1.refs_0_), channel_id=1, source_target_pairs={{0,1},{1,0},{2,3},{3,2},{4,5},{5,4},{6,7},{7,6},{8,9},{9,8},{10,11... | collective-permute-start | bytes 393224 | tf_op jit(solution)/shard_map/ppermute | solution.py:41
  169.4 18.6 %collective-permute-start.43 = (bf16[64,1024]{1,0:T(8,128)(2,1)S(1)}, bf16[64,1024]{1,0:T(8,128)(2,1)S(1)}, u32[]{:S(2)}, u32[]{:S(2)}) collective-permute-start(bf16[64,1024]{1,0:T(8,128)(2,1)S(1)} %get-tuple-element.298), channel_id=1, source_target_pairs={{0,4},{4,0},{8,12},{12,8},{1,5},{5,1},{9,13},{13,9},{2,6},{6,2},{1... | collective-permute-start | bytes 393224 | tf_op jit(solution)/shard_map/ppermute | solution.py:41
  169.5 18.5 %collective-permute-start.38 = (bf16[64,1024]{1,0:T(8,128)(2,1)}, bf16[64,1024]{1,0:T(8,128)(2,1)S(1)}, u32[]{:S(2)}, u32[]{:S(2)}) collective-permute-start(bf16[64,1024]{1,0:T(8,128)(2,1)} %input_grad.1.refs_0_), channel_id=1, source_target_pairs={{0,2},{1,3},{2,0},{3,1},{4,6},{5,7},{6,4},{7,5},{8,10},{9,11},{10,... | collective-permute-start | bytes 393224 | tf_op jit(solution)/shard_map/ppermute | solution.py:41
  175.0 13.0 %collective-permute-start.39 = (bf16[64,1024]{1,0:T(8,128)(2,1)}, bf16[64,1024]{1,0:T(8,128)(2,1)S(1)}, u32[]{:S(2)}, u32[]{:S(2)}) collective-permute-start(bf16[64,1024]{1,0:T(8,128)(2,1)} %input_grad.1.refs_0_), channel_id=1, source_target_pairs={{0,3},{1,2},{2,1},{3,0},{4,7},{5,6},{6,5},{7,4},{8,11},{9,10},{10,... | collective-permute-start | bytes 393224 | tf_op jit(solution)/shard_map/ppermute | solution.py:41
  176.7 12.4 %collective-permute-start.44 = (bf16[64,1024]{1,0:T(8,128)(2,1)S(1)}, bf16[64,1024]{1,0:T(8,128)(2,1)S(1)}, u32[]{:S(2)}, u32[]{:S(2)}) collective-permute-start(bf16[64,1024]{1,0:T(8,128)(2,1)S(1)} %get-tuple-element.299), channel_id=1, source_target_pairs={{0,8},{4,12},{8,0},{12,4},{1,9},{5,13},{9,1},{13,5},{2,10},{6,14},... | collective-permute-start | bytes 393224 | tf_op jit(solution)/shard_map/ppermute | solution.py:41
  179.2 10.0 %collective-permute-start.45 = (bf16[64,1024]{1,0:T(8,128)(2,1)S(1)}, bf16[64,1024]{1,0:T(8,128)(2,1)S(1)}, u32[]{:S(2)}, u32[]{:S(2)}) collective-permute-start(bf16[64,1024]{1,0:T(8,128)(2,1)S(1)} %get-tuple-element.300), channel_id=1, source_target_pairs={{0,12},{4,8},{8,4},{12,0},{1,13},{5,9},{9,5},{13,1},{2,14},{6,10},... | collective-permute-start | bytes 393224 | tf_op jit(solution)/shard_map/ppermute | solution.py:41
  189.2 10.1 %collective-permute-start.46 = (bf16[80,1024]{1,0:T(8,128)(2,1)S(1)}, bf16[80,1024]{1,0:T(8,128)(2,1)S(1)}, u32[]{:S(2)}, u32[]{:S(2)}) collective-permute-start(bf16[80,1024]{1,0:T(8,128)(2,1)S(1)} %out_piece.1.refs_0_), channel_id=1, source_target_pairs={{0,1},{1,0},{2,3},{3,2},{4,5},{5,4},{6,7},{7,6},{8,9},{9,8},{10,11... | collective-permute-start | bytes 491528 | tf_op jit(solution)/shard_map/ppermute | solution.py:41
  190.1 9.2 %collective-permute-start.47 = (bf16[80,1024]{1,0:T(8,128)(2,1)S(1)}, bf16[80,1024]{1,0:T(8,128)(2,1)S(1)}, u32[]{:S(2)}, u32[]{:S(2)}) collective-permute-start(bf16[80,1024]{1,0:T(8,128)(2,1)S(1)} %out_piece.1.refs_0_), channel_id=1, source_target_pairs={{0,2},{1,3},{2,0},{3,1},{4,6},{5,7},{6,4},{7,5},{8,10},{9,11},{10,... | collective-permute-start | bytes 491528 | tf_op jit(solution)/shard_map/ppermute | solution.py:41
  191.4 7.9 %collective-permute-start.48 = (bf16[80,1024]{1,0:T(8,128)(2,1)S(1)}, bf16[80,1024]{1,0:T(8,128)(2,1)S(1)}, u32[]{:S(2)}, u32[]{:S(2)}) collective-permute-start(bf16[80,1024]{1,0:T(8,128)(2,1)S(1)} %out_piece.1.refs_0_), channel_id=1, source_target_pairs={{0,3},{1,2},{2,1},{3,0},{4,7},{5,6},{6,5},{7,4},{8,11},{9,10},{10,... | collective-permute-start | bytes 491528 | tf_op jit(solution)/shard_map/ppermute | solution.py:41
  (38 other events, 436.3 us)

commit v10 on v9

--- a/solution.py
+++ b/solution.py
@@ -279,7 +279,7 @@
 
 
 def experts_kernel(experts, base_ref, x_ref, own_ref, far_ref, router_ref, wcat, wd_ref, *refs):
-    cot_ref, dgu_ref, hg_ref, *ds, m_ref = refs
+    cot_ref, dgu_ref, hg_ref, *ds, m_ref, v_ref = refs
     hidden = LANES
     pair = 2 * hidden
     rows, width = cot_ref.shape
@@ -294,11 +294,12 @@
     _, gates = router_of(x, router_ref, routes, experts)
     lane = lane_of(gates.shape)
     dots = jnp.zeros(gates.shape, F32)
+    v_ref[...] = nt(cot_ref[...], wd_ref[...])
     for e in range(hg_ref.shape[1] // hidden):
         mine = lane == base_ref[0] + e
         g = jnp.sum(jnp.where(mine, gates, 0.0), axis=-1, keepdims=True)
         both = nn(x, wcat[:, e * pair : (e + 1) * pair])
-        v = nt(cot_ref[...], wd_ref[e * hidden : (e + 1) * hidden, :])
+        v = v_ref[:, e * hidden : (e + 1) * hidden]
         gate, up = both[:, :hidden], both[:, hidden:]
         sig = 1.0 / (1.0 + jnp.exp(-gate))
         act = gate * sig
@@ -366,6 +367,7 @@
             *d_shapes,
             shape(dims(width), kind),
         ],
+        scratch_shapes=[pltpu.VMEM((step, inner), F32)],
         compiler_params=pltpu.CompilerParams(vmem_limit_bytes=(14 if few else 30) * MIB),
         cost_estimate=pl.CostEstimate(flops=int(100.0*(total * width * inner // 8)), bytes_accessed=0, transcendentals=0),
         name="experts",
@@ -492,12 +494,13 @@
 
 def attend_back_kernel(
     me_ref, w0, w1, w2, w3, x_ref, q_ref, k_ref, v_ref, lse_ref, wq_ref, wk_ref, wv_ref, wo_ref, cos_ref, sin_ref,
-    small_in, wide_ref, dq_ref, small_ref, p0, p1, p2, p3, do_ref, whole
+    small_in, a0, a1, a2, a3, o_ref, n_ref, small_ref, p0, p1, p2, p3, kept_ref, sent_ref,
+    do_ref, whole, wide_ref, dq_ref, two_ref, dense
 ):
     rows = w0.shape[0]
     width = x_ref.shape[1]
     for r, piece in enumerate((w0, w1, w2, w3)):
-        start = pl.multiple_of((me_ref[0] ^ r) * rows, rows)
+        start = pl.multiple_of((me_ref[1] ^ r) * rows, rows)
         wide_ref[pl.ds(start, rows), :] = piece[...]
     do_ref[...] = nt(wide_ref[:, :width], wo_ref[...]).astype(BF)
     cosine, sine = cos_ref[...], sin_ref[...]
@@ -551,22 +554,18 @@
     small_ref[...] = small_in[...]
     small_ref[0:1, :] = jnp.sum(whole[...] * x * inv, axis=0, keepdims=True)
     for r, part in enumerate((p0, p1, p2, p3)):
-        start = pl.multiple_of((me_ref[0] ^ r) * rows, rows)
+        start = pl.multiple_of((me_ref[1] ^ r) * rows, rows)
         part[...] = whole[pl.ds(start, rows), :].astype(part.dtype)
-
-
-def dense_kernel(me_ref, a0, a1, a2, a3, wide_ref, o_ref, n_ref, dq_ref, kept_ref, sent_ref, two_ref, whole):
-    rows, width = a0.shape[1:]
     for r, piece in enumerate((a0, a1, a2, a3)):
         start = pl.multiple_of((me_ref[1] ^ r) * rows, rows)
         two_ref[pl.ds(start, rows), :] = piece[0]
-    columns, heads = dq_ref.shape[1], o_ref.shape[1]
-    whole[:, :columns] = tn(n_ref[...], dq_ref[...])
-    whole[:, columns : columns + heads] = tn(wide_ref[:, :width], o_ref[...])
-    whole[:, columns + heads :] = tn(two_ref[...], wide_ref[:, width:])
+    columns = dq_ref.shape[1]
+    dense[:, :columns] = tn(n_ref[...], dq_ref[...])
+    dense[:, columns : columns + heads] = tn(wide_ref[:, :width], o_ref[...])
+    dense[:, columns + heads :] = tn(two_ref[...], wide_ref[:, width:])
     half = kept_ref.shape[0]
-    kept_ref[...] = whole[pl.ds(pl.multiple_of(me_ref[0] * half, half), half), :]
-    sent_ref[...] = whole[pl.ds(pl.multiple_of((1 - me_ref[0]) * half, half), half), :].astype(BF)
+    kept_ref[...] = dense[pl.ds(pl.multiple_of(me_ref[0] * half, half), half), :]
+    sent_ref[...] = dense[pl.ds(pl.multiple_of((1 - me_ref[0]) * half, half), half), :].astype(BF)
 
 
 def input_grad_kernel(x_ref, gain_ref, dh_ref, *refs):
@@ -805,47 +804,33 @@
     wides, moe_last = tied(wides, moes[last])
     moe_got.append(swap(moe_last, "tensor", last))
 
-    wide_all, dqkv, small, *back_parts = call(
+    half = width // dp_size
+    chunk = half // expert_size
+    columns = heads + 2 * keys_wide
+    all_columns = columns + heads + LANES
+    own_block = pl.BlockSpec((1, rows, width), lambda i: (0, 0, 0))
+    small, *back_parts, kept, sent = call(
         attend_back_kernel,
-        [
-            shape((seq_len, wide_width), BF),
-            shape((seq_len, heads + 2 * keys_wide), BF),
-            shape((8, width), F32),
-            shape((rows, width), F32),
-        ]
-        + [shape((rows, width), BF)] * last,
-        (t_at, *wides, tokens, q, k, v, lse, w_query, w_key, w_value, w_output, cosine, sine, small),
+        [shape((8, width), F32), shape((rows, width), F32)]
+        + [shape((rows, width), BF)] * last
+        + [shape((half, all_columns), F32), shape((half, all_columns), BF)],
+        (d_at, *wides, tokens, q, k, v, lse, w_query, w_key, w_value, w_output, cosine, sine, small)
+        + (*twos, o, n_one),
         "attend_back",
-        "s" + "v" * tensor_size + "b" * 11,
-        "bb",
+        ["s"] + ["v"] * tensor_size + ["b"] * 12 + [own_block] * tensor_size + ["b"] * 2,
+        "bvvvvbb",
         limit=58,
         scratch=[
             pltpu.VMEM((seq_len, heads), BF),
             pltpu.VMEM((seq_len, width), F32),
-        ],
-        flops=2 * seq_len * width * 4 * heads,
-    )
-    part_sums = [back_parts[0]] + backwards(lambda r: swap(back_parts[r], "tensor", r), tensor_size)
-    half = width // dp_size
-    chunk = half // expert_size
-
-    columns = heads + 2 * keys_wide
-    all_columns = columns + heads + LANES
-    own_block = pl.BlockSpec((1, rows, width), lambda i: (0, 0, 0))
-    kept, sent = call(
-        dense_kernel,
-        [shape((half, all_columns), F32), shape((half, all_columns), BF)],
-        (d_at, *twos, wide_all, o, n_one, dqkv),
-        "dense",
-        ["s"] + [own_block] * tensor_size + ["b"] * 4,
-        "vv",
-        limit=54,
-        scratch=[
+            pltpu.VMEM((seq_len, wide_width), BF),
+            pltpu.VMEM((seq_len, columns), BF),
             pltpu.VMEM((seq_len, width), BF),
             pltpu.VMEM((width, all_columns), F32),
         ],
-        flops=1,
-    )
+        flops=2 * seq_len * width * 4 * heads,
+    )
+    part_sums = [back_parts[0]] + backwards(lambda r: swap(back_parts[r], "tensor", r), tensor_size)
     mine, *others, small = call(
         kept_and_dealt_kernel,
         [shape((chunk, all_columns), F32)]

time: 202 us -> 203 us (level)
  Pallas kernels: 78.1 us -> 74.7 us
  local copies, waits for them, and re-layouts: 8.43 us -> 11.5 us
    unnamed x75 -> x81, local copies, waits for them, and re-layouts: 7.92 us -> 11 us
    pallas_call x18 -> x17, Pallas kernels: 29.4 us -> 27.4 us  [call(): pl.pallas_call(kernel, grid=(1,), out_shape=outs, in_specs=[spec(p, x) fo...]
  transfers between devices with their start and end apart: 49 -> 49, of which waited for: 15 -> 17; matrix products, arithmetic and copies ran while one was open for 1% -> 1% of each run, Pallas kernels for 31% -> 31%
where the time goes in v10:
time: 203 us; the launch traced here: 202 us
  Pallas kernels  74.7 us (37%)
  starting transfers between devices  66.4 us (33%)
  waiting for transfers between devices  47.1 us (23%)
  local copies, waits for them, and re-layouts  11.5 us (6%)
    ppermute x49, starting transfers between devices, swap(): return lax.ppermute(x, axis, [(i, i ^ distance) for i in range(size)])  66.4 us
    ppermute x49, waiting for transfers between devices, swap(): return lax.ppermute(x, axis, [(i, i ^ distance) for i in range(size)])  47.1 us
    pallas_call x17, Pallas kernels, call(): pl.pallas_call(kernel, grid=(1,), out_shape=outs, in_specs=[spec(p, x) fo...  27.4 us
    pallas_call x4, Pallas kernels, run_experts(): pl.pallas_call(kernel, grid=(total // step,), in_specs=[pl.BlockSpec(memo...  20.9 us
    pallas_call x3, Pallas kernels, both_copies(): pl.pallas_call(both_copies_kernel, grid=(local // step,), in_specs=[block...  14.3 us
    unnamed x81, local copies, waits for them, and re-layouts  11 us
    pallas_call x1, Pallas kernels, run_grads(): pl.pallas_call(grads_kernel, grid=(local,), in_specs=whole(n) + cols(dgu,...  10.7 us
  transfers between devices with their start and end apart: 49, of which 17 were waited for; matrix products, arithmetic and copies ran while one was open for 1% of the time, Pallas kernels for 31%

profile of v10, /device:TPU:0, one launch (start us, length us, event | category | flops | bytes accessed | tf_op | source)
XLA Modules:
  0.0 201.9 jit_solution(8171592016891566194)
XLA Ops:
  0.6 2.2 %pieces.1 = (bf16[64,1152]{1,0:T(8,128)(2,1)}, bf16[64,1152]{1,0:T(8,128)(2,1)}, bf16[64,1152]{1,0:T(8,128)(2,1)}, bf16[64,1152]{1,0:T(8,128)(2,1)}, bf16[128,1024]{1,0:T(8,128)(2,1)}) custom-call(s32[1]{0:T(128)} %bitcast.me_ref, bf16[256,1024]{1,0:T(8,128)(2,1)} %cot_ref.1, s32[8,256]{1,0:T(8,128)} %bitcast.32, bf16[32,1024]{1,0:T(8,128)(2,1)} %bitcast.31), custom_call_target="tpu_custom_call" | custom-call | tf_op jit(solution)/shard_map/pieces/pallas_call | solution.py:122
  2.8 3.0 %collective-permute-start = (bf16[64,1152]{1,0:T(8,128)(2,1)}, bf16[64,1152]{1,0:T(8,128)(2,1)S(1)}, u32[]{:S(2)}, u32[]{:S(2)}) collective-permute-start(bf16[64,1152]{1,0:T(8,128)(2,1)} %get-tuple-element.164.own_ref.refs_0_.cot_ref), channel_id=1, source_target_pairs={{0,4},{4,0},{8,12},{12,8},{1,5},{5,1},{9,13},{13,9},{2,6},{6,2},{1... | collective-permute-start | bytes 442376 | tf_op jit(solution)/shard_map/ppermute | solution.py:41
  5.8 2.6 %collective-permute-start.4 = (bf16[64,1152]{1,0:T(8,128)(2,1)}, bf16[64,1152]{1,0:T(8,128)(2,1)S(1)}, u32[]{:S(2)}, u32[]{:S(2)}) collective-permute-start(bf16[64,1152]{1,0:T(8,128)(2,1)} %get-tuple-element.164.own_ref.refs_0_.cot_ref), channel_id=1, source_target_pairs={{0,8},{4,12},{8,0},{12,4},{1,9},{5,13},{9,1},{13,5},{2,10},{6,14},... | collective-permute-start | bytes 442376 | tf_op jit(solution)/shard_map/ppermute | solution.py:41
  8.4 3.5 %collective-permute-done.refs_0_ = bf16[64,1152]{1,0:T(8,128)(2,1)S(1)} collective-permute-done((bf16[64,1152]{1,0:T(8,128)(2,1)}, bf16[64,1152]{1,0:T(8,128)(2,1)S(1)}, u32[]{:S(2)}, u32[]{:S(2)}) %collective-permute-start) | collective-permute-done | bytes 147488 | tf_op jit(solution)/shard_map/ppermute | solution.py:41
  11.9 4.6 %attend.1 = (bf16[256,1024]{1,0:T(8,128)(2,1)}, bf16[256,256]{1,0:T(8,128)(2,1)}, bf16[256,128]{1,0:T(8,128)(2,1)}, bf16[256,128]{1,0:T(8,128)(2,1)}, bf16[256,2...) custom-call(s32[1]{0:T(128)} %bitcast.me_ref, ...), custom_call_target="tpu_custom_call" | custom-call | flops 53687091200 | tf_op jit(solution)/shard_map/attend/pallas_call | solution.py:122
  16.6 1.7 collective-permute-start.1
  18.3 1.5 collective-permute-start.2
  20.0 1.7 collective-permute-done.1.refs_0_
  21.7 1.7 collective-permute-done.2.refs_1_
  23.5 2.4 %collective-permute-done.3.refs_2_ = bf16[64,1024]{1,0:T(8,128)(2,1)S(1)} collective-permute-done((bf16[64,1024]{1,0:T(8,128)(2,1)}, bf16[64,1024]{1,0:T(8,128)(2,1)S(1)}, u32[]{:S(2)}, u32[]{:S(2)}) %collective-permute-start.3) | collective-permute-done | bytes 131104 | tf_op jit(solution)/shard_map/ppermute | solution.py:41
  26.5 2.0 norm_two.1
  30.1 3.7 %collective-permute-done.6.refs_1_ = bf16[64,1024]{1,0:T(8,128)(2,1)S(1)} collective-permute-done((bf16[64,1024]{1,0:T(8,128)(2,1)}, bf16[64,1024]{1,0:T(8,128)(2,1)S(1)}, u32[]{:S(2)}, u32[]{:S(2)}) %collective-permute-start.6) | collective-permute-done | bytes 131104 | tf_op jit(solution)/shard_map/ppermute | solution.py:41
  35.0 2.6 %collective-permute-start.7 = (bf16[64,1024]{1,0:T(8,128)(2,1)}, bf16[64,1024]{1,0:T(8,128)(2,1)S(1)}, u32[]{:S(2)}, u32[]{:S(2)}) collective-permute-start(bf16[64,1024]{1,0:T(8,128)(2,1)} %get-tuple-element.173.refs_0_.n_ref), channel_id=1, source_target_pairs={{0,8},{4,12},{8,0},{12,4},{1,9},{5,13},{9,1},{13,5},{2,10},{6,14},... | collective-permute-start | bytes 393224 | tf_op jit(solution)/shard_map/ppermute | solution.py:41
  39.0 1.6 copy-done.1
  40.7 1.5 gate_up_weights.1.wcat
  42.2 2.8 %collective-permute-done.7.refs_2_ = bf16[64,1024]{1,0:T(8,128)(2,1)S(1)} collective-permute-done((bf16[64,1024]{1,0:T(8,128)(2,1)}, bf16[64,1024]{1,0:T(8,128)(2,1)S(1)}, u32[]{:S(2)}, u32[]{:S(2)}) %collective-permute-start.7) | collective-permute-done | bytes 131104 | tf_op jit(solution)/shard_map/ppermute | solution.py:41
  48.2 1.5 collective-permute-start.9
  49.7 1.6 collective-permute-start.10
  51.4 2.2 %counts.1 = f32[1,128]{1,0:T(1,128)S(1)} custom-call(bf16[64,1152]{1,0:T(8,128)(2,1)S(1)} %copy-done.4, bf16[64,1152]{1,0:T(8,128)(2,1)S(1)} %copy-done.14, bf16[64,1152]{1,0:T(8,128)(2,1)S(1)} %copy-done.13, bf16[64,1152]{1,0:T(8,128)(2,1)S(1)} %copy-done.12, bf16[3,64,1152]{2,1,0:T(8,128)(2,1)S(1)} %together.2.far_ref.refs_4_, ...), custom_call_target="tpu_custom_call" | custom-call | tf_op jit(solution)/shard_map/counts/pallas_call | solution.py:122
  53.7 4.1 %experts.4 = (bf16[256,1024]{1,0:T(8,128)(2,1)S(1)}, bf16[256,2048]{1,0:T(8,128)(2,1)S(1)}, bf16[256,1024]{1,0:T(8,128)(2,1)S(1)}, f32[4,64,1152]{2,1,0:T(8,128)S(1)}, f32[4,64,1024]{2,1,0:T(8,128)S(1)}) custom-call(s32[1]{0:T(128)} %bitcast.9.base_ref, bf16[4,64,1024]{2,1,0:T(8,128)(2,1)S(1)} %together.3.x_ref.a0, bf16[64,1152]{1,0:T(8,128)(2,1)S(1)} %copy-done.4, ...), custom_call_target="tpu_custom_call" | custom-call | flops 3355443200 | tf_op jit(solution)/shard_map/experts/pallas_call | solution.py:354
  59.0 5.9 %experts.5 = (bf16[256,1024]{1,0:T(8,128)(2,1)S(1)}, bf16[256,2048]{1,0:T(8,128)(2,1)S(1)}, bf16[256,1024]{1,0:T(8,128)(2,1)S(1)}, bf16[4,64,1152]{2,1,0:T(8,128)(2,1)}, bf16[4,64,1024]{2,1,0:T(8,128)(2,1)S(1)}) custom-call(s32[1]{0:T(128)} %bitcast.9.base_ref, bf16[4,64,1024]{2,1,0:T(8,128)(2,1)S(1)} %collective-permute-done.9.x_ref.a1, ...), custom_call_target="tpu_custom_call" | custom-call | flops 3355443200 | tf_op jit(solution)/shard_map/experts/pallas_call | solution.py:354
  66.0 6.2 %experts.6 = (bf16[256,1024]{1,0:T(8,128)(2,1)S(1)}, bf16[256,2048]{1,0:T(8,128)(2,1)S(1)}, bf16[256,1024]{1,0:T(8,128)(2,1)S(1)}, bf16[4,64,1152]{2,1,0:T(8,128)(2,1)}, bf16[4,64,1024]{2,1,0:T(8,128)(2,1)S(1)}) custom-call(s32[1]{0:T(128)} %bitcast.9.base_ref, bf16[4,64,1024]{2,1,0:T(8,128)(2,1)S(1)} %collective-permute-done.10.x_ref.a2, ...), custom_call_target="tpu_custom_call" | custom-call | flops 3355443200 | tf_op jit(solution)/shard_map/experts/pallas_call | solution.py:354
  73.5 4.6 %experts.7 = (bf16[256,1024]{1,0:T(8,128)(2,1)S(1)}, bf16[256,2048]{1,0:T(8,128)(2,1)S(1)}, bf16[256,1024]{1,0:T(8,128)(2,1)S(1)}, f32[64,1152]{1,0:T(8,128)S(1)...) custom-call(s32[1]{0:T(128)} %bitcast.9.base_ref, ...), custom_call_target="tpu_custom_call" | custom-call | flops 3355443200 | tf_op jit(solution)/shard_map/experts/pallas_call | solution.py:354
  78.2 9.0 %collective-permute-start.18 = (bf16[64,1152]{1,0:T(8,128)(2,1)}, bf16[64,1152]{1,0:T(8,128)(2,1)}, u32[]{:S(2)}, u32[]{:S(2)}) collective-permute-start(bf16[64,1152]{1,0:T(8,128)(2,1)} %get-tuple-element.218), channel_id=1, source_target_pairs={{0,4},{4,0},{8,12},{12,8},{1,5},{5,1},{9,13},{13,9},{2,6},{6,2},{1... | collective-permute-start | bytes 442376 | tf_op jit(solution)/shard_map/ppermute | solution.py:41
  87.2 1.9 collective-permute-start.19
  90.6 10.7 %expert_grads.1.mine_ref = bf16[8,3072,128]{2,1,0:T(8,128)(2,1)} custom-call(bf16[256,1024]{1,0:T(8,128)(2,1)S(1)} %bitcast.20, bf16[256,1024]{1,0:T(8,128)(2,1)S(1)} %bitcast.28, bf16[256,1024]{1,0:T(8,128)(2,1)S(1)} %bitcast.29, bf16[256,1024]{1,0:T(8,128)(2,1)S(1)} %bitcast.30, bf16[256,2048]{1,0:T(8,128)(2,1)S(1)} %get-tuple-element.185.refs_4_, ...), custom_call_target="tpu_custom_call" | custom-call | flops 644245094400 | tf_op jit(solution)/shard_map/expert_grads/pallas_call | solution.py:428
  103.8 2.3 %collective-permute-start.25 = (bf16[64,1152]{1,0:T(8,128)(2,1)S(1)}, bf16[64,1152]{1,0:T(8,128)(2,1)S(1)}, u32[]{:S(2)}, u32[]{:S(2)}) collective-permute-start(bf16[64,1152]{1,0:T(8,128)(2,1)S(1)} %get-tuple-element.240), channel_id=1, source_target_pairs={{0,8},{4,12},{8,0},{12,4},{1,9},{5,13},{9,1},{13,5},{2,10},{6,14},... | collective-permute-start | bytes 442376 | tf_op jit(solution)/shard_map/ppermute | solution.py:41
  106.1 1.5 collective-permute-start.26
  107.6 2.3 %collective-permute-done.23.refs_2_ = bf16[64,1152]{1,0:T(8,128)(2,1)S(1)} collective-permute-done((bf16[64,1152]{1,0:T(8,128)(2,1)S(1)}, bf16[64,1152]{1,0:T(8,128)(2,1)S(1)}, u32[]{:S(2)}, u32[]{:S(2)}) %collective-permute-start.23) | collective-permute-done | bytes 147488 | tf_op jit(solution)/shard_map/ppermute | solution.py:41
  111.0 1.7 collective-permute-start.24
  113.1 4.0 %collective-permute-done.24.refs_1_ = bf16[64,1152]{1,0:T(8,128)(2,1)S(1)} collective-permute-done((bf16[64,1152]{1,0:T(8,128)(2,1)S(1)}, bf16[64,1152]{1,0:T(8,128)(2,1)S(1)}, u32[]{:S(2)}, u32[]{:S(2)}) %collective-permute-start.24) | collective-permute-done | bytes 147488 | tf_op jit(solution)/shard_map/ppermute | solution.py:41
  119.4 2.0 collective-permute-start.29
  123.3 2.6 %collective-permute-done.28.w1 = bf16[64,1152]{1,0:T(8,128)(2,1)S(1)} collective-permute-done((bf16[64,1152]{1,0:T(8,128)(2,1)S(1)}, bf16[64,1152]{1,0:T(8,128)(2,1)S(1)}, u32[]{:S(2)}, u32[]{:S(2)}) %collective-permute-start.28) | collective-permute-done | bytes 147488 | tf_op jit(solution)/shard_map/ppermute | solution.py:41
  125.9 2.9 %collective-permute-done.29.w2 = bf16[64,1152]{1,0:T(8,128)(2,1)S(1)} collective-permute-done((bf16[64,1152]{1,0:T(8,128)(2,1)S(1)}, bf16[64,1152]{1,0:T(8,128)(2,1)S(1)}, u32[]{:S(2)}, u32[]{:S(2)}) %collective-permute-start.29) | collective-permute-done | bytes 147488 | tf_op jit(solution)/shard_map/ppermute | solution.py:41
  129.8 7.5 %attend_back.1 = (f32[8,1024]{1,0:T(8,128)}, f32[64,1024]{1,0:T(8,128)}, bf16[64,1024]{1,0:T(8,128)(2,1)}, bf16[64,1024]{1,0:T(8,128)(2,1)}, bf16[64,1024]{1,0:T...) custom-call(s32[2]{0:T(128)} %pad_add_fusion.me_ref, bf16[64,1152]{1,0:T(8,128)(2,1)} %copy-done.29, ...), custom_call_target="tpu_custom_call" | custom-call | flops 53687091200 | tf_op jit(solution)/shard_map/attend_back/pallas_call | solution.py:122
  137.5 1.6 collective-permute-start.42
  140.5 1.5 copy-done.2
  145.4 1.8 collective-permute-start.36
  147.2 8.7 %collective-permute-done.34.refs_1_ = bf16[64,1024]{1,0:T(8,128)(2,1)S(1)} collective-permute-done((bf16[64,1024]{1,0:T(8,128)(2,1)}, bf16[64,1024]{1,0:T(8,128)(2,1)S(1)}, u32[]{:S(2)}, u32[]{:S(2)}) %collective-permute-start.34) | collective-permute-done | bytes 131104 | tf_op jit(solution)/shard_map/ppermute | solution.py:41
  155.9 2.0 collective-permute-start.40
  158.9 4.7 %both_copies.4 = f32[8,1024,128]{2,1,0:T(8,128)} custom-call(bf16[8,3072,128]{2,1,0:T(8,128)(2,1)} %expert_grads.1.mine_ref, bf16[8,3072,128]{2,1,0:T(8,128)(2,1)} %collective-permute-done.27.other_ref), custom_call_target="tpu_custom_call" | custom-call | bytes 25165824 | tf_op jit(solution)/shard_map/both_copies/pallas_call | solution.py:457
  164.3 2.1 %input_grad.1.refs_0_ = bf16[64,1024]{1,0:T(8,128)(2,1)} custom-call(bf16[64,1024]{1,0:T(8,128)(2,1)} %get-tuple-element.166.x_ref, f32[1,1024]{1,0:T(1,128)} %bitcast.34, f32[64,1024]{1,0:T(8,128)} %copy-done.11, f32[64,1024]{1,0:T(8,128)} %get-tuple-element.275.refs_0_, bf16[64,1024]{1,0:T(8,128)(2,1)} %copy-done.31, bf16[64,1024]{1,0:T(8,128)(2,1)} %copy-done.32, ...), custom_call_target="tpu_custom_call" | custom-call | tf_op jit(solution)/shard_map/input_grad/pallas_call | solution.py:122
  169.1 4.4 %collective-permute-done.40.refs_1_ = bf16[128,896]{1,0:T(8,128)(2,1)S(1)} collective-permute-done((bf16[128,896]{1,0:T(8,128)(2,1)S(1)}, bf16[128,896]{1,0:T(8,128)(2,1)S(1)}, u32[]{:S(2)}, u32[]{:S(2)}) %collective-permute-start.40) | collective-permute-done | bytes 229408 | tf_op jit(solution)/shard_map/ppermute | solution.py:41
  174.6 5.1 %collective-permute-start.44 = (bf16[64,1024]{1,0:T(8,128)(2,1)S(1)}, bf16[64,1024]{1,0:T(8,128)(2,1)S(1)}, u32[]{:S(2)}, u32[]{:S(2)}) collective-permute-start(bf16[64,1024]{1,0:T(8,128)(2,1)S(1)} %get-tuple-element.295), channel_id=1, source_target_pairs={{0,8},{4,12},{8,0},{12,4},{1,9},{5,13},{9,1},{13,5},{2,10},{6,14},... | collective-permute-start | bytes 393224 | tf_op jit(solution)/shard_map/ppermute | solution.py:41
  181.2 4.7 %both_copies.5 = f32[8,1024,128]{2,1,0:T(8,128)} custom-call(bf16[8,3072,128]{2,1,0:T(8,128)(2,1)} %expert_grads.1.mine_ref, bf16[8,3072,128]{2,1,0:T(8,128)(2,1)} %collective-permute-done.27.other_ref), custom_call_target="tpu_custom_call" | custom-call | bytes 25165824 | tf_op jit(solution)/shard_map/both_copies/pallas_call | solution.py:457
  186.8 2.9 %collective-permute-done.44.refs_2_ = bf16[64,1024]{1,0:T(8,128)(2,1)S(1)} collective-permute-done((bf16[64,1024]{1,0:T(8,128)(2,1)S(1)}, bf16[64,1024]{1,0:T(8,128)(2,1)S(1)}, u32[]{:S(2)}, u32[]{:S(2)}) %collective-permute-start.44) | collective-permute-done | bytes 131104 | tf_op jit(solution)/shard_map/ppermute | solution.py:41
  191.6 1.8 collective-permute-start.48
  193.4 4.8 %both_copies.3 = f32[8,128,1024]{2,1,0:T(8,128)} custom-call(bf16[8,3072,128]{2,1,0:T(8,128)(2,1)} %expert_grads.1.mine_ref, bf16[8,3072,128]{2,1,0:T(8,128)(2,1)} %collective-permute-done.27.other_ref), custom_call_target="tpu_custom_call" | custom-call | bytes 25165824 | tf_op jit(solution)/shard_map/both_copies/pallas_call | solution.py:457
  (161 shorter events, 40.9 us)
Async XLA Ops:
  2.8 9.1 %collective-permute-start = (bf16[64,1152]{1,0:T(8,128)(2,1)}, bf16[64,1152]{1,0:T(8,128)(2,1)S(1)}, u32[]{:S(2)}, u32[]{:S(2)}) collective-permute-start(bf16[64,1152]{1,0:T(8,128)(2,1)} %get-tuple-element.164.own_ref.refs_0_.cot_ref), channel_id=1, source_target_pairs={{0,4},{4,0},{8,12},{12,8},{1,5},{5,1},{9,13},{13,9},{2,6},{6,2},{1... | collective-permute-start | bytes 442376 | tf_op jit(solution)/shard_map/ppermute | solution.py:41
  5.8 22.7 %collective-permute-start.4 = (bf16[64,1152]{1,0:T(8,128)(2,1)}, bf16[64,1152]{1,0:T(8,128)(2,1)S(1)}, u32[]{:S(2)}, u32[]{:S(2)}) collective-permute-start(bf16[64,1152]{1,0:T(8,128)(2,1)} %get-tuple-element.164.own_ref.refs_0_.cot_ref), channel_id=1, source_target_pairs={{0,8},{4,12},{8,0},{12,4},{1,9},{5,13},{9,1},{13,5},{2,10},{6,14},... | collective-permute-start | bytes 442376 | tf_op jit(solution)/shard_map/ppermute | solution.py:41
  8.4 20.1 %collective-permute-start.5 = (bf16[64,1152]{1,0:T(8,128)(2,1)}, bf16[64,1152]{1,0:T(8,128)(2,1)S(1)}, u32[]{:S(2)}, u32[]{:S(2)}) collective-permute-start(bf16[64,1152]{1,0:T(8,128)(2,1)} %get-tuple-element.164.own_ref.refs_0_.cot_ref), channel_id=1, source_target_pairs={{0,12},{4,8},{8,4},{12,0},{1,13},{5,9},{9,5},{13,1},{2,14},{6,10},... | collective-permute-start | bytes 442376 | tf_op jit(solution)/shard_map/ppermute | solution.py:41
  16.6 5.2 %collective-permute-start.1 = (bf16[64,1024]{1,0:T(8,128)(2,1)}, bf16[64,1024]{1,0:T(8,128)(2,1)S(1)}, u32[]{:S(2)}, u32[]{:S(2)}) collective-permute-start(bf16[64,1024]{1,0:T(8,128)(2,1)} %get-tuple-element.168), channel_id=1, source_target_pairs={{0,1},{1,0},{2,3},{3,2},{4,5},{5,4},{6,7},{7,6},{8,9},{9,8},{10,11... | collective-permute-start | bytes 393224 | tf_op jit(solution)/shard_map/ppermute | solution.py:41
  18.3 5.2 %collective-permute-start.2 = (bf16[64,1024]{1,0:T(8,128)(2,1)}, bf16[64,1024]{1,0:T(8,128)(2,1)S(1)}, u32[]{:S(2)}, u32[]{:S(2)}) collective-permute-start(bf16[64,1024]{1,0:T(8,128)(2,1)} %get-tuple-element.169), channel_id=1, source_target_pairs={{0,2},{1,3},{2,0},{3,1},{4,6},{5,7},{6,4},{7,5},{8,10},{9,11},{10,... | collective-permute-start | bytes 393224 | tf_op jit(solution)/shard_map/ppermute | solution.py:41
  19.8 6.1 %collective-permute-start.3 = (bf16[64,1024]{1,0:T(8,128)(2,1)}, bf16[64,1024]{1,0:T(8,128)(2,1)S(1)}, u32[]{:S(2)}, u32[]{:S(2)}) collective-permute-start(bf16[64,1024]{1,0:T(8,128)(2,1)} %get-tuple-element.170), channel_id=1, source_target_pairs={{0,3},{1,2},{2,1},{3,0},{4,7},{5,6},{6,5},{7,4},{8,11},{9,10},{10,... | collective-permute-start | bytes 393224 | tf_op jit(solution)/shard_map/ppermute | solution.py:41
  28.5 5.2 %collective-permute-start.6 = (bf16[64,1024]{1,0:T(8,128)(2,1)}, bf16[64,1024]{1,0:T(8,128)(2,1)S(1)}, u32[]{:S(2)}, u32[]{:S(2)}) collective-permute-start(bf16[64,1024]{1,0:T(8,128)(2,1)} %get-tuple-element.173.refs_0_.n_ref), channel_id=1, source_target_pairs={{0,4},{4,0},{8,12},{12,8},{1,5},{5,1},{9,13},{13,9},{2,6},{6,2},{1... | collective-permute-start | bytes 393224 | tf_op jit(solution)/shard_map/ppermute | solution.py:41
  29.0 22.3 %collective-permute-start.11 = (bf16[3,64,1152]{2,1,0:T(8,128)(2,1)S(1)}, bf16[3,64,1152]{2,1,0:T(8,128)(2,1)}, u32[]{:S(2)}, u32[]{:S(2)}) collective-permute-start(bf16[3,64,1152]{2,1,0:T(8,128)(2,1)S(1)} %together.2.far_ref.refs_4_), channel_id=1, source_target_pairs={{0,1},{1,0},{2,3},{3,2},{4,5},{5,4},{6,7},{7,6},{8,9},{9,8},{10,11... | collective-permute-start | bytes 1327112 | tf_op jit(solution)/shard_map/ppermute | solution.py:41
  29.6 21.7 %collective-permute-start.12 = (bf16[3,64,1152]{2,1,0:T(8,128)(2,1)S(1)}, bf16[3,64,1152]{2,1,0:T(8,128)(2,1)}, u32[]{:S(2)}, u32[]{:S(2)}) collective-permute-start(bf16[3,64,1152]{2,1,0:T(8,128)(2,1)S(1)} %together.2.far_ref.refs_4_), channel_id=1, source_target_pairs={{0,2},{1,3},{2,0},{3,1},{4,6},{5,7},{6,4},{7,5},{8,10},{9,11},{10,... | collective-permute-start | bytes 1327112 | tf_op jit(solution)/shard_map/ppermute | solution.py:41
  34.4 16.9 %collective-permute-start.14 = (bf16[3,64,1152]{2,1,0:T(8,128)(2,1)S(1)}, bf16[3,64,1152]{2,1,0:T(8,128)(2,1)S(1)}, u32[]{:S(2)}, u32[]{:S(2)}) collective-permute-start(bf16[3,64,1152]{2,1,0:T(8,128)(2,1)S(1)} %together.2.far_ref.refs_4_), channel_id=1, source_target_pairs={{0,3},{1,2},{2,1},{3,0},{4,7},{5,6},{6,5},{7,4},{8,11},{9,10},{10,... | collective-permute-start | bytes 1327112 | tf_op jit(solution)/shard_map/ppermute | solution.py:41
  35.0 10.1 %collective-permute-start.7 = (bf16[64,1024]{1,0:T(8,128)(2,1)}, bf16[64,1024]{1,0:T(8,128)(2,1)S(1)}, u32[]{:S(2)}, u32[]{:S(2)}) collective-permute-start(bf16[64,1024]{1,0:T(8,128)(2,1)} %get-tuple-element.173.refs_0_.n_ref), channel_id=1, source_target_pairs={{0,8},{4,12},{8,0},{12,4},{1,9},{5,13},{9,1},{13,5},{2,10},{6,14},... | collective-permute-start | bytes 393224 | tf_op jit(solution)/shard_map/ppermute | solution.py:41
  37.6 8.1 %collective-permute-start.8 = (bf16[64,1024]{1,0:T(8,128)(2,1)}, bf16[64,1024]{1,0:T(8,128)(2,1)S(1)}, u32[]{:S(2)}, u32[]{:S(2)}) collective-permute-start(bf16[64,1024]{1,0:T(8,128)(2,1)} %get-tuple-element.173.refs_0_.n_ref), channel_id=1, source_target_pairs={{0,12},{4,8},{8,4},{12,0},{1,13},{5,9},{9,5},{13,1},{2,14},{6,10},... | collective-permute-start | bytes 393224 | tf_op jit(solution)/shard_map/ppermute | solution.py:41
  48.2 10.8 %collective-permute-start.9 = (bf16[4,64,1024]{2,1,0:T(8,128)(2,1)S(1)}, bf16[4,64,1024]{2,1,0:T(8,128)(2,1)S(1)}, u32[]{:S(2)}, u32[]{:S(2)}) collective-permute-start(bf16[4,64,1024]{2,1,0:T(8,128)(2,1)S(1)} %together.3.x_ref.a0), channel_id=1, source_target_pairs={{0,1},{1,0},{2,3},{3,2},{4,5},{5,4},{6,7},{7,6},{8,9},{9,8},{10,11... | collective-permute-start | bytes 1572872 | tf_op jit(solution)/shard_map/ppermute | solution.py:41
  49.7 16.3 %collective-permute-start.10 = (bf16[4,64,1024]{2,1,0:T(8,128)(2,1)S(1)}, bf16[4,64,1024]{2,1,0:T(8,128)(2,1)S(1)}, u32[]{:S(2)}, u32[]{:S(2)}) collective-permute-start(bf16[4,64,1024]{2,1,0:T(8,128)(2,1)S(1)} %together.3.x_ref.a0), channel_id=1, source_target_pairs={{0,2},{1,3},{2,0},{3,1},{4,6},{5,7},{6,4},{7,5},{8,10},{9,11},{10,... | collective-permute-start | bytes 1572872 | tf_op jit(solution)/shard_map/ppermute | solution.py:41
  53.6 4.8 %collective-permute-start.15 = (f32[1,128]{1,0:T(1,128)S(1)}, f32[1,128]{1,0:T(1,128)S(1)}, u32[]{:S(2)}, u32[]{:S(2)}) collective-permute-start(f32[1,128]{1,0:T(1,128)S(1)} %counts.1), channel_id=1, source_target_pairs={{0,16},{16,0},{1,17},{17,1},{2,18},{18,2},{3,19},{19,3},{4,20},{20... | collective-permute-start | bytes 1544 | tf_op jit(solution)/shard_map/ppermute | solution.py:41
  57.8 15.7 %collective-permute-start.13 = (bf16[4,64,1024]{2,1,0:T(8,128)(2,1)S(1)}, bf16[4,64,1024]{2,1,0:T(8,128)(2,1)S(1)}, u32[]{:S(2)}, u32[]{:S(2)}) collective-permute-start(bf16[4,64,1024]{2,1,0:T(8,128)(2,1)S(1)} %together.3.x_ref.a0), channel_id=1, source_target_pairs={{0,3},{1,2},{2,1},{3,0},{4,7},{5,6},{6,5},{7,4},{8,11},{9,10},{10,... | collective-permute-start | bytes 1572872 | tf_op jit(solution)/shard_map/ppermute | solution.py:41
  65.0 36.3 %collective-permute-start.16 = (bf16[4,64,1152]{2,1,0:T(8,128)(2,1)}, bf16[4,64,1152]{2,1,0:T(8,128)(2,1)}, u32[]{:S(2)}, u32[]{:S(2)}) collective-permute-start(bf16[4,64,1152]{2,1,0:T(8,128)(2,1)} %get-tuple-element.192), channel_id=1, source_target_pairs={{0,1},{1,0},{2,3},{3,2},{4,5},{5,4},{6,7},{7,6},{8,9},{9,8},{10,11... | collective-permute-start | bytes 1769480 | tf_op jit(solution)/shard_map/ppermute | solution.py:41
  72.2 29.1 %collective-permute-start.17 = (bf16[4,64,1152]{2,1,0:T(8,128)(2,1)}, bf16[4,64,1152]{2,1,0:T(8,128)(2,1)}, u32[]{:S(2)}, u32[]{:S(2)}) collective-permute-start(bf16[4,64,1152]{2,1,0:T(8,128)(2,1)} %get-tuple-element.201), channel_id=1, source_target_pairs={{0,2},{1,3},{2,0},{3,1},{4,6},{5,7},{6,4},{7,5},{8,10},{9,11},{10,... | collective-permute-start | bytes 1769480 | tf_op jit(solution)/shard_map/ppermute | solution.py:41
  78.2 23.1 %collective-permute-start.18 = (bf16[64,1152]{1,0:T(8,128)(2,1)}, bf16[64,1152]{1,0:T(8,128)(2,1)}, u32[]{:S(2)}, u32[]{:S(2)}) collective-permute-start(bf16[64,1152]{1,0:T(8,128)(2,1)} %get-tuple-element.218), channel_id=1, source_target_pairs={{0,4},{4,0},{8,12},{12,8},{1,5},{5,1},{9,13},{13,9},{2,6},{6,2},{1... | collective-permute-start | bytes 442376 | tf_op jit(solution)/shard_map/ppermute | solution.py:41
  87.2 14.1 %collective-permute-start.19 = (bf16[64,1152]{1,0:T(8,128)(2,1)}, bf16[64,1152]{1,0:T(8,128)(2,1)}, u32[]{:S(2)}, u32[]{:S(2)}) collective-permute-start(bf16[64,1152]{1,0:T(8,128)(2,1)} %get-tuple-element.219), channel_id=1, source_target_pairs={{0,8},{4,12},{8,0},{12,4},{1,9},{5,13},{9,1},{13,5},{2,10},{6,14},... | collective-permute-start | bytes 442376 | tf_op jit(solution)/shard_map/ppermute | solution.py:41
  89.1 12.2 %collective-permute-start.20 = (bf16[64,1152]{1,0:T(8,128)(2,1)}, bf16[64,1152]{1,0:T(8,128)(2,1)}, u32[]{:S(2)}, u32[]{:S(2)}) collective-permute-start(bf16[64,1152]{1,0:T(8,128)(2,1)} %get-tuple-element.220), channel_id=1, source_target_pairs={{0,12},{4,8},{8,4},{12,0},{1,13},{5,9},{9,5},{13,1},{2,14},{6,10},... | collective-permute-start | bytes 442376 | tf_op jit(solution)/shard_map/ppermute | solution.py:41
  102.7 14.4 %collective-permute-start.21 = (bf16[4,64,1024]{2,1,0:T(8,128)(2,1)S(1)}, bf16[4,64,1024]{2,1,0:T(8,128)(2,1)S(1)}, u32[]{:S(2)}, u32[]{:S(2)}) collective-permute-start(bf16[4,64,1024]{2,1,0:T(8,128)(2,1)S(1)} %get-tuple-element.230), channel_id=1, source_target_pairs={{0,1},{1,0},{2,3},{3,2},{4,5},{5,4},{6,7},{7,6},{8,9},{9,8},{10,11... | collective-permute-start | bytes 1572872 | tf_op jit(solution)/shard_map/ppermute | solution.py:41
  103.2 13.9 %collective-permute-start.22 = (bf16[4,64,1024]{2,1,0:T(8,128)(2,1)S(1)}, bf16[4,64,1024]{2,1,0:T(8,128)(2,1)S(1)}, u32[]{:S(2)}, u32[]{:S(2)}) collective-permute-start(bf16[4,64,1024]{2,1,0:T(8,128)(2,1)S(1)} %get-tuple-element.231), channel_id=1, source_target_pairs={{0,2},{1,3},{2,0},{3,1},{4,6},{5,7},{6,4},{7,5},{8,10},{9,11},{10,... | collective-permute-start | bytes 1572872 | tf_op jit(solution)/shard_map/ppermute | solution.py:41
  103.2 6.7 %collective-permute-start.23 = (bf16[64,1152]{1,0:T(8,128)(2,1)S(1)}, bf16[64,1152]{1,0:T(8,128)(2,1)S(1)}, u32[]{:S(2)}, u32[]{:S(2)}) collective-permute-start(bf16[64,1152]{1,0:T(8,128)(2,1)S(1)} %get-tuple-element.233), channel_id=1, source_target_pairs={{0,4},{4,0},{8,12},{12,8},{1,5},{5,1},{9,13},{13,9},{2,6},{6,2},{1... | collective-permute-start | bytes 442376 | tf_op jit(solution)/shard_map/ppermute | solution.py:41
  103.8 8.9 %collective-permute-start.25 = (bf16[64,1152]{1,0:T(8,128)(2,1)S(1)}, bf16[64,1152]{1,0:T(8,128)(2,1)S(1)}, u32[]{:S(2)}, u32[]{:S(2)}) collective-permute-start(bf16[64,1152]{1,0:T(8,128)(2,1)S(1)} %get-tuple-element.240), channel_id=1, source_target_pairs={{0,8},{4,12},{8,0},{12,4},{1,9},{5,13},{9,1},{13,5},{2,10},{6,14},... | collective-permute-start | bytes 442376 | tf_op jit(solution)/shard_map/ppermute | solution.py:41
  106.1 7.0 %collective-permute-start.26 = (bf16[64,1152]{1,0:T(8,128)(2,1)S(1)}, bf16[64,1152]{1,0:T(8,128)(2,1)S(1)}, u32[]{:S(2)}, u32[]{:S(2)}) collective-permute-start(bf16[64,1152]{1,0:T(8,128)(2,1)S(1)} %get-tuple-element.241), channel_id=1, source_target_pairs={{0,12},{4,8},{8,4},{12,0},{1,13},{5,9},{9,5},{13,1},{2,14},{6,10},... | collective-permute-start | bytes 442376 | tf_op jit(solution)/shard_map/ppermute | solution.py:41
  111.0 6.1 %collective-permute-start.24 = (bf16[64,1152]{1,0:T(8,128)(2,1)S(1)}, bf16[64,1152]{1,0:T(8,128)(2,1)S(1)}, u32[]{:S(2)}, u32[]{:S(2)}) collective-permute-start(bf16[64,1152]{1,0:T(8,128)(2,1)S(1)} %through.1), channel_id=1, source_target_pairs={{0,3},{1,2},{2,1},{3,0},{4,7},{5,6},{6,5},{7,4},{8,11},{9,10},{10,... | collective-permute-start | bytes 442376 | tf_op jit(solution)/shard_map/ppermute | solution.py:41
  119.2 10.5 %collective-permute-start.27 = (bf16[8,3072,128]{2,1,0:T(8,128)(2,1)}, bf16[8,3072,128]{2,1,0:T(8,128)(2,1)}, u32[]{:S(2)}, u32[]{:S(2)}) collective-permute-start(bf16[8,3072,128]{2,1,0:T(8,128)(2,1)} %expert_grads.1.mine_ref), channel_id=1, source_target_pairs={{0,16},{16,0},{1,17},{17,1},{2,18},{18,2},{3,19},{19,3},{4,20},{20... | collective-permute-start | bytes 18874376 | tf_op jit(solution)/shard_map/ppermute | solution.py:41
  119.2 6.6 %collective-permute-start.28 = (bf16[64,1152]{1,0:T(8,128)(2,1)S(1)}, bf16[64,1152]{1,0:T(8,128)(2,1)S(1)}, u32[]{:S(2)}, u32[]{:S(2)}) collective-permute-start(bf16[64,1152]{1,0:T(8,128)(2,1)S(1)} %get-tuple-element.256.w0), channel_id=1, source_target_pairs={{0,1},{1,0},{2,3},{3,2},{4,5},{5,4},{6,7},{7,6},{8,9},{9,8},{10,11... | collective-permute-start | bytes 442376 | tf_op jit(solution)/shard_map/ppermute | solution.py:41
  119.4 9.4 %collective-permute-start.29 = (bf16[64,1152]{1,0:T(8,128)(2,1)S(1)}, bf16[64,1152]{1,0:T(8,128)(2,1)S(1)}, u32[]{:S(2)}, u32[]{:S(2)}) collective-permute-start(bf16[64,1152]{1,0:T(8,128)(2,1)S(1)} %get-tuple-element.256.w0), channel_id=1, source_target_pairs={{0,2},{1,3},{2,0},{3,1},{4,6},{5,7},{6,4},{7,5},{8,10},{9,11},{10,... | collective-permute-start | bytes 442376 | tf_op jit(solution)/shard_map/ppermute | solution.py:41
  121.4 7.4 %collective-permute-start.30 = (bf16[64,1152]{1,0:T(8,128)(2,1)S(1)}, bf16[64,1152]{1,0:T(8,128)(2,1)S(1)}, u32[]{:S(2)}, u32[]{:S(2)}) collective-permute-start(bf16[64,1152]{1,0:T(8,128)(2,1)S(1)} %get-tuple-element.256.w0), channel_id=1, source_target_pairs={{0,3},{1,2},{2,1},{3,0},{4,7},{5,6},{6,5},{7,4},{8,11},{9,10},{10,... | collective-permute-start | bytes 442376 | tf_op jit(solution)/shard_map/ppermute | solution.py:41
  137.3 3.2 %collective-permute-start.31 = (bf16[512,896]{1,0:T(8,128)(2,1)}, bf16[512,896]{1,0:T(8,128)(2,1)S(1)}, u32[]{:S(2)}, u32[]{:S(2)}) collective-permute-start(bf16[512,896]{1,0:T(8,128)(2,1)} %get-tuple-element.268), channel_id=1, source_target_pairs={{0,16},{16,0},{1,17},{17,1},{2,18},{18,2},{3,19},{19,3},{4,20},{20... | collective-permute-start | bytes 2752520 | tf_op jit(solution)/shard_map/ppermute | solution.py:41
  137.5 29.6 %collective-permute-start.42 = (bf16[4,64,1024]{2,1,0:T(8,128)(2,1)S(1)}, bf16[4,64,1024]{2,1,0:T(8,128)(2,1)S(1)}, u32[]{:S(2)}, u32[]{:S(2)}) collective-permute-start(bf16[4,64,1024]{2,1,0:T(8,128)(2,1)S(1)} %copy-done.25), channel_id=1, source_target_pairs={{0,3},{1,2},{2,1},{3,0},{4,7},{5,6},{6,5},{7,4},{8,11},{9,10},{10,... | collective-permute-start | bytes 1572872 | tf_op jit(solution)/shard_map/ppermute | solution.py:41
  143.1 20.6 %collective-permute-start.33 = (bf16[128,896]{1,0:T(8,128)(2,1)S(1)}, bf16[128,896]{1,0:T(8,128)(2,1)S(1)}, u32[]{:S(2)}, u32[]{:S(2)}) collective-permute-start(bf16[128,896]{1,0:T(8,128)(2,1)S(1)} %get-tuple-element.270), channel_id=1, source_target_pairs={{0,4},{4,0},{8,12},{12,8},{1,5},{5,1},{9,13},{13,9},{2,6},{6,2},{1... | collective-permute-start | bytes 688136 | tf_op jit(solution)/shard_map/ppermute | solution.py:41
  143.7 12.2 %collective-permute-start.34 = (bf16[64,1024]{1,0:T(8,128)(2,1)}, bf16[64,1024]{1,0:T(8,128)(2,1)S(1)}, u32[]{:S(2)}, u32[]{:S(2)}) collective-permute-start(bf16[64,1024]{1,0:T(8,128)(2,1)} %get-tuple-element.272), channel_id=1, source_target_pairs={{0,1},{1,0},{2,3},{3,2},{4,5},{5,4},{6,7},{7,6},{8,9},{9,8},{10,11... | collective-permute-start | bytes 393224 | tf_op jit(solution)/shard_map/ppermute | solution.py:41
  144.9 13.0 %collective-permute-start.35 = (bf16[64,1024]{1,0:T(8,128)(2,1)}, bf16[64,1024]{1,0:T(8,128)(2,1)S(1)}, u32[]{:S(2)}, u32[]{:S(2)}) collective-permute-start(bf16[64,1024]{1,0:T(8,128)(2,1)} %get-tuple-element.273), channel_id=1, source_target_pairs={{0,2},{1,3},{2,0},{3,1},{4,6},{5,7},{6,4},{7,5},{8,10},{9,11},{10,... | collective-permute-start | bytes 393224 | tf_op jit(solution)/shard_map/ppermute | solution.py:41
  145.4 18.2 %collective-permute-start.36 = (bf16[64,1024]{1,0:T(8,128)(2,1)}, bf16[64,1024]{1,0:T(8,128)(2,1)S(1)}, u32[]{:S(2)}, u32[]{:S(2)}) collective-permute-start(bf16[64,1024]{1,0:T(8,128)(2,1)} %get-tuple-element.274), channel_id=1, source_target_pairs={{0,3},{1,2},{2,1},{3,0},{4,7},{5,6},{6,5},{7,4},{8,11},{9,10},{10,... | collective-permute-start | bytes 393224 | tf_op jit(solution)/shard_map/ppermute | solution.py:41
  155.9 17.6 %collective-permute-start.40 = (bf16[128,896]{1,0:T(8,128)(2,1)S(1)}, bf16[128,896]{1,0:T(8,128)(2,1)S(1)}, u32[]{:S(2)}, u32[]{:S(2)}) collective-permute-start(bf16[128,896]{1,0:T(8,128)(2,1)S(1)} %get-tuple-element.282), channel_id=1, source_target_pairs={{0,8},{4,12},{8,0},{12,4},{1,9},{5,13},{9,1},{13,5},{2,10},{6,14},... | collective-permute-start | bytes 688136 | tf_op jit(solution)/shard_map/ppermute | solution.py:41
  157.9 16.7 %collective-permute-start.41 = (bf16[128,896]{1,0:T(8,128)(2,1)S(1)}, bf16[128,896]{1,0:T(8,128)(2,1)S(1)}, u32[]{:S(2)}, u32[]{:S(2)}) collective-permute-start(bf16[128,896]{1,0:T(8,128)(2,1)S(1)} %get-tuple-element.283), channel_id=1, source_target_pairs={{0,12},{4,8},{8,4},{12,0},{1,13},{5,9},{9,5},{13,1},{2,14},{6,10},... | collective-permute-start | bytes 688136 | tf_op jit(solution)/shard_map/ppermute | solution.py:41
  166.4 13.4 %collective-permute-start.37 = (bf16[64,1024]{1,0:T(8,128)(2,1)}, bf16[64,1024]{1,0:T(8,128)(2,1)S(1)}, u32[]{:S(2)}, u32[]{:S(2)}) collective-permute-start(bf16[64,1024]{1,0:T(8,128)(2,1)} %input_grad.1.refs_0_), channel_id=1, source_target_pairs={{0,1},{1,0},{2,3},{3,2},{4,5},{5,4},{6,7},{7,6},{8,9},{9,8},{10,11... | collective-permute-start | bytes 393224 | tf_op jit(solution)/shard_map/ppermute | solution.py:41
  167.4 19.5 %collective-permute-start.43 = (bf16[64,1024]{1,0:T(8,128)(2,1)S(1)}, bf16[64,1024]{1,0:T(8,128)(2,1)S(1)}, u32[]{:S(2)}, u32[]{:S(2)}) collective-permute-start(bf16[64,1024]{1,0:T(8,128)(2,1)S(1)} %get-tuple-element.294), channel_id=1, source_target_pairs={{0,4},{4,0},{8,12},{12,8},{1,5},{5,1},{9,13},{13,9},{2,6},{6,2},{1... | collective-permute-start | bytes 393224 | tf_op jit(solution)/shard_map/ppermute | solution.py:41
  168.0 18.8 %collective-permute-start.38 = (bf16[64,1024]{1,0:T(8,128)(2,1)}, bf16[64,1024]{1,0:T(8,128)(2,1)S(1)}, u32[]{:S(2)}, u32[]{:S(2)}) collective-permute-start(bf16[64,1024]{1,0:T(8,128)(2,1)} %input_grad.1.refs_0_), channel_id=1, source_target_pairs={{0,2},{1,3},{2,0},{3,1},{4,6},{5,7},{6,4},{7,5},{8,10},{9,11},{10,... | collective-permute-start | bytes 393224 | tf_op jit(solution)/shard_map/ppermute | solution.py:41
  173.5 13.3 %collective-permute-start.39 = (bf16[64,1024]{1,0:T(8,128)(2,1)}, bf16[64,1024]{1,0:T(8,128)(2,1)S(1)}, u32[]{:S(2)}, u32[]{:S(2)}) collective-permute-start(bf16[64,1024]{1,0:T(8,128)(2,1)} %input_grad.1.refs_0_), channel_id=1, source_target_pairs={{0,3},{1,2},{2,1},{3,0},{4,7},{5,6},{6,5},{7,4},{8,11},{9,10},{10,... | collective-permute-start | bytes 393224 | tf_op jit(solution)/shard_map/ppermute | solution.py:41
  174.6 15.2 %collective-permute-start.44 = (bf16[64,1024]{1,0:T(8,128)(2,1)S(1)}, bf16[64,1024]{1,0:T(8,128)(2,1)S(1)}, u32[]{:S(2)}, u32[]{:S(2)}) collective-permute-start(bf16[64,1024]{1,0:T(8,128)(2,1)S(1)} %get-tuple-element.295), channel_id=1, source_target_pairs={{0,8},{4,12},{8,0},{12,4},{1,9},{5,13},{9,1},{13,5},{2,10},{6,14},... | collective-permute-start | bytes 393224 | tf_op jit(solution)/shard_map/ppermute | solution.py:41
  179.8 10.0 %collective-permute-start.45 = (bf16[64,1024]{1,0:T(8,128)(2,1)S(1)}, bf16[64,1024]{1,0:T(8,128)(2,1)S(1)}, u32[]{:S(2)}, u32[]{:S(2)}) collective-permute-start(bf16[64,1024]{1,0:T(8,128)(2,1)S(1)} %get-tuple-element.296), channel_id=1, source_target_pairs={{0,12},{4,8},{8,4},{12,0},{1,13},{5,9},{9,5},{13,1},{2,14},{6,10},... | collective-permute-start | bytes 393224 | tf_op jit(solution)/shard_map/ppermute | solution.py:41
  189.8 10.1 %collective-permute-start.46 = (bf16[80,1024]{1,0:T(8,128)(2,1)S(1)}, bf16[80,1024]{1,0:T(8,128)(2,1)S(1)}, u32[]{:S(2)}, u32[]{:S(2)}) collective-permute-start(bf16[80,1024]{1,0:T(8,128)(2,1)S(1)} %out_piece.1.refs_0_), channel_id=1, source_target_pairs={{0,1},{1,0},{2,3},{3,2},{4,5},{5,4},{6,7},{7,6},{8,9},{9,8},{10,11... | collective-permute-start | bytes 491528 | tf_op jit(solution)/shard_map/ppermute | solution.py:41
  190.5 9.4 %collective-permute-start.47 = (bf16[80,1024]{1,0:T(8,128)(2,1)S(1)}, bf16[80,1024]{1,0:T(8,128)(2,1)S(1)}, u32[]{:S(2)}, u32[]{:S(2)}) collective-permute-start(bf16[80,1024]{1,0:T(8,128)(2,1)S(1)} %out_piece.1.refs_0_), channel_id=1, source_target_pairs={{0,2},{1,3},{2,0},{3,1},{4,6},{5,7},{6,4},{7,5},{8,10},{9,11},{10,... | collective-permute-start | bytes 491528 | tf_op jit(solution)/shard_map/ppermute | solution.py:41
  191.6 8.4 %collective-permute-start.48 = (bf16[80,1024]{1,0:T(8,128)(2,1)S(1)}, bf16[80,1024]{1,0:T(8,128)(2,1)S(1)}, u32[]{:S(2)}, u32[]{:S(2)}) collective-permute-start(bf16[80,1024]{1,0:T(8,128)(2,1)S(1)} %out_piece.1.refs_0_), channel_id=1, source_target_pairs={{0,3},{1,2},{2,1},{3,0},{4,7},{5,6},{6,5},{7,4},{8,11},{9,10},{10,... | collective-permute-start | bytes 491528 | tf_op jit(solution)/shard_map/ppermute | solution.py:41
  (41 other events, 413.3 us)

commit v11 on v9

--- a/solution.py
+++ b/solution.py
@@ -247,14 +247,17 @@
     pieces, out = refs[:-1], refs[-1]
     total = 0.0
     for piece in pieces:
-        width = piece.shape[-1] - LANES
-        blocks = [piece[:, width:]] if len(piece.shape) == 2 else [
-            piece[i, :, width:] for i in range(piece.shape[0])
-        ]
-        for routes in blocks:
+        blocks = [piece] if len(piece.shape) == 2 else [piece.at[i] for i in range(piece.shape[0])]
+        for block in blocks:
+            routes = block[...]
             named = chosen_of(lane_of(routes.shape), routes).astype(F32)
             total = total + jnp.sum(named, axis=0, keepdims=True)
     out[...] = total
+
+
+def last_lanes(x):
+    at = x.shape[-1] // LANES - 1
+    return pl.BlockSpec((*x.shape[:-1], LANES), lambda i: (0,) * (x.ndim - 1) + (at,))
 
 
 def weights_kernel(wg_ref, wu_ref, out_ref):
@@ -279,7 +282,7 @@
 
 
 def experts_kernel(experts, base_ref, x_ref, own_ref, far_ref, router_ref, wcat, wd_ref, *refs):
-    cot_ref, dgu_ref, hg_ref, *ds, m_ref = refs
+    cot_ref, dgu_ref, hg_ref, *ds, m_ref, v_ref = refs
     hidden = LANES
     pair = 2 * hidden
     rows, width = cot_ref.shape
@@ -294,11 +297,12 @@
     _, gates = router_of(x, router_ref, routes, experts)
     lane = lane_of(gates.shape)
     dots = jnp.zeros(gates.shape, F32)
+    v_ref[...] = nt(cot_ref[...], wd_ref[...])
     for e in range(hg_ref.shape[1] // hidden):
         mine = lane == base_ref[0] + e
         g = jnp.sum(jnp.where(mine, gates, 0.0), axis=-1, keepdims=True)
         both = nn(x, wcat[:, e * pair : (e + 1) * pair])
-        v = nt(cot_ref[...], wd_ref[e * hidden : (e + 1) * hidden, :])
+        v = v_ref[:, e * hidden : (e + 1) * hidden]
         gate, up = both[:, :hidden], both[:, hidden:]
         sig = 1.0 / (1.0 + jnp.exp(-gate))
         act = gate * sig
@@ -366,6 +370,7 @@
             *d_shapes,
             shape(dims(width), kind),
         ],
+        scratch_shapes=[pltpu.VMEM((step, inner), F32)],
         compiler_params=pltpu.CompilerParams(vmem_limit_bytes=(14 if few else 30) * MIB),
         cost_estimate=pl.CostEstimate(flops=int(100.0*(total * width * inner // 8)), bytes_accessed=0, transcendentals=0),
         name="experts",
@@ -764,7 +769,10 @@
     run = functools.partial(
         run_experts, experts, base, router=router, wcat=wcat, down_flat=down_flat
     )
-    counts = call(counts_kernel, [shape((1, LANES), F32)], (*cot_near, *cot_far), "counts")[0]
+    named = (*cot_near, *cot_far)
+    counts = call(
+        counts_kernel, [shape((1, LANES), F32)], named, "counts", [last_lanes(x) for x in named]
+    )[0]
     counts = counts + swap(counts, "dp", 1)
     balance = experts * (counts / (token_count * TOP)) / token_count
     made = [run(twos[0], cot_near[0], cot_far[0], kind=F32)]

time: 202 us -> 203 us (level)
  no operation moved by 1% of the time
where the time goes in v11:
time: 203 us; the launch traced here: 202 us
  Pallas kernels  76.5 us (38%)
  starting transfers between devices  65.4 us (32%)
  waiting for transfers between devices  49.4 us (24%)
  local copies, waits for them, and re-layouts  8.43 us (4%)
    ppermute x49, starting transfers between devices, swap(): return lax.ppermute(x, axis, [(i, i ^ distance) for i in range(size)])  65.4 us
    ppermute x49, waiting for transfers between devices, swap(): return lax.ppermute(x, axis, [(i, i ^ distance) for i in range(size)])  49.4 us
    pallas_call x18, Pallas kernels, call(): pl.pallas_call(kernel, grid=(1,), out_shape=outs, in_specs=[spec(p, x) fo...  29.1 us
    pallas_call x4, Pallas kernels, run_experts(): pl.pallas_call(kernel, grid=(total // step,), in_specs=[pl.BlockSpec(memo...  20.9 us
    pallas_call x3, Pallas kernels, both_copies(): pl.pallas_call(both_copies_kernel, grid=(local // step,), in_specs=[block...  14.3 us
    pallas_call x1, Pallas kernels, run_grads(): pl.pallas_call(grads_kernel, grid=(local,), in_specs=whole(n) + cols(dgu,...  10.7 us
    unnamed x75, local copies, waits for them, and re-layouts  7.92 us
  transfers between devices with their start and end apart: 49, of which 15 were waited for; matrix products, arithmetic and copies ran while one was open for 1% of the time, Pallas kernels for 31%

profile of v11, /device:TPU:0, one launch (start us, length us, event | category | flops | bytes accessed | tf_op | source)
XLA Modules:
  0.0 202.0 jit_solution(13116877250551494446)
XLA Ops:
  0.6 2.2 %pieces.1 = (bf16[64,1152]{1,0:T(8,128)(2,1)}, bf16[64,1152]{1,0:T(8,128)(2,1)}, bf16[64,1152]{1,0:T(8,128)(2,1)}, bf16[64,1152]{1,0:T(8,128)(2,1)}, bf16[128,1024]{1,0:T(8,128)(2,1)}) custom-call(s32[1]{0:T(128)} %bitcast.me_ref, bf16[256,1024]{1,0:T(8,128)(2,1)} %cot_ref.1, s32[8,256]{1,0:T(8,128)} %bitcast.32, bf16[32,1024]{1,0:T(8,128)(2,1)} %bitcast.31), custom_call_target="tpu_custom_call" | custom-call | tf_op jit(solution)/shard_map/pieces/pallas_call | solution.py:122
  2.8 3.0 %collective-permute-start = (bf16[64,1152]{1,0:T(8,128)(2,1)}, bf16[64,1152]{1,0:T(8,128)(2,1)S(1)}, u32[]{:S(2)}, u32[]{:S(2)}) collective-permute-start(bf16[64,1152]{1,0:T(8,128)(2,1)} %get-tuple-element.166.own_ref.refs_0_.cot_ref), channel_id=1, source_target_pairs={{0,4},{4,0},{8,12},{12,8},{1,5},{5,1},{9,13},{13,9},{2,6},{6,2},{1... | collective-permute-start | bytes 442376 | tf_op jit(solution)/shard_map/ppermute | solution.py:41
  5.8 2.6 %collective-permute-start.4 = (bf16[64,1152]{1,0:T(8,128)(2,1)}, bf16[64,1152]{1,0:T(8,128)(2,1)S(1)}, u32[]{:S(2)}, u32[]{:S(2)}) collective-permute-start(bf16[64,1152]{1,0:T(8,128)(2,1)} %get-tuple-element.166.own_ref.refs_0_.cot_ref), channel_id=1, source_target_pairs={{0,8},{4,12},{8,0},{12,4},{1,9},{5,13},{9,1},{13,5},{2,10},{6,14},... | collective-permute-start | bytes 442376 | tf_op jit(solution)/shard_map/ppermute | solution.py:41
  8.4 3.5 %collective-permute-done.refs_0_ = bf16[64,1152]{1,0:T(8,128)(2,1)S(1)} collective-permute-done((bf16[64,1152]{1,0:T(8,128)(2,1)}, bf16[64,1152]{1,0:T(8,128)(2,1)S(1)}, u32[]{:S(2)}, u32[]{:S(2)}) %collective-permute-start) | collective-permute-done | bytes 147488 | tf_op jit(solution)/shard_map/ppermute | solution.py:41
  11.9 4.7 %attend.1 = (bf16[256,1024]{1,0:T(8,128)(2,1)}, bf16[256,256]{1,0:T(8,128)(2,1)}, bf16[256,128]{1,0:T(8,128)(2,1)}, bf16[256,128]{1,0:T(8,128)(2,1)}, bf16[256,2...) custom-call(s32[1]{0:T(128)} %bitcast.me_ref, ...), custom_call_target="tpu_custom_call" | custom-call | flops 53687091200 | tf_op jit(solution)/shard_map/attend/pallas_call | solution.py:122
  16.6 1.7 collective-permute-start.1
  18.3 1.5 collective-permute-start.2
  20.1 1.7 collective-permute-done.1.refs_0_
  21.8 1.7 collective-permute-done.2.refs_1_
  23.5 2.4 %collective-permute-done.3.refs_2_ = bf16[64,1024]{1,0:T(8,128)(2,1)S(1)} collective-permute-done((bf16[64,1024]{1,0:T(8,128)(2,1)}, bf16[64,1024]{1,0:T(8,128)(2,1)S(1)}, u32[]{:S(2)}, u32[]{:S(2)}) %collective-permute-start.3) | collective-permute-done | bytes 131104 | tf_op jit(solution)/shard_map/ppermute | solution.py:41
  26.5 2.0 norm_two.1
  30.1 3.7 %collective-permute-done.6.refs_1_ = bf16[64,1024]{1,0:T(8,128)(2,1)S(1)} collective-permute-done((bf16[64,1024]{1,0:T(8,128)(2,1)}, bf16[64,1024]{1,0:T(8,128)(2,1)S(1)}, u32[]{:S(2)}, u32[]{:S(2)}) %collective-permute-start.6) | collective-permute-done | bytes 131104 | tf_op jit(solution)/shard_map/ppermute | solution.py:41
  34.3 2.6 %collective-permute-start.7 = (bf16[64,1024]{1,0:T(8,128)(2,1)}, bf16[64,1024]{1,0:T(8,128)(2,1)S(1)}, u32[]{:S(2)}, u32[]{:S(2)}) collective-permute-start(bf16[64,1024]{1,0:T(8,128)(2,1)} %get-tuple-element.175.refs_0_.n_ref), channel_id=1, source_target_pairs={{0,8},{4,12},{8,0},{12,4},{1,9},{5,13},{9,1},{13,5},{2,10},{6,14},... | collective-permute-start | bytes 393224 | tf_op jit(solution)/shard_map/ppermute | solution.py:41
  38.4 1.6 copy-done.1
  41.5 2.9 %collective-permute-done.7.refs_2_ = bf16[64,1024]{1,0:T(8,128)(2,1)S(1)} collective-permute-done((bf16[64,1024]{1,0:T(8,128)(2,1)}, bf16[64,1024]{1,0:T(8,128)(2,1)S(1)}, u32[]{:S(2)}, u32[]{:S(2)}) %collective-permute-start.7) | collective-permute-done | bytes 131104 | tf_op jit(solution)/shard_map/ppermute | solution.py:41
  46.0 1.6 collective-permute-start.10
  47.6 4.4 %collective-permute-done.14.refs_7_.far_ref = bf16[3,64,1152]{2,1,0:T(8,128)(2,1)S(1)} collective-permute-done((bf16[3,64,1152]{2,1,0:T(8,128)(2,1)S(1)}, bf16[3,64,1152]{2,1,0:T(8,128)(2,1)S(1)}, u32[]{:S(2)}, u32[]{:S(2)}) %collective-permute-start.14) | collective-permute-done | bytes 442400 | tf_op jit(solution)/shard_map/ppermute | solution.py:41
  51.9 1.9 counts.1
  54.0 4.1 %experts.4 = (bf16[256,1024]{1,0:T(8,128)(2,1)S(1)}, bf16[256,2048]{1,0:T(8,128)(2,1)S(1)}, bf16[256,1024]{1,0:T(8,128)(2,1)S(1)}, f32[4,64,1152]{2,1,0:T(8,128)S(1)}, f32[4,64,1024]{2,1,0:T(8,128)S(1)}) custom-call(s32[1]{0:T(128)} %bitcast.9.base_ref, bf16[4,64,1024]{2,1,0:T(8,128)(2,1)S(1)} %together.3.x_ref.a0, bf16[64,1152]{1,0:T(8,128)(2,1)S(1)} %copy-done.5, ...), custom_call_target="tpu_custom_call" | custom-call | flops 3355443200 | tf_op jit(solution)/shard_map/experts/pallas_call | solution.py:357
  59.4 5.9 %experts.5 = (bf16[256,1024]{1,0:T(8,128)(2,1)S(1)}, bf16[256,2048]{1,0:T(8,128)(2,1)S(1)}, bf16[256,1024]{1,0:T(8,128)(2,1)S(1)}, bf16[4,64,1152]{2,1,0:T(8,128)(2,1)}, bf16[4,64,1024]{2,1,0:T(8,128)(2,1)S(1)}) custom-call(s32[1]{0:T(128)} %bitcast.9.base_ref, bf16[4,64,1024]{2,1,0:T(8,128)(2,1)S(1)} %collective-permute-done.9.x_ref.a1, ...), custom_call_target="tpu_custom_call" | custom-call | flops 3355443200 | tf_op jit(solution)/shard_map/experts/pallas_call | solution.py:357
  66.8 6.2 %experts.6 = (bf16[256,1024]{1,0:T(8,128)(2,1)S(1)}, bf16[256,2048]{1,0:T(8,128)(2,1)S(1)}, bf16[256,1024]{1,0:T(8,128)(2,1)S(1)}, bf16[4,64,1152]{2,1,0:T(8,128)(2,1)}, bf16[4,64,1024]{2,1,0:T(8,128)(2,1)S(1)}) custom-call(s32[1]{0:T(128)} %bitcast.9.base_ref, bf16[4,64,1024]{2,1,0:T(8,128)(2,1)S(1)} %collective-permute-done.10.x_ref.a2, ...), custom_call_target="tpu_custom_call" | custom-call | flops 3355443200 | tf_op jit(solution)/shard_map/experts/pallas_call | solution.py:357
  73.8 4.7 %experts.7 = (bf16[256,1024]{1,0:T(8,128)(2,1)S(1)}, bf16[256,2048]{1,0:T(8,128)(2,1)S(1)}, bf16[256,1024]{1,0:T(8,128)(2,1)S(1)}, f32[64,1152]{1,0:T(8,128)S(1)...) custom-call(s32[1]{0:T(128)} %bitcast.9.base_ref, ...), custom_call_target="tpu_custom_call" | custom-call | flops 3355443200 | tf_op jit(solution)/shard_map/experts/pallas_call | solution.py:357
  78.5 5.6 %collective-permute-start.18 = (bf16[64,1152]{1,0:T(8,128)(2,1)}, bf16[64,1152]{1,0:T(8,128)(2,1)}, u32[]{:S(2)}, u32[]{:S(2)}) collective-permute-start(bf16[64,1152]{1,0:T(8,128)(2,1)} %get-tuple-element.220), channel_id=1, source_target_pairs={{0,4},{4,0},{8,12},{12,8},{1,5},{5,1},{9,13},{13,9},{2,6},{6,2},{1... | collective-permute-start | bytes 442376 | tf_op jit(solution)/shard_map/ppermute | solution.py:41
  84.1 2.4 %collective-permute-start.20 = (bf16[64,1152]{1,0:T(8,128)(2,1)}, bf16[64,1152]{1,0:T(8,128)(2,1)}, u32[]{:S(2)}, u32[]{:S(2)}) collective-permute-start(bf16[64,1152]{1,0:T(8,128)(2,1)} %get-tuple-element.222), channel_id=1, source_target_pairs={{0,12},{4,8},{8,4},{12,0},{1,13},{5,9},{9,5},{13,1},{2,14},{6,10},... | collective-permute-start | bytes 442376 | tf_op jit(solution)/shard_map/ppermute | solution.py:41
  86.5 10.7 %expert_grads.1.mine_ref = bf16[8,3072,128]{2,1,0:T(8,128)(2,1)} custom-call(bf16[256,1024]{1,0:T(8,128)(2,1)S(1)} %bitcast.20, bf16[256,1024]{1,0:T(8,128)(2,1)S(1)} %bitcast.21, bf16[256,1024]{1,0:T(8,128)(2,1)S(1)} %bitcast.22, bf16[256,1024]{1,0:T(8,128)(2,1)S(1)} %bitcast.23, bf16[256,2048]{1,0:T(8,128)(2,1)S(1)} %get-tuple-element.187.refs_4_, ...), custom_call_target="tpu_custom_call" | custom-call | flops 644245094400 | tf_op jit(solution)/shard_map/expert_grads/pallas_call | solution.py:431
  101.4 2.1 %collective-permute-start.26 = (bf16[64,1152]{1,0:T(8,128)(2,1)S(1)}, bf16[64,1152]{1,0:T(8,128)(2,1)S(1)}, u32[]{:S(2)}, u32[]{:S(2)}) collective-permute-start(bf16[64,1152]{1,0:T(8,128)(2,1)S(1)} %get-tuple-element.243), channel_id=1, source_target_pairs={{0,12},{4,8},{8,4},{12,0},{1,13},{5,9},{9,5},{13,1},{2,14},{6,10},... | collective-permute-start | bytes 442376 | tf_op jit(solution)/shard_map/ppermute | solution.py:41
  103.5 2.0 collective-permute-done.23.refs_2_
  106.6 2.0 collective-permute-start.24
  108.5 5.2 %collective-permute-done.25.refs_3_ = bf16[64,1152]{1,0:T(8,128)(2,1)S(1)} collective-permute-done((bf16[64,1152]{1,0:T(8,128)(2,1)S(1)}, bf16[64,1152]{1,0:T(8,128)(2,1)S(1)}, u32[]{:S(2)}, u32[]{:S(2)}) %collective-permute-start.25) | collective-permute-done | bytes 147488 | tf_op jit(solution)/shard_map/ppermute | solution.py:41
  115.9 1.7 collective-permute-start.28
  117.9 1.5 collective-permute-start.30
  120.0 2.6 %collective-permute-done.28.w1 = bf16[64,1152]{1,0:T(8,128)(2,1)S(1)} collective-permute-done((bf16[64,1152]{1,0:T(8,128)(2,1)S(1)}, bf16[64,1152]{1,0:T(8,128)(2,1)S(1)}, u32[]{:S(2)}, u32[]{:S(2)}) %collective-permute-start.28) | collective-permute-done | bytes 147488 | tf_op jit(solution)/shard_map/ppermute | solution.py:41
  122.6 4.2 %collective-permute-done.29.w2 = bf16[64,1152]{1,0:T(8,128)(2,1)S(1)} collective-permute-done((bf16[64,1152]{1,0:T(8,128)(2,1)S(1)}, bf16[64,1152]{1,0:T(8,128)(2,1)S(1)}, u32[]{:S(2)}, u32[]{:S(2)}) %collective-permute-start.29) | collective-permute-done | bytes 147488 | tf_op jit(solution)/shard_map/ppermute | solution.py:41
  127.5 5.5 %attend_back.1 = (bf16[256,1152]{1,0:T(8,128)(2,1)}, bf16[256,512]{1,0:T(8,128)(2,1)}, f32[8,1024]{1,0:T(8,128)}, f32[64,1024]{1,0:T(8,128)}, bf16[64,1024]{1,0:...) custom-call(s32[1]{0:T(128)} %bitcast.me_ref, bf16[64,1152]{1,0:T(8,128)(2,1)} %copy-done.23, ...), custom_call_target="tpu_custom_call" | custom-call | flops 53687091200 | tf_op jit(solution)/shard_map/attend_back/pallas_call | solution.py:122
  133.0 4.0 %dense.1 = (f32[512,896]{1,0:T(8,128)}, bf16[512,896]{1,0:T(8,128)(2,1)}) custom-call(s32[2]{0:T(128)} %pad_add_fusion.me_ref, bf16[4,64,1024]{2,1,0:T(8,128)(2,1)} %copy-done.2, bf16[4,64,1024]{2,1,0:T(8,128)(2,1)} %copy-done.9, bf16[4,64,1024]{2,1,0:T(8,128)(2,1)} %copy-done.10, bf16[4,64,1024]{2,1,0:T(8,128)(2,1)} %copy-done.11, ...), custom_call_target="tpu_custom_call" | custom-call | flops 100 | tf_op jit(solution)/shard_map/dense/pallas_call | solution.py:122
  142.3 2.2 %collective-permute-start.33 = (bf16[128,896]{1,0:T(8,128)(2,1)S(1)}, bf16[128,896]{1,0:T(8,128)(2,1)S(1)}, u32[]{:S(2)}, u32[]{:S(2)}) collective-permute-start(bf16[128,896]{1,0:T(8,128)(2,1)S(1)} %get-tuple-element.274), channel_id=1, source_target_pairs={{0,4},{4,0},{8,12},{12,8},{1,5},{5,1},{9,13},{13,9},{2,6},{6,2},{1... | collective-permute-start | bytes 688136 | tf_op jit(solution)/shard_map/ppermute | solution.py:41
  145.2 1.6 collective-permute-start.35
  148.0 6.4 %collective-permute-done.34.refs_1_ = bf16[64,1024]{1,0:T(8,128)(2,1)S(1)} collective-permute-done((bf16[64,1024]{1,0:T(8,128)(2,1)S(1)}, bf16[64,1024]{1,0:T(8,128)(2,1)S(1)}, u32[]{:S(2)}, u32[]{:S(2)}) %collective-permute-start.34) | collective-permute-done | bytes 131104 | tf_op jit(solution)/shard_map/ppermute | solution.py:41
  154.4 4.0 %collective-permute-start.40 = (bf16[128,896]{1,0:T(8,128)(2,1)S(1)}, bf16[128,896]{1,0:T(8,128)(2,1)S(1)}, u32[]{:S(2)}, u32[]{:S(2)}) collective-permute-start(bf16[128,896]{1,0:T(8,128)(2,1)S(1)} %get-tuple-element.286), channel_id=1, source_target_pairs={{0,8},{4,12},{8,0},{12,4},{1,9},{5,13},{9,1},{13,5},{2,10},{6,14},... | collective-permute-start | bytes 688136 | tf_op jit(solution)/shard_map/ppermute | solution.py:41
  158.9 4.7 %both_copies.4 = f32[8,1024,128]{2,1,0:T(8,128)} custom-call(bf16[8,3072,128]{2,1,0:T(8,128)(2,1)} %expert_grads.1.mine_ref, bf16[8,3072,128]{2,1,0:T(8,128)(2,1)} %collective-permute-done.27.other_ref), custom_call_target="tpu_custom_call" | custom-call | bytes 25165824 | tf_op jit(solution)/shard_map/both_copies/pallas_call | solution.py:460
  164.3 2.1 %input_grad.1.refs_0_ = bf16[64,1024]{1,0:T(8,128)(2,1)} custom-call(bf16[64,1024]{1,0:T(8,128)(2,1)} %get-tuple-element.168.x_ref, f32[1,1024]{1,0:T(1,128)} %bitcast.34, f32[64,1024]{1,0:T(8,128)} %copy-done.14, f32[64,1024]{1,0:T(8,128)} %get-tuple-element.279.refs_0_, bf16[64,1024]{1,0:T(8,128)(2,1)} %copy-done.25, bf16[64,1024]{1,0:T(8,128)(2,1)} %copy-done.26, ...), custom_call_target="tpu_custom_call" | custom-call | tf_op jit(solution)/shard_map/input_grad/pallas_call | solution.py:122
  169.3 4.3 %collective-permute-done.40.refs_1_ = bf16[128,896]{1,0:T(8,128)(2,1)S(1)} collective-permute-done((bf16[128,896]{1,0:T(8,128)(2,1)S(1)}, bf16[128,896]{1,0:T(8,128)(2,1)S(1)}, u32[]{:S(2)}, u32[]{:S(2)}) %collective-permute-start.40) | collective-permute-done | bytes 229408 | tf_op jit(solution)/shard_map/ppermute | solution.py:41
  173.5 1.8 collective-permute-start.39
  175.4 4.6 %collective-permute-start.44 = (bf16[64,1024]{1,0:T(8,128)(2,1)S(1)}, bf16[64,1024]{1,0:T(8,128)(2,1)S(1)}, u32[]{:S(2)}, u32[]{:S(2)}) collective-permute-start(bf16[64,1024]{1,0:T(8,128)(2,1)S(1)} %get-tuple-element.299), channel_id=1, source_target_pairs={{0,8},{4,12},{8,0},{12,4},{1,9},{5,13},{9,1},{13,5},{2,10},{6,14},... | collective-permute-start | bytes 393224 | tf_op jit(solution)/shard_map/ppermute | solution.py:41
  181.0 4.7 %both_copies.5 = f32[8,1024,128]{2,1,0:T(8,128)} custom-call(bf16[8,3072,128]{2,1,0:T(8,128)(2,1)} %expert_grads.1.mine_ref, bf16[8,3072,128]{2,1,0:T(8,128)(2,1)} %collective-permute-done.27.other_ref), custom_call_target="tpu_custom_call" | custom-call | bytes 25165824 | tf_op jit(solution)/shard_map/both_copies/pallas_call | solution.py:460
  186.7 3.1 %collective-permute-done.44.refs_2_ = bf16[64,1024]{1,0:T(8,128)(2,1)S(1)} collective-permute-done((bf16[64,1024]{1,0:T(8,128)(2,1)S(1)}, bf16[64,1024]{1,0:T(8,128)(2,1)S(1)}, u32[]{:S(2)}, u32[]{:S(2)}) %collective-permute-start.44) | collective-permute-done | bytes 131104 | tf_op jit(solution)/shard_map/ppermute | solution.py:41
  191.1 2.3 %collective-permute-start.48 = (bf16[80,1024]{1,0:T(8,128)(2,1)S(1)}, bf16[80,1024]{1,0:T(8,128)(2,1)S(1)}, u32[]{:S(2)}, u32[]{:S(2)}) collective-permute-start(bf16[80,1024]{1,0:T(8,128)(2,1)S(1)} %out_piece.1.refs_0_), channel_id=1, source_target_pairs={{0,3},{1,2},{2,1},{3,0},{4,7},{5,6},{6,5},{7,4},{8,11},{9,10},{10,... | collective-permute-start | bytes 491528 | tf_op jit(solution)/shard_map/ppermute | solution.py:41
  193.5 4.8 %both_copies.3 = f32[8,128,1024]{2,1,0:T(8,128)} custom-call(bf16[8,3072,128]{2,1,0:T(8,128)(2,1)} %expert_grads.1.mine_ref, bf16[8,3072,128]{2,1,0:T(8,128)(2,1)} %collective-permute-done.27.other_ref), custom_call_target="tpu_custom_call" | custom-call | bytes 25165824 | tf_op jit(solution)/shard_map/both_copies/pallas_call | solution.py:460
  (156 shorter events, 38.3 us)
Async XLA Ops:
  2.8 9.1 %collective-permute-start = (bf16[64,1152]{1,0:T(8,128)(2,1)}, bf16[64,1152]{1,0:T(8,128)(2,1)S(1)}, u32[]{:S(2)}, u32[]{:S(2)}) collective-permute-start(bf16[64,1152]{1,0:T(8,128)(2,1)} %get-tuple-element.166.own_ref.refs_0_.cot_ref), channel_id=1, source_target_pairs={{0,4},{4,0},{8,12},{12,8},{1,5},{5,1},{9,13},{13,9},{2,6},{6,2},{1... | collective-permute-start | bytes 442376 | tf_op jit(solution)/shard_map/ppermute | solution.py:41
  5.8 22.7 %collective-permute-start.4 = (bf16[64,1152]{1,0:T(8,128)(2,1)}, bf16[64,1152]{1,0:T(8,128)(2,1)S(1)}, u32[]{:S(2)}, u32[]{:S(2)}) collective-permute-start(bf16[64,1152]{1,0:T(8,128)(2,1)} %get-tuple-element.166.own_ref.refs_0_.cot_ref), channel_id=1, source_target_pairs={{0,8},{4,12},{8,0},{12,4},{1,9},{5,13},{9,1},{13,5},{2,10},{6,14},... | collective-permute-start | bytes 442376 | tf_op jit(solution)/shard_map/ppermute | solution.py:41
  8.4 20.1 %collective-permute-start.5 = (bf16[64,1152]{1,0:T(8,128)(2,1)}, bf16[64,1152]{1,0:T(8,128)(2,1)S(1)}, u32[]{:S(2)}, u32[]{:S(2)}) collective-permute-start(bf16[64,1152]{1,0:T(8,128)(2,1)} %get-tuple-element.166.own_ref.refs_0_.cot_ref), channel_id=1, source_target_pairs={{0,12},{4,8},{8,4},{12,0},{1,13},{5,9},{9,5},{13,1},{2,14},{6,10},... | collective-permute-start | bytes 442376 | tf_op jit(solution)/shard_map/ppermute | solution.py:41
  16.6 5.2 %collective-permute-start.1 = (bf16[64,1024]{1,0:T(8,128)(2,1)}, bf16[64,1024]{1,0:T(8,128)(2,1)S(1)}, u32[]{:S(2)}, u32[]{:S(2)}) collective-permute-start(bf16[64,1024]{1,0:T(8,128)(2,1)} %get-tuple-element.170), channel_id=1, source_target_pairs={{0,1},{1,0},{2,3},{3,2},{4,5},{5,4},{6,7},{7,6},{8,9},{9,8},{10,11... | collective-permute-start | bytes 393224 | tf_op jit(solution)/shard_map/ppermute | solution.py:41
  18.3 5.2 %collective-permute-start.2 = (bf16[64,1024]{1,0:T(8,128)(2,1)}, bf16[64,1024]{1,0:T(8,128)(2,1)S(1)}, u32[]{:S(2)}, u32[]{:S(2)}) collective-permute-start(bf16[64,1024]{1,0:T(8,128)(2,1)} %get-tuple-element.171), channel_id=1, source_target_pairs={{0,2},{1,3},{2,0},{3,1},{4,6},{5,7},{6,4},{7,5},{8,10},{9,11},{10,... | collective-permute-start | bytes 393224 | tf_op jit(solution)/shard_map/ppermute | solution.py:41
  19.8 6.1 %collective-permute-start.3 = (bf16[64,1024]{1,0:T(8,128)(2,1)}, bf16[64,1024]{1,0:T(8,128)(2,1)S(1)}, u32[]{:S(2)}, u32[]{:S(2)}) collective-permute-start(bf16[64,1024]{1,0:T(8,128)(2,1)} %get-tuple-element.172), channel_id=1, source_target_pairs={{0,3},{1,2},{2,1},{3,0},{4,7},{5,6},{6,5},{7,4},{8,11},{9,10},{10,... | collective-permute-start | bytes 393224 | tf_op jit(solution)/shard_map/ppermute | solution.py:41
  28.6 5.2 %collective-permute-start.6 = (bf16[64,1024]{1,0:T(8,128)(2,1)}, bf16[64,1024]{1,0:T(8,128)(2,1)S(1)}, u32[]{:S(2)}, u32[]{:S(2)}) collective-permute-start(bf16[64,1024]{1,0:T(8,128)(2,1)} %get-tuple-element.175.refs_0_.n_ref), channel_id=1, source_target_pairs={{0,4},{4,0},{8,12},{12,8},{1,5},{5,1},{9,13},{13,9},{2,6},{6,2},{1... | collective-permute-start | bytes 393224 | tf_op jit(solution)/shard_map/ppermute | solution.py:41
  29.0 18.5 %collective-permute-start.11 = (bf16[3,64,1152]{2,1,0:T(8,128)(2,1)S(1)}, bf16[3,64,1152]{2,1,0:T(8,128)(2,1)}, u32[]{:S(2)}, u32[]{:S(2)}) collective-permute-start(bf16[3,64,1152]{2,1,0:T(8,128)(2,1)S(1)} %together.2.far_ref.refs_4_), channel_id=1, source_target_pairs={{0,1},{1,0},{2,3},{3,2},{4,5},{5,4},{6,7},{7,6},{8,9},{9,8},{10,11... | collective-permute-start | bytes 1327112 | tf_op jit(solution)/shard_map/ppermute | solution.py:41
  29.6 17.9 %collective-permute-start.12 = (bf16[3,64,1152]{2,1,0:T(8,128)(2,1)S(1)}, bf16[3,64,1152]{2,1,0:T(8,128)(2,1)}, u32[]{:S(2)}, u32[]{:S(2)}) collective-permute-start(bf16[3,64,1152]{2,1,0:T(8,128)(2,1)S(1)} %together.2.far_ref.refs_4_), channel_id=1, source_target_pairs={{0,2},{1,3},{2,0},{3,1},{4,6},{5,7},{6,4},{7,5},{8,10},{9,11},{10,... | collective-permute-start | bytes 1327112 | tf_op jit(solution)/shard_map/ppermute | solution.py:41
  33.8 18.1 %collective-permute-start.14 = (bf16[3,64,1152]{2,1,0:T(8,128)(2,1)S(1)}, bf16[3,64,1152]{2,1,0:T(8,128)(2,1)S(1)}, u32[]{:S(2)}, u32[]{:S(2)}) collective-permute-start(bf16[3,64,1152]{2,1,0:T(8,128)(2,1)S(1)} %together.2.far_ref.refs_4_), channel_id=1, source_target_pairs={{0,3},{1,2},{2,1},{3,0},{4,7},{5,6},{6,5},{7,4},{8,11},{9,10},{10,... | collective-permute-start | bytes 1327112 | tf_op jit(solution)/shard_map/ppermute | solution.py:41
  34.3 10.1 %collective-permute-start.7 = (bf16[64,1024]{1,0:T(8,128)(2,1)}, bf16[64,1024]{1,0:T(8,128)(2,1)S(1)}, u32[]{:S(2)}, u32[]{:S(2)}) collective-permute-start(bf16[64,1024]{1,0:T(8,128)(2,1)} %get-tuple-element.175.refs_0_.n_ref), channel_id=1, source_target_pairs={{0,8},{4,12},{8,0},{12,4},{1,9},{5,13},{9,1},{13,5},{2,10},{6,14},... | collective-permute-start | bytes 393224 | tf_op jit(solution)/shard_map/ppermute | solution.py:41
  36.9 7.5 %collective-permute-start.8 = (bf16[64,1024]{1,0:T(8,128)(2,1)}, bf16[64,1024]{1,0:T(8,128)(2,1)S(1)}, u32[]{:S(2)}, u32[]{:S(2)}) collective-permute-start(bf16[64,1024]{1,0:T(8,128)(2,1)} %get-tuple-element.175.refs_0_.n_ref), channel_id=1, source_target_pairs={{0,12},{4,8},{8,4},{12,0},{1,13},{5,9},{9,5},{13,1},{2,14},{6,10},... | collective-permute-start | bytes 393224 | tf_op jit(solution)/shard_map/ppermute | solution.py:41
  44.5 15.0 %collective-permute-start.9 = (bf16[4,64,1024]{2,1,0:T(8,128)(2,1)S(1)}, bf16[4,64,1024]{2,1,0:T(8,128)(2,1)S(1)}, u32[]{:S(2)}, u32[]{:S(2)}) collective-permute-start(bf16[4,64,1024]{2,1,0:T(8,128)(2,1)S(1)} %together.3.x_ref.a0), channel_id=1, source_target_pairs={{0,1},{1,0},{2,3},{3,2},{4,5},{5,4},{6,7},{7,6},{8,9},{9,8},{10,11... | collective-permute-start | bytes 1572872 | tf_op jit(solution)/shard_map/ppermute | solution.py:41
  46.0 20.8 %collective-permute-start.10 = (bf16[4,64,1024]{2,1,0:T(8,128)(2,1)S(1)}, bf16[4,64,1024]{2,1,0:T(8,128)(2,1)S(1)}, u32[]{:S(2)}, u32[]{:S(2)}) collective-permute-start(bf16[4,64,1024]{2,1,0:T(8,128)(2,1)S(1)} %together.3.x_ref.a0), channel_id=1, source_target_pairs={{0,2},{1,3},{2,0},{3,1},{4,6},{5,7},{6,4},{7,5},{8,10},{9,11},{10,... | collective-permute-start | bytes 1572872 | tf_op jit(solution)/shard_map/ppermute | solution.py:41
  53.9 5.6 %collective-permute-start.15 = (f32[1,128]{1,0:T(1,128)S(1)}, f32[1,128]{1,0:T(1,128)S(1)}, u32[]{:S(2)}, u32[]{:S(2)}) collective-permute-start(f32[1,128]{1,0:T(1,128)S(1)} %counts.1), channel_id=1, source_target_pairs={{0,16},{16,0},{1,17},{17,1},{2,18},{18,2},{3,19},{19,3},{4,20},{20... | collective-permute-start | bytes 1544 | tf_op jit(solution)/shard_map/ppermute | solution.py:41
  58.1 15.7 %collective-permute-start.13 = (bf16[4,64,1024]{2,1,0:T(8,128)(2,1)S(1)}, bf16[4,64,1024]{2,1,0:T(8,128)(2,1)S(1)}, u32[]{:S(2)}, u32[]{:S(2)}) collective-permute-start(bf16[4,64,1024]{2,1,0:T(8,128)(2,1)S(1)} %together.3.x_ref.a0), channel_id=1, source_target_pairs={{0,3},{1,2},{2,1},{3,0},{4,7},{5,6},{6,5},{7,4},{8,11},{9,10},{10,... | collective-permute-start | bytes 1572872 | tf_op jit(solution)/shard_map/ppermute | solution.py:41
  65.4 31.8 %collective-permute-start.16 = (bf16[4,64,1152]{2,1,0:T(8,128)(2,1)}, bf16[4,64,1152]{2,1,0:T(8,128)(2,1)}, u32[]{:S(2)}, u32[]{:S(2)}) collective-permute-start(bf16[4,64,1152]{2,1,0:T(8,128)(2,1)} %get-tuple-element.194), channel_id=1, source_target_pairs={{0,1},{1,0},{2,3},{3,2},{4,5},{5,4},{6,7},{7,6},{8,9},{9,8},{10,11... | collective-permute-start | bytes 1769480 | tf_op jit(solution)/shard_map/ppermute | solution.py:41
  73.0 24.2 %collective-permute-start.17 = (bf16[4,64,1152]{2,1,0:T(8,128)(2,1)}, bf16[4,64,1152]{2,1,0:T(8,128)(2,1)}, u32[]{:S(2)}, u32[]{:S(2)}) collective-permute-start(bf16[4,64,1152]{2,1,0:T(8,128)(2,1)} %get-tuple-element.203), channel_id=1, source_target_pairs={{0,2},{1,3},{2,0},{3,1},{4,6},{5,7},{6,4},{7,5},{8,10},{9,11},{10,... | collective-permute-start | bytes 1769480 | tf_op jit(solution)/shard_map/ppermute | solution.py:41
  78.5 18.7 %collective-permute-start.18 = (bf16[64,1152]{1,0:T(8,128)(2,1)}, bf16[64,1152]{1,0:T(8,128)(2,1)}, u32[]{:S(2)}, u32[]{:S(2)}) collective-permute-start(bf16[64,1152]{1,0:T(8,128)(2,1)} %get-tuple-element.220), channel_id=1, source_target_pairs={{0,4},{4,0},{8,12},{12,8},{1,5},{5,1},{9,13},{13,9},{2,6},{6,2},{1... | collective-permute-start | bytes 442376 | tf_op jit(solution)/shard_map/ppermute | solution.py:41
  84.1 13.1 %collective-permute-start.19 = (bf16[64,1152]{1,0:T(8,128)(2,1)}, bf16[64,1152]{1,0:T(8,128)(2,1)}, u32[]{:S(2)}, u32[]{:S(2)}) collective-permute-start(bf16[64,1152]{1,0:T(8,128)(2,1)} %get-tuple-element.221), channel_id=1, source_target_pairs={{0,8},{4,12},{8,0},{12,4},{1,9},{5,13},{9,1},{13,5},{2,10},{6,14},... | collective-permute-start | bytes 442376 | tf_op jit(solution)/shard_map/ppermute | solution.py:41
  84.1 13.1 %collective-permute-start.20 = (bf16[64,1152]{1,0:T(8,128)(2,1)}, bf16[64,1152]{1,0:T(8,128)(2,1)}, u32[]{:S(2)}, u32[]{:S(2)}) collective-permute-start(bf16[64,1152]{1,0:T(8,128)(2,1)} %get-tuple-element.222), channel_id=1, source_target_pairs={{0,12},{4,8},{8,4},{12,0},{1,13},{5,9},{9,5},{13,1},{2,14},{6,10},... | collective-permute-start | bytes 442376 | tf_op jit(solution)/shard_map/ppermute | solution.py:41
  98.6 15.1 %collective-permute-start.21 = (bf16[4,64,1024]{2,1,0:T(8,128)(2,1)S(1)}, bf16[4,64,1024]{2,1,0:T(8,128)(2,1)S(1)}, u32[]{:S(2)}, u32[]{:S(2)}) collective-permute-start(bf16[4,64,1024]{2,1,0:T(8,128)(2,1)S(1)} %get-tuple-element.232), channel_id=1, source_target_pairs={{0,1},{1,0},{2,3},{3,2},{4,5},{5,4},{6,7},{7,6},{8,9},{9,8},{10,11... | collective-permute-start | bytes 1572872 | tf_op jit(solution)/shard_map/ppermute | solution.py:41
  99.1 14.7 %collective-permute-start.22 = (bf16[4,64,1024]{2,1,0:T(8,128)(2,1)S(1)}, bf16[4,64,1024]{2,1,0:T(8,128)(2,1)S(1)}, u32[]{:S(2)}, u32[]{:S(2)}) collective-permute-start(bf16[4,64,1024]{2,1,0:T(8,128)(2,1)S(1)} %get-tuple-element.233), channel_id=1, source_target_pairs={{0,2},{1,3},{2,0},{3,1},{4,6},{5,7},{6,4},{7,5},{8,10},{9,11},{10,... | collective-permute-start | bytes 1572872 | tf_op jit(solution)/shard_map/ppermute | solution.py:41
  99.1 6.4 %collective-permute-start.23 = (bf16[64,1152]{1,0:T(8,128)(2,1)S(1)}, bf16[64,1152]{1,0:T(8,128)(2,1)S(1)}, u32[]{:S(2)}, u32[]{:S(2)}) collective-permute-start(bf16[64,1152]{1,0:T(8,128)(2,1)S(1)} %get-tuple-element.235), channel_id=1, source_target_pairs={{0,4},{4,0},{8,12},{12,8},{1,5},{5,1},{9,13},{13,9},{2,6},{6,2},{1... | collective-permute-start | bytes 442376 | tf_op jit(solution)/shard_map/ppermute | solution.py:41
  100.2 13.6 %collective-permute-start.25 = (bf16[64,1152]{1,0:T(8,128)(2,1)S(1)}, bf16[64,1152]{1,0:T(8,128)(2,1)S(1)}, u32[]{:S(2)}, u32[]{:S(2)}) collective-permute-start(bf16[64,1152]{1,0:T(8,128)(2,1)S(1)} %get-tuple-element.242), channel_id=1, source_target_pairs={{0,8},{4,12},{8,0},{12,4},{1,9},{5,13},{9,1},{13,5},{2,10},{6,14},... | collective-permute-start | bytes 442376 | tf_op jit(solution)/shard_map/ppermute | solution.py:41
  101.4 12.4 %collective-permute-start.26 = (bf16[64,1152]{1,0:T(8,128)(2,1)S(1)}, bf16[64,1152]{1,0:T(8,128)(2,1)S(1)}, u32[]{:S(2)}, u32[]{:S(2)}) collective-permute-start(bf16[64,1152]{1,0:T(8,128)(2,1)S(1)} %get-tuple-element.243), channel_id=1, source_target_pairs={{0,12},{4,8},{8,4},{12,0},{1,13},{5,9},{9,5},{13,1},{2,14},{6,10},... | collective-permute-start | bytes 442376 | tf_op jit(solution)/shard_map/ppermute | solution.py:41
  106.6 7.2 %collective-permute-start.24 = (bf16[64,1152]{1,0:T(8,128)(2,1)S(1)}, bf16[64,1152]{1,0:T(8,128)(2,1)S(1)}, u32[]{:S(2)}, u32[]{:S(2)}) collective-permute-start(bf16[64,1152]{1,0:T(8,128)(2,1)S(1)} %through.1), channel_id=1, source_target_pairs={{0,3},{1,2},{2,1},{3,0},{4,7},{5,6},{6,5},{7,4},{8,11},{9,10},{10,... | collective-permute-start | bytes 442376 | tf_op jit(solution)/shard_map/ppermute | solution.py:41
  115.9 10.8 %collective-permute-start.27 = (bf16[8,3072,128]{2,1,0:T(8,128)(2,1)}, bf16[8,3072,128]{2,1,0:T(8,128)(2,1)}, u32[]{:S(2)}, u32[]{:S(2)}) collective-permute-start(bf16[8,3072,128]{2,1,0:T(8,128)(2,1)} %expert_grads.1.mine_ref), channel_id=1, source_target_pairs={{0,16},{16,0},{1,17},{17,1},{2,18},{18,2},{3,19},{19,3},{4,20},{20... | collective-permute-start | bytes 18874376 | tf_op jit(solution)/shard_map/ppermute | solution.py:41
  115.9 6.6 %collective-permute-start.28 = (bf16[64,1152]{1,0:T(8,128)(2,1)S(1)}, bf16[64,1152]{1,0:T(8,128)(2,1)S(1)}, u32[]{:S(2)}, u32[]{:S(2)}) collective-permute-start(bf16[64,1152]{1,0:T(8,128)(2,1)S(1)} %get-tuple-element.258.w0), channel_id=1, source_target_pairs={{0,1},{1,0},{2,3},{3,2},{4,5},{5,4},{6,7},{7,6},{8,9},{9,8},{10,11... | collective-permute-start | bytes 442376 | tf_op jit(solution)/shard_map/ppermute | solution.py:41
  117.6 9.1 %collective-permute-start.29 = (bf16[64,1152]{1,0:T(8,128)(2,1)S(1)}, bf16[64,1152]{1,0:T(8,128)(2,1)S(1)}, u32[]{:S(2)}, u32[]{:S(2)}) collective-permute-start(bf16[64,1152]{1,0:T(8,128)(2,1)S(1)} %get-tuple-element.258.w0), channel_id=1, source_target_pairs={{0,2},{1,3},{2,0},{3,1},{4,6},{5,7},{6,4},{7,5},{8,10},{9,11},{10,... | collective-permute-start | bytes 442376 | tf_op jit(solution)/shard_map/ppermute | solution.py:41
  117.9 8.9 %collective-permute-start.30 = (bf16[64,1152]{1,0:T(8,128)(2,1)S(1)}, bf16[64,1152]{1,0:T(8,128)(2,1)S(1)}, u32[]{:S(2)}, u32[]{:S(2)}) collective-permute-start(bf16[64,1152]{1,0:T(8,128)(2,1)S(1)} %get-tuple-element.258.w0), channel_id=1, source_target_pairs={{0,3},{1,2},{2,1},{3,0},{4,7},{5,6},{6,5},{7,4},{8,11},{9,10},{10,... | collective-permute-start | bytes 442376 | tf_op jit(solution)/shard_map/ppermute | solution.py:41
  137.0 2.7 %collective-permute-start.31 = (bf16[512,896]{1,0:T(8,128)(2,1)}, bf16[512,896]{1,0:T(8,128)(2,1)S(1)}, u32[]{:S(2)}, u32[]{:S(2)}) collective-permute-start(bf16[512,896]{1,0:T(8,128)(2,1)} %get-tuple-element.272), channel_id=1, source_target_pairs={{0,16},{16,0},{1,17},{17,1},{2,18},{18,2},{3,19},{19,3},{4,20},{20... | collective-permute-start | bytes 2752520 | tf_op jit(solution)/shard_map/ppermute | solution.py:41
  137.0 30.8 %collective-permute-start.42 = (bf16[4,64,1024]{2,1,0:T(8,128)(2,1)S(1)}, bf16[4,64,1024]{2,1,0:T(8,128)(2,1)S(1)}, u32[]{:S(2)}, u32[]{:S(2)}) collective-permute-start(bf16[4,64,1024]{2,1,0:T(8,128)(2,1)S(1)} %copy-done.22), channel_id=1, source_target_pairs={{0,3},{1,2},{2,1},{3,0},{4,7},{5,6},{6,5},{7,4},{8,11},{9,10},{10,... | collective-permute-start | bytes 1572872 | tf_op jit(solution)/shard_map/ppermute | solution.py:41
  142.3 21.4 %collective-permute-start.33 = (bf16[128,896]{1,0:T(8,128)(2,1)S(1)}, bf16[128,896]{1,0:T(8,128)(2,1)S(1)}, u32[]{:S(2)}, u32[]{:S(2)}) collective-permute-start(bf16[128,896]{1,0:T(8,128)(2,1)S(1)} %get-tuple-element.274), channel_id=1, source_target_pairs={{0,4},{4,0},{8,12},{12,8},{1,5},{5,1},{9,13},{13,9},{2,6},{6,2},{1... | collective-permute-start | bytes 688136 | tf_op jit(solution)/shard_map/ppermute | solution.py:41
  144.5 9.9 %collective-permute-start.34 = (bf16[64,1024]{1,0:T(8,128)(2,1)S(1)}, bf16[64,1024]{1,0:T(8,128)(2,1)S(1)}, u32[]{:S(2)}, u32[]{:S(2)}) collective-permute-start(bf16[64,1024]{1,0:T(8,128)(2,1)S(1)} %copy-done.36), channel_id=1, source_target_pairs={{0,1},{1,0},{2,3},{3,2},{4,5},{5,4},{6,7},{7,6},{8,9},{9,8},{10,11... | collective-permute-start | bytes 393224 | tf_op jit(solution)/shard_map/ppermute | solution.py:41
  145.2 13.2 %collective-permute-start.35 = (bf16[64,1024]{1,0:T(8,128)(2,1)S(1)}, bf16[64,1024]{1,0:T(8,128)(2,1)S(1)}, u32[]{:S(2)}, u32[]{:S(2)}) collective-permute-start(bf16[64,1024]{1,0:T(8,128)(2,1)S(1)} %copy-done.35), channel_id=1, source_target_pairs={{0,2},{1,3},{2,0},{3,1},{4,6},{5,7},{6,4},{7,5},{8,10},{9,11},{10,... | collective-permute-start | bytes 393224 | tf_op jit(solution)/shard_map/ppermute | solution.py:41
  146.7 16.9 %collective-permute-start.36 = (bf16[64,1024]{1,0:T(8,128)(2,1)S(1)}, bf16[64,1024]{1,0:T(8,128)(2,1)S(1)}, u32[]{:S(2)}, u32[]{:S(2)}) collective-permute-start(bf16[64,1024]{1,0:T(8,128)(2,1)S(1)} %copy-done.34), channel_id=1, source_target_pairs={{0,3},{1,2},{2,1},{3,0},{4,7},{5,6},{6,5},{7,4},{8,11},{9,10},{10,... | collective-permute-start | bytes 393224 | tf_op jit(solution)/shard_map/ppermute | solution.py:41
  154.4 19.1 %collective-permute-start.40 = (bf16[128,896]{1,0:T(8,128)(2,1)S(1)}, bf16[128,896]{1,0:T(8,128)(2,1)S(1)}, u32[]{:S(2)}, u32[]{:S(2)}) collective-permute-start(bf16[128,896]{1,0:T(8,128)(2,1)S(1)} %get-tuple-element.286), channel_id=1, source_target_pairs={{0,8},{4,12},{8,0},{12,4},{1,9},{5,13},{9,1},{13,5},{2,10},{6,14},... | collective-permute-start | bytes 688136 | tf_op jit(solution)/shard_map/ppermute | solution.py:41
  158.4 17.0 %collective-permute-start.41 = (bf16[128,896]{1,0:T(8,128)(2,1)S(1)}, bf16[128,896]{1,0:T(8,128)(2,1)S(1)}, u32[]{:S(2)}, u32[]{:S(2)}) collective-permute-start(bf16[128,896]{1,0:T(8,128)(2,1)S(1)} %get-tuple-element.287), channel_id=1, source_target_pairs={{0,12},{4,8},{8,4},{12,0},{1,13},{5,9},{9,5},{13,1},{2,14},{6,10},... | collective-permute-start | bytes 688136 | tf_op jit(solution)/shard_map/ppermute | solution.py:41
  166.4 13.6 %collective-permute-start.37 = (bf16[64,1024]{1,0:T(8,128)(2,1)}, bf16[64,1024]{1,0:T(8,128)(2,1)S(1)}, u32[]{:S(2)}, u32[]{:S(2)}) collective-permute-start(bf16[64,1024]{1,0:T(8,128)(2,1)} %input_grad.1.refs_0_), channel_id=1, source_target_pairs={{0,1},{1,0},{2,3},{3,2},{4,5},{5,4},{6,7},{7,6},{8,9},{9,8},{10,11... | collective-permute-start | bytes 393224 | tf_op jit(solution)/shard_map/ppermute | solution.py:41
  168.0 18.6 %collective-permute-start.43 = (bf16[64,1024]{1,0:T(8,128)(2,1)S(1)}, bf16[64,1024]{1,0:T(8,128)(2,1)S(1)}, u32[]{:S(2)}, u32[]{:S(2)}) collective-permute-start(bf16[64,1024]{1,0:T(8,128)(2,1)S(1)} %get-tuple-element.298), channel_id=1, source_target_pairs={{0,4},{4,0},{8,12},{12,8},{1,5},{5,1},{9,13},{13,9},{2,6},{6,2},{1... | collective-permute-start | bytes 393224 | tf_op jit(solution)/shard_map/ppermute | solution.py:41
  168.1 18.5 %collective-permute-start.38 = (bf16[64,1024]{1,0:T(8,128)(2,1)}, bf16[64,1024]{1,0:T(8,128)(2,1)S(1)}, u32[]{:S(2)}, u32[]{:S(2)}) collective-permute-start(bf16[64,1024]{1,0:T(8,128)(2,1)} %input_grad.1.refs_0_), channel_id=1, source_target_pairs={{0,2},{1,3},{2,0},{3,1},{4,6},{5,7},{6,4},{7,5},{8,10},{9,11},{10,... | collective-permute-start | bytes 393224 | tf_op jit(solution)/shard_map/ppermute | solution.py:41
  173.5 13.1 %collective-permute-start.39 = (bf16[64,1024]{1,0:T(8,128)(2,1)}, bf16[64,1024]{1,0:T(8,128)(2,1)S(1)}, u32[]{:S(2)}, u32[]{:S(2)}) collective-permute-start(bf16[64,1024]{1,0:T(8,128)(2,1)} %input_grad.1.refs_0_), channel_id=1, source_target_pairs={{0,3},{1,2},{2,1},{3,0},{4,7},{5,6},{6,5},{7,4},{8,11},{9,10},{10,... | collective-permute-start | bytes 393224 | tf_op jit(solution)/shard_map/ppermute | solution.py:41
  175.4 14.4 %collective-permute-start.44 = (bf16[64,1024]{1,0:T(8,128)(2,1)S(1)}, bf16[64,1024]{1,0:T(8,128)(2,1)S(1)}, u32[]{:S(2)}, u32[]{:S(2)}) collective-permute-start(bf16[64,1024]{1,0:T(8,128)(2,1)S(1)} %get-tuple-element.299), channel_id=1, source_target_pairs={{0,8},{4,12},{8,0},{12,4},{1,9},{5,13},{9,1},{13,5},{2,10},{6,14},... | collective-permute-start | bytes 393224 | tf_op jit(solution)/shard_map/ppermute | solution.py:41
  180.0 9.8 %collective-permute-start.45 = (bf16[64,1024]{1,0:T(8,128)(2,1)S(1)}, bf16[64,1024]{1,0:T(8,128)(2,1)S(1)}, u32[]{:S(2)}, u32[]{:S(2)}) collective-permute-start(bf16[64,1024]{1,0:T(8,128)(2,1)S(1)} %get-tuple-element.300), channel_id=1, source_target_pairs={{0,12},{4,8},{8,4},{12,0},{1,13},{5,9},{9,5},{13,1},{2,14},{6,10},... | collective-permute-start | bytes 393224 | tf_op jit(solution)/shard_map/ppermute | solution.py:41
  189.9 10.1 %collective-permute-start.46 = (bf16[80,1024]{1,0:T(8,128)(2,1)S(1)}, bf16[80,1024]{1,0:T(8,128)(2,1)S(1)}, u32[]{:S(2)}, u32[]{:S(2)}) collective-permute-start(bf16[80,1024]{1,0:T(8,128)(2,1)S(1)} %out_piece.1.refs_0_), channel_id=1, source_target_pairs={{0,1},{1,0},{2,3},{3,2},{4,5},{5,4},{6,7},{7,6},{8,9},{9,8},{10,11... | collective-permute-start | bytes 491528 | tf_op jit(solution)/shard_map/ppermute | solution.py:41
  190.0 10.0 %collective-permute-start.47 = (bf16[80,1024]{1,0:T(8,128)(2,1)S(1)}, bf16[80,1024]{1,0:T(8,128)(2,1)S(1)}, u32[]{:S(2)}, u32[]{:S(2)}) collective-permute-start(bf16[80,1024]{1,0:T(8,128)(2,1)S(1)} %out_piece.1.refs_0_), channel_id=1, source_target_pairs={{0,2},{1,3},{2,0},{3,1},{4,6},{5,7},{6,4},{7,5},{8,10},{9,11},{10,... | collective-permute-start | bytes 491528 | tf_op jit(solution)/shard_map/ppermute | solution.py:41
  191.1 8.9 %collective-permute-start.48 = (bf16[80,1024]{1,0:T(8,128)(2,1)S(1)}, bf16[80,1024]{1,0:T(8,128)(2,1)S(1)}, u32[]{:S(2)}, u32[]{:S(2)}) collective-permute-start(bf16[80,1024]{1,0:T(8,128)(2,1)S(1)} %out_piece.1.refs_0_), channel_id=1, source_target_pairs={{0,3},{1,2},{2,1},{3,0},{4,7},{5,6},{6,5},{7,4},{8,11},{9,10},{10,... | collective-permute-start | bytes 491528 | tf_op jit(solution)/shard_map/ppermute | solution.py:41
  (38 other events, 434.1 us)

commit v12 on v9

--- a/solution.py
+++ b/solution.py
@@ -859,6 +859,7 @@
     grad_gate = both_copies(grads, grads_got, 0)
     (grad_gate, others[0]), part_sums = tied((grad_gate, others[0]), part_sums)
     moe_near, *moe_across = split_sum([moes[0], *moe_got], "moe_sum")
+    moe_across, part_sums = tied(moe_across, part_sums)
     moe_sums = [moe_near, *deal(moe_across, "expert")]
     ig = call(
         input_grad_kernel, [shape((rows, width), BF)], (xq, gain_one, dh, *part_sums), "input_grad", "bbbb", limit=58

time: 202 us -> 203 us (level)
    unnamed x75 -> x67, local copies, waits for them, and re-layouts: 7.92 us -> 8.03 us
where the time goes in v12:
time: 203 us; the launch traced here: 201 us
  Pallas kernels  77.5 us (38%)
  starting transfers between devices  65.2 us (32%)
  waiting for transfers between devices  47.8 us (24%)
  local copies, waits for them, and re-layouts  8.54 us (4%)
    ppermute x49, starting transfers between devices, swap(): return lax.ppermute(x, axis, [(i, i ^ distance) for i in range(size)])  65.2 us
    ppermute x49, waiting for transfers between devices, swap(): return lax.ppermute(x, axis, [(i, i ^ distance) for i in range(size)])  47.8 us
    pallas_call x18, Pallas kernels, call(): pl.pallas_call(kernel, grid=(1,), out_shape=outs, in_specs=[spec(p, x) fo...  29.3 us
    pallas_call x4, Pallas kernels, run_experts(): pl.pallas_call(kernel, grid=(total // step,), in_specs=[pl.BlockSpec(memo...  21.6 us
    pallas_call x3, Pallas kernels, both_copies(): pl.pallas_call(both_copies_kernel, grid=(local // step,), in_specs=[block...  14.3 us
    pallas_call x1, Pallas kernels, run_grads(): pl.pallas_call(grads_kernel, grid=(local,), in_specs=whole(n) + cols(dgu,...  10.7 us
    unnamed x67, local copies, waits for them, and re-layouts  8.03 us
  transfers between devices with their start and end apart: 49, of which 15 were waited for; matrix products, arithmetic and copies ran while one was open for 1% of the time, Pallas kernels for 31%

profile of v12, /device:TPU:0, one launch (start us, length us, event | category | flops | bytes accessed | tf_op | source)
XLA Modules:
  0.0 201.2 jit_solution(1620805254248944950)
XLA Ops:
  0.6 2.2 %pieces.1 = (bf16[64,1152]{1,0:T(8,128)(2,1)}, bf16[64,1152]{1,0:T(8,128)(2,1)}, bf16[64,1152]{1,0:T(8,128)(2,1)}, bf16[64,1152]{1,0:T(8,128)(2,1)}, bf16[128,1024]{1,0:T(8,128)(2,1)}) custom-call(s32[1]{0:T(128)} %bitcast.me_ref, bf16[256,1024]{1,0:T(8,128)(2,1)} %cot_ref.1, s32[8,256]{1,0:T(8,128)} %bitcast.32, bf16[32,1024]{1,0:T(8,128)(2,1)} %bitcast.31), custom_call_target="tpu_custom_call" | custom-call | tf_op jit(solution)/shard_map/pieces/pallas_call | solution.py:122
  2.8 3.0 %collective-permute-start = (bf16[64,1152]{1,0:T(8,128)(2,1)}, bf16[64,1152]{1,0:T(8,128)(2,1)S(1)}, u32[]{:S(2)}, u32[]{:S(2)}) collective-permute-start(bf16[64,1152]{1,0:T(8,128)(2,1)} %get-tuple-element.173.own_ref.refs_0_.cot_ref), channel_id=1, source_target_pairs={{0,4},{4,0},{8,12},{12,8},{1,5},{5,1},{9,13},{13,9},{2,6},{6,2},{1... | collective-permute-start | bytes 442376 | tf_op jit(solution)/shard_map/ppermute | solution.py:41
  5.8 2.6 %collective-permute-start.4 = (bf16[64,1152]{1,0:T(8,128)(2,1)}, bf16[64,1152]{1,0:T(8,128)(2,1)S(1)}, u32[]{:S(2)}, u32[]{:S(2)}) collective-permute-start(bf16[64,1152]{1,0:T(8,128)(2,1)} %get-tuple-element.173.own_ref.refs_0_.cot_ref), channel_id=1, source_target_pairs={{0,8},{4,12},{8,0},{12,4},{1,9},{5,13},{9,1},{13,5},{2,10},{6,14},... | collective-permute-start | bytes 442376 | tf_op jit(solution)/shard_map/ppermute | solution.py:41
  8.4 3.5 %collective-permute-done.refs_0_ = bf16[64,1152]{1,0:T(8,128)(2,1)S(1)} collective-permute-done((bf16[64,1152]{1,0:T(8,128)(2,1)}, bf16[64,1152]{1,0:T(8,128)(2,1)S(1)}, u32[]{:S(2)}, u32[]{:S(2)}) %collective-permute-start) | collective-permute-done | bytes 147488 | tf_op jit(solution)/shard_map/ppermute | solution.py:41
  11.9 4.7 %attend.1 = (bf16[256,1024]{1,0:T(8,128)(2,1)}, bf16[256,256]{1,0:T(8,128)(2,1)}, bf16[256,128]{1,0:T(8,128)(2,1)}, bf16[256,128]{1,0:T(8,128)(2,1)}, bf16[256,2...) custom-call(s32[1]{0:T(128)} %bitcast.me_ref, ...), custom_call_target="tpu_custom_call" | custom-call | flops 53687091200 | tf_op jit(solution)/shard_map/attend/pallas_call | solution.py:122
  16.6 1.7 collective-permute-start.1
  18.3 1.5 collective-permute-start.2
  20.1 1.7 collective-permute-done.1.refs_0_
  21.8 1.7 collective-permute-done.2.refs_1_
  23.5 2.4 %collective-permute-done.3.refs_2_ = bf16[64,1024]{1,0:T(8,128)(2,1)S(1)} collective-permute-done((bf16[64,1024]{1,0:T(8,128)(2,1)}, bf16[64,1024]{1,0:T(8,128)(2,1)S(1)}, u32[]{:S(2)}, u32[]{:S(2)}) %collective-permute-start.3) | collective-permute-done | bytes 131104 | tf_op jit(solution)/shard_map/ppermute | solution.py:41
  26.5 2.0 norm_two.1
  30.1 3.7 %collective-permute-done.6.refs_1_ = bf16[64,1024]{1,0:T(8,128)(2,1)S(1)} collective-permute-done((bf16[64,1024]{1,0:T(8,128)(2,1)}, bf16[64,1024]{1,0:T(8,128)(2,1)S(1)}, u32[]{:S(2)}, u32[]{:S(2)}) %collective-permute-start.6) | collective-permute-done | bytes 131104 | tf_op jit(solution)/shard_map/ppermute | solution.py:41
  34.3 2.6 %collective-permute-start.7 = (bf16[64,1024]{1,0:T(8,128)(2,1)}, bf16[64,1024]{1,0:T(8,128)(2,1)S(1)}, u32[]{:S(2)}, u32[]{:S(2)}) collective-permute-start(bf16[64,1024]{1,0:T(8,128)(2,1)} %get-tuple-element.182.refs_0_.n_ref), channel_id=1, source_target_pairs={{0,8},{4,12},{8,0},{12,4},{1,9},{5,13},{9,1},{13,5},{2,10},{6,14},... | collective-permute-start | bytes 393224 | tf_op jit(solution)/shard_map/ppermute | solution.py:41
  38.3 1.6 copy-done.1
  40.0 1.5 gate_up_weights.1.wcat
  41.5 2.9 %collective-permute-done.7.refs_2_ = bf16[64,1024]{1,0:T(8,128)(2,1)S(1)} collective-permute-done((bf16[64,1024]{1,0:T(8,128)(2,1)}, bf16[64,1024]{1,0:T(8,128)(2,1)S(1)}, u32[]{:S(2)}, u32[]{:S(2)}) %collective-permute-start.7) | collective-permute-done | bytes 131104 | tf_op jit(solution)/shard_map/ppermute | solution.py:41
  45.9 1.6 collective-permute-start.10
  47.5 4.4 %collective-permute-done.14.refs_7_.far_ref = bf16[3,64,1152]{2,1,0:T(8,128)(2,1)S(1)} collective-permute-done((bf16[3,64,1152]{2,1,0:T(8,128)(2,1)S(1)}, bf16[3,64,1152]{2,1,0:T(8,128)(2,1)S(1)}, u32[]{:S(2)}, u32[]{:S(2)}) %collective-permute-start.14) | collective-permute-done | bytes 442400 | tf_op jit(solution)/shard_map/ppermute | solution.py:41
  51.9 2.2 %counts.1 = f32[1,128]{1,0:T(1,128)S(1)} custom-call(bf16[64,1152]{1,0:T(8,128)(2,1)S(1)} %copy-done.5, bf16[64,1152]{1,0:T(8,128)(2,1)S(1)} %copy-done.17, bf16[64,1152]{1,0:T(8,128)(2,1)S(1)} %copy-done.16, bf16[64,1152]{1,0:T(8,128)(2,1)S(1)} %copy-done.15, bf16[3,64,1152]{2,1,0:T(8,128)(2,1)S(1)} %together.2.far_ref.refs_4_, ...), custom_call_target="tpu_custom_call" | custom-call | tf_op jit(solution)/shard_map/counts/pallas_call | solution.py:122
  54.2 4.3 %experts.4 = (bf16[256,1024]{1,0:T(8,128)(2,1)S(1)}, bf16[256,2048]{1,0:T(8,128)(2,1)S(1)}, bf16[256,1024]{1,0:T(8,128)(2,1)S(1)}, f32[4,64,1152]{2,1,0:T(8,128)S(1)}, f32[4,64,1024]{2,1,0:T(8,128)S(1)}) custom-call(s32[1]{0:T(128)} %bitcast.9.base_ref, bf16[4,64,1024]{2,1,0:T(8,128)(2,1)S(1)} %together.3.x_ref.a0, bf16[64,1152]{1,0:T(8,128)(2,1)S(1)} %copy-done.5, ...), custom_call_target="tpu_custom_call" | custom-call | flops 3355443200 | tf_op jit(solution)/shard_map/experts/pallas_call | solution.py:353
  59.9 6.1 %experts.5 = (bf16[256,1024]{1,0:T(8,128)(2,1)S(1)}, bf16[256,2048]{1,0:T(8,128)(2,1)S(1)}, bf16[256,1024]{1,0:T(8,128)(2,1)S(1)}, bf16[4,64,1152]{2,1,0:T(8,128)(2,1)}, bf16[4,64,1024]{2,1,0:T(8,128)(2,1)S(1)}) custom-call(s32[1]{0:T(128)} %bitcast.9.base_ref, bf16[4,64,1024]{2,1,0:T(8,128)(2,1)S(1)} %collective-permute-done.9.x_ref.a1, ...), custom_call_target="tpu_custom_call" | custom-call | flops 3355443200 | tf_op jit(solution)/shard_map/experts/pallas_call | solution.py:353
  67.4 6.4 %experts.6 = (bf16[256,1024]{1,0:T(8,128)(2,1)S(1)}, bf16[256,2048]{1,0:T(8,128)(2,1)S(1)}, bf16[256,1024]{1,0:T(8,128)(2,1)S(1)}, bf16[4,64,1152]{2,1,0:T(8,128)(2,1)}, bf16[4,64,1024]{2,1,0:T(8,128)(2,1)S(1)}) custom-call(s32[1]{0:T(128)} %bitcast.9.base_ref, bf16[4,64,1024]{2,1,0:T(8,128)(2,1)S(1)} %collective-permute-done.10.x_ref.a2, ...), custom_call_target="tpu_custom_call" | custom-call | flops 3355443200 | tf_op jit(solution)/shard_map/experts/pallas_call | solution.py:353
  74.6 4.8 %experts.7 = (bf16[256,1024]{1,0:T(8,128)(2,1)S(1)}, bf16[256,2048]{1,0:T(8,128)(2,1)S(1)}, bf16[256,1024]{1,0:T(8,128)(2,1)S(1)}, f32[64,1152]{1,0:T(8,128)S(1)...) custom-call(s32[1]{0:T(128)} %bitcast.9.base_ref, ...), custom_call_target="tpu_custom_call" | custom-call | flops 3355443200 | tf_op jit(solution)/shard_map/experts/pallas_call | solution.py:353
  80.3 5.0 %collective-permute-start.18 = (bf16[64,1152]{1,0:T(8,128)(2,1)}, bf16[64,1152]{1,0:T(8,128)(2,1)}, u32[]{:S(2)}, u32[]{:S(2)}) collective-permute-start(bf16[64,1152]{1,0:T(8,128)(2,1)} %get-tuple-element.227), channel_id=1, source_target_pairs={{0,4},{4,0},{8,12},{12,8},{1,5},{5,1},{9,13},{13,9},{2,6},{6,2},{1... | collective-permute-start | bytes 442376 | tf_op jit(solution)/shard_map/ppermute | solution.py:41
  85.2 2.4 %collective-permute-start.20 = (bf16[64,1152]{1,0:T(8,128)(2,1)}, bf16[64,1152]{1,0:T(8,128)(2,1)}, u32[]{:S(2)}, u32[]{:S(2)}) collective-permute-start(bf16[64,1152]{1,0:T(8,128)(2,1)} %get-tuple-element.229), channel_id=1, source_target_pairs={{0,12},{4,8},{8,4},{12,0},{1,13},{5,9},{9,5},{13,1},{2,14},{6,10},... | collective-permute-start | bytes 442376 | tf_op jit(solution)/shard_map/ppermute | solution.py:41
  87.6 10.7 %expert_grads.1.mine_ref = bf16[8,3072,128]{2,1,0:T(8,128)(2,1)} custom-call(bf16[256,1024]{1,0:T(8,128)(2,1)S(1)} %bitcast.20, bf16[256,1024]{1,0:T(8,128)(2,1)S(1)} %bitcast.21, bf16[256,1024]{1,0:T(8,128)(2,1)S(1)} %bitcast.22, bf16[256,1024]{1,0:T(8,128)(2,1)S(1)} %bitcast.23, bf16[256,2048]{1,0:T(8,128)(2,1)S(1)} %get-tuple-element.194.refs_4_, ...), custom_call_target="tpu_custom_call" | custom-call | flops 644245094400 | tf_op jit(solution)/shard_map/expert_grads/pallas_call | solution.py:426
  100.2 1.6 collective-permute-start.23
  103.1 1.5 collective-permute-start.26
  104.6 2.6 %collective-permute-done.23.refs_2_ = bf16[64,1152]{1,0:T(8,128)(2,1)S(1)} collective-permute-done((bf16[64,1152]{1,0:T(8,128)(2,1)S(1)}, bf16[64,1152]{1,0:T(8,128)(2,1)S(1)}, u32[]{:S(2)}, u32[]{:S(2)}) %collective-permute-start.23) | collective-permute-done | bytes 147488 | tf_op jit(solution)/shard_map/ppermute | solution.py:41
  108.3 1.7 collective-permute-start.24
  109.9 5.6 %collective-permute-done.25.refs_3_ = bf16[64,1152]{1,0:T(8,128)(2,1)S(1)} collective-permute-done((bf16[64,1152]{1,0:T(8,128)(2,1)S(1)}, bf16[64,1152]{1,0:T(8,128)(2,1)S(1)}, u32[]{:S(2)}, u32[]{:S(2)}) %collective-permute-start.25) | collective-permute-done | bytes 147488 | tf_op jit(solution)/shard_map/ppermute | solution.py:41
  117.7 1.7 collective-permute-start.28
  119.6 1.5 collective-permute-start.30
  121.7 2.6 %collective-permute-done.28.w1 = bf16[64,1152]{1,0:T(8,128)(2,1)S(1)} collective-permute-done((bf16[64,1152]{1,0:T(8,128)(2,1)S(1)}, bf16[64,1152]{1,0:T(8,128)(2,1)S(1)}, u32[]{:S(2)}, u32[]{:S(2)}) %collective-permute-start.28) | collective-permute-done | bytes 147488 | tf_op jit(solution)/shard_map/ppermute | solution.py:41
  124.3 4.2 %collective-permute-done.29.w2 = bf16[64,1152]{1,0:T(8,128)(2,1)S(1)} collective-permute-done((bf16[64,1152]{1,0:T(8,128)(2,1)S(1)}, bf16[64,1152]{1,0:T(8,128)(2,1)S(1)}, u32[]{:S(2)}, u32[]{:S(2)}) %collective-permute-start.29) | collective-permute-done | bytes 147488 | tf_op jit(solution)/shard_map/ppermute | solution.py:41
  129.2 5.5 %attend_back.1 = (bf16[256,1152]{1,0:T(8,128)(2,1)}, bf16[256,512]{1,0:T(8,128)(2,1)}, f32[8,1024]{1,0:T(8,128)}, f32[64,1024]{1,0:T(8,128)}, bf16[64,1024]{1,0:...) custom-call(s32[1]{0:T(128)} %bitcast.me_ref, bf16[64,1152]{1,0:T(8,128)(2,1)} %copy-done.23, ...), custom_call_target="tpu_custom_call" | custom-call | flops 53687091200 | tf_op jit(solution)/shard_map/attend_back/pallas_call | solution.py:122
  134.7 4.0 %dense.1 = (f32[512,896]{1,0:T(8,128)}, bf16[512,896]{1,0:T(8,128)(2,1)}) custom-call(s32[2]{0:T(128)} %pad_add_fusion.me_ref, bf16[4,64,1024]{2,1,0:T(8,128)(2,1)} %copy-done.2, bf16[4,64,1024]{2,1,0:T(8,128)(2,1)} %copy-done.9, bf16[4,64,1024]{2,1,0:T(8,128)(2,1)} %copy-done.10, bf16[4,64,1024]{2,1,0:T(8,128)(2,1)} %copy-done.11, ...), custom_call_target="tpu_custom_call" | custom-call | flops 100 | tf_op jit(solution)/shard_map/dense/pallas_call | solution.py:122
  144.0 2.2 %collective-permute-start.34 = (bf16[128,896]{1,0:T(8,128)(2,1)S(1)}, bf16[128,896]{1,0:T(8,128)(2,1)S(1)}, u32[]{:S(2)}, u32[]{:S(2)}) collective-permute-start(bf16[128,896]{1,0:T(8,128)(2,1)S(1)} %get-tuple-element.288), channel_id=1, source_target_pairs={{0,4},{4,0},{8,12},{12,8},{1,5},{5,1},{9,13},{13,9},{2,6},{6,2},{1... | collective-permute-start | bytes 688136 | tf_op jit(solution)/shard_map/ppermute | solution.py:41
  146.9 1.6 collective-permute-start.36
  149.7 6.4 %collective-permute-done.35.refs_1_ = bf16[64,1024]{1,0:T(8,128)(2,1)S(1)} collective-permute-done((bf16[64,1024]{1,0:T(8,128)(2,1)S(1)}, bf16[64,1024]{1,0:T(8,128)(2,1)S(1)}, u32[]{:S(2)}, u32[]{:S(2)}) %collective-permute-start.35) | collective-permute-done | bytes 131104 | tf_op jit(solution)/shard_map/ppermute | solution.py:41
  156.1 4.0 %collective-permute-start.41 = (bf16[128,896]{1,0:T(8,128)(2,1)S(1)}, bf16[128,896]{1,0:T(8,128)(2,1)S(1)}, u32[]{:S(2)}, u32[]{:S(2)}) collective-permute-start(bf16[128,896]{1,0:T(8,128)(2,1)S(1)} %get-tuple-element.304), channel_id=1, source_target_pairs={{0,8},{4,12},{8,0},{12,4},{1,9},{5,13},{9,1},{13,5},{2,10},{6,14},... | collective-permute-start | bytes 688136 | tf_op jit(solution)/shard_map/ppermute | solution.py:41
  160.6 4.7 %both_copies.4 = f32[8,1024,128]{2,1,0:T(8,128)} custom-call(bf16[8,3072,128]{2,1,0:T(8,128)(2,1)} %expert_grads.1.mine_ref, bf16[8,3072,128]{2,1,0:T(8,128)(2,1)} %collective-permute-done.27.other_ref), custom_call_target="tpu_custom_call" | custom-call | bytes 25165824 | tf_op jit(solution)/shard_map/both_copies/pallas_call | solution.py:455
  165.6 2.1 %input_grad.1.refs_0_ = bf16[64,1024]{1,0:T(8,128)(2,1)} custom-call(bf16[64,1024]{1,0:T(8,128)(2,1)} %get-tuple-element.175.x_ref, f32[1,1024]{1,0:T(1,128)} %bitcast.34, f32[64,1024]{1,0:T(8,128)} %copy-done.14, f32[64,1024]{1,0:T(8,128)} %get-tuple-element.297.refs_0_, bf16[64,1024]{1,0:T(8,128)(2,1)} %copy-done.25, ...), custom_call_target="tpu_custom_call" | custom-call | tf_op jit(solution)/shard_map/input_grad/pallas_call | solution.py:122
  171.2 4.2 %collective-permute-done.41.refs_1_ = bf16[128,896]{1,0:T(8,128)(2,1)S(1)} collective-permute-done((bf16[128,896]{1,0:T(8,128)(2,1)S(1)}, bf16[128,896]{1,0:T(8,128)(2,1)S(1)}, u32[]{:S(2)}, u32[]{:S(2)}) %collective-permute-start.41) | collective-permute-done | bytes 229408 | tf_op jit(solution)/shard_map/ppermute | solution.py:41
  175.3 4.2 %collective-permute-start.44 = (bf16[64,1024]{1,0:T(8,128)(2,1)S(1)}, bf16[64,1024]{1,0:T(8,128)(2,1)S(1)}, u32[]{:S(2)}, u32[]{:S(2)}) collective-permute-start(bf16[64,1024]{1,0:T(8,128)(2,1)S(1)} %get-tuple-element.313), channel_id=1, source_target_pairs={{0,8},{4,12},{8,0},{12,4},{1,9},{5,13},{9,1},{13,5},{2,10},{6,14},... | collective-permute-start | bytes 393224 | tf_op jit(solution)/shard_map/ppermute | solution.py:41
  179.5 3.3 %collective-permute-start.45 = (bf16[64,1024]{1,0:T(8,128)(2,1)S(1)}, bf16[64,1024]{1,0:T(8,128)(2,1)S(1)}, u32[]{:S(2)}, u32[]{:S(2)}) collective-permute-start(bf16[64,1024]{1,0:T(8,128)(2,1)S(1)} %get-tuple-element.314), channel_id=1, source_target_pairs={{0,12},{4,8},{8,4},{12,0},{1,13},{5,9},{9,5},{13,1},{2,14},{6,10},... | collective-permute-start | bytes 393224 | tf_op jit(solution)/shard_map/ppermute | solution.py:41
  182.8 4.7 %both_copies.5 = f32[8,1024,128]{2,1,0:T(8,128)} custom-call(bf16[8,3072,128]{2,1,0:T(8,128)(2,1)} %expert_grads.1.mine_ref, bf16[8,3072,128]{2,1,0:T(8,128)(2,1)} %collective-permute-done.27.other_ref), custom_call_target="tpu_custom_call" | custom-call | bytes 25165824 | tf_op jit(solution)/shard_map/both_copies/pallas_call | solution.py:455
  192.7 4.8 %both_copies.3 = f32[8,128,1024]{2,1,0:T(8,128)} custom-call(bf16[8,3072,128]{2,1,0:T(8,128)(2,1)} %expert_grads.1.mine_ref, bf16[8,3072,128]{2,1,0:T(8,128)(2,1)} %collective-permute-done.27.other_ref), custom_call_target="tpu_custom_call" | custom-call | bytes 25165824 | tf_op jit(solution)/shard_map/both_copies/pallas_call | solution.py:455
  (148 shorter events, 38.6 us)
Async XLA Ops:
  2.8 9.1 %collective-permute-start = (bf16[64,1152]{1,0:T(8,128)(2,1)}, bf16[64,1152]{1,0:T(8,128)(2,1)S(1)}, u32[]{:S(2)}, u32[]{:S(2)}) collective-permute-start(bf16[64,1152]{1,0:T(8,128)(2,1)} %get-tuple-element.173.own_ref.refs_0_.cot_ref), channel_id=1, source_target_pairs={{0,4},{4,0},{8,12},{12,8},{1,5},{5,1},{9,13},{13,9},{2,6},{6,2},{1... | collective-permute-start | bytes 442376 | tf_op jit(solution)/shard_map/ppermute | solution.py:41
  5.8 22.7 %collective-permute-start.4 = (bf16[64,1152]{1,0:T(8,128)(2,1)}, bf16[64,1152]{1,0:T(8,128)(2,1)S(1)}, u32[]{:S(2)}, u32[]{:S(2)}) collective-permute-start(bf16[64,1152]{1,0:T(8,128)(2,1)} %get-tuple-element.173.own_ref.refs_0_.cot_ref), channel_id=1, source_target_pairs={{0,8},{4,12},{8,0},{12,4},{1,9},{5,13},{9,1},{13,5},{2,10},{6,14},... | collective-permute-start | bytes 442376 | tf_op jit(solution)/shard_map/ppermute | solution.py:41
  8.4 20.1 %collective-permute-start.5 = (bf16[64,1152]{1,0:T(8,128)(2,1)}, bf16[64,1152]{1,0:T(8,128)(2,1)S(1)}, u32[]{:S(2)}, u32[]{:S(2)}) collective-permute-start(bf16[64,1152]{1,0:T(8,128)(2,1)} %get-tuple-element.173.own_ref.refs_0_.cot_ref), channel_id=1, source_target_pairs={{0,12},{4,8},{8,4},{12,0},{1,13},{5,9},{9,5},{13,1},{2,14},{6,10},... | collective-permute-start | bytes 442376 | tf_op jit(solution)/shard_map/ppermute | solution.py:41
  16.6 5.2 %collective-permute-start.1 = (bf16[64,1024]{1,0:T(8,128)(2,1)}, bf16[64,1024]{1,0:T(8,128)(2,1)S(1)}, u32[]{:S(2)}, u32[]{:S(2)}) collective-permute-start(bf16[64,1024]{1,0:T(8,128)(2,1)} %get-tuple-element.177), channel_id=1, source_target_pairs={{0,1},{1,0},{2,3},{3,2},{4,5},{5,4},{6,7},{7,6},{8,9},{9,8},{10,11... | collective-permute-start | bytes 393224 | tf_op jit(solution)/shard_map/ppermute | solution.py:41
  18.3 5.2 %collective-permute-start.2 = (bf16[64,1024]{1,0:T(8,128)(2,1)}, bf16[64,1024]{1,0:T(8,128)(2,1)S(1)}, u32[]{:S(2)}, u32[]{:S(2)}) collective-permute-start(bf16[64,1024]{1,0:T(8,128)(2,1)} %get-tuple-element.178), channel_id=1, source_target_pairs={{0,2},{1,3},{2,0},{3,1},{4,6},{5,7},{6,4},{7,5},{8,10},{9,11},{10,... | collective-permute-start | bytes 393224 | tf_op jit(solution)/shard_map/ppermute | solution.py:41
  19.8 6.1 %collective-permute-start.3 = (bf16[64,1024]{1,0:T(8,128)(2,1)}, bf16[64,1024]{1,0:T(8,128)(2,1)S(1)}, u32[]{:S(2)}, u32[]{:S(2)}) collective-permute-start(bf16[64,1024]{1,0:T(8,128)(2,1)} %get-tuple-element.179), channel_id=1, source_target_pairs={{0,3},{1,2},{2,1},{3,0},{4,7},{5,6},{6,5},{7,4},{8,11},{9,10},{10,... | collective-permute-start | bytes 393224 | tf_op jit(solution)/shard_map/ppermute | solution.py:41
  28.5 5.2 %collective-permute-start.6 = (bf16[64,1024]{1,0:T(8,128)(2,1)}, bf16[64,1024]{1,0:T(8,128)(2,1)S(1)}, u32[]{:S(2)}, u32[]{:S(2)}) collective-permute-start(bf16[64,1024]{1,0:T(8,128)(2,1)} %get-tuple-element.182.refs_0_.n_ref), channel_id=1, source_target_pairs={{0,4},{4,0},{8,12},{12,8},{1,5},{5,1},{9,13},{13,9},{2,6},{6,2},{1... | collective-permute-start | bytes 393224 | tf_op jit(solution)/shard_map/ppermute | solution.py:41
  29.0 18.6 %collective-permute-start.11 = (bf16[3,64,1152]{2,1,0:T(8,128)(2,1)S(1)}, bf16[3,64,1152]{2,1,0:T(8,128)(2,1)}, u32[]{:S(2)}, u32[]{:S(2)}) collective-permute-start(bf16[3,64,1152]{2,1,0:T(8,128)(2,1)S(1)} %together.2.far_ref.refs_4_), channel_id=1, source_target_pairs={{0,1},{1,0},{2,3},{3,2},{4,5},{5,4},{6,7},{7,6},{8,9},{9,8},{10,11... | collective-permute-start | bytes 1327112 | tf_op jit(solution)/shard_map/ppermute | solution.py:41
  29.6 18.0 %collective-permute-start.12 = (bf16[3,64,1152]{2,1,0:T(8,128)(2,1)S(1)}, bf16[3,64,1152]{2,1,0:T(8,128)(2,1)}, u32[]{:S(2)}, u32[]{:S(2)}) collective-permute-start(bf16[3,64,1152]{2,1,0:T(8,128)(2,1)S(1)} %together.2.far_ref.refs_4_), channel_id=1, source_target_pairs={{0,2},{1,3},{2,0},{3,1},{4,6},{5,7},{6,4},{7,5},{8,10},{9,11},{10,... | collective-permute-start | bytes 1327112 | tf_op jit(solution)/shard_map/ppermute | solution.py:41
  33.8 18.1 %collective-permute-start.14 = (bf16[3,64,1152]{2,1,0:T(8,128)(2,1)S(1)}, bf16[3,64,1152]{2,1,0:T(8,128)(2,1)S(1)}, u32[]{:S(2)}, u32[]{:S(2)}) collective-permute-start(bf16[3,64,1152]{2,1,0:T(8,128)(2,1)S(1)} %together.2.far_ref.refs_4_), channel_id=1, source_target_pairs={{0,3},{1,2},{2,1},{3,0},{4,7},{5,6},{6,5},{7,4},{8,11},{9,10},{10,... | collective-permute-start | bytes 1327112 | tf_op jit(solution)/shard_map/ppermute | solution.py:41
  34.3 10.1 %collective-permute-start.7 = (bf16[64,1024]{1,0:T(8,128)(2,1)}, bf16[64,1024]{1,0:T(8,128)(2,1)S(1)}, u32[]{:S(2)}, u32[]{:S(2)}) collective-permute-start(bf16[64,1024]{1,0:T(8,128)(2,1)} %get-tuple-element.182.refs_0_.n_ref), channel_id=1, source_target_pairs={{0,8},{4,12},{8,0},{12,4},{1,9},{5,13},{9,1},{13,5},{2,10},{6,14},... | collective-permute-start | bytes 393224 | tf_op jit(solution)/shard_map/ppermute | solution.py:41
  36.9 7.5 %collective-permute-start.8 = (bf16[64,1024]{1,0:T(8,128)(2,1)}, bf16[64,1024]{1,0:T(8,128)(2,1)S(1)}, u32[]{:S(2)}, u32[]{:S(2)}) collective-permute-start(bf16[64,1024]{1,0:T(8,128)(2,1)} %get-tuple-element.182.refs_0_.n_ref), channel_id=1, source_target_pairs={{0,12},{4,8},{8,4},{12,0},{1,13},{5,9},{9,5},{13,1},{2,14},{6,10},... | collective-permute-start | bytes 393224 | tf_op jit(solution)/shard_map/ppermute | solution.py:41
  44.4 15.5 %collective-permute-start.9 = (bf16[4,64,1024]{2,1,0:T(8,128)(2,1)S(1)}, bf16[4,64,1024]{2,1,0:T(8,128)(2,1)S(1)}, u32[]{:S(2)}, u32[]{:S(2)}) collective-permute-start(bf16[4,64,1024]{2,1,0:T(8,128)(2,1)S(1)} %together.3.x_ref.a0), channel_id=1, source_target_pairs={{0,1},{1,0},{2,3},{3,2},{4,5},{5,4},{6,7},{7,6},{8,9},{9,8},{10,11... | collective-permute-start | bytes 1572872 | tf_op jit(solution)/shard_map/ppermute | solution.py:41
  45.9 21.5 %collective-permute-start.10 = (bf16[4,64,1024]{2,1,0:T(8,128)(2,1)S(1)}, bf16[4,64,1024]{2,1,0:T(8,128)(2,1)S(1)}, u32[]{:S(2)}, u32[]{:S(2)}) collective-permute-start(bf16[4,64,1024]{2,1,0:T(8,128)(2,1)S(1)} %together.3.x_ref.a0), channel_id=1, source_target_pairs={{0,2},{1,3},{2,0},{3,1},{4,6},{5,7},{6,4},{7,5},{8,10},{9,11},{10,... | collective-permute-start | bytes 1572872 | tf_op jit(solution)/shard_map/ppermute | solution.py:41
  54.1 5.7 %collective-permute-start.15 = (f32[1,128]{1,0:T(1,128)S(1)}, f32[1,128]{1,0:T(1,128)S(1)}, u32[]{:S(2)}, u32[]{:S(2)}) collective-permute-start(f32[1,128]{1,0:T(1,128)S(1)} %counts.1), channel_id=1, source_target_pairs={{0,16},{16,0},{1,17},{17,1},{2,18},{18,2},{3,19},{19,3},{4,20},{20... | collective-permute-start | bytes 1544 | tf_op jit(solution)/shard_map/ppermute | solution.py:41
  58.6 16.0 %collective-permute-start.13 = (bf16[4,64,1024]{2,1,0:T(8,128)(2,1)S(1)}, bf16[4,64,1024]{2,1,0:T(8,128)(2,1)S(1)}, u32[]{:S(2)}, u32[]{:S(2)}) collective-permute-start(bf16[4,64,1024]{2,1,0:T(8,128)(2,1)S(1)} %together.3.x_ref.a0), channel_id=1, source_target_pairs={{0,3},{1,2},{2,1},{3,0},{4,7},{5,6},{6,5},{7,4},{8,11},{9,10},{10,... | collective-permute-start | bytes 1572872 | tf_op jit(solution)/shard_map/ppermute | solution.py:41
  66.0 32.3 %collective-permute-start.16 = (bf16[4,64,1152]{2,1,0:T(8,128)(2,1)}, bf16[4,64,1152]{2,1,0:T(8,128)(2,1)}, u32[]{:S(2)}, u32[]{:S(2)}) collective-permute-start(bf16[4,64,1152]{2,1,0:T(8,128)(2,1)} %get-tuple-element.201), channel_id=1, source_target_pairs={{0,1},{1,0},{2,3},{3,2},{4,5},{5,4},{6,7},{7,6},{8,9},{9,8},{10,11... | collective-permute-start | bytes 1769480 | tf_op jit(solution)/shard_map/ppermute | solution.py:41
  73.8 24.5 %collective-permute-start.17 = (bf16[4,64,1152]{2,1,0:T(8,128)(2,1)}, bf16[4,64,1152]{2,1,0:T(8,128)(2,1)}, u32[]{:S(2)}, u32[]{:S(2)}) collective-permute-start(bf16[4,64,1152]{2,1,0:T(8,128)(2,1)} %get-tuple-element.210), channel_id=1, source_target_pairs={{0,2},{1,3},{2,0},{3,1},{4,6},{5,7},{6,4},{7,5},{8,10},{9,11},{10,... | collective-permute-start | bytes 1769480 | tf_op jit(solution)/shard_map/ppermute | solution.py:41
  80.3 18.0 %collective-permute-start.18 = (bf16[64,1152]{1,0:T(8,128)(2,1)}, bf16[64,1152]{1,0:T(8,128)(2,1)}, u32[]{:S(2)}, u32[]{:S(2)}) collective-permute-start(bf16[64,1152]{1,0:T(8,128)(2,1)} %get-tuple-element.227), channel_id=1, source_target_pairs={{0,4},{4,0},{8,12},{12,8},{1,5},{5,1},{9,13},{13,9},{2,6},{6,2},{1... | collective-permute-start | bytes 442376 | tf_op jit(solution)/shard_map/ppermute | solution.py:41
  85.2 13.1 %collective-permute-start.19 = (bf16[64,1152]{1,0:T(8,128)(2,1)}, bf16[64,1152]{1,0:T(8,128)(2,1)}, u32[]{:S(2)}, u32[]{:S(2)}) collective-permute-start(bf16[64,1152]{1,0:T(8,128)(2,1)} %get-tuple-element.228), channel_id=1, source_target_pairs={{0,8},{4,12},{8,0},{12,4},{1,9},{5,13},{9,1},{13,5},{2,10},{6,14},... | collective-permute-start | bytes 442376 | tf_op jit(solution)/shard_map/ppermute | solution.py:41
  85.2 13.1 %collective-permute-start.20 = (bf16[64,1152]{1,0:T(8,128)(2,1)}, bf16[64,1152]{1,0:T(8,128)(2,1)}, u32[]{:S(2)}, u32[]{:S(2)}) collective-permute-start(bf16[64,1152]{1,0:T(8,128)(2,1)} %get-tuple-element.229), channel_id=1, source_target_pairs={{0,12},{4,8},{8,4},{12,0},{1,13},{5,9},{9,5},{13,1},{2,14},{6,10},... | collective-permute-start | bytes 442376 | tf_op jit(solution)/shard_map/ppermute | solution.py:41
  99.7 15.8 %collective-permute-start.21 = (bf16[4,64,1024]{2,1,0:T(8,128)(2,1)S(1)}, bf16[4,64,1024]{2,1,0:T(8,128)(2,1)S(1)}, u32[]{:S(2)}, u32[]{:S(2)}) collective-permute-start(bf16[4,64,1024]{2,1,0:T(8,128)(2,1)S(1)} %get-tuple-element.239), channel_id=1, source_target_pairs={{0,1},{1,0},{2,3},{3,2},{4,5},{5,4},{6,7},{7,6},{8,9},{9,8},{10,11... | collective-permute-start | bytes 1572872 | tf_op jit(solution)/shard_map/ppermute | solution.py:41
  100.2 15.4 %collective-permute-start.22 = (bf16[4,64,1024]{2,1,0:T(8,128)(2,1)S(1)}, bf16[4,64,1024]{2,1,0:T(8,128)(2,1)S(1)}, u32[]{:S(2)}, u32[]{:S(2)}) collective-permute-start(bf16[4,64,1024]{2,1,0:T(8,128)(2,1)S(1)} %get-tuple-element.240), channel_id=1, source_target_pairs={{0,2},{1,3},{2,0},{3,1},{4,6},{5,7},{6,4},{7,5},{8,10},{9,11},{10,... | collective-permute-start | bytes 1572872 | tf_op jit(solution)/shard_map/ppermute | solution.py:41
  100.2 7.0 %collective-permute-start.23 = (bf16[64,1152]{1,0:T(8,128)(2,1)S(1)}, bf16[64,1152]{1,0:T(8,128)(2,1)S(1)}, u32[]{:S(2)}, u32[]{:S(2)}) collective-permute-start(bf16[64,1152]{1,0:T(8,128)(2,1)S(1)} %get-tuple-element.242), channel_id=1, source_target_pairs={{0,4},{4,0},{8,12},{12,8},{1,5},{5,1},{9,13},{13,9},{2,6},{6,2},{1... | collective-permute-start | bytes 442376 | tf_op jit(solution)/shard_map/ppermute | solution.py:41
  101.8 13.7 %collective-permute-start.25 = (bf16[64,1152]{1,0:T(8,128)(2,1)S(1)}, bf16[64,1152]{1,0:T(8,128)(2,1)S(1)}, u32[]{:S(2)}, u32[]{:S(2)}) collective-permute-start(bf16[64,1152]{1,0:T(8,128)(2,1)S(1)} %get-tuple-element.249), channel_id=1, source_target_pairs={{0,8},{4,12},{8,0},{12,4},{1,9},{5,13},{9,1},{13,5},{2,10},{6,14},... | collective-permute-start | bytes 442376 | tf_op jit(solution)/shard_map/ppermute | solution.py:41
  103.1 12.5 %collective-permute-start.26 = (bf16[64,1152]{1,0:T(8,128)(2,1)S(1)}, bf16[64,1152]{1,0:T(8,128)(2,1)S(1)}, u32[]{:S(2)}, u32[]{:S(2)}) collective-permute-start(bf16[64,1152]{1,0:T(8,128)(2,1)S(1)} %get-tuple-element.250), channel_id=1, source_target_pairs={{0,12},{4,8},{8,4},{12,0},{1,13},{5,9},{9,5},{13,1},{2,14},{6,10},... | collective-permute-start | bytes 442376 | tf_op jit(solution)/shard_map/ppermute | solution.py:41
  108.3 7.3 %collective-permute-start.24 = (bf16[64,1152]{1,0:T(8,128)(2,1)S(1)}, bf16[64,1152]{1,0:T(8,128)(2,1)S(1)}, u32[]{:S(2)}, u32[]{:S(2)}) collective-permute-start(bf16[64,1152]{1,0:T(8,128)(2,1)S(1)} %through.1), channel_id=1, source_target_pairs={{0,3},{1,2},{2,1},{3,0},{4,7},{5,6},{6,5},{7,4},{8,11},{9,10},{10,... | collective-permute-start | bytes 442376 | tf_op jit(solution)/shard_map/ppermute | solution.py:41
  117.7 10.8 %collective-permute-start.27 = (bf16[8,3072,128]{2,1,0:T(8,128)(2,1)}, bf16[8,3072,128]{2,1,0:T(8,128)(2,1)}, u32[]{:S(2)}, u32[]{:S(2)}) collective-permute-start(bf16[8,3072,128]{2,1,0:T(8,128)(2,1)} %expert_grads.1.mine_ref), channel_id=1, source_target_pairs={{0,16},{16,0},{1,17},{17,1},{2,18},{18,2},{3,19},{19,3},{4,20},{20... | collective-permute-start | bytes 18874376 | tf_op jit(solution)/shard_map/ppermute | solution.py:41
  117.7 6.6 %collective-permute-start.28 = (bf16[64,1152]{1,0:T(8,128)(2,1)S(1)}, bf16[64,1152]{1,0:T(8,128)(2,1)S(1)}, u32[]{:S(2)}, u32[]{:S(2)}) collective-permute-start(bf16[64,1152]{1,0:T(8,128)(2,1)S(1)} %get-tuple-element.272.w0), channel_id=1, source_target_pairs={{0,1},{1,0},{2,3},{3,2},{4,5},{5,4},{6,7},{7,6},{8,9},{9,8},{10,11... | collective-permute-start | bytes 442376 | tf_op jit(solution)/shard_map/ppermute | solution.py:41
  119.3 9.1 %collective-permute-start.29 = (bf16[64,1152]{1,0:T(8,128)(2,1)S(1)}, bf16[64,1152]{1,0:T(8,128)(2,1)S(1)}, u32[]{:S(2)}, u32[]{:S(2)}) collective-permute-start(bf16[64,1152]{1,0:T(8,128)(2,1)S(1)} %get-tuple-element.272.w0), channel_id=1, source_target_pairs={{0,2},{1,3},{2,0},{3,1},{4,6},{5,7},{6,4},{7,5},{8,10},{9,11},{10,... | collective-permute-start | bytes 442376 | tf_op jit(solution)/shard_map/ppermute | solution.py:41
  119.6 8.9 %collective-permute-start.30 = (bf16[64,1152]{1,0:T(8,128)(2,1)S(1)}, bf16[64,1152]{1,0:T(8,128)(2,1)S(1)}, u32[]{:S(2)}, u32[]{:S(2)}) collective-permute-start(bf16[64,1152]{1,0:T(8,128)(2,1)S(1)} %get-tuple-element.272.w0), channel_id=1, source_target_pairs={{0,3},{1,2},{2,1},{3,0},{4,7},{5,6},{6,5},{7,4},{8,11},{9,10},{10,... | collective-permute-start | bytes 442376 | tf_op jit(solution)/shard_map/ppermute | solution.py:41
  138.7 2.7 %collective-permute-start.32 = (bf16[512,896]{1,0:T(8,128)(2,1)}, bf16[512,896]{1,0:T(8,128)(2,1)S(1)}, u32[]{:S(2)}, u32[]{:S(2)}) collective-permute-start(bf16[512,896]{1,0:T(8,128)(2,1)} %get-tuple-element.286), channel_id=1, source_target_pairs={{0,16},{16,0},{1,17},{17,1},{2,18},{18,2},{3,19},{19,3},{4,20},{20... | collective-permute-start | bytes 2752520 | tf_op jit(solution)/shard_map/ppermute | solution.py:41
  138.7 21.3 %collective-permute-start.31 = (bf16[4,64,1024]{2,1,0:T(8,128)(2,1)S(1)}, bf16[4,64,1024]{2,1,0:T(8,128)(2,1)S(1)}, u32[]{:S(2)}, u32[]{:S(2)}) collective-permute-start(bf16[4,64,1024]{2,1,0:T(8,128)(2,1)S(1)} %copy-done.22), channel_id=1, source_target_pairs={{0,3},{1,2},{2,1},{3,0},{4,7},{5,6},{6,5},{7,4},{8,11},{9,10},{10,... | collective-permute-start | bytes 1572872 | tf_op jit(solution)/shard_map/ppermute | solution.py:41
  144.0 21.6 %collective-permute-start.34 = (bf16[128,896]{1,0:T(8,128)(2,1)S(1)}, bf16[128,896]{1,0:T(8,128)(2,1)S(1)}, u32[]{:S(2)}, u32[]{:S(2)}) collective-permute-start(bf16[128,896]{1,0:T(8,128)(2,1)S(1)} %get-tuple-element.288), channel_id=1, source_target_pairs={{0,4},{4,0},{8,12},{12,8},{1,5},{5,1},{9,13},{13,9},{2,6},{6,2},{1... | collective-permute-start | bytes 688136 | tf_op jit(solution)/shard_map/ppermute | solution.py:41
  146.2 9.9 %collective-permute-start.35 = (bf16[64,1024]{1,0:T(8,128)(2,1)S(1)}, bf16[64,1024]{1,0:T(8,128)(2,1)S(1)}, u32[]{:S(2)}, u32[]{:S(2)}) collective-permute-start(bf16[64,1024]{1,0:T(8,128)(2,1)S(1)} %copy-done.32), channel_id=1, source_target_pairs={{0,1},{1,0},{2,3},{3,2},{4,5},{5,4},{6,7},{7,6},{8,9},{9,8},{10,11... | collective-permute-start | bytes 393224 | tf_op jit(solution)/shard_map/ppermute | solution.py:41
  146.9 18.7 %collective-permute-start.36 = (bf16[64,1024]{1,0:T(8,128)(2,1)}, bf16[64,1024]{1,0:T(8,128)(2,1)}, u32[]{:S(2)}, u32[]{:S(2)}) collective-permute-start(bf16[64,1024]{1,0:T(8,128)(2,1)} %get-tuple-element.291), channel_id=1, source_target_pairs={{0,2},{1,3},{2,0},{3,1},{4,6},{5,7},{6,4},{7,5},{8,10},{9,11},{10,... | collective-permute-start | bytes 393224 | tf_op jit(solution)/shard_map/ppermute | solution.py:41
  148.4 17.2 %collective-permute-start.37 = (bf16[64,1024]{1,0:T(8,128)(2,1)}, bf16[64,1024]{1,0:T(8,128)(2,1)}, u32[]{:S(2)}, u32[]{:S(2)}) collective-permute-start(bf16[64,1024]{1,0:T(8,128)(2,1)} %get-tuple-element.292), channel_id=1, source_target_pairs={{0,3},{1,2},{2,1},{3,0},{4,7},{5,6},{6,5},{7,4},{8,11},{9,10},{10,... | collective-permute-start | bytes 393224 | tf_op jit(solution)/shard_map/ppermute | solution.py:41
  156.1 19.2 %collective-permute-start.41 = (bf16[128,896]{1,0:T(8,128)(2,1)S(1)}, bf16[128,896]{1,0:T(8,128)(2,1)S(1)}, u32[]{:S(2)}, u32[]{:S(2)}) collective-permute-start(bf16[128,896]{1,0:T(8,128)(2,1)S(1)} %get-tuple-element.304), channel_id=1, source_target_pairs={{0,8},{4,12},{8,0},{12,4},{1,9},{5,13},{9,1},{13,5},{2,10},{6,14},... | collective-permute-start | bytes 688136 | tf_op jit(solution)/shard_map/ppermute | solution.py:41
  160.1 15.3 %collective-permute-start.42 = (bf16[128,896]{1,0:T(8,128)(2,1)S(1)}, bf16[128,896]{1,0:T(8,128)(2,1)S(1)}, u32[]{:S(2)}, u32[]{:S(2)}) collective-permute-start(bf16[128,896]{1,0:T(8,128)(2,1)S(1)} %get-tuple-element.305), channel_id=1, source_target_pairs={{0,12},{4,8},{8,4},{12,0},{1,13},{5,9},{9,5},{13,1},{2,14},{6,10},... | collective-permute-start | bytes 688136 | tf_op jit(solution)/shard_map/ppermute | solution.py:41
  167.7 11.8 %collective-permute-start.38 = (bf16[64,1024]{1,0:T(8,128)(2,1)}, bf16[64,1024]{1,0:T(8,128)(2,1)S(1)}, u32[]{:S(2)}, u32[]{:S(2)}) collective-permute-start(bf16[64,1024]{1,0:T(8,128)(2,1)} %input_grad.1.refs_0_), channel_id=1, source_target_pairs={{0,1},{1,0},{2,3},{3,2},{4,5},{5,4},{6,7},{7,6},{8,9},{9,8},{10,11... | collective-permute-start | bytes 393224 | tf_op jit(solution)/shard_map/ppermute | solution.py:41
  169.1 19.3 %collective-permute-start.39 = (bf16[64,1024]{1,0:T(8,128)(2,1)}, bf16[64,1024]{1,0:T(8,128)(2,1)S(1)}, u32[]{:S(2)}, u32[]{:S(2)}) collective-permute-start(bf16[64,1024]{1,0:T(8,128)(2,1)} %input_grad.1.refs_0_), channel_id=1, source_target_pairs={{0,2},{1,3},{2,0},{3,1},{4,6},{5,7},{6,4},{7,5},{8,10},{9,11},{10,... | collective-permute-start | bytes 393224 | tf_op jit(solution)/shard_map/ppermute | solution.py:41
  170.2 18.2 %collective-permute-start.40 = (bf16[64,1024]{1,0:T(8,128)(2,1)}, bf16[64,1024]{1,0:T(8,128)(2,1)S(1)}, u32[]{:S(2)}, u32[]{:S(2)}) collective-permute-start(bf16[64,1024]{1,0:T(8,128)(2,1)} %input_grad.1.refs_0_), channel_id=1, source_target_pairs={{0,3},{1,2},{2,1},{3,0},{4,7},{5,6},{6,5},{7,4},{8,11},{9,10},{10,... | collective-permute-start | bytes 393224 | tf_op jit(solution)/shard_map/ppermute | solution.py:41
  175.3 13.1 %collective-permute-start.43 = (bf16[64,1024]{1,0:T(8,128)(2,1)S(1)}, bf16[64,1024]{1,0:T(8,128)(2,1)S(1)}, u32[]{:S(2)}, u32[]{:S(2)}) collective-permute-start(bf16[64,1024]{1,0:T(8,128)(2,1)S(1)} %get-tuple-element.312), channel_id=1, source_target_pairs={{0,4},{4,0},{8,12},{12,8},{1,5},{5,1},{9,13},{13,9},{2,6},{6,2},{1... | collective-permute-start | bytes 393224 | tf_op jit(solution)/shard_map/ppermute | solution.py:41
  175.3 13.7 %collective-permute-start.44 = (bf16[64,1024]{1,0:T(8,128)(2,1)S(1)}, bf16[64,1024]{1,0:T(8,128)(2,1)S(1)}, u32[]{:S(2)}, u32[]{:S(2)}) collective-permute-start(bf16[64,1024]{1,0:T(8,128)(2,1)S(1)} %get-tuple-element.313), channel_id=1, source_target_pairs={{0,8},{4,12},{8,0},{12,4},{1,9},{5,13},{9,1},{13,5},{2,10},{6,14},... | collective-permute-start | bytes 393224 | tf_op jit(solution)/shard_map/ppermute | solution.py:41
  179.5 9.5 %collective-permute-start.45 = (bf16[64,1024]{1,0:T(8,128)(2,1)S(1)}, bf16[64,1024]{1,0:T(8,128)(2,1)S(1)}, u32[]{:S(2)}, u32[]{:S(2)}) collective-permute-start(bf16[64,1024]{1,0:T(8,128)(2,1)S(1)} %get-tuple-element.314), channel_id=1, source_target_pairs={{0,12},{4,8},{8,4},{12,0},{1,13},{5,9},{9,5},{13,1},{2,14},{6,10},... | collective-permute-start | bytes 393224 | tf_op jit(solution)/shard_map/ppermute | solution.py:41
  189.1 10.1 %collective-permute-start.46 = (bf16[80,1024]{1,0:T(8,128)(2,1)S(1)}, bf16[80,1024]{1,0:T(8,128)(2,1)S(1)}, u32[]{:S(2)}, u32[]{:S(2)}) collective-permute-start(bf16[80,1024]{1,0:T(8,128)(2,1)S(1)} %out_piece.1.refs_0_), channel_id=1, source_target_pairs={{0,1},{1,0},{2,3},{3,2},{4,5},{5,4},{6,7},{7,6},{8,9},{9,8},{10,11... | collective-permute-start | bytes 491528 | tf_op jit(solution)/shard_map/ppermute | solution.py:41
  190.5 8.7 %collective-permute-start.47 = (bf16[80,1024]{1,0:T(8,128)(2,1)S(1)}, bf16[80,1024]{1,0:T(8,128)(2,1)S(1)}, u32[]{:S(2)}, u32[]{:S(2)}) collective-permute-start(bf16[80,1024]{1,0:T(8,128)(2,1)S(1)} %out_piece.1.refs_0_), channel_id=1, source_target_pairs={{0,2},{1,3},{2,0},{3,1},{4,6},{5,7},{6,4},{7,5},{8,10},{9,11},{10,... | collective-permute-start | bytes 491528 | tf_op jit(solution)/shard_map/ppermute | solution.py:41
  191.8 7.5 %collective-permute-start.48 = (bf16[80,1024]{1,0:T(8,128)(2,1)S(1)}, bf16[80,1024]{1,0:T(8,128)(2,1)S(1)}, u32[]{:S(2)}, u32[]{:S(2)}) collective-permute-start(bf16[80,1024]{1,0:T(8,128)(2,1)S(1)} %out_piece.1.refs_0_), channel_id=1, source_target_pairs={{0,3},{1,2},{2,1},{3,0},{4,7},{5,6},{6,5},{7,4},{8,11},{9,10},{10,... | collective-permute-start | bytes 491528 | tf_op jit(solution)/shard_map/ppermute | solution.py:41
  (34 other events, 389.8 us)
